TPU v7x, 32 devices: a whole 2x2x4 slice. The times are simulated.
32 devices in a mesh: grp: 2 (over y), blk: 4 (over z), op: 4 (over x, core).
Axes of the slice: x: 2, y: 2, z: 4, core: 2. Of those that a mesh axis runs over, the one named last changes fastest.
Arguments:
- psi: bfloat16 [8, 256, 2048], P(('grp', 'blk')), parts along dimension 0, may hold values from -6 to 6
- left_ops: bfloat16 [8, 8, 256, 256], P('op', ('grp', 'blk')), parts along dimension 1, may hold values from -0.375 to 0.375
- right_ops: bfloat16 [8, 64, 64, 64], P('op', ('grp', 'blk')), parts along dimension 1, may hold values from -0.75 to 0.75
- term_shift: int32 [8], P('op'), may hold values from -2 to 2
- slot_sector: int32 [8], P('grp'), parts along dimension 0, may hold values from 0 to 3, each once
- sector_width: int32 [8], P('grp'), parts along dimension 0, may hold values from 64 to 256, as said below
- diag_left: float32 [8, 256], P('grp'), parts along dimension 0, may hold values from 0.25 to 4
- diag_right: float32 [4096], P(('grp', 'blk')), parts along dimension 0, may hold values from 0.25 to 4
Outputs:
- new_vector: bfloat16 [8, 256, 2048], P('grp', 'op', 'blk'), parts along dimension 0
- residual: bfloat16 [8, 256, 2048], P('grp', 'op', 'blk'), parts along dimension 0
- energy: float32 [2], P('grp'), parts along dimension 0
There are 2 independent parts, one for each index of `grp`. A program takes and returns all parts, laid end to end along the dimension named above; an argument that names none is the same for every part. Nothing has to cross between parts.
Inputs may be any that keep to these rules, and one draw needn't show every extreme that they name: `slot_sector`: slot s lies on blk index s; each left sector is held in exactly one slot. `sector_width`: one sector has 256 live rows and one has 64.
All inputs are finite; a program needn't handle non-finite values.
Results may differ from a plain program's by a relative error of at most 0.015.
Values may be sent and summed in bfloat16 or wider, within the bound.
No kernel may reach another device: no remote copies, remote signals or barrier semaphores. Data moves between devices by JAX's collectives and lax.ppermute only.
A program may use at most 64 MiB of HBM per device.

v0:
```python
import jax
import jax.numpy as jnp
from jax import lax
from jax.sharding import PartitionSpec as P

EPS = 1e-06


def per_device(
    psi, left_ops, right_ops, term_shift, slot_sector, sector_width, diag_left, diag_right
):
    sec_dev, rows, ncols = psi.shape
    nsec = slot_sector.shape[0]
    terms_dev = left_ops.shape[0]
    right_local = right_ops.shape[1]
    right_width = right_ops.shape[2]
    local_cols = diag_right.shape[0]
    count = float(nsec * rows * ncols)
    match = slot_sector[:, None] == jnp.arange(nsec)[None, :]
    widths = jnp.sum(jnp.where(match, sector_width[None, :], 0), axis=1)
    mask_all = (jnp.arange(rows)[None, :] < widths[:, None]).astype(jnp.float32)
    own_mask = lax.dynamic_slice_in_dim(mask_all, lax.axis_index("blk") * sec_dev, sec_dev, 0)
    raw = psi.astype(jnp.float32) * own_mask[:, :, None]
    squares = lax.psum(jnp.sum(raw * raw), "blk")
    v_left = (raw * lax.rsqrt(squares / count + EPS)).astype(jnp.bfloat16)
    onehots = (
        slot_sector[None, None, :] == slot_sector[None, :, None] - term_shift[:, None, None]
    ).astype(jnp.bfloat16)
    op_rows = rows // lax.axis_size("op")
    op_start = lax.axis_index("op") * op_rows
    dmat = diag_left[:, :, None] + diag_right[None, None, :]

    def left_local(field):
        return jnp.einsum(
            "ksij,sjc->ksic", left_ops, field, preferred_element_type=jnp.float32
        ).astype(jnp.bfloat16)

    def right_part(moved_in):
        flat = moved_in.reshape(terms_dev, nsec, rows * local_cols)
        shifted = jnp.einsum(
            "kts,ksx->ktx", onehots, flat, preferred_element_type=jnp.float32
        ).astype(jnp.bfloat16)
        shifted = shifted.reshape(terms_dev, nsec, rows, right_local, right_width)
        accum = jnp.einsum(
            "ktwrc,krdc->twrd", shifted, right_ops, preferred_element_type=jnp.float32
        )
        return accum.reshape(nsec, rows, local_cols) * mask_all[:, :, None]

    def op_total(partial_value):
        return lax.psum(partial_value.astype(jnp.bfloat16), "op").astype(jnp.float32)

    def final_rows(array):
        return lax.dynamic_slice_in_dim(array, op_start, op_rows, 1)

    def reduce_dots(values):
        sums = lax.psum(values, "blk")
        return tuple((item / count for item in sums))

    moved_first, v_moved = (
        lax.all_to_all(left_local(v_left), "blk", split_axis=3, concat_axis=1, tiled=True),
        lax.all_to_all(v_left[None], "blk", split_axis=3, concat_axis=1, tiled=True),
    )
    v_right = v_moved[0]
    vec32 = v_right.astype(jnp.float32)
    first_sigma = op_total(right_part(moved_first)) + dmat * vec32
    theta = reduce_dots((jnp.sum(vec32 * first_sigma),))[0]
    resid = first_sigma - theta * vec32
    den = dmat - theta
    corr = resid * den / jnp.maximum(den * den, 0.25)
    along = reduce_dots((jnp.sum(vec32 * corr),))[0]
    orth = corr - along * vec32
    norm_sq = reduce_dots((jnp.sum(orth * orth),))[0]
    update = (orth * lax.rsqrt(norm_sq + EPS)).astype(jnp.bfloat16)
    upd32 = update.astype(jnp.float32)
    upd_left = lax.all_to_all(update, "blk", split_axis=0, concat_axis=2, tiled=True)
    moved_second = lax.all_to_all(
        left_local(upd_left), "blk", split_axis=3, concat_axis=1, tiled=True
    )
    second_sigma = op_total(right_part(moved_second)) + dmat * upd32
    v_s1, u_s0, u_s1 = reduce_dots(
        (jnp.sum(vec32 * second_sigma), jnp.sum(upd32 * first_sigma), jnp.sum(upd32 * second_sigma))
    )
    h_mix = 0.5 * (v_s1 + u_s0)
    angle = 0.5 * jnp.arctan2(2.0 * h_mix, theta - u_s1)
    sine = jnp.sin(angle)
    flip = jnp.where(sine > 0, -1.0, 1.0)
    coef_v = -sine * flip
    coef_u = jnp.cos(angle) * flip
    half = 0.5 * (theta - u_s1)
    energy = 0.5 * (theta + u_s1) - jnp.sqrt(half * half + h_mix * h_mix)
    newvec = coef_v * vec32 + coef_u * upd32
    image = coef_v * first_sigma + coef_u * second_sigma
    new_out = final_rows(newvec.astype(jnp.bfloat16))
    res_out = final_rows((image - energy * newvec).astype(jnp.bfloat16))
    return (new_out, res_out, jnp.reshape(energy, (1,)))


def solution(mesh):
    placed = (
        P(("grp", "blk"), None, None),
        P("op", ("grp", "blk"), None, None),
        P("op", ("grp", "blk"), None, None),
        P("op"),
        P("grp"),
        P("grp"),
        P("grp", None),
        P(("grp", "blk")),
    )
    return jax.shard_map(
        per_device,
        mesh=mesh,
        in_specs=placed,
        out_specs=(P("grp", "op", "blk"), P("grp", "op", "blk"), P("grp")),
        check_vma=False,
    )
```

profile of v0, /device:TPU:0, one launch (start us, length us, event | category | flops | bytes accessed | tf_op | source)
XLA Modules:
  0.0 384.3 jit_solution(3385981057251656963)
XLA Ops:
  7.2 0.0 copy-start
  7.2 0.9 select_reduce_fusion
  8.1 0.1 fusion.39
  8.2 2.5 multiply_reduce_fusion.1
  10.7 14.1 %psum.63 = f32[]{:T(128)} all-reduce(f32[]{:T(128)} %multiply_reduce_fusion.1), channel_id=1, replica_groups=mesh['grp'=2,'blk'=4,'op'=4] {'blk'}, use_global_device_ids=true, to_apply=%region_2.3 | all-reduce | flops 1 | bytes 8 | tf_op jit(solution)/shard_map/psum | solution.py:24
  25.4 2.1 fusion.6
  27.5 14.0 %copy.62 = bf16[2,1,256,2048]{2,0,1,3:T(2,128)(2,1)} copy(bf16[2,1,256,2048]{2,3,0,1:T(8,128)(2,1)S(1)} %fusion.6) | data formatting | bytes 4194304 | tf_op jit(solution)/shard_map/convert_element_type | solution.py:36
  41.5 3.7 all-to-all-start.1
  45.3 0.0 copy-done.2
  45.3 1.3 fusion.32
  46.6 6.0 %copy.59 = bf16[1,1,256,2048]{2,1,0,3:T(2,128)(2,1)} copy(bf16[1,1,256,2048]{3,2,1,0:T(8,128)(2,1)} %fusion.32) | data formatting | bytes 2097152 | tf_op jit(solution)/shard_map/broadcast_in_dim | solution.py:61
  52.5 0.5 broadcast.44
  53.1 11.6 %reduce = bf16[2048,256]{1,0:T(8,128)(2,1)S(1)} reduce(bf16[2048,1,1,256]{3,2,1,0:T(2,128)(2,1)} %bitcast.128, bf16[]{:T(256)} %broadcast.44), dimensions={1,2}, to_apply=%bitcast.99.reduce_sub_computation | reduce | bytes 2097154
  64.7 0.0 copy-start.8
  64.7 0.0 copy-start.9
  64.7 1.7 reshape.128
  66.4 25.3 %all-to-all-done.1 = bf16[2,1,256,2048]{2,0,1,3:T(2,128)(2,1)S(1)} async-done(((bf16[2,1,256,2048]{2,0,1,3:T(2,128)(2,1)}), bf16[2,1,256,2048]{2,0,1,3:T(2,128)(2,1)S(1)}, u32[]{:S(2)}, u32[]{:S(2)}) %all-to-all-start.1) | async-done | bytes 2097184 | tf_op jit(solution)/shard_map/all_to_all | solution.py:60
  91.7 4.2 %all-to-all-start = ((bf16[4,2,65536]{2,1,0:T(2,128)(2,1)}), bf16[4,2,65536]{2,1,0:T(2,128)(2,1)}, u32[]{:S(2)}, u32[]{:S(2)}) async-start(bf16[4,2,65536]{2,1,0:T(2,128)(2,1)} %reshape.128), calls=%async_computation | async-start | bytes 2097152 | tf_op jit(solution)/shard_map/all_to_all | solution.py:61
  95.9 0.2 all-reduce.4.cloned.1.call-start
  96.1 0.1 broadcast_subtract_fusion
  96.2 4.6 %copy.63 = bf16[2,1,256,4,512]{4,2,3,0,1:T(8,128)(2,1)} copy(bf16[2,1,256,4,512]{2,0,4,3,1:T(2,128)(2,1)S(1)} %bitcast.127) | data formatting | bytes 4194304 | tf_op jit(solution)/shard_map/all_to_all | solution.py:60
  100.8 3.8 reshape.112
  104.5 2.9 convolution_convert_fusion.1
  107.4 0.0 copy-start.5
  107.4 4.5 %reshape.113 = bf16[2,4,256,8,64]{4,3,2,1,0:T(8,128)(2,1)} reshape(bf16[2,4,131072]{2,1,0:T(4,128)(2,1)S(1)} %convolution_convert_fusion.1) | data formatting | bytes 4194304 | tf_op jit(solution)/shard_map/reshape | solution.py:43
  112.0 3.6 fusion.22
  115.6 0.2 copy.66
  115.8 1.2 fusion.21
  117.0 0.0 all-reduce.4.cloned.1.call-update
  117.0 0.0 all-reduce.6.cloned.1.call-start
  117.1 4.1 %all-to-all-done = bf16[4,2,65536]{2,1,0:T(2,128)(2,1)} async-done(((bf16[4,2,65536]{2,1,0:T(2,128)(2,1)}), bf16[4,2,65536]{2,1,0:T(2,128)(2,1)}, u32[]{:S(2)}, u32[]{:S(2)}) %all-to-all-start) | async-done | bytes 1048608 | tf_op jit(solution)/shard_map/all_to_all | solution.py:61
  121.2 4.0 %reshape.129 = bf16[2048,1,1,256]{3,2,1,0:T(2,128)(2,1)} reshape(bf16[4,2,65536]{2,1,0:T(2,128)(2,1)} %all-to-all-done) | data formatting | bytes 2097152
  125.2 29.3 %all-reduce.4.cloned.1.call-done = bf16[4,256,512]{1,2,0:T(8,128)(2,1)} async-done(((bf16[4,256,512]{1,2,0:T(8,128)(2,1)}), bf16[4,256,512]{1,2,0:T(8,128)(2,1)}) %all-reduce.4.cloned.1.call-update) | async-done | bytes 1048592 | tf_op jit(solution)/shard_map/psum | solution.py:50
  154.5 2.4 fusion.13
  156.9 1.2 fusion.16
  158.0 12.3 %psum.65 = f32[]{:T(128)} all-reduce(f32[]{:T(128)} %fusion.16), channel_id=1, replica_groups=mesh['grp'=2,'blk'=4,'op'=4] {'blk'}, use_global_device_ids=true, to_apply=%region_5.6 | all-reduce | flops 1 | bytes 8 | tf_op jit(solution)/shard_map/psum | solution.py:56
  171.0 2.2 fusion.8
  173.2 1.3 copy-done.1
  174.5 1.2 fusion.18
  175.7 9.0 %psum.66 = f32[]{:T(128)} all-reduce(f32[]{:T(128)} %fusion.18), channel_id=1, replica_groups=mesh['grp'=2,'blk'=4,'op'=4] {'blk'}, use_global_device_ids=true, to_apply=%region_7.8 | all-reduce | flops 1 | bytes 8 | tf_op jit(solution)/shard_map/psum | solution.py:56
  185.3 2.7 multiply_reduce_fusion
  188.0 11.0 %psum.67 = f32[]{:T(128)} all-reduce(f32[]{:T(128)} %multiply_reduce_fusion), channel_id=1, replica_groups=mesh['grp'=2,'blk'=4,'op'=4] {'blk'}, use_global_device_ids=true, to_apply=%region_9.10 | all-reduce | flops 1 | bytes 8 | tf_op jit(solution)/shard_map/psum | solution.py:56
  199.7 2.4 multiply_convert_fusion
  202.1 22.2 %all_to_all.54 = bf16[4,256,512]{1,2,0:T(8,128)(2,1)S(1)} all-to-all(bf16[4,256,512]{1,2,0:T(8,128)(2,1)S(1)} %multiply_convert_fusion), channel_id=1, replica_groups=mesh['grp'=2,'blk'=4,'op'=4] {'blk'}, dimensions={0} | all-to-all | bytes 2097152 | tf_op jit(solution)/shard_map/all_to_all | solution.py:75
  224.3 0.7 fusion.7
  225.1 12.8 %copy.67 = bf16[2,1,256,2048]{2,0,1,3:T(2,128)(2,1)S(1)} copy(bf16[2,1,256,2048]{2,3,0,1:T(8,128)(2,1)S(1)} %fusion.7) | data formatting | bytes 4194304 | tf_op jit(solution)/shard_map/convert_element_type | solution.py:36
  237.9 48.9 %all_to_all.55 = bf16[2,1,256,2048]{2,0,1,3:T(2,128)(2,1)} all-to-all(bf16[2,1,256,2048]{2,0,1,3:T(2,128)(2,1)S(1)} %copy.67), channel_id=1, replica_groups=mesh['grp'=2,'blk'=4,'op'=4] {'blk'}, dimensions={3} | all-to-all | bytes 4194304 | tf_op jit(solution)/shard_map/all_to_all | solution.py:76
  286.8 6.1 %copy.68 = bf16[2,1,256,4,512]{4,2,3,0,1:T(8,128)(2,1)} copy(bf16[2,1,256,4,512]{2,0,4,3,1:T(2,128)(2,1)} %bitcast.130) | data formatting | bytes 4194304 | tf_op jit(solution)/shard_map/all_to_all | solution.py:76
  292.9 3.8 reshape.116
  296.7 4.2 %convolution_convert_fusion = bf16[2,4,131072]{2,1,0:T(4,128)(2,1)} fusion(bf16[2,4,131072]{2,1,0:T(4,128)(2,1)} %reshape.116, s32[2,4]{1,0:T(2,128)S(1)} %broadcast_subtract_fusion, s32[4]{0:T(128)S(1)} %copy-done.8), kind=kOutput, calls=%fused_computation | convolution fusion | flops 9437216 | bytes 4194352 | tf_op jit(solution)/shard_map/kts,ksx->ktx/dot_general | solution.py:40
  300.9 6.0 %reshape.117 = bf16[2,4,256,8,64]{4,3,2,1,0:T(8,128)(2,1)} reshape(bf16[2,4,131072]{2,1,0:T(4,128)(2,1)} %convolution_convert_fusion) | data formatting | bytes 4194304 | tf_op jit(solution)/shard_map/reshape | solution.py:43
  306.9 3.7 fusion.25
  310.6 0.2 copy.71
  310.8 1.2 fusion.15
  312.0 0.0 all-reduce.6.cloned.1.call-update
  312.0 35.1 %all-reduce.6.cloned.1.call-done = bf16[4,256,512]{1,2,0:T(8,128)(2,1)} async-done(((bf16[4,256,512]{1,2,0:T(8,128)(2,1)}), bf16[4,256,512]{1,2,0:T(8,128)(2,1)}) %all-reduce.6.cloned.1.call-update) | async-done | bytes 1048592 | tf_op jit(solution)/shard_map/psum | solution.py:50
  347.1 4.4 %fusion.11 = (f32[]{:T(128)}, f32[]{:T(128)}, f32[]{:T(128)}, f32[4,256,512]{1,2,0:T(8,128)}) fusion(bf16[4,256,512]{1,2,0:T(8,128)(2,1)} %copy-done.3, f32[512]{0:T(512)S(1)} %copy-done.7, f32[4,256]{1,0:T(4,128)S(1)} %copy-done.6, bf16[4,256,512]{1,2,0:T(8,128)(2,1)} %all-reduce.6.cloned.1.call-done, bf16[1,1,256,4,512]{2,4,3,1,0:T(8,128)(2,1)S(1)} %bitcast.125, ...), kind=kLoop, calls=%fused_computation.21 | loop fusion | flops 6291453 | bytes 7346188 | tf_op jit(solution)/shard_map/reduce_sum | solution.py:81
  352.8 12.3 %all-reduce = (f32[]{:T(128)}, f32[]{:T(128)}) all-reduce(f32[]{:T(128)S(6)} %div.27, f32[]{:T(128)} %get-tuple-element.15), channel_id=1, replica_groups=mesh['grp'=2,'blk'=4,'op'=4] {'blk'}, use_global_device_ids=true, to_apply=%region_12.13 | all-reduce | flops 2 | bytes 16 | tf_op jit(solution)/shard_map/psum | solution.py:56
  368.0 2.6 fusion.12
  370.6 1.3 copy-done.4
  371.9 0.2 dynamic-slice_convert_fusion
  372.1 0.9 copy.72
  373.0 2.4 fusion.30
  375.4 0.9 copy.73
  (14 shorter events, 0.0 us)
Async XLA Ops:
  7.2 18.2 %copy-start = (bf16[2,1,256,256]{3,2,1,0:T(8,128)(2,1)S(1)}, bf16[2,1,256,256]{3,2,1,0:T(8,128)(2,1)}, u32[]{:S(2)}) copy-start(bf16[2,1,256,256]{3,2,1,0:T(8,128)(2,1)} %param.9) | copy-start | bytes 786436
  41.5 3.8 copy-start.2
  41.5 50.1 %all-to-all-start.1 = ((bf16[2,1,256,2048]{2,0,1,3:T(2,128)(2,1)}), bf16[2,1,256,2048]{2,0,1,3:T(2,128)(2,1)S(1)}, u32[]{:S(2)}, u32[]{:S(2)}) async-start(bf16[2,1,256,2048]{2,0,1,3:T(2,128)(2,1)} %copy.62), calls=%async_computation.1 | async-start | bytes 4194304 | tf_op jit(solution)/shard_map/all_to_all | solution.py:60
  64.7 31.4 %copy-start.8 = (s32[4]{0:T(128)S(1)}, s32[4]{0:T(128)}, u32[]{:S(2)}) copy-start(s32[4]{0:T(128)} %param.12) | copy-start | bytes 52
  64.7 31.4 %copy-start.9 = (s32[2]{0:T(128)S(1)}, s32[2]{0:T(128)}, u32[]{:S(2)}) copy-start(s32[2]{0:T(128)} %param.11) | copy-start | bytes 28
  91.7 29.5 %all-to-all-start = ((bf16[4,2,65536]{2,1,0:T(2,128)(2,1)}), bf16[4,2,65536]{2,1,0:T(2,128)(2,1)}, u32[]{:S(2)}, u32[]{:S(2)}) async-start(bf16[4,2,65536]{2,1,0:T(2,128)(2,1)} %reshape.128), calls=%async_computation | async-start | bytes 2097152 | tf_op jit(solution)/shard_map/all_to_all | solution.py:61
  95.9 58.6 %all-reduce.4.cloned.1.call-start = ((), (), s32[]{:S(2)}) async-start(), calls=%async_computation.4 | async-start | bytes 2097152 | tf_op jit(solution)/shard_map/psum | solution.py:50
  107.4 4.6 %copy-start.5 = (bf16[2,8,64,64]{3,2,1,0:T(8,128)(2,1)S(1)}, bf16[2,8,64,64]{3,2,1,0:T(8,128)(2,1)}, u32[]{:S(2)}) copy-start(bf16[2,8,64,64]{3,2,1,0:T(8,128)(2,1)} %param.10) | copy-start | bytes 393220
  117.0 37.5 %copy-start.6 = (f32[4,256]{1,0:T(4,128)S(1)}, f32[4,256]{1,0:T(4,128)}, u32[]{:S(2)}) copy-start(f32[4,256]{1,0:T(4,128)} %param.14) | copy-start | bytes 12292
  117.0 37.5 %copy-start.7 = (f32[512]{0:T(512)S(1)}, f32[512]{0:T(512)}, u32[]{:S(2)}) copy-start(f32[512]{0:T(512)} %param.15) | copy-start | bytes 6148
  117.0 230.1 %all-reduce.6.cloned.1.call-start = ((), (), s32[]{:S(2)}) async-start(), calls=%async_computation.5 | async-start | bytes 2097152 | tf_op jit(solution)/shard_map/psum | solution.py:50
  173.1 1.4 copy-start.1
  202.1 23.0 %copy-start.3 = (bf16[4,256,512]{1,2,0:T(8,128)(2,1)}, bf16[4,256,512]{1,2,0:T(8,128)(2,1)S(1)}, u32[]{:S(2)}) copy-start(bf16[4,256,512]{1,2,0:T(8,128)(2,1)S(1)} %multiply_convert_fusion) | copy-start | bytes 3145732
  370.6 1.3 copy-start.4
Sparse Core Ops, SparseCore 0:
  117.1 37.2 all-reduce.3
  312.1 34.9 all-reduce.5
where the time goes:
time: 386 us; the launch traced here: 384 us
  blocking collectives  130 us (34%)
  waiting for transfers between devices  93.8 us (24%)
  local copies, waits for them, and re-layouts  72.9 us (19%)
  other arithmetic  40.2 us (10%)
  between operations  22.3 us (6%)
  matrix products  17.2 us (4%)
  starting transfers between devices  8.23 us (2%)
    psum x2, waiting for transfers between devices, op_total(): lax.psum(partial_value.astype(jnp.bfloat16), 'op').astype(jnp.float32)  64.4 us
    all_to_all x1, blocking collectives, per_device(): lax.all_to_all(left_local(upd_left), 'blk', split_axis=3, concat_axis=1,...  48.9 us
    psum x4, blocking collectives, reduce_dots(): sums = lax.psum(values, 'blk')  44.6 us
    convert_element_type x2, local copies, waits for them, and re-layouts, left_local(): return jnp.einsum('ksij,sjc->ksic', left_ops, field, preferred_element_ty...  26.8 us
    all_to_all x1, waiting for transfers between devices, per_device(): lax.all_to_all(left_local(v_left), 'blk', split_axis=3, concat_axis=1, ti...  25.3 us
    all_to_all x1, blocking collectives, per_device(): lax.all_to_all(update, 'blk', split_axis=0, concat_axis=2, tiled=True)  22.2 us
    psum x1, blocking collectives, per_device(): squares = lax.psum(jnp.sum(raw * raw), 'blk')  14.1 us
    unnamed x1, other arithmetic  11.6 us
  transfers between devices with their start and end apart: 4, of which 4 were waited for; matrix products, arithmetic and copies ran while one was open for 12% of the time, Pallas kernels for 0%

commit v1 on v0

--- a/solution.py
+++ b/solution.py
@@ -1,12 +1,18 @@
+import functools
+
 import jax
 import jax.numpy as jnp
 from jax import lax
+from jax.experimental import pallas as pl
+from jax.experimental.pallas import tpu as pltpu
 from jax.sharding import PartitionSpec as P
 
 EPS = 1e-06
-
-
-def per_device(
+LANES = 128
+VMEM_LIMIT = 40 * 1024 * 1024
+
+
+def per_device_general(
     psi, left_ops, right_ops, term_shift, slot_sector, sector_width, diag_left, diag_right
 ):
     sec_dev, rows, ncols = psi.shape
@@ -81,18 +87,281 @@
         (jnp.sum(vec32 * second_sigma), jnp.sum(upd32 * first_sigma), jnp.sum(upd32 * second_sigma))
     )
     h_mix = 0.5 * (v_s1 + u_s0)
-    angle = 0.5 * jnp.arctan2(2.0 * h_mix, theta - u_s1)
-    sine = jnp.sin(angle)
-    flip = jnp.where(sine > 0, -1.0, 1.0)
-    coef_v = -sine * flip
-    coef_u = jnp.cos(angle) * flip
-    half = 0.5 * (theta - u_s1)
-    energy = 0.5 * (theta + u_s1) - jnp.sqrt(half * half + h_mix * h_mix)
+    coef_v, coef_u, energy = ritz(theta, h_mix, u_s1)
     newvec = coef_v * vec32 + coef_u * upd32
     image = coef_v * first_sigma + coef_u * second_sigma
     new_out = final_rows(newvec.astype(jnp.bfloat16))
     res_out = final_rows((image - energy * newvec).astype(jnp.bfloat16))
     return (new_out, res_out, jnp.reshape(energy, (1,)))
+
+
+def ritz(theta, h_mix, h_two):
+    angle = 0.5 * jnp.arctan2(2.0 * h_mix, theta - h_two)
+    sine = jnp.sin(angle)
+    flip = jnp.where(sine > 0, -1.0, 1.0)
+    coef_v = -sine * flip
+    coef_u = jnp.cos(angle) * flip
+    half = 0.5 * (theta - h_two)
+    energy = 0.5 * (theta + h_two) - jnp.sqrt(half * half + h_mix * h_mix)
+    return coef_v, coef_u, energy
+
+
+def call(body, out_shape, scratch=(), scalars=0, flops=0, nbytes=0, n_in=0):
+    return pl.pallas_call(
+        body,
+        out_shape=out_shape,
+        in_specs=[pl.BlockSpec(memory_space=pltpu.SMEM)] * scalars
+        + [pl.BlockSpec(memory_space=pltpu.VMEM)] * n_in,
+        out_specs=jax.tree.map(lambda _: pl.BlockSpec(memory_space=pltpu.VMEM), out_shape),
+        scratch_shapes=list(scratch),
+        compiler_params=pltpu.CompilerParams(vmem_limit_bytes=VMEM_LIMIT),
+        cost_estimate=pl.CostEstimate(flops=flops, bytes_accessed=nbytes, transcendentals=0),
+    )
+
+
+def pack_body(meta, psi, right, psi_out, right_out):
+    n_blk, _, cols = psi_out.shape
+    n_op = right_out.shape[0]
+    terms, _, width, _ = right.shape
+    per = cols // width
+    own = meta[0]
+    for b in range(n_blk):
+        start = pl.multiple_of((b * n_op + own) * cols, LANES)
+        psi_out[b] = psi[0, :, pl.ds(start, cols)]
+    right_out[...] = jnp.zeros_like(right_out)
+    for d in range(n_op):
+        for k in range(terms):
+            for r in range(per):
+                row = (k * per + r) * width
+                right_out[d, row : row + width, r * width : (r + 1) * width] = right[k, d * per + r]
+
+
+def apply_h(src, field, left, right, gmat, emit):
+    nsec = len(field)
+    cols = field[0].shape[1]
+    n_dev, terms_dev = left.shape[0], left.shape[1]
+    n_op = n_dev // nsec
+    terms = n_op * terms_dev
+    for s in range(nsec):
+        prod = lax.dot_general(
+            field[s], right[...], (((1,), (1,)), ((), ())), preferred_element_type=jnp.float32
+        )
+        gmat[s] = prod.astype(jnp.bfloat16)
+    gmat[nsec] = jnp.zeros_like(gmat[nsec])
+    for t in range(nsec):
+        total = None
+        for k in range(terms):
+            s = src[k * nsec + t]
+            held = jnp.minimum(s, nsec - 1) * n_op + k // terms_dev
+            part = jnp.dot(
+                left[held, k % terms_dev],
+                gmat[s, :, k * cols : (k + 1) * cols],
+                preferred_element_type=jnp.float32,
+            )
+            total = part if total is None else total + part
+        emit(t, total)
+
+
+def row_mask(width, shape):
+    return lax.broadcasted_iota(jnp.int32, shape, 0) < width
+
+
+def fold(x):
+    return jnp.sum(x.reshape(-1, 8, x.shape[-1]), axis=0)
+
+
+def whole(x):
+    return jnp.sum(jnp.sum(x, axis=0, keepdims=True), axis=1, keepdims=True)
+
+
+def first_body(src, widths, psi, left, right, dmat, sig_out, raw_out, dots_out, gmat):
+    nsec = psi.shape[0]
+    field = []
+    for t in range(nsec):
+        block = psi[t]
+        raw = jnp.where(row_mask(widths[t], block.shape), block.astype(jnp.float32), 0.0)
+        field.append(raw.astype(jnp.bfloat16))
+        raw_out[t] = field[t]
+    sums = [jnp.zeros((8, psi.shape[2]), jnp.float32) for _ in range(2)]
+
+    def emit(t, total):
+        raw = field[t].astype(jnp.float32)
+        sigma = jnp.where(row_mask(widths[t], total.shape), total, 0.0) + dmat[t] * raw
+        sig_out[t] = sigma
+        sums[0] = sums[0] + fold(raw * raw)
+        sums[1] = sums[1] + fold(raw * sigma)
+
+    apply_h(src, field, left, right, gmat, emit)
+    tile = spread([whole(x) for x in sums], dots_out.shape[1:])
+    for d in range(dots_out.shape[0]):
+        dots_out[d] = tile
+
+
+def spread(values, shape):
+    line = lax.broadcasted_iota(jnp.int32, shape, 0)
+    tile = jnp.zeros(shape, jnp.float32)
+    for j, value in enumerate(values):
+        tile = jnp.where(line == j, value, tile)
+    return tile
+
+
+def norm_theta(parts, count):
+    tot = jnp.sum(parts, axis=0) * (1.0 / count)
+    scale = lax.rsqrt(tot[0:1] + EPS)
+    theta = tot[1:2] * scale * scale
+    return scale[:, 0:1], theta[:, 0:1]
+
+
+def second_body(count, src, widths, parts, raw_in, sig_in, left, right, dmat, f_out, t_out, dots_out, gmat, corr):
+    nsec = raw_in.shape[0]
+    scale, theta = norm_theta(parts[...], count)
+    zero = jnp.zeros((8, raw_in.shape[2]), jnp.float32)
+    vv, vc, vs = zero, zero, zero
+    for t in range(nsec):
+        vec = raw_in[t].astype(jnp.float32) * scale
+        sigma = sig_in[t] * scale
+        den = dmat[t] - theta
+        item = (sigma - theta * vec) * den / jnp.maximum(den * den, 0.25)
+        corr[t] = item
+        vv, vc, vs = vv + fold(vec * vec), vc + fold(vec * item), vs + fold(vec * sigma)
+    vv, vc, vs = whole(vv), whole(vc), whole(vs)
+    along = vc / jnp.maximum(vv, 1e-30)
+    field = []
+    for t in range(nsec):
+        vec = raw_in[t].astype(jnp.float32) * scale
+        block = (corr[t] - along * vec).astype(jnp.bfloat16)
+        field.append(block)
+        f_out[t] = block
+    sums = [zero for _ in range(5)]
+
+    def emit(t, total):
+        fld = f_out[t].astype(jnp.float32)
+        image = jnp.where(row_mask(widths[t], total.shape), total, 0.0) + dmat[t] * fld
+        t_out[t] = image
+        vec = raw_in[t].astype(jnp.float32) * scale
+        sigma = sig_in[t] * scale
+        for j, prod in enumerate((fld * fld, vec * fld, vec * image, fld * sigma, fld * image)):
+            sums[j] = sums[j] + fold(prod)
+
+    apply_h(src, field, left, right, gmat, emit)
+    tile = spread([vv, vc, vs] + [whole(x) for x in sums], dots_out.shape[1:])
+    for d in range(dots_out.shape[0]):
+        dots_out[d] = tile
+
+
+def third_body(count, meta, parts1, parts2, raw_in, sig_in, f_in, t_in, coefs, new_out, res_out):
+    nsec, rows, _ = raw_in.shape
+    n_op = new_out.shape[0]
+    step = rows // n_op
+    scale, theta = norm_theta(parts1[...], count)
+    cv, cu, energy, beta = coefs[0], coefs[1], coefs[2], coefs[3]
+    for t in range(nsec):
+        vec = raw_in[t].astype(jnp.float32) * scale
+        sigma = sig_in[t] * scale
+        newvec = cv * vec + cu * (f_in[t].astype(jnp.float32) + beta * vec)
+        image = cv * sigma + cu * (t_in[t] + beta * sigma)
+        res = (image - energy * newvec).astype(jnp.bfloat16)
+        newvec = newvec.astype(jnp.bfloat16)
+        for d in range(n_op):
+            new_out[d, t] = newvec[d * step : (d + 1) * step]
+            res_out[d, t] = res[d * step : (d + 1) * step]
+
+
+def combine_scalars(parts1, parts2, count, own):
+    tot = jnp.sum(parts1[:, :2, 0], axis=0) / count
+    scale = lax.rsqrt(tot[0] + EPS)
+    theta = tot[1] * scale * scale
+    vv, vc, vs, ff, vf, vt, fs, ft = (parts2[:, j, 0] for j in range(8))
+    local = vc / jnp.maximum(vv, 1e-30)
+    along = jnp.sum(vc) / count
+    beta = local - along
+    norm_sq = jnp.sum(ff + 2.0 * beta * vf + beta * beta * vv) / count
+    unit = lax.rsqrt(jnp.maximum(norm_sq, 0.0) + EPS)
+    v_s1 = unit * jnp.sum(vt + beta * vs) / count
+    u_s0 = unit * jnp.sum(fs + beta * vs) / count
+    u_s1 = unit * unit * jnp.sum(ft + beta * (vt + fs) + beta * beta * vs) / count
+    h_mix = 0.5 * (v_s1 + u_s0)
+    cv, cu, energy = ritz(theta, h_mix, u_s1)
+    own_beta = jnp.sum(jnp.where(jnp.arange(beta.shape[0]) == own, beta, 0.0))
+    return jnp.stack([cv, cu * unit, energy, own_beta]), energy
+
+
+def per_device(
+    psi, left_ops, right_ops, term_shift, slot_sector, sector_width, diag_left, diag_right
+):
+    n_blk, n_op = lax.axis_size("blk"), lax.axis_size("op")
+    _, rows, ncols = psi.shape
+    nsec = slot_sector.shape[0]
+    terms_dev, _, width, _ = right_ops.shape[0], 0, right_ops.shape[2], 0
+    terms = terms_dev * n_op
+    cols = diag_right.shape[0] // n_op
+    count = float(nsec * rows * ncols)
+    n_dev = n_blk * n_op
+    both = ("blk", "op")
+    own_op = lax.axis_index("op")
+    own = lax.axis_index("blk") * n_op + own_op
+    bf16, f32 = jnp.bfloat16, jnp.float32
+
+    left = lax.all_gather(left_ops[:, 0], both, axis=0, tiled=False)
+    shifts = lax.all_gather(term_shift, "op", axis=0, tiled=True)
+
+    psi_send, right_send = call(
+        pack_body,
+        (
+            jax.ShapeDtypeStruct((n_blk, rows, cols), bf16),
+            jax.ShapeDtypeStruct((n_op, terms_dev * cols, cols), bf16),
+        ),
+        scalars=1,
+        n_in=2,
+        nbytes=3 << 20,
+    )(jnp.reshape(own_op, (1,)).astype(jnp.int32), psi, right_ops)
+    psi_cols = lax.all_to_all(psi_send, "blk", 0, 0, tiled=True)
+    right = lax.all_to_all(right_send, "op", 0, 0, tiled=True).reshape(terms * cols, cols)
+
+    match = slot_sector[:, None] == jnp.arange(nsec)[None, :]
+    widths = jnp.sum(jnp.where(match, sector_width[None, :], 0), axis=1).astype(jnp.int32)
+    hit = slot_sector[None, None, :] == slot_sector[None, :, None] - shifts[:, None, None]
+    src = jnp.min(jnp.where(hit, jnp.arange(nsec), nsec), axis=2).astype(jnp.int32).reshape(-1)
+    dr = lax.dynamic_slice_in_dim(diag_right, own_op * cols, cols, 0)
+    dmat = diag_left[:, :, None] + dr[None, None, :]
+
+    field_f32 = jax.ShapeDtypeStruct((nsec, rows, cols), f32)
+    field_bf16 = jax.ShapeDtypeStruct((nsec, rows, cols), bf16)
+    dots = jax.ShapeDtypeStruct((n_dev, 8, LANES), f32)
+    gmat = pltpu.VMEM((nsec + 1, rows, terms * cols), bf16)
+    flops = 2 * nsec * rows * cols * terms * (rows + cols)
+
+    sig, raw, dots1 = call(
+        first_body, (field_f32, field_bf16, dots), [gmat], 2, flops, 8 << 20, 4
+    )(src, widths, psi_cols, left, right, dmat)
+    parts1 = lax.all_to_all(dots1, both, 0, 0, tiled=True)
+
+    fld, img, dots2 = call(
+        functools.partial(second_body, count),
+        (field_bf16, field_f32, dots),
+        [gmat, pltpu.VMEM((nsec, rows, cols), f32)],
+        2,
+        flops,
+        8 << 20,
+        6,
+    )(src, widths, parts1, raw, sig, left, right, dmat)
+    parts2 = lax.all_to_all(dots2, both, 0, 0, tiled=True)
+
+    coefs, energy = combine_scalars(parts1, parts2, count, own)
+    pieces = jax.ShapeDtypeStruct((n_op, nsec, rows // n_op, cols), bf16)
+    new_send, res_send = pl.pallas_call(
+        functools.partial(third_body, count, None),
+        out_shape=(pieces, pieces),
+        in_specs=[pl.BlockSpec(memory_space=pltpu.VMEM)] * 6 + [pl.BlockSpec(memory_space=pltpu.SMEM)],
+        out_specs=(pl.BlockSpec(memory_space=pltpu.VMEM),) * 2,
+        compiler_params=pltpu.CompilerParams(vmem_limit_bytes=VMEM_LIMIT),
+    )(parts1, parts2, raw, sig, fld, img, coefs)
+
+    def final(send):
+        got = lax.all_to_all(send, "op", 0, 0, tiled=True)
+        return got.transpose(1, 2, 0, 3).reshape(nsec, rows // n_op, n_op * cols)
+
+    return final(new_send), final(res_send), jnp.reshape(energy, (1,))
 
 
 def solution(mesh):
@@ -106,8 +375,23 @@
         P("grp", None),
         P(("grp", "blk")),
     )
+
+    def body(*args):
+        psi, left_ops, right_ops, diag_right = args[0], args[1], args[2], args[7]
+        n_op = mesh.shape["op"]
+        cols = diag_right.shape[0] // n_op
+        fits = (
+            psi.shape[0] == 1
+            and diag_right.shape[0] % n_op == 0
+            and cols % LANES == 0
+            and cols % right_ops.shape[2] == 0
+            and cols // right_ops.shape[2] * n_op == right_ops.shape[1]
+            and psi.shape[1] % (16 * n_op) == 0
+        )
+        return (per_device if fits else per_device_general)(*args)
+
     return jax.shard_map(
-        per_device,
+        body,
         mesh=mesh,
         in_specs=placed,
         out_specs=(P("grp", "op", "blk"), P("grp", "op", "blk"), P("grp")),

time: 386 us -> 133 us (0.34)
  blocking collectives: 130 us -> 15.5 us
  local copies, waits for them, and re-layouts: 72.9 us -> 11.6 us
  waiting for transfers between devices: 93.8 us -> 48 us
  other arithmetic: 40.2 us -> 5.65 us
  matrix products: 17.2 us -> 0 us
  starting transfers between devices: 8.23 us -> 21.2 us
  Pallas kernels: 0 us -> 9.74 us
    psum x2 -> x0, waiting for transfers between devices: 64.4 us -> none  [op_total(): lax.psum(partial_value.astype(jnp.bfloat16), 'op').astype(jnp.float32)]
    all_to_all x2 -> x1, blocking collectives: 71.1 us -> 8.41 us  [final(): got = lax.all_to_all(send, 'op', 0, 0, tiled=True)]
    psum x5 -> x0, blocking collectives: 58.6 us -> none  [the longest x4 44.6 us: reduce_dots(): sums = lax.psum(values, 'blk')]
    convert_element_type x3 -> x0, local copies, waits for them, and re-layouts: 27 us -> none  [the longest x2 26.8 us: left_local(): return jnp.einsum('ksij,sjc->ksic', left_ops, field, preferred_element_ty...]
    all_gather x0 -> x1, waiting for transfers between devices: none -> 24.7 us  [per_device(): left = lax.all_gather(left_ops[:, 0], both, axis=0, tiled=False)]
    dot_general x6 -> x0, matrix products: 17.2 us -> none  [the longest x2 7.26 us: right_part(): jnp.einsum('ktwrc,krdc->twrd', shifted, right_ops, preferred_element_type...]
    reshape x4 -> x3, local copies, waits for them, and re-layouts: 18.1 us -> 1.55 us  [the longest x2 1.47 us: final(): return got.transpose(1, 2, 0, 3).reshape(nsec, rows // n_op, n_op * cols)]
    all_to_all x2 -> x5, starting transfers between devices: 7.97 us -> 21.1 us  [the longest x1 6.51 us: per_device(): psi_cols = lax.all_to_all(psi_send, 'blk', 0, 0, tiled=True)]
  transfers between devices with their start and end apart: 4 -> 6, of which waited for: 4 -> 5; matrix products, arithmetic and copies ran while one was open for 12% -> 6% of each run, Pallas kernels for 0% -> 1%
where the time goes in v1:
time: 133 us; the launch traced here: 132 us
  waiting for transfers between devices  48 us (36%)
  starting transfers between devices  21.2 us (16%)
  between operations  20.7 us (16%)
  blocking collectives  15.5 us (12%)
  local copies, waits for them, and re-layouts  11.6 us (9%)
  Pallas kernels  9.74 us (7%)
  other arithmetic  5.65 us (4%)
    all_gather x1, waiting for transfers between devices, per_device(): left = lax.all_gather(left_ops[:, 0], both, axis=0, tiled=False)  24.7 us
    unnamed x11, local copies, waits for them, and re-layouts  8.65 us
    all_to_all x1, blocking collectives, final(): got = lax.all_to_all(send, 'op', 0, 0, tiled=True)  8.41 us
    unnamed x1, blocking collectives  7.04 us
    all_to_all x1, waiting for transfers between devices, per_device(): parts1 = lax.all_to_all(dots1, both, 0, 0, tiled=True)  6.85 us
    all_to_all x1, starting transfers between devices, per_device(): psi_cols = lax.all_to_all(psi_send, 'blk', 0, 0, tiled=True)  6.51 us
    all_to_all x1, waiting for transfers between devices, per_device(): psi_cols = lax.all_to_all(psi_send, 'blk', 0, 0, tiled=True)  5.72 us
    all_to_all x1, waiting for transfers between devices, final(): got = lax.all_to_all(send, 'op', 0, 0, tiled=True)  5.27 us
  transfers between devices with their start and end apart: 6, of which 5 were waited for; matrix products, arithmetic and copies ran while one was open for 6% of the time, Pallas kernels for 1%

profile of v1, /device:TPU:0, one launch (start us, length us, event | category | flops | bytes accessed | tf_op | source)
XLA Modules:
  0.0 132.3 jit_solution(3704353345978581725)
XLA Ops:
  7.2 0.0 all-gather.3.cloned.1.call-start
  7.2 0.7 all-gather.3.cloned.1.call-update
  7.9 1.2 dynamic-slice
  9.8 0.9 dynamic-update-slice
  10.7 0.0 copy-start.2
  10.7 1.2 copy-done.2
  11.9 0.0 copy-start.3
  11.9 0.9 copy-done.3
  12.8 0.9 shard_map.103
  13.8 4.2 %all-to-all-start.1 = ((bf16[4,256,128]{2,1,0:T(8,128)(2,1)}), bf16[4,256,128]{2,1,0:T(8,128)(2,1)S(1)}, u32[]{:S(2)}, u32[]{:S(2)}) async-start(bf16[4,256,128]{2,1,0:T(8,128)(2,1)} %get-tuple-element.14), calls=%async_computation.1 | async-start | bytes 524288 | tf_op jit(solution)/shard_map/all_to_all | solution.py:319
  18.0 7.0 %all-reduce = s32[8]{0:T(128)S(1)} all-reduce(s32[8]{0:T(128)S(1)} %dynamic-update-slice), channel_id=1, replica_groups=mesh['grp'=2,'blk'=4,'op'=4] {'op'}, use_global_device_ids=true, to_apply=%add | all-reduce | flops 8 | bytes 64
  25.0 0.7 broadcast_subtract_fusion
  25.7 0.0 all-to-all-done.1
  25.7 6.5 %all-to-all-start = ((bf16[4,256,128]{2,1,0:T(8,128)(2,1)}), bf16[4,256,128]{2,1,0:T(8,128)(2,1)S(1)}, u32[]{:S(2)}, u32[]{:S(2)}) async-start(bf16[4,256,128]{2,1,0:T(8,128)(2,1)} %get-tuple-element.13), calls=%async_computation | async-start | bytes 524288 | tf_op jit(solution)/shard_map/all_to_all | solution.py:318
  32.2 0.7 select_reduce_fusion
  33.0 0.1 copy.15
  33.1 0.1 reshape.62.src
  33.1 0.8 dynamic_slice.3
  33.9 0.9 select_reduce_fusion.1.widths
  34.8 0.9 broadcast_add_fusion.dmat
  35.6 5.7 %all-to-all-done.psi = bf16[4,256,128]{2,1,0:T(8,128)(2,1)S(1)} async-done(((bf16[4,256,128]{2,1,0:T(8,128)(2,1)}), bf16[4,256,128]{2,1,0:T(8,128)(2,1)S(1)}, u32[]{:S(2)}, u32[]{:S(2)}) %all-to-all-start) | async-done | bytes 262176 | tf_op jit(solution)/shard_map/all_to_all | solution.py:318
  41.4 24.7 %all-gather.3.cloned.1.call-done = bf16[32,1,256,256]{3,2,1,0:T(8,128)(2,1)} async-done(((bf16[2,1,256,256]{3,2,1,0:T(8,128)(2,1)}), bf16[32,1,256,256]{3,2,1,0:T(8,128)(2,1)}) %all-gather.3.cloned.1.call-update) | async-done | bytes 4194320 | tf_op jit(solution)/shard_map/all_gather | solution.py:305
  66.0 0.0 copy-start
  66.0 2.2 %copy-done = bf16[32,1,256,256]{3,2,1,0:T(8,128)(2,1)S(1)} copy-done((bf16[32,1,256,256]{3,2,1,0:T(8,128)(2,1)S(1)}, bf16[32,1,256,256]{3,2,1,0:T(8,128)(2,1)}, u32[]{:S(2)}) %copy-start) | copy-done | bytes 4194328
  68.2 3.3 %shard_map.104 = (f32[4,256,128]{2,1,0:T(8,128)S(1)}, bf16[4,256,128]{2,1,0:T(8,128)(2,1)S(1)}, f32[16,8,128]{2,1,0:T(8,128)}) custom-call(s32[32]{0:T(128)S(1)} %reshape.62.src, s32[4]{0:T(128)S(1)} %select_reduce_fusion.1.widths, bf16[4,256,128]{2,1,0:T(8,128)(2,1)S(1)} %all-to-all-done.psi, bf16[16,2,256,256]{3,2,1,0:T(8,128)(2,1)S(1)} %bitcast.22, ...), custom_call_target="tpu_custom_call" | custom-call | flops 805306368 | bytes 8388608 | tf_op jit(solution)/shard_map/pallas_call | solution.py:334
  71.5 3.5 %all-to-all-start.2 = ((f32[16,8,128]{2,1,0:T(8,128)}), f32[16,8,128]{2,1,0:T(8,128)S(1)}, u32[]{:S(2)}, u32[]{:S(2)}) async-start(f32[16,8,128]{2,1,0:T(8,128)} %get-tuple-element.15), calls=%async_computation.2 | async-start | bytes 131072 | tf_op jit(solution)/shard_map/all_to_all | solution.py:337
  75.0 6.8 %all-to-all-done.2.parts.parts1 = f32[16,8,128]{2,1,0:T(8,128)S(1)} async-done(((f32[16,8,128]{2,1,0:T(8,128)}), f32[16,8,128]{2,1,0:T(8,128)S(1)}, u32[]{:S(2)}, u32[]{:S(2)}) %all-to-all-start.2) | async-done | bytes 65568 | tf_op jit(solution)/shard_map/all_to_all | solution.py:337
  81.9 0.0 copy-start.1
  81.9 2.2 %copy-done.1 = bf16[32,1,256,256]{3,2,1,0:T(8,128)(2,1)S(1)} copy-done((bf16[32,1,256,256]{3,2,1,0:T(8,128)(2,1)S(1)}, bf16[32,1,256,256]{3,2,1,0:T(8,128)(2,1)}, u32[]{:S(2)}) %copy-start.1) | copy-done | bytes 4194328
  84.1 3.9 %shard_map.105 = (bf16[4,256,128]{2,1,0:T(8,128)(2,1)S(1)}, f32[4,256,128]{2,1,0:T(8,128)S(1)}, f32[16,8,128]{2,1,0:T(8,128)}) custom-call(s32[32]{0:T(128)S(1)} %reshape.62.src, s32[4]{0:T(128)S(1)} %select_reduce_fusion.1.widths, f32[16,8,128]{2,1,0:T(8,128)S(1)} %all-to-all-done.2.parts.parts1, bf16[4,256,128]{2,1,0:T(8,128)(2,1)S(1)} %get-tuple-element.16.raw_in, ...), custom_call_target="tpu_custom_call" | custom-call | flops 805306368 | bytes 8388608 | tf_op jit(solution)/shard_map/pallas_call | solution.py:339
  88.0 3.5 %all-to-all-start.3 = ((f32[16,8,128]{2,1,0:T(8,128)}), f32[16,8,128]{2,1,0:T(8,128)S(1)}, u32[]{:S(2)}, u32[]{:S(2)}) async-start(f32[16,8,128]{2,1,0:T(8,128)} %get-tuple-element.18), calls=%async_computation.3 | async-start | bytes 131072 | tf_op jit(solution)/shard_map/all_to_all | solution.py:348
  91.5 0.1 slice_reduce_fusion
  91.6 0.6 fusion.2
  93.6 4.8 %all-to-all-done.3.parts2 = f32[16,8,128]{2,1,0:T(8,128)S(1)} async-done(((f32[16,8,128]{2,1,0:T(8,128)}), f32[16,8,128]{2,1,0:T(8,128)S(1)}, u32[]{:S(2)}, u32[]{:S(2)}) %all-to-all-start.3) | async-done | bytes 65568 | tf_op jit(solution)/shard_map/all_to_all | solution.py:348
  98.3 0.8 slice_reduce_fusion.4
  99.8 0.7 add_reduce_fusion.1
  103.4 0.8 pad_maximum_fusion.coefs
  104.1 1.7 %shard_map.106 = (bf16[4,4,64,128]{3,2,1,0:T(8,128)(2,1)S(1)}, bf16[4,4,64,128]{3,2,1,0:T(8,128)(2,1)}) custom-call(f32[16,8,128]{2,1,0:T(8,128)S(1)} %all-to-all-done.2.parts.parts1, f32[16,8,128]{2,1,0:T(8,128)S(1)} %all-to-all-done.3.parts2, bf16[4,256,128]{2,1,0:T(8,128)(2,1)S(1)} %get-tuple-element.16.raw_in, ...), custom_call_target="tpu_custom_call" | custom-call | tf_op jit(solution)/shard_map/pallas_call | solution.py:352
  105.8 8.4 %all_to_all.30 = bf16[4,4,64,128]{3,2,1,0:T(8,128)(2,1)S(1)} all-to-all(bf16[4,4,64,128]{3,2,1,0:T(8,128)(2,1)S(1)} %get-tuple-element.21), channel_id=1, replica_groups=mesh['grp'=2,'blk'=4,'op'=4] {'op'}, dimensions={0} | all-to-all | bytes 524288 | tf_op jit(solution)/shard_map/all_to_all | solution.py:361
  114.2 3.4 %all-to-all-start.5 = ((bf16[4,4,64,128]{3,2,1,0:T(8,128)(2,1)}), bf16[4,4,64,128]{3,2,1,0:T(8,128)(2,1)S(1)}, u32[]{:S(2)}, u32[]{:S(2)}) async-start(bf16[4,4,64,128]{3,2,1,0:T(8,128)(2,1)} %get-tuple-element.22), calls=%async_computation.5 | async-start | bytes 524288 | tf_op jit(solution)/shard_map/all_to_all | solution.py:361
  117.6 0.7 copy_bitcast_fusion.1
  118.4 5.3 %all-to-all-done.5 = bf16[4,4,64,128]{3,2,1,0:T(8,128)(2,1)S(1)} async-done(((bf16[4,4,64,128]{3,2,1,0:T(8,128)(2,1)}), bf16[4,4,64,128]{3,2,1,0:T(8,128)(2,1)S(1)}, u32[]{:S(2)}, u32[]{:S(2)}) %all-to-all-start.5) | async-done | bytes 262176 | tf_op jit(solution)/shard_map/all_to_all | solution.py:361
  123.6 0.7 copy_bitcast_fusion
  (2 shorter events, 0.0 us)
Async XLA Ops:
  7.2 58.9 %all-gather.3.cloned.1.call-start = ((), (), s32[]{:S(2)}) async-start(), calls=%async_computation.6 | async-start | bytes 4456448 | tf_op jit(solution)/shard_map/all_gather | solution.py:305
  10.7 1.2 copy-start.2
  11.9 0.9 copy-start.3
  13.8 12.0 %all-to-all-start.1 = ((bf16[4,256,128]{2,1,0:T(8,128)(2,1)}), bf16[4,256,128]{2,1,0:T(8,128)(2,1)S(1)}, u32[]{:S(2)}, u32[]{:S(2)}) async-start(bf16[4,256,128]{2,1,0:T(8,128)(2,1)} %get-tuple-element.14), calls=%async_computation.1 | async-start | bytes 524288 | tf_op jit(solution)/shard_map/all_to_all | solution.py:319
  25.7 15.6 %all-to-all-start = ((bf16[4,256,128]{2,1,0:T(8,128)(2,1)}), bf16[4,256,128]{2,1,0:T(8,128)(2,1)S(1)}, u32[]{:S(2)}, u32[]{:S(2)}) async-start(bf16[4,256,128]{2,1,0:T(8,128)(2,1)} %get-tuple-element.13), calls=%async_computation | async-start | bytes 524288 | tf_op jit(solution)/shard_map/all_to_all | solution.py:318
  66.0 2.2 %copy-start = (bf16[32,1,256,256]{3,2,1,0:T(8,128)(2,1)S(1)}, bf16[32,1,256,256]{3,2,1,0:T(8,128)(2,1)}, u32[]{:S(2)}) copy-start(bf16[32,1,256,256]{3,2,1,0:T(8,128)(2,1)} %all-gather.3.cloned.1.call-done) | copy-start | bytes 12582916
  71.5 10.4 %all-to-all-start.2 = ((f32[16,8,128]{2,1,0:T(8,128)}), f32[16,8,128]{2,1,0:T(8,128)S(1)}, u32[]{:S(2)}, u32[]{:S(2)}) async-start(f32[16,8,128]{2,1,0:T(8,128)} %get-tuple-element.15), calls=%async_computation.2 | async-start | bytes 131072 | tf_op jit(solution)/shard_map/all_to_all | solution.py:337
  81.9 2.2 %copy-start.1 = (bf16[32,1,256,256]{3,2,1,0:T(8,128)(2,1)S(1)}, bf16[32,1,256,256]{3,2,1,0:T(8,128)(2,1)}, u32[]{:S(2)}) copy-start(bf16[32,1,256,256]{3,2,1,0:T(8,128)(2,1)} %all-gather.3.cloned.1.call-done) | copy-start | bytes 12582916
  88.0 10.4 %all-to-all-start.3 = ((f32[16,8,128]{2,1,0:T(8,128)}), f32[16,8,128]{2,1,0:T(8,128)S(1)}, u32[]{:S(2)}, u32[]{:S(2)}) async-start(f32[16,8,128]{2,1,0:T(8,128)} %get-tuple-element.18), calls=%async_computation.3 | async-start | bytes 131072 | tf_op jit(solution)/shard_map/all_to_all | solution.py:348
  114.2 9.4 %all-to-all-start.5 = ((bf16[4,4,64,128]{3,2,1,0:T(8,128)(2,1)}), bf16[4,4,64,128]{3,2,1,0:T(8,128)(2,1)S(1)}, u32[]{:S(2)}, u32[]{:S(2)}) async-start(bf16[4,4,64,128]{3,2,1,0:T(8,128)(2,1)} %get-tuple-element.22), calls=%async_computation.5 | async-start | bytes 524288 | tf_op jit(solution)/shard_map/all_to_all | solution.py:361
Sparse Core Ops, SparseCore 0:
  10.2 55.8 all-gather.2

commit v2 on v1

--- a/solution.py
+++ b/solution.py
@@ -106,11 +106,12 @@
     return coef_v, coef_u, energy
 
 
-def call(body, out_shape, scratch=(), scalars=0, flops=0, nbytes=0, n_in=0):
+def call(body, out_shape, scratch=(), scalars=0, flops=0, nbytes=0, n_in=0, n_any=0):
     return pl.pallas_call(
         body,
         out_shape=out_shape,
         in_specs=[pl.BlockSpec(memory_space=pltpu.SMEM)] * scalars
+        + [pl.BlockSpec(memory_space=pl.ANY)] * n_any
         + [pl.BlockSpec(memory_space=pltpu.VMEM)] * n_in,
         out_specs=jax.tree.map(lambda _: pl.BlockSpec(memory_space=pltpu.VMEM), out_shape),
         scratch_shapes=list(scratch),
@@ -136,7 +137,7 @@
                 right_out[d, row : row + width, r * width : (r + 1) * width] = right[k, d * per + r]
 
 
-def apply_h(src, field, left, right, gmat, emit):
+def apply_h(src, field, left, right, gmat, emit, ready=None):
     nsec = len(field)
     cols = field[0].shape[1]
     n_dev, terms_dev = left.shape[0], left.shape[1]
@@ -148,6 +149,8 @@
         )
         gmat[s] = prod.astype(jnp.bfloat16)
     gmat[nsec] = jnp.zeros_like(gmat[nsec])
+    if ready is not None:
+        ready()
     for t in range(nsec):
         total = None
         for k in range(terms):
@@ -174,8 +177,21 @@
     return jnp.sum(jnp.sum(x, axis=0, keepdims=True), axis=1, keepdims=True)
 
 
-def first_body(src, widths, psi, left, right, dmat, sig_out, raw_out, dots_out, gmat):
+def first_body(place, src, widths, *refs):
+    pieces, refs = refs[: place.shape[0]], refs[place.shape[0] :]
+    psi, right, dmat, sig_out, raw_out, dots_out, left, gmat, sems = refs
     nsec = psi.shape[0]
+    copies = [
+        pltpu.make_async_copy(piece, left.at[place[j]], sems.at[j])
+        for j, piece in enumerate(pieces)
+    ]
+    for copy in copies:
+        copy.start()
+
+    def ready():
+        for copy in copies:
+            copy.wait()
+
     field = []
     for t in range(nsec):
         block = psi[t]
@@ -191,7 +207,7 @@
         sums[0] = sums[0] + fold(raw * raw)
         sums[1] = sums[1] + fold(raw * sigma)
 
-    apply_h(src, field, left, right, gmat, emit)
+    apply_h(src, field, left, right, gmat, emit, ready)
     tile = spread([whole(x) for x in sums], dots_out.shape[1:])
     for d in range(dots_out.shape[0]):
         dots_out[d] = tile
@@ -286,6 +302,21 @@
     return jnp.stack([cv, cu * unit, energy, own_beta]), energy
 
 
+def gather_pieces(own, n_blk, n_op):
+    pieces, held = [own], [(0, 0)]
+    for d in sorted(range(1, n_blk), key=lambda d: min(d, n_blk - d)):
+        pairs = [(i, (i + d) % n_blk) for i in range(n_blk)]
+        pieces.append(lax.ppermute(own, "blk", pairs))
+        held.append((d, 0))
+    bit = n_op // 2
+    while bit:
+        pairs = [(i, i ^ bit) for i in range(n_op)]
+        pieces += [lax.ppermute(piece, "op", pairs) for piece in pieces]
+        held += [(d, e ^ bit) for d, e in held]
+        bit //= 2
+    return pieces, held
+
+
 def per_device(
     psi, left_ops, right_ops, term_shift, slot_sector, sector_width, diag_left, diag_right
 ):
@@ -302,7 +333,9 @@
     own = lax.axis_index("blk") * n_op + own_op
     bf16, f32 = jnp.bfloat16, jnp.float32
 
-    left = lax.all_gather(left_ops[:, 0], both, axis=0, tiled=False)
+    pieces, held = gather_pieces(left_ops[:, 0], n_blk, n_op)
+    own_blk = lax.axis_index("blk")
+    place = jnp.stack([lax.rem(own_blk - d + n_blk, n_blk) * n_op + (own_op ^ e) for d, e in held])
     shifts = lax.all_gather(term_shift, "op", axis=0, tiled=True)
 
     psi_send, right_send = call(
@@ -331,9 +364,17 @@
     gmat = pltpu.VMEM((nsec + 1, rows, terms * cols), bf16)
     flops = 2 * nsec * rows * cols * terms * (rows + cols)
 
-    sig, raw, dots1 = call(
-        first_body, (field_f32, field_bf16, dots), [gmat], 2, flops, 8 << 20, 4
-    )(src, widths, psi_cols, left, right, dmat)
+    left_all = jax.ShapeDtypeStruct((n_dev, terms_dev, rows, rows), bf16)
+    sig, raw, dots1, left = call(
+        first_body,
+        (field_f32, field_bf16, dots, left_all),
+        [gmat, pltpu.SemaphoreType.DMA((n_dev,))],
+        3,
+        flops,
+        8 << 20,
+        3,
+        n_dev,
+    )(place, src, widths, *pieces, psi_cols, right, dmat)
     parts1 = lax.all_to_all(dots1, both, 0, 0, tiled=True)
 
     fld, img, dots2 = call(
@@ -387,6 +428,7 @@
             and cols % right_ops.shape[2] == 0
             and cols // right_ops.shape[2] * n_op == right_ops.shape[1]
             and psi.shape[1] % (16 * n_op) == 0
+            and n_op & (n_op - 1) == 0
         )
         return (per_device if fits else per_device_general)(*args)
 

time: 133 us -> 115 us (0.86)
  waiting for transfers between devices: 48 us -> 24.2 us
  between operations: 20.7 us -> 7.45 us
  starting transfers between devices: 21.2 us -> 33.4 us
  local copies, waits for them, and re-layouts: 11.6 us -> 17.6 us
    all_gather x1 -> x0, waiting for transfers between devices: 24.7 us -> none  [per_device(): left = lax.all_gather(left_ops[:, 0], both, axis=0, tiled=False)]
    ppermute x0 -> x15, starting transfers between devices: none -> 12.1 us  [the longest x3 6.13 us: gather_pieces(): pieces.append(lax.ppermute(own, 'blk', pairs))]
    ppermute x0 -> x15, waiting for transfers between devices: none -> 7.28 us  [the longest x12 7.27 us: gather_pieces(): pieces += [lax.ppermute(piece, 'op', pairs) for piece in pieces]]
    unnamed x11 -> x29, local copies, waits for them, and re-layouts: 8.65 us -> 14.5 us
    all_to_all x1, waiting for transfers between devices: 5.72 us -> 0.01 us  [per_device(): psi_cols = lax.all_to_all(psi_send, 'blk', 0, 0, tiled=True)]
    all_to_all x1, starting transfers between devices: 3.5 us -> 4.96 us  [per_device(): parts1 = lax.all_to_all(dots1, both, 0, 0, tiled=True)]
  transfers between devices with their start and end apart: 6 -> 20, of which waited for: 5 -> 5; matrix products, arithmetic and copies ran while one was open for 6% -> 7% of each run, Pallas kernels for 1% -> 1%
where the time goes in v2:
time: 115 us; the launch traced here: 114 us
  starting transfers between devices  33.4 us (29%)
  waiting for transfers between devices  24.2 us (21%)
  local copies, waits for them, and re-layouts  17.6 us (15%)
  blocking collectives  14.5 us (13%)
  Pallas kernels  11 us (10%)
  between operations  7.45 us (6%)
  other arithmetic  5.65 us (5%)
    unnamed x29, local copies, waits for them, and re-layouts  14.5 us
    all_to_all x1, blocking collectives, final(): got = lax.all_to_all(send, 'op', 0, 0, tiled=True)  8.41 us
    ppermute x12, waiting for transfers between devices, gather_pieces(): pieces += [lax.ppermute(piece, 'op', pairs) for piece in pieces]  7.27 us
    all_to_all x1, waiting for transfers between devices, per_device(): parts1 = lax.all_to_all(dots1, both, 0, 0, tiled=True)  6.89 us
    ppermute x3, starting transfers between devices, gather_pieces(): pieces.append(lax.ppermute(own, 'blk', pairs))  6.13 us
    unnamed x1, blocking collectives  6.1 us
    all_to_all x1, starting transfers between devices, per_device(): psi_cols = lax.all_to_all(psi_send, 'blk', 0, 0, tiled=True)  6.03 us
    ppermute x12, starting transfers between devices, gather_pieces(): pieces += [lax.ppermute(piece, 'op', pairs) for piece in pieces]  5.98 us
  transfers between devices with their start and end apart: 20, of which 5 were waited for; matrix products, arithmetic and copies ran while one was open for 7% of the time, Pallas kernels for 1%

profile of v2, /device:TPU:0, one launch (start us, length us, event | category | flops | bytes accessed | tf_op | source)
XLA Modules:
  0.0 113.9 jit_solution(6360627945032608937)
XLA Ops:
  0.6 4.1 %collective-permute-start.2 = (bf16[2,256,256]{2,1,0:T(8,128)(2,1)}, bf16[2,256,256]{2,1,0:T(8,128)(2,1)S(1)}, u32[]{:S(2)}, u32[]{:S(2)}) collective-permute-start(bf16[2,256,256]{2,1,0:T(8,128)(2,1)} %bitcast.40), channel_id=1, source_target_pairs={{0,8},{4,12},{8,0},{12,4},{1,9},{5,13},{9,1},{13,5},{2,10},{6,14},... | collective-permute-start | bytes 786440 | tf_op jit(solution)/shard_map/ppermute | solution.py:309
  4.7 0.0 collective-permute-start.7
  4.7 1.5 %collective-permute-start.3 = (bf16[2,256,256]{2,1,0:T(8,128)(2,1)}, bf16[2,256,256]{2,1,0:T(8,128)(2,1)S(1)}, u32[]{:S(2)}, u32[]{:S(2)}) collective-permute-start(bf16[2,256,256]{2,1,0:T(8,128)(2,1)} %bitcast.42), channel_id=1, source_target_pairs={{0,2},{1,3},{2,0},{3,1},{4,6},{5,7},{6,4},{7,5},{8,10},{9,11},{10,... | collective-permute-start | bytes 786440 | tf_op jit(solution)/shard_map/ppermute | solution.py:314
  6.2 1.3 %collective-permute-start.1 = (bf16[2,256,256]{2,1,0:T(8,128)(2,1)}, bf16[2,256,256]{2,1,0:T(8,128)(2,1)S(1)}, u32[]{:S(2)}, u32[]{:S(2)}) collective-permute-start(bf16[2,256,256]{2,1,0:T(8,128)(2,1)} %bitcast.43), channel_id=1, source_target_pairs={{0,12},{4,0},{8,4},{12,8},{1,13},{5,1},{9,5},{13,9},{2,14},{6,2},{... | collective-permute-start | bytes 786440 | tf_op jit(solution)/shard_map/ppermute | solution.py:309
  7.6 0.7 collective-permute-start
  8.3 1.2 %dynamic-slice = u32[1]{0:T(128)} dynamic-slice(u32[32]{0:T(128)} %constant.75, u32[]{:T(128)S(6)} %add.177), dynamic_slice_sizes={1} | dynamic-slice | bytes 12
  10.2 0.9 dynamic-update-slice
  11.0 1.2 %copy-done.2 = bf16[1,256,2048]{2,1,0:T(8,128)(2,1)S(1)} copy-done((bf16[1,256,2048]{2,1,0:T(8,128)(2,1)S(1)}, bf16[1,256,2048]{2,1,0:T(8,128)(2,1)}, u32[]{:S(2)}) %copy-start.2) | copy-done | bytes 1048600
  12.2 0.9 copy-done.3
  13.2 0.9 shard_map.103
  14.1 3.4 %all-to-all-start.1 = ((bf16[4,256,128]{2,1,0:T(8,128)(2,1)}), bf16[4,256,128]{2,1,0:T(8,128)(2,1)S(1)}, u32[]{:S(2)}, u32[]{:S(2)}) async-start(bf16[4,256,128]{2,1,0:T(8,128)(2,1)} %get-tuple-element.15), calls=%async_computation.1 | async-start | bytes 524288 | tf_op jit(solution)/shard_map/all_to_all | solution.py:352
  17.5 6.1 %all-reduce = s32[8]{0:T(128)S(1)} all-reduce(s32[8]{0:T(128)S(1)} %dynamic-update-slice), channel_id=1, replica_groups=mesh['grp'=2,'blk'=4,'op'=4] {'op'}, use_global_device_ids=true, to_apply=%add | all-reduce | flops 8 | bytes 64
  23.6 0.0 collective-permute-done.2.refs_3_
  23.6 0.0 collective-permute-start.10
  23.6 0.0 collective-permute-done.7.refs_8_
  23.6 1.6 %collective-permute-start.6 = (bf16[2,256,256]{2,1,0:T(8,128)(2,1)S(1)}, bf16[2,256,256]{2,1,0:T(8,128)(2,1)S(1)}, u32[]{:S(2)}, u32[]{:S(2)}) collective-permute-start(bf16[2,256,256]{2,1,0:T(8,128)(2,1)S(1)} %collective-permute-done.2.refs_3_), channel_id=1, source_target_pairs={{0,2},{1,3},{2,0},{3,1},{4,6},{5,7},{6,4},{7,5},{8,10},{9,11},{10,... | collective-permute-start | bytes 786440 | tf_op jit(solution)/shard_map/ppermute | solution.py:314
  25.3 0.0 collective-permute-done.3.refs_4_
  25.3 0.2 collective-permute-start.11
  25.5 0.4 collective-permute-start.5
  25.9 0.0 collective-permute-done.refs_1_
  25.9 1.6 %collective-permute-start.4 = (bf16[2,256,256]{2,1,0:T(8,128)(2,1)S(1)}, bf16[2,256,256]{2,1,0:T(8,128)(2,1)S(1)}, u32[]{:S(2)}, u32[]{:S(2)}) collective-permute-start(bf16[2,256,256]{2,1,0:T(8,128)(2,1)S(1)} %collective-permute-done.refs_1_), channel_id=1, source_target_pairs={{0,2},{1,3},{2,0},{3,1},{4,6},{5,7},{6,4},{7,5},{8,10},{9,11},{10,... | collective-permute-start | bytes 786440 | tf_op jit(solution)/shard_map/ppermute | solution.py:314
  27.5 0.7 broadcast_subtract_fusion
  28.2 0.0 all-to-all-done.1
  28.2 6.0 %all-to-all-start = ((bf16[4,256,128]{2,1,0:T(8,128)(2,1)}), bf16[4,256,128]{2,1,0:T(8,128)(2,1)S(1)}, u32[]{:S(2)}, u32[]{:S(2)}) async-start(bf16[4,256,128]{2,1,0:T(8,128)(2,1)} %get-tuple-element.14), calls=%async_computation | async-start | bytes 524288 | tf_op jit(solution)/shard_map/all_to_all | solution.py:351
  34.3 0.7 select_reduce_fusion
  35.0 0.7 copy-done.7
  35.7 0.0 collective-permute-start.9
  35.7 0.5 collective-permute-start.8
  36.2 0.1 collective-permute-start.14
  36.3 2.1 %collective-permute-done.5.refs_6_ = bf16[2,256,256]{2,1,0:T(8,128)(2,1)S(1)} collective-permute-done((bf16[2,256,256]{2,1,0:T(8,128)(2,1)S(1)}, bf16[2,256,256]{2,1,0:T(8,128)(2,1)S(1)}, u32[]{:S(2)}, u32[]{:S(2)}) %collective-permute-start.5) | collective-permute-done | bytes 262176 | tf_op jit(solution)/shard_map/ppermute | solution.py:314
  38.4 0.0 collective-permute-start.13
  38.4 5.2 %collective-permute-done.4.refs_5_ = bf16[2,256,256]{2,1,0:T(8,128)(2,1)S(1)} collective-permute-done((bf16[2,256,256]{2,1,0:T(8,128)(2,1)S(1)}, bf16[2,256,256]{2,1,0:T(8,128)(2,1)S(1)}, u32[]{:S(2)}, u32[]{:S(2)}) %collective-permute-start.4) | collective-permute-done | bytes 262176 | tf_op jit(solution)/shard_map/ppermute | solution.py:314
  43.6 0.7 copy-done.11
  44.3 0.9 select_reduce_fusion.1.widths
  45.2 0.1 copy.13
  45.2 0.1 reshape.62.src
  45.3 0.8 dynamic_slice.3
  46.1 0.1 stack.82.place
  46.2 0.9 broadcast_add_fusion.refs_18_.dmat
  47.1 0.0 copy-start.4
  47.2 0.9 copy-done.4
  48.1 0.9 copy-done.6
  49.0 0.9 copy-done.8
  50.0 0.9 copy-done.10
  50.9 0.9 copy-done.12
  51.9 4.6 %shard_map.104 = (f32[4,256,128]{2,1,0:T(8,128)S(1)}, bf16[4,256,128]{2,1,0:T(8,128)(2,1)S(1)}, f32[16,8,128]{2,1,0:T(8,128)}, bf16[16,2,256,256]{3,2,1,0:T(8,128)(2,1)S(1)}) custom-call(s32[16]{0:T(128)S(1)} %stack.82.place, s32[32]{0:T(128)S(1)} %reshape.62.src, s32[4]{0:T(128)S(1)} %select_reduce_fusion.1.widths, bf16[2,256,256]{2,1,0:T(8,128)(2,1)S(1)} %bitcast.45, ...), custom_call_target="tpu_custom_call" | custom-call | flops 805306368 | bytes 8388608 | tf_op jit(solution)/shard_map/pallas_call | solution.py:368
  56.5 1.9 %copy-done = bf16[16,2,256,256]{3,2,1,0:T(8,128)(2,1)} copy-done((bf16[16,2,256,256]{3,2,1,0:T(8,128)(2,1)}, bf16[16,2,256,256]{3,2,1,0:T(8,128)(2,1)S(1)}, u32[]{:S(2)}) %copy-start) | copy-done | bytes 4194328
  58.4 5.0 %all-to-all-start.2 = ((f32[16,8,128]{2,1,0:T(8,128)}), f32[16,8,128]{2,1,0:T(8,128)S(1)}, u32[]{:S(2)}, u32[]{:S(2)}) async-start(f32[16,8,128]{2,1,0:T(8,128)} %get-tuple-element.16), calls=%async_computation.2 | async-start | bytes 131072 | tf_op jit(solution)/shard_map/all_to_all | solution.py:378
  63.4 6.9 %all-to-all-done.2.parts.parts1 = f32[16,8,128]{2,1,0:T(8,128)S(1)} async-done(((f32[16,8,128]{2,1,0:T(8,128)}), f32[16,8,128]{2,1,0:T(8,128)S(1)}, u32[]{:S(2)}, u32[]{:S(2)}) %all-to-all-start.2) | async-done | bytes 65568 | tf_op jit(solution)/shard_map/all_to_all | solution.py:378
  70.3 2.2 %copy-done.1 = bf16[16,2,256,256]{3,2,1,0:T(8,128)(2,1)S(1)} copy-done((bf16[16,2,256,256]{3,2,1,0:T(8,128)(2,1)S(1)}, bf16[16,2,256,256]{3,2,1,0:T(8,128)(2,1)}, u32[]{:S(2)}) %copy-start.1) | copy-done | bytes 4194328
  72.4 3.9 %shard_map.105 = (bf16[4,256,128]{2,1,0:T(8,128)(2,1)S(1)}, f32[4,256,128]{2,1,0:T(8,128)S(1)}, f32[16,8,128]{2,1,0:T(8,128)}) custom-call(s32[32]{0:T(128)S(1)} %reshape.62.src, s32[4]{0:T(128)S(1)} %select_reduce_fusion.1.widths, f32[16,8,128]{2,1,0:T(8,128)S(1)} %all-to-all-done.2.parts.parts1, bf16[4,256,128]{2,1,0:T(8,128)(2,1)S(1)} %get-tuple-element.17.raw_in, ...), custom_call_target="tpu_custom_call" | custom-call | flops 805306368 | bytes 8388608 | tf_op jit(solution)/shard_map/pallas_call | solution.py:380
  76.3 3.5 %all-to-all-start.3 = ((f32[16,8,128]{2,1,0:T(8,128)}), f32[16,8,128]{2,1,0:T(8,128)S(1)}, u32[]{:S(2)}, u32[]{:S(2)}) async-start(f32[16,8,128]{2,1,0:T(8,128)} %get-tuple-element.20), calls=%async_computation.3 | async-start | bytes 131072 | tf_op jit(solution)/shard_map/all_to_all | solution.py:389
  79.9 0.1 slice_reduce_fusion
  80.0 0.6 fusion.2
  81.9 4.8 %all-to-all-done.3.parts2 = f32[16,8,128]{2,1,0:T(8,128)S(1)} async-done(((f32[16,8,128]{2,1,0:T(8,128)}), f32[16,8,128]{2,1,0:T(8,128)S(1)}, u32[]{:S(2)}, u32[]{:S(2)}) %all-to-all-start.3) | async-done | bytes 65568 | tf_op jit(solution)/shard_map/all_to_all | solution.py:389
  86.7 0.8 slice_reduce_fusion.4
  88.2 0.7 add_reduce_fusion.1
  91.7 0.8 pad_maximum_fusion.coefs
  92.5 1.7 %shard_map.106 = (bf16[4,4,64,128]{3,2,1,0:T(8,128)(2,1)S(1)}, bf16[4,4,64,128]{3,2,1,0:T(8,128)(2,1)}) custom-call(f32[16,8,128]{2,1,0:T(8,128)S(1)} %all-to-all-done.2.parts.parts1, f32[16,8,128]{2,1,0:T(8,128)S(1)} %all-to-all-done.3.parts2, bf16[4,256,128]{2,1,0:T(8,128)(2,1)S(1)} %get-tuple-element.17.raw_in, ...), custom_call_target="tpu_custom_call" | custom-call | tf_op jit(solution)/shard_map/pallas_call | solution.py:393
  94.2 8.4 %all_to_all.30 = bf16[4,4,64,128]{3,2,1,0:T(8,128)(2,1)S(1)} all-to-all(bf16[4,4,64,128]{3,2,1,0:T(8,128)(2,1)S(1)} %get-tuple-element.23), channel_id=1, replica_groups=mesh['grp'=2,'blk'=4,'op'=4] {'op'}, dimensions={0} | all-to-all | bytes 524288 | tf_op jit(solution)/shard_map/all_to_all | solution.py:402
  102.6 3.4 %all-to-all-start.5 = ((bf16[4,4,64,128]{3,2,1,0:T(8,128)(2,1)}), bf16[4,4,64,128]{3,2,1,0:T(8,128)(2,1)S(1)}, u32[]{:S(2)}, u32[]{:S(2)}) async-start(bf16[4,4,64,128]{3,2,1,0:T(8,128)(2,1)} %get-tuple-element.24), calls=%async_computation.5 | async-start | bytes 524288 | tf_op jit(solution)/shard_map/all_to_all | solution.py:402
  106.0 0.7 copy_bitcast_fusion.1
  106.7 5.3 %all-to-all-done.5 = bf16[4,4,64,128]{3,2,1,0:T(8,128)(2,1)S(1)} async-done(((bf16[4,4,64,128]{3,2,1,0:T(8,128)(2,1)}), bf16[4,4,64,128]{3,2,1,0:T(8,128)(2,1)S(1)}, u32[]{:S(2)}, u32[]{:S(2)}) %all-to-all-start.5) | async-done | bytes 262176 | tf_op jit(solution)/shard_map/all_to_all | solution.py:402
  112.0 0.7 copy_bitcast_fusion
  (27 shorter events, 0.1 us)
Async XLA Ops:
  0.6 23.0 %collective-permute-start.2 = (bf16[2,256,256]{2,1,0:T(8,128)(2,1)}, bf16[2,256,256]{2,1,0:T(8,128)(2,1)S(1)}, u32[]{:S(2)}, u32[]{:S(2)}) collective-permute-start(bf16[2,256,256]{2,1,0:T(8,128)(2,1)} %bitcast.40), channel_id=1, source_target_pairs={{0,8},{4,12},{8,0},{12,4},{1,9},{5,13},{9,1},{13,5},{2,10},{6,14},... | collective-permute-start | bytes 786440 | tf_op jit(solution)/shard_map/ppermute | solution.py:309
  4.7 18.9 %collective-permute-start.7 = (bf16[2,256,256]{2,1,0:T(8,128)(2,1)}, bf16[2,256,256]{2,1,0:T(8,128)(2,1)S(1)}, u32[]{:S(2)}, u32[]{:S(2)}) collective-permute-start(bf16[2,256,256]{2,1,0:T(8,128)(2,1)} %bitcast.41), channel_id=1, source_target_pairs={{0,1},{1,0},{2,3},{3,2},{4,5},{5,4},{6,7},{7,6},{8,9},{9,8},{10,11... | collective-permute-start | bytes 786440 | tf_op jit(solution)/shard_map/ppermute | solution.py:314
  4.7 20.5 %collective-permute-start.3 = (bf16[2,256,256]{2,1,0:T(8,128)(2,1)}, bf16[2,256,256]{2,1,0:T(8,128)(2,1)S(1)}, u32[]{:S(2)}, u32[]{:S(2)}) collective-permute-start(bf16[2,256,256]{2,1,0:T(8,128)(2,1)} %bitcast.42), channel_id=1, source_target_pairs={{0,2},{1,3},{2,0},{3,1},{4,6},{5,7},{6,4},{7,5},{8,10},{9,11},{10,... | collective-permute-start | bytes 786440 | tf_op jit(solution)/shard_map/ppermute | solution.py:314
  6.2 19.3 %collective-permute-start.1 = (bf16[2,256,256]{2,1,0:T(8,128)(2,1)}, bf16[2,256,256]{2,1,0:T(8,128)(2,1)S(1)}, u32[]{:S(2)}, u32[]{:S(2)}) collective-permute-start(bf16[2,256,256]{2,1,0:T(8,128)(2,1)} %bitcast.43), channel_id=1, source_target_pairs={{0,12},{4,0},{8,4},{12,8},{1,13},{5,1},{9,5},{13,9},{2,14},{6,2},{... | collective-permute-start | bytes 786440 | tf_op jit(solution)/shard_map/ppermute | solution.py:309
  7.6 18.3 %collective-permute-start = (bf16[2,256,256]{2,1,0:T(8,128)(2,1)}, bf16[2,256,256]{2,1,0:T(8,128)(2,1)S(1)}, u32[]{:S(2)}, u32[]{:S(2)}) collective-permute-start(bf16[2,256,256]{2,1,0:T(8,128)(2,1)} %bitcast.44), channel_id=1, source_target_pairs={{0,4},{4,8},{8,12},{12,0},{1,5},{5,9},{9,13},{13,1},{2,6},{6,10},{... | collective-permute-start | bytes 786440 | tf_op jit(solution)/shard_map/ppermute | solution.py:309
  11.0 1.2 %copy-start.2 = (bf16[1,256,2048]{2,1,0:T(8,128)(2,1)S(1)}, bf16[1,256,2048]{2,1,0:T(8,128)(2,1)}, u32[]{:S(2)}) copy-start(bf16[1,256,2048]{2,1,0:T(8,128)(2,1)} %psi.1) | copy-start | bytes 3145732
  12.2 0.9 copy-start.3
  14.1 14.2 %all-to-all-start.1 = ((bf16[4,256,128]{2,1,0:T(8,128)(2,1)}), bf16[4,256,128]{2,1,0:T(8,128)(2,1)S(1)}, u32[]{:S(2)}, u32[]{:S(2)}) async-start(bf16[4,256,128]{2,1,0:T(8,128)(2,1)} %get-tuple-element.15), calls=%async_computation.1 | async-start | bytes 524288 | tf_op jit(solution)/shard_map/all_to_all | solution.py:352
  23.6 12.1 %collective-permute-start.10 = (bf16[2,256,256]{2,1,0:T(8,128)(2,1)S(1)}, bf16[2,256,256]{2,1,0:T(8,128)(2,1)S(1)}, u32[]{:S(2)}, u32[]{:S(2)}) collective-permute-start(bf16[2,256,256]{2,1,0:T(8,128)(2,1)S(1)} %collective-permute-done.2.refs_3_), channel_id=1, source_target_pairs={{0,1},{1,0},{2,3},{3,2},{4,5},{5,4},{6,7},{7,6},{8,9},{9,8},{10,11... | collective-permute-start | bytes 786440 | tf_op jit(solution)/shard_map/ppermute | solution.py:314
  23.6 12.6 %collective-permute-start.6 = (bf16[2,256,256]{2,1,0:T(8,128)(2,1)S(1)}, bf16[2,256,256]{2,1,0:T(8,128)(2,1)S(1)}, u32[]{:S(2)}, u32[]{:S(2)}) collective-permute-start(bf16[2,256,256]{2,1,0:T(8,128)(2,1)S(1)} %collective-permute-done.2.refs_3_), channel_id=1, source_target_pairs={{0,2},{1,3},{2,0},{3,1},{4,6},{5,7},{6,4},{7,5},{8,10},{9,11},{10,... | collective-permute-start | bytes 786440 | tf_op jit(solution)/shard_map/ppermute | solution.py:314
  25.3 9.8 %collective-permute-start.11 = (bf16[2,256,256]{2,1,0:T(8,128)(2,1)S(1)}, bf16[2,256,256]{2,1,0:T(8,128)(2,1)S(1)}, u32[]{:S(2)}, u32[]{:S(2)}) collective-permute-start(bf16[2,256,256]{2,1,0:T(8,128)(2,1)S(1)} %collective-permute-done.3.refs_4_), channel_id=1, source_target_pairs={{0,1},{1,0},{2,3},{3,2},{4,5},{5,4},{6,7},{7,6},{8,9},{9,8},{10,11... | collective-permute-start | bytes 786440 | tf_op jit(solution)/shard_map/ppermute | solution.py:314
  25.5 12.9 %collective-permute-start.5 = (bf16[2,256,256]{2,1,0:T(8,128)(2,1)S(1)}, bf16[2,256,256]{2,1,0:T(8,128)(2,1)S(1)}, u32[]{:S(2)}, u32[]{:S(2)}) collective-permute-start(bf16[2,256,256]{2,1,0:T(8,128)(2,1)S(1)} %collective-permute-done.1.refs_2_), channel_id=1, source_target_pairs={{0,2},{1,3},{2,0},{3,1},{4,6},{5,7},{6,4},{7,5},{8,10},{9,11},{10,... | collective-permute-start | bytes 786440 | tf_op jit(solution)/shard_map/ppermute | solution.py:314
  25.9 17.7 %collective-permute-start.4 = (bf16[2,256,256]{2,1,0:T(8,128)(2,1)S(1)}, bf16[2,256,256]{2,1,0:T(8,128)(2,1)S(1)}, u32[]{:S(2)}, u32[]{:S(2)}) collective-permute-start(bf16[2,256,256]{2,1,0:T(8,128)(2,1)S(1)} %collective-permute-done.refs_1_), channel_id=1, source_target_pairs={{0,2},{1,3},{2,0},{3,1},{4,6},{5,7},{6,4},{7,5},{8,10},{9,11},{10,... | collective-permute-start | bytes 786440 | tf_op jit(solution)/shard_map/ppermute | solution.py:314
  28.2 18.8 %all-to-all-start = ((bf16[4,256,128]{2,1,0:T(8,128)(2,1)}), bf16[4,256,128]{2,1,0:T(8,128)(2,1)S(1)}, u32[]{:S(2)}, u32[]{:S(2)}) async-start(bf16[4,256,128]{2,1,0:T(8,128)(2,1)} %get-tuple-element.14), calls=%async_computation | async-start | bytes 524288 | tf_op jit(solution)/shard_map/all_to_all | solution.py:351
  35.0 0.7 copy-start.7
  35.7 11.3 %collective-permute-start.9 = (bf16[2,256,256]{2,1,0:T(8,128)(2,1)S(1)}, bf16[2,256,256]{2,1,0:T(8,128)(2,1)}, u32[]{:S(2)}, u32[]{:S(2)}) collective-permute-start(bf16[2,256,256]{2,1,0:T(8,128)(2,1)S(1)} %collective-permute-done.1.refs_2_), channel_id=1, source_target_pairs={{0,1},{1,0},{2,3},{3,2},{4,5},{5,4},{6,7},{7,6},{8,9},{9,8},{10,11... | collective-permute-start | bytes 786440 | tf_op jit(solution)/shard_map/ppermute | solution.py:314
  35.7 11.3 %collective-permute-start.8 = (bf16[2,256,256]{2,1,0:T(8,128)(2,1)S(1)}, bf16[2,256,256]{2,1,0:T(8,128)(2,1)}, u32[]{:S(2)}, u32[]{:S(2)}) collective-permute-start(bf16[2,256,256]{2,1,0:T(8,128)(2,1)S(1)} %collective-permute-done.refs_1_), channel_id=1, source_target_pairs={{0,1},{1,0},{2,3},{3,2},{4,5},{5,4},{6,7},{7,6},{8,9},{9,8},{10,11... | collective-permute-start | bytes 786440 | tf_op jit(solution)/shard_map/ppermute | solution.py:314
  36.2 10.9 %copy-start.5 = (bf16[2,256,256]{2,1,0:T(8,128)(2,1)}, bf16[2,256,256]{2,1,0:T(8,128)(2,1)S(1)}, u32[]{:S(2)}) copy-start(bf16[2,256,256]{2,1,0:T(8,128)(2,1)S(1)} %collective-permute-done.6.refs_7_) | copy-start | bytes 786436
  36.2 10.8 %collective-permute-start.14 = (bf16[2,256,256]{2,1,0:T(8,128)(2,1)S(1)}, bf16[2,256,256]{2,1,0:T(8,128)(2,1)}, u32[]{:S(2)}, u32[]{:S(2)}) collective-permute-start(bf16[2,256,256]{2,1,0:T(8,128)(2,1)S(1)} %collective-permute-done.6.refs_7_), channel_id=1, source_target_pairs={{0,1},{1,0},{2,3},{3,2},{4,5},{5,4},{6,7},{7,6},{8,9},{9,8},{10,11... | collective-permute-start | bytes 786440 | tf_op jit(solution)/shard_map/ppermute | solution.py:314
  38.4 8.7 %copy-start.9 = (bf16[2,256,256]{2,1,0:T(8,128)(2,1)}, bf16[2,256,256]{2,1,0:T(8,128)(2,1)S(1)}, u32[]{:S(2)}) copy-start(bf16[2,256,256]{2,1,0:T(8,128)(2,1)S(1)} %collective-permute-done.5.refs_6_) | copy-start | bytes 786436
  38.4 8.7 %collective-permute-start.13 = (bf16[2,256,256]{2,1,0:T(8,128)(2,1)S(1)}, bf16[2,256,256]{2,1,0:T(8,128)(2,1)}, u32[]{:S(2)}, u32[]{:S(2)}) collective-permute-start(bf16[2,256,256]{2,1,0:T(8,128)(2,1)S(1)} %collective-permute-done.5.refs_6_), channel_id=1, source_target_pairs={{0,1},{1,0},{2,3},{3,2},{4,5},{5,4},{6,7},{7,6},{8,9},{9,8},{10,11... | collective-permute-start | bytes 786440 | tf_op jit(solution)/shard_map/ppermute | solution.py:314
  43.6 3.5 %collective-permute-start.12 = (bf16[2,256,256]{2,1,0:T(8,128)(2,1)S(1)}, bf16[2,256,256]{2,1,0:T(8,128)(2,1)}, u32[]{:S(2)}, u32[]{:S(2)}) collective-permute-start(bf16[2,256,256]{2,1,0:T(8,128)(2,1)S(1)} %collective-permute-done.4.refs_5_), channel_id=1, source_target_pairs={{0,1},{1,0},{2,3},{3,2},{4,5},{5,4},{6,7},{7,6},{8,9},{9,8},{10,11... | collective-permute-start | bytes 786440 | tf_op jit(solution)/shard_map/ppermute | solution.py:314
  43.6 0.7 copy-start.11
  47.1 1.0 copy-start.4
  48.1 0.9 copy-start.6
  49.0 0.9 copy-start.8
  50.0 0.9 copy-start.10
  50.9 0.9 copy-start.12
  56.5 1.9 %copy-start = (bf16[16,2,256,256]{3,2,1,0:T(8,128)(2,1)}, bf16[16,2,256,256]{3,2,1,0:T(8,128)(2,1)S(1)}, u32[]{:S(2)}) copy-start(bf16[16,2,256,256]{3,2,1,0:T(8,128)(2,1)S(1)} %get-tuple-element.19.left) | copy-start | bytes 12582916
  58.4 11.9 %all-to-all-start.2 = ((f32[16,8,128]{2,1,0:T(8,128)}), f32[16,8,128]{2,1,0:T(8,128)S(1)}, u32[]{:S(2)}, u32[]{:S(2)}) async-start(f32[16,8,128]{2,1,0:T(8,128)} %get-tuple-element.16), calls=%async_computation.2 | async-start | bytes 131072 | tf_op jit(solution)/shard_map/all_to_all | solution.py:378
  70.3 2.2 %copy-start.1 = (bf16[16,2,256,256]{3,2,1,0:T(8,128)(2,1)S(1)}, bf16[16,2,256,256]{3,2,1,0:T(8,128)(2,1)}, u32[]{:S(2)}) copy-start(bf16[16,2,256,256]{3,2,1,0:T(8,128)(2,1)} %copy-done) | copy-start | bytes 12582916
  76.3 10.4 %all-to-all-start.3 = ((f32[16,8,128]{2,1,0:T(8,128)}), f32[16,8,128]{2,1,0:T(8,128)S(1)}, u32[]{:S(2)}, u32[]{:S(2)}) async-start(f32[16,8,128]{2,1,0:T(8,128)} %get-tuple-element.20), calls=%async_computation.3 | async-start | bytes 131072 | tf_op jit(solution)/shard_map/all_to_all | solution.py:389
  102.6 9.4 %all-to-all-start.5 = ((bf16[4,4,64,128]{3,2,1,0:T(8,128)(2,1)}), bf16[4,4,64,128]{3,2,1,0:T(8,128)(2,1)S(1)}, u32[]{:S(2)}, u32[]{:S(2)}) async-start(bf16[4,4,64,128]{3,2,1,0:T(8,128)(2,1)} %get-tuple-element.24), calls=%async_computation.5 | async-start | bytes 524288 | tf_op jit(solution)/shard_map/all_to_all | solution.py:402

commit v3 on v0

--- a/solution.py
+++ b/solution.py
@@ -1,12 +1,18 @@
+import functools
+
 import jax
 import jax.numpy as jnp
 from jax import lax
+from jax.experimental import pallas as pl
+from jax.experimental.pallas import tpu as pltpu
 from jax.sharding import PartitionSpec as P
 
 EPS = 1e-06
-
-
-def per_device(
+LANES = 128
+VMEM_LIMIT = 40 * 1024 * 1024
+
+
+def per_device_general(
     psi, left_ops, right_ops, term_shift, slot_sector, sector_width, diag_left, diag_right
 ):
     sec_dev, rows, ncols = psi.shape
@@ -81,18 +87,351 @@
         (jnp.sum(vec32 * second_sigma), jnp.sum(upd32 * first_sigma), jnp.sum(upd32 * second_sigma))
     )
     h_mix = 0.5 * (v_s1 + u_s0)
-    angle = 0.5 * jnp.arctan2(2.0 * h_mix, theta - u_s1)
-    sine = jnp.sin(angle)
-    flip = jnp.where(sine > 0, -1.0, 1.0)
-    coef_v = -sine * flip
-    coef_u = jnp.cos(angle) * flip
-    half = 0.5 * (theta - u_s1)
-    energy = 0.5 * (theta + u_s1) - jnp.sqrt(half * half + h_mix * h_mix)
+    coef_v, coef_u, energy = ritz(theta, h_mix, u_s1)
     newvec = coef_v * vec32 + coef_u * upd32
     image = coef_v * first_sigma + coef_u * second_sigma
     new_out = final_rows(newvec.astype(jnp.bfloat16))
     res_out = final_rows((image - energy * newvec).astype(jnp.bfloat16))
     return (new_out, res_out, jnp.reshape(energy, (1,)))
+
+
+def ritz(theta, h_mix, h_two):
+    angle = 0.5 * jnp.arctan2(2.0 * h_mix, theta - h_two)
+    sine = jnp.sin(angle)
+    flip = jnp.where(sine > 0, -1.0, 1.0)
+    coef_v = -sine * flip
+    coef_u = jnp.cos(angle) * flip
+    half = 0.5 * (theta - h_two)
+    energy = 0.5 * (theta + h_two) - jnp.sqrt(half * half + h_mix * h_mix)
+    return coef_v, coef_u, energy
+
+
+VMEM, SMEM, ANY = pltpu.VMEM, pltpu.SMEM, pl.ANY
+
+
+def kernel(body, ins, outs, scratch=(), flops=0, nbytes=0):
+    return pl.pallas_call(
+        body,
+        out_shape=[jax.ShapeDtypeStruct(shape, dtype) for shape, dtype, _ in outs],
+        in_specs=[pl.BlockSpec(memory_space=space) for _, space in ins],
+        out_specs=[pl.BlockSpec(memory_space=space) for _, _, space in outs],
+        scratch_shapes=list(scratch),
+        compiler_params=pltpu.CompilerParams(vmem_limit_bytes=VMEM_LIMIT),
+        cost_estimate=pl.CostEstimate(flops=flops, bytes_accessed=nbytes, transcendentals=0),
+    )(*[array for array, _ in ins])
+
+
+def by_distance(own, n_blk, start):
+    out = [own]
+    for d in range(1, n_blk):
+        pairs = [(i, (i + d) % n_blk) for i in range(n_blk)]
+        out.append(lax.ppermute(start(d), "blk", pairs))
+    return out
+
+
+def swap(block, e, n_op):
+    return lax.ppermute(block, "op", [(i, i ^ e) for i in range(n_op)])
+
+
+def gather_left(own, n_blk, n_op):
+    held = dict(enumerate(by_distance(own, n_blk, lambda d: own)))
+    held = {(d, 0): block for d, block in held.items()}
+    bit = n_op // 2
+    while bit:
+        held.update({(d, e ^ bit): swap(block, bit, n_op) for (d, e), block in held.items()})
+        bit //= 2
+    return held
+
+
+def pack_body(n_blk, n_op, meta, shift, psi, right, *outs):
+    psi_out, right_out, sems = outs[:n_blk], outs[n_blk : n_blk + n_op], outs[-1]
+    cols = psi_out[0].shape[1]
+    terms, _, width, _ = right.shape
+    per = cols // width
+    own_blk, own_op = meta[0], meta[1]
+    copies = []
+    for d in range(n_blk):
+        there = lax.rem(own_blk + d, n_blk)
+        start = pl.multiple_of((there * n_op + own_op) * cols, LANES)
+        copies.append(
+            pltpu.make_async_copy(psi.at[0, :, pl.ds(start, cols)], psi_out[d], sems.at[d])
+        )
+        copies[-1].start()
+    lane = lax.broadcasted_iota(jnp.int32, (16, cols), 1)
+    line = jnp.zeros((16, cols), jnp.float32)
+    for k in range(terms):
+        line = jnp.where(lane == k, shift[k].astype(jnp.float32), line)
+    for e in range(n_op):
+        there = (own_op ^ e) * per
+        right_out[e][...] = jnp.zeros_like(right_out[e])
+        for k in range(terms):
+            for r in range(per):
+                row = (k * per + r) * width
+                right_out[e][row : row + width, r * width : (r + 1) * width] = right[k, there + r]
+        right_out[e][terms * cols :] = line.astype(jnp.bfloat16)
+    for copy in copies:
+        copy.wait()
+
+
+def row_mask(width, shape):
+    return lax.broadcasted_iota(jnp.int32, shape, 0) < width
+
+
+def fold(x):
+    return jnp.sum(x.reshape(-1, 8, x.shape[-1]), axis=0)
+
+
+def whole(x):
+    return jnp.sum(jnp.sum(x, axis=0, keepdims=True), axis=1, keepdims=True)
+
+
+def spread(values, out):
+    line = lax.broadcasted_iota(jnp.int32, out.shape[1:], 0)
+    tile = jnp.zeros(out.shape[1:], jnp.float32)
+    for j, value in enumerate(values):
+        tile = jnp.where(line == j, value, tile)
+    for d in range(out.shape[0]):
+        out[d] = tile
+
+
+def apply_h(dst, field, left, right, acc):
+    n_blk, n_op = len(left), len(right)
+    terms, cols = left[0][0].shape[0], acc.shape[2]
+    acc[...] = jnp.zeros_like(acc)
+    for d in range(n_blk):
+        block = field(d)
+        for e in range(n_op):
+            prod = lax.dot_general(
+                block,
+                right[e][: terms * cols],
+                (((1,), (1,)), ((), ())),
+                preferred_element_type=jnp.float32,
+            ).astype(jnp.bfloat16)
+            for k in range(terms):
+                there = dst[(d * n_op + e) * terms + k]
+                acc[there] += jnp.dot(
+                    left[d][e][k],
+                    prod[:, k * cols : (k + 1) * cols],
+                    preferred_element_type=jnp.float32,
+                )
+
+
+def split_refs(refs, n_blk, n_op):
+    left = [refs[d * n_op : (d + 1) * n_op] for d in range(n_blk)]
+    right = refs[n_blk * n_op : (n_blk + 1) * n_op]
+    return left, right, refs[(n_blk + 1) * n_op :]
+
+
+def send_rows(own_op, sends, j, d, ref):
+    step = sends[0].shape[2]
+    for e, send in enumerate(sends, 1):
+        start = pl.multiple_of((own_op ^ e) * step, step)
+        send[j, d] = ref[d, pl.ds(start, step)].astype(send.dtype)
+
+
+def first_body(n_blk, n_op, meta, dst, slots, widths, *refs):
+    left, right, refs = split_refs(refs, n_blk, n_op)
+    psi, refs = refs[:n_blk], refs[n_blk:]
+    dmat, sig_out, raw_out, dots_out = refs[:4]
+    sends, acc = refs[4:-1], refs[-1]
+
+    def field(d):
+        block = psi[d][...].astype(jnp.float32)
+        block = jnp.where(row_mask(widths[slots[d]], block.shape), block, 0.0)
+        raw_out[d] = block.astype(jnp.bfloat16)
+        return raw_out[d]
+
+    apply_h(dst, field, left, right, acc)
+    zero = jnp.zeros((8, dmat.shape[2]), jnp.float32)
+    sums = [zero, zero]
+    for d in range(n_blk):
+        raw = raw_out[d].astype(jnp.float32)
+        total = jnp.where(row_mask(widths[slots[d]], raw.shape), acc[d], 0.0)
+        sigma = total + dmat[slots[d]] * raw
+        sig_out[d] = sigma
+        sums = [sums[0] + fold(raw * raw), sums[1] + fold(raw * sigma)]
+        send_rows(meta[1], sends, 0, d, raw_out)
+        send_rows(meta[1], sends, 1, d, sig_out)
+    spread([whole(x) for x in sums], dots_out)
+
+
+def norm_theta(parts, count):
+    tot = jnp.sum(parts, axis=0) * (1.0 / count)
+    scale = lax.rsqrt(tot[0:1] + EPS)
+    return scale, tot[1:2] * scale * scale
+
+
+def second_body(n_blk, n_op, count, meta, dst, slots, widths, *refs):
+    left, right, refs = split_refs(refs, n_blk, n_op)
+    parts, raw_in, sig_in, dmat, f_out, t_out, dots_out = refs[:7]
+    sends, acc, corr = refs[7:-2], refs[-2], refs[-1]
+    scale, theta = norm_theta(parts[...], count)
+    zero = jnp.zeros((8, raw_in.shape[2]), jnp.float32)
+    vv, vc, vs = zero, zero, zero
+    for d in range(n_blk):
+        vec = raw_in[d].astype(jnp.float32) * scale
+        sigma = sig_in[d] * scale
+        den = dmat[slots[d]] - theta
+        item = (sigma - theta * vec) * den / jnp.maximum(den * den, 0.25)
+        corr[d] = item
+        vv, vc, vs = vv + fold(vec * vec), vc + fold(vec * item), vs + fold(vec * sigma)
+    vv, vc, vs = whole(vv), whole(vc), whole(vs)
+    along = vc / jnp.maximum(vv, 1e-30)
+
+    def field(d):
+        vec = raw_in[d].astype(jnp.float32) * scale
+        f_out[d] = (corr[d] - along * vec).astype(jnp.bfloat16)
+        return f_out[d]
+
+    apply_h(dst, field, left, right, acc)
+    sums = [zero for _ in range(5)]
+    for d in range(n_blk):
+        fld = f_out[d].astype(jnp.float32)
+        total = jnp.where(row_mask(widths[slots[d]], fld.shape), acc[d], 0.0)
+        image = total + dmat[slots[d]] * fld
+        t_out[d] = image
+        vec = raw_in[d].astype(jnp.float32) * scale
+        sigma = sig_in[d] * scale
+        prods = (fld * fld, vec * fld, vec * image, fld * sigma, fld * image)
+        sums = [held + fold(prod) for held, prod in zip(sums, prods)]
+        send_rows(meta[1], sends, 0, d, f_out)
+        send_rows(meta[1], sends, 1, d, t_out)
+    spread([vv, vc, vs] + [whole(x) for x in sums], dots_out)
+
+
+def ritz_pair(theta, h_mix, h_two):
+    diff, twice = theta - h_two, 2.0 * h_mix
+    size = jnp.sqrt(diff * diff + twice * twice)
+    some = size > 0.0
+    safe = jnp.where(some, size, 1.0)
+    big = jnp.sqrt(0.5 + 0.5 * jnp.abs(diff) / safe)
+    small = 0.5 * jnp.abs(twice) / (safe * big)
+    sine = jnp.where(diff >= 0.0, small, big)
+    cosine = jnp.where(diff >= 0.0, big, small)
+    sine = jnp.where(some, sine, 0.0)
+    cosine = jnp.where(some, cosine, 1.0)
+    upward = (twice > 0.0) | ((twice == 0.0) & (diff < 0.0))
+    return sine, jnp.where(upward, -cosine, cosine), 0.5 * (theta + h_two) - 0.5 * size
+
+
+def third_body(n_blk, n_op, count, meta, slots, parts1, parts2, raw_in, sig_in, f_in, t_in, *refs):
+    got1, got2 = refs[: n_op - 1], refs[n_op - 1 : 2 * (n_op - 1)]
+    new_out, res_out, energy_out = refs[2 * (n_op - 1) :]
+    step, cols = new_out.shape[1], raw_in.shape[2]
+    own_blk, own_op = meta[0], meta[1]
+    scale, theta = norm_theta(parts1[...], count)
+    vv, vc, vs, ff, vf, vt, fs, ft = (parts2[:, j, :] for j in range(8))
+
+    def mean(x):
+        return jnp.sum(x, axis=0, keepdims=True) * (1.0 / count)
+
+    along = mean(vc)
+    beta = vc / jnp.maximum(vv, 1e-30) - along
+    norm_sq = mean(ff + 2.0 * beta * vf + beta * beta * vv)
+    unit = lax.rsqrt(jnp.maximum(norm_sq, 0.0) + EPS)
+    v_s1 = unit * mean(vt + beta * vs)
+    u_s0 = unit * mean(fs + beta * vs)
+    u_s1 = unit * unit * mean(ft + beta * (vt + fs) + beta * beta * vs)
+    cv, cu, energy = ritz_pair(theta, 0.5 * (v_s1 + u_s0), u_s1)
+    energy_out[0] = jnp.max(energy)
+    cu = cu * unit
+    for e in range(n_op):
+        there = own_op ^ e
+        tile = parts2[own_blk * n_op + there]
+        back = tile[1:2] / jnp.maximum(tile[0:1], 1e-30) - along
+        on_vec = (cv + cu * back) * scale
+        at = pl.multiple_of(there * cols, LANES)
+        for d in range(n_blk):
+            if e:
+                blocks = got1[e - 1][0, d], got1[e - 1][1, d], got2[e - 1][0, d], got2[e - 1][1, d]
+            else:
+                rows = pl.ds(pl.multiple_of(own_op * step, step), step)
+                blocks = raw_in[d, rows], sig_in[d, rows], f_in[d, rows], t_in[d, rows]
+            raw, sigma, fld, image = (block.astype(jnp.float32) for block in blocks)
+            newvec = on_vec * raw + cu * fld
+            res = on_vec * sigma + cu * image - energy * newvec
+            new_out[slots[d], :, pl.ds(at, cols)] = newvec.astype(jnp.bfloat16)
+            res_out[slots[d], :, pl.ds(at, cols)] = res.astype(jnp.bfloat16)
+
+
+def per_device(
+    psi, left_ops, right_ops, term_shift, slot_sector, sector_width, diag_left, diag_right
+):
+    n_blk, n_op = lax.axis_size("blk"), lax.axis_size("op")
+    _, rows, ncols = psi.shape
+    terms = right_ops.shape[0]
+    cols = diag_right.shape[0] // n_op
+    step = rows // n_op
+    count = float(n_blk * rows * ncols)
+    n_dev = n_blk * n_op
+    own_blk, own_op = lax.axis_index("blk"), lax.axis_index("op")
+    meta = jnp.stack([own_blk, own_op]).astype(jnp.int32)
+    bf16, f32 = jnp.bfloat16, jnp.float32
+
+    left = gather_left(left_ops[:, 0], n_blk, n_op)
+    left_ins = [(left[d, e], VMEM) for d in range(n_blk) for e in range(n_op)]
+
+    sent = kernel(
+        functools.partial(pack_body, n_blk, n_op),
+        [(meta, SMEM), (term_shift, SMEM), (psi, ANY), (right_ops, VMEM)],
+        [((rows, cols), bf16, VMEM)] * n_blk + [((terms * cols + 16, cols), bf16, VMEM)] * n_op,
+        [pltpu.SemaphoreType.DMA((n_blk,))],
+        nbytes=1 << 20,
+    )
+    right = [sent[n_blk]] + [swap(sent[n_blk + e], e, n_op) for e in range(1, n_op)]
+    right_ins = [(block, VMEM) for block in right]
+    psi_ins = [(block, VMEM) for block in by_distance(sent[0], n_blk, lambda d: sent[d])]
+
+    places = jnp.arange(n_blk)
+    slots = lax.rem(own_blk - places + n_blk, n_blk).astype(jnp.int32)
+    shifts = jnp.stack([block[terms * cols, :terms] for block in right]).astype(jnp.int32)
+    match = slot_sector[:, None] == places[None, :]
+    widths = jnp.sum(jnp.where(match, sector_width[None, :], 0), axis=1).astype(jnp.int32)
+    turned = jnp.sum(jnp.where(slots[:, None] == places[None, :], slot_sector[None, :], 0), axis=1)
+    hit = turned[None, None, None, :] == turned[:, None, None, None] + shifts[None, :, :, None]
+    dst = jnp.min(jnp.where(hit, places, n_blk), axis=3).astype(jnp.int32).reshape(-1)
+    dr = lax.dynamic_slice_in_dim(diag_right, own_op * cols, cols, 0)
+    dmat = diag_left[:, :, None] + dr[None, None, :]
+
+    tables = [(meta, SMEM), (dst, SMEM), (slots, SMEM), (widths, SMEM)]
+    wide = ((n_blk, rows, cols), f32, VMEM)
+    narrow = ((n_blk, rows, cols), bf16, VMEM)
+    dots = ((n_dev, 8, LANES), f32, VMEM)
+    sends = [((2, n_blk, step, cols), bf16, VMEM)] * (n_op - 1)
+    acc = pltpu.VMEM((n_blk + 1, rows, cols), f32)
+    flops = 2 * n_blk * rows * cols * terms * n_op * (rows + cols)
+    cost = dict(flops=flops, nbytes=8 << 20)
+
+    def totals(parts):
+        return lax.all_to_all(parts, ("blk", "op"), 0, 0, tiled=True)
+
+    sig, raw, dots1, *out1 = kernel(
+        functools.partial(first_body, n_blk, n_op),
+        tables + left_ins + right_ins + psi_ins + [(dmat, VMEM)],
+        [wide, narrow, dots] + sends,
+        [acc],
+        **cost,
+    )
+    parts1 = totals(dots1)
+    got1 = [swap(block, e, n_op) for e, block in enumerate(out1, 1)]
+    fld, img, dots2, *out2 = kernel(
+        functools.partial(second_body, n_blk, n_op, count),
+        tables + left_ins + right_ins + [(x, VMEM) for x in (parts1, raw, sig, dmat)],
+        [narrow, wide, dots] + sends,
+        [acc, pltpu.VMEM((n_blk, rows, cols), f32)],
+        **cost,
+    )
+    parts2 = totals(dots2)
+    got2 = [swap(block, e, n_op) for e, block in enumerate(out2, 1)]
+    final = ((n_blk, step, n_op * cols), bf16, VMEM)
+    new, res, energy = kernel(
+        functools.partial(third_body, n_blk, n_op, count),
+        [(meta, SMEM), (slots, SMEM)]
+        + [(x, VMEM) for x in (parts1, parts2, raw, sig, fld, img, *got1, *got2)],
+        [final, final, ((1,), f32, SMEM)],
+        nbytes=4 << 20,
+    )
+    return new, res, energy
 
 
 def solution(mesh):
@@ -106,8 +445,24 @@
         P("grp", None),
         P(("grp", "blk")),
     )
+
+    def body(*args):
+        psi, left_ops, right_ops, diag_right = args[0], args[1], args[2], args[7]
+        n_op = mesh.shape["op"]
+        cols = diag_right.shape[0] // n_op
+        fits = (
+            psi.shape[0] == 1
+            and diag_right.shape[0] % n_op == 0
+            and cols % LANES == 0
+            and cols % right_ops.shape[2] == 0
+            and cols // right_ops.shape[2] * n_op == right_ops.shape[1]
+            and psi.shape[1] % (16 * n_op) == 0
+            and n_op & (n_op - 1) == 0
+        )
+        return (per_device if fits else per_device_general)(*args)
+
     return jax.shard_map(
-        per_device,
+        body,
         mesh=mesh,
         in_specs=placed,
         out_specs=(P("grp", "op", "blk"), P("grp", "op", "blk"), P("grp")),

time: 386 us -> 117 us (0.30)
  blocking collectives: 130 us -> 0 us
  waiting for transfers between devices: 93.8 us -> 33.4 us
  local copies, waits for them, and re-layouts: 72.9 us -> 31.2 us
  other arithmetic: 40.2 us -> 1.41 us
  starting transfers between devices: 8.23 us -> 32.6 us
  between operations: 22.3 us -> 0.86 us
  matrix products: 17.2 us -> 0 us
  Pallas kernels: 0 us -> 16.1 us
    all_to_all x2 -> x0, blocking collectives: 71.1 us -> none  [the longest x1 48.9 us: per_device(): lax.all_to_all(left_local(upd_left), 'blk', split_axis=3, concat_axis=1,...]
    psum x2 -> x0, waiting for transfers between devices: 64.4 us -> none  [op_total(): lax.psum(partial_value.astype(jnp.bfloat16), 'op').astype(jnp.float32)]
    psum x5 -> x0, blocking collectives: 58.6 us -> none  [the longest x4 44.6 us: reduce_dots(): sums = lax.psum(values, 'blk')]
    convert_element_type x3 -> x1, local copies, waits for them, and re-layouts: 27 us -> 0.68 us  [per_device(): jnp.stack([block[terms * cols, :terms] for block in right])]
    ppermute x0 -> x27, starting transfers between devices: none -> 25.1 us  [the longest x21 13.4 us: swap(): return lax.ppermute(block, 'op', [(i, i ^ e) for i in range(n_op)])]
    ppermute x0 -> x27, waiting for transfers between devices: none -> 21.8 us  [the longest x6 15.5 us: by_distance(): out.append(lax.ppermute(start(d), 'blk', pairs))]
    all_to_all x2, waiting for transfers between devices: 29.4 us -> 11.6 us  [totals(): return lax.all_to_all(parts, ('blk', 'op'), 0, 0, tiled=True)]
    reshape x4 -> x1, local copies, waits for them, and re-layouts: 18.1 us -> 0.78 us  [per_device(): jnp.min(jnp.where(hit, places, n_blk), axis=3).astype(jnp.int32).reshape(-1)]
  transfers between devices with their start and end apart: 4 -> 29, of which waited for: 4 -> 7; matrix products, arithmetic and copies ran while one was open for 12% -> 5% of each run, Pallas kernels for 0% -> 6%
where the time goes in v3:
time: 117 us; the launch traced here: 116 us
  waiting for transfers between devices  33.4 us (29%)
  starting transfers between devices  32.6 us (28%)
  local copies, waits for them, and re-layouts  31.2 us (27%)
  Pallas kernels  16.1 us (14%)
  other arithmetic  1.41 us (1%)
    unnamed x76, local copies, waits for them, and re-layouts  26.3 us
    pallas_call x4, Pallas kernels, kernel(): pl.pallas_call(body, out_shape=[jax.ShapeDtypeStruct(shape, dtype) for sh...  16.1 us
    ppermute x6, waiting for transfers between devices, by_distance(): out.append(lax.ppermute(start(d), 'blk', pairs))  15.5 us
    ppermute x21, starting transfers between devices, swap(): return lax.ppermute(block, 'op', [(i, i ^ e) for i in range(n_op)])  13.4 us
    ppermute x6, starting transfers between devices, by_distance(): out.append(lax.ppermute(start(d), 'blk', pairs))  11.7 us
    all_to_all x2, waiting for transfers between devices, totals(): return lax.all_to_all(parts, ('blk', 'op'), 0, 0, tiled=True)  11.6 us
    all_to_all x2, starting transfers between devices, totals(): return lax.all_to_all(parts, ('blk', 'op'), 0, 0, tiled=True)  7.54 us
    ppermute x21, waiting for transfers between devices, swap(): return lax.ppermute(block, 'op', [(i, i ^ e) for i in range(n_op)])  6.22 us
  transfers between devices with their start and end apart: 29, of which 7 were waited for; matrix products, arithmetic and copies ran while one was open for 5% of the time, Pallas kernels for 6%

profile of v3, /device:TPU:0, one launch (start us, length us, event | category | flops | bytes accessed | tf_op | source)
XLA Modules:
  0.0 115.6 jit_solution(6651936059187460218)
XLA Ops:
  0.7 0.6 copy-done.29
  1.3 1.2 %copy-done = bf16[1,256,2048]{2,1,0:T(8,128)(2,1)S(1)} copy-done((bf16[1,256,2048]{2,1,0:T(8,128)(2,1)S(1)}, bf16[1,256,2048]{2,1,0:T(8,128)(2,1)}, u32[]{:S(2)}) %copy-start) | copy-done | bytes 1048600
  2.5 0.9 copy-done.18
  3.5 0.8 shard_map.103
  4.3 3.1 %collective-permute-start.18 = (bf16[256,128]{1,0:T(8,128)(2,1)S(1)}, bf16[256,128]{1,0:T(8,128)(2,1)S(1)}, u32[]{:S(2)}, u32[]{:S(2)}) collective-permute-start(bf16[256,128]{1,0:T(8,128)(2,1)S(1)} %get-tuple-element.28), channel_id=1, source_target_pairs={{0,4},{4,8},{8,12},{12,0},{1,5},{5,9},{9,13},{13,1},{2,6},{6,10},{... | collective-permute-start | bytes 196616 | tf_op jit(solution)/shard_map/ppermute | solution.py:128
  7.4 1.5 %collective-permute-start.1 = (bf16[272,128]{1,0:T(8,128)(2,1)S(1)}, bf16[272,128]{1,0:T(8,128)(2,1)}, u32[]{:S(2)}, u32[]{:S(2)}) collective-permute-start(bf16[272,128]{1,0:T(8,128)(2,1)S(1)} %get-tuple-element.25), channel_id=1, source_target_pairs={{0,2},{1,3},{2,0},{3,1},{4,6},{5,7},{6,4},{7,5},{8,10},{9,11},{10,... | collective-permute-start | bytes 208904 | tf_op jit(solution)/shard_map/ppermute | solution.py:133
  9.3 2.6 %collective-permute-start.19 = (bf16[256,128]{1,0:T(8,128)(2,1)S(1)}, bf16[256,128]{1,0:T(8,128)(2,1)S(1)}, u32[]{:S(2)}, u32[]{:S(2)}) collective-permute-start(bf16[256,128]{1,0:T(8,128)(2,1)S(1)} %get-tuple-element.29), channel_id=1, source_target_pairs={{0,8},{4,12},{8,0},{12,4},{1,9},{5,13},{9,1},{13,5},{2,10},{6,14},... | collective-permute-start | bytes 196616 | tf_op jit(solution)/shard_map/ppermute | solution.py:128
  11.9 0.6 copy-done.19
  12.5 1.8 %collective-permute-start.20 = (bf16[256,128]{1,0:T(8,128)(2,1)S(1)}, bf16[256,128]{1,0:T(8,128)(2,1)S(1)}, u32[]{:S(2)}, u32[]{:S(2)}) collective-permute-start(bf16[256,128]{1,0:T(8,128)(2,1)S(1)} %get-tuple-element.30), channel_id=1, source_target_pairs={{0,12},{4,0},{8,4},{12,8},{1,13},{5,1},{9,5},{13,9},{2,14},{6,2},{... | collective-permute-start | bytes 196616 | tf_op jit(solution)/shard_map/ppermute | solution.py:128
  14.3 1.8 %collective-permute-done.19.refs_22_ = bf16[256,128]{1,0:T(8,128)(2,1)S(1)} collective-permute-done((bf16[256,128]{1,0:T(8,128)(2,1)S(1)}, bf16[256,128]{1,0:T(8,128)(2,1)S(1)}, u32[]{:S(2)}, u32[]{:S(2)}) %collective-permute-start.19) | collective-permute-done | bytes 65568 | tf_op jit(solution)/shard_map/ppermute | solution.py:128
  16.1 0.6 copy-done.21
  17.3 0.6 copy-done.23
  17.9 1.4 %collective-permute-start.10 = (bf16[2,256,256]{2,1,0:T(8,128)(2,1)S(1)}, bf16[2,256,256]{2,1,0:T(8,128)(2,1)S(1)}, u32[]{:S(2)}, u32[]{:S(2)}) collective-permute-start(bf16[2,256,256]{2,1,0:T(8,128)(2,1)S(1)} %bitcast.4), channel_id=1, source_target_pairs={{0,8},{4,12},{8,0},{12,4},{1,9},{5,13},{9,1},{13,5},{2,10},{6,14},... | collective-permute-start | bytes 786440 | tf_op jit(solution)/shard_map/ppermute | solution.py:128
  19.3 2.2 %collective-permute-start.6 = (bf16[2,256,256]{2,1,0:T(8,128)(2,1)S(1)}, bf16[2,256,256]{2,1,0:T(8,128)(2,1)S(1)}, u32[]{:S(2)}, u32[]{:S(2)}) collective-permute-start(bf16[2,256,256]{2,1,0:T(8,128)(2,1)S(1)} %bitcast.5), channel_id=1, source_target_pairs={{0,4},{4,8},{8,12},{12,0},{1,5},{5,9},{9,13},{13,1},{2,6},{6,10},{... | collective-permute-start | bytes 786440 | tf_op jit(solution)/shard_map/ppermute | solution.py:128
  21.6 1.5 %collective-permute-start.4 = (bf16[2,256,256]{2,1,0:T(8,128)(2,1)S(1)}, bf16[2,256,256]{2,1,0:T(8,128)(2,1)S(1)}, u32[]{:S(2)}, u32[]{:S(2)}) collective-permute-start(bf16[2,256,256]{2,1,0:T(8,128)(2,1)S(1)} %bitcast.6), channel_id=1, source_target_pairs={{0,2},{1,3},{2,0},{3,1},{4,6},{5,7},{6,4},{7,5},{8,10},{9,11},{10,... | collective-permute-start | bytes 786440 | tf_op jit(solution)/shard_map/ppermute | solution.py:133
  23.1 0.8 dynamic_slice.3
  24.2 2.8 %collective-permute-start.16 = (bf16[2,256,256]{2,1,0:T(8,128)(2,1)S(1)}, bf16[2,256,256]{2,1,0:T(8,128)(2,1)S(1)}, u32[]{:S(2)}, u32[]{:S(2)}) collective-permute-start(bf16[2,256,256]{2,1,0:T(8,128)(2,1)S(1)} %collective-permute-done.14.refs_12_), channel_id=1, source_target_pairs={{0,2},{1,3},{2,0},{3,1},{4,6},{5,7},{6,4},{7,5},{8,10},{9,11},{10,... | collective-permute-start | bytes 786440 | tf_op jit(solution)/shard_map/ppermute | solution.py:133
  27.0 13.6 %collective-permute-done.10.refs_8_ = bf16[2,256,256]{2,1,0:T(8,128)(2,1)S(1)} collective-permute-done((bf16[2,256,256]{2,1,0:T(8,128)(2,1)S(1)}, bf16[2,256,256]{2,1,0:T(8,128)(2,1)S(1)}, u32[]{:S(2)}, u32[]{:S(2)}) %collective-permute-start.10) | collective-permute-done | bytes 262176 | tf_op jit(solution)/shard_map/ppermute | solution.py:128
  40.6 1.5 %collective-permute-start.12 = (bf16[2,256,256]{2,1,0:T(8,128)(2,1)S(1)}, bf16[2,256,256]{2,1,0:T(8,128)(2,1)S(1)}, u32[]{:S(2)}, u32[]{:S(2)}) collective-permute-start(bf16[2,256,256]{2,1,0:T(8,128)(2,1)S(1)} %collective-permute-done.10.refs_8_), channel_id=1, source_target_pairs={{0,2},{1,3},{2,0},{3,1},{4,6},{5,7},{6,4},{7,5},{8,10},{9,11},{10,... | collective-permute-start | bytes 786440 | tf_op jit(solution)/shard_map/ppermute | solution.py:133
  42.9 0.6 copy-done.36
  43.6 0.8 select_reduce_fusion.1
  44.3 0.7 slice.16
  45.0 0.7 slice.17
  45.7 0.7 slice.18
  46.4 0.7 copy.11
  47.6 2.2 %collective-permute-done.12.refs_10_ = bf16[2,256,256]{2,1,0:T(8,128)(2,1)S(1)} collective-permute-done((bf16[2,256,256]{2,1,0:T(8,128)(2,1)S(1)}, bf16[2,256,256]{2,1,0:T(8,128)(2,1)S(1)}, u32[]{:S(2)}, u32[]{:S(2)}) %collective-permute-start.12) | collective-permute-done | bytes 262176 | tf_op jit(solution)/shard_map/ppermute | solution.py:133
  49.7 0.7 copy-done.2
  50.9 4.0 %collective-permute-done.8.refs_6_ = bf16[2,256,256]{2,1,0:T(8,128)(2,1)S(1)} collective-permute-done((bf16[2,256,256]{2,1,0:T(8,128)(2,1)S(1)}, bf16[2,256,256]{2,1,0:T(8,128)(2,1)S(1)}, u32[]{:S(2)}, u32[]{:S(2)}) %collective-permute-start.8) | collective-permute-done | bytes 262176 | tf_op jit(solution)/shard_map/ppermute | solution.py:133
  55.0 0.7 copy-done.5
  56.0 0.7 copy.12
  56.7 0.8 reshape.62.dst
  57.6 0.7 copy-done.11
  58.3 0.7 copy-done.27
  58.9 0.9 copy-done.3
  59.9 0.9 copy-done.6
  60.8 0.9 copy-done.12
  61.8 0.8 copy-done.20
  62.6 0.8 copy-done.22
  63.5 0.8 copy-done.24
  64.3 5.9 %shard_map.104 = (f32[4,256,128]{2,1,0:T(8,128)S(1)}, bf16[4,256,128]{2,1,0:T(8,128)(2,1)S(1)}, f32[16,8,128]{2,1,0:T(8,128)S(1)}, bf16[2,4,64,128]{3,2,1,0:T(8,...) custom-call(s32[2]{0:T(128)S(1)} %pad_add_fusion.meta, s32[32]{0:T(128)S(1)} %reshape.62.dst, ...), custom_call_target="tpu_custom_call" | custom-call | flops 805306368 | bytes 8388608 | tf_op jit(solution)/shard_map/pallas_call | solution.py:113
  70.3 0.7 copy-done.8
  71.0 0.6 copy-done.26
  71.6 0.7 copy-done.30
  72.3 0.6 copy-done.31
  72.9 0.6 copy-done.32
  73.6 4.0 %all-to-all-start = ((f32[16,8,128]{2,1,0:T(8,128)}), f32[16,8,128]{2,1,0:T(8,128)S(1)}, u32[]{:S(2)}, u32[]{:S(2)}) async-start(f32[16,8,128]{2,1,0:T(8,128)} %copy-done.26), calls=%async_computation | async-start | bytes 131072 | tf_op jit(solution)/shard_map/all_to_all | solution.py:406
  78.0 1.7 %collective-permute-start.22 = (bf16[2,4,64,128]{3,2,1,0:T(8,128)(2,1)}, bf16[2,4,64,128]{3,2,1,0:T(8,128)(2,1)}, u32[]{:S(2)}, u32[]{:S(2)}) collective-permute-start(bf16[2,4,64,128]{3,2,1,0:T(8,128)(2,1)} %copy-done.31), channel_id=1, source_target_pairs={{0,2},{1,3},{2,0},{3,1},{4,6},{5,7},{6,4},{7,5},{8,10},{9,11},{10,... | collective-permute-start | bytes 393224 | tf_op jit(solution)/shard_map/ppermute | solution.py:133
  79.7 4.8 %all-to-all-done.refs_20_.parts1 = f32[16,8,128]{2,1,0:T(8,128)S(1)} async-done(((f32[16,8,128]{2,1,0:T(8,128)}), f32[16,8,128]{2,1,0:T(8,128)S(1)}, u32[]{:S(2)}, u32[]{:S(2)}) %all-to-all-start) | async-done | bytes 65568 | tf_op jit(solution)/shard_map/all_to_all | solution.py:406
  84.5 0.7 copy-done.28
  85.2 0.9 copy-done.4
  86.1 0.9 copy-done.7
  87.1 0.9 copy-done.9
  88.0 0.9 copy-done.13
  89.0 7.1 %shard_map.105 = (bf16[4,256,128]{2,1,0:T(8,128)(2,1)S(1)}, f32[4,256,128]{2,1,0:T(8,128)S(1)}, f32[16,8,128]{2,1,0:T(8,128)S(1)}, bf16[2,4,64,128]{3,2,1,0:T(8,...) custom-call(s32[2]{0:T(128)S(1)} %pad_add_fusion.meta, s32[32]{0:T(128)S(1)} %reshape.62.dst, ...), custom_call_target="tpu_custom_call" | custom-call | flops 805306368 | bytes 8388608 | tf_op jit(solution)/shard_map/pallas_call | solution.py:113
  96.1 0.8 copy-done.14
  96.9 0.7 copy-done.16
  97.6 0.6 copy-done.25
  98.4 1.6 %collective-permute-start.26 = (bf16[2,4,64,128]{3,2,1,0:T(8,128)(2,1)}, bf16[2,4,64,128]{3,2,1,0:T(8,128)(2,1)S(1)}, u32[]{:S(2)}, u32[]{:S(2)}) collective-permute-start(bf16[2,4,64,128]{3,2,1,0:T(8,128)(2,1)} %get-tuple-element.42), channel_id=1, source_target_pairs={{0,3},{1,2},{2,1},{3,0},{4,7},{5,6},{6,5},{7,4},{8,11},{9,10},{10,... | collective-permute-start | bytes 393224 | tf_op jit(solution)/shard_map/ppermute | solution.py:133
  100.1 3.5 %all-to-all-start.1 = ((f32[16,8,128]{2,1,0:T(8,128)}), f32[16,8,128]{2,1,0:T(8,128)S(1)}, u32[]{:S(2)}, u32[]{:S(2)}) async-start(f32[16,8,128]{2,1,0:T(8,128)} %copy-done.25), calls=%async_computation.1 | async-start | bytes 131072 | tf_op jit(solution)/shard_map/all_to_all | solution.py:406
  103.6 6.8 %all-to-all-done.1.parts2 = f32[16,8,128]{2,1,0:T(8,128)S(1)} async-done(((f32[16,8,128]{2,1,0:T(8,128)}), f32[16,8,128]{2,1,0:T(8,128)S(1)}, u32[]{:S(2)}, u32[]{:S(2)}) %all-to-all-start.1) | async-done | bytes 65568 | tf_op jit(solution)/shard_map/all_to_all | solution.py:406
  110.5 0.9 copy-done.10
  111.4 1.0 copy-done.15
  112.4 0.9 copy-done.17
  113.4 2.2 %shard_map.106 = (bf16[4,64,512]{2,1,0:T(8,128)(2,1)}, bf16[4,64,512]{2,1,0:T(8,128)(2,1)}, f32[1]{0:T(128)}) custom-call(s32[2]{0:T(128)S(1)} %pad_add_fusion.meta, s32[4]{0:T(128)S(1)} %compare_select_fusion.slots, f32[16,8,128]{2,1,0:T(8,128)S(1)} %all-to-all-done.refs_20_.parts1, f32[16,8,128]{2,1,0:T(8,128)S(1)} %all-to-all-done.1.parts2, ...), custom_call_target="tpu_custom_call" | custom-call | bytes 4194304 | tf_op jit(solution)/shard_map/pallas_call | solution.py:113
  (89 shorter events, 4.2 us)
Async XLA Ops:
  0.6 0.7 copy-start.29
  1.3 1.2 %copy-start = (bf16[1,256,2048]{2,1,0:T(8,128)(2,1)S(1)}, bf16[1,256,2048]{2,1,0:T(8,128)(2,1)}, u32[]{:S(2)}) copy-start(bf16[1,256,2048]{2,1,0:T(8,128)(2,1)} %psi.1) | copy-start | bytes 3145732
  2.5 0.9 copy-start.18
  3.5 13.3 %copy-start.1 = (bf16[2,1,256,256]{3,2,1,0:T(8,128)(2,1)S(1)}, bf16[2,1,256,256]{3,2,1,0:T(8,128)(2,1)}, u32[]{:S(2)}) copy-start(bf16[2,1,256,256]{3,2,1,0:T(8,128)(2,1)} %param.9) | copy-start | bytes 786436
  4.3 7.5 %collective-permute-start.18 = (bf16[256,128]{1,0:T(8,128)(2,1)S(1)}, bf16[256,128]{1,0:T(8,128)(2,1)S(1)}, u32[]{:S(2)}, u32[]{:S(2)}) collective-permute-start(bf16[256,128]{1,0:T(8,128)(2,1)S(1)} %get-tuple-element.28), channel_id=1, source_target_pairs={{0,4},{4,8},{8,12},{12,0},{1,5},{5,9},{9,13},{13,1},{2,6},{6,10},{... | collective-permute-start | bytes 196616 | tf_op jit(solution)/shard_map/ppermute | solution.py:128
  7.4 11.9 %collective-permute-start = (bf16[272,128]{1,0:T(8,128)(2,1)S(1)}, bf16[272,128]{1,0:T(8,128)(2,1)}, u32[]{:S(2)}, u32[]{:S(2)}) collective-permute-start(bf16[272,128]{1,0:T(8,128)(2,1)S(1)} %get-tuple-element.24), channel_id=1, source_target_pairs={{0,1},{1,0},{2,3},{3,2},{4,5},{5,4},{6,7},{7,6},{8,9},{9,8},{10,11... | collective-permute-start | bytes 208904 | tf_op jit(solution)/shard_map/ppermute | solution.py:133
  7.4 14.2 %collective-permute-start.1 = (bf16[272,128]{1,0:T(8,128)(2,1)S(1)}, bf16[272,128]{1,0:T(8,128)(2,1)}, u32[]{:S(2)}, u32[]{:S(2)}) collective-permute-start(bf16[272,128]{1,0:T(8,128)(2,1)S(1)} %get-tuple-element.25), channel_id=1, source_target_pairs={{0,2},{1,3},{2,0},{3,1},{4,6},{5,7},{6,4},{7,5},{8,10},{9,11},{10,... | collective-permute-start | bytes 208904 | tf_op jit(solution)/shard_map/ppermute | solution.py:133
  8.9 14.2 %collective-permute-start.2 = (bf16[272,128]{1,0:T(8,128)(2,1)S(1)}, bf16[272,128]{1,0:T(8,128)(2,1)}, u32[]{:S(2)}, u32[]{:S(2)}) collective-permute-start(bf16[272,128]{1,0:T(8,128)(2,1)S(1)} %get-tuple-element.26), channel_id=1, source_target_pairs={{0,3},{1,2},{2,1},{3,0},{4,7},{5,6},{6,5},{7,4},{8,11},{9,10},{10,... | collective-permute-start | bytes 208904 | tf_op jit(solution)/shard_map/ppermute | solution.py:133
  9.3 6.9 %collective-permute-start.19 = (bf16[256,128]{1,0:T(8,128)(2,1)S(1)}, bf16[256,128]{1,0:T(8,128)(2,1)S(1)}, u32[]{:S(2)}, u32[]{:S(2)}) collective-permute-start(bf16[256,128]{1,0:T(8,128)(2,1)S(1)} %get-tuple-element.29), channel_id=1, source_target_pairs={{0,8},{4,12},{8,0},{12,4},{1,9},{5,13},{9,1},{13,5},{2,10},{6,14},... | collective-permute-start | bytes 196616 | tf_op jit(solution)/shard_map/ppermute | solution.py:128
  11.8 0.6 copy-start.19
  12.5 4.8 %collective-permute-start.20 = (bf16[256,128]{1,0:T(8,128)(2,1)S(1)}, bf16[256,128]{1,0:T(8,128)(2,1)S(1)}, u32[]{:S(2)}, u32[]{:S(2)}) collective-permute-start(bf16[256,128]{1,0:T(8,128)(2,1)S(1)} %get-tuple-element.30), channel_id=1, source_target_pairs={{0,12},{4,0},{8,4},{12,8},{1,13},{5,1},{9,5},{13,9},{2,14},{6,2},{... | collective-permute-start | bytes 196616 | tf_op jit(solution)/shard_map/ppermute | solution.py:128
  16.1 0.6 copy-start.21
  16.8 7.4 %collective-permute-start.14 = (bf16[2,256,256]{2,1,0:T(8,128)(2,1)S(1)}, bf16[2,256,256]{2,1,0:T(8,128)(2,1)S(1)}, u32[]{:S(2)}, u32[]{:S(2)}) collective-permute-start(bf16[2,256,256]{2,1,0:T(8,128)(2,1)S(1)} %bitcast.3), channel_id=1, source_target_pairs={{0,12},{4,0},{8,4},{12,8},{1,13},{5,1},{9,5},{13,9},{2,14},{6,2},{... | collective-permute-start | bytes 786440 | tf_op jit(solution)/shard_map/ppermute | solution.py:128
  17.9 22.7 %collective-permute-start.10 = (bf16[2,256,256]{2,1,0:T(8,128)(2,1)S(1)}, bf16[2,256,256]{2,1,0:T(8,128)(2,1)S(1)}, u32[]{:S(2)}, u32[]{:S(2)}) collective-permute-start(bf16[2,256,256]{2,1,0:T(8,128)(2,1)S(1)} %bitcast.4), channel_id=1, source_target_pairs={{0,8},{4,12},{8,0},{12,4},{1,9},{5,13},{9,1},{13,5},{2,10},{6,14},... | collective-permute-start | bytes 786440 | tf_op jit(solution)/shard_map/ppermute | solution.py:128
  19.3 21.3 %collective-permute-start.6 = (bf16[2,256,256]{2,1,0:T(8,128)(2,1)S(1)}, bf16[2,256,256]{2,1,0:T(8,128)(2,1)S(1)}, u32[]{:S(2)}, u32[]{:S(2)}) collective-permute-start(bf16[2,256,256]{2,1,0:T(8,128)(2,1)S(1)} %bitcast.5), channel_id=1, source_target_pairs={{0,4},{4,8},{8,12},{12,0},{1,5},{5,9},{9,13},{13,1},{2,6},{6,10},{... | collective-permute-start | bytes 786440 | tf_op jit(solution)/shard_map/ppermute | solution.py:128
  21.6 20.5 %collective-permute-start.4 = (bf16[2,256,256]{2,1,0:T(8,128)(2,1)S(1)}, bf16[2,256,256]{2,1,0:T(8,128)(2,1)S(1)}, u32[]{:S(2)}, u32[]{:S(2)}) collective-permute-start(bf16[2,256,256]{2,1,0:T(8,128)(2,1)S(1)} %bitcast.6), channel_id=1, source_target_pairs={{0,2},{1,3},{2,0},{3,1},{4,6},{5,7},{6,4},{7,5},{8,10},{9,11},{10,... | collective-permute-start | bytes 786440 | tf_op jit(solution)/shard_map/ppermute | solution.py:133
  23.1 19.3 %collective-permute-start.3 = (bf16[2,256,256]{2,1,0:T(8,128)(2,1)S(1)}, bf16[2,256,256]{2,1,0:T(8,128)(2,1)S(1)}, u32[]{:S(2)}, u32[]{:S(2)}) collective-permute-start(bf16[2,256,256]{2,1,0:T(8,128)(2,1)S(1)} %bitcast.7), channel_id=1, source_target_pairs={{0,1},{1,0},{2,3},{3,2},{4,5},{5,4},{6,7},{7,6},{8,9},{9,8},{10,11... | collective-permute-start | bytes 786440 | tf_op jit(solution)/shard_map/ppermute | solution.py:133
  23.1 0.8 copy-start.34
  24.2 22.9 %collective-permute-start.16 = (bf16[2,256,256]{2,1,0:T(8,128)(2,1)S(1)}, bf16[2,256,256]{2,1,0:T(8,128)(2,1)S(1)}, u32[]{:S(2)}, u32[]{:S(2)}) collective-permute-start(bf16[2,256,256]{2,1,0:T(8,128)(2,1)S(1)} %collective-permute-done.14.refs_12_), channel_id=1, source_target_pairs={{0,2},{1,3},{2,0},{3,1},{4,6},{5,7},{6,4},{7,5},{8,10},{9,11},{10,... | collective-permute-start | bytes 786440 | tf_op jit(solution)/shard_map/ppermute | solution.py:133
  40.6 6.5 %collective-permute-start.15 = (bf16[2,256,256]{2,1,0:T(8,128)(2,1)S(1)}, bf16[2,256,256]{2,1,0:T(8,128)(2,1)S(1)}, u32[]{:S(2)}, u32[]{:S(2)}) collective-permute-start(bf16[2,256,256]{2,1,0:T(8,128)(2,1)S(1)} %collective-permute-done.14.refs_12_), channel_id=1, source_target_pairs={{0,1},{1,0},{2,3},{3,2},{4,5},{5,4},{6,7},{7,6},{8,9},{9,8},{10,11... | collective-permute-start | bytes 786440 | tf_op jit(solution)/shard_map/ppermute | solution.py:133
  40.6 9.1 %collective-permute-start.12 = (bf16[2,256,256]{2,1,0:T(8,128)(2,1)S(1)}, bf16[2,256,256]{2,1,0:T(8,128)(2,1)S(1)}, u32[]{:S(2)}, u32[]{:S(2)}) collective-permute-start(bf16[2,256,256]{2,1,0:T(8,128)(2,1)S(1)} %collective-permute-done.10.refs_8_), channel_id=1, source_target_pairs={{0,2},{1,3},{2,0},{3,1},{4,6},{5,7},{6,4},{7,5},{8,10},{9,11},{10,... | collective-permute-start | bytes 786440 | tf_op jit(solution)/shard_map/ppermute | solution.py:133
  42.1 7.6 %collective-permute-start.11 = (bf16[2,256,256]{2,1,0:T(8,128)(2,1)S(1)}, bf16[2,256,256]{2,1,0:T(8,128)(2,1)S(1)}, u32[]{:S(2)}, u32[]{:S(2)}) collective-permute-start(bf16[2,256,256]{2,1,0:T(8,128)(2,1)S(1)} %collective-permute-done.10.refs_8_), channel_id=1, source_target_pairs={{0,1},{1,0},{2,3},{3,2},{4,5},{5,4},{6,7},{7,6},{8,9},{9,8},{10,11... | collective-permute-start | bytes 786440 | tf_op jit(solution)/shard_map/ppermute | solution.py:133
  42.3 12.6 %collective-permute-start.8 = (bf16[2,256,256]{2,1,0:T(8,128)(2,1)S(1)}, bf16[2,256,256]{2,1,0:T(8,128)(2,1)S(1)}, u32[]{:S(2)}, u32[]{:S(2)}) collective-permute-start(bf16[2,256,256]{2,1,0:T(8,128)(2,1)S(1)} %collective-permute-done.6.refs_4_), channel_id=1, source_target_pairs={{0,2},{1,3},{2,0},{3,1},{4,6},{5,7},{6,4},{7,5},{8,10},{9,11},{10,... | collective-permute-start | bytes 786440 | tf_op jit(solution)/shard_map/ppermute | solution.py:133
  42.9 0.7 copy-start.36
  42.9 0.7 copy-start.37
  47.0 8.6 %copy-start.33 = (s32[4]{0:T(128)S(1)}, s32[4]{0:T(128)}, u32[]{:S(2)}) copy-start(s32[4]{0:T(128)} %get-tuple-element.44) | copy-start | bytes 52
  47.1 8.6 %copy-start.35 = (s32[4,2]{0,1:T(2,128)S(1)}, s32[4,2]{0,1:T(2,128)}, u32[]{:S(2)}) copy-start(s32[4,2]{0,1:T(2,128)} %copy.11) | copy-start | bytes 100
  47.1 10.5 %collective-permute-start.7 = (bf16[2,256,256]{2,1,0:T(8,128)(2,1)S(1)}, bf16[2,256,256]{2,1,0:T(8,128)(2,1)}, u32[]{:S(2)}, u32[]{:S(2)}) collective-permute-start(bf16[2,256,256]{2,1,0:T(8,128)(2,1)S(1)} %collective-permute-done.6.refs_4_), channel_id=1, source_target_pairs={{0,1},{1,0},{2,3},{3,2},{4,5},{5,4},{6,7},{7,6},{8,9},{9,8},{10,11... | collective-permute-start | bytes 786440 | tf_op jit(solution)/shard_map/ppermute | solution.py:133
  47.1 10.5 %collective-permute-start.5 = (bf16[2,256,256]{2,1,0:T(8,128)(2,1)S(1)}, bf16[2,256,256]{2,1,0:T(8,128)(2,1)}, u32[]{:S(2)}, u32[]{:S(2)}) collective-permute-start(bf16[2,256,256]{2,1,0:T(8,128)(2,1)S(1)} %collective-permute-done.4.refs_2_), channel_id=1, source_target_pairs={{0,1},{1,0},{2,3},{3,2},{4,5},{5,4},{6,7},{7,6},{8,9},{9,8},{10,11... | collective-permute-start | bytes 786440 | tf_op jit(solution)/shard_map/ppermute | solution.py:133
  49.7 7.8 %collective-permute-start.17 = (bf16[2,256,256]{2,1,0:T(8,128)(2,1)S(1)}, bf16[2,256,256]{2,1,0:T(8,128)(2,1)}, u32[]{:S(2)}, u32[]{:S(2)}) collective-permute-start(bf16[2,256,256]{2,1,0:T(8,128)(2,1)S(1)} %collective-permute-done.16.refs_14_), channel_id=1, source_target_pairs={{0,1},{1,0},{2,3},{3,2},{4,5},{5,4},{6,7},{7,6},{8,9},{9,8},{10,11... | collective-permute-start | bytes 786440 | tf_op jit(solution)/shard_map/ppermute | solution.py:133
  49.7 0.7 copy-start.2
  50.4 7.1 %collective-permute-start.13 = (bf16[2,256,256]{2,1,0:T(8,128)(2,1)S(1)}, bf16[2,256,256]{2,1,0:T(8,128)(2,1)S(1)}, u32[]{:S(2)}, u32[]{:S(2)}) collective-permute-start(bf16[2,256,256]{2,1,0:T(8,128)(2,1)S(1)} %collective-permute-done.12.refs_10_), channel_id=1, source_target_pairs={{0,1},{1,0},{2,3},{3,2},{4,5},{5,4},{6,7},{7,6},{8,9},{9,8},{10,11... | collective-permute-start | bytes 786440 | tf_op jit(solution)/shard_map/ppermute | solution.py:133
  55.0 3.3 %collective-permute-start.9 = (bf16[2,256,256]{2,1,0:T(8,128)(2,1)S(1)}, bf16[2,256,256]{2,1,0:T(8,128)(2,1)}, u32[]{:S(2)}, u32[]{:S(2)}) collective-permute-start(bf16[2,256,256]{2,1,0:T(8,128)(2,1)S(1)} %collective-permute-done.8.refs_6_), channel_id=1, source_target_pairs={{0,1},{1,0},{2,3},{3,2},{4,5},{5,4},{6,7},{7,6},{8,9},{9,8},{10,11... | collective-permute-start | bytes 786440 | tf_op jit(solution)/shard_map/ppermute | solution.py:133
  55.0 0.7 copy-start.5
  57.6 0.7 copy-start.11
  58.3 0.7 copy-start.27
  58.9 0.9 copy-start.3
  59.9 0.9 copy-start.6
  60.8 0.9 copy-start.12
  61.8 0.8 copy-start.20
  62.6 0.8 copy-start.22
  63.5 0.8 copy-start.24
  70.3 0.7 copy-start.8
  71.6 0.7 copy-start.30
  72.3 0.6 copy-start.31
  72.9 0.6 copy-start.32
  73.6 10.9 %all-to-all-start = ((f32[16,8,128]{2,1,0:T(8,128)}), f32[16,8,128]{2,1,0:T(8,128)S(1)}, u32[]{:S(2)}, u32[]{:S(2)}) async-start(f32[16,8,128]{2,1,0:T(8,128)} %copy-done.26), calls=%async_computation | async-start | bytes 131072 | tf_op jit(solution)/shard_map/all_to_all | solution.py:406
  77.6 20.8 %collective-permute-start.21 = (bf16[2,4,64,128]{3,2,1,0:T(8,128)(2,1)}, bf16[2,4,64,128]{3,2,1,0:T(8,128)(2,1)}, u32[]{:S(2)}, u32[]{:S(2)}) collective-permute-start(bf16[2,4,64,128]{3,2,1,0:T(8,128)(2,1)} %copy-done.32), channel_id=1, source_target_pairs={{0,1},{1,0},{2,3},{3,2},{4,5},{5,4},{6,7},{7,6},{8,9},{9,8},{10,11... | collective-permute-start | bytes 393224 | tf_op jit(solution)/shard_map/ppermute | solution.py:133
  78.0 25.5 %collective-permute-start.22 = (bf16[2,4,64,128]{3,2,1,0:T(8,128)(2,1)}, bf16[2,4,64,128]{3,2,1,0:T(8,128)(2,1)}, u32[]{:S(2)}, u32[]{:S(2)}) collective-permute-start(bf16[2,4,64,128]{3,2,1,0:T(8,128)(2,1)} %copy-done.31), channel_id=1, source_target_pairs={{0,2},{1,3},{2,0},{3,1},{4,6},{5,7},{6,4},{7,5},{8,10},{9,11},{10,... | collective-permute-start | bytes 393224 | tf_op jit(solution)/shard_map/ppermute | solution.py:133
  79.7 23.9 %collective-permute-start.23 = (bf16[2,4,64,128]{3,2,1,0:T(8,128)(2,1)}, bf16[2,4,64,128]{3,2,1,0:T(8,128)(2,1)}, u32[]{:S(2)}, u32[]{:S(2)}) collective-permute-start(bf16[2,4,64,128]{3,2,1,0:T(8,128)(2,1)} %copy-done.30), channel_id=1, source_target_pairs={{0,3},{1,2},{2,1},{3,0},{4,7},{5,6},{6,5},{7,4},{8,11},{9,10},{10,... | collective-permute-start | bytes 393224 | tf_op jit(solution)/shard_map/ppermute | solution.py:133
  84.5 0.7 copy-start.28
  85.2 0.9 copy-start.4
  86.1 0.9 copy-start.7
  87.1 0.9 copy-start.9
  88.0 0.9 copy-start.13
  96.1 0.8 copy-start.14
  96.9 0.7 copy-start.16
  98.2 12.2 %collective-permute-start.24 = (bf16[2,4,64,128]{3,2,1,0:T(8,128)(2,1)}, bf16[2,4,64,128]{3,2,1,0:T(8,128)(2,1)S(1)}, u32[]{:S(2)}, u32[]{:S(2)}) collective-permute-start(bf16[2,4,64,128]{3,2,1,0:T(8,128)(2,1)} %get-tuple-element.40), channel_id=1, source_target_pairs={{0,1},{1,0},{2,3},{3,2},{4,5},{5,4},{6,7},{7,6},{8,9},{9,8},{10,11... | collective-permute-start | bytes 393224 | tf_op jit(solution)/shard_map/ppermute | solution.py:133
  98.2 12.2 %collective-permute-start.25 = (bf16[2,4,64,128]{3,2,1,0:T(8,128)(2,1)}, bf16[2,4,64,128]{3,2,1,0:T(8,128)(2,1)S(1)}, u32[]{:S(2)}, u32[]{:S(2)}) collective-permute-start(bf16[2,4,64,128]{3,2,1,0:T(8,128)(2,1)} %get-tuple-element.41), channel_id=1, source_target_pairs={{0,2},{1,3},{2,0},{3,1},{4,6},{5,7},{6,4},{7,5},{8,10},{9,11},{10,... | collective-permute-start | bytes 393224 | tf_op jit(solution)/shard_map/ppermute | solution.py:133
  98.4 12.0 %collective-permute-start.26 = (bf16[2,4,64,128]{3,2,1,0:T(8,128)(2,1)}, bf16[2,4,64,128]{3,2,1,0:T(8,128)(2,1)S(1)}, u32[]{:S(2)}, u32[]{:S(2)}) collective-permute-start(bf16[2,4,64,128]{3,2,1,0:T(8,128)(2,1)} %get-tuple-element.42), channel_id=1, source_target_pairs={{0,3},{1,2},{2,1},{3,0},{4,7},{5,6},{6,5},{7,4},{8,11},{9,10},{10,... | collective-permute-start | bytes 393224 | tf_op jit(solution)/shard_map/ppermute | solution.py:133
  100.1 10.4 %all-to-all-start.1 = ((f32[16,8,128]{2,1,0:T(8,128)}), f32[16,8,128]{2,1,0:T(8,128)S(1)}, u32[]{:S(2)}, u32[]{:S(2)}) async-start(f32[16,8,128]{2,1,0:T(8,128)} %copy-done.25), calls=%async_computation.1 | async-start | bytes 131072 | tf_op jit(solution)/shard_map/all_to_all | solution.py:406
  110.4 1.0 copy-start.10
  111.4 1.0 copy-start.15
  112.4 0.9 copy-start.17
  (3 other events, 1.9 us)

commit v4 on v3

--- a/solution.py
+++ b/solution.py
@@ -9,7 +9,7 @@
 
 EPS = 1e-06
 LANES = 128
-VMEM_LIMIT = 40 * 1024 * 1024
+VMEM_LIMIT = 20 * 1024 * 1024
 
 
 def per_device_general(
@@ -106,7 +106,7 @@
     return coef_v, coef_u, energy
 
 
-VMEM, SMEM, ANY = pltpu.VMEM, pltpu.SMEM, pl.ANY
+VMEM, SMEM, HBM, ANY = pltpu.VMEM, pltpu.SMEM, pltpu.HBM, pl.ANY
 
 
 def kernel(body, ins, outs, scratch=(), flops=0, nbytes=0):
@@ -143,7 +143,7 @@
     return held
 
 
-def pack_body(n_blk, n_op, meta, shift, psi, right, *outs):
+def pack_body(n_blk, n_op, meta, shift, psi, right, _, *outs):
     psi_out, right_out, sems = outs[:n_blk], outs[n_blk : n_blk + n_op], outs[-1]
     cols = psi_out[0].shape[1]
     terms, _, width, _ = right.shape
@@ -161,16 +161,46 @@
     line = jnp.zeros((16, cols), jnp.float32)
     for k in range(terms):
         line = jnp.where(lane == k, shift[k].astype(jnp.float32), line)
+    square = [lax.broadcasted_iota(jnp.int32, (width, width), axis) for axis in (0, 1)]
+    unit = (square[0] == square[1]).astype(jnp.bfloat16)
     for e in range(n_op):
         there = (own_op ^ e) * per
         right_out[e][...] = jnp.zeros_like(right_out[e])
         for k in range(terms):
             for r in range(per):
                 row = (k * per + r) * width
-                right_out[e][row : row + width, r * width : (r + 1) * width] = right[k, there + r]
+                turned = lax.dot_general(
+                    right[k, there + r], unit, (((0,), (0,)), ((), ())),
+                    preferred_element_type=jnp.float32,
+                )
+                right_out[e][row : row + width, r * width : (r + 1) * width] = turned.astype(jnp.bfloat16)
         right_out[e][terms * cols :] = line.astype(jnp.bfloat16)
     for copy in copies:
         copy.wait()
+
+
+def table_body(n_blk, n_op, terms, meta, sector, width, left_diag, right_diag, *refs):
+    tails, src, widths, slots, dmat = refs[:n_op], *refs[n_op:]
+    cols = tails[0].shape[1]
+    own_blk = meta[0]
+    lane = lax.broadcasted_iota(jnp.int32, (16, cols), 1)
+    for d in range(n_blk):
+        slot = lax.rem(own_blk - d + n_blk, n_blk)
+        slots[d] = slot
+        widths[d] = width[sector[slot]]
+    for e in range(n_op):
+        tail = tails[e][terms * cols :].astype(jnp.float32)
+        for k in range(terms):
+            shift = jnp.max(jnp.where(lane == k, tail, -1e9)).astype(jnp.int32)
+            for t in range(n_blk):
+                want = sector[slots[t]] - shift
+                found = jnp.int32(n_blk)
+                for d in range(n_blk):
+                    found = jnp.where(sector[slots[d]] == want, d, found)
+                src[(t * n_op + e) * terms + k] = found
+    for d in range(n_blk):
+        row = left_diag[pl.ds(slots[d], 1), :]
+        dmat[d] = jnp.transpose(jnp.broadcast_to(row, (cols, row.shape[1]))) + right_diag[...]
 
 
 def row_mask(width, shape):
@@ -194,32 +224,31 @@
         out[d] = tile
 
 
-def apply_h(dst, field, left, right, acc):
-    n_blk, n_op = len(left), len(right)
-    terms, cols = left[0][0].shape[0], acc.shape[2]
-    acc[...] = jnp.zeros_like(acc)
+def apply_h(src, field, left, right, inter, emit):
+    n_blk, n_op = inter.shape[0] - 1, len(right)
+    rows, cols = inter.shape[2], inter.shape[3]
+    terms = inter.shape[1] // n_op
+    inter[n_blk] = jnp.zeros_like(inter[n_blk])
     for d in range(n_blk):
         block = field(d)
         for e in range(n_op):
-            prod = lax.dot_general(
-                block,
-                right[e][: terms * cols],
-                (((1,), (1,)), ((), ())),
-                preferred_element_type=jnp.float32,
-            ).astype(jnp.bfloat16)
-            for k in range(terms):
-                there = dst[(d * n_op + e) * terms + k]
-                acc[there] += jnp.dot(
-                    left[d][e][k],
-                    prod[:, k * cols : (k + 1) * cols],
-                    preferred_element_type=jnp.float32,
-                )
+            ops = left(d, e).reshape(terms * rows, rows)
+            prod = jnp.dot(ops, block, preferred_element_type=jnp.float32)
+            prod = prod.astype(jnp.bfloat16).reshape(terms, rows, cols)
+            inter[d, e * terms : (e + 1) * terms] = prod
+    for t in range(n_blk):
+        total = None
+        for e in range(n_op):
+            js = range(e * terms, (e + 1) * terms)
+            moved = jnp.concatenate([inter[src[t * n_op * terms + j], j] for j in js], axis=1)
+            part = jnp.dot(moved, right[e][: terms * cols], preferred_element_type=jnp.float32)
+            total = part if total is None else total + part
+        emit(t, total)
 
 
 def split_refs(refs, n_blk, n_op):
     left = [refs[d * n_op : (d + 1) * n_op] for d in range(n_blk)]
-    right = refs[n_blk * n_op : (n_blk + 1) * n_op]
-    return left, right, refs[(n_blk + 1) * n_op :]
+    return left, refs[n_blk * n_op :]
 
 
 def send_rows(own_op, sends, j, d, ref):
@@ -229,30 +258,41 @@
         send[j, d] = ref[d, pl.ds(start, step)].astype(send.dtype)
 
 
-def first_body(n_blk, n_op, meta, dst, slots, widths, *refs):
-    left, right, refs = split_refs(refs, n_blk, n_op)
-    psi, refs = refs[:n_blk], refs[n_blk:]
-    dmat, sig_out, raw_out, dots_out = refs[:4]
-    sends, acc = refs[4:-1], refs[-1]
+def first_body(n_blk, n_op, meta, src, widths, *refs):
+    left, refs = split_refs(refs, n_blk, n_op)
+    right, psi, refs = refs[:n_op], refs[n_op : n_op + n_blk], refs[n_op + n_blk :]
+    dmat, sig_out, raw_out, dots_out, left_out = refs[:5]
+    sends, inter, sems = refs[5:-2], refs[-2], refs[-1]
+    copies = []
+    for d in range(n_blk):
+        for e in range(n_op):
+            copies.append(
+                pltpu.make_async_copy(left[d][e], left_out.at[d, e], sems.at[d * n_op + e])
+            )
+            copies[-1].start()
 
     def field(d):
         block = psi[d][...].astype(jnp.float32)
-        block = jnp.where(row_mask(widths[slots[d]], block.shape), block, 0.0)
+        block = jnp.where(row_mask(widths[d], block.shape), block, 0.0)
         raw_out[d] = block.astype(jnp.bfloat16)
         return raw_out[d]
 
-    apply_h(dst, field, left, right, acc)
     zero = jnp.zeros((8, dmat.shape[2]), jnp.float32)
     sums = [zero, zero]
-    for d in range(n_blk):
+
+    def emit(d, total):
         raw = raw_out[d].astype(jnp.float32)
-        total = jnp.where(row_mask(widths[slots[d]], raw.shape), acc[d], 0.0)
-        sigma = total + dmat[slots[d]] * raw
+        sigma = jnp.where(row_mask(widths[d], raw.shape), total, 0.0) + dmat[d] * raw
         sig_out[d] = sigma
-        sums = [sums[0] + fold(raw * raw), sums[1] + fold(raw * sigma)]
+        sums[0] = sums[0] + fold(raw * raw)
+        sums[1] = sums[1] + fold(raw * sigma)
         send_rows(meta[1], sends, 0, d, raw_out)
         send_rows(meta[1], sends, 1, d, sig_out)
+
+    apply_h(src, field, lambda d, e: left[d][e][...], right, inter, emit)
     spread([whole(x) for x in sums], dots_out)
+    for copy in copies:
+        copy.wait()
 
 
 def norm_theta(parts, count):
@@ -261,17 +301,20 @@
     return scale, tot[1:2] * scale * scale
 
 
-def second_body(n_blk, n_op, count, meta, dst, slots, widths, *refs):
-    left, right, refs = split_refs(refs, n_blk, n_op)
+def second_body(n_blk, n_op, count, meta, src, widths, left_in, *refs):
+    right, refs = refs[:n_op], refs[n_op:]
     parts, raw_in, sig_in, dmat, f_out, t_out, dots_out = refs[:7]
-    sends, acc, corr = refs[7:-2], refs[-2], refs[-1]
+    sends, inter, corr, held, sems = refs[7:-4], *refs[-4:]
+    copies = [pltpu.make_async_copy(left_in.at[d], held.at[d], sems.at[d]) for d in range(n_blk)]
+    for copy in copies:
+        copy.start()
     scale, theta = norm_theta(parts[...], count)
     zero = jnp.zeros((8, raw_in.shape[2]), jnp.float32)
     vv, vc, vs = zero, zero, zero
     for d in range(n_blk):
         vec = raw_in[d].astype(jnp.float32) * scale
         sigma = sig_in[d] * scale
-        den = dmat[slots[d]] - theta
+        den = dmat[d] - theta
         item = (sigma - theta * vec) * den / jnp.maximum(den * den, 0.25)
         corr[d] = item
         vv, vc, vs = vv + fold(vec * vec), vc + fold(vec * item), vs + fold(vec * sigma)
@@ -281,21 +324,23 @@
     def field(d):
         vec = raw_in[d].astype(jnp.float32) * scale
         f_out[d] = (corr[d] - along * vec).astype(jnp.bfloat16)
+        copies[d].wait()
         return f_out[d]
 
-    apply_h(dst, field, left, right, acc)
     sums = [zero for _ in range(5)]
-    for d in range(n_blk):
+
+    def emit(d, total):
         fld = f_out[d].astype(jnp.float32)
-        total = jnp.where(row_mask(widths[slots[d]], fld.shape), acc[d], 0.0)
-        image = total + dmat[slots[d]] * fld
+        image = jnp.where(row_mask(widths[d], fld.shape), total, 0.0) + dmat[d] * fld
         t_out[d] = image
         vec = raw_in[d].astype(jnp.float32) * scale
         sigma = sig_in[d] * scale
         prods = (fld * fld, vec * fld, vec * image, fld * sigma, fld * image)
-        sums = [held + fold(prod) for held, prod in zip(sums, prods)]
+        sums[:] = [one + fold(prod) for one, prod in zip(sums, prods)]
         send_rows(meta[1], sends, 0, d, f_out)
         send_rows(meta[1], sends, 1, d, t_out)
+
+    apply_h(src, field, lambda d, e: held[d, e], right, inter, emit)
     spread([vv, vc, vs] + [whole(x) for x in sums], dots_out)
 
 
@@ -373,7 +418,7 @@
 
     sent = kernel(
         functools.partial(pack_body, n_blk, n_op),
-        [(meta, SMEM), (term_shift, SMEM), (psi, ANY), (right_ops, VMEM)],
+        [(meta, SMEM), (term_shift, SMEM), (psi, HBM), (right_ops, VMEM), (left[0, n_op // 2], ANY)],
         [((rows, cols), bf16, VMEM)] * n_blk + [((terms * cols + 16, cols), bf16, VMEM)] * n_op,
         [pltpu.SemaphoreType.DMA((n_blk,))],
         nbytes=1 << 20,
@@ -381,44 +426,44 @@
     right = [sent[n_blk]] + [swap(sent[n_blk + e], e, n_op) for e in range(1, n_op)]
     right_ins = [(block, VMEM) for block in right]
     psi_ins = [(block, VMEM) for block in by_distance(sent[0], n_blk, lambda d: sent[d])]
-
-    places = jnp.arange(n_blk)
-    slots = lax.rem(own_blk - places + n_blk, n_blk).astype(jnp.int32)
-    shifts = jnp.stack([block[terms * cols, :terms] for block in right]).astype(jnp.int32)
-    match = slot_sector[:, None] == places[None, :]
-    widths = jnp.sum(jnp.where(match, sector_width[None, :], 0), axis=1).astype(jnp.int32)
-    turned = jnp.sum(jnp.where(slots[:, None] == places[None, :], slot_sector[None, :], 0), axis=1)
-    hit = turned[None, None, None, :] == turned[:, None, None, None] + shifts[None, :, :, None]
-    dst = jnp.min(jnp.where(hit, places, n_blk), axis=3).astype(jnp.int32).reshape(-1)
     dr = lax.dynamic_slice_in_dim(diag_right, own_op * cols, cols, 0)
-    dmat = diag_left[:, :, None] + dr[None, None, :]
-
-    tables = [(meta, SMEM), (dst, SMEM), (slots, SMEM), (widths, SMEM)]
+    src, widths, slots, dmat = kernel(
+        functools.partial(table_body, n_blk, n_op, terms),
+        [(meta, SMEM), (slot_sector, SMEM), (sector_width, SMEM)]
+        + [(diag_left, VMEM), (dr[None], VMEM)]
+        + right_ins,
+        [((n_blk * n_op * terms,), jnp.int32, SMEM)]
+        + [((n_blk,), jnp.int32, SMEM)] * 2
+        + [((n_blk, rows, cols), f32, VMEM)],
+    )
+
+    tables = [(meta, SMEM), (src, SMEM), (widths, SMEM)]
     wide = ((n_blk, rows, cols), f32, VMEM)
     narrow = ((n_blk, rows, cols), bf16, VMEM)
     dots = ((n_dev, 8, LANES), f32, VMEM)
     sends = [((2, n_blk, step, cols), bf16, VMEM)] * (n_op - 1)
-    acc = pltpu.VMEM((n_blk + 1, rows, cols), f32)
+    inter = pltpu.VMEM((n_blk + 1, n_op * terms, rows, cols), bf16)
+    left_all = (n_blk, n_op, terms, rows, rows)
     flops = 2 * n_blk * rows * cols * terms * n_op * (rows + cols)
     cost = dict(flops=flops, nbytes=8 << 20)
 
     def totals(parts):
         return lax.all_to_all(parts, ("blk", "op"), 0, 0, tiled=True)
 
-    sig, raw, dots1, *out1 = kernel(
+    sig, raw, dots1, kept, *out1 = kernel(
         functools.partial(first_body, n_blk, n_op),
         tables + left_ins + right_ins + psi_ins + [(dmat, VMEM)],
-        [wide, narrow, dots] + sends,
-        [acc],
+        [wide, narrow, dots, (left_all, bf16, HBM)] + sends,
+        [inter, pltpu.SemaphoreType.DMA((n_dev,))],
         **cost,
     )
     parts1 = totals(dots1)
     got1 = [swap(block, e, n_op) for e, block in enumerate(out1, 1)]
     fld, img, dots2, *out2 = kernel(
         functools.partial(second_body, n_blk, n_op, count),
-        tables + left_ins + right_ins + [(x, VMEM) for x in (parts1, raw, sig, dmat)],
+        tables + [(kept, HBM)] + right_ins + [(x, VMEM) for x in (parts1, raw, sig, dmat)],
         [narrow, wide, dots] + sends,
-        [acc, pltpu.VMEM((n_blk, rows, cols), f32)],
+        [inter, pltpu.VMEM((n_blk, rows, cols), f32), pltpu.VMEM(left_all, bf16), pltpu.SemaphoreType.DMA((n_blk,))],
         **cost,
     )
     parts2 = totals(dots2)

time: 117 us -> 110 us (0.940)
  waiting for transfers between devices: 33.4 us -> 45.5 us
  local copies, waits for them, and re-layouts: 31.2 us -> 23 us
  starting transfers between devices: 32.6 us -> 27.8 us
  Pallas kernels: 16.1 us -> 12.6 us
  other arithmetic: 1.41 us -> 0.07 us
    ppermute x21, waiting for transfers between devices: 6.22 us -> 15.7 us  [swap(): return lax.ppermute(block, 'op', [(i, i ^ e) for i in range(n_op)])]
    pallas_call x4 -> x5, Pallas kernels: 16.1 us -> 12.6 us  [kernel(): pl.pallas_call(body, out_shape=[jax.ShapeDtypeStruct(shape, dtype) for sh...]
    unnamed x76 -> x56, local copies, waits for them, and re-layouts: 26.3 us -> 22.9 us
    ppermute x6, starting transfers between devices: 11.7 us -> 8.66 us  [by_distance(): out.append(lax.ppermute(start(d), 'blk', pairs))]
    ppermute x6, waiting for transfers between devices: 15.5 us -> 18.1 us  [by_distance(): out.append(lax.ppermute(start(d), 'blk', pairs))]
    slice x4 -> x0, local copies, waits for them, and re-layouts: 2.04 us -> none  [per_device(): block[terms * cols, :terms]]
    ppermute x21, starting transfers between devices: 13.4 us -> 12.1 us  [swap(): return lax.ppermute(block, 'op', [(i, i ^ e) for i in range(n_op)])]
  transfers between devices with their start and end apart: 29 -> 29, of which waited for: 7 -> 8; matrix products, arithmetic and copies ran while one was open for 5% -> 0% of each run, Pallas kernels for 6% -> 6%
where the time goes in v4:
time: 110 us
  waiting for transfers between devices  45.5 us (41%)
  starting transfers between devices  27.8 us (25%)
  local copies, waits for them, and re-layouts  23 us (21%)
  Pallas kernels  12.6 us (11%)
    unnamed x56, local copies, waits for them, and re-layouts  22.9 us
    ppermute x6, waiting for transfers between devices, by_distance(): out.append(lax.ppermute(start(d), 'blk', pairs))  18.1 us
    ppermute x21, waiting for transfers between devices, swap(): return lax.ppermute(block, 'op', [(i, i ^ e) for i in range(n_op)])  15.7 us
    pallas_call x5, Pallas kernels, kernel(): pl.pallas_call(body, out_shape=[jax.ShapeDtypeStruct(shape, dtype) for sh...  12.6 us
    ppermute x21, starting transfers between devices, swap(): return lax.ppermute(block, 'op', [(i, i ^ e) for i in range(n_op)])  12.1 us
    all_to_all x2, waiting for transfers between devices, totals(): return lax.all_to_all(parts, ('blk', 'op'), 0, 0, tiled=True)  11.7 us
    ppermute x6, starting transfers between devices, by_distance(): out.append(lax.ppermute(start(d), 'blk', pairs))  8.66 us
    all_to_all x2, starting transfers between devices, totals(): return lax.all_to_all(parts, ('blk', 'op'), 0, 0, tiled=True)  6.99 us
  transfers between devices with their start and end apart: 29, of which 8 were waited for; matrix products, arithmetic and copies ran while one was open for 0% of the time, Pallas kernels for 6%

profile of v4, /device:TPU:0, one launch (start us, length us, event | category | flops | bytes accessed | tf_op | source)
XLA Modules:
  0.0 109.7 jit_solution(15613523490762510472)
XLA Ops:
  0.6 0.0 copy-start
  0.6 3.0 %collective-permute-start = (bf16[2,256,256]{2,1,0:T(8,128)(2,1)}, bf16[2,256,256]{2,1,0:T(8,128)(2,1)S(1)}, u32[]{:S(2)}, u32[]{:S(2)}) collective-permute-start(bf16[2,256,256]{2,1,0:T(8,128)(2,1)} %bitcast.5), channel_id=1, source_target_pairs={{0,2},{1,3},{2,0},{3,1},{4,6},{5,7},{6,4},{7,5},{8,10},{9,11},{10,... | collective-permute-start | bytes 786440 | tf_op jit(solution)/shard_map/ppermute | solution.py:133
  3.6 3.6 %collective-permute-start.14 = (bf16[2,256,256]{2,1,0:T(8,128)(2,1)}, bf16[2,256,256]{2,1,0:T(8,128)(2,1)S(1)}, u32[]{:S(2)}, u32[]{:S(2)}) collective-permute-start(bf16[2,256,256]{2,1,0:T(8,128)(2,1)} %bitcast.6), channel_id=1, source_target_pairs={{0,12},{4,0},{8,4},{12,8},{1,13},{5,1},{9,5},{13,9},{2,14},{6,2},{... | collective-permute-start | bytes 786440 | tf_op jit(solution)/shard_map/ppermute | solution.py:128
  7.3 1.0 collective-permute-start.6
  8.3 0.1 pad_add_fusion.meta
  8.3 1.8 %collective-permute-done._.refs_2_ = bf16[2,256,256]{2,1,0:T(8,128)(2,1)S(1)} collective-permute-done((bf16[2,256,256]{2,1,0:T(8,128)(2,1)}, bf16[2,256,256]{2,1,0:T(8,128)(2,1)S(1)}, u32[]{:S(2)}, u32[]{:S(2)}) %collective-permute-start) | collective-permute-done | bytes 262176 | tf_op jit(solution)/shard_map/ppermute | solution.py:133
  10.2 1.2 %copy-done.3 = bf16[1,256,2048]{2,1,0:T(8,128)(2,1)S(1)} copy-done((bf16[1,256,2048]{2,1,0:T(8,128)(2,1)S(1)}, bf16[1,256,2048]{2,1,0:T(8,128)(2,1)}, u32[]{:S(2)}) %copy-start.3) | copy-done | bytes 1048600
  11.4 0.9 copy-done.13
  12.3 0.7 copy-done.22
  13.0 1.0 shard_map.103
  14.0 1.9 %collective-permute-start.18 = (bf16[256,128]{1,0:T(8,128)(2,1)S(1)}, bf16[256,128]{1,0:T(8,128)(2,1)S(1)}, u32[]{:S(2)}, u32[]{:S(2)}) collective-permute-start(bf16[256,128]{1,0:T(8,128)(2,1)S(1)} %get-tuple-element.36), channel_id=1, source_target_pairs={{0,4},{4,8},{8,12},{12,0},{1,5},{5,9},{9,13},{13,1},{2,6},{6,10},{... | collective-permute-start | bytes 196616 | tf_op jit(solution)/shard_map/ppermute | solution.py:128
  15.9 15.0 %collective-permute-done.10.refs_8_ = bf16[2,256,256]{2,1,0:T(8,128)(2,1)S(1)} collective-permute-done((bf16[2,256,256]{2,1,0:T(8,128)(2,1)}, bf16[2,256,256]{2,1,0:T(8,128)(2,1)S(1)}, u32[]{:S(2)}, u32[]{:S(2)}) %collective-permute-start.10) | collective-permute-done | bytes 262176 | tf_op jit(solution)/shard_map/ppermute | solution.py:128
  30.9 0.5 collective-permute-start.2
  31.4 1.6 %collective-permute-start.19 = (bf16[256,128]{1,0:T(8,128)(2,1)S(1)}, bf16[256,128]{1,0:T(8,128)(2,1)S(1)}, u32[]{:S(2)}, u32[]{:S(2)}) collective-permute-start(bf16[256,128]{1,0:T(8,128)(2,1)S(1)} %get-tuple-element.37), channel_id=1, source_target_pairs={{0,8},{4,12},{8,0},{12,4},{1,9},{5,13},{9,1},{13,5},{2,10},{6,14},... | collective-permute-start | bytes 196616 | tf_op jit(solution)/shard_map/ppermute | solution.py:128
  33.1 0.6 copy-done.14
  33.7 0.6 collective-permute-start.20
  34.2 3.1 %collective-permute-done.19.refs_22_ = bf16[256,128]{1,0:T(8,128)(2,1)S(1)} collective-permute-done((bf16[256,128]{1,0:T(8,128)(2,1)S(1)}, bf16[256,128]{1,0:T(8,128)(2,1)S(1)}, u32[]{:S(2)}, u32[]{:S(2)}) %collective-permute-start.19) | collective-permute-done | bytes 65568 | tf_op jit(solution)/shard_map/ppermute | solution.py:128
  37.4 0.6 copy-done.16
  38.0 1.4 %collective-permute-start.16 = (bf16[2,256,256]{2,1,0:T(8,128)(2,1)S(1)}, bf16[2,256,256]{2,1,0:T(8,128)(2,1)S(1)}, u32[]{:S(2)}, u32[]{:S(2)}) collective-permute-start(bf16[2,256,256]{2,1,0:T(8,128)(2,1)S(1)} %collective-permute-done.14.refs_12_), channel_id=1, source_target_pairs={{0,2},{1,3},{2,0},{3,1},{4,6},{5,7},{6,4},{7,5},{8,10},{9,11},{10,... | collective-permute-start | bytes 786440 | tf_op jit(solution)/shard_map/ppermute | solution.py:133
  39.4 0.6 copy-done.18
  40.0 0.7 collective-permute-start.12
  40.8 0.2 collective-permute-start.11
  40.9 1.4 %collective-permute-start.8 = (bf16[2,256,256]{2,1,0:T(8,128)(2,1)S(1)}, bf16[2,256,256]{2,1,0:T(8,128)(2,1)S(1)}, u32[]{:S(2)}, u32[]{:S(2)}) collective-permute-start(bf16[2,256,256]{2,1,0:T(8,128)(2,1)S(1)} %collective-permute-done.6.refs_4_), channel_id=1, source_target_pairs={{0,2},{1,3},{2,0},{3,1},{4,6},{5,7},{6,4},{7,5},{8,10},{9,11},{10,... | collective-permute-start | bytes 786440 | tf_op jit(solution)/shard_map/ppermute | solution.py:133
  42.3 4.8 %collective-permute-done.16.refs_14_ = bf16[2,256,256]{2,1,0:T(8,128)(2,1)S(1)} collective-permute-done((bf16[2,256,256]{2,1,0:T(8,128)(2,1)S(1)}, bf16[2,256,256]{2,1,0:T(8,128)(2,1)S(1)}, u32[]{:S(2)}, u32[]{:S(2)}) %collective-permute-start.16) | collective-permute-done | bytes 262176 | tf_op jit(solution)/shard_map/ppermute | solution.py:133
  47.2 0.5 collective-permute-start.5
  47.7 5.1 %collective-permute-done.12.refs_10_ = bf16[2,256,256]{2,1,0:T(8,128)(2,1)S(1)} collective-permute-done((bf16[2,256,256]{2,1,0:T(8,128)(2,1)S(1)}, bf16[2,256,256]{2,1,0:T(8,128)(2,1)S(1)}, u32[]{:S(2)}, u32[]{:S(2)}) %collective-permute-start.12) | collective-permute-done | bytes 262176 | tf_op jit(solution)/shard_map/ppermute | solution.py:133
  52.8 0.7 copy-done.7
  53.5 0.5 collective-permute-start.13
  54.0 3.8 %collective-permute-done.8.refs_6_ = bf16[2,256,256]{2,1,0:T(8,128)(2,1)S(1)} collective-permute-done((bf16[2,256,256]{2,1,0:T(8,128)(2,1)S(1)}, bf16[2,256,256]{2,1,0:T(8,128)(2,1)S(1)}, u32[]{:S(2)}, u32[]{:S(2)}) %collective-permute-start.8) | collective-permute-done | bytes 262176 | tf_op jit(solution)/shard_map/ppermute | solution.py:133
  57.8 0.7 copy-done.9
  58.5 0.1 dynamic-slice_bitcast_fusion.right_diag
  58.6 0.7 copy-done.21
  59.3 0.7 copy-done.23
  60.0 0.7 copy-done.24
  60.6 1.4 %shard_map.104 = (s32[32]{0:T(128)S(1)}, s32[4]{0:T(128)S(1)}, s32[4]{0:T(128)S(1)}, f32[4,256,128]{2,1,0:T(8,128)S(1)}) custom-call(s32[2]{0:T(128)S(1)} %pad_add_fusion.meta, s32[4]{0:T(128)S(1)} %copy-done.23, s32[4]{0:T(128)S(1)} %copy-done.24, f32[4,256]{1,0:T(4,128)S(1)} %copy-done.21, f32[1,128]{1,0:T(1,128)S(1)} %dynamic-slice_bitcast_fusion.right_diag, ...), custom_call_target="tpu_custom_call" | custom-call | tf_op jit(solution)/shard_map/pallas_call | solution.py:113
  62.1 0.0 copy-start.11
  62.1 0.7 copy-done.11
  62.8 0.0 copy-start.4
  62.8 0.9 copy-done.4
  63.8 0.9 copy-done.6
  64.7 0.9 copy-done.8
  65.7 0.9 copy-done.10
  66.6 0.9 copy-done.12
  67.6 0.8 copy-done.15
  68.4 0.8 copy-done.17
  69.2 0.8 copy-done.19
  70.1 3.8 %shard_map.105 = (f32[4,256,128]{2,1,0:T(8,128)S(1)}, bf16[4,256,128]{2,1,0:T(8,128)(2,1)S(1)}, f32[16,8,128]{2,1,0:T(8,128)S(1)}, bf16[4,4,2,256,256]{4,3,2,1,0...) custom-call(s32[2]{0:T(128)S(1)} %pad_add_fusion.meta, ...), custom_call_target="tpu_custom_call" | custom-call | flops 805306368 | bytes 8388608 | tf_op jit(solution)/shard_map/pallas_call | solution.py:113
  73.9 2.0 %copy-done.1 = bf16[4,4,2,256,256]{4,3,2,1,0:T(8,128)(2,1)} copy-done((bf16[4,4,2,256,256]{4,3,2,1,0:T(8,128)(2,1)}, bf16[4,4,2,256,256]{4,3,2,1,0:T(8,128)(2,1)S(1)}, u32[]{:S(2)}) %copy-start.1) | copy-done | bytes 4194328
  75.9 0.6 copy-done.20
  76.5 0.7 copy-done.25
  77.2 0.7 copy-done.26
  77.9 0.7 copy-done.27
  78.5 3.5 %all-to-all-start = ((f32[16,8,128]{2,1,0:T(8,128)}), f32[16,8,128]{2,1,0:T(8,128)S(1)}, u32[]{:S(2)}, u32[]{:S(2)}) async-start(f32[16,8,128]{2,1,0:T(8,128)} %copy-done.20), calls=%async_computation | async-start | bytes 131072 | tf_op jit(solution)/shard_map/all_to_all | solution.py:451
  82.0 0.5 collective-permute-start.21
  82.5 1.5 %collective-permute-start.22 = (bf16[2,4,64,128]{3,2,1,0:T(8,128)(2,1)}, bf16[2,4,64,128]{3,2,1,0:T(8,128)(2,1)S(1)}, u32[]{:S(2)}, u32[]{:S(2)}) collective-permute-start(bf16[2,4,64,128]{3,2,1,0:T(8,128)(2,1)} %copy-done.26), channel_id=1, source_target_pairs={{0,2},{1,3},{2,0},{3,1},{4,6},{5,7},{6,4},{7,5},{8,10},{9,11},{10,... | collective-permute-start | bytes 393224 | tf_op jit(solution)/shard_map/ppermute | solution.py:133
  84.0 4.9 %all-to-all-done.refs_4_.parts1 = f32[16,8,128]{2,1,0:T(8,128)S(1)} async-done(((f32[16,8,128]{2,1,0:T(8,128)}), f32[16,8,128]{2,1,0:T(8,128)S(1)}, u32[]{:S(2)}, u32[]{:S(2)}) %all-to-all-start) | async-done | bytes 65568 | tf_op jit(solution)/shard_map/all_to_all | solution.py:451
  88.9 2.2 %copy-done.2 = bf16[4,4,2,256,256]{4,3,2,1,0:T(8,128)(2,1)S(1)} copy-done((bf16[4,4,2,256,256]{4,3,2,1,0:T(8,128)(2,1)S(1)}, bf16[4,4,2,256,256]{4,3,2,1,0:T(8,128)(2,1)}, u32[]{:S(2)}) %copy-start.2) | copy-done | bytes 4194328
  91.1 4.6 %shard_map.106 = (bf16[4,256,128]{2,1,0:T(8,128)(2,1)S(1)}, f32[4,256,128]{2,1,0:T(8,128)S(1)}, f32[16,8,128]{2,1,0:T(8,128)}, bf16[2,4,64,128]{3,2,1,0:T(8,128)...) custom-call(s32[2]{0:T(128)S(1)} %pad_add_fusion.meta, s32[32]{0:T(128)S(1)} %get-tuple-element.33.src, ...), custom_call_target="tpu_custom_call" | custom-call | flops 805306368 | bytes 8388608 | tf_op jit(solution)/shard_map/pallas_call | solution.py:113
  95.7 0.1 collective-permute-start.24
  95.8 0.2 collective-permute-start.25
  96.0 1.7 %collective-permute-start.26 = (bf16[2,4,64,128]{3,2,1,0:T(8,128)(2,1)S(1)}, bf16[2,4,64,128]{3,2,1,0:T(8,128)(2,1)S(1)}, u32[]{:S(2)}, u32[]{:S(2)}) collective-permute-start(bf16[2,4,64,128]{3,2,1,0:T(8,128)(2,1)S(1)} %get-tuple-element.52), channel_id=1, source_target_pairs={{0,3},{1,2},{2,1},{3,0},{4,7},{5,6},{6,5},{7,4},{8,11},{9,10},{10,... | collective-permute-start | bytes 393224 | tf_op jit(solution)/shard_map/ppermute | solution.py:133
  97.6 3.5 %all-to-all-start.1 = ((f32[16,8,128]{2,1,0:T(8,128)}), f32[16,8,128]{2,1,0:T(8,128)S(1)}, u32[]{:S(2)}, u32[]{:S(2)}) async-start(f32[16,8,128]{2,1,0:T(8,128)} %get-tuple-element.44), calls=%async_computation.1 | async-start | bytes 131072 | tf_op jit(solution)/shard_map/all_to_all | solution.py:451
  101.2 6.8 %all-to-all-done.1.parts2 = f32[16,8,128]{2,1,0:T(8,128)S(1)} async-done(((f32[16,8,128]{2,1,0:T(8,128)}), f32[16,8,128]{2,1,0:T(8,128)S(1)}, u32[]{:S(2)}, u32[]{:S(2)}) %all-to-all-start.1) | async-done | bytes 65568 | tf_op jit(solution)/shard_map/all_to_all | solution.py:451
  108.0 1.7 %shard_map.107 = (bf16[4,64,512]{2,1,0:T(8,128)(2,1)}, bf16[4,64,512]{2,1,0:T(8,128)(2,1)}, f32[1]{0:T(128)}) custom-call(s32[2]{0:T(128)S(1)} %pad_add_fusion.meta, s32[4]{0:T(128)S(1)} %get-tuple-element.32.slots, f32[16,8,128]{2,1,0:T(8,128)S(1)} %all-to-all-done.refs_4_.parts1, f32[16,8,128]{2,1,0:T(8,128)S(1)} %all-to-all-done.1.parts2, ...), custom_call_target="tpu_custom_call" | custom-call | bytes 4194304 | tf_op jit(solution)/shard_map/pallas_call | solution.py:113
  (57 shorter events, 0.1 us)
Async XLA Ops:
  0.6 57.9 %copy-start = (f32[512]{0:T(512)S(1)}, f32[512]{0:T(512)}, u32[]{:S(2)}) copy-start(f32[512]{0:T(512)} %param.15) | copy-start | bytes 6148
  0.6 9.5 %collective-permute-start = (bf16[2,256,256]{2,1,0:T(8,128)(2,1)}, bf16[2,256,256]{2,1,0:T(8,128)(2,1)S(1)}, u32[]{:S(2)}, u32[]{:S(2)}) collective-permute-start(bf16[2,256,256]{2,1,0:T(8,128)(2,1)} %bitcast.5), channel_id=1, source_target_pairs={{0,2},{1,3},{2,0},{3,1},{4,6},{5,7},{6,4},{7,5},{8,10},{9,11},{10,... | collective-permute-start | bytes 786440 | tf_op jit(solution)/shard_map/ppermute | solution.py:133
  3.6 12.3 %collective-permute-start.14 = (bf16[2,256,256]{2,1,0:T(8,128)(2,1)}, bf16[2,256,256]{2,1,0:T(8,128)(2,1)S(1)}, u32[]{:S(2)}, u32[]{:S(2)}) collective-permute-start(bf16[2,256,256]{2,1,0:T(8,128)(2,1)} %bitcast.6), channel_id=1, source_target_pairs={{0,12},{4,0},{8,4},{12,8},{1,13},{5,1},{9,5},{13,9},{2,14},{6,2},{... | collective-permute-start | bytes 786440 | tf_op jit(solution)/shard_map/ppermute | solution.py:128
  7.3 23.6 %collective-permute-start.10 = (bf16[2,256,256]{2,1,0:T(8,128)(2,1)}, bf16[2,256,256]{2,1,0:T(8,128)(2,1)S(1)}, u32[]{:S(2)}, u32[]{:S(2)}) collective-permute-start(bf16[2,256,256]{2,1,0:T(8,128)(2,1)} %bitcast.7), channel_id=1, source_target_pairs={{0,8},{4,12},{8,0},{12,4},{1,9},{5,13},{9,1},{13,5},{2,10},{6,14},... | collective-permute-start | bytes 786440 | tf_op jit(solution)/shard_map/ppermute | solution.py:128
  7.3 24.2 %collective-permute-start.6 = (bf16[2,256,256]{2,1,0:T(8,128)(2,1)}, bf16[2,256,256]{2,1,0:T(8,128)(2,1)S(1)}, u32[]{:S(2)}, u32[]{:S(2)}) collective-permute-start(bf16[2,256,256]{2,1,0:T(8,128)(2,1)} %bitcast.8), channel_id=1, source_target_pairs={{0,4},{4,8},{8,12},{12,0},{1,5},{5,9},{9,13},{13,1},{2,6},{6,10},{... | collective-permute-start | bytes 786440 | tf_op jit(solution)/shard_map/ppermute | solution.py:128
  8.3 23.2 %collective-permute-start.4 = (bf16[2,256,256]{2,1,0:T(8,128)(2,1)}, bf16[2,256,256]{2,1,0:T(8,128)(2,1)S(1)}, u32[]{:S(2)}, u32[]{:S(2)}) collective-permute-start(bf16[2,256,256]{2,1,0:T(8,128)(2,1)} %bitcast.9), channel_id=1, source_target_pairs={{0,1},{1,0},{2,3},{3,2},{4,5},{5,4},{6,7},{7,6},{8,9},{9,8},{10,11... | collective-permute-start | bytes 786440 | tf_op jit(solution)/shard_map/ppermute | solution.py:133
  10.2 1.2 %copy-start.3 = (bf16[1,256,2048]{2,1,0:T(8,128)(2,1)S(1)}, bf16[1,256,2048]{2,1,0:T(8,128)(2,1)}, u32[]{:S(2)}) copy-start(bf16[1,256,2048]{2,1,0:T(8,128)(2,1)} %psi.1) | copy-start | bytes 3145732
  11.4 0.9 copy-start.13
  12.3 0.7 copy-start.22
  14.0 19.0 %collective-permute-start.18 = (bf16[256,128]{1,0:T(8,128)(2,1)S(1)}, bf16[256,128]{1,0:T(8,128)(2,1)S(1)}, u32[]{:S(2)}, u32[]{:S(2)}) collective-permute-start(bf16[256,128]{1,0:T(8,128)(2,1)S(1)} %get-tuple-element.36), channel_id=1, source_target_pairs={{0,4},{4,8},{8,12},{12,0},{1,5},{5,9},{9,13},{13,1},{2,6},{6,10},{... | collective-permute-start | bytes 196616 | tf_op jit(solution)/shard_map/ppermute | solution.py:128
  15.9 24.1 %collective-permute-start.1 = (bf16[272,128]{1,0:T(8,128)(2,1)S(1)}, bf16[272,128]{1,0:T(8,128)(2,1)S(1)}, u32[]{:S(2)}, u32[]{:S(2)}) collective-permute-start(bf16[272,128]{1,0:T(8,128)(2,1)S(1)} %get-tuple-element.29), channel_id=1, source_target_pairs={{0,1},{1,0},{2,3},{3,2},{4,5},{5,4},{6,7},{7,6},{8,9},{9,8},{10,11... | collective-permute-start | bytes 208904 | tf_op jit(solution)/shard_map/ppermute | solution.py:133
  30.9 9.9 %collective-permute-start.2 = (bf16[272,128]{1,0:T(8,128)(2,1)S(1)}, bf16[272,128]{1,0:T(8,128)(2,1)S(1)}, u32[]{:S(2)}, u32[]{:S(2)}) collective-permute-start(bf16[272,128]{1,0:T(8,128)(2,1)S(1)} %get-tuple-element.30), channel_id=1, source_target_pairs={{0,2},{1,3},{2,0},{3,1},{4,6},{5,7},{6,4},{7,5},{8,10},{9,11},{10,... | collective-permute-start | bytes 208904 | tf_op jit(solution)/shard_map/ppermute | solution.py:133
  31.4 9.5 %collective-permute-start.3 = (bf16[272,128]{1,0:T(8,128)(2,1)S(1)}, bf16[272,128]{1,0:T(8,128)(2,1)S(1)}, u32[]{:S(2)}, u32[]{:S(2)}) collective-permute-start(bf16[272,128]{1,0:T(8,128)(2,1)S(1)} %get-tuple-element.31), channel_id=1, source_target_pairs={{0,3},{1,2},{2,1},{3,0},{4,7},{5,6},{6,5},{7,4},{8,11},{9,10},{10,... | collective-permute-start | bytes 208904 | tf_op jit(solution)/shard_map/ppermute | solution.py:133
  31.4 5.9 %collective-permute-start.19 = (bf16[256,128]{1,0:T(8,128)(2,1)S(1)}, bf16[256,128]{1,0:T(8,128)(2,1)S(1)}, u32[]{:S(2)}, u32[]{:S(2)}) collective-permute-start(bf16[256,128]{1,0:T(8,128)(2,1)S(1)} %get-tuple-element.37), channel_id=1, source_target_pairs={{0,8},{4,12},{8,0},{12,4},{1,9},{5,13},{9,1},{13,5},{2,10},{6,14},... | collective-permute-start | bytes 196616 | tf_op jit(solution)/shard_map/ppermute | solution.py:128
  33.1 0.6 copy-start.14
  33.7 5.7 %collective-permute-start.20 = (bf16[256,128]{1,0:T(8,128)(2,1)S(1)}, bf16[256,128]{1,0:T(8,128)(2,1)S(1)}, u32[]{:S(2)}, u32[]{:S(2)}) collective-permute-start(bf16[256,128]{1,0:T(8,128)(2,1)S(1)} %get-tuple-element.38), channel_id=1, source_target_pairs={{0,12},{4,0},{8,4},{12,8},{1,13},{5,1},{9,5},{13,9},{2,14},{6,2},{... | collective-permute-start | bytes 196616 | tf_op jit(solution)/shard_map/ppermute | solution.py:128
  37.4 0.6 copy-start.16
  38.0 9.2 %collective-permute-start.16 = (bf16[2,256,256]{2,1,0:T(8,128)(2,1)S(1)}, bf16[2,256,256]{2,1,0:T(8,128)(2,1)S(1)}, u32[]{:S(2)}, u32[]{:S(2)}) collective-permute-start(bf16[2,256,256]{2,1,0:T(8,128)(2,1)S(1)} %collective-permute-done.14.refs_12_), channel_id=1, source_target_pairs={{0,2},{1,3},{2,0},{3,1},{4,6},{5,7},{6,4},{7,5},{8,10},{9,11},{10,... | collective-permute-start | bytes 786440 | tf_op jit(solution)/shard_map/ppermute | solution.py:133
  39.4 0.6 copy-start.18
  40.0 7.1 %collective-permute-start.15 = (bf16[2,256,256]{2,1,0:T(8,128)(2,1)S(1)}, bf16[2,256,256]{2,1,0:T(8,128)(2,1)S(1)}, u32[]{:S(2)}, u32[]{:S(2)}) collective-permute-start(bf16[2,256,256]{2,1,0:T(8,128)(2,1)S(1)} %collective-permute-done.14.refs_12_), channel_id=1, source_target_pairs={{0,1},{1,0},{2,3},{3,2},{4,5},{5,4},{6,7},{7,6},{8,9},{9,8},{10,11... | collective-permute-start | bytes 786440 | tf_op jit(solution)/shard_map/ppermute | solution.py:133
  40.0 12.7 %collective-permute-start.12 = (bf16[2,256,256]{2,1,0:T(8,128)(2,1)S(1)}, bf16[2,256,256]{2,1,0:T(8,128)(2,1)S(1)}, u32[]{:S(2)}, u32[]{:S(2)}) collective-permute-start(bf16[2,256,256]{2,1,0:T(8,128)(2,1)S(1)} %collective-permute-done.10.refs_8_), channel_id=1, source_target_pairs={{0,2},{1,3},{2,0},{3,1},{4,6},{5,7},{6,4},{7,5},{8,10},{9,11},{10,... | collective-permute-start | bytes 786440 | tf_op jit(solution)/shard_map/ppermute | solution.py:133
  40.8 12.0 %collective-permute-start.11 = (bf16[2,256,256]{2,1,0:T(8,128)(2,1)S(1)}, bf16[2,256,256]{2,1,0:T(8,128)(2,1)S(1)}, u32[]{:S(2)}, u32[]{:S(2)}) collective-permute-start(bf16[2,256,256]{2,1,0:T(8,128)(2,1)S(1)} %collective-permute-done.10.refs_8_), channel_id=1, source_target_pairs={{0,1},{1,0},{2,3},{3,2},{4,5},{5,4},{6,7},{7,6},{8,9},{9,8},{10,11... | collective-permute-start | bytes 786440 | tf_op jit(solution)/shard_map/ppermute | solution.py:133
  40.9 16.9 %collective-permute-start.8 = (bf16[2,256,256]{2,1,0:T(8,128)(2,1)S(1)}, bf16[2,256,256]{2,1,0:T(8,128)(2,1)S(1)}, u32[]{:S(2)}, u32[]{:S(2)}) collective-permute-start(bf16[2,256,256]{2,1,0:T(8,128)(2,1)S(1)} %collective-permute-done.6.refs_4_), channel_id=1, source_target_pairs={{0,2},{1,3},{2,0},{3,1},{4,6},{5,7},{6,4},{7,5},{8,10},{9,11},{10,... | collective-permute-start | bytes 786440 | tf_op jit(solution)/shard_map/ppermute | solution.py:133
  47.1 14.9 %collective-permute-start.7 = (bf16[2,256,256]{2,1,0:T(8,128)(2,1)S(1)}, bf16[2,256,256]{2,1,0:T(8,128)(2,1)S(1)}, u32[]{:S(2)}, u32[]{:S(2)}) collective-permute-start(bf16[2,256,256]{2,1,0:T(8,128)(2,1)S(1)} %collective-permute-done.6.refs_4_), channel_id=1, source_target_pairs={{0,1},{1,0},{2,3},{3,2},{4,5},{5,4},{6,7},{7,6},{8,9},{9,8},{10,11... | collective-permute-start | bytes 786440 | tf_op jit(solution)/shard_map/ppermute | solution.py:133
  47.2 15.6 %collective-permute-start.5 = (bf16[2,256,256]{2,1,0:T(8,128)(2,1)S(1)}, bf16[2,256,256]{2,1,0:T(8,128)(2,1)}, u32[]{:S(2)}, u32[]{:S(2)}) collective-permute-start(bf16[2,256,256]{2,1,0:T(8,128)(2,1)S(1)} %collective-permute-done._.refs_2_), channel_id=1, source_target_pairs={{0,1},{1,0},{2,3},{3,2},{4,5},{5,4},{6,7},{7,6},{8,9},{9,8},{10,11... | collective-permute-start | bytes 786440 | tf_op jit(solution)/shard_map/ppermute | solution.py:133
  52.8 10.0 %copy-start.5 = (bf16[2,256,256]{2,1,0:T(8,128)(2,1)}, bf16[2,256,256]{2,1,0:T(8,128)(2,1)S(1)}, u32[]{:S(2)}) copy-start(bf16[2,256,256]{2,1,0:T(8,128)(2,1)S(1)} %collective-permute-done.12.refs_10_) | copy-start | bytes 786436
  52.8 10.0 %collective-permute-start.17 = (bf16[2,256,256]{2,1,0:T(8,128)(2,1)S(1)}, bf16[2,256,256]{2,1,0:T(8,128)(2,1)}, u32[]{:S(2)}, u32[]{:S(2)}) collective-permute-start(bf16[2,256,256]{2,1,0:T(8,128)(2,1)S(1)} %collective-permute-done.16.refs_14_), channel_id=1, source_target_pairs={{0,1},{1,0},{2,3},{3,2},{4,5},{5,4},{6,7},{7,6},{8,9},{9,8},{10,11... | collective-permute-start | bytes 786440 | tf_op jit(solution)/shard_map/ppermute | solution.py:133
  52.8 0.7 copy-start.7
  53.5 9.3 %collective-permute-start.13 = (bf16[2,256,256]{2,1,0:T(8,128)(2,1)S(1)}, bf16[2,256,256]{2,1,0:T(8,128)(2,1)}, u32[]{:S(2)}, u32[]{:S(2)}) collective-permute-start(bf16[2,256,256]{2,1,0:T(8,128)(2,1)S(1)} %collective-permute-done.12.refs_10_), channel_id=1, source_target_pairs={{0,1},{1,0},{2,3},{3,2},{4,5},{5,4},{6,7},{7,6},{8,9},{9,8},{10,11... | collective-permute-start | bytes 786440 | tf_op jit(solution)/shard_map/ppermute | solution.py:133
  57.8 4.9 %collective-permute-start.9 = (bf16[2,256,256]{2,1,0:T(8,128)(2,1)S(1)}, bf16[2,256,256]{2,1,0:T(8,128)(2,1)}, u32[]{:S(2)}, u32[]{:S(2)}) collective-permute-start(bf16[2,256,256]{2,1,0:T(8,128)(2,1)S(1)} %collective-permute-done.8.refs_6_), channel_id=1, source_target_pairs={{0,1},{1,0},{2,3},{3,2},{4,5},{5,4},{6,7},{7,6},{8,9},{9,8},{10,11... | collective-permute-start | bytes 786440 | tf_op jit(solution)/shard_map/ppermute | solution.py:133
  57.8 0.7 copy-start.9
  58.6 0.7 copy-start.21
  59.3 0.7 copy-start.23
  60.0 0.7 copy-start.24
  62.1 0.7 copy-start.11
  62.8 1.0 copy-start.4
  63.8 0.9 copy-start.6
  64.7 0.9 copy-start.8
  65.7 0.9 copy-start.10
  66.6 0.9 copy-start.12
  67.6 0.8 copy-start.15
  68.4 0.8 copy-start.17
  69.2 0.8 copy-start.19
  73.9 2.0 %copy-start.1 = (bf16[4,4,2,256,256]{4,3,2,1,0:T(8,128)(2,1)}, bf16[4,4,2,256,256]{4,3,2,1,0:T(8,128)(2,1)S(1)}, u32[]{:S(2)}) copy-start(bf16[4,4,2,256,256]{4,3,2,1,0:T(8,128)(2,1)S(1)} %get-tuple-element.41.left_in) | copy-start | bytes 12582916
  75.9 0.6 copy-start.20
  76.5 0.7 copy-start.25
  77.2 0.7 copy-start.26
  77.9 0.7 copy-start.27
  78.5 10.4 %all-to-all-start = ((f32[16,8,128]{2,1,0:T(8,128)}), f32[16,8,128]{2,1,0:T(8,128)S(1)}, u32[]{:S(2)}, u32[]{:S(2)}) async-start(f32[16,8,128]{2,1,0:T(8,128)} %copy-done.20), calls=%async_computation | async-start | bytes 131072 | tf_op jit(solution)/shard_map/all_to_all | solution.py:451
  82.0 14.0 %collective-permute-start.21 = (bf16[2,4,64,128]{3,2,1,0:T(8,128)(2,1)}, bf16[2,4,64,128]{3,2,1,0:T(8,128)(2,1)S(1)}, u32[]{:S(2)}, u32[]{:S(2)}) collective-permute-start(bf16[2,4,64,128]{3,2,1,0:T(8,128)(2,1)} %copy-done.27), channel_id=1, source_target_pairs={{0,1},{1,0},{2,3},{3,2},{4,5},{5,4},{6,7},{7,6},{8,9},{9,8},{10,11... | collective-permute-start | bytes 393224 | tf_op jit(solution)/shard_map/ppermute | solution.py:133
  82.5 18.6 %collective-permute-start.22 = (bf16[2,4,64,128]{3,2,1,0:T(8,128)(2,1)}, bf16[2,4,64,128]{3,2,1,0:T(8,128)(2,1)S(1)}, u32[]{:S(2)}, u32[]{:S(2)}) collective-permute-start(bf16[2,4,64,128]{3,2,1,0:T(8,128)(2,1)} %copy-done.26), channel_id=1, source_target_pairs={{0,2},{1,3},{2,0},{3,1},{4,6},{5,7},{6,4},{7,5},{8,10},{9,11},{10,... | collective-permute-start | bytes 393224 | tf_op jit(solution)/shard_map/ppermute | solution.py:133
  84.0 17.1 %collective-permute-start.23 = (bf16[2,4,64,128]{3,2,1,0:T(8,128)(2,1)}, bf16[2,4,64,128]{3,2,1,0:T(8,128)(2,1)S(1)}, u32[]{:S(2)}, u32[]{:S(2)}) collective-permute-start(bf16[2,4,64,128]{3,2,1,0:T(8,128)(2,1)} %copy-done.25), channel_id=1, source_target_pairs={{0,3},{1,2},{2,1},{3,0},{4,7},{5,6},{6,5},{7,4},{8,11},{9,10},{10,... | collective-permute-start | bytes 393224 | tf_op jit(solution)/shard_map/ppermute | solution.py:133
  88.9 2.2 %copy-start.2 = (bf16[4,4,2,256,256]{4,3,2,1,0:T(8,128)(2,1)S(1)}, bf16[4,4,2,256,256]{4,3,2,1,0:T(8,128)(2,1)}, u32[]{:S(2)}) copy-start(bf16[4,4,2,256,256]{4,3,2,1,0:T(8,128)(2,1)} %copy-done.1) | copy-start | bytes 12582916
  95.7 12.3 %collective-permute-start.24 = (bf16[2,4,64,128]{3,2,1,0:T(8,128)(2,1)}, bf16[2,4,64,128]{3,2,1,0:T(8,128)(2,1)S(1)}, u32[]{:S(2)}, u32[]{:S(2)}) collective-permute-start(bf16[2,4,64,128]{3,2,1,0:T(8,128)(2,1)} %get-tuple-element.50), channel_id=1, source_target_pairs={{0,1},{1,0},{2,3},{3,2},{4,5},{5,4},{6,7},{7,6},{8,9},{9,8},{10,11... | collective-permute-start | bytes 393224 | tf_op jit(solution)/shard_map/ppermute | solution.py:133
  95.8 12.2 %collective-permute-start.25 = (bf16[2,4,64,128]{3,2,1,0:T(8,128)(2,1)}, bf16[2,4,64,128]{3,2,1,0:T(8,128)(2,1)S(1)}, u32[]{:S(2)}, u32[]{:S(2)}) collective-permute-start(bf16[2,4,64,128]{3,2,1,0:T(8,128)(2,1)} %get-tuple-element.51), channel_id=1, source_target_pairs={{0,2},{1,3},{2,0},{3,1},{4,6},{5,7},{6,4},{7,5},{8,10},{9,11},{10,... | collective-permute-start | bytes 393224 | tf_op jit(solution)/shard_map/ppermute | solution.py:133
  96.0 12.0 %collective-permute-start.26 = (bf16[2,4,64,128]{3,2,1,0:T(8,128)(2,1)S(1)}, bf16[2,4,64,128]{3,2,1,0:T(8,128)(2,1)S(1)}, u32[]{:S(2)}, u32[]{:S(2)}) collective-permute-start(bf16[2,4,64,128]{3,2,1,0:T(8,128)(2,1)S(1)} %get-tuple-element.52), channel_id=1, source_target_pairs={{0,3},{1,2},{2,1},{3,0},{4,7},{5,6},{6,5},{7,4},{8,11},{9,10},{10,... | collective-permute-start | bytes 393224 | tf_op jit(solution)/shard_map/ppermute | solution.py:133
  97.6 10.4 %all-to-all-start.1 = ((f32[16,8,128]{2,1,0:T(8,128)}), f32[16,8,128]{2,1,0:T(8,128)S(1)}, u32[]{:S(2)}, u32[]{:S(2)}) async-start(f32[16,8,128]{2,1,0:T(8,128)} %get-tuple-element.44), calls=%async_computation.1 | async-start | bytes 131072 | tf_op jit(solution)/shard_map/all_to_all | solution.py:451

commit v5 on v4

--- a/solution.py
+++ b/solution.py
@@ -112,21 +112,20 @@
 def kernel(body, ins, outs, scratch=(), flops=0, nbytes=0):
     return pl.pallas_call(
         body,
-        out_shape=[jax.ShapeDtypeStruct(shape, dtype) for shape, dtype, _ in outs],
+        out_shape=[
+            HBM(shape, dtype) if space == HBM else jax.ShapeDtypeStruct(shape, dtype)
+            for shape, dtype, space in outs
+        ],
         in_specs=[pl.BlockSpec(memory_space=space) for _, space in ins],
         out_specs=[pl.BlockSpec(memory_space=space) for _, _, space in outs],
         scratch_shapes=list(scratch),
         compiler_params=pltpu.CompilerParams(vmem_limit_bytes=VMEM_LIMIT),
         cost_estimate=pl.CostEstimate(flops=flops, bytes_accessed=nbytes, transcendentals=0),
-    )(*[array for array, _ in ins])
-
-
-def by_distance(own, n_blk, start):
-    out = [own]
-    for d in range(1, n_blk):
-        pairs = [(i, (i + d) % n_blk) for i in range(n_blk)]
-        out.append(lax.ppermute(start(d), "blk", pairs))
-    return out
+    )(*[pltpu.with_memory_space_constraint(x, HBM) if space == HBM else x for x, space in ins])
+
+
+def onward(block, d, n_blk):
+    return lax.ppermute(block, "blk", [(i, (i + d) % n_blk) for i in range(n_blk)])
 
 
 def swap(block, e, n_op):
@@ -134,8 +133,9 @@
 
 
 def gather_left(own, n_blk, n_op):
-    held = dict(enumerate(by_distance(own, n_blk, lambda d: own)))
-    held = {(d, 0): block for d, block in held.items()}
+    held = {(0, 0): own}
+    for d in range(1, n_blk):
+        held[d, 0] = onward(held[d - 1, 0], 1, n_blk)
     bit = n_op // 2
     while bit:
         held.update({(d, e ^ bit): swap(block, bit, n_op) for (d, e), block in held.items()})
@@ -143,12 +143,16 @@
     return held
 
 
-def pack_body(n_blk, n_op, meta, shift, psi, right, _, *outs):
+def place_of():
+    return lax.axis_index("blk"), lax.axis_index("op")
+
+
+def pack_body(n_blk, n_op, shift, psi, right, _, *outs):
     psi_out, right_out, sems = outs[:n_blk], outs[n_blk : n_blk + n_op], outs[-1]
     cols = psi_out[0].shape[1]
     terms, _, width, _ = right.shape
     per = cols // width
-    own_blk, own_op = meta[0], meta[1]
+    own_blk, own_op = place_of()
     copies = []
     for d in range(n_blk):
         there = lax.rem(own_blk + d, n_blk)
@@ -165,31 +169,32 @@
     unit = (square[0] == square[1]).astype(jnp.bfloat16)
     for e in range(n_op):
         there = (own_op ^ e) * per
-        right_out[e][...] = jnp.zeros_like(right_out[e])
         for k in range(terms):
-            for r in range(per):
-                row = (k * per + r) * width
-                turned = lax.dot_general(
+            turned = [
+                lax.dot_general(
                     right[k, there + r], unit, (((0,), (0,)), ((), ())),
                     preferred_element_type=jnp.float32,
                 )
-                right_out[e][row : row + width, r * width : (r + 1) * width] = turned.astype(jnp.bfloat16)
-        right_out[e][terms * cols :] = line.astype(jnp.bfloat16)
+                for r in range(per)
+            ]
+            line_up = jnp.concatenate(turned, axis=1).astype(jnp.bfloat16)
+            right_out[e][k * width : (k + 1) * width] = line_up
+        right_out[e][terms * width :] = line.astype(jnp.bfloat16)
     for copy in copies:
         copy.wait()
 
 
-def table_body(n_blk, n_op, terms, meta, sector, width, left_diag, right_diag, *refs):
+def table_body(n_blk, n_op, terms, sector, width, left_diag, right_diag, *refs):
     tails, src, widths, slots, dmat = refs[:n_op], *refs[n_op:]
-    cols = tails[0].shape[1]
-    own_blk = meta[0]
+    rows, cols = tails[0].shape
+    own_blk, own_op = place_of()
     lane = lax.broadcasted_iota(jnp.int32, (16, cols), 1)
     for d in range(n_blk):
         slot = lax.rem(own_blk - d + n_blk, n_blk)
         slots[d] = slot
         widths[d] = width[sector[slot]]
     for e in range(n_op):
-        tail = tails[e][terms * cols :].astype(jnp.float32)
+        tail = tails[e][rows - 16 :].astype(jnp.float32)
         for k in range(terms):
             shift = jnp.max(jnp.where(lane == k, tail, -1e9)).astype(jnp.int32)
             for t in range(n_blk):
@@ -198,9 +203,10 @@
                 for d in range(n_blk):
                     found = jnp.where(sector[slots[d]] == want, d, found)
                 src[(t * n_op + e) * terms + k] = found
+    on_cols = right_diag[:, pl.ds(pl.multiple_of(own_op * cols, LANES), cols)]
     for d in range(n_blk):
         row = left_diag[pl.ds(slots[d], 1), :]
-        dmat[d] = jnp.transpose(jnp.broadcast_to(row, (cols, row.shape[1]))) + right_diag[...]
+        dmat[d] = jnp.transpose(jnp.broadcast_to(row, (cols, row.shape[1]))) + on_cols
 
 
 def row_mask(width, shape):
@@ -224,11 +230,24 @@
         out[d] = tile
 
 
+def by_block(packed, terms, cols):
+    width = (packed.shape[0] - 16) // terms
+    lane = lax.broadcasted_iota(jnp.int32, (width, cols), 1)
+    parts = []
+    for k in range(terms):
+        block = packed[k * width : (k + 1) * width].astype(jnp.float32)
+        for r in range(cols // width):
+            inside = (lane >= r * width) & (lane < (r + 1) * width)
+            parts.append(jnp.where(inside, block, 0.0).astype(jnp.bfloat16))
+    return jnp.concatenate(parts, axis=0)
+
+
 def apply_h(src, field, left, right, inter, emit):
     n_blk, n_op = inter.shape[0] - 1, len(right)
     rows, cols = inter.shape[2], inter.shape[3]
     terms = inter.shape[1] // n_op
     inter[n_blk] = jnp.zeros_like(inter[n_blk])
+    diagonal = [by_block(ref, terms, cols) for ref in right]
     for d in range(n_blk):
         block = field(d)
         for e in range(n_op):
@@ -241,7 +260,7 @@
         for e in range(n_op):
             js = range(e * terms, (e + 1) * terms)
             moved = jnp.concatenate([inter[src[t * n_op * terms + j], j] for j in js], axis=1)
-            part = jnp.dot(moved, right[e][: terms * cols], preferred_element_type=jnp.float32)
+            part = jnp.dot(moved, diagonal[e], preferred_element_type=jnp.float32)
             total = part if total is None else total + part
         emit(t, total)
 
@@ -251,14 +270,15 @@
     return left, refs[n_blk * n_op :]
 
 
-def send_rows(own_op, sends, j, d, ref):
+def send_rows(sends, j, d, ref):
+    _, own_op = place_of()
     step = sends[0].shape[2]
     for e, send in enumerate(sends, 1):
         start = pl.multiple_of((own_op ^ e) * step, step)
         send[j, d] = ref[d, pl.ds(start, step)].astype(send.dtype)
 
 
-def first_body(n_blk, n_op, meta, src, widths, *refs):
+def first_body(n_blk, n_op, src, widths, *refs):
     left, refs = split_refs(refs, n_blk, n_op)
     right, psi, refs = refs[:n_op], refs[n_op : n_op + n_blk], refs[n_op + n_blk :]
     dmat, sig_out, raw_out, dots_out, left_out = refs[:5]
@@ -286,8 +306,8 @@
         sig_out[d] = sigma
         sums[0] = sums[0] + fold(raw * raw)
         sums[1] = sums[1] + fold(raw * sigma)
-        send_rows(meta[1], sends, 0, d, raw_out)
-        send_rows(meta[1], sends, 1, d, sig_out)
+        send_rows(sends, 0, d, raw_out)
+        send_rows(sends, 1, d, sig_out)
 
     apply_h(src, field, lambda d, e: left[d][e][...], right, inter, emit)
     spread([whole(x) for x in sums], dots_out)
@@ -301,7 +321,7 @@
     return scale, tot[1:2] * scale * scale
 
 
-def second_body(n_blk, n_op, count, meta, src, widths, left_in, *refs):
+def second_body(n_blk, n_op, count, src, widths, left_in, *refs):
     right, refs = refs[:n_op], refs[n_op:]
     parts, raw_in, sig_in, dmat, f_out, t_out, dots_out = refs[:7]
     sends, inter, corr, held, sems = refs[7:-4], *refs[-4:]
@@ -337,8 +357,8 @@
         sigma = sig_in[d] * scale
         prods = (fld * fld, vec * fld, vec * image, fld * sigma, fld * image)
         sums[:] = [one + fold(prod) for one, prod in zip(sums, prods)]
-        send_rows(meta[1], sends, 0, d, f_out)
-        send_rows(meta[1], sends, 1, d, t_out)
+        send_rows(sends, 0, d, f_out)
+        send_rows(sends, 1, d, t_out)
 
     apply_h(src, field, lambda d, e: held[d, e], right, inter, emit)
     spread([vv, vc, vs] + [whole(x) for x in sums], dots_out)
@@ -359,11 +379,11 @@
     return sine, jnp.where(upward, -cosine, cosine), 0.5 * (theta + h_two) - 0.5 * size
 
 
-def third_body(n_blk, n_op, count, meta, slots, parts1, parts2, raw_in, sig_in, f_in, t_in, *refs):
+def third_body(n_blk, n_op, count, slots, parts1, parts2, raw_in, sig_in, f_in, t_in, *refs):
     got1, got2 = refs[: n_op - 1], refs[n_op - 1 : 2 * (n_op - 1)]
     new_out, res_out, energy_out = refs[2 * (n_op - 1) :]
     step, cols = new_out.shape[1], raw_in.shape[2]
-    own_blk, own_op = meta[0], meta[1]
+    own_blk, own_op = place_of()
     scale, theta = norm_theta(parts1[...], count)
     vv, vc, vs, ff, vf, vt, fs, ft = (parts2[:, j, :] for j in range(8))
 
@@ -404,13 +424,11 @@
 ):
     n_blk, n_op = lax.axis_size("blk"), lax.axis_size("op")
     _, rows, ncols = psi.shape
-    terms = right_ops.shape[0]
+    terms, _, width, _ = right_ops.shape
     cols = diag_right.shape[0] // n_op
     step = rows // n_op
     count = float(n_blk * rows * ncols)
     n_dev = n_blk * n_op
-    own_blk, own_op = lax.axis_index("blk"), lax.axis_index("op")
-    meta = jnp.stack([own_blk, own_op]).astype(jnp.int32)
     bf16, f32 = jnp.bfloat16, jnp.float32
 
     left = gather_left(left_ops[:, 0], n_blk, n_op)
@@ -418,26 +436,24 @@
 
     sent = kernel(
         functools.partial(pack_body, n_blk, n_op),
-        [(meta, SMEM), (term_shift, SMEM), (psi, HBM), (right_ops, VMEM), (left[0, n_op // 2], ANY)],
-        [((rows, cols), bf16, VMEM)] * n_blk + [((terms * cols + 16, cols), bf16, VMEM)] * n_op,
+        [(term_shift, SMEM), (psi, ANY), (right_ops, VMEM), (left[0, 1], ANY)],
+        [((rows, cols), bf16, VMEM)] * n_blk + [((terms * width + 16, cols), bf16, VMEM)] * n_op,
         [pltpu.SemaphoreType.DMA((n_blk,))],
         nbytes=1 << 20,
     )
     right = [sent[n_blk]] + [swap(sent[n_blk + e], e, n_op) for e in range(1, n_op)]
     right_ins = [(block, VMEM) for block in right]
-    psi_ins = [(block, VMEM) for block in by_distance(sent[0], n_blk, lambda d: sent[d])]
-    dr = lax.dynamic_slice_in_dim(diag_right, own_op * cols, cols, 0)
+    psi_ins = [(sent[0], VMEM)] + [(onward(sent[d], d, n_blk), VMEM) for d in range(1, n_blk)]
     src, widths, slots, dmat = kernel(
         functools.partial(table_body, n_blk, n_op, terms),
-        [(meta, SMEM), (slot_sector, SMEM), (sector_width, SMEM)]
-        + [(diag_left, VMEM), (dr[None], VMEM)]
+        [(slot_sector, SMEM), (sector_width, SMEM), (diag_left, VMEM), (diag_right[None], VMEM)]
         + right_ins,
         [((n_blk * n_op * terms,), jnp.int32, SMEM)]
         + [((n_blk,), jnp.int32, SMEM)] * 2
         + [((n_blk, rows, cols), f32, VMEM)],
     )
 
-    tables = [(meta, SMEM), (src, SMEM), (widths, SMEM)]
+    tables = [(src, SMEM), (widths, SMEM)]
     wide = ((n_blk, rows, cols), f32, VMEM)
     narrow = ((n_blk, rows, cols), bf16, VMEM)
     dots = ((n_dev, 8, LANES), f32, VMEM)
@@ -471,7 +487,7 @@
     final = ((n_blk, step, n_op * cols), bf16, VMEM)
     new, res, energy = kernel(
         functools.partial(third_body, n_blk, n_op, count),
-        [(meta, SMEM), (slots, SMEM)]
+        [(slots, SMEM)]
         + [(x, VMEM) for x in (parts1, parts2, raw, sig, fld, img, *got1, *got2)],
         [final, final, ((1,), f32, SMEM)],
         nbytes=4 << 20,

time: 110 us -> 94.8 us (0.86)
  local copies, waits for them, and re-layouts: 23 us -> 6.45 us
  starting transfers between devices: 27.8 us -> 25.3 us
  Pallas kernels: 12.6 us -> 14.4 us
  waiting for transfers between devices: 45.5 us -> 47.3 us
    unnamed x56 -> x16, local copies, waits for them, and re-layouts: 22.9 us -> 6.45 us
    ppermute x21, waiting for transfers between devices: 15.7 us -> 18.7 us  [swap(): return lax.ppermute(block, 'op', [(i, i ^ e) for i in range(n_op)])]
    pallas_call x5, Pallas kernels: 12.6 us -> 14.4 us  [kernel(): pl.pallas_call(body, out_shape=[HBM(shape, dtype) if space == HBM else ja...]
    ppermute x21, starting transfers between devices: 12.1 us -> 10.6 us  [swap(): return lax.ppermute(block, 'op', [(i, i ^ e) for i in range(n_op)])]
    ppermute x6, starting transfers between devices: 8.66 us -> 7.47 us  [onward(): lax.ppermute(block, 'blk', [(i, (i + d) % n_blk) for i in range(n_blk)])]
    ppermute x6, waiting for transfers between devices: 18.1 us -> 17 us  [onward(): lax.ppermute(block, 'blk', [(i, (i + d) % n_blk) for i in range(n_blk)])]
  transfers between devices with their start and end apart: 29 -> 29, of which waited for: 8 -> 10; matrix products, arithmetic and copies ran while one was open for 0% -> 0% of each run, Pallas kernels for 6% -> 8%
where the time goes in v5:
time: 94.8 us; the launch traced here: 94.3 us
  waiting for transfers between devices  47.3 us (50%)
  starting transfers between devices  25.3 us (27%)
  Pallas kernels  14.4 us (15%)
  local copies, waits for them, and re-layouts  6.45 us (7%)
    ppermute x21, waiting for transfers between devices, swap(): return lax.ppermute(block, 'op', [(i, i ^ e) for i in range(n_op)])  18.7 us
    ppermute x6, waiting for transfers between devices, onward(): lax.ppermute(block, 'blk', [(i, (i + d) % n_blk) for i in range(n_blk)])  17 us
    pallas_call x5, Pallas kernels, kernel(): pl.pallas_call(body, out_shape=[HBM(shape, dtype) if space == HBM else ja...  14.4 us
    all_to_all x2, waiting for transfers between devices, totals(): return lax.all_to_all(parts, ('blk', 'op'), 0, 0, tiled=True)  11.6 us
    ppermute x21, starting transfers between devices, swap(): return lax.ppermute(block, 'op', [(i, i ^ e) for i in range(n_op)])  10.6 us
    ppermute x6, starting transfers between devices, onward(): lax.ppermute(block, 'blk', [(i, (i + d) % n_blk) for i in range(n_blk)])  7.47 us
    all_to_all x2, starting transfers between devices, totals(): return lax.all_to_all(parts, ('blk', 'op'), 0, 0, tiled=True)  7.27 us
    unnamed x16, local copies, waits for them, and re-layouts  6.45 us
  transfers between devices with their start and end apart: 29, of which 10 were waited for; matrix products, arithmetic and copies ran while one was open for 0% of the time, Pallas kernels for 8%

profile of v5, /device:TPU:0, one launch (start us, length us, event | category | flops | bytes accessed | tf_op | source)
XLA Modules:
  0.0 94.3 jit_solution(16458805615724002397)
XLA Ops:
  0.6 3.1 %collective-permute-start.6 = (bf16[2,256,256]{2,1,0:T(8,128)(2,1)}, bf16[2,256,256]{2,1,0:T(8,128)(2,1)S(1)}, u32[]{:S(2)}, u32[]{:S(2)}) collective-permute-start(bf16[2,256,256]{2,1,0:T(8,128)(2,1)} %bitcast.2), channel_id=1, source_target_pairs={{0,4},{4,8},{8,12},{12,0},{1,5},{5,9},{9,13},{13,1},{2,6},{6,10},{... | collective-permute-start | bytes 786440 | tf_op jit(solution)/shard_map/ppermute | solution.py:128
  3.7 8.5 %collective-permute-done.6.refs_4_ = bf16[2,256,256]{2,1,0:T(8,128)(2,1)S(1)} collective-permute-done((bf16[2,256,256]{2,1,0:T(8,128)(2,1)}, bf16[2,256,256]{2,1,0:T(8,128)(2,1)S(1)}, u32[]{:S(2)}, u32[]{:S(2)}) %collective-permute-start.6) | collective-permute-done | bytes 262176 | tf_op jit(solution)/shard_map/ppermute | solution.py:128
  12.3 0.0 collective-permute-start.10
  12.3 0.0 collective-permute-start
  12.3 1.5 %collective-permute-start.4 = (bf16[2,256,256]{2,1,0:T(8,128)(2,1)}, bf16[2,256,256]{2,1,0:T(8,128)(2,1)S(1)}, u32[]{:S(2)}, u32[]{:S(2)}) collective-permute-start(bf16[2,256,256]{2,1,0:T(8,128)(2,1)} %bitcast.4), channel_id=1, source_target_pairs={{0,2},{1,3},{2,0},{3,1},{4,6},{5,7},{6,4},{7,5},{8,10},{9,11},{10,... | collective-permute-start | bytes 786440 | tf_op jit(solution)/shard_map/ppermute | solution.py:132
  13.7 7.8 %collective-permute-done.10.refs_8_ = bf16[2,256,256]{2,1,0:T(8,128)(2,1)S(1)} collective-permute-done((bf16[2,256,256]{2,1,0:T(8,128)(2,1)S(1)}, bf16[2,256,256]{2,1,0:T(8,128)(2,1)S(1)}, u32[]{:S(2)}, u32[]{:S(2)}) %collective-permute-start.10) | collective-permute-done | bytes 262176 | tf_op jit(solution)/shard_map/ppermute | solution.py:128
  21.5 0.0 collective-permute-start.14
  21.5 0.0 collective-permute-done._.refs_1_
  21.6 1.2 %copy-done = bf16[1,256,2048]{2,1,0:T(8,128)(2,1)S(1)} copy-done((bf16[1,256,2048]{2,1,0:T(8,128)(2,1)S(1)}, bf16[1,256,2048]{2,1,0:T(8,128)(2,1)}, u32[]{:S(2)}) %copy-start) | copy-done | bytes 1048600
  22.8 0.9 %copy-done.2 = bf16[2,8,64,64]{3,2,1,0:T(8,128)(2,1)S(1)} copy-done((bf16[2,8,64,64]{3,2,1,0:T(8,128)(2,1)S(1)}, bf16[2,8,64,64]{3,2,1,0:T(8,128)(2,1)}, u32[]{:S(2)}) %copy-start.2) | copy-done | bytes 131096
  23.7 0.7 copy-done.5
  24.4 1.0 %shard_map.103 = (bf16[256,128]{1,0:T(8,128)(2,1)S(1)}, bf16[256,128]{1,0:T(8,128)(2,1)S(1)}, bf16[256,128]{1,0:T(8,128)(2,1)S(1)}, bf16[256,128]{1,0:T(8,128)(2...) custom-call(s32[2]{0:T(128)S(1)} %copy-done.5, ...), custom_call_target="tpu_custom_call" | custom-call | bytes 1048576 | tf_op jit(solution)/shard_map/pallas_call | solution.py:113
  25.4 0.1 collective-permute-start.1
  25.5 1.3 %collective-permute-start.2 = (bf16[144,128]{1,0:T(8,128)(2,1)S(1)}, bf16[144,128]{1,0:T(8,128)(2,1)S(1)}, u32[]{:S(2)}, u32[]{:S(2)}) collective-permute-start(bf16[144,128]{1,0:T(8,128)(2,1)S(1)} %get-tuple-element.30), channel_id=1, source_target_pairs={{0,2},{1,3},{2,0},{3,1},{4,6},{5,7},{6,4},{7,5},{8,10},{9,11},{10,... | collective-permute-start | bytes 110600 | tf_op jit(solution)/shard_map/ppermute | solution.py:132
  26.8 0.0 collective-permute-start.18
  26.8 0.0 collective-permute-done.4.refs_2_
  26.8 4.4 %collective-permute-start.19 = (bf16[256,128]{1,0:T(8,128)(2,1)S(1)}, bf16[256,128]{1,0:T(8,128)(2,1)S(1)}, u32[]{:S(2)}, u32[]{:S(2)}) collective-permute-start(bf16[256,128]{1,0:T(8,128)(2,1)S(1)} %get-tuple-element.37), channel_id=1, source_target_pairs={{0,8},{4,12},{8,0},{12,4},{1,9},{5,13},{9,1},{13,5},{2,10},{6,14},... | collective-permute-start | bytes 196616 | tf_op jit(solution)/shard_map/ppermute | solution.py:128
  31.2 0.0 collective-permute-done.1.refs_1_.refs_17_
  31.2 0.0 collective-permute-start.20
  31.2 0.0 collective-permute-done.2.refs_2_.refs_18_
  31.2 0.1 collective-permute-start.3
  31.3 3.5 %collective-permute-done.3.refs_3_.refs_19_ = bf16[144,128]{1,0:T(8,128)(2,1)S(1)} collective-permute-done((bf16[144,128]{1,0:T(8,128)(2,1)S(1)}, bf16[144,128]{1,0:T(8,128)(2,1)S(1)}, u32[]{:S(2)}, u32[]{:S(2)}) %collective-permute-start.3) | collective-permute-done | bytes 36896 | tf_op jit(solution)/shard_map/ppermute | solution.py:132
  34.8 0.8 collective-permute-start.8
  35.6 0.0 collective-permute-done.18.refs_21_
  35.6 0.0 collective-permute-start.7
  35.6 0.3 collective-permute-done.19.refs_22_
  35.9 0.2 collective-permute-start.5
  36.1 0.3 collective-permute-done.20.refs_23_
  36.5 0.9 collective-permute-start.12
  37.4 0.0 collective-permute-done.14.refs_12_
  37.4 1.1 %collective-permute-start.16 = (bf16[2,256,256]{2,1,0:T(8,128)(2,1)S(1)}, bf16[2,256,256]{2,1,0:T(8,128)(2,1)S(1)}, u32[]{:S(2)}, u32[]{:S(2)}) collective-permute-start(bf16[2,256,256]{2,1,0:T(8,128)(2,1)S(1)} %collective-permute-done.14.refs_12_), channel_id=1, source_target_pairs={{0,2},{1,3},{2,0},{3,1},{4,6},{5,7},{6,4},{7,5},{8,10},{9,11},{10,... | collective-permute-start | bytes 786440 | tf_op jit(solution)/shard_map/ppermute | solution.py:132
  38.5 5.5 %collective-permute-done.8.refs_6_ = bf16[2,256,256]{2,1,0:T(8,128)(2,1)S(1)} collective-permute-done((bf16[2,256,256]{2,1,0:T(8,128)(2,1)S(1)}, bf16[2,256,256]{2,1,0:T(8,128)(2,1)S(1)}, u32[]{:S(2)}, u32[]{:S(2)}) %collective-permute-start.8) | collective-permute-done | bytes 262176 | tf_op jit(solution)/shard_map/ppermute | solution.py:132
  44.0 0.0 collective-permute-done.7.refs_5_
  44.0 0.5 collective-permute-start.9
  44.5 0.0 collective-permute-done.5.refs_3_
  44.5 0.1 collective-permute-start.15
  44.6 5.0 %collective-permute-done.12.refs_10_ = bf16[2,256,256]{2,1,0:T(8,128)(2,1)S(1)} collective-permute-done((bf16[2,256,256]{2,1,0:T(8,128)(2,1)S(1)}, bf16[2,256,256]{2,1,0:T(8,128)(2,1)S(1)}, u32[]{:S(2)}, u32[]{:S(2)}) %collective-permute-start.12) | collective-permute-done | bytes 262176 | tf_op jit(solution)/shard_map/ppermute | solution.py:132
  49.6 0.0 collective-permute-start.13
  49.6 4.5 %collective-permute-done.16.refs_14_ = bf16[2,256,256]{2,1,0:T(8,128)(2,1)S(1)} collective-permute-done((bf16[2,256,256]{2,1,0:T(8,128)(2,1)S(1)}, bf16[2,256,256]{2,1,0:T(8,128)(2,1)S(1)}, u32[]{:S(2)}, u32[]{:S(2)}) %collective-permute-start.16) | collective-permute-done | bytes 262176 | tf_op jit(solution)/shard_map/ppermute | solution.py:132
  54.2 0.7 copy-done.3
  54.9 0.7 copy-done.4
  55.5 0.7 copy-done.6
  56.2 0.7 copy-done.7
  56.9 1.4 %shard_map.104 = (s32[32]{0:T(128)S(1)}, s32[4]{0:T(128)S(1)}, s32[4]{0:T(128)S(1)}, f32[4,256,128]{2,1,0:T(8,128)S(1)}) custom-call(s32[4]{0:T(128)S(1)} %copy-done.6, s32[4]{0:T(128)S(1)} %copy-done.7, f32[4,256]{1,0:T(4,128)S(1)} %copy-done.3, f32[1,512]{1,0:T(1,128)S(1)} %bitcast.6, bf16[144,128]{1,0:T(8,128)(2,1)S(1)} %get-tuple-element.28.refs_0_.refs_16_, ...), custom_call_target="tpu_custom_call" | custom-call | tf_op jit(solution)/shard_map/pallas_call | solution.py:113
  58.3 0.0 collective-permute-done.9.refs_7_
  58.3 0.0 collective-permute-done.15.refs_13_
  58.3 0.0 copy-start.1
  58.3 0.9 copy-done.1
  59.3 5.3 %shard_map.105 = (f32[4,256,128]{2,1,0:T(8,128)S(1)}, bf16[4,256,128]{2,1,0:T(8,128)(2,1)S(1)}, f32[16,8,128]{2,1,0:T(8,128)}, bf16[4,4,2,256,256]{4,3,2,1,0:T(8...) custom-call(s32[32]{0:T(128)S(1)} %get-tuple-element.33.src, ...), custom_call_target="tpu_custom_call" | custom-call | flops 805306368 | bytes 8388608 | tf_op jit(solution)/shard_map/pallas_call | solution.py:113
  64.6 3.8 %all-to-all-start = ((f32[16,8,128]{2,1,0:T(8,128)}), f32[16,8,128]{2,1,0:T(8,128)S(1)}, u32[]{:S(2)}, u32[]{:S(2)}) async-start(f32[16,8,128]{2,1,0:T(8,128)} %get-tuple-element.40), calls=%async_computation | async-start | bytes 131072 | tf_op jit(solution)/shard_map/all_to_all | solution.py:467
  68.4 0.4 collective-permute-start.21
  68.8 1.7 %collective-permute-start.22 = (bf16[2,4,64,128]{3,2,1,0:T(8,128)(2,1)S(1)}, bf16[2,4,64,128]{3,2,1,0:T(8,128)(2,1)S(1)}, u32[]{:S(2)}, u32[]{:S(2)}) collective-permute-start(bf16[2,4,64,128]{3,2,1,0:T(8,128)(2,1)S(1)} %get-tuple-element.48), channel_id=1, source_target_pairs={{0,2},{1,3},{2,0},{3,1},{4,6},{5,7},{6,4},{7,5},{8,10},{9,11},{10,... | collective-permute-start | bytes 393224 | tf_op jit(solution)/shard_map/ppermute | solution.py:132
  70.5 4.8 %all-to-all-done.refs_4_.parts1 = f32[16,8,128]{2,1,0:T(8,128)S(1)} async-done(((f32[16,8,128]{2,1,0:T(8,128)}), f32[16,8,128]{2,1,0:T(8,128)S(1)}, u32[]{:S(2)}, u32[]{:S(2)}) %all-to-all-start) | async-done | bytes 65568 | tf_op jit(solution)/shard_map/all_to_all | solution.py:467
  75.3 5.0 %shard_map.106 = (bf16[4,256,128]{2,1,0:T(8,128)(2,1)S(1)}, f32[4,256,128]{2,1,0:T(8,128)S(1)}, f32[16,8,128]{2,1,0:T(8,128)}, bf16[2,4,64,128]{3,2,1,0:T(8,128)...) custom-call(s32[32]{0:T(128)S(1)} %get-tuple-element.33.src, ...), custom_call_target="tpu_custom_call" | custom-call | flops 805306368 | bytes 8388608 | tf_op jit(solution)/shard_map/pallas_call | solution.py:113
  80.3 0.1 collective-permute-start.24
  80.4 0.2 collective-permute-start.25
  80.6 0.0 collective-permute-done.21.refs_0_
  80.6 1.6 %collective-permute-start.26 = (bf16[2,4,64,128]{3,2,1,0:T(8,128)(2,1)S(1)}, bf16[2,4,64,128]{3,2,1,0:T(8,128)(2,1)S(1)}, u32[]{:S(2)}, u32[]{:S(2)}) collective-permute-start(bf16[2,4,64,128]{3,2,1,0:T(8,128)(2,1)S(1)} %get-tuple-element.52), channel_id=1, source_target_pairs={{0,3},{1,2},{2,1},{3,0},{4,7},{5,6},{6,5},{7,4},{8,11},{9,10},{10,... | collective-permute-start | bytes 393224 | tf_op jit(solution)/shard_map/ppermute | solution.py:132
  82.2 3.5 %all-to-all-start.1 = ((f32[16,8,128]{2,1,0:T(8,128)}), f32[16,8,128]{2,1,0:T(8,128)S(1)}, u32[]{:S(2)}, u32[]{:S(2)}) async-start(f32[16,8,128]{2,1,0:T(8,128)} %get-tuple-element.44), calls=%async_computation.1 | async-start | bytes 131072 | tf_op jit(solution)/shard_map/all_to_all | solution.py:467
  85.7 0.0 collective-permute-done.22.refs_1_
  85.8 6.8 %all-to-all-done.1.parts2 = f32[16,8,128]{2,1,0:T(8,128)S(1)} async-done(((f32[16,8,128]{2,1,0:T(8,128)}), f32[16,8,128]{2,1,0:T(8,128)S(1)}, u32[]{:S(2)}, u32[]{:S(2)}) %all-to-all-start.1) | async-done | bytes 65568 | tf_op jit(solution)/shard_map/all_to_all | solution.py:467
  92.6 0.0 collective-permute-done.24.refs_3_
  92.6 0.0 collective-permute-done.25.refs_4_
  92.6 1.7 %shard_map.107 = (bf16[4,64,512]{2,1,0:T(8,128)(2,1)}, bf16[4,64,512]{2,1,0:T(8,128)(2,1)}, f32[1]{0:T(128)}) custom-call(s32[4]{0:T(128)S(1)} %get-tuple-element.32.slots, f32[16,8,128]{2,1,0:T(8,128)S(1)} %all-to-all-done.refs_4_.parts1, f32[16,8,128]{2,1,0:T(8,128)S(1)} %all-to-all-done.1.parts2, ...), custom_call_target="tpu_custom_call" | custom-call | bytes 4194304 | tf_op jit(solution)/shard_map/pallas_call | solution.py:113
  (15 shorter events, 0.0 us)
Async XLA Ops:
  0.6 11.6 %collective-permute-start.6 = (bf16[2,256,256]{2,1,0:T(8,128)(2,1)}, bf16[2,256,256]{2,1,0:T(8,128)(2,1)S(1)}, u32[]{:S(2)}, u32[]{:S(2)}) collective-permute-start(bf16[2,256,256]{2,1,0:T(8,128)(2,1)} %bitcast.2), channel_id=1, source_target_pairs={{0,4},{4,8},{8,12},{12,0},{1,5},{5,9},{9,13},{13,1},{2,6},{6,10},{... | collective-permute-start | bytes 786440 | tf_op jit(solution)/shard_map/ppermute | solution.py:128
  12.3 9.3 %collective-permute-start.10 = (bf16[2,256,256]{2,1,0:T(8,128)(2,1)S(1)}, bf16[2,256,256]{2,1,0:T(8,128)(2,1)S(1)}, u32[]{:S(2)}, u32[]{:S(2)}) collective-permute-start(bf16[2,256,256]{2,1,0:T(8,128)(2,1)S(1)} %collective-permute-done.6.refs_4_), channel_id=1, source_target_pairs={{0,4},{4,8},{8,12},{12,0},{1,5},{5,9},{9,13},{13,1},{2,6},{6,10},{... | collective-permute-start | bytes 786440 | tf_op jit(solution)/shard_map/ppermute | solution.py:128
  12.3 9.3 %collective-permute-start = (bf16[2,256,256]{2,1,0:T(8,128)(2,1)}, bf16[2,256,256]{2,1,0:T(8,128)(2,1)S(1)}, u32[]{:S(2)}, u32[]{:S(2)}) collective-permute-start(bf16[2,256,256]{2,1,0:T(8,128)(2,1)} %bitcast.3), channel_id=1, source_target_pairs={{0,1},{1,0},{2,3},{3,2},{4,5},{5,4},{6,7},{7,6},{8,9},{9,8},{10,11... | collective-permute-start | bytes 786440 | tf_op jit(solution)/shard_map/ppermute | solution.py:132
  12.3 14.5 %collective-permute-start.4 = (bf16[2,256,256]{2,1,0:T(8,128)(2,1)}, bf16[2,256,256]{2,1,0:T(8,128)(2,1)S(1)}, u32[]{:S(2)}, u32[]{:S(2)}) collective-permute-start(bf16[2,256,256]{2,1,0:T(8,128)(2,1)} %bitcast.4), channel_id=1, source_target_pairs={{0,2},{1,3},{2,0},{3,1},{4,6},{5,7},{6,4},{7,5},{8,10},{9,11},{10,... | collective-permute-start | bytes 786440 | tf_op jit(solution)/shard_map/ppermute | solution.py:132
  21.5 15.8 %collective-permute-start.14 = (bf16[2,256,256]{2,1,0:T(8,128)(2,1)S(1)}, bf16[2,256,256]{2,1,0:T(8,128)(2,1)S(1)}, u32[]{:S(2)}, u32[]{:S(2)}) collective-permute-start(bf16[2,256,256]{2,1,0:T(8,128)(2,1)S(1)} %collective-permute-done.10.refs_8_), channel_id=1, source_target_pairs={{0,4},{4,8},{8,12},{12,0},{1,5},{5,9},{9,13},{13,1},{2,6},{6,10},{... | collective-permute-start | bytes 786440 | tf_op jit(solution)/shard_map/ppermute | solution.py:128
  21.5 1.2 %copy-start = (bf16[1,256,2048]{2,1,0:T(8,128)(2,1)S(1)}, bf16[1,256,2048]{2,1,0:T(8,128)(2,1)}, u32[]{:S(2)}) copy-start(bf16[1,256,2048]{2,1,0:T(8,128)(2,1)} %psi.1) | copy-start | bytes 3145732
  22.8 0.9 %copy-start.2 = (bf16[2,8,64,64]{3,2,1,0:T(8,128)(2,1)S(1)}, bf16[2,8,64,64]{3,2,1,0:T(8,128)(2,1)}, u32[]{:S(2)}) copy-start(bf16[2,8,64,64]{3,2,1,0:T(8,128)(2,1)} %right.1) | copy-start | bytes 393220
  23.7 0.7 copy-start.5
  25.4 5.8 %collective-permute-start.1 = (bf16[144,128]{1,0:T(8,128)(2,1)S(1)}, bf16[144,128]{1,0:T(8,128)(2,1)S(1)}, u32[]{:S(2)}, u32[]{:S(2)}) collective-permute-start(bf16[144,128]{1,0:T(8,128)(2,1)S(1)} %get-tuple-element.29), channel_id=1, source_target_pairs={{0,1},{1,0},{2,3},{3,2},{4,5},{5,4},{6,7},{7,6},{8,9},{9,8},{10,11... | collective-permute-start | bytes 110600 | tf_op jit(solution)/shard_map/ppermute | solution.py:132
  25.5 5.7 %collective-permute-start.2 = (bf16[144,128]{1,0:T(8,128)(2,1)S(1)}, bf16[144,128]{1,0:T(8,128)(2,1)S(1)}, u32[]{:S(2)}, u32[]{:S(2)}) collective-permute-start(bf16[144,128]{1,0:T(8,128)(2,1)S(1)} %get-tuple-element.30), channel_id=1, source_target_pairs={{0,2},{1,3},{2,0},{3,1},{4,6},{5,7},{6,4},{7,5},{8,10},{9,11},{10,... | collective-permute-start | bytes 110600 | tf_op jit(solution)/shard_map/ppermute | solution.py:132
  26.8 8.8 %collective-permute-start.18 = (bf16[256,128]{1,0:T(8,128)(2,1)S(1)}, bf16[256,128]{1,0:T(8,128)(2,1)S(1)}, u32[]{:S(2)}, u32[]{:S(2)}) collective-permute-start(bf16[256,128]{1,0:T(8,128)(2,1)S(1)} %get-tuple-element.36), channel_id=1, source_target_pairs={{0,4},{4,8},{8,12},{12,0},{1,5},{5,9},{9,13},{13,1},{2,6},{6,10},{... | collective-permute-start | bytes 196616 | tf_op jit(solution)/shard_map/ppermute | solution.py:128
  26.8 9.2 %collective-permute-start.19 = (bf16[256,128]{1,0:T(8,128)(2,1)S(1)}, bf16[256,128]{1,0:T(8,128)(2,1)S(1)}, u32[]{:S(2)}, u32[]{:S(2)}) collective-permute-start(bf16[256,128]{1,0:T(8,128)(2,1)S(1)} %get-tuple-element.37), channel_id=1, source_target_pairs={{0,8},{4,12},{8,0},{12,4},{1,9},{5,13},{9,1},{13,5},{2,10},{6,14},... | collective-permute-start | bytes 196616 | tf_op jit(solution)/shard_map/ppermute | solution.py:128
  31.2 5.3 %collective-permute-start.20 = (bf16[256,128]{1,0:T(8,128)(2,1)S(1)}, bf16[256,128]{1,0:T(8,128)(2,1)S(1)}, u32[]{:S(2)}, u32[]{:S(2)}) collective-permute-start(bf16[256,128]{1,0:T(8,128)(2,1)S(1)} %get-tuple-element.38), channel_id=1, source_target_pairs={{0,12},{4,0},{8,4},{12,8},{1,13},{5,1},{9,5},{13,9},{2,14},{6,2},{... | collective-permute-start | bytes 196616 | tf_op jit(solution)/shard_map/ppermute | solution.py:128
  31.2 3.6 %collective-permute-start.3 = (bf16[144,128]{1,0:T(8,128)(2,1)S(1)}, bf16[144,128]{1,0:T(8,128)(2,1)S(1)}, u32[]{:S(2)}, u32[]{:S(2)}) collective-permute-start(bf16[144,128]{1,0:T(8,128)(2,1)S(1)} %get-tuple-element.31), channel_id=1, source_target_pairs={{0,3},{1,2},{2,1},{3,0},{4,7},{5,6},{6,5},{7,4},{8,11},{9,10},{10,... | collective-permute-start | bytes 110600 | tf_op jit(solution)/shard_map/ppermute | solution.py:132
  34.8 9.2 %collective-permute-start.8 = (bf16[2,256,256]{2,1,0:T(8,128)(2,1)S(1)}, bf16[2,256,256]{2,1,0:T(8,128)(2,1)S(1)}, u32[]{:S(2)}, u32[]{:S(2)}) collective-permute-start(bf16[2,256,256]{2,1,0:T(8,128)(2,1)S(1)} %collective-permute-done.6.refs_4_), channel_id=1, source_target_pairs={{0,2},{1,3},{2,0},{3,1},{4,6},{5,7},{6,4},{7,5},{8,10},{9,11},{10,... | collective-permute-start | bytes 786440 | tf_op jit(solution)/shard_map/ppermute | solution.py:132
  35.6 8.4 %collective-permute-start.7 = (bf16[2,256,256]{2,1,0:T(8,128)(2,1)S(1)}, bf16[2,256,256]{2,1,0:T(8,128)(2,1)S(1)}, u32[]{:S(2)}, u32[]{:S(2)}) collective-permute-start(bf16[2,256,256]{2,1,0:T(8,128)(2,1)S(1)} %collective-permute-done.6.refs_4_), channel_id=1, source_target_pairs={{0,1},{1,0},{2,3},{3,2},{4,5},{5,4},{6,7},{7,6},{8,9},{9,8},{10,11... | collective-permute-start | bytes 786440 | tf_op jit(solution)/shard_map/ppermute | solution.py:132
  35.9 8.6 %collective-permute-start.5 = (bf16[2,256,256]{2,1,0:T(8,128)(2,1)S(1)}, bf16[2,256,256]{2,1,0:T(8,128)(2,1)S(1)}, u32[]{:S(2)}, u32[]{:S(2)}) collective-permute-start(bf16[2,256,256]{2,1,0:T(8,128)(2,1)S(1)} %collective-permute-done.4.refs_2_), channel_id=1, source_target_pairs={{0,1},{1,0},{2,3},{3,2},{4,5},{5,4},{6,7},{7,6},{8,9},{9,8},{10,11... | collective-permute-start | bytes 786440 | tf_op jit(solution)/shard_map/ppermute | solution.py:132
  36.5 13.2 %collective-permute-start.12 = (bf16[2,256,256]{2,1,0:T(8,128)(2,1)S(1)}, bf16[2,256,256]{2,1,0:T(8,128)(2,1)S(1)}, u32[]{:S(2)}, u32[]{:S(2)}) collective-permute-start(bf16[2,256,256]{2,1,0:T(8,128)(2,1)S(1)} %collective-permute-done.10.refs_8_), channel_id=1, source_target_pairs={{0,2},{1,3},{2,0},{3,1},{4,6},{5,7},{6,4},{7,5},{8,10},{9,11},{10,... | collective-permute-start | bytes 786440 | tf_op jit(solution)/shard_map/ppermute | solution.py:132
  37.4 16.8 %collective-permute-start.16 = (bf16[2,256,256]{2,1,0:T(8,128)(2,1)S(1)}, bf16[2,256,256]{2,1,0:T(8,128)(2,1)S(1)}, u32[]{:S(2)}, u32[]{:S(2)}) collective-permute-start(bf16[2,256,256]{2,1,0:T(8,128)(2,1)S(1)} %collective-permute-done.14.refs_12_), channel_id=1, source_target_pairs={{0,2},{1,3},{2,0},{3,1},{4,6},{5,7},{6,4},{7,5},{8,10},{9,11},{10,... | collective-permute-start | bytes 786440 | tf_op jit(solution)/shard_map/ppermute | solution.py:132
  44.0 14.3 %collective-permute-start.11 = (bf16[2,256,256]{2,1,0:T(8,128)(2,1)S(1)}, bf16[2,256,256]{2,1,0:T(8,128)(2,1)S(1)}, u32[]{:S(2)}, u32[]{:S(2)}) collective-permute-start(bf16[2,256,256]{2,1,0:T(8,128)(2,1)S(1)} %collective-permute-done.10.refs_8_), channel_id=1, source_target_pairs={{0,1},{1,0},{2,3},{3,2},{4,5},{5,4},{6,7},{7,6},{8,9},{9,8},{10,11... | collective-permute-start | bytes 786440 | tf_op jit(solution)/shard_map/ppermute | solution.py:132
  44.0 14.3 %collective-permute-start.9 = (bf16[2,256,256]{2,1,0:T(8,128)(2,1)S(1)}, bf16[2,256,256]{2,1,0:T(8,128)(2,1)S(1)}, u32[]{:S(2)}, u32[]{:S(2)}) collective-permute-start(bf16[2,256,256]{2,1,0:T(8,128)(2,1)S(1)} %collective-permute-done.8.refs_6_), channel_id=1, source_target_pairs={{0,1},{1,0},{2,3},{3,2},{4,5},{5,4},{6,7},{7,6},{8,9},{9,8},{10,11... | collective-permute-start | bytes 786440 | tf_op jit(solution)/shard_map/ppermute | solution.py:132
  44.5 13.8 %collective-permute-start.15 = (bf16[2,256,256]{2,1,0:T(8,128)(2,1)S(1)}, bf16[2,256,256]{2,1,0:T(8,128)(2,1)S(1)}, u32[]{:S(2)}, u32[]{:S(2)}) collective-permute-start(bf16[2,256,256]{2,1,0:T(8,128)(2,1)S(1)} %collective-permute-done.14.refs_12_), channel_id=1, source_target_pairs={{0,1},{1,0},{2,3},{3,2},{4,5},{5,4},{6,7},{7,6},{8,9},{9,8},{10,11... | collective-permute-start | bytes 786440 | tf_op jit(solution)/shard_map/ppermute | solution.py:132
  49.6 8.7 %collective-permute-start.13 = (bf16[2,256,256]{2,1,0:T(8,128)(2,1)S(1)}, bf16[2,256,256]{2,1,0:T(8,128)(2,1)S(1)}, u32[]{:S(2)}, u32[]{:S(2)}) collective-permute-start(bf16[2,256,256]{2,1,0:T(8,128)(2,1)S(1)} %collective-permute-done.12.refs_10_), channel_id=1, source_target_pairs={{0,1},{1,0},{2,3},{3,2},{4,5},{5,4},{6,7},{7,6},{8,9},{9,8},{10,11... | collective-permute-start | bytes 786440 | tf_op jit(solution)/shard_map/ppermute | solution.py:132
  54.2 4.2 %collective-permute-start.17 = (bf16[2,256,256]{2,1,0:T(8,128)(2,1)S(1)}, bf16[2,256,256]{2,1,0:T(8,128)(2,1)S(1)}, u32[]{:S(2)}, u32[]{:S(2)}) collective-permute-start(bf16[2,256,256]{2,1,0:T(8,128)(2,1)S(1)} %collective-permute-done.16.refs_14_), channel_id=1, source_target_pairs={{0,1},{1,0},{2,3},{3,2},{4,5},{5,4},{6,7},{7,6},{8,9},{9,8},{10,11... | collective-permute-start | bytes 786440 | tf_op jit(solution)/shard_map/ppermute | solution.py:132
  54.2 0.7 copy-start.3
  54.9 0.7 copy-start.4
  55.5 0.7 copy-start.6
  56.2 0.7 copy-start.7
  58.3 1.0 %copy-start.1 = (bf16[2,1,256,256]{3,2,1,0:T(8,128)(2,1)S(1)}, bf16[2,1,256,256]{3,2,1,0:T(8,128)(2,1)}, u32[]{:S(2)}) copy-start(bf16[2,1,256,256]{3,2,1,0:T(8,128)(2,1)} %param.9) | copy-start | bytes 786436
  64.6 10.7 %all-to-all-start = ((f32[16,8,128]{2,1,0:T(8,128)}), f32[16,8,128]{2,1,0:T(8,128)S(1)}, u32[]{:S(2)}, u32[]{:S(2)}) async-start(f32[16,8,128]{2,1,0:T(8,128)} %get-tuple-element.40), calls=%async_computation | async-start | bytes 131072 | tf_op jit(solution)/shard_map/all_to_all | solution.py:467
  68.4 12.2 %collective-permute-start.21 = (bf16[2,4,64,128]{3,2,1,0:T(8,128)(2,1)S(1)}, bf16[2,4,64,128]{3,2,1,0:T(8,128)(2,1)S(1)}, u32[]{:S(2)}, u32[]{:S(2)}) collective-permute-start(bf16[2,4,64,128]{3,2,1,0:T(8,128)(2,1)S(1)} %get-tuple-element.47), channel_id=1, source_target_pairs={{0,1},{1,0},{2,3},{3,2},{4,5},{5,4},{6,7},{7,6},{8,9},{9,8},{10,11... | collective-permute-start | bytes 393224 | tf_op jit(solution)/shard_map/ppermute | solution.py:132
  68.8 17.0 %collective-permute-start.22 = (bf16[2,4,64,128]{3,2,1,0:T(8,128)(2,1)S(1)}, bf16[2,4,64,128]{3,2,1,0:T(8,128)(2,1)S(1)}, u32[]{:S(2)}, u32[]{:S(2)}) collective-permute-start(bf16[2,4,64,128]{3,2,1,0:T(8,128)(2,1)S(1)} %get-tuple-element.48), channel_id=1, source_target_pairs={{0,2},{1,3},{2,0},{3,1},{4,6},{5,7},{6,4},{7,5},{8,10},{9,11},{10,... | collective-permute-start | bytes 393224 | tf_op jit(solution)/shard_map/ppermute | solution.py:132
  70.5 15.3 %collective-permute-start.23 = (bf16[2,4,64,128]{3,2,1,0:T(8,128)(2,1)S(1)}, bf16[2,4,64,128]{3,2,1,0:T(8,128)(2,1)S(1)}, u32[]{:S(2)}, u32[]{:S(2)}) collective-permute-start(bf16[2,4,64,128]{3,2,1,0:T(8,128)(2,1)S(1)} %get-tuple-element.49), channel_id=1, source_target_pairs={{0,3},{1,2},{2,1},{3,0},{4,7},{5,6},{6,5},{7,4},{8,11},{9,10},{10,... | collective-permute-start | bytes 393224 | tf_op jit(solution)/shard_map/ppermute | solution.py:132
  80.3 12.3 %collective-permute-start.24 = (bf16[2,4,64,128]{3,2,1,0:T(8,128)(2,1)S(1)}, bf16[2,4,64,128]{3,2,1,0:T(8,128)(2,1)S(1)}, u32[]{:S(2)}, u32[]{:S(2)}) collective-permute-start(bf16[2,4,64,128]{3,2,1,0:T(8,128)(2,1)S(1)} %get-tuple-element.50), channel_id=1, source_target_pairs={{0,1},{1,0},{2,3},{3,2},{4,5},{5,4},{6,7},{7,6},{8,9},{9,8},{10,11... | collective-permute-start | bytes 393224 | tf_op jit(solution)/shard_map/ppermute | solution.py:132
  80.4 12.2 %collective-permute-start.25 = (bf16[2,4,64,128]{3,2,1,0:T(8,128)(2,1)S(1)}, bf16[2,4,64,128]{3,2,1,0:T(8,128)(2,1)S(1)}, u32[]{:S(2)}, u32[]{:S(2)}) collective-permute-start(bf16[2,4,64,128]{3,2,1,0:T(8,128)(2,1)S(1)} %get-tuple-element.51), channel_id=1, source_target_pairs={{0,2},{1,3},{2,0},{3,1},{4,6},{5,7},{6,4},{7,5},{8,10},{9,11},{10,... | collective-permute-start | bytes 393224 | tf_op jit(solution)/shard_map/ppermute | solution.py:132
  80.6 12.0 %collective-permute-start.26 = (bf16[2,4,64,128]{3,2,1,0:T(8,128)(2,1)S(1)}, bf16[2,4,64,128]{3,2,1,0:T(8,128)(2,1)S(1)}, u32[]{:S(2)}, u32[]{:S(2)}) collective-permute-start(bf16[2,4,64,128]{3,2,1,0:T(8,128)(2,1)S(1)} %get-tuple-element.52), channel_id=1, source_target_pairs={{0,3},{1,2},{2,1},{3,0},{4,7},{5,6},{6,5},{7,4},{8,11},{9,10},{10,... | collective-permute-start | bytes 393224 | tf_op jit(solution)/shard_map/ppermute | solution.py:132
  82.2 10.4 %all-to-all-start.1 = ((f32[16,8,128]{2,1,0:T(8,128)}), f32[16,8,128]{2,1,0:T(8,128)S(1)}, u32[]{:S(2)}, u32[]{:S(2)}) async-start(f32[16,8,128]{2,1,0:T(8,128)} %get-tuple-element.44), calls=%async_computation.1 | async-start | bytes 131072 | tf_op jit(solution)/shard_map/all_to_all | solution.py:467

commit v6 on v5

--- a/solution.py
+++ b/solution.py
@@ -132,22 +132,47 @@
     return lax.ppermute(block, "op", [(i, i ^ e) for i in range(n_op)])
 
 
-def gather_left(own, n_blk, n_op):
-    held = {(0, 0): own}
-    for d in range(1, n_blk):
-        held[d, 0] = onward(held[d - 1, 0], 1, n_blk)
-    bit = n_op // 2
-    while bit:
-        held.update({(d, e ^ bit): swap(block, bit, n_op) for (d, e), block in held.items()})
-        bit //= 2
-    return held
+def gather(own, n_blk, n_op, pack, table):
+    bits = [1 << b for b in reversed(range(n_op.bit_length() - 1))]
+    order = sorted(range(1, n_blk), key=lambda d: min(d, n_blk - d))
+    left, psi, right, tables = {(0, 0): own}, {}, {}, None
+    waiting = {(0, 0): 0}
+    for j in range(n_blk + len(bits)):
+        new, moved = {}, {}
+        for (d, e), done in waiting.items():
+            if e == 0 and d + 1 < n_blk:
+                new[d + 1, 0] = onward(left[d, 0], 1, n_blk), 0
+            for b in range(done, len(bits)):
+                new[d, e ^ bits[b]] = swap(left[d, e], bits[b], n_op), b + 1
+        kept = {key: block for key, (block, _) in new.items()}
+        if j == 0:
+            sent = pack(kept[0, bits[-1]])
+            moved["sent"] = sent
+        if j == 1:
+            moved["right"] = [swap(sent[1][e], e, n_op) for e in range(1, n_op)]
+        if 1 <= j < n_blk:
+            d = order[j - 1]
+            moved["psi"] = onward(sent[0][d], d, n_blk)
+        if j == 2:
+            moved["tables"] = table([sent[1][0]] + right)
+        if not kept and not moved:
+            break
+        waiting = {key: done for key, (_, done) in new.items()}
+        kept, moved = lax.optimization_barrier((kept, moved))
+        left.update(kept)
+        sent = moved.get("sent", sent)
+        right = moved.get("right", right)
+        tables = moved.get("tables", tables)
+        if "psi" in moved:
+            psi[d] = moved["psi"]
+    return left, [sent[0][0]] + [psi[d] for d in range(1, n_blk)], [sent[1][0]] + right, tables
 
 
 def place_of():
     return lax.axis_index("blk"), lax.axis_index("op")
 
 
-def pack_body(n_blk, n_op, shift, psi, right, _, *outs):
+def pack_body(n_blk, n_op, shift, psi, right, *outs):
     psi_out, right_out, sems = outs[:n_blk], outs[n_blk : n_blk + n_op], outs[-1]
     cols = psi_out[0].shape[1]
     terms, _, width, _ = right.shape
@@ -431,27 +456,31 @@
     n_dev = n_blk * n_op
     bf16, f32 = jnp.bfloat16, jnp.float32
 
-    left = gather_left(left_ops[:, 0], n_blk, n_op)
+    def pack(after):
+        given = lax.optimization_barrier((term_shift, psi, right_ops, after))
+        sent = kernel(
+            functools.partial(pack_body, n_blk, n_op),
+            list(zip(given, (SMEM, ANY, VMEM))),
+            [((rows, cols), bf16, VMEM)] * n_blk + [((terms * width + 16, cols), bf16, VMEM)] * n_op,
+            [pltpu.SemaphoreType.DMA((n_blk,))],
+            nbytes=1 << 20,
+        )
+        return sent[:n_blk], sent[n_blk:]
+
+    def table(right):
+        return kernel(
+            functools.partial(table_body, n_blk, n_op, terms),
+            [(slot_sector, SMEM), (sector_width, SMEM), (diag_left, VMEM), (diag_right[None], VMEM)]
+            + [(block, VMEM) for block in right],
+            [((n_blk * n_op * terms,), jnp.int32, SMEM)]
+            + [((n_blk,), jnp.int32, SMEM)] * 2
+            + [((n_blk, rows, cols), f32, VMEM)],
+        )
+
+    left, psi_by, right, (src, widths, slots, dmat) = gather(left_ops[:, 0], n_blk, n_op, pack, table)
     left_ins = [(left[d, e], VMEM) for d in range(n_blk) for e in range(n_op)]
-
-    sent = kernel(
-        functools.partial(pack_body, n_blk, n_op),
-        [(term_shift, SMEM), (psi, ANY), (right_ops, VMEM), (left[0, 1], ANY)],
-        [((rows, cols), bf16, VMEM)] * n_blk + [((terms * width + 16, cols), bf16, VMEM)] * n_op,
-        [pltpu.SemaphoreType.DMA((n_blk,))],
-        nbytes=1 << 20,
-    )
-    right = [sent[n_blk]] + [swap(sent[n_blk + e], e, n_op) for e in range(1, n_op)]
     right_ins = [(block, VMEM) for block in right]
-    psi_ins = [(sent[0], VMEM)] + [(onward(sent[d], d, n_blk), VMEM) for d in range(1, n_blk)]
-    src, widths, slots, dmat = kernel(
-        functools.partial(table_body, n_blk, n_op, terms),
-        [(slot_sector, SMEM), (sector_width, SMEM), (diag_left, VMEM), (diag_right[None], VMEM)]
-        + right_ins,
-        [((n_blk * n_op * terms,), jnp.int32, SMEM)]
-        + [((n_blk,), jnp.int32, SMEM)] * 2
-        + [((n_blk, rows, cols), f32, VMEM)],
-    )
+    psi_ins = [(block, VMEM) for block in psi_by]
 
     tables = [(src, SMEM), (widths, SMEM)]
     wide = ((n_blk, rows, cols), f32, VMEM)

time: 94.8 us -> 91 us (0.960)
  waiting for transfers between devices: 47.3 us -> 40 us
  starting transfers between devices: 25.3 us -> 28.8 us
    ppermute x21, waiting for transfers between devices: 18.7 us -> 12.8 us  [swap(): return lax.ppermute(block, 'op', [(i, i ^ e) for i in range(n_op)])]
    ppermute x6, starting transfers between devices: 7.47 us -> 10.3 us  [onward(): lax.ppermute(block, 'blk', [(i, (i + d) % n_blk) for i in range(n_blk)])]
    ppermute x6, waiting for transfers between devices: 17 us -> 15.5 us  [onward(): lax.ppermute(block, 'blk', [(i, (i + d) % n_blk) for i in range(n_blk)])]
  transfers between devices with their start and end apart: 29 -> 29, of which waited for: 10 -> 11; matrix products, arithmetic and copies ran while one was open for 0% -> 0% of each run, Pallas kernels for 8% -> 8%
where the time goes in v6:
time: 91 us; the launch traced here: 90.6 us
  waiting for transfers between devices  40 us (44%)
  starting transfers between devices  28.8 us (32%)
  Pallas kernels  14.4 us (16%)
  local copies, waits for them, and re-layouts  6.46 us (7%)
    ppermute x6, waiting for transfers between devices, onward(): lax.ppermute(block, 'blk', [(i, (i + d) % n_blk) for i in range(n_blk)])  15.5 us
    pallas_call x5, Pallas kernels, kernel(): pl.pallas_call(body, out_shape=[HBM(shape, dtype) if space == HBM else ja...  14.4 us
    ppermute x21, waiting for transfers between devices, swap(): return lax.ppermute(block, 'op', [(i, i ^ e) for i in range(n_op)])  12.8 us
    all_to_all x2, waiting for transfers between devices, totals(): return lax.all_to_all(parts, ('blk', 'op'), 0, 0, tiled=True)  11.7 us
    ppermute x21, starting transfers between devices, swap(): return lax.ppermute(block, 'op', [(i, i ^ e) for i in range(n_op)])  11.5 us
    ppermute x6, starting transfers between devices, onward(): lax.ppermute(block, 'blk', [(i, (i + d) % n_blk) for i in range(n_blk)])  10.3 us
    all_to_all x2, starting transfers between devices, totals(): return lax.all_to_all(parts, ('blk', 'op'), 0, 0, tiled=True)  7.02 us
    unnamed x16, local copies, waits for them, and re-layouts  6.46 us
  transfers between devices with their start and end apart: 29, of which 11 were waited for; matrix products, arithmetic and copies ran while one was open for 0% of the time, Pallas kernels for 8%

profile of v6, /device:TPU:0, one launch (start us, length us, event | category | flops | bytes accessed | tf_op | source)
XLA Modules:
  0.0 90.6 jit_solution(5624744373617198867)
XLA Ops:
  0.6 0.5 collective-permute-start
  1.1 2.6 %collective-permute-start.2 = (bf16[2,256,256]{2,1,0:T(8,128)(2,1)}, bf16[2,256,256]{2,1,0:T(8,128)(2,1)S(1)}, u32[]{:S(2)}, u32[]{:S(2)}) collective-permute-start(bf16[2,256,256]{2,1,0:T(8,128)(2,1)} %bitcast.3), channel_id=1, source_target_pairs={{0,4},{4,8},{8,12},{12,0},{1,5},{5,9},{9,13},{13,1},{2,6},{6,10},{... | collective-permute-start | bytes 786440 | tf_op jit(solution)/shard_map/ppermute | solution.py:128
  3.8 1.5 %collective-permute-start.1 = (bf16[2,256,256]{2,1,0:T(8,128)(2,1)}, bf16[2,256,256]{2,1,0:T(8,128)(2,1)S(1)}, u32[]{:S(2)}, u32[]{:S(2)}) collective-permute-start(bf16[2,256,256]{2,1,0:T(8,128)(2,1)} %bitcast.4), channel_id=1, source_target_pairs={{0,2},{1,3},{2,0},{3,1},{4,6},{5,7},{6,4},{7,5},{8,10},{9,11},{10,... | collective-permute-start | bytes 786440 | tf_op jit(solution)/shard_map/ppermute | solution.py:132
  5.3 0.0 collective-permute-done.refs_1_
  5.3 1.2 %copy-done = bf16[1,256,2048]{2,1,0:T(8,128)(2,1)S(1)} copy-done((bf16[1,256,2048]{2,1,0:T(8,128)(2,1)S(1)}, bf16[1,256,2048]{2,1,0:T(8,128)(2,1)}, u32[]{:S(2)}) %copy-start) | copy-done | bytes 1048600
  6.5 0.9 %copy-done.1 = bf16[2,8,64,64]{3,2,1,0:T(8,128)(2,1)S(1)} copy-done((bf16[2,8,64,64]{3,2,1,0:T(8,128)(2,1)S(1)}, bf16[2,8,64,64]{3,2,1,0:T(8,128)(2,1)}, u32[]{:S(2)}) %copy-start.1) | copy-done | bytes 131096
  7.5 0.7 copy-done.5
  8.1 1.0 %shard_map.103 = (bf16[256,128]{1,0:T(8,128)(2,1)S(1)}, bf16[256,128]{1,0:T(8,128)(2,1)S(1)}, bf16[256,128]{1,0:T(8,128)(2,1)S(1)}, bf16[256,128]{1,0:T(8,128)(2...) custom-call(s32[2]{0:T(128)S(1)} %copy-done.5, ...), custom_call_target="tpu_custom_call" | custom-call | bytes 1048576 | tf_op jit(solution)/shard_map/pallas_call | solution.py:113
  9.1 3.8 %collective-permute-done.2.refs_4_ = bf16[2,256,256]{2,1,0:T(8,128)(2,1)S(1)} collective-permute-done((bf16[2,256,256]{2,1,0:T(8,128)(2,1)}, bf16[2,256,256]{2,1,0:T(8,128)(2,1)S(1)}, u32[]{:S(2)}, u32[]{:S(2)}) %collective-permute-start.2) | collective-permute-done | bytes 262176 | tf_op jit(solution)/shard_map/ppermute | solution.py:128
  12.9 0.0 collective-permute-done.1.refs_2_
  12.9 0.0 collective-permute-start.3
  12.9 1.0 %collective-permute-start.6 = (bf16[2,256,256]{2,1,0:T(8,128)(2,1)S(1)}, bf16[2,256,256]{2,1,0:T(8,128)(2,1)S(1)}, u32[]{:S(2)}, u32[]{:S(2)}) collective-permute-start(bf16[2,256,256]{2,1,0:T(8,128)(2,1)S(1)} %collective-permute-done.2.refs_4_), channel_id=1, source_target_pairs={{0,4},{4,8},{8,12},{12,0},{1,5},{5,9},{9,13},{13,1},{2,6},{6,10},{... | collective-permute-start | bytes 786440 | tf_op jit(solution)/shard_map/ppermute | solution.py:128
  14.0 1.5 %collective-permute-start.5 = (bf16[2,256,256]{2,1,0:T(8,128)(2,1)S(1)}, bf16[2,256,256]{2,1,0:T(8,128)(2,1)S(1)}, u32[]{:S(2)}, u32[]{:S(2)}) collective-permute-start(bf16[2,256,256]{2,1,0:T(8,128)(2,1)S(1)} %collective-permute-done.2.refs_4_), channel_id=1, source_target_pairs={{0,2},{1,3},{2,0},{3,1},{4,6},{5,7},{6,4},{7,5},{8,10},{9,11},{10,... | collective-permute-start | bytes 786440 | tf_op jit(solution)/shard_map/ppermute | solution.py:132
  15.4 0.0 collective-permute-start.4
  15.4 0.5 collective-permute-start.8
  16.0 1.1 %collective-permute-done.8.refs_1_.refs_17_ = bf16[144,128]{1,0:T(8,128)(2,1)S(1)} collective-permute-done((bf16[144,128]{1,0:T(8,128)(2,1)S(1)}, bf16[144,128]{1,0:T(8,128)(2,1)S(1)}, u32[]{:S(2)}, u32[]{:S(2)}) %collective-permute-start.8) | collective-permute-done | bytes 36896 | tf_op jit(solution)/shard_map/ppermute | solution.py:132
  17.0 0.5 collective-permute-start.9
  17.6 5.6 %collective-permute-done.9.refs_2_.refs_18_ = bf16[144,128]{1,0:T(8,128)(2,1)S(1)} collective-permute-done((bf16[144,128]{1,0:T(8,128)(2,1)S(1)}, bf16[144,128]{1,0:T(8,128)(2,1)S(1)}, u32[]{:S(2)}, u32[]{:S(2)}) %collective-permute-start.9) | collective-permute-done | bytes 36896 | tf_op jit(solution)/shard_map/ppermute | solution.py:132
  23.2 0.5 collective-permute-start.10
  23.7 3.2 %collective-permute-done.10.refs_3_.refs_19_ = bf16[144,128]{1,0:T(8,128)(2,1)S(1)} collective-permute-done((bf16[144,128]{1,0:T(8,128)(2,1)S(1)}, bf16[144,128]{1,0:T(8,128)(2,1)S(1)}, u32[]{:S(2)}, u32[]{:S(2)}) %collective-permute-start.10) | collective-permute-done | bytes 36896 | tf_op jit(solution)/shard_map/ppermute | solution.py:132
  26.9 1.6 %collective-permute-start.7 = (bf16[256,128]{1,0:T(8,128)(2,1)S(1)}, bf16[256,128]{1,0:T(8,128)(2,1)S(1)}, u32[]{:S(2)}, u32[]{:S(2)}) collective-permute-start(bf16[256,128]{1,0:T(8,128)(2,1)S(1)} %get-tuple-element.76), channel_id=1, source_target_pairs={{0,4},{4,8},{8,12},{12,0},{1,5},{5,9},{9,13},{13,1},{2,6},{6,10},{... | collective-permute-start | bytes 196616 | tf_op jit(solution)/shard_map/ppermute | solution.py:128
  28.5 4.5 %collective-permute-done.7.refs_21_ = bf16[256,128]{1,0:T(8,128)(2,1)S(1)} collective-permute-done((bf16[256,128]{1,0:T(8,128)(2,1)S(1)}, bf16[256,128]{1,0:T(8,128)(2,1)S(1)}, u32[]{:S(2)}, u32[]{:S(2)}) %collective-permute-start.7) | collective-permute-done | bytes 65568 | tf_op jit(solution)/shard_map/ppermute | solution.py:128
  33.0 0.0 collective-permute-done.3.refs_3_
  33.0 0.0 collective-permute-done.6.refs_8_
  33.0 0.0 collective-permute-done.5.refs_6_
  33.0 0.0 collective-permute-done.4.refs_5_
  33.0 0.1 collective-permute-start.11
  33.1 0.1 collective-permute-start.14
  33.1 1.2 %collective-permute-start.13 = (bf16[2,256,256]{2,1,0:T(8,128)(2,1)S(1)}, bf16[2,256,256]{2,1,0:T(8,128)(2,1)S(1)}, u32[]{:S(2)}, u32[]{:S(2)}) collective-permute-start(bf16[2,256,256]{2,1,0:T(8,128)(2,1)S(1)} %collective-permute-done.6.refs_8_), channel_id=1, source_target_pairs={{0,2},{1,3},{2,0},{3,1},{4,6},{5,7},{6,4},{7,5},{8,10},{9,11},{10,... | collective-permute-start | bytes 786440 | tf_op jit(solution)/shard_map/ppermute | solution.py:132
  34.4 0.1 collective-permute-start.12
  34.4 3.7 %collective-permute-start.15 = (bf16[256,128]{1,0:T(8,128)(2,1)S(1)}, bf16[256,128]{1,0:T(8,128)(2,1)S(1)}, u32[]{:S(2)}, u32[]{:S(2)}) collective-permute-start(bf16[256,128]{1,0:T(8,128)(2,1)S(1)} %get-tuple-element.82), channel_id=1, source_target_pairs={{0,12},{4,0},{8,4},{12,8},{1,13},{5,1},{9,5},{13,9},{2,14},{6,2},{... | collective-permute-start | bytes 196616 | tf_op jit(solution)/shard_map/ppermute | solution.py:128
  38.1 0.7 copy-done.3
  38.8 0.7 copy-done.4
  39.5 0.7 copy-done.6
  40.1 0.7 copy-done.7
  40.8 1.4 %shard_map.104 = (s32[32]{0:T(128)S(1)}, s32[4]{0:T(128)S(1)}, s32[4]{0:T(128)S(1)}, f32[4,256,128]{2,1,0:T(8,128)S(1)}) custom-call(s32[4]{0:T(128)S(1)} %copy-done.6, s32[4]{0:T(128)S(1)} %copy-done.7, f32[4,256]{1,0:T(4,128)S(1)} %copy-done.3, f32[1,512]{1,0:T(1,128)S(1)} %bitcast.6, bf16[144,128]{1,0:T(8,128)(2,1)S(1)} %get-tuple-element.83.refs_0_.refs_16_, ...), custom_call_target="tpu_custom_call" | custom-call | tf_op jit(solution)/shard_map/pallas_call | solution.py:113
  42.2 2.3 %collective-permute-done.15.refs_23_ = bf16[256,128]{1,0:T(8,128)(2,1)S(1)} collective-permute-done((bf16[256,128]{1,0:T(8,128)(2,1)S(1)}, bf16[256,128]{1,0:T(8,128)(2,1)S(1)}, u32[]{:S(2)}, u32[]{:S(2)}) %collective-permute-start.15) | collective-permute-done | bytes 65568 | tf_op jit(solution)/shard_map/ppermute | solution.py:128
  44.5 0.0 collective-permute-done.11.refs_7_
  44.5 0.0 collective-permute-done.12.refs_9_
  44.5 0.1 collective-permute-start.16
  44.6 1.0 %collective-permute-start.18 = (bf16[2,256,256]{2,1,0:T(8,128)(2,1)S(1)}, bf16[2,256,256]{2,1,0:T(8,128)(2,1)S(1)}, u32[]{:S(2)}, u32[]{:S(2)}) collective-permute-start(bf16[2,256,256]{2,1,0:T(8,128)(2,1)S(1)} %collective-permute-done.14.refs_12_), channel_id=1, source_target_pairs={{0,2},{1,3},{2,0},{3,1},{4,6},{5,7},{6,4},{7,5},{8,10},{9,11},{10,... | collective-permute-start | bytes 786440 | tf_op jit(solution)/shard_map/ppermute | solution.py:132
  45.5 0.2 collective-permute-start.17
  45.7 1.4 %collective-permute-start.19 = (bf16[256,128]{1,0:T(8,128)(2,1)S(1)}, bf16[256,128]{1,0:T(8,128)(2,1)S(1)}, u32[]{:S(2)}, u32[]{:S(2)}) collective-permute-start(bf16[256,128]{1,0:T(8,128)(2,1)S(1)} %get-tuple-element.101), channel_id=1, source_target_pairs={{0,8},{4,12},{8,0},{12,4},{1,9},{5,13},{9,1},{13,5},{2,10},{6,14},... | collective-permute-start | bytes 196616 | tf_op jit(solution)/shard_map/ppermute | solution.py:128
  47.1 4.9 %collective-permute-done.19.refs_22_ = bf16[256,128]{1,0:T(8,128)(2,1)S(1)} collective-permute-done((bf16[256,128]{1,0:T(8,128)(2,1)S(1)}, bf16[256,128]{1,0:T(8,128)(2,1)S(1)}, u32[]{:S(2)}, u32[]{:S(2)}) %collective-permute-start.19) | collective-permute-done | bytes 65568 | tf_op jit(solution)/shard_map/ppermute | solution.py:128
  52.0 0.0 collective-permute-done.16.refs_11_
  52.0 1.3 %collective-permute-done.18.refs_14_ = bf16[2,256,256]{2,1,0:T(8,128)(2,1)S(1)} collective-permute-done((bf16[2,256,256]{2,1,0:T(8,128)(2,1)S(1)}, bf16[2,256,256]{2,1,0:T(8,128)(2,1)S(1)}, u32[]{:S(2)}, u32[]{:S(2)}) %collective-permute-start.18) | collective-permute-done | bytes 262176 | tf_op jit(solution)/shard_map/ppermute | solution.py:132
  53.3 1.5 %collective-permute-done.20.refs_15_ = bf16[2,256,256]{2,1,0:T(8,128)(2,1)S(1)} collective-permute-done((bf16[2,256,256]{2,1,0:T(8,128)(2,1)S(1)}, bf16[2,256,256]{2,1,0:T(8,128)(2,1)S(1)}, u32[]{:S(2)}, u32[]{:S(2)}) %collective-permute-start.20) | collective-permute-done | bytes 262176 | tf_op jit(solution)/shard_map/ppermute | solution.py:132
  54.9 0.9 %copy-done.2 = bf16[2,1,256,256]{3,2,1,0:T(8,128)(2,1)S(1)} copy-done((bf16[2,1,256,256]{3,2,1,0:T(8,128)(2,1)S(1)}, bf16[2,1,256,256]{3,2,1,0:T(8,128)(2,1)}, u32[]{:S(2)}) %copy-start.2) | copy-done | bytes 262168
  55.8 5.3 %shard_map.105 = (f32[4,256,128]{2,1,0:T(8,128)S(1)}, bf16[4,256,128]{2,1,0:T(8,128)(2,1)S(1)}, f32[16,8,128]{2,1,0:T(8,128)}, bf16[4,4,2,256,256]{4,3,2,1,0:T(8...) custom-call(s32[32]{0:T(128)S(1)} %get-tuple-element.92.src, ...), custom_call_target="tpu_custom_call" | custom-call | flops 805306368 | bytes 8388608 | tf_op jit(solution)/shard_map/pallas_call | solution.py:113
  61.1 3.5 %all-to-all-start = ((f32[16,8,128]{2,1,0:T(8,128)}), f32[16,8,128]{2,1,0:T(8,128)S(1)}, u32[]{:S(2)}, u32[]{:S(2)}) async-start(f32[16,8,128]{2,1,0:T(8,128)} %get-tuple-element.110), calls=%async_computation | async-start | bytes 131072 | tf_op jit(solution)/shard_map/all_to_all | solution.py:496
  64.6 0.3 collective-permute-start.21
  64.9 1.7 %collective-permute-start.22 = (bf16[2,4,64,128]{3,2,1,0:T(8,128)(2,1)S(1)}, bf16[2,4,64,128]{3,2,1,0:T(8,128)(2,1)S(1)}, u32[]{:S(2)}, u32[]{:S(2)}) collective-permute-start(bf16[2,4,64,128]{3,2,1,0:T(8,128)(2,1)S(1)} %get-tuple-element.118), channel_id=1, source_target_pairs={{0,2},{1,3},{2,0},{3,1},{4,6},{5,7},{6,4},{7,5},{8,10},{9,11},{10,... | collective-permute-start | bytes 393224 | tf_op jit(solution)/shard_map/ppermute | solution.py:132
  66.6 0.0 collective-permute-start.23
  66.6 4.9 %all-to-all-done.refs_4_.parts1 = f32[16,8,128]{2,1,0:T(8,128)S(1)} async-done(((f32[16,8,128]{2,1,0:T(8,128)}), f32[16,8,128]{2,1,0:T(8,128)S(1)}, u32[]{:S(2)}, u32[]{:S(2)}) %all-to-all-start) | async-done | bytes 65568 | tf_op jit(solution)/shard_map/all_to_all | solution.py:496
  71.5 5.0 %shard_map.106 = (bf16[4,256,128]{2,1,0:T(8,128)(2,1)S(1)}, f32[4,256,128]{2,1,0:T(8,128)S(1)}, f32[16,8,128]{2,1,0:T(8,128)}, bf16[2,4,64,128]{3,2,1,0:T(8,128)...) custom-call(s32[32]{0:T(128)S(1)} %get-tuple-element.92.src, ...), custom_call_target="tpu_custom_call" | custom-call | flops 805306368 | bytes 8388608 | tf_op jit(solution)/shard_map/pallas_call | solution.py:113
  76.5 0.1 collective-permute-start.24
  76.6 0.2 collective-permute-start.25
  76.8 1.7 %collective-permute-start.26 = (bf16[2,4,64,128]{3,2,1,0:T(8,128)(2,1)S(1)}, bf16[2,4,64,128]{3,2,1,0:T(8,128)(2,1)S(1)}, u32[]{:S(2)}, u32[]{:S(2)}) collective-permute-start(bf16[2,4,64,128]{3,2,1,0:T(8,128)(2,1)S(1)} %get-tuple-element.122), channel_id=1, source_target_pairs={{0,3},{1,2},{2,1},{3,0},{4,7},{5,6},{6,5},{7,4},{8,11},{9,10},{10,... | collective-permute-start | bytes 393224 | tf_op jit(solution)/shard_map/ppermute | solution.py:132
  78.5 3.5 %all-to-all-start.1 = ((f32[16,8,128]{2,1,0:T(8,128)}), f32[16,8,128]{2,1,0:T(8,128)S(1)}, u32[]{:S(2)}, u32[]{:S(2)}) async-start(f32[16,8,128]{2,1,0:T(8,128)} %get-tuple-element.114), calls=%async_computation.1 | async-start | bytes 131072 | tf_op jit(solution)/shard_map/all_to_all | solution.py:496
  82.0 6.8 %all-to-all-done.1.parts2 = f32[16,8,128]{2,1,0:T(8,128)S(1)} async-done(((f32[16,8,128]{2,1,0:T(8,128)}), f32[16,8,128]{2,1,0:T(8,128)S(1)}, u32[]{:S(2)}, u32[]{:S(2)}) %all-to-all-start.1) | async-done | bytes 65568 | tf_op jit(solution)/shard_map/all_to_all | solution.py:496
  88.8 0.0 collective-permute-done.24.refs_3_
  88.8 0.0 collective-permute-done.25.refs_4_
  88.8 0.0 collective-permute-done.26.refs_5_
  88.9 1.7 %shard_map.107 = (bf16[4,64,512]{2,1,0:T(8,128)(2,1)}, bf16[4,64,512]{2,1,0:T(8,128)(2,1)}, f32[1]{0:T(128)}) custom-call(s32[4]{0:T(128)S(1)} %get-tuple-element.91.slots, f32[16,8,128]{2,1,0:T(8,128)S(1)} %all-to-all-done.refs_4_.parts1, f32[16,8,128]{2,1,0:T(8,128)S(1)} %all-to-all-done.1.parts2, ...), custom_call_target="tpu_custom_call" | custom-call | bytes 4194304 | tf_op jit(solution)/shard_map/pallas_call | solution.py:113
  (15 shorter events, 0.0 us)
Async XLA Ops:
  0.6 4.7 %collective-permute-start = (bf16[2,256,256]{2,1,0:T(8,128)(2,1)}, bf16[2,256,256]{2,1,0:T(8,128)(2,1)S(1)}, u32[]{:S(2)}, u32[]{:S(2)}) collective-permute-start(bf16[2,256,256]{2,1,0:T(8,128)(2,1)} %bitcast.2), channel_id=1, source_target_pairs={{0,1},{1,0},{2,3},{3,2},{4,5},{5,4},{6,7},{7,6},{8,9},{9,8},{10,11... | collective-permute-start | bytes 786440 | tf_op jit(solution)/shard_map/ppermute | solution.py:132
  1.1 11.8 %collective-permute-start.2 = (bf16[2,256,256]{2,1,0:T(8,128)(2,1)}, bf16[2,256,256]{2,1,0:T(8,128)(2,1)S(1)}, u32[]{:S(2)}, u32[]{:S(2)}) collective-permute-start(bf16[2,256,256]{2,1,0:T(8,128)(2,1)} %bitcast.3), channel_id=1, source_target_pairs={{0,4},{4,8},{8,12},{12,0},{1,5},{5,9},{9,13},{13,1},{2,6},{6,10},{... | collective-permute-start | bytes 786440 | tf_op jit(solution)/shard_map/ppermute | solution.py:128
  3.8 9.1 %collective-permute-start.1 = (bf16[2,256,256]{2,1,0:T(8,128)(2,1)}, bf16[2,256,256]{2,1,0:T(8,128)(2,1)S(1)}, u32[]{:S(2)}, u32[]{:S(2)}) collective-permute-start(bf16[2,256,256]{2,1,0:T(8,128)(2,1)} %bitcast.4), channel_id=1, source_target_pairs={{0,2},{1,3},{2,0},{3,1},{4,6},{5,7},{6,4},{7,5},{8,10},{9,11},{10,... | collective-permute-start | bytes 786440 | tf_op jit(solution)/shard_map/ppermute | solution.py:132
  5.3 1.2 %copy-start = (bf16[1,256,2048]{2,1,0:T(8,128)(2,1)S(1)}, bf16[1,256,2048]{2,1,0:T(8,128)(2,1)}, u32[]{:S(2)}) copy-start(bf16[1,256,2048]{2,1,0:T(8,128)(2,1)} %psi) | copy-start | bytes 3145732
  6.5 0.9 %copy-start.1 = (bf16[2,8,64,64]{3,2,1,0:T(8,128)(2,1)S(1)}, bf16[2,8,64,64]{3,2,1,0:T(8,128)(2,1)}, u32[]{:S(2)}) copy-start(bf16[2,8,64,64]{3,2,1,0:T(8,128)(2,1)} %right) | copy-start | bytes 393220
  7.5 0.7 copy-start.5
  12.9 20.0 %collective-permute-start.3 = (bf16[2,256,256]{2,1,0:T(8,128)(2,1)S(1)}, bf16[2,256,256]{2,1,0:T(8,128)(2,1)S(1)}, u32[]{:S(2)}, u32[]{:S(2)}) collective-permute-start(bf16[2,256,256]{2,1,0:T(8,128)(2,1)S(1)} %collective-permute-done.1.refs_2_), channel_id=1, source_target_pairs={{0,1},{1,0},{2,3},{3,2},{4,5},{5,4},{6,7},{7,6},{8,9},{9,8},{10,11... | collective-permute-start | bytes 786440 | tf_op jit(solution)/shard_map/ppermute | solution.py:132
  12.9 20.0 %collective-permute-start.6 = (bf16[2,256,256]{2,1,0:T(8,128)(2,1)S(1)}, bf16[2,256,256]{2,1,0:T(8,128)(2,1)S(1)}, u32[]{:S(2)}, u32[]{:S(2)}) collective-permute-start(bf16[2,256,256]{2,1,0:T(8,128)(2,1)S(1)} %collective-permute-done.2.refs_4_), channel_id=1, source_target_pairs={{0,4},{4,8},{8,12},{12,0},{1,5},{5,9},{9,13},{13,1},{2,6},{6,10},{... | collective-permute-start | bytes 786440 | tf_op jit(solution)/shard_map/ppermute | solution.py:128
  14.0 19.0 %collective-permute-start.5 = (bf16[2,256,256]{2,1,0:T(8,128)(2,1)S(1)}, bf16[2,256,256]{2,1,0:T(8,128)(2,1)S(1)}, u32[]{:S(2)}, u32[]{:S(2)}) collective-permute-start(bf16[2,256,256]{2,1,0:T(8,128)(2,1)S(1)} %collective-permute-done.2.refs_4_), channel_id=1, source_target_pairs={{0,2},{1,3},{2,0},{3,1},{4,6},{5,7},{6,4},{7,5},{8,10},{9,11},{10,... | collective-permute-start | bytes 786440 | tf_op jit(solution)/shard_map/ppermute | solution.py:132
  15.4 17.6 %collective-permute-start.4 = (bf16[2,256,256]{2,1,0:T(8,128)(2,1)S(1)}, bf16[2,256,256]{2,1,0:T(8,128)(2,1)S(1)}, u32[]{:S(2)}, u32[]{:S(2)}) collective-permute-start(bf16[2,256,256]{2,1,0:T(8,128)(2,1)S(1)} %collective-permute-done.2.refs_4_), channel_id=1, source_target_pairs={{0,1},{1,0},{2,3},{3,2},{4,5},{5,4},{6,7},{7,6},{8,9},{9,8},{10,11... | collective-permute-start | bytes 786440 | tf_op jit(solution)/shard_map/ppermute | solution.py:132
  15.4 1.6 %collective-permute-start.8 = (bf16[144,128]{1,0:T(8,128)(2,1)S(1)}, bf16[144,128]{1,0:T(8,128)(2,1)S(1)}, u32[]{:S(2)}, u32[]{:S(2)}) collective-permute-start(bf16[144,128]{1,0:T(8,128)(2,1)S(1)} %get-tuple-element.77), channel_id=1, source_target_pairs={{0,1},{1,0},{2,3},{3,2},{4,5},{5,4},{6,7},{7,6},{8,9},{9,8},{10,11... | collective-permute-start | bytes 110600 | tf_op jit(solution)/shard_map/ppermute | solution.py:132
  17.0 6.1 %collective-permute-start.9 = (bf16[144,128]{1,0:T(8,128)(2,1)S(1)}, bf16[144,128]{1,0:T(8,128)(2,1)S(1)}, u32[]{:S(2)}, u32[]{:S(2)}) collective-permute-start(bf16[144,128]{1,0:T(8,128)(2,1)S(1)} %get-tuple-element.78), channel_id=1, source_target_pairs={{0,2},{1,3},{2,0},{3,1},{4,6},{5,7},{6,4},{7,5},{8,10},{9,11},{10,... | collective-permute-start | bytes 110600 | tf_op jit(solution)/shard_map/ppermute | solution.py:132
  23.2 3.7 %collective-permute-start.10 = (bf16[144,128]{1,0:T(8,128)(2,1)S(1)}, bf16[144,128]{1,0:T(8,128)(2,1)S(1)}, u32[]{:S(2)}, u32[]{:S(2)}) collective-permute-start(bf16[144,128]{1,0:T(8,128)(2,1)S(1)} %get-tuple-element.79), channel_id=1, source_target_pairs={{0,3},{1,2},{2,1},{3,0},{4,7},{5,6},{6,5},{7,4},{8,11},{9,10},{10,... | collective-permute-start | bytes 110600 | tf_op jit(solution)/shard_map/ppermute | solution.py:132
  26.9 6.1 %collective-permute-start.7 = (bf16[256,128]{1,0:T(8,128)(2,1)S(1)}, bf16[256,128]{1,0:T(8,128)(2,1)S(1)}, u32[]{:S(2)}, u32[]{:S(2)}) collective-permute-start(bf16[256,128]{1,0:T(8,128)(2,1)S(1)} %get-tuple-element.76), channel_id=1, source_target_pairs={{0,4},{4,8},{8,12},{12,0},{1,5},{5,9},{9,13},{13,1},{2,6},{6,10},{... | collective-permute-start | bytes 196616 | tf_op jit(solution)/shard_map/ppermute | solution.py:128
  33.0 11.5 %collective-permute-start.11 = (bf16[2,256,256]{2,1,0:T(8,128)(2,1)S(1)}, bf16[2,256,256]{2,1,0:T(8,128)(2,1)S(1)}, u32[]{:S(2)}, u32[]{:S(2)}) collective-permute-start(bf16[2,256,256]{2,1,0:T(8,128)(2,1)S(1)} %collective-permute-done.5.refs_6_), channel_id=1, source_target_pairs={{0,1},{1,0},{2,3},{3,2},{4,5},{5,4},{6,7},{7,6},{8,9},{9,8},{10,11... | collective-permute-start | bytes 786440 | tf_op jit(solution)/shard_map/ppermute | solution.py:132
  33.1 11.4 %collective-permute-start.14 = (bf16[2,256,256]{2,1,0:T(8,128)(2,1)S(1)}, bf16[2,256,256]{2,1,0:T(8,128)(2,1)S(1)}, u32[]{:S(2)}, u32[]{:S(2)}) collective-permute-start(bf16[2,256,256]{2,1,0:T(8,128)(2,1)S(1)} %collective-permute-done.6.refs_8_), channel_id=1, source_target_pairs={{0,4},{4,8},{8,12},{12,0},{1,5},{5,9},{9,13},{13,1},{2,6},{6,10},{... | collective-permute-start | bytes 786440 | tf_op jit(solution)/shard_map/ppermute | solution.py:128
  33.1 11.4 %collective-permute-start.13 = (bf16[2,256,256]{2,1,0:T(8,128)(2,1)S(1)}, bf16[2,256,256]{2,1,0:T(8,128)(2,1)S(1)}, u32[]{:S(2)}, u32[]{:S(2)}) collective-permute-start(bf16[2,256,256]{2,1,0:T(8,128)(2,1)S(1)} %collective-permute-done.6.refs_8_), channel_id=1, source_target_pairs={{0,2},{1,3},{2,0},{3,1},{4,6},{5,7},{6,4},{7,5},{8,10},{9,11},{10,... | collective-permute-start | bytes 786440 | tf_op jit(solution)/shard_map/ppermute | solution.py:132
  34.4 10.1 %collective-permute-start.12 = (bf16[2,256,256]{2,1,0:T(8,128)(2,1)S(1)}, bf16[2,256,256]{2,1,0:T(8,128)(2,1)S(1)}, u32[]{:S(2)}, u32[]{:S(2)}) collective-permute-start(bf16[2,256,256]{2,1,0:T(8,128)(2,1)S(1)} %collective-permute-done.6.refs_8_), channel_id=1, source_target_pairs={{0,1},{1,0},{2,3},{3,2},{4,5},{5,4},{6,7},{7,6},{8,9},{9,8},{10,11... | collective-permute-start | bytes 786440 | tf_op jit(solution)/shard_map/ppermute | solution.py:132
  34.4 10.1 %collective-permute-start.15 = (bf16[256,128]{1,0:T(8,128)(2,1)S(1)}, bf16[256,128]{1,0:T(8,128)(2,1)S(1)}, u32[]{:S(2)}, u32[]{:S(2)}) collective-permute-start(bf16[256,128]{1,0:T(8,128)(2,1)S(1)} %get-tuple-element.82), channel_id=1, source_target_pairs={{0,12},{4,0},{8,4},{12,8},{1,13},{5,1},{9,5},{13,9},{2,14},{6,2},{... | collective-permute-start | bytes 196616 | tf_op jit(solution)/shard_map/ppermute | solution.py:128
  38.1 0.7 copy-start.3
  38.8 0.7 copy-start.4
  39.5 0.7 copy-start.6
  40.1 0.7 copy-start.7
  44.5 7.5 %collective-permute-start.16 = (bf16[2,256,256]{2,1,0:T(8,128)(2,1)S(1)}, bf16[2,256,256]{2,1,0:T(8,128)(2,1)S(1)}, u32[]{:S(2)}, u32[]{:S(2)}) collective-permute-start(bf16[2,256,256]{2,1,0:T(8,128)(2,1)S(1)} %collective-permute-done.13.refs_10_), channel_id=1, source_target_pairs={{0,1},{1,0},{2,3},{3,2},{4,5},{5,4},{6,7},{7,6},{8,9},{9,8},{10,11... | collective-permute-start | bytes 786440 | tf_op jit(solution)/shard_map/ppermute | solution.py:132
  44.6 8.7 %collective-permute-start.18 = (bf16[2,256,256]{2,1,0:T(8,128)(2,1)S(1)}, bf16[2,256,256]{2,1,0:T(8,128)(2,1)S(1)}, u32[]{:S(2)}, u32[]{:S(2)}) collective-permute-start(bf16[2,256,256]{2,1,0:T(8,128)(2,1)S(1)} %collective-permute-done.14.refs_12_), channel_id=1, source_target_pairs={{0,2},{1,3},{2,0},{3,1},{4,6},{5,7},{6,4},{7,5},{8,10},{9,11},{10,... | collective-permute-start | bytes 786440 | tf_op jit(solution)/shard_map/ppermute | solution.py:132
  45.5 7.8 %collective-permute-start.17 = (bf16[2,256,256]{2,1,0:T(8,128)(2,1)S(1)}, bf16[2,256,256]{2,1,0:T(8,128)(2,1)S(1)}, u32[]{:S(2)}, u32[]{:S(2)}) collective-permute-start(bf16[2,256,256]{2,1,0:T(8,128)(2,1)S(1)} %collective-permute-done.14.refs_12_), channel_id=1, source_target_pairs={{0,1},{1,0},{2,3},{3,2},{4,5},{5,4},{6,7},{7,6},{8,9},{9,8},{10,11... | collective-permute-start | bytes 786440 | tf_op jit(solution)/shard_map/ppermute | solution.py:132
  45.7 6.3 %collective-permute-start.19 = (bf16[256,128]{1,0:T(8,128)(2,1)S(1)}, bf16[256,128]{1,0:T(8,128)(2,1)S(1)}, u32[]{:S(2)}, u32[]{:S(2)}) collective-permute-start(bf16[256,128]{1,0:T(8,128)(2,1)S(1)} %get-tuple-element.101), channel_id=1, source_target_pairs={{0,8},{4,12},{8,0},{12,4},{1,9},{5,13},{9,1},{13,5},{2,10},{6,14},... | collective-permute-start | bytes 196616 | tf_op jit(solution)/shard_map/ppermute | solution.py:128
  53.3 1.5 %collective-permute-start.20 = (bf16[2,256,256]{2,1,0:T(8,128)(2,1)S(1)}, bf16[2,256,256]{2,1,0:T(8,128)(2,1)S(1)}, u32[]{:S(2)}, u32[]{:S(2)}) collective-permute-start(bf16[2,256,256]{2,1,0:T(8,128)(2,1)S(1)} %collective-permute-done.18.refs_14_), channel_id=1, source_target_pairs={{0,1},{1,0},{2,3},{3,2},{4,5},{5,4},{6,7},{7,6},{8,9},{9,8},{10,11... | collective-permute-start | bytes 786440 | tf_op jit(solution)/shard_map/ppermute | solution.py:132
  54.9 1.0 %copy-start.2 = (bf16[2,1,256,256]{3,2,1,0:T(8,128)(2,1)S(1)}, bf16[2,1,256,256]{3,2,1,0:T(8,128)(2,1)}, u32[]{:S(2)}) copy-start(bf16[2,1,256,256]{3,2,1,0:T(8,128)(2,1)} %param.9) | copy-start | bytes 786436
  61.1 10.4 %all-to-all-start = ((f32[16,8,128]{2,1,0:T(8,128)}), f32[16,8,128]{2,1,0:T(8,128)S(1)}, u32[]{:S(2)}, u32[]{:S(2)}) async-start(f32[16,8,128]{2,1,0:T(8,128)} %get-tuple-element.110), calls=%async_computation | async-start | bytes 131072 | tf_op jit(solution)/shard_map/all_to_all | solution.py:496
  64.6 12.2 %collective-permute-start.21 = (bf16[2,4,64,128]{3,2,1,0:T(8,128)(2,1)S(1)}, bf16[2,4,64,128]{3,2,1,0:T(8,128)(2,1)S(1)}, u32[]{:S(2)}, u32[]{:S(2)}) collective-permute-start(bf16[2,4,64,128]{3,2,1,0:T(8,128)(2,1)S(1)} %get-tuple-element.117), channel_id=1, source_target_pairs={{0,1},{1,0},{2,3},{3,2},{4,5},{5,4},{6,7},{7,6},{8,9},{9,8},{10,11... | collective-permute-start | bytes 393224 | tf_op jit(solution)/shard_map/ppermute | solution.py:132
  64.9 17.1 %collective-permute-start.22 = (bf16[2,4,64,128]{3,2,1,0:T(8,128)(2,1)S(1)}, bf16[2,4,64,128]{3,2,1,0:T(8,128)(2,1)S(1)}, u32[]{:S(2)}, u32[]{:S(2)}) collective-permute-start(bf16[2,4,64,128]{3,2,1,0:T(8,128)(2,1)S(1)} %get-tuple-element.118), channel_id=1, source_target_pairs={{0,2},{1,3},{2,0},{3,1},{4,6},{5,7},{6,4},{7,5},{8,10},{9,11},{10,... | collective-permute-start | bytes 393224 | tf_op jit(solution)/shard_map/ppermute | solution.py:132
  66.6 15.4 %collective-permute-start.23 = (bf16[2,4,64,128]{3,2,1,0:T(8,128)(2,1)S(1)}, bf16[2,4,64,128]{3,2,1,0:T(8,128)(2,1)S(1)}, u32[]{:S(2)}, u32[]{:S(2)}) collective-permute-start(bf16[2,4,64,128]{3,2,1,0:T(8,128)(2,1)S(1)} %get-tuple-element.119), channel_id=1, source_target_pairs={{0,3},{1,2},{2,1},{3,0},{4,7},{5,6},{6,5},{7,4},{8,11},{9,10},{10,... | collective-permute-start | bytes 393224 | tf_op jit(solution)/shard_map/ppermute | solution.py:132
  76.5 12.3 %collective-permute-start.24 = (bf16[2,4,64,128]{3,2,1,0:T(8,128)(2,1)S(1)}, bf16[2,4,64,128]{3,2,1,0:T(8,128)(2,1)S(1)}, u32[]{:S(2)}, u32[]{:S(2)}) collective-permute-start(bf16[2,4,64,128]{3,2,1,0:T(8,128)(2,1)S(1)} %get-tuple-element.120), channel_id=1, source_target_pairs={{0,1},{1,0},{2,3},{3,2},{4,5},{5,4},{6,7},{7,6},{8,9},{9,8},{10,11... | collective-permute-start | bytes 393224 | tf_op jit(solution)/shard_map/ppermute | solution.py:132
  76.6 12.2 %collective-permute-start.25 = (bf16[2,4,64,128]{3,2,1,0:T(8,128)(2,1)S(1)}, bf16[2,4,64,128]{3,2,1,0:T(8,128)(2,1)S(1)}, u32[]{:S(2)}, u32[]{:S(2)}) collective-permute-start(bf16[2,4,64,128]{3,2,1,0:T(8,128)(2,1)S(1)} %get-tuple-element.121), channel_id=1, source_target_pairs={{0,2},{1,3},{2,0},{3,1},{4,6},{5,7},{6,4},{7,5},{8,10},{9,11},{10,... | collective-permute-start | bytes 393224 | tf_op jit(solution)/shard_map/ppermute | solution.py:132
  76.8 12.0 %collective-permute-start.26 = (bf16[2,4,64,128]{3,2,1,0:T(8,128)(2,1)S(1)}, bf16[2,4,64,128]{3,2,1,0:T(8,128)(2,1)S(1)}, u32[]{:S(2)}, u32[]{:S(2)}) collective-permute-start(bf16[2,4,64,128]{3,2,1,0:T(8,128)(2,1)S(1)} %get-tuple-element.122), channel_id=1, source_target_pairs={{0,3},{1,2},{2,1},{3,0},{4,7},{5,6},{6,5},{7,4},{8,11},{9,10},{10,... | collective-permute-start | bytes 393224 | tf_op jit(solution)/shard_map/ppermute | solution.py:132
  78.5 10.4 %all-to-all-start.1 = ((f32[16,8,128]{2,1,0:T(8,128)}), f32[16,8,128]{2,1,0:T(8,128)S(1)}, u32[]{:S(2)}, u32[]{:S(2)}) async-start(f32[16,8,128]{2,1,0:T(8,128)} %get-tuple-element.114), calls=%async_computation.1 | async-start | bytes 131072 | tf_op jit(solution)/shard_map/all_to_all | solution.py:496

commit v7 on v6

--- a/solution.py
+++ b/solution.py
@@ -132,10 +132,9 @@
     return lax.ppermute(block, "op", [(i, i ^ e) for i in range(n_op)])
 
 
-def gather(own, n_blk, n_op, pack, table):
+def gather(own, n_blk, n_op, pack, table, early):
     bits = [1 << b for b in reversed(range(n_op.bit_length() - 1))]
-    order = sorted(range(1, n_blk), key=lambda d: min(d, n_blk - d))
-    left, psi, right, tables = {(0, 0): own}, {}, {}, None
+    left, psi, right, made = {(0, 0): own}, [], [], {}
     waiting = {(0, 0): 0}
     for j in range(n_blk + len(bits)):
         new, moved = {}, {}
@@ -146,38 +145,42 @@
                 new[d, e ^ bits[b]] = swap(left[d, e], bits[b], n_op), b + 1
         kept = {key: block for key, (block, _) in new.items()}
         if j == 0:
-            sent = pack(kept[0, bits[-1]])
-            moved["sent"] = sent
+            columns, packed = pack(kept[0, bits[-1]])
+            moved["right"] = [packed[0]] + [swap(packed[e], e, n_op) for e in range(1, n_op)]
+            moved["columns"] = columns
+        elif j < n_blk:
+            moved["psi"] = onward(columns[j], j, n_blk)
         if j == 1:
-            moved["right"] = [swap(sent[1][e], e, n_op) for e in range(1, n_op)]
-        if 1 <= j < n_blk:
-            d = order[j - 1]
-            moved["psi"] = onward(sent[0][d], d, n_blk)
-        if j == 2:
-            moved["tables"] = table([sent[1][0]] + right)
+            moved["tables"] = table(right)
+        full = j - len(bits) + 1
+        if j == n_blk - 1 and full > 0:
+            moved["early"] = early(left, psi, full, made["tables"])
         if not kept and not moved:
             break
         waiting = {key: done for key, (_, done) in new.items()}
         kept, moved = lax.optimization_barrier((kept, moved))
         left.update(kept)
-        sent = moved.get("sent", sent)
-        right = moved.get("right", right)
-        tables = moved.get("tables", tables)
-        if "psi" in moved:
-            psi[d] = moved["psi"]
-    return left, [sent[0][0]] + [psi[d] for d in range(1, n_blk)], [sent[1][0]] + right, tables
+        if j == 0:
+            columns, right = moved["columns"], moved["right"]
+            psi = list(columns[:1])
+        elif j < n_blk:
+            psi = psi + [moved["psi"]]
+        made.update({key: moved[key] for key in ("tables", "early") if key in moved})
+    return left, psi, right, made["tables"], made.get("early")
 
 
 def place_of():
     return lax.axis_index("blk"), lax.axis_index("op")
 
 
-def pack_body(n_blk, n_op, shift, psi, right, *outs):
-    psi_out, right_out, sems = outs[:n_blk], outs[n_blk : n_blk + n_op], outs[-1]
+def pack_body(n_blk, n_op, shift, psi, right_in, *outs):
+    psi_out, right_out, right, sems = outs[:n_blk], outs[n_blk : n_blk + n_op], outs[-2], outs[-1]
     cols = psi_out[0].shape[1]
     terms, _, width, _ = right.shape
     per = cols // width
     own_blk, own_op = place_of()
+    fetch = pltpu.make_async_copy(right_in, right, sems.at[n_blk])
+    fetch.start()
     copies = []
     for d in range(n_blk):
         there = lax.rem(own_blk + d, n_blk)
@@ -192,6 +195,7 @@
         line = jnp.where(lane == k, shift[k].astype(jnp.float32), line)
     square = [lax.broadcasted_iota(jnp.int32, (width, width), axis) for axis in (0, 1)]
     unit = (square[0] == square[1]).astype(jnp.bfloat16)
+    fetch.wait()
     for e in range(n_op):
         there = (own_op ^ e) * per
         for k in range(terms):
@@ -267,32 +271,58 @@
     return jnp.concatenate(parts, axis=0)
 
 
-def apply_h(src, field, left, right, inter, emit):
-    n_blk, n_op = inter.shape[0] - 1, len(right)
-    rows, cols = inter.shape[2], inter.shape[3]
-    terms = inter.shape[1] // n_op
-    inter[n_blk] = jnp.zeros_like(inter[n_blk])
+def left_products(block, left, inter):
+    n_terms, rows, cols = inter.shape
+    at = 0
+    while at < n_terms:
+        ops = left(at)
+        terms = ops.shape[0]
+        prod = jnp.dot(ops.reshape(terms * rows, rows), block, preferred_element_type=jnp.float32)
+        inter[at : at + terms] = prod.astype(jnp.bfloat16).reshape(terms, rows, cols)
+        at += terms
+
+
+def sum_terms(src, inter, right, emit):
+    n_blk, n_terms, _, cols = inter.shape
+    n_blk, n_op = n_blk - 1, len(right)
+    terms = n_terms // n_op
     diagonal = [by_block(ref, terms, cols) for ref in right]
-    for d in range(n_blk):
-        block = field(d)
-        for e in range(n_op):
-            ops = left(d, e).reshape(terms * rows, rows)
-            prod = jnp.dot(ops, block, preferred_element_type=jnp.float32)
-            prod = prod.astype(jnp.bfloat16).reshape(terms, rows, cols)
-            inter[d, e * terms : (e + 1) * terms] = prod
     for t in range(n_blk):
         total = None
         for e in range(n_op):
             js = range(e * terms, (e + 1) * terms)
-            moved = jnp.concatenate([inter[src[t * n_op * terms + j], j] for j in js], axis=1)
+            moved = jnp.concatenate([inter[src[t * n_terms + j], j] for j in js], axis=1)
             part = jnp.dot(moved, diagonal[e], preferred_element_type=jnp.float32)
             total = part if total is None else total + part
         emit(t, total)
 
 
-def split_refs(refs, n_blk, n_op):
+def keep(left, left_out, sems):
+    copies = []
+    for d, line in enumerate(left):
+        for e, ref in enumerate(line):
+            copies.append(pltpu.make_async_copy(ref, left_out.at[d, e], sems.at[d * len(line) + e]))
+            copies[-1].start()
+    return copies
+
+
+def masked(ref, width):
+    block = ref[...].astype(jnp.float32)
+    return jnp.where(row_mask(width, block.shape), block, 0.0).astype(jnp.bfloat16)
+
+
+def early_body(n_blk, n_op, widths, *refs):
     left = [refs[d * n_op : (d + 1) * n_op] for d in range(n_blk)]
-    return left, refs[n_blk * n_op :]
+    psi, refs = refs[n_blk * n_op : n_blk * (n_op + 1)], refs[n_blk * (n_op + 1) :]
+    inter_out, left_out, sems = refs
+    copies = keep(left, left_out, sems)
+    for d in range(n_blk):
+        terms = left[d][0].shape[0]
+        left_products(
+            masked(psi[d], widths[d]), lambda at: left[d][at // terms][...], inter_out.at[d]
+        )
+    for copy in copies:
+        copy.wait()
 
 
 def send_rows(sends, j, d, ref):
@@ -303,25 +333,25 @@
         send[j, d] = ref[d, pl.ds(start, step)].astype(send.dtype)
 
 
-def first_body(n_blk, n_op, src, widths, *refs):
-    left, refs = split_refs(refs, n_blk, n_op)
+def first_body(n_blk, n_op, n_early, src, widths, *refs):
+    n_late = n_blk - n_early
+    left = [refs[d * n_op : (d + 1) * n_op] for d in range(n_late)]
+    refs = refs[n_late * n_op :]
     right, psi, refs = refs[:n_op], refs[n_op : n_op + n_blk], refs[n_op + n_blk :]
-    dmat, sig_out, raw_out, dots_out, left_out = refs[:5]
-    sends, inter, sems = refs[5:-2], refs[-2], refs[-1]
-    copies = []
-    for d in range(n_blk):
-        for e in range(n_op):
-            copies.append(
-                pltpu.make_async_copy(left[d][e], left_out.at[d, e], sems.at[d * n_op + e])
-            )
-            copies[-1].start()
-
-    def field(d):
-        block = psi[d][...].astype(jnp.float32)
-        block = jnp.where(row_mask(widths[d], block.shape), block, 0.0)
-        raw_out[d] = block.astype(jnp.bfloat16)
-        return raw_out[d]
-
+    dmat, inter_in, sig_out, raw_out, dots_out, left_out = refs[:6]
+    sends, inter, sems = refs[6:-2], refs[-2], refs[-1]
+    copies = keep(left, left_out, sems)
+    ready = pltpu.make_async_copy(inter_in, inter.at[:n_early], sems.at[n_late * n_op])
+    ready.start()
+    inter[n_blk] = jnp.zeros_like(inter[n_blk])
+    for d in range(n_blk):
+        raw_out[d] = masked(psi[d], widths[d])
+    for d in range(n_late):
+        terms = left[d][0].shape[0]
+        left_products(
+            raw_out[n_early + d], lambda at: left[d][at // terms][...], inter.at[n_early + d]
+        )
+    ready.wait()
     zero = jnp.zeros((8, dmat.shape[2]), jnp.float32)
     sums = [zero, zero]
 
@@ -334,7 +364,7 @@
         send_rows(sends, 0, d, raw_out)
         send_rows(sends, 1, d, sig_out)
 
-    apply_h(src, field, lambda d, e: left[d][e][...], right, inter, emit)
+    sum_terms(src, inter, right, emit)
     spread([whole(x) for x in sums], dots_out)
     for copy in copies:
         copy.wait()
@@ -346,13 +376,17 @@
     return scale, tot[1:2] * scale * scale
 
 
-def second_body(n_blk, n_op, count, src, widths, left_in, *refs):
+def second_body(n_blk, n_op, count, src, widths, left_early, left_late, *refs):
     right, refs = refs[:n_op], refs[n_op:]
+    n_early = left_early.shape[0]
     parts, raw_in, sig_in, dmat, f_out, t_out, dots_out = refs[:7]
     sends, inter, corr, held, sems = refs[7:-4], *refs[-4:]
-    copies = [pltpu.make_async_copy(left_in.at[d], held.at[d], sems.at[d]) for d in range(n_blk)]
-    for copy in copies:
-        copy.start()
+    copies = []
+    for d in range(n_blk):
+        kept = left_early.at[d] if d < n_early else left_late.at[d - n_early]
+        copies.append(pltpu.make_async_copy(kept, held.at[d], sems.at[d]))
+        copies[-1].start()
+    inter[n_blk] = jnp.zeros_like(inter[n_blk])
     scale, theta = norm_theta(parts[...], count)
     zero = jnp.zeros((8, raw_in.shape[2]), jnp.float32)
     vv, vc, vs = zero, zero, zero
@@ -366,12 +400,12 @@
     vv, vc, vs = whole(vv), whole(vc), whole(vs)
     along = vc / jnp.maximum(vv, 1e-30)
 
-    def field(d):
+    for d in range(n_blk):
         vec = raw_in[d].astype(jnp.float32) * scale
         f_out[d] = (corr[d] - along * vec).astype(jnp.bfloat16)
         copies[d].wait()
-        return f_out[d]
-
+        terms = held.shape[2]
+        left_products(f_out[d], lambda at: held[d, at // terms], inter.at[d])
     sums = [zero for _ in range(5)]
 
     def emit(d, total):
@@ -385,7 +419,7 @@
         send_rows(sends, 0, d, f_out)
         send_rows(sends, 1, d, t_out)
 
-    apply_h(src, field, lambda d, e: held[d, e], right, inter, emit)
+    sum_terms(src, inter, right, emit)
     spread([vv, vc, vs] + [whole(x) for x in sums], dots_out)
 
 
@@ -460,9 +494,9 @@
         given = lax.optimization_barrier((term_shift, psi, right_ops, after))
         sent = kernel(
             functools.partial(pack_body, n_blk, n_op),
-            list(zip(given, (SMEM, ANY, VMEM))),
+            list(zip(given, (SMEM, HBM, HBM))),
             [((rows, cols), bf16, VMEM)] * n_blk + [((terms * width + 16, cols), bf16, VMEM)] * n_op,
-            [pltpu.SemaphoreType.DMA((n_blk,))],
+            [pltpu.VMEM(right_ops.shape, bf16), pltpu.SemaphoreType.DMA((n_blk + 1,))],
             nbytes=1 << 20,
         )
         return sent[:n_blk], sent[n_blk:]
@@ -477,8 +511,28 @@
             + [((n_blk, rows, cols), f32, VMEM)],
         )
 
-    left, psi_by, right, (src, widths, slots, dmat) = gather(left_ops[:, 0], n_blk, n_op, pack, table)
-    left_ins = [(left[d, e], VMEM) for d in range(n_blk) for e in range(n_op)]
+    def early(left, psi, n_early, tables):
+        outs = [
+            ((n_early, n_op * terms, rows, cols), bf16, VMEM),
+            ((n_early, n_op, terms, rows, rows), bf16, HBM),
+        ]
+        return kernel(
+            functools.partial(early_body, n_early, n_op),
+            [(tables[1], SMEM)]
+            + [(left[d, e], VMEM) for d in range(n_early) for e in range(n_op)]
+            + [(psi[d], VMEM) for d in range(n_early)],
+            outs,
+            [pltpu.SemaphoreType.DMA((n_early * n_op,))],
+            flops=2 * n_early * rows * rows * cols * terms * n_op,
+            nbytes=8 << 20,
+        )
+
+    left, psi_by, right, (src, widths, slots, dmat), (inter_early, left_early) = gather(
+        left_ops[:, 0], n_blk, n_op, pack, table, early
+    )
+    n_early = inter_early.shape[0]
+    n_late = n_blk - n_early
+    left_ins = [(left[d, e], VMEM) for d in range(n_early, n_blk) for e in range(n_op)]
     right_ins = [(block, VMEM) for block in right]
     psi_ins = [(block, VMEM) for block in psi_by]
 
@@ -488,7 +542,7 @@
     dots = ((n_dev, 8, LANES), f32, VMEM)
     sends = [((2, n_blk, step, cols), bf16, VMEM)] * (n_op - 1)
     inter = pltpu.VMEM((n_blk + 1, n_op * terms, rows, cols), bf16)
-    left_all = (n_blk, n_op, terms, rows, rows)
+    left_late = (n_late, n_op, terms, rows, rows)
     flops = 2 * n_blk * rows * cols * terms * n_op * (rows + cols)
     cost = dict(flops=flops, nbytes=8 << 20)
 
@@ -496,19 +550,19 @@
         return lax.all_to_all(parts, ("blk", "op"), 0, 0, tiled=True)
 
     sig, raw, dots1, kept, *out1 = kernel(
-        functools.partial(first_body, n_blk, n_op),
-        tables + left_ins + right_ins + psi_ins + [(dmat, VMEM)],
-        [wide, narrow, dots, (left_all, bf16, HBM)] + sends,
-        [inter, pltpu.SemaphoreType.DMA((n_dev,))],
+        functools.partial(first_body, n_blk, n_op, n_early),
+        tables + left_ins + right_ins + psi_ins + [(dmat, VMEM), (inter_early, VMEM)],
+        [wide, narrow, dots, (left_late, bf16, HBM)] + sends,
+        [inter, pltpu.SemaphoreType.DMA((n_late * n_op + 1,))],
         **cost,
     )
     parts1 = totals(dots1)
     got1 = [swap(block, e, n_op) for e, block in enumerate(out1, 1)]
     fld, img, dots2, *out2 = kernel(
         functools.partial(second_body, n_blk, n_op, count),
-        tables + [(kept, HBM)] + right_ins + [(x, VMEM) for x in (parts1, raw, sig, dmat)],
+        tables + [(left_early, HBM), (kept, HBM)] + right_ins + [(x, VMEM) for x in (parts1, raw, sig, dmat)],
         [narrow, wide, dots] + sends,
-        [inter, pltpu.VMEM((n_blk, rows, cols), f32), pltpu.VMEM(left_all, bf16), pltpu.SemaphoreType.DMA((n_blk,))],
+        [inter, pltpu.VMEM((n_blk, rows, cols), f32), pltpu.VMEM((n_blk, *left_late[1:]), bf16), pltpu.SemaphoreType.DMA((n_blk,))],
         **cost,
     )
     parts2 = totals(dots2)
@@ -548,6 +602,7 @@
             and cols // right_ops.shape[2] * n_op == right_ops.shape[1]
             and psi.shape[1] % (16 * n_op) == 0
             and n_op & (n_op - 1) == 0
+            and mesh.shape["blk"] >= n_op.bit_length()
         )
         return (per_device if fits else per_device_general)(*args)
 

time: 91 us -> 82.1 us (0.902)
  waiting for transfers between devices: 40 us -> 34.8 us
  local copies, waits for them, and re-layouts: 6.46 us -> 4.28 us
  starting transfers between devices: 28.8 us -> 26.8 us
    ppermute x21, waiting for transfers between devices: 12.8 us -> 5.06 us  [swap(): return lax.ppermute(block, 'op', [(i, i ^ e) for i in range(n_op)])]
    ppermute x6, starting transfers between devices: 10.3 us -> 6.86 us  [onward(): lax.ppermute(block, 'blk', [(i, (i + d) % n_blk) for i in range(n_blk)])]
    ppermute x6, waiting for transfers between devices: 15.5 us -> 18.1 us  [onward(): lax.ppermute(block, 'blk', [(i, (i + d) % n_blk) for i in range(n_blk)])]
    unnamed x16 -> x12, local copies, waits for them, and re-layouts: 6.46 us -> 4.28 us
    ppermute x21, starting transfers between devices: 11.5 us -> 12.9 us  [swap(): return lax.ppermute(block, 'op', [(i, i ^ e) for i in range(n_op)])]
    pallas_call x5 -> x6, Pallas kernels: 14.4 us -> 15 us  [kernel(): pl.pallas_call(body, out_shape=[HBM(shape, dtype) if space == HBM else ja...]
  transfers between devices with their start and end apart: 29 -> 29, of which waited for: 11 -> 10; matrix products, arithmetic and copies ran while one was open for 0% -> 0% of each run, Pallas kernels for 8% -> 13%
where the time goes in v7:
time: 82.1 us; the launch traced here: 81.7 us
  waiting for transfers between devices  34.8 us (42%)
  starting transfers between devices  26.8 us (33%)
  Pallas kernels  15 us (18%)
  local copies, waits for them, and re-layouts  4.28 us (5%)
    ppermute x6, waiting for transfers between devices, onward(): lax.ppermute(block, 'blk', [(i, (i + d) % n_blk) for i in range(n_blk)])  18.1 us
    pallas_call x6, Pallas kernels, kernel(): pl.pallas_call(body, out_shape=[HBM(shape, dtype) if space == HBM else ja...  15 us
    ppermute x21, starting transfers between devices, swap(): return lax.ppermute(block, 'op', [(i, i ^ e) for i in range(n_op)])  12.9 us
    all_to_all x2, waiting for transfers between devices, totals(): return lax.all_to_all(parts, ('blk', 'op'), 0, 0, tiled=True)  11.7 us
    all_to_all x2, starting transfers between devices, totals(): return lax.all_to_all(parts, ('blk', 'op'), 0, 0, tiled=True)  7.02 us
    ppermute x6, starting transfers between devices, onward(): lax.ppermute(block, 'blk', [(i, (i + d) % n_blk) for i in range(n_blk)])  6.86 us
    ppermute x21, waiting for transfers between devices, swap(): return lax.ppermute(block, 'op', [(i, i ^ e) for i in range(n_op)])  5.06 us
    unnamed x12, local copies, waits for them, and re-layouts  4.28 us
  transfers between devices with their start and end apart: 29, of which 10 were waited for; matrix products, arithmetic and copies ran while one was open for 0% of the time, Pallas kernels for 13%

profile of v7, /device:TPU:0, one launch (start us, length us, event | category | flops | bytes accessed | tf_op | source)
XLA Modules:
  0.0 81.7 jit_solution(3033358793255708547)
XLA Ops:
  0.6 0.5 collective-permute-start
  1.1 2.6 %collective-permute-start.2 = (bf16[2,256,256]{2,1,0:T(8,128)(2,1)}, bf16[2,256,256]{2,1,0:T(8,128)(2,1)S(1)}, u32[]{:S(2)}, u32[]{:S(2)}) collective-permute-start(bf16[2,256,256]{2,1,0:T(8,128)(2,1)} %bitcast.3), channel_id=1, source_target_pairs={{0,4},{4,8},{8,12},{12,0},{1,5},{5,9},{9,13},{13,1},{2,6},{6,10},{... | collective-permute-start | bytes 786440 | tf_op jit(solution)/shard_map/ppermute | solution.py:128
  3.8 1.5 %collective-permute-start.1 = (bf16[2,256,256]{2,1,0:T(8,128)(2,1)}, bf16[2,256,256]{2,1,0:T(8,128)(2,1)S(1)}, u32[]{:S(2)}, u32[]{:S(2)}) collective-permute-start(bf16[2,256,256]{2,1,0:T(8,128)(2,1)} %bitcast.4), channel_id=1, source_target_pairs={{0,2},{1,3},{2,0},{3,1},{4,6},{5,7},{6,4},{7,5},{8,10},{9,11},{10,... | collective-permute-start | bytes 786440 | tf_op jit(solution)/shard_map/ppermute | solution.py:132
  5.3 0.0 collective-permute-done.refs_1_
  5.3 0.7 copy-done.3
  5.9 1.9 %shard_map.103 = (bf16[256,128]{1,0:T(8,128)(2,1)S(1)}, bf16[256,128]{1,0:T(8,128)(2,1)S(1)}, bf16[256,128]{1,0:T(8,128)(2,1)S(1)}, bf16[256,128]{1,0:T(8,128)(2...) custom-call(s32[2]{0:T(128)S(1)} %copy-done.3, ...), custom_call_target="tpu_custom_call" | custom-call | bytes 1048576 | tf_op jit(solution)/shard_map/pallas_call | solution.py:113
  7.8 0.1 collective-permute-start.3
  7.9 0.6 collective-permute-start.4
  8.5 1.3 %collective-permute-start.5 = (bf16[144,128]{1,0:T(8,128)(2,1)S(1)}, bf16[144,128]{1,0:T(8,128)(2,1)S(1)}, u32[]{:S(2)}, u32[]{:S(2)}) collective-permute-start(bf16[144,128]{1,0:T(8,128)(2,1)S(1)} %get-tuple-element.74), channel_id=1, source_target_pairs={{0,3},{1,2},{2,1},{3,0},{4,7},{5,6},{6,5},{7,4},{8,11},{9,10},{10,... | collective-permute-start | bytes 110600 | tf_op jit(solution)/shard_map/ppermute | solution.py:132
  9.8 3.2 %collective-permute-done.2.refs_4_ = bf16[2,256,256]{2,1,0:T(8,128)(2,1)S(1)} collective-permute-done((bf16[2,256,256]{2,1,0:T(8,128)(2,1)}, bf16[2,256,256]{2,1,0:T(8,128)(2,1)S(1)}, u32[]{:S(2)}, u32[]{:S(2)}) %collective-permute-start.2) | collective-permute-done | bytes 262176 | tf_op jit(solution)/shard_map/ppermute | solution.py:128
  12.9 0.2 collective-permute-done.1.refs_2_
  13.2 0.0 collective-permute-done.3.refs_1_.refs_9_
  13.2 0.4 collective-permute-done.4.refs_2_.refs_10_
  13.6 0.0 collective-permute-done.5.refs_3_.refs_11_
  13.6 0.2 collective-permute-start.6
  13.8 1.6 %collective-permute-start.9 = (bf16[2,256,256]{2,1,0:T(8,128)(2,1)S(1)}, bf16[2,256,256]{2,1,0:T(8,128)(2,1)S(1)}, u32[]{:S(2)}, u32[]{:S(2)}) collective-permute-start(bf16[2,256,256]{2,1,0:T(8,128)(2,1)S(1)} %collective-permute-done.2.refs_4_), channel_id=1, source_target_pairs={{0,4},{4,8},{8,12},{12,0},{1,5},{5,9},{9,13},{13,1},{2,6},{6,10},{... | collective-permute-start | bytes 786440 | tf_op jit(solution)/shard_map/ppermute | solution.py:128
  15.3 1.5 %collective-permute-start.8 = (bf16[2,256,256]{2,1,0:T(8,128)(2,1)S(1)}, bf16[2,256,256]{2,1,0:T(8,128)(2,1)S(1)}, u32[]{:S(2)}, u32[]{:S(2)}) collective-permute-start(bf16[2,256,256]{2,1,0:T(8,128)(2,1)S(1)} %collective-permute-done.2.refs_4_), channel_id=1, source_target_pairs={{0,2},{1,3},{2,0},{3,1},{4,6},{5,7},{6,4},{7,5},{8,10},{9,11},{10,... | collective-permute-start | bytes 786440 | tf_op jit(solution)/shard_map/ppermute | solution.py:132
  16.8 0.0 collective-permute-start.7
  16.8 1.6 %collective-permute-start.10 = (bf16[256,128]{1,0:T(8,128)(2,1)S(1)}, bf16[256,128]{1,0:T(8,128)(2,1)S(1)}, u32[]{:S(2)}, u32[]{:S(2)}) collective-permute-start(bf16[256,128]{1,0:T(8,128)(2,1)S(1)} %get-tuple-element.77), channel_id=1, source_target_pairs={{0,4},{4,8},{8,12},{12,0},{1,5},{5,9},{9,13},{13,1},{2,6},{6,10},{... | collective-permute-start | bytes 196616 | tf_op jit(solution)/shard_map/ppermute | solution.py:128
  18.4 0.7 copy-done.1
  19.1 0.7 copy-done.2
  19.8 0.7 copy-done.4
  20.4 0.7 copy-done.5
  21.1 1.4 %shard_map.104 = (s32[32]{0:T(128)S(1)}, s32[4]{0:T(128)S(1)}, s32[4]{0:T(128)S(1)}, f32[4,256,128]{2,1,0:T(8,128)S(1)}) custom-call(s32[4]{0:T(128)S(1)} %copy-done.4, s32[4]{0:T(128)S(1)} %copy-done.5, f32[4,256]{1,0:T(4,128)S(1)} %copy-done.1, f32[1,512]{1,0:T(1,128)S(1)} %bitcast.6, bf16[144,128]{1,0:T(8,128)(2,1)S(1)} %get-tuple-element.78.refs_0_.refs_8_, ...), custom_call_target="tpu_custom_call" | custom-call | tf_op jit(solution)/shard_map/pallas_call | solution.py:113
  22.5 3.0 %collective-permute-done.10.refs_9_.refs_13_ = bf16[256,128]{1,0:T(8,128)(2,1)S(1)} collective-permute-done((bf16[256,128]{1,0:T(8,128)(2,1)S(1)}, bf16[256,128]{1,0:T(8,128)(2,1)S(1)}, u32[]{:S(2)}, u32[]{:S(2)}) %collective-permute-start.10) | collective-permute-done | bytes 65568 | tf_op jit(solution)/shard_map/ppermute | solution.py:128
  25.5 0.0 collective-permute-done.6.refs_3_
  25.5 0.0 collective-permute-done.9.refs_0_
  25.5 0.0 collective-permute-done.8.refs_6_
  25.5 0.0 collective-permute-done.7.refs_5_
  25.5 0.1 collective-permute-start.11
  25.6 0.1 collective-permute-start.14
  25.7 1.6 %collective-permute-start.13 = (bf16[2,256,256]{2,1,0:T(8,128)(2,1)S(1)}, bf16[2,256,256]{2,1,0:T(8,128)(2,1)S(1)}, u32[]{:S(2)}, u32[]{:S(2)}) collective-permute-start(bf16[2,256,256]{2,1,0:T(8,128)(2,1)S(1)} %collective-permute-done.9.refs_0_), channel_id=1, source_target_pairs={{0,2},{1,3},{2,0},{3,1},{4,6},{5,7},{6,4},{7,5},{8,10},{9,11},{10,... | collective-permute-start | bytes 786440 | tf_op jit(solution)/shard_map/ppermute | solution.py:132
  27.2 0.1 collective-permute-start.12
  27.3 0.9 %collective-permute-start.15 = (bf16[256,128]{1,0:T(8,128)(2,1)S(1)}, bf16[256,128]{1,0:T(8,128)(2,1)S(1)}, u32[]{:S(2)}, u32[]{:S(2)}) collective-permute-start(bf16[256,128]{1,0:T(8,128)(2,1)S(1)} %get-tuple-element.91), channel_id=1, source_target_pairs={{0,8},{4,12},{8,0},{12,4},{1,9},{5,13},{9,1},{13,5},{2,10},{6,14},... | collective-permute-start | bytes 196616 | tf_op jit(solution)/shard_map/ppermute | solution.py:128
  28.2 10.7 %collective-permute-done.15.refs_14_ = bf16[256,128]{1,0:T(8,128)(2,1)S(1)} collective-permute-done((bf16[256,128]{1,0:T(8,128)(2,1)S(1)}, bf16[256,128]{1,0:T(8,128)(2,1)S(1)}, u32[]{:S(2)}, u32[]{:S(2)}) %collective-permute-start.15) | collective-permute-done | bytes 65568 | tf_op jit(solution)/shard_map/ppermute | solution.py:128
  38.9 0.0 collective-permute-done.11.refs_7_
  38.9 0.0 collective-permute-done.12.refs_1_
  38.9 0.1 collective-permute-start.16
  39.1 1.3 %collective-permute-start.18 = (bf16[2,256,256]{2,1,0:T(8,128)(2,1)S(1)}, bf16[2,256,256]{2,1,0:T(8,128)(2,1)S(1)}, u32[]{:S(2)}, u32[]{:S(2)}) collective-permute-start(bf16[2,256,256]{2,1,0:T(8,128)(2,1)S(1)} %collective-permute-done.14.refs_4_), channel_id=1, source_target_pairs={{0,2},{1,3},{2,0},{3,1},{4,6},{5,7},{6,4},{7,5},{8,10},{9,11},{10,... | collective-permute-start | bytes 786440 | tf_op jit(solution)/shard_map/ppermute | solution.py:132
  40.4 0.2 collective-permute-start.17
  40.5 0.1 collective-permute-start.19
  40.6 0.9 %copy-done = bf16[2,1,256,256]{3,2,1,0:T(8,128)(2,1)S(1)} copy-done((bf16[2,1,256,256]{3,2,1,0:T(8,128)(2,1)S(1)}, bf16[2,1,256,256]{3,2,1,0:T(8,128)(2,1)}, u32[]{:S(2)}) %copy-start) | copy-done | bytes 262168
  41.6 2.1 %shard_map.105 = (bf16[2,8,256,128]{3,2,1,0:T(8,128)(2,1)S(1)}, bf16[2,4,2,256,256]{4,3,2,1,0:T(8,128)(2,1)}) custom-call(s32[4]{0:T(128)S(1)} %get-tuple-element.88.widths, bf16[2,256,256]{2,1,0:T(8,128)(2,1)S(1)} %bitcast.5, bf16[2,256,256]{2,1,0:T(8,128)(2,1)S(1)} %collective-permute-done.refs_1_, ...), custom_call_target="tpu_custom_call" | custom-call | flops 268435456 | bytes 8388608 | tf_op jit(solution)/shard_map/pallas_call | solution.py:113
  43.6 1.2 %collective-permute-done.19.refs_15_ = bf16[256,128]{1,0:T(8,128)(2,1)S(1)} collective-permute-done((bf16[256,128]{1,0:T(8,128)(2,1)S(1)}, bf16[256,128]{1,0:T(8,128)(2,1)S(1)}, u32[]{:S(2)}, u32[]{:S(2)}) %collective-permute-start.19) | collective-permute-done | bytes 65568 | tf_op jit(solution)/shard_map/ppermute | solution.py:128
  44.9 0.0 collective-permute-done.16.refs_3_
  44.9 2.9 %collective-permute-done.18.refs_6_ = bf16[2,256,256]{2,1,0:T(8,128)(2,1)S(1)} collective-permute-done((bf16[2,256,256]{2,1,0:T(8,128)(2,1)S(1)}, bf16[2,256,256]{2,1,0:T(8,128)(2,1)S(1)}, u32[]{:S(2)}, u32[]{:S(2)}) %collective-permute-start.18) | collective-permute-done | bytes 262176 | tf_op jit(solution)/shard_map/ppermute | solution.py:132
  47.7 0.0 collective-permute-start.20
  47.7 1.5 %collective-permute-done.20.refs_7_ = bf16[2,256,256]{2,1,0:T(8,128)(2,1)S(1)} collective-permute-done((bf16[2,256,256]{2,1,0:T(8,128)(2,1)S(1)}, bf16[2,256,256]{2,1,0:T(8,128)(2,1)S(1)}, u32[]{:S(2)}, u32[]{:S(2)}) %collective-permute-start.20) | collective-permute-done | bytes 262176 | tf_op jit(solution)/shard_map/ppermute | solution.py:132
  49.3 3.0 %shard_map.106 = (f32[4,256,128]{2,1,0:T(8,128)S(1)}, bf16[4,256,128]{2,1,0:T(8,128)(2,1)S(1)}, f32[16,8,128]{2,1,0:T(8,128)}, bf16[2,4,2,256,256]{4,3,2,1,0:T(8...) custom-call(s32[32]{0:T(128)S(1)} %get-tuple-element.87.src, ...), custom_call_target="tpu_custom_call" | custom-call | flops 805306368 | bytes 8388608 | tf_op jit(solution)/shard_map/pallas_call | solution.py:113
  52.2 3.5 %all-to-all-start = ((f32[16,8,128]{2,1,0:T(8,128)}), f32[16,8,128]{2,1,0:T(8,128)S(1)}, u32[]{:S(2)}, u32[]{:S(2)}) async-start(f32[16,8,128]{2,1,0:T(8,128)} %get-tuple-element.111), calls=%async_computation | async-start | bytes 131072 | tf_op jit(solution)/shard_map/all_to_all | solution.py:550
  55.8 0.3 collective-permute-start.21
  56.1 1.7 %collective-permute-start.22 = (bf16[2,4,64,128]{3,2,1,0:T(8,128)(2,1)S(1)}, bf16[2,4,64,128]{3,2,1,0:T(8,128)(2,1)S(1)}, u32[]{:S(2)}, u32[]{:S(2)}) collective-permute-start(bf16[2,4,64,128]{3,2,1,0:T(8,128)(2,1)S(1)} %get-tuple-element.120), channel_id=1, source_target_pairs={{0,2},{1,3},{2,0},{3,1},{4,6},{5,7},{6,4},{7,5},{8,10},{9,11},{10,... | collective-permute-start | bytes 393224 | tf_op jit(solution)/shard_map/ppermute | solution.py:132
  57.8 0.0 collective-permute-start.23
  57.8 4.9 %all-to-all-done.refs_4_.parts1 = f32[16,8,128]{2,1,0:T(8,128)S(1)} async-done(((f32[16,8,128]{2,1,0:T(8,128)}), f32[16,8,128]{2,1,0:T(8,128)S(1)}, u32[]{:S(2)}, u32[]{:S(2)}) %all-to-all-start) | async-done | bytes 65568 | tf_op jit(solution)/shard_map/all_to_all | solution.py:550
  62.6 5.0 %shard_map.107 = (bf16[4,256,128]{2,1,0:T(8,128)(2,1)S(1)}, f32[4,256,128]{2,1,0:T(8,128)S(1)}, f32[16,8,128]{2,1,0:T(8,128)}, bf16[2,4,64,128]{3,2,1,0:T(8,128)...) custom-call(s32[32]{0:T(128)S(1)} %get-tuple-element.87.src, ...), custom_call_target="tpu_custom_call" | custom-call | flops 805306368 | bytes 8388608 | tf_op jit(solution)/shard_map/pallas_call | solution.py:113
  67.7 0.1 collective-permute-start.24
  67.7 0.2 collective-permute-start.25
  68.0 0.0 collective-permute-done.21.refs_0_
  68.0 1.6 %collective-permute-start.26 = (bf16[2,4,64,128]{3,2,1,0:T(8,128)(2,1)S(1)}, bf16[2,4,64,128]{3,2,1,0:T(8,128)(2,1)S(1)}, u32[]{:S(2)}, u32[]{:S(2)}) collective-permute-start(bf16[2,4,64,128]{3,2,1,0:T(8,128)(2,1)S(1)} %get-tuple-element.124), channel_id=1, source_target_pairs={{0,3},{1,2},{2,1},{3,0},{4,7},{5,6},{6,5},{7,4},{8,11},{9,10},{10,... | collective-permute-start | bytes 393224 | tf_op jit(solution)/shard_map/ppermute | solution.py:132
  69.6 3.5 %all-to-all-start.1 = ((f32[16,8,128]{2,1,0:T(8,128)}), f32[16,8,128]{2,1,0:T(8,128)S(1)}, u32[]{:S(2)}, u32[]{:S(2)}) async-start(f32[16,8,128]{2,1,0:T(8,128)} %get-tuple-element.116), calls=%async_computation.1 | async-start | bytes 131072 | tf_op jit(solution)/shard_map/all_to_all | solution.py:550
  73.1 0.0 collective-permute-done.22.refs_1_
  73.1 0.0 collective-permute-done.23.refs_2_
  73.1 6.8 %all-to-all-done.1.parts2 = f32[16,8,128]{2,1,0:T(8,128)S(1)} async-done(((f32[16,8,128]{2,1,0:T(8,128)}), f32[16,8,128]{2,1,0:T(8,128)S(1)}, u32[]{:S(2)}, u32[]{:S(2)}) %all-to-all-start.1) | async-done | bytes 65568 | tf_op jit(solution)/shard_map/all_to_all | solution.py:550
  80.0 1.7 %shard_map.108 = (bf16[4,64,512]{2,1,0:T(8,128)(2,1)}, bf16[4,64,512]{2,1,0:T(8,128)(2,1)}, f32[1]{0:T(128)}) custom-call(s32[4]{0:T(128)S(1)} %get-tuple-element.86.slots, f32[16,8,128]{2,1,0:T(8,128)S(1)} %all-to-all-done.refs_4_.parts1, f32[16,8,128]{2,1,0:T(8,128)S(1)} %all-to-all-done.1.parts2, ...), custom_call_target="tpu_custom_call" | custom-call | bytes 4194304 | tf_op jit(solution)/shard_map/pallas_call | solution.py:113
  (12 shorter events, 0.0 us)
Async XLA Ops:
  0.6 4.7 %collective-permute-start = (bf16[2,256,256]{2,1,0:T(8,128)(2,1)}, bf16[2,256,256]{2,1,0:T(8,128)(2,1)S(1)}, u32[]{:S(2)}, u32[]{:S(2)}) collective-permute-start(bf16[2,256,256]{2,1,0:T(8,128)(2,1)} %bitcast.2), channel_id=1, source_target_pairs={{0,1},{1,0},{2,3},{3,2},{4,5},{5,4},{6,7},{7,6},{8,9},{9,8},{10,11... | collective-permute-start | bytes 786440 | tf_op jit(solution)/shard_map/ppermute | solution.py:132
  1.1 11.8 %collective-permute-start.2 = (bf16[2,256,256]{2,1,0:T(8,128)(2,1)}, bf16[2,256,256]{2,1,0:T(8,128)(2,1)S(1)}, u32[]{:S(2)}, u32[]{:S(2)}) collective-permute-start(bf16[2,256,256]{2,1,0:T(8,128)(2,1)} %bitcast.3), channel_id=1, source_target_pairs={{0,4},{4,8},{8,12},{12,0},{1,5},{5,9},{9,13},{13,1},{2,6},{6,10},{... | collective-permute-start | bytes 786440 | tf_op jit(solution)/shard_map/ppermute | solution.py:128
  3.8 9.4 %collective-permute-start.1 = (bf16[2,256,256]{2,1,0:T(8,128)(2,1)}, bf16[2,256,256]{2,1,0:T(8,128)(2,1)S(1)}, u32[]{:S(2)}, u32[]{:S(2)}) collective-permute-start(bf16[2,256,256]{2,1,0:T(8,128)(2,1)} %bitcast.4), channel_id=1, source_target_pairs={{0,2},{1,3},{2,0},{3,1},{4,6},{5,7},{6,4},{7,5},{8,10},{9,11},{10,... | collective-permute-start | bytes 786440 | tf_op jit(solution)/shard_map/ppermute | solution.py:132
  5.3 0.7 copy-start.3
  7.8 5.3 %collective-permute-start.3 = (bf16[144,128]{1,0:T(8,128)(2,1)S(1)}, bf16[144,128]{1,0:T(8,128)(2,1)S(1)}, u32[]{:S(2)}, u32[]{:S(2)}) collective-permute-start(bf16[144,128]{1,0:T(8,128)(2,1)S(1)} %get-tuple-element.72), channel_id=1, source_target_pairs={{0,1},{1,0},{2,3},{3,2},{4,5},{5,4},{6,7},{7,6},{8,9},{9,8},{10,11... | collective-permute-start | bytes 110600 | tf_op jit(solution)/shard_map/ppermute | solution.py:132
  7.9 5.7 %collective-permute-start.4 = (bf16[144,128]{1,0:T(8,128)(2,1)S(1)}, bf16[144,128]{1,0:T(8,128)(2,1)S(1)}, u32[]{:S(2)}, u32[]{:S(2)}) collective-permute-start(bf16[144,128]{1,0:T(8,128)(2,1)S(1)} %get-tuple-element.73), channel_id=1, source_target_pairs={{0,2},{1,3},{2,0},{3,1},{4,6},{5,7},{6,4},{7,5},{8,10},{9,11},{10,... | collective-permute-start | bytes 110600 | tf_op jit(solution)/shard_map/ppermute | solution.py:132
  8.5 5.1 %collective-permute-start.5 = (bf16[144,128]{1,0:T(8,128)(2,1)S(1)}, bf16[144,128]{1,0:T(8,128)(2,1)S(1)}, u32[]{:S(2)}, u32[]{:S(2)}) collective-permute-start(bf16[144,128]{1,0:T(8,128)(2,1)S(1)} %get-tuple-element.74), channel_id=1, source_target_pairs={{0,3},{1,2},{2,1},{3,0},{4,7},{5,6},{6,5},{7,4},{8,11},{9,10},{10,... | collective-permute-start | bytes 110600 | tf_op jit(solution)/shard_map/ppermute | solution.py:132
  13.6 11.9 %collective-permute-start.6 = (bf16[2,256,256]{2,1,0:T(8,128)(2,1)S(1)}, bf16[2,256,256]{2,1,0:T(8,128)(2,1)S(1)}, u32[]{:S(2)}, u32[]{:S(2)}) collective-permute-start(bf16[2,256,256]{2,1,0:T(8,128)(2,1)S(1)} %collective-permute-done.1.refs_2_), channel_id=1, source_target_pairs={{0,1},{1,0},{2,3},{3,2},{4,5},{5,4},{6,7},{7,6},{8,9},{9,8},{10,11... | collective-permute-start | bytes 786440 | tf_op jit(solution)/shard_map/ppermute | solution.py:132
  13.8 11.7 %collective-permute-start.9 = (bf16[2,256,256]{2,1,0:T(8,128)(2,1)S(1)}, bf16[2,256,256]{2,1,0:T(8,128)(2,1)S(1)}, u32[]{:S(2)}, u32[]{:S(2)}) collective-permute-start(bf16[2,256,256]{2,1,0:T(8,128)(2,1)S(1)} %collective-permute-done.2.refs_4_), channel_id=1, source_target_pairs={{0,4},{4,8},{8,12},{12,0},{1,5},{5,9},{9,13},{13,1},{2,6},{6,10},{... | collective-permute-start | bytes 786440 | tf_op jit(solution)/shard_map/ppermute | solution.py:128
  15.3 10.1 %collective-permute-start.8 = (bf16[2,256,256]{2,1,0:T(8,128)(2,1)S(1)}, bf16[2,256,256]{2,1,0:T(8,128)(2,1)S(1)}, u32[]{:S(2)}, u32[]{:S(2)}) collective-permute-start(bf16[2,256,256]{2,1,0:T(8,128)(2,1)S(1)} %collective-permute-done.2.refs_4_), channel_id=1, source_target_pairs={{0,2},{1,3},{2,0},{3,1},{4,6},{5,7},{6,4},{7,5},{8,10},{9,11},{10,... | collective-permute-start | bytes 786440 | tf_op jit(solution)/shard_map/ppermute | solution.py:132
  16.8 8.7 %collective-permute-start.7 = (bf16[2,256,256]{2,1,0:T(8,128)(2,1)S(1)}, bf16[2,256,256]{2,1,0:T(8,128)(2,1)S(1)}, u32[]{:S(2)}, u32[]{:S(2)}) collective-permute-start(bf16[2,256,256]{2,1,0:T(8,128)(2,1)S(1)} %collective-permute-done.2.refs_4_), channel_id=1, source_target_pairs={{0,1},{1,0},{2,3},{3,2},{4,5},{5,4},{6,7},{7,6},{8,9},{9,8},{10,11... | collective-permute-start | bytes 786440 | tf_op jit(solution)/shard_map/ppermute | solution.py:132
  16.8 8.6 %collective-permute-start.10 = (bf16[256,128]{1,0:T(8,128)(2,1)S(1)}, bf16[256,128]{1,0:T(8,128)(2,1)S(1)}, u32[]{:S(2)}, u32[]{:S(2)}) collective-permute-start(bf16[256,128]{1,0:T(8,128)(2,1)S(1)} %get-tuple-element.77), channel_id=1, source_target_pairs={{0,4},{4,8},{8,12},{12,0},{1,5},{5,9},{9,13},{13,1},{2,6},{6,10},{... | collective-permute-start | bytes 196616 | tf_op jit(solution)/shard_map/ppermute | solution.py:128
  18.4 0.7 copy-start.1
  19.1 0.7 copy-start.2
  19.8 0.7 copy-start.4
  20.4 0.7 copy-start.5
  25.5 13.4 %collective-permute-start.11 = (bf16[2,256,256]{2,1,0:T(8,128)(2,1)S(1)}, bf16[2,256,256]{2,1,0:T(8,128)(2,1)S(1)}, u32[]{:S(2)}, u32[]{:S(2)}) collective-permute-start(bf16[2,256,256]{2,1,0:T(8,128)(2,1)S(1)} %collective-permute-done.8.refs_6_), channel_id=1, source_target_pairs={{0,1},{1,0},{2,3},{3,2},{4,5},{5,4},{6,7},{7,6},{8,9},{9,8},{10,11... | collective-permute-start | bytes 786440 | tf_op jit(solution)/shard_map/ppermute | solution.py:132
  25.6 13.3 %collective-permute-start.14 = (bf16[2,256,256]{2,1,0:T(8,128)(2,1)S(1)}, bf16[2,256,256]{2,1,0:T(8,128)(2,1)S(1)}, u32[]{:S(2)}, u32[]{:S(2)}) collective-permute-start(bf16[2,256,256]{2,1,0:T(8,128)(2,1)S(1)} %collective-permute-done.9.refs_0_), channel_id=1, source_target_pairs={{0,4},{4,8},{8,12},{12,0},{1,5},{5,9},{9,13},{13,1},{2,6},{6,10},{... | collective-permute-start | bytes 786440 | tf_op jit(solution)/shard_map/ppermute | solution.py:128
  25.7 13.3 %collective-permute-start.13 = (bf16[2,256,256]{2,1,0:T(8,128)(2,1)S(1)}, bf16[2,256,256]{2,1,0:T(8,128)(2,1)S(1)}, u32[]{:S(2)}, u32[]{:S(2)}) collective-permute-start(bf16[2,256,256]{2,1,0:T(8,128)(2,1)S(1)} %collective-permute-done.9.refs_0_), channel_id=1, source_target_pairs={{0,2},{1,3},{2,0},{3,1},{4,6},{5,7},{6,4},{7,5},{8,10},{9,11},{10,... | collective-permute-start | bytes 786440 | tf_op jit(solution)/shard_map/ppermute | solution.py:132
  27.2 11.7 %collective-permute-start.12 = (bf16[2,256,256]{2,1,0:T(8,128)(2,1)S(1)}, bf16[2,256,256]{2,1,0:T(8,128)(2,1)S(1)}, u32[]{:S(2)}, u32[]{:S(2)}) collective-permute-start(bf16[2,256,256]{2,1,0:T(8,128)(2,1)S(1)} %collective-permute-done.9.refs_0_), channel_id=1, source_target_pairs={{0,1},{1,0},{2,3},{3,2},{4,5},{5,4},{6,7},{7,6},{8,9},{9,8},{10,11... | collective-permute-start | bytes 786440 | tf_op jit(solution)/shard_map/ppermute | solution.py:132
  27.3 11.6 %collective-permute-start.15 = (bf16[256,128]{1,0:T(8,128)(2,1)S(1)}, bf16[256,128]{1,0:T(8,128)(2,1)S(1)}, u32[]{:S(2)}, u32[]{:S(2)}) collective-permute-start(bf16[256,128]{1,0:T(8,128)(2,1)S(1)} %get-tuple-element.91), channel_id=1, source_target_pairs={{0,8},{4,12},{8,0},{12,4},{1,9},{5,13},{9,1},{13,5},{2,10},{6,14},... | collective-permute-start | bytes 196616 | tf_op jit(solution)/shard_map/ppermute | solution.py:128
  38.9 5.9 %collective-permute-start.16 = (bf16[2,256,256]{2,1,0:T(8,128)(2,1)S(1)}, bf16[2,256,256]{2,1,0:T(8,128)(2,1)S(1)}, u32[]{:S(2)}, u32[]{:S(2)}) collective-permute-start(bf16[2,256,256]{2,1,0:T(8,128)(2,1)S(1)} %collective-permute-done.13.refs_2_), channel_id=1, source_target_pairs={{0,1},{1,0},{2,3},{3,2},{4,5},{5,4},{6,7},{7,6},{8,9},{9,8},{10,11... | collective-permute-start | bytes 786440 | tf_op jit(solution)/shard_map/ppermute | solution.py:132
  39.1 8.7 %collective-permute-start.18 = (bf16[2,256,256]{2,1,0:T(8,128)(2,1)S(1)}, bf16[2,256,256]{2,1,0:T(8,128)(2,1)S(1)}, u32[]{:S(2)}, u32[]{:S(2)}) collective-permute-start(bf16[2,256,256]{2,1,0:T(8,128)(2,1)S(1)} %collective-permute-done.14.refs_4_), channel_id=1, source_target_pairs={{0,2},{1,3},{2,0},{3,1},{4,6},{5,7},{6,4},{7,5},{8,10},{9,11},{10,... | collective-permute-start | bytes 786440 | tf_op jit(solution)/shard_map/ppermute | solution.py:132
  40.4 7.4 %collective-permute-start.17 = (bf16[2,256,256]{2,1,0:T(8,128)(2,1)S(1)}, bf16[2,256,256]{2,1,0:T(8,128)(2,1)S(1)}, u32[]{:S(2)}, u32[]{:S(2)}) collective-permute-start(bf16[2,256,256]{2,1,0:T(8,128)(2,1)S(1)} %collective-permute-done.14.refs_4_), channel_id=1, source_target_pairs={{0,1},{1,0},{2,3},{3,2},{4,5},{5,4},{6,7},{7,6},{8,9},{9,8},{10,11... | collective-permute-start | bytes 786440 | tf_op jit(solution)/shard_map/ppermute | solution.py:132
  40.5 4.3 %collective-permute-start.19 = (bf16[256,128]{1,0:T(8,128)(2,1)S(1)}, bf16[256,128]{1,0:T(8,128)(2,1)S(1)}, u32[]{:S(2)}, u32[]{:S(2)}) collective-permute-start(bf16[256,128]{1,0:T(8,128)(2,1)S(1)} %get-tuple-element.103), channel_id=1, source_target_pairs={{0,12},{4,0},{8,4},{12,8},{1,13},{5,1},{9,5},{13,9},{2,14},{6,2},{... | collective-permute-start | bytes 196616 | tf_op jit(solution)/shard_map/ppermute | solution.py:128
  40.6 0.9 %copy-start = (bf16[2,1,256,256]{3,2,1,0:T(8,128)(2,1)S(1)}, bf16[2,1,256,256]{3,2,1,0:T(8,128)(2,1)}, u32[]{:S(2)}) copy-start(bf16[2,1,256,256]{3,2,1,0:T(8,128)(2,1)} %param.9) | copy-start | bytes 786436
  47.7 1.5 %collective-permute-start.20 = (bf16[2,256,256]{2,1,0:T(8,128)(2,1)S(1)}, bf16[2,256,256]{2,1,0:T(8,128)(2,1)S(1)}, u32[]{:S(2)}, u32[]{:S(2)}) collective-permute-start(bf16[2,256,256]{2,1,0:T(8,128)(2,1)S(1)} %collective-permute-done.18.refs_6_), channel_id=1, source_target_pairs={{0,1},{1,0},{2,3},{3,2},{4,5},{5,4},{6,7},{7,6},{8,9},{9,8},{10,11... | collective-permute-start | bytes 786440 | tf_op jit(solution)/shard_map/ppermute | solution.py:132
  52.2 10.4 %all-to-all-start = ((f32[16,8,128]{2,1,0:T(8,128)}), f32[16,8,128]{2,1,0:T(8,128)S(1)}, u32[]{:S(2)}, u32[]{:S(2)}) async-start(f32[16,8,128]{2,1,0:T(8,128)} %get-tuple-element.111), calls=%async_computation | async-start | bytes 131072 | tf_op jit(solution)/shard_map/all_to_all | solution.py:550
  55.8 12.2 %collective-permute-start.21 = (bf16[2,4,64,128]{3,2,1,0:T(8,128)(2,1)S(1)}, bf16[2,4,64,128]{3,2,1,0:T(8,128)(2,1)S(1)}, u32[]{:S(2)}, u32[]{:S(2)}) collective-permute-start(bf16[2,4,64,128]{3,2,1,0:T(8,128)(2,1)S(1)} %get-tuple-element.119), channel_id=1, source_target_pairs={{0,1},{1,0},{2,3},{3,2},{4,5},{5,4},{6,7},{7,6},{8,9},{9,8},{10,11... | collective-permute-start | bytes 393224 | tf_op jit(solution)/shard_map/ppermute | solution.py:132
  56.1 17.1 %collective-permute-start.22 = (bf16[2,4,64,128]{3,2,1,0:T(8,128)(2,1)S(1)}, bf16[2,4,64,128]{3,2,1,0:T(8,128)(2,1)S(1)}, u32[]{:S(2)}, u32[]{:S(2)}) collective-permute-start(bf16[2,4,64,128]{3,2,1,0:T(8,128)(2,1)S(1)} %get-tuple-element.120), channel_id=1, source_target_pairs={{0,2},{1,3},{2,0},{3,1},{4,6},{5,7},{6,4},{7,5},{8,10},{9,11},{10,... | collective-permute-start | bytes 393224 | tf_op jit(solution)/shard_map/ppermute | solution.py:132
  57.8 15.4 %collective-permute-start.23 = (bf16[2,4,64,128]{3,2,1,0:T(8,128)(2,1)S(1)}, bf16[2,4,64,128]{3,2,1,0:T(8,128)(2,1)S(1)}, u32[]{:S(2)}, u32[]{:S(2)}) collective-permute-start(bf16[2,4,64,128]{3,2,1,0:T(8,128)(2,1)S(1)} %get-tuple-element.121), channel_id=1, source_target_pairs={{0,3},{1,2},{2,1},{3,0},{4,7},{5,6},{6,5},{7,4},{8,11},{9,10},{10,... | collective-permute-start | bytes 393224 | tf_op jit(solution)/shard_map/ppermute | solution.py:132
  67.7 12.3 %collective-permute-start.24 = (bf16[2,4,64,128]{3,2,1,0:T(8,128)(2,1)S(1)}, bf16[2,4,64,128]{3,2,1,0:T(8,128)(2,1)S(1)}, u32[]{:S(2)}, u32[]{:S(2)}) collective-permute-start(bf16[2,4,64,128]{3,2,1,0:T(8,128)(2,1)S(1)} %get-tuple-element.122), channel_id=1, source_target_pairs={{0,1},{1,0},{2,3},{3,2},{4,5},{5,4},{6,7},{7,6},{8,9},{9,8},{10,11... | collective-permute-start | bytes 393224 | tf_op jit(solution)/shard_map/ppermute | solution.py:132
  67.7 12.2 %collective-permute-start.25 = (bf16[2,4,64,128]{3,2,1,0:T(8,128)(2,1)S(1)}, bf16[2,4,64,128]{3,2,1,0:T(8,128)(2,1)S(1)}, u32[]{:S(2)}, u32[]{:S(2)}) collective-permute-start(bf16[2,4,64,128]{3,2,1,0:T(8,128)(2,1)S(1)} %get-tuple-element.123), channel_id=1, source_target_pairs={{0,2},{1,3},{2,0},{3,1},{4,6},{5,7},{6,4},{7,5},{8,10},{9,11},{10,... | collective-permute-start | bytes 393224 | tf_op jit(solution)/shard_map/ppermute | solution.py:132
  68.0 12.0 %collective-permute-start.26 = (bf16[2,4,64,128]{3,2,1,0:T(8,128)(2,1)S(1)}, bf16[2,4,64,128]{3,2,1,0:T(8,128)(2,1)S(1)}, u32[]{:S(2)}, u32[]{:S(2)}) collective-permute-start(bf16[2,4,64,128]{3,2,1,0:T(8,128)(2,1)S(1)} %get-tuple-element.124), channel_id=1, source_target_pairs={{0,3},{1,2},{2,1},{3,0},{4,7},{5,6},{6,5},{7,4},{8,11},{9,10},{10,... | collective-permute-start | bytes 393224 | tf_op jit(solution)/shard_map/ppermute | solution.py:132
  69.6 10.4 %all-to-all-start.1 = ((f32[16,8,128]{2,1,0:T(8,128)}), f32[16,8,128]{2,1,0:T(8,128)S(1)}, u32[]{:S(2)}, u32[]{:S(2)}) async-start(f32[16,8,128]{2,1,0:T(8,128)} %get-tuple-element.116), calls=%async_computation.1 | async-start | bytes 131072 | tf_op jit(solution)/shard_map/all_to_all | solution.py:550

commit v8 on v7

--- a/solution.py
+++ b/solution.py
@@ -124,8 +124,22 @@
     )(*[pltpu.with_memory_space_constraint(x, HBM) if space == HBM else x for x, space in ins])
 
 
+def ring_at(place, n_blk):
+    place = place % n_blk if isinstance(place, int) else lax.rem(place + n_blk, n_blk)
+    odd, even = 2 * place - 1, 2 * (n_blk - place)
+    if isinstance(place, int):
+        return 0 if place == 0 else odd if odd < n_blk else even
+    return jnp.where(place == 0, 0, jnp.where(odd < n_blk, odd, even))
+
+
+def ring_place(index, n_blk):
+    odd, even = (index + 1) // 2, lax.rem(n_blk - index // 2, n_blk)
+    return jnp.where(lax.rem(index, 2) == 1, odd, even)
+
+
 def onward(block, d, n_blk):
-    return lax.ppermute(block, "blk", [(i, (i + d) % n_blk) for i in range(n_blk)])
+    pairs = [(ring_at(i, n_blk), ring_at(i + d, n_blk)) for i in range(n_blk)]
+    return lax.ppermute(block, "blk", pairs)
 
 
 def swap(block, e, n_op):
@@ -148,14 +162,15 @@
             columns, packed = pack(kept[0, bits[-1]])
             moved["right"] = [packed[0]] + [swap(packed[e], e, n_op) for e in range(1, n_op)]
             moved["columns"] = columns
-        elif j < n_blk:
-            moved["psi"] = onward(columns[j], j, n_blk)
+        else:
+            due = {1: [1], n_blk - 1: list(range(2, n_blk))}.get(j, [])
+            moved["psi"] = [onward(columns[d], d, n_blk) for d in due]
         if j == 1:
             moved["tables"] = table(right)
         full = j - len(bits) + 1
         if j == n_blk - 1 and full > 0:
             moved["early"] = early(left, psi, full, made["tables"])
-        if not kept and not moved:
+        if not kept:
             break
         waiting = {key: done for key, (_, done) in new.items()}
         kept, moved = lax.optimization_barrier((kept, moved))
@@ -163,8 +178,8 @@
         if j == 0:
             columns, right = moved["columns"], moved["right"]
             psi = list(columns[:1])
-        elif j < n_blk:
-            psi = psi + [moved["psi"]]
+        else:
+            psi = psi + moved["psi"]
         made.update({key: moved[key] for key in ("tables", "early") if key in moved})
     return left, psi, right, made["tables"], made.get("early")
 
@@ -183,7 +198,7 @@
     fetch.start()
     copies = []
     for d in range(n_blk):
-        there = lax.rem(own_blk + d, n_blk)
+        there = ring_at(ring_place(own_blk, n_blk) + d, n_blk)
         start = pl.multiple_of((there * n_op + own_op) * cols, LANES)
         copies.append(
             pltpu.make_async_copy(psi.at[0, :, pl.ds(start, cols)], psi_out[d], sems.at[d])
@@ -219,7 +234,7 @@
     own_blk, own_op = place_of()
     lane = lax.broadcasted_iota(jnp.int32, (16, cols), 1)
     for d in range(n_blk):
-        slot = lax.rem(own_blk - d + n_blk, n_blk)
+        slot = ring_at(ring_place(own_blk, n_blk) - d, n_blk)
         slots[d] = slot
         widths[d] = width[sector[slot]]
     for e in range(n_op):

time: 82.1 us -> 78.7 us (0.959)
  waiting for transfers between devices: 34.8 us -> 27.7 us
  starting transfers between devices: 26.8 us -> 30.5 us
    ppermute x6, waiting for transfers between devices: 18.1 us -> 12.3 us  [onward(): return lax.ppermute(block, 'blk', pairs)]
    ppermute x6, starting transfers between devices: 6.86 us -> 10.2 us  [onward(): return lax.ppermute(block, 'blk', pairs)]
    ppermute x21, waiting for transfers between devices: 5.06 us -> 3.71 us  [swap(): return lax.ppermute(block, 'op', [(i, i ^ e) for i in range(n_op)])]
  transfers between devices with their start and end apart: 29 -> 29, of which waited for: 10 -> 11; matrix products, arithmetic and copies ran while one was open for 0% -> 0% of each run, Pallas kernels for 13% -> 13%
where the time goes in v8:
time: 78.7 us; the launch traced here: 78.3 us
  starting transfers between devices  30.5 us (39%)
  waiting for transfers between devices  27.7 us (35%)
  Pallas kernels  15 us (19%)
  local copies, waits for them, and re-layouts  4.28 us (5%)
    pallas_call x6, Pallas kernels, kernel(): pl.pallas_call(body, out_shape=[HBM(shape, dtype) if space == HBM else ja...  15 us
    ppermute x21, starting transfers between devices, swap(): return lax.ppermute(block, 'op', [(i, i ^ e) for i in range(n_op)])  13 us
    ppermute x6, waiting for transfers between devices, onward(): return lax.ppermute(block, 'blk', pairs)  12.3 us
    all_to_all x2, waiting for transfers between devices, totals(): return lax.all_to_all(parts, ('blk', 'op'), 0, 0, tiled=True)  11.6 us
    ppermute x6, starting transfers between devices, onward(): return lax.ppermute(block, 'blk', pairs)  10.2 us
    all_to_all x2, starting transfers between devices, totals(): return lax.all_to_all(parts, ('blk', 'op'), 0, 0, tiled=True)  7.27 us
    unnamed x12, local copies, waits for them, and re-layouts  4.28 us
    ppermute x21, waiting for transfers between devices, swap(): return lax.ppermute(block, 'op', [(i, i ^ e) for i in range(n_op)])  3.71 us
  transfers between devices with their start and end apart: 29, of which 11 were waited for; matrix products, arithmetic and copies ran while one was open for 0% of the time, Pallas kernels for 13%

profile of v8, /device:TPU:0, one launch (start us, length us, event | category | flops | bytes accessed | tf_op | source)
XLA Modules:
  0.0 78.3 jit_solution(2217604023847951194)
XLA Ops:
  0.6 0.5 collective-permute-start
  1.1 2.6 %collective-permute-start.2 = (bf16[2,256,256]{2,1,0:T(8,128)(2,1)}, bf16[2,256,256]{2,1,0:T(8,128)(2,1)S(1)}, u32[]{:S(2)}, u32[]{:S(2)}) collective-permute-start(bf16[2,256,256]{2,1,0:T(8,128)(2,1)} %bitcast.3), channel_id=1, source_target_pairs={{0,4},{4,12},{12,8},{8,0},{1,5},{5,13},{13,9},{9,1},{2,6},{6,14},{... | collective-permute-start | bytes 786440 | tf_op jit(solution)/shard_map/ppermute | solution.py:142
  3.8 1.5 %collective-permute-start.1 = (bf16[2,256,256]{2,1,0:T(8,128)(2,1)}, bf16[2,256,256]{2,1,0:T(8,128)(2,1)S(1)}, u32[]{:S(2)}, u32[]{:S(2)}) collective-permute-start(bf16[2,256,256]{2,1,0:T(8,128)(2,1)} %bitcast.4), channel_id=1, source_target_pairs={{0,2},{1,3},{2,0},{3,1},{4,6},{5,7},{6,4},{7,5},{8,10},{9,11},{10,... | collective-permute-start | bytes 786440 | tf_op jit(solution)/shard_map/ppermute | solution.py:146
  5.3 0.0 collective-permute-done.refs_1_
  5.3 0.7 copy-done.3
  5.9 1.9 %shard_map.103 = (bf16[256,128]{1,0:T(8,128)(2,1)S(1)}, bf16[256,128]{1,0:T(8,128)(2,1)S(1)}, bf16[256,128]{1,0:T(8,128)(2,1)S(1)}, bf16[256,128]{1,0:T(8,128)(2...) custom-call(s32[2]{0:T(128)S(1)} %copy-done.3, ...), custom_call_target="tpu_custom_call" | custom-call | bytes 1048576 | tf_op jit(solution)/shard_map/pallas_call | solution.py:113
  7.8 0.1 collective-permute-start.3
  7.9 0.6 collective-permute-start.4
  8.5 1.3 %collective-permute-start.5 = (bf16[144,128]{1,0:T(8,128)(2,1)S(1)}, bf16[144,128]{1,0:T(8,128)(2,1)S(1)}, u32[]{:S(2)}, u32[]{:S(2)}) collective-permute-start(bf16[144,128]{1,0:T(8,128)(2,1)S(1)} %get-tuple-element.74), channel_id=1, source_target_pairs={{0,3},{1,2},{2,1},{3,0},{4,7},{5,6},{6,5},{7,4},{8,11},{9,10},{10,... | collective-permute-start | bytes 110600 | tf_op jit(solution)/shard_map/ppermute | solution.py:146
  9.7 2.2 %collective-permute-done.2.refs_4_ = bf16[2,256,256]{2,1,0:T(8,128)(2,1)S(1)} collective-permute-done((bf16[2,256,256]{2,1,0:T(8,128)(2,1)}, bf16[2,256,256]{2,1,0:T(8,128)(2,1)S(1)}, u32[]{:S(2)}, u32[]{:S(2)}) %collective-permute-start.2) | collective-permute-done | bytes 262176 | tf_op jit(solution)/shard_map/ppermute | solution.py:142
  11.9 1.2 %collective-permute-done.1.refs_2_ = bf16[2,256,256]{2,1,0:T(8,128)(2,1)S(1)} collective-permute-done((bf16[2,256,256]{2,1,0:T(8,128)(2,1)}, bf16[2,256,256]{2,1,0:T(8,128)(2,1)S(1)}, u32[]{:S(2)}, u32[]{:S(2)}) %collective-permute-start.1) | collective-permute-done | bytes 262176 | tf_op jit(solution)/shard_map/ppermute | solution.py:146
  13.2 0.0 collective-permute-done.3.refs_1_.refs_9_
  13.2 0.4 collective-permute-done.4.refs_2_.refs_10_
  13.6 0.0 collective-permute-done.5.refs_3_.refs_11_
  13.6 0.2 collective-permute-start.6
  13.8 2.6 %collective-permute-start.9 = (bf16[2,256,256]{2,1,0:T(8,128)(2,1)S(1)}, bf16[2,256,256]{2,1,0:T(8,128)(2,1)S(1)}, u32[]{:S(2)}, u32[]{:S(2)}) collective-permute-start(bf16[2,256,256]{2,1,0:T(8,128)(2,1)S(1)} %collective-permute-done.2.refs_4_), channel_id=1, source_target_pairs={{0,4},{4,12},{12,8},{8,0},{1,5},{5,13},{13,9},{9,1},{2,6},{6,14},{... | collective-permute-start | bytes 786440 | tf_op jit(solution)/shard_map/ppermute | solution.py:142
  16.4 1.5 %collective-permute-start.8 = (bf16[2,256,256]{2,1,0:T(8,128)(2,1)S(1)}, bf16[2,256,256]{2,1,0:T(8,128)(2,1)S(1)}, u32[]{:S(2)}, u32[]{:S(2)}) collective-permute-start(bf16[2,256,256]{2,1,0:T(8,128)(2,1)S(1)} %collective-permute-done.2.refs_4_), channel_id=1, source_target_pairs={{0,2},{1,3},{2,0},{3,1},{4,6},{5,7},{6,4},{7,5},{8,10},{9,11},{10,... | collective-permute-start | bytes 786440 | tf_op jit(solution)/shard_map/ppermute | solution.py:146
  17.9 0.0 collective-permute-start.7
  17.9 0.4 collective-permute-start.10
  18.3 0.7 copy-done.1
  19.0 0.7 copy-done.2
  19.7 0.7 copy-done.4
  20.3 0.7 copy-done.5
  21.0 1.4 %shard_map.104 = (s32[32]{0:T(128)S(1)}, s32[4]{0:T(128)S(1)}, s32[4]{0:T(128)S(1)}, f32[4,256,128]{2,1,0:T(8,128)S(1)}) custom-call(s32[4]{0:T(128)S(1)} %copy-done.4, s32[4]{0:T(128)S(1)} %copy-done.5, f32[4,256]{1,0:T(4,128)S(1)} %copy-done.1, f32[1,512]{1,0:T(1,128)S(1)} %bitcast.6, bf16[144,128]{1,0:T(8,128)(2,1)S(1)} %get-tuple-element.78.refs_0_.refs_8_, ...), custom_call_target="tpu_custom_call" | custom-call | tf_op jit(solution)/shard_map/pallas_call | solution.py:113
  22.4 2.2 %collective-permute-done.10.refs_9_.refs_13_ = bf16[256,128]{1,0:T(8,128)(2,1)S(1)} collective-permute-done((bf16[256,128]{1,0:T(8,128)(2,1)S(1)}, bf16[256,128]{1,0:T(8,128)(2,1)S(1)}, u32[]{:S(2)}, u32[]{:S(2)}) %collective-permute-start.10) | collective-permute-done | bytes 65568 | tf_op jit(solution)/shard_map/ppermute | solution.py:142
  24.6 0.0 collective-permute-done.6.refs_3_
  24.6 0.0 collective-permute-done.9.refs_0_
  24.6 0.0 collective-permute-done.8.refs_6_
  24.6 0.0 collective-permute-done.7.refs_5_
  24.6 0.1 collective-permute-start.11
  24.7 1.7 %collective-permute-start.14 = (bf16[2,256,256]{2,1,0:T(8,128)(2,1)S(1)}, bf16[2,256,256]{2,1,0:T(8,128)(2,1)S(1)}, u32[]{:S(2)}, u32[]{:S(2)}) collective-permute-start(bf16[2,256,256]{2,1,0:T(8,128)(2,1)S(1)} %collective-permute-done.9.refs_0_), channel_id=1, source_target_pairs={{0,4},{4,12},{12,8},{8,0},{1,5},{5,13},{13,9},{9,1},{2,6},{6,14},{... | collective-permute-start | bytes 786440 | tf_op jit(solution)/shard_map/ppermute | solution.py:142
  26.4 1.5 %collective-permute-start.13 = (bf16[2,256,256]{2,1,0:T(8,128)(2,1)S(1)}, bf16[2,256,256]{2,1,0:T(8,128)(2,1)S(1)}, u32[]{:S(2)}, u32[]{:S(2)}) collective-permute-start(bf16[2,256,256]{2,1,0:T(8,128)(2,1)S(1)} %collective-permute-done.9.refs_0_), channel_id=1, source_target_pairs={{0,2},{1,3},{2,0},{3,1},{4,6},{5,7},{6,4},{7,5},{8,10},{9,11},{10,... | collective-permute-start | bytes 786440 | tf_op jit(solution)/shard_map/ppermute | solution.py:146
  27.9 0.0 collective-permute-start.12
  27.9 0.0 collective-permute-done.11.refs_7_
  27.9 6.4 %collective-permute-done.14.refs_4_ = bf16[2,256,256]{2,1,0:T(8,128)(2,1)S(1)} collective-permute-done((bf16[2,256,256]{2,1,0:T(8,128)(2,1)S(1)}, bf16[2,256,256]{2,1,0:T(8,128)(2,1)S(1)}, u32[]{:S(2)}, u32[]{:S(2)}) %collective-permute-start.14) | collective-permute-done | bytes 262176 | tf_op jit(solution)/shard_map/ppermute | solution.py:142
  34.3 0.5 collective-permute-done.13.refs_2_
  34.8 0.0 collective-permute-done.12.refs_1_
  34.8 0.0 collective-permute-start.15
  34.8 1.5 %collective-permute-start.17 = (bf16[2,256,256]{2,1,0:T(8,128)(2,1)S(1)}, bf16[2,256,256]{2,1,0:T(8,128)(2,1)S(1)}, u32[]{:S(2)}, u32[]{:S(2)}) collective-permute-start(bf16[2,256,256]{2,1,0:T(8,128)(2,1)S(1)} %collective-permute-done.14.refs_4_), channel_id=1, source_target_pairs={{0,2},{1,3},{2,0},{3,1},{4,6},{5,7},{6,4},{7,5},{8,10},{9,11},{10,... | collective-permute-start | bytes 786440 | tf_op jit(solution)/shard_map/ppermute | solution.py:146
  36.3 0.2 collective-permute-start.16
  36.5 2.0 %collective-permute-start.18 = (bf16[256,128]{1,0:T(8,128)(2,1)S(1)}, bf16[256,128]{1,0:T(8,128)(2,1)S(1)}, u32[]{:S(2)}, u32[]{:S(2)}) collective-permute-start(bf16[256,128]{1,0:T(8,128)(2,1)S(1)} %get-tuple-element.102), channel_id=1, source_target_pairs={{0,12},{4,8},{12,0},{8,4},{1,13},{5,9},{13,1},{9,5},{2,14},{6,10},... | collective-permute-start | bytes 196616 | tf_op jit(solution)/shard_map/ppermute | solution.py:142
  38.5 0.8 %collective-permute-start.19 = (bf16[256,128]{1,0:T(8,128)(2,1)S(1)}, bf16[256,128]{1,0:T(8,128)(2,1)S(1)}, u32[]{:S(2)}, u32[]{:S(2)}) collective-permute-start(bf16[256,128]{1,0:T(8,128)(2,1)S(1)} %get-tuple-element.103), channel_id=1, source_target_pairs={{0,8},{4,0},{12,4},{8,12},{1,9},{5,1},{13,5},{9,13},{2,10},{6,2},{... | collective-permute-start | bytes 196616 | tf_op jit(solution)/shard_map/ppermute | solution.py:142
  39.3 0.9 %copy-done = bf16[2,1,256,256]{3,2,1,0:T(8,128)(2,1)S(1)} copy-done((bf16[2,1,256,256]{3,2,1,0:T(8,128)(2,1)S(1)}, bf16[2,1,256,256]{3,2,1,0:T(8,128)(2,1)}, u32[]{:S(2)}) %copy-start) | copy-done | bytes 262168
  40.3 2.1 %shard_map.105 = (bf16[2,8,256,128]{3,2,1,0:T(8,128)(2,1)S(1)}, bf16[2,4,2,256,256]{4,3,2,1,0:T(8,128)(2,1)}) custom-call(s32[4]{0:T(128)S(1)} %get-tuple-element.88.widths, bf16[2,256,256]{2,1,0:T(8,128)(2,1)S(1)} %bitcast.5, bf16[2,256,256]{2,1,0:T(8,128)(2,1)S(1)} %collective-permute-done.refs_1_, ...), custom_call_target="tpu_custom_call" | custom-call | flops 268435456 | bytes 8388608 | tf_op jit(solution)/shard_map/pallas_call | solution.py:113
  42.4 1.0 %collective-permute-done.18.refs_14_ = bf16[256,128]{1,0:T(8,128)(2,1)S(1)} collective-permute-done((bf16[256,128]{1,0:T(8,128)(2,1)S(1)}, bf16[256,128]{1,0:T(8,128)(2,1)S(1)}, u32[]{:S(2)}, u32[]{:S(2)}) %collective-permute-start.18) | collective-permute-done | bytes 65568 | tf_op jit(solution)/shard_map/ppermute | solution.py:142
  43.4 0.6 collective-permute-done.19.refs_15_
  44.0 0.1 collective-permute-start.20
  44.1 1.5 %collective-permute-done.20.refs_7_ = bf16[2,256,256]{2,1,0:T(8,128)(2,1)S(1)} collective-permute-done((bf16[2,256,256]{2,1,0:T(8,128)(2,1)S(1)}, bf16[2,256,256]{2,1,0:T(8,128)(2,1)S(1)}, u32[]{:S(2)}, u32[]{:S(2)}) %collective-permute-start.20) | collective-permute-done | bytes 262176 | tf_op jit(solution)/shard_map/ppermute | solution.py:146
  45.6 3.0 %shard_map.106 = (f32[4,256,128]{2,1,0:T(8,128)S(1)}, bf16[4,256,128]{2,1,0:T(8,128)(2,1)S(1)}, f32[16,8,128]{2,1,0:T(8,128)}, bf16[2,4,2,256,256]{4,3,2,1,0:T(8...) custom-call(s32[32]{0:T(128)S(1)} %get-tuple-element.87.src, ...), custom_call_target="tpu_custom_call" | custom-call | flops 805306368 | bytes 8388608 | tf_op jit(solution)/shard_map/pallas_call | solution.py:113
  48.6 3.8 %all-to-all-start = ((f32[16,8,128]{2,1,0:T(8,128)}), f32[16,8,128]{2,1,0:T(8,128)S(1)}, u32[]{:S(2)}, u32[]{:S(2)}) async-start(f32[16,8,128]{2,1,0:T(8,128)} %get-tuple-element.111), calls=%async_computation | async-start | bytes 131072 | tf_op jit(solution)/shard_map/all_to_all | solution.py:565
  52.4 0.4 collective-permute-start.21
  52.8 1.7 %collective-permute-start.22 = (bf16[2,4,64,128]{3,2,1,0:T(8,128)(2,1)S(1)}, bf16[2,4,64,128]{3,2,1,0:T(8,128)(2,1)S(1)}, u32[]{:S(2)}, u32[]{:S(2)}) collective-permute-start(bf16[2,4,64,128]{3,2,1,0:T(8,128)(2,1)S(1)} %get-tuple-element.120), channel_id=1, source_target_pairs={{0,2},{1,3},{2,0},{3,1},{4,6},{5,7},{6,4},{7,5},{8,10},{9,11},{10,... | collective-permute-start | bytes 393224 | tf_op jit(solution)/shard_map/ppermute | solution.py:146
  54.4 4.8 %all-to-all-done.refs_4_.parts1 = f32[16,8,128]{2,1,0:T(8,128)S(1)} async-done(((f32[16,8,128]{2,1,0:T(8,128)}), f32[16,8,128]{2,1,0:T(8,128)S(1)}, u32[]{:S(2)}, u32[]{:S(2)}) %all-to-all-start) | async-done | bytes 65568 | tf_op jit(solution)/shard_map/all_to_all | solution.py:565
  59.2 5.0 %shard_map.107 = (bf16[4,256,128]{2,1,0:T(8,128)(2,1)S(1)}, f32[4,256,128]{2,1,0:T(8,128)S(1)}, f32[16,8,128]{2,1,0:T(8,128)}, bf16[2,4,64,128]{3,2,1,0:T(8,128)...) custom-call(s32[32]{0:T(128)S(1)} %get-tuple-element.87.src, ...), custom_call_target="tpu_custom_call" | custom-call | flops 805306368 | bytes 8388608 | tf_op jit(solution)/shard_map/pallas_call | solution.py:113
  64.3 0.1 collective-permute-start.24
  64.4 0.2 collective-permute-start.25
  64.6 0.0 collective-permute-done.21.refs_0_
  64.6 1.6 %collective-permute-start.26 = (bf16[2,4,64,128]{3,2,1,0:T(8,128)(2,1)S(1)}, bf16[2,4,64,128]{3,2,1,0:T(8,128)(2,1)S(1)}, u32[]{:S(2)}, u32[]{:S(2)}) collective-permute-start(bf16[2,4,64,128]{3,2,1,0:T(8,128)(2,1)S(1)} %get-tuple-element.124), channel_id=1, source_target_pairs={{0,3},{1,2},{2,1},{3,0},{4,7},{5,6},{6,5},{7,4},{8,11},{9,10},{10,... | collective-permute-start | bytes 393224 | tf_op jit(solution)/shard_map/ppermute | solution.py:146
  66.2 3.5 %all-to-all-start.1 = ((f32[16,8,128]{2,1,0:T(8,128)}), f32[16,8,128]{2,1,0:T(8,128)S(1)}, u32[]{:S(2)}, u32[]{:S(2)}) async-start(f32[16,8,128]{2,1,0:T(8,128)} %get-tuple-element.116), calls=%async_computation.1 | async-start | bytes 131072 | tf_op jit(solution)/shard_map/all_to_all | solution.py:565
  69.7 0.0 collective-permute-done.22.refs_1_
  69.7 0.0 collective-permute-done.23.refs_2_
  69.8 6.8 %all-to-all-done.1.parts2 = f32[16,8,128]{2,1,0:T(8,128)S(1)} async-done(((f32[16,8,128]{2,1,0:T(8,128)}), f32[16,8,128]{2,1,0:T(8,128)S(1)}, u32[]{:S(2)}, u32[]{:S(2)}) %all-to-all-start.1) | async-done | bytes 65568 | tf_op jit(solution)/shard_map/all_to_all | solution.py:565
  76.6 0.0 collective-permute-done.26.refs_5_
  76.6 1.7 %shard_map.108 = (bf16[4,64,512]{2,1,0:T(8,128)(2,1)}, bf16[4,64,512]{2,1,0:T(8,128)(2,1)}, f32[1]{0:T(128)}) custom-call(s32[4]{0:T(128)S(1)} %get-tuple-element.86.slots, f32[16,8,128]{2,1,0:T(8,128)S(1)} %all-to-all-done.refs_4_.parts1, f32[16,8,128]{2,1,0:T(8,128)S(1)} %all-to-all-done.1.parts2, ...), custom_call_target="tpu_custom_call" | custom-call | bytes 4194304 | tf_op jit(solution)/shard_map/pallas_call | solution.py:113
  (12 shorter events, 0.0 us)
Async XLA Ops:
  0.6 4.7 %collective-permute-start = (bf16[2,256,256]{2,1,0:T(8,128)(2,1)}, bf16[2,256,256]{2,1,0:T(8,128)(2,1)S(1)}, u32[]{:S(2)}, u32[]{:S(2)}) collective-permute-start(bf16[2,256,256]{2,1,0:T(8,128)(2,1)} %bitcast.2), channel_id=1, source_target_pairs={{0,1},{1,0},{2,3},{3,2},{4,5},{5,4},{6,7},{7,6},{8,9},{9,8},{10,11... | collective-permute-start | bytes 786440 | tf_op jit(solution)/shard_map/ppermute | solution.py:146
  1.1 10.8 %collective-permute-start.2 = (bf16[2,256,256]{2,1,0:T(8,128)(2,1)}, bf16[2,256,256]{2,1,0:T(8,128)(2,1)S(1)}, u32[]{:S(2)}, u32[]{:S(2)}) collective-permute-start(bf16[2,256,256]{2,1,0:T(8,128)(2,1)} %bitcast.3), channel_id=1, source_target_pairs={{0,4},{4,12},{12,8},{8,0},{1,5},{5,13},{13,9},{9,1},{2,6},{6,14},{... | collective-permute-start | bytes 786440 | tf_op jit(solution)/shard_map/ppermute | solution.py:142
  3.8 9.4 %collective-permute-start.1 = (bf16[2,256,256]{2,1,0:T(8,128)(2,1)}, bf16[2,256,256]{2,1,0:T(8,128)(2,1)S(1)}, u32[]{:S(2)}, u32[]{:S(2)}) collective-permute-start(bf16[2,256,256]{2,1,0:T(8,128)(2,1)} %bitcast.4), channel_id=1, source_target_pairs={{0,2},{1,3},{2,0},{3,1},{4,6},{5,7},{6,4},{7,5},{8,10},{9,11},{10,... | collective-permute-start | bytes 786440 | tf_op jit(solution)/shard_map/ppermute | solution.py:146
  5.3 0.7 copy-start.3
  7.8 5.3 %collective-permute-start.3 = (bf16[144,128]{1,0:T(8,128)(2,1)S(1)}, bf16[144,128]{1,0:T(8,128)(2,1)S(1)}, u32[]{:S(2)}, u32[]{:S(2)}) collective-permute-start(bf16[144,128]{1,0:T(8,128)(2,1)S(1)} %get-tuple-element.72), channel_id=1, source_target_pairs={{0,1},{1,0},{2,3},{3,2},{4,5},{5,4},{6,7},{7,6},{8,9},{9,8},{10,11... | collective-permute-start | bytes 110600 | tf_op jit(solution)/shard_map/ppermute | solution.py:146
  7.9 5.7 %collective-permute-start.4 = (bf16[144,128]{1,0:T(8,128)(2,1)S(1)}, bf16[144,128]{1,0:T(8,128)(2,1)S(1)}, u32[]{:S(2)}, u32[]{:S(2)}) collective-permute-start(bf16[144,128]{1,0:T(8,128)(2,1)S(1)} %get-tuple-element.73), channel_id=1, source_target_pairs={{0,2},{1,3},{2,0},{3,1},{4,6},{5,7},{6,4},{7,5},{8,10},{9,11},{10,... | collective-permute-start | bytes 110600 | tf_op jit(solution)/shard_map/ppermute | solution.py:146
  8.5 5.1 %collective-permute-start.5 = (bf16[144,128]{1,0:T(8,128)(2,1)S(1)}, bf16[144,128]{1,0:T(8,128)(2,1)S(1)}, u32[]{:S(2)}, u32[]{:S(2)}) collective-permute-start(bf16[144,128]{1,0:T(8,128)(2,1)S(1)} %get-tuple-element.74), channel_id=1, source_target_pairs={{0,3},{1,2},{2,1},{3,0},{4,7},{5,6},{6,5},{7,4},{8,11},{9,10},{10,... | collective-permute-start | bytes 110600 | tf_op jit(solution)/shard_map/ppermute | solution.py:146
  13.6 11.0 %collective-permute-start.6 = (bf16[2,256,256]{2,1,0:T(8,128)(2,1)S(1)}, bf16[2,256,256]{2,1,0:T(8,128)(2,1)S(1)}, u32[]{:S(2)}, u32[]{:S(2)}) collective-permute-start(bf16[2,256,256]{2,1,0:T(8,128)(2,1)S(1)} %collective-permute-done.1.refs_2_), channel_id=1, source_target_pairs={{0,1},{1,0},{2,3},{3,2},{4,5},{5,4},{6,7},{7,6},{8,9},{9,8},{10,11... | collective-permute-start | bytes 786440 | tf_op jit(solution)/shard_map/ppermute | solution.py:146
  13.8 10.8 %collective-permute-start.9 = (bf16[2,256,256]{2,1,0:T(8,128)(2,1)S(1)}, bf16[2,256,256]{2,1,0:T(8,128)(2,1)S(1)}, u32[]{:S(2)}, u32[]{:S(2)}) collective-permute-start(bf16[2,256,256]{2,1,0:T(8,128)(2,1)S(1)} %collective-permute-done.2.refs_4_), channel_id=1, source_target_pairs={{0,4},{4,12},{12,8},{8,0},{1,5},{5,13},{13,9},{9,1},{2,6},{6,14},{... | collective-permute-start | bytes 786440 | tf_op jit(solution)/shard_map/ppermute | solution.py:142
  16.4 8.2 %collective-permute-start.8 = (bf16[2,256,256]{2,1,0:T(8,128)(2,1)S(1)}, bf16[2,256,256]{2,1,0:T(8,128)(2,1)S(1)}, u32[]{:S(2)}, u32[]{:S(2)}) collective-permute-start(bf16[2,256,256]{2,1,0:T(8,128)(2,1)S(1)} %collective-permute-done.2.refs_4_), channel_id=1, source_target_pairs={{0,2},{1,3},{2,0},{3,1},{4,6},{5,7},{6,4},{7,5},{8,10},{9,11},{10,... | collective-permute-start | bytes 786440 | tf_op jit(solution)/shard_map/ppermute | solution.py:146
  17.9 6.7 %collective-permute-start.7 = (bf16[2,256,256]{2,1,0:T(8,128)(2,1)S(1)}, bf16[2,256,256]{2,1,0:T(8,128)(2,1)S(1)}, u32[]{:S(2)}, u32[]{:S(2)}) collective-permute-start(bf16[2,256,256]{2,1,0:T(8,128)(2,1)S(1)} %collective-permute-done.2.refs_4_), channel_id=1, source_target_pairs={{0,1},{1,0},{2,3},{3,2},{4,5},{5,4},{6,7},{7,6},{8,9},{9,8},{10,11... | collective-permute-start | bytes 786440 | tf_op jit(solution)/shard_map/ppermute | solution.py:146
  17.9 6.7 %collective-permute-start.10 = (bf16[256,128]{1,0:T(8,128)(2,1)S(1)}, bf16[256,128]{1,0:T(8,128)(2,1)S(1)}, u32[]{:S(2)}, u32[]{:S(2)}) collective-permute-start(bf16[256,128]{1,0:T(8,128)(2,1)S(1)} %get-tuple-element.77), channel_id=1, source_target_pairs={{0,4},{4,12},{12,8},{8,0},{1,5},{5,13},{13,9},{9,1},{2,6},{6,14},{... | collective-permute-start | bytes 196616 | tf_op jit(solution)/shard_map/ppermute | solution.py:142
  18.3 0.7 copy-start.1
  19.0 0.7 copy-start.2
  19.7 0.7 copy-start.4
  20.3 0.7 copy-start.5
  24.6 3.3 %collective-permute-start.11 = (bf16[2,256,256]{2,1,0:T(8,128)(2,1)S(1)}, bf16[2,256,256]{2,1,0:T(8,128)(2,1)S(1)}, u32[]{:S(2)}, u32[]{:S(2)}) collective-permute-start(bf16[2,256,256]{2,1,0:T(8,128)(2,1)S(1)} %collective-permute-done.8.refs_6_), channel_id=1, source_target_pairs={{0,1},{1,0},{2,3},{3,2},{4,5},{5,4},{6,7},{7,6},{8,9},{9,8},{10,11... | collective-permute-start | bytes 786440 | tf_op jit(solution)/shard_map/ppermute | solution.py:146
  24.7 9.6 %collective-permute-start.14 = (bf16[2,256,256]{2,1,0:T(8,128)(2,1)S(1)}, bf16[2,256,256]{2,1,0:T(8,128)(2,1)S(1)}, u32[]{:S(2)}, u32[]{:S(2)}) collective-permute-start(bf16[2,256,256]{2,1,0:T(8,128)(2,1)S(1)} %collective-permute-done.9.refs_0_), channel_id=1, source_target_pairs={{0,4},{4,12},{12,8},{8,0},{1,5},{5,13},{13,9},{9,1},{2,6},{6,14},{... | collective-permute-start | bytes 786440 | tf_op jit(solution)/shard_map/ppermute | solution.py:142
  26.4 8.4 %collective-permute-start.13 = (bf16[2,256,256]{2,1,0:T(8,128)(2,1)S(1)}, bf16[2,256,256]{2,1,0:T(8,128)(2,1)S(1)}, u32[]{:S(2)}, u32[]{:S(2)}) collective-permute-start(bf16[2,256,256]{2,1,0:T(8,128)(2,1)S(1)} %collective-permute-done.9.refs_0_), channel_id=1, source_target_pairs={{0,2},{1,3},{2,0},{3,1},{4,6},{5,7},{6,4},{7,5},{8,10},{9,11},{10,... | collective-permute-start | bytes 786440 | tf_op jit(solution)/shard_map/ppermute | solution.py:146
  27.9 6.9 %collective-permute-start.12 = (bf16[2,256,256]{2,1,0:T(8,128)(2,1)S(1)}, bf16[2,256,256]{2,1,0:T(8,128)(2,1)S(1)}, u32[]{:S(2)}, u32[]{:S(2)}) collective-permute-start(bf16[2,256,256]{2,1,0:T(8,128)(2,1)S(1)} %collective-permute-done.9.refs_0_), channel_id=1, source_target_pairs={{0,1},{1,0},{2,3},{3,2},{4,5},{5,4},{6,7},{7,6},{8,9},{9,8},{10,11... | collective-permute-start | bytes 786440 | tf_op jit(solution)/shard_map/ppermute | solution.py:146
  34.8 9.2 %collective-permute-start.15 = (bf16[2,256,256]{2,1,0:T(8,128)(2,1)S(1)}, bf16[2,256,256]{2,1,0:T(8,128)(2,1)S(1)}, u32[]{:S(2)}, u32[]{:S(2)}) collective-permute-start(bf16[2,256,256]{2,1,0:T(8,128)(2,1)S(1)} %collective-permute-done.13.refs_2_), channel_id=1, source_target_pairs={{0,1},{1,0},{2,3},{3,2},{4,5},{5,4},{6,7},{7,6},{8,9},{9,8},{10,11... | collective-permute-start | bytes 786440 | tf_op jit(solution)/shard_map/ppermute | solution.py:146
  34.8 9.2 %collective-permute-start.17 = (bf16[2,256,256]{2,1,0:T(8,128)(2,1)S(1)}, bf16[2,256,256]{2,1,0:T(8,128)(2,1)S(1)}, u32[]{:S(2)}, u32[]{:S(2)}) collective-permute-start(bf16[2,256,256]{2,1,0:T(8,128)(2,1)S(1)} %collective-permute-done.14.refs_4_), channel_id=1, source_target_pairs={{0,2},{1,3},{2,0},{3,1},{4,6},{5,7},{6,4},{7,5},{8,10},{9,11},{10,... | collective-permute-start | bytes 786440 | tf_op jit(solution)/shard_map/ppermute | solution.py:146
  36.3 7.7 %collective-permute-start.16 = (bf16[2,256,256]{2,1,0:T(8,128)(2,1)S(1)}, bf16[2,256,256]{2,1,0:T(8,128)(2,1)S(1)}, u32[]{:S(2)}, u32[]{:S(2)}) collective-permute-start(bf16[2,256,256]{2,1,0:T(8,128)(2,1)S(1)} %collective-permute-done.14.refs_4_), channel_id=1, source_target_pairs={{0,1},{1,0},{2,3},{3,2},{4,5},{5,4},{6,7},{7,6},{8,9},{9,8},{10,11... | collective-permute-start | bytes 786440 | tf_op jit(solution)/shard_map/ppermute | solution.py:146
  36.5 6.8 %collective-permute-start.18 = (bf16[256,128]{1,0:T(8,128)(2,1)S(1)}, bf16[256,128]{1,0:T(8,128)(2,1)S(1)}, u32[]{:S(2)}, u32[]{:S(2)}) collective-permute-start(bf16[256,128]{1,0:T(8,128)(2,1)S(1)} %get-tuple-element.102), channel_id=1, source_target_pairs={{0,12},{4,8},{12,0},{8,4},{1,13},{5,9},{13,1},{9,5},{2,14},{6,10},... | collective-permute-start | bytes 196616 | tf_op jit(solution)/shard_map/ppermute | solution.py:142
  38.5 5.5 %collective-permute-start.19 = (bf16[256,128]{1,0:T(8,128)(2,1)S(1)}, bf16[256,128]{1,0:T(8,128)(2,1)S(1)}, u32[]{:S(2)}, u32[]{:S(2)}) collective-permute-start(bf16[256,128]{1,0:T(8,128)(2,1)S(1)} %get-tuple-element.103), channel_id=1, source_target_pairs={{0,8},{4,0},{12,4},{8,12},{1,9},{5,1},{13,5},{9,13},{2,10},{6,2},{... | collective-permute-start | bytes 196616 | tf_op jit(solution)/shard_map/ppermute | solution.py:142
  39.3 0.9 %copy-start = (bf16[2,1,256,256]{3,2,1,0:T(8,128)(2,1)S(1)}, bf16[2,1,256,256]{3,2,1,0:T(8,128)(2,1)}, u32[]{:S(2)}) copy-start(bf16[2,1,256,256]{3,2,1,0:T(8,128)(2,1)} %param.9) | copy-start | bytes 786436
  44.0 1.6 %collective-permute-start.20 = (bf16[2,256,256]{2,1,0:T(8,128)(2,1)S(1)}, bf16[2,256,256]{2,1,0:T(8,128)(2,1)S(1)}, u32[]{:S(2)}, u32[]{:S(2)}) collective-permute-start(bf16[2,256,256]{2,1,0:T(8,128)(2,1)S(1)} %collective-permute-done.17.refs_6_), channel_id=1, source_target_pairs={{0,1},{1,0},{2,3},{3,2},{4,5},{5,4},{6,7},{7,6},{8,9},{9,8},{10,11... | collective-permute-start | bytes 786440 | tf_op jit(solution)/shard_map/ppermute | solution.py:146
  48.6 10.7 %all-to-all-start = ((f32[16,8,128]{2,1,0:T(8,128)}), f32[16,8,128]{2,1,0:T(8,128)S(1)}, u32[]{:S(2)}, u32[]{:S(2)}) async-start(f32[16,8,128]{2,1,0:T(8,128)} %get-tuple-element.111), calls=%async_computation | async-start | bytes 131072 | tf_op jit(solution)/shard_map/all_to_all | solution.py:565
  52.4 12.2 %collective-permute-start.21 = (bf16[2,4,64,128]{3,2,1,0:T(8,128)(2,1)S(1)}, bf16[2,4,64,128]{3,2,1,0:T(8,128)(2,1)S(1)}, u32[]{:S(2)}, u32[]{:S(2)}) collective-permute-start(bf16[2,4,64,128]{3,2,1,0:T(8,128)(2,1)S(1)} %get-tuple-element.119), channel_id=1, source_target_pairs={{0,1},{1,0},{2,3},{3,2},{4,5},{5,4},{6,7},{7,6},{8,9},{9,8},{10,11... | collective-permute-start | bytes 393224 | tf_op jit(solution)/shard_map/ppermute | solution.py:146
  52.8 17.0 %collective-permute-start.22 = (bf16[2,4,64,128]{3,2,1,0:T(8,128)(2,1)S(1)}, bf16[2,4,64,128]{3,2,1,0:T(8,128)(2,1)S(1)}, u32[]{:S(2)}, u32[]{:S(2)}) collective-permute-start(bf16[2,4,64,128]{3,2,1,0:T(8,128)(2,1)S(1)} %get-tuple-element.120), channel_id=1, source_target_pairs={{0,2},{1,3},{2,0},{3,1},{4,6},{5,7},{6,4},{7,5},{8,10},{9,11},{10,... | collective-permute-start | bytes 393224 | tf_op jit(solution)/shard_map/ppermute | solution.py:146
  54.4 15.3 %collective-permute-start.23 = (bf16[2,4,64,128]{3,2,1,0:T(8,128)(2,1)S(1)}, bf16[2,4,64,128]{3,2,1,0:T(8,128)(2,1)S(1)}, u32[]{:S(2)}, u32[]{:S(2)}) collective-permute-start(bf16[2,4,64,128]{3,2,1,0:T(8,128)(2,1)S(1)} %get-tuple-element.121), channel_id=1, source_target_pairs={{0,3},{1,2},{2,1},{3,0},{4,7},{5,6},{6,5},{7,4},{8,11},{9,10},{10,... | collective-permute-start | bytes 393224 | tf_op jit(solution)/shard_map/ppermute | solution.py:146
  64.3 12.3 %collective-permute-start.24 = (bf16[2,4,64,128]{3,2,1,0:T(8,128)(2,1)S(1)}, bf16[2,4,64,128]{3,2,1,0:T(8,128)(2,1)S(1)}, u32[]{:S(2)}, u32[]{:S(2)}) collective-permute-start(bf16[2,4,64,128]{3,2,1,0:T(8,128)(2,1)S(1)} %get-tuple-element.122), channel_id=1, source_target_pairs={{0,1},{1,0},{2,3},{3,2},{4,5},{5,4},{6,7},{7,6},{8,9},{9,8},{10,11... | collective-permute-start | bytes 393224 | tf_op jit(solution)/shard_map/ppermute | solution.py:146
  64.4 12.2 %collective-permute-start.25 = (bf16[2,4,64,128]{3,2,1,0:T(8,128)(2,1)S(1)}, bf16[2,4,64,128]{3,2,1,0:T(8,128)(2,1)S(1)}, u32[]{:S(2)}, u32[]{:S(2)}) collective-permute-start(bf16[2,4,64,128]{3,2,1,0:T(8,128)(2,1)S(1)} %get-tuple-element.123), channel_id=1, source_target_pairs={{0,2},{1,3},{2,0},{3,1},{4,6},{5,7},{6,4},{7,5},{8,10},{9,11},{10,... | collective-permute-start | bytes 393224 | tf_op jit(solution)/shard_map/ppermute | solution.py:146
  64.6 12.0 %collective-permute-start.26 = (bf16[2,4,64,128]{3,2,1,0:T(8,128)(2,1)S(1)}, bf16[2,4,64,128]{3,2,1,0:T(8,128)(2,1)S(1)}, u32[]{:S(2)}, u32[]{:S(2)}) collective-permute-start(bf16[2,4,64,128]{3,2,1,0:T(8,128)(2,1)S(1)} %get-tuple-element.124), channel_id=1, source_target_pairs={{0,3},{1,2},{2,1},{3,0},{4,7},{5,6},{6,5},{7,4},{8,11},{9,10},{10,... | collective-permute-start | bytes 393224 | tf_op jit(solution)/shard_map/ppermute | solution.py:146
  66.2 10.4 %all-to-all-start.1 = ((f32[16,8,128]{2,1,0:T(8,128)}), f32[16,8,128]{2,1,0:T(8,128)S(1)}, u32[]{:S(2)}, u32[]{:S(2)}) async-start(f32[16,8,128]{2,1,0:T(8,128)} %get-tuple-element.116), calls=%async_computation.1 | async-start | bytes 131072 | tf_op jit(solution)/shard_map/all_to_all | solution.py:565

commit v9 on v0

--- a/solution.py
+++ b/solution.py
@@ -1,12 +1,18 @@
+import functools
+
 import jax
 import jax.numpy as jnp
 from jax import lax
+from jax.experimental import pallas as pl
+from jax.experimental.pallas import tpu as pltpu
 from jax.sharding import PartitionSpec as P
 
 EPS = 1e-06
-
-
-def per_device(
+LANES = 128
+VMEM_LIMIT = 20 * 1024 * 1024
+
+
+def per_device_general(
     psi, left_ops, right_ops, term_shift, slot_sector, sector_width, diag_left, diag_right
 ):
     sec_dev, rows, ncols = psi.shape
@@ -81,18 +87,521 @@
         (jnp.sum(vec32 * second_sigma), jnp.sum(upd32 * first_sigma), jnp.sum(upd32 * second_sigma))
     )
     h_mix = 0.5 * (v_s1 + u_s0)
-    angle = 0.5 * jnp.arctan2(2.0 * h_mix, theta - u_s1)
-    sine = jnp.sin(angle)
-    flip = jnp.where(sine > 0, -1.0, 1.0)
-    coef_v = -sine * flip
-    coef_u = jnp.cos(angle) * flip
-    half = 0.5 * (theta - u_s1)
-    energy = 0.5 * (theta + u_s1) - jnp.sqrt(half * half + h_mix * h_mix)
+    coef_v, coef_u, energy = ritz(theta, h_mix, u_s1)
     newvec = coef_v * vec32 + coef_u * upd32
     image = coef_v * first_sigma + coef_u * second_sigma
     new_out = final_rows(newvec.astype(jnp.bfloat16))
     res_out = final_rows((image - energy * newvec).astype(jnp.bfloat16))
     return (new_out, res_out, jnp.reshape(energy, (1,)))
+
+
+def ritz(theta, h_mix, h_two):
+    angle = 0.5 * jnp.arctan2(2.0 * h_mix, theta - h_two)
+    sine = jnp.sin(angle)
+    flip = jnp.where(sine > 0, -1.0, 1.0)
+    coef_v = -sine * flip
+    coef_u = jnp.cos(angle) * flip
+    half = 0.5 * (theta - h_two)
+    energy = 0.5 * (theta + h_two) - jnp.sqrt(half * half + h_mix * h_mix)
+    return coef_v, coef_u, energy
+
+
+VMEM, SMEM, HBM = pltpu.VMEM, pltpu.SMEM, pltpu.HBM
+
+
+def kernel(body, ins, outs, scratch=(), flops=0, nbytes=0):
+    return pl.pallas_call(
+        body,
+        out_shape=[
+            HBM(shape, dtype) if space == HBM else jax.ShapeDtypeStruct(shape, dtype)
+            for shape, dtype, space in outs
+        ],
+        in_specs=[pl.BlockSpec(memory_space=space) for _, space in ins],
+        out_specs=[pl.BlockSpec(memory_space=space) for _, _, space in outs],
+        scratch_shapes=list(scratch),
+        compiler_params=pltpu.CompilerParams(vmem_limit_bytes=VMEM_LIMIT),
+        cost_estimate=pl.CostEstimate(flops=flops, bytes_accessed=nbytes, transcendentals=0),
+    )(*[pltpu.with_memory_space_constraint(x, HBM) if space == HBM else x for x, space in ins])
+
+
+def ring_at(place, n_blk):
+    place = place % n_blk if isinstance(place, int) else lax.rem(place + n_blk, n_blk)
+    odd, even = 2 * place - 1, 2 * (n_blk - place)
+    if isinstance(place, int):
+        return 0 if place == 0 else odd if odd < n_blk else even
+    return jnp.where(place == 0, 0, jnp.where(odd < n_blk, odd, even))
+
+
+def ring_place(index, n_blk):
+    odd, even = (index + 1) // 2, lax.rem(n_blk - index // 2, n_blk)
+    return jnp.where(lax.rem(index, 2) == 1, odd, even)
+
+
+def onward(block, d, n_blk):
+    pairs = [(ring_at(i, n_blk), ring_at(i + d, n_blk)) for i in range(n_blk)]
+    return lax.ppermute(block, "blk", pairs)
+
+
+def swap(block, e, n_op):
+    return lax.ppermute(block, "op", [(i, i ^ e) for i in range(n_op)])
+
+
+def gather(own, n_blk, n_op, pack, table):
+    bits = [1 << b for b in reversed(range(1, n_op.bit_length() - 1))]
+    order = sorted(range(1, n_blk), key=lambda d: min(d, n_blk - d))
+    left, psi, right, tables, columns = {(0, 0): own}, {}, None, None, None
+    waiting, late = {(0, 0): 0}, None
+    for j in range(n_blk + len(bits)):
+        new, moved = {}, {}
+        for (d, e), done in waiting.items():
+            if e == 0 and d + 1 < n_blk:
+                new[d + 1, 0] = onward(left[d, 0], 1, n_blk), 0
+            for b in range(done, len(bits)):
+                new[d, e ^ bits[b]] = swap(left[d, e], bits[b], n_op), b + 1
+        kept = {key: block for key, (block, _) in new.items()}
+        if late is not None:
+            moved["psi"] = late
+        if j == 0:
+            columns, packed = pack()
+            moved["right"] = [packed[0]]
+            moved["right"] += [swap(part, 2 * e, n_op) for e, part in enumerate(packed[1:], 1)]
+        if j == 1:
+            moved["tables"] = table(right)
+        if 2 <= j < n_blk:
+            moved["other"] = swap(psi[order[j - 2]][0], 1, n_op)
+        late = onward(columns[order[j]], order[j], n_blk) if j < n_blk - 1 else None
+        if not kept and not moved:
+            break
+        waiting = {key: done for key, (_, done) in new.items()}
+        kept, moved = lax.optimization_barrier((kept, moved))
+        left.update(kept)
+        right, tables = moved.get("right", right), moved.get("tables", tables)
+        if "psi" in moved:
+            psi[order[j - 1]] = [moved["psi"]]
+        if "other" in moved:
+            psi[order[j - 2]].append(moved["other"])
+    psi[0] = [columns[0]]
+    return left, psi, right, tables
+
+
+def place_of():
+    return lax.axis_index("blk"), lax.axis_index("op")
+
+
+def pack_body(n_blk, n_op, shift, _, psi, right_in, *outs):
+    n_pair = n_op // 2
+    psi_out, right_out, right, sems = outs[:n_blk], outs[n_blk : n_blk + n_pair], outs[-2], outs[-1]
+    terms, local, width, _ = right.shape
+    cols = local * width // n_op
+    per = cols // width
+    own_blk, own_op = place_of()
+    fetch = pltpu.make_async_copy(right_in, right, sems.at[2 * n_blk])
+    fetch.start()
+    copies = []
+    for d in range(n_blk):
+        there = ring_at(ring_place(own_blk, n_blk) + d, n_blk) * n_op
+        for h in range(psi_out[d].shape[1] // cols):
+            start = pl.multiple_of((there + (own_op ^ h)) * cols, LANES)
+            copy = pltpu.make_async_copy(
+                psi.at[0, :, pl.ds(start, cols)],
+                psi_out[d].at[:, h * cols : (h + 1) * cols],
+                sems.at[2 * d + h],
+            )
+            copy.start()
+            copies.append(copy)
+    lane = lax.broadcasted_iota(jnp.int32, (16, 2 * cols), 1)
+    line = jnp.zeros((16, 2 * cols), jnp.float32)
+    for k in range(terms):
+        line = jnp.where(lane == k, shift[k].astype(jnp.float32), line)
+    square = [lax.broadcasted_iota(jnp.int32, (width, width), axis) for axis in (0, 1)]
+    unit = (square[0] == square[1]).astype(jnp.bfloat16)
+    fetch.wait()
+    for e in range(n_pair):
+        for k in range(terms):
+            turned = []
+            for h in range(2):
+                first = (own_op ^ (2 * e) ^ h) * per
+                for r in range(per):
+                    turned.append(
+                        lax.dot_general(
+                            right[k, first + r], unit, (((0,), (0,)), ((), ())),
+                            preferred_element_type=jnp.float32,
+                        )
+                    )
+            side_by_side = jnp.concatenate(turned, axis=1).astype(jnp.bfloat16)
+            right_out[e][k * width : (k + 1) * width] = side_by_side
+        right_out[e][terms * width :] = line.astype(jnp.bfloat16)
+    for copy in copies:
+        copy.wait()
+
+
+def table_body(n_blk, terms, sector, width, left_diag, *refs):
+    tails, src, widths, slots, diag = refs[:-4], *refs[-4:]
+    n_pair = len(tails)
+    rows, cols = tails[0].shape
+    own_blk, _ = place_of()
+    lane = lax.broadcasted_iota(jnp.int32, (16, cols), 1)
+    for d in range(n_blk):
+        slot = ring_at(ring_place(own_blk, n_blk) - d, n_blk)
+        slots[d] = slot
+        widths[d] = width[sector[slot]]
+    for e in range(n_pair):
+        tail = tails[e][rows - 16 :].astype(jnp.float32)
+        for k in range(terms):
+            shift = jnp.max(jnp.where(lane == k, tail, -1e9)).astype(jnp.int32)
+            for t in range(n_blk):
+                want = sector[slots[t]] - shift
+                found = jnp.int32(n_blk)
+                for d in range(n_blk):
+                    found = jnp.where(sector[slots[d]] == want, d, found)
+                src[(t * n_pair + e) * terms + k] = found
+    for d in range(n_blk):
+        row = left_diag[pl.ds(slots[d], 1), :]
+        diag[d] = jnp.transpose(jnp.broadcast_to(row, (diag.shape[2], row.shape[1])))
+
+
+def diagonal(diag, right_diag, d, h):
+    cols = diag.shape[2]
+    _, own_op = place_of()
+    start = pl.multiple_of((own_op ^ h) * cols, LANES)
+    return diag[d] + right_diag[:, pl.ds(start, cols)]
+
+
+def row_mask(width, shape):
+    return lax.broadcasted_iota(jnp.int32, shape, 0) < width
+
+
+def fold(x):
+    return jnp.sum(x.reshape(-1, 8, x.shape[-1]), axis=0)
+
+
+def whole(x):
+    return jnp.sum(jnp.sum(x, axis=0, keepdims=True), axis=1, keepdims=True)
+
+
+def spread(values, out):
+    line = lax.broadcasted_iota(jnp.int32, out.shape[1:], 0)
+    tile = jnp.zeros(out.shape[1:], jnp.float32)
+    for j, value in enumerate(values):
+        tile = jnp.where(line == j, value, tile)
+    for d in range(out.shape[0]):
+        out[d] = tile
+
+
+def by_block(packed, terms, k):
+    rows, cols = packed.shape
+    width = (rows - 16) // terms
+    lane = lax.broadcasted_iota(jnp.int32, (width, cols), 1)
+    block = packed[k * width : (k + 1) * width].astype(jnp.float32)
+    parts = []
+    for r in range(cols // width):
+        inside = (lane >= r * width) & (lane < (r + 1) * width)
+        parts.append(jnp.where(inside, block, 0.0).astype(jnp.bfloat16))
+    return jnp.concatenate(parts, axis=0)
+
+
+def left_products(block, left, inter):
+    n_terms, rows, cols = inter.shape
+    at = 0
+    while at < n_terms:
+        ops = left(at)
+        terms = ops.shape[0]
+        prod = jnp.dot(ops.reshape(terms * rows, rows), block, preferred_element_type=jnp.float32)
+        inter[at : at + terms] = prod.astype(jnp.bfloat16).reshape(terms, rows, cols)
+        at += terms
+
+
+def sum_terms(src, widths, inter, right, out):
+    n_blk, n_terms, _, _ = inter.shape
+    n_blk -= 1
+    terms = n_terms // len(right)
+    turned = [by_block(right[j // terms], terms, j % terms) for j in range(n_terms)]
+    for t in range(n_blk):
+        total = None
+        for j in range(n_terms):
+            part = jnp.dot(
+                inter[src[t * n_terms + j], j], turned[j], preferred_element_type=jnp.float32
+            )
+            total = part if total is None else total + part
+        out[t] = jnp.where(row_mask(widths[t], total.shape), total, 0.0).astype(jnp.bfloat16)
+
+
+def first_body(n_blk, n_pair, src, widths, *refs):
+    left = [refs[d * n_pair : (d + 1) * n_pair] for d in range(n_blk)]
+    refs = refs[n_blk * n_pair :]
+    right, refs = refs[:n_pair], refs[n_pair:]
+    psi, part_out, raw_out, left_out, inter, sems = refs[:-5], *refs[-5:]
+    copies = []
+    for d in range(n_blk):
+        for e in range(n_pair):
+            copies.append(
+                pltpu.make_async_copy(left[d][e], left_out.at[d, e], sems.at[d * n_pair + e])
+            )
+            copies[-1].start()
+    inter[n_blk] = jnp.zeros_like(inter[n_blk])
+    cols = raw_out.shape[2] // 2
+    for d in range(n_blk):
+        at = 0
+        while at < 2 * cols:
+            block = psi[0][...].astype(jnp.float32)
+            psi = psi[1:]
+            block = jnp.where(row_mask(widths[d], block.shape), block, 0.0)
+            raw_out[d, :, at : at + block.shape[1]] = block.astype(jnp.bfloat16)
+            at += block.shape[1]
+        terms = left[d][0].shape[0]
+        left_products(raw_out[d], lambda at: left[d][at // terms][...], inter.at[d])
+    sum_terms(src, widths, inter, right, part_out)
+    for copy in copies:
+        copy.wait()
+
+
+def send_rows(sends, j, d, h, block):
+    _, own_op = place_of()
+    step, cols = sends[0].shape[2], block.shape[1]
+    for e, send in enumerate(sends):
+        start = pl.multiple_of((own_op ^ (2 * e)) * step, step)
+        send[j, d, :, h * cols : (h + 1) * cols] = block[pl.ds(start, step)].astype(send.dtype)
+
+
+def total_of(mine, other, d, h, cols):
+    own = mine[d, :, h * cols : (h + 1) * cols].astype(jnp.float32)
+    return own + other[d, :, (1 - h) * cols : (2 - h) * cols].astype(jnp.float32)
+
+
+def sigma_body(mine, other, raw_in, diag, right_diag, sig_out, dots_out, *sends):
+    n_blk, _, cols = diag.shape
+    sums = [jnp.zeros((8, cols), jnp.float32) for _ in range(2)]
+    for d in range(n_blk):
+        for h in range(2):
+            part = slice(h * cols, (h + 1) * cols)
+            raw = raw_in[d, :, part].astype(jnp.float32)
+            sigma = total_of(mine, other, d, h, cols) + diagonal(diag, right_diag, d, h) * raw
+            sig_out[d, :, part] = sigma
+            if h == 0:
+                sums = [sums[0] + fold(raw * raw), sums[1] + fold(raw * sigma)]
+    for d in range(n_blk):
+        for h in range(2):
+            send_rows(sends, 0, d, h, raw_in.at[d, :, h * cols : (h + 1) * cols])
+            send_rows(sends, 1, d, h, sig_out.at[d, :, h * cols : (h + 1) * cols])
+    spread([whole(x) for x in sums], dots_out)
+
+
+def norm_theta(parts, count):
+    tot = jnp.sum(parts, axis=0) * (1.0 / count)
+    scale = lax.rsqrt(tot[0:1] + EPS)
+    return scale, tot[1:2] * scale * scale
+
+
+def second_body(n_blk, n_pair, count, src, widths, left_in, *refs):
+    right, refs = refs[:n_pair], refs[n_pair:]
+    parts, raw_in, sig_in, diag, right_diag, f_out, part_out, half_out = refs[:8]
+    inter, corr, held, sems = refs[8:]
+    copies = []
+    for d in range(n_blk):
+        copies.append(pltpu.make_async_copy(left_in.at[d], held.at[d], sems.at[d]))
+        copies[-1].start()
+    inter[n_blk] = jnp.zeros_like(inter[n_blk])
+    scale, theta = norm_theta(parts[...], count)
+    cols = diag.shape[2]
+    halves = []
+    for h in range(2):
+        part = slice(h * cols, (h + 1) * cols)
+        vv = vc = vs = jnp.zeros((8, cols), jnp.float32)
+        for d in range(n_blk):
+            vec = raw_in[d, :, part].astype(jnp.float32) * scale
+            sigma = sig_in[d, :, part] * scale
+            den = diagonal(diag, right_diag, d, h) - theta
+            item = (sigma - theta * vec) * den / jnp.maximum(den * den, 0.25)
+            corr[d, :, part] = item
+            vv, vc, vs = vv + fold(vec * vec), vc + fold(vec * item), vs + fold(vec * sigma)
+        halves.append((whole(vv), whole(vc), whole(vs)))
+    along = (halves[0][1] + halves[1][1]) / jnp.maximum(halves[0][0] + halves[1][0], 1e-30)
+    terms = held.shape[2]
+    for d in range(n_blk):
+        for h in range(2):
+            part = slice(h * cols, (h + 1) * cols)
+            vec = raw_in[d, :, part].astype(jnp.float32) * scale
+            f_out[d, :, part] = (corr[d, :, part] - along * vec).astype(jnp.bfloat16)
+        copies[d].wait()
+        left_products(f_out[d], lambda at: held[d, at // terms], inter.at[d])
+    sum_terms(src, widths, inter, right, part_out)
+    spread(halves[0] + (along,), half_out)
+
+
+def image_body(count, half, parts, mine, other, raw_in, sig_in, f_in, diag, right_diag, dots_out, *sends):
+    n_blk, _, cols = diag.shape
+    scale, _ = norm_theta(parts[...], count)
+    sums = [jnp.zeros((8, cols), jnp.float32) for _ in range(5)]
+    for d in range(n_blk):
+        for h in range(2):
+            part = slice(h * cols, (h + 1) * cols)
+            fld = f_in[d, :, part].astype(jnp.float32)
+            image = total_of(mine, other, d, h, cols) + diagonal(diag, right_diag, d, h) * fld
+            sends[-1][h] = image
+            send_rows(sends[:-1], 0, d, h, f_in.at[d, :, part])
+            send_rows(sends[:-1], 1, d, h, sends[-1].at[h])
+            if h == 0:
+                vec = raw_in[d, :, part].astype(jnp.float32) * scale
+                sigma = sig_in[d, :, part] * scale
+                prods = (fld * fld, vec * fld, vec * image, fld * sigma, fld * image)
+                sums = [one + fold(prod) for one, prod in zip(sums, prods)]
+    known = [half[0, j : j + 1] for j in range(4)]
+    spread(known + [whole(x) for x in sums], dots_out)
+
+
+def ritz_pair(theta, h_mix, h_two):
+    diff, twice = theta - h_two, 2.0 * h_mix
+    size = jnp.sqrt(diff * diff + twice * twice)
+    some = size > 0.0
+    safe = jnp.where(some, size, 1.0)
+    big = jnp.sqrt(0.5 + 0.5 * jnp.abs(diff) / safe)
+    small = 0.5 * jnp.abs(twice) / (safe * big)
+    sine = jnp.where(diff >= 0.0, small, big)
+    cosine = jnp.where(diff >= 0.0, big, small)
+    sine = jnp.where(some, sine, 0.0)
+    cosine = jnp.where(some, cosine, 1.0)
+    upward = (twice > 0.0) | ((twice == 0.0) & (diff < 0.0))
+    return sine, jnp.where(upward, -cosine, cosine), 0.5 * (theta + h_two) - 0.5 * size
+
+
+def third_body(n_blk, n_op, count, slots, parts1, parts2, *refs):
+    n_pair = n_op // 2
+    got1, got2 = refs[:n_pair], refs[n_pair : 2 * n_pair]
+    new_out, res_out, energy_out = refs[2 * n_pair :]
+    cols = new_out.shape[2] // n_op
+    own_blk, own_op = place_of()
+    scale, theta = norm_theta(parts1[...], count)
+    vv, vc, vs, local, ff, vf, vt, fs, ft = (parts2[:, j, :] for j in range(9))
+
+    def mean(x):
+        return jnp.sum(x, axis=0, keepdims=True) * (1.0 / count)
+
+    along = mean(vc)
+    beta = local - along
+    norm_sq = mean(ff + 2.0 * beta * vf + beta * beta * vv)
+    unit = lax.rsqrt(jnp.maximum(norm_sq, 0.0) + EPS)
+    v_s1 = unit * mean(vt + beta * vs)
+    u_s0 = unit * mean(fs + beta * vs)
+    u_s1 = unit * unit * mean(ft + beta * (vt + fs) + beta * beta * vs)
+    cv, cu, energy = ritz_pair(theta, 0.5 * (v_s1 + u_s0), u_s1)
+    energy_out[0] = jnp.max(energy)
+    cu = cu * unit
+    for e in range(n_pair):
+        there = own_op ^ (2 * e)
+        back = parts2[own_blk * n_op + there][3:4] - along
+        on_vec = (cv + cu * back) * scale
+        for h in range(2):
+            at = pl.multiple_of((there ^ h) * cols, LANES)
+            part = slice(h * cols, (h + 1) * cols)
+            for d in range(n_blk):
+                blocks = (got[e][j, d, :, part] for got in (got1, got2) for j in range(2))
+                raw, sigma, fld, image = (block.astype(jnp.float32) for block in blocks)
+                newvec = on_vec * raw + cu * fld
+                res = on_vec * sigma + cu * image - energy * newvec
+                new_out[slots[d], :, pl.ds(at, cols)] = newvec.astype(jnp.bfloat16)
+                res_out[slots[d], :, pl.ds(at, cols)] = res.astype(jnp.bfloat16)
+
+
+def per_device(
+    psi, left_ops, right_ops, term_shift, slot_sector, sector_width, diag_left, diag_right
+):
+    n_blk, n_op = lax.axis_size("blk"), lax.axis_size("op")
+    _, rows, ncols = psi.shape
+    terms, _, width, _ = right_ops.shape
+    n_pair = n_op // 2
+    cols = diag_right.shape[0] // n_op
+    step = rows // n_op
+    count = float(n_blk * rows * ncols)
+    n_dev = n_blk * n_op
+    bf16, f32, i32 = jnp.bfloat16, jnp.float32, jnp.int32
+    last = sorted(range(1, n_blk), key=lambda d: min(d, n_blk - d))[-1]
+
+    def pack():
+        first = swap(term_shift, 1, n_op)
+        sent = kernel(
+            functools.partial(pack_body, n_blk, n_op),
+            [(term_shift, SMEM), (first, SMEM), (psi, HBM), (right_ops, HBM)],
+            [((rows, 2 * cols if d in (0, last) else cols), bf16, VMEM) for d in range(n_blk)]
+            + [((terms * width + 16, 2 * cols), bf16, VMEM)] * n_pair,
+            [pltpu.VMEM(right_ops.shape, bf16), pltpu.SemaphoreType.DMA((2 * n_blk + 1,))],
+            nbytes=1 << 20,
+        )
+        return sent[:n_blk], sent[n_blk:]
+
+    def table(right):
+        return kernel(
+            functools.partial(table_body, n_blk, terms),
+            [(slot_sector, SMEM), (sector_width, SMEM), (diag_left, VMEM)]
+            + [(block, VMEM) for block in right],
+            [((n_blk * n_pair * terms,), i32, SMEM)]
+            + [((n_blk,), i32, SMEM)] * 2
+            + [((n_blk, rows, LANES), f32, VMEM)],
+        )
+
+    left, psi_by, right, (src, widths, slots, diag) = gather(left_ops[:, 0], n_blk, n_op, pack, table)
+    left_ins = [(left[d, 2 * e], VMEM) for d in range(n_blk) for e in range(n_pair)]
+    right_ins = [(block, VMEM) for block in right]
+    psi_ins = [(block, VMEM) for d in range(n_blk) for block in psi_by[d]]
+    diags = [(diag, VMEM), (diag_right[None], VMEM)]
+
+    tables = [(src, SMEM), (widths, SMEM)]
+    narrow = ((n_blk, rows, 2 * cols), bf16, VMEM)
+    wide = ((n_blk, rows, 2 * cols), f32, VMEM)
+    sends = [((2, n_blk, step, 2 * cols), bf16, VMEM)] * n_pair
+    inter = pltpu.VMEM((n_blk + 1, n_pair * terms, rows, 2 * cols), bf16)
+    left_all = (n_blk, n_pair, terms, rows, rows)
+    cost = dict(flops=2 * n_blk * rows * 2 * cols * terms * n_pair * (rows + 2 * cols), nbytes=6 << 20)
+
+    def totals(parts):
+        return lax.all_to_all(parts, ("blk", "op"), 0, 0, tiled=True)
+
+    def exchange(out):
+        return [out[0]] + [swap(block, 2 * e, n_op) for e, block in enumerate(out[1:], 1)]
+
+    part1, raw, kept = kernel(
+        functools.partial(first_body, n_blk, n_pair),
+        tables + left_ins + right_ins + psi_ins,
+        [narrow, narrow, (left_all, bf16, HBM)],
+        [inter, pltpu.SemaphoreType.DMA((n_blk * n_pair,))],
+        **cost,
+    )
+    sig, dots1, *out1 = kernel(
+        sigma_body,
+        [(x, VMEM) for x in (part1, swap(part1, 1, n_op), raw)] + diags,
+        [wide, ((n_dev, 8, LANES), f32, VMEM)] + sends,
+        nbytes=4 << 20,
+    )
+    parts1 = totals(dots1)
+    got1 = exchange(out1)
+    fld, part2, half = kernel(
+        functools.partial(second_body, n_blk, n_pair, count),
+        tables + [(kept, HBM)] + right_ins + [(x, VMEM) for x in (parts1, raw, sig)] + diags,
+        [narrow, narrow, ((1, 8, LANES), f32, VMEM)],
+        [
+            inter,
+            pltpu.VMEM((n_blk, rows, 2 * cols), f32),
+            pltpu.VMEM(left_all, bf16),
+            pltpu.SemaphoreType.DMA((n_blk,)),
+        ],
+        **cost,
+    )
+    dots2, *out2 = kernel(
+        functools.partial(image_body, count),
+        [(x, VMEM) for x in (half, parts1, part2, swap(part2, 1, n_op), raw, sig, fld)] + diags,
+        [((n_dev, 16, LANES), f32, VMEM)] + sends,
+        [pltpu.VMEM((2, rows, cols), f32)],
+        nbytes=4 << 20,
+    )
+    parts2 = totals(dots2)
+    got2 = exchange(out2)
+    final = ((n_blk, step, n_op * cols), bf16, VMEM)
+    new, res, energy = kernel(
+        functools.partial(third_body, n_blk, n_op, count),
+        [(slots, SMEM)] + [(x, VMEM) for x in (parts1, parts2, *got1, *got2)],
+        [final, final, ((1,), f32, SMEM)],
+        nbytes=4 << 20,
+    )
+    return new, res, energy
 
 
 def solution(mesh):
@@ -106,8 +615,26 @@
         P("grp", None),
         P(("grp", "blk")),
     )
+
+    def body(*args):
+        psi, left_ops, right_ops, diag_right = args[0], args[1], args[2], args[7]
+        n_op = mesh.shape["op"]
+        cols = diag_right.shape[0] // n_op
+        fits = (
+            psi.shape[0] == 1
+            and diag_right.shape[0] % n_op == 0
+            and cols == LANES
+            and n_op % 2 == 0
+            and cols % right_ops.shape[2] == 0
+            and cols // right_ops.shape[2] * n_op == right_ops.shape[1]
+            and psi.shape[1] % (16 * n_op) == 0
+            and n_op & (n_op - 1) == 0
+            and mesh.shape["blk"] > 1
+        )
+        return (per_device if fits else per_device_general)(*args)
+
     return jax.shard_map(
-        per_device,
+        body,
         mesh=mesh,
         in_specs=placed,
         out_specs=(P("grp", "op", "blk"), P("grp", "op", "blk"), P("grp")),

time: 386 us -> 79.2 us (0.21)
  blocking collectives: 130 us -> 10.9 us
  local copies, waits for them, and re-layouts: 72.9 us -> 3.61 us
  waiting for transfers between devices: 93.8 us -> 29.1 us
  other arithmetic: 40.2 us -> 0 us
  between operations: 22.3 us -> 0.73 us
  matrix products: 17.2 us -> 0 us
  Pallas kernels: 0 us -> 13.3 us
  starting transfers between devices: 8.23 us -> 21.3 us
    psum x2 -> x0, waiting for transfers between devices: 64.4 us -> none  [op_total(): lax.psum(partial_value.astype(jnp.bfloat16), 'op').astype(jnp.float32)]
    all_to_all x2 -> x1, blocking collectives: 71.1 us -> 10.9 us  [totals(): return lax.all_to_all(parts, ('blk', 'op'), 0, 0, tiled=True)]
    psum x5 -> x0, blocking collectives: 58.6 us -> none  [the longest x4 44.6 us: reduce_dots(): sums = lax.psum(values, 'blk')]
    convert_element_type x3 -> x0, local copies, waits for them, and re-layouts: 27 us -> none  [the longest x2 26.8 us: left_local(): return jnp.einsum('ksij,sjc->ksic', left_ops, field, preferred_element_ty...]
    all_to_all x2 -> x1, waiting for transfers between devices: 29.4 us -> 6.48 us  [totals(): return lax.all_to_all(parts, ('blk', 'op'), 0, 0, tiled=True)]
    ppermute x0 -> x18, waiting for transfers between devices: none -> 22.6 us  [the longest x6 11.7 us: onward(): return lax.ppermute(block, 'blk', pairs)]
    reshape x4 -> x0, local copies, waits for them, and re-layouts: 18.1 us -> none  [the longest x2 10.5 us: right_part(): shifted = shifted.reshape(terms_dev, nsec, rows, right_local, right_width)]
    ppermute x0 -> x18, starting transfers between devices: none -> 17.8 us  [the longest x6 11.1 us: onward(): return lax.ppermute(block, 'blk', pairs)]
  transfers between devices with their start and end apart: 4 -> 19, of which waited for: 4 -> 9; matrix products, arithmetic and copies ran while one was open for 12% -> 0% of each run, Pallas kernels for 0% -> 6%
where the time goes in v9:
time: 79.2 us; the launch traced here: 78.9 us
  waiting for transfers between devices  29.1 us (37%)
  starting transfers between devices  21.3 us (27%)
  Pallas kernels  13.3 us (17%)
  blocking collectives  10.9 us (14%)
  local copies, waits for them, and re-layouts  3.61 us (5%)
    pallas_call x7, Pallas kernels, kernel(): pl.pallas_call(body, out_shape=[HBM(shape, dtype) if space == HBM else ja...  13.3 us
    ppermute x6, waiting for transfers between devices, onward(): return lax.ppermute(block, 'blk', pairs)  11.7 us
    ppermute x6, starting transfers between devices, onward(): return lax.ppermute(block, 'blk', pairs)  11.1 us
    all_to_all x1, blocking collectives, totals(): return lax.all_to_all(parts, ('blk', 'op'), 0, 0, tiled=True)  10.9 us
    ppermute x12, waiting for transfers between devices, swap(): return lax.ppermute(block, 'op', [(i, i ^ e) for i in range(n_op)])  10.9 us
    ppermute x12, starting transfers between devices, swap(): return lax.ppermute(block, 'op', [(i, i ^ e) for i in range(n_op)])  6.7 us
    all_to_all x1, waiting for transfers between devices, totals(): return lax.all_to_all(parts, ('blk', 'op'), 0, 0, tiled=True)  6.48 us
    unnamed x12, local copies, waits for them, and re-layouts  3.61 us
  transfers between devices with their start and end apart: 19, of which 9 were waited for; matrix products, arithmetic and copies ran while one was open for 0% of the time, Pallas kernels for 6%

profile of v9, /device:TPU:0, one launch (start us, length us, event | category | flops | bytes accessed | tf_op | source)
XLA Modules:
  0.0 78.9 jit_solution(16072808871895377892)
XLA Ops:
  0.6 3.1 %collective-permute-start.1 = (bf16[2,256,256]{2,1,0:T(8,128)(2,1)}, bf16[2,256,256]{2,1,0:T(8,128)(2,1)S(1)}, u32[]{:S(2)}, u32[]{:S(2)}) collective-permute-start(bf16[2,256,256]{2,1,0:T(8,128)(2,1)} %bitcast.5), channel_id=1, source_target_pairs={{0,4},{4,12},{12,8},{8,0},{1,5},{5,13},{13,9},{9,1},{2,6},{6,14},{... | collective-permute-start | bytes 786440 | tf_op jit(solution)/shard_map/ppermute | solution.py:142
  3.7 1.5 %collective-permute-start = (bf16[2,256,256]{2,1,0:T(8,128)(2,1)}, bf16[2,256,256]{2,1,0:T(8,128)(2,1)S(1)}, u32[]{:S(2)}, u32[]{:S(2)}) collective-permute-start(bf16[2,256,256]{2,1,0:T(8,128)(2,1)} %bitcast.6), channel_id=1, source_target_pairs={{0,2},{1,3},{2,0},{3,1},{4,6},{5,7},{6,4},{7,5},{8,10},{9,11},{10,... | collective-permute-start | bytes 786440 | tf_op jit(solution)/shard_map/ppermute | solution.py:146
  5.2 0.0 collective-permute-start.2
  5.2 1.3 %collective-permute-done.2._ = s32[2]{0:T(128)S(1)} collective-permute-done((s32[2]{0:T(128)}, s32[2]{0:T(128)S(1)}, u32[]{:S(2)}, u32[]{:S(2)}) %collective-permute-start.2) | collective-permute-done | bytes 40 | tf_op jit(solution)/shard_map/ppermute | solution.py:146
  6.5 0.0 copy-start.2
  6.5 0.7 copy-done.2
  7.1 1.9 %shard_map.103 = (bf16[256,256]{1,0:T(8,128)(2,1)S(1)}, bf16[256,128]{1,0:T(8,128)(2,1)S(1)}, bf16[256,256]{1,0:T(8,128)(2,1)S(1)}, bf16[256,128]{1,0:T(8,128)(2...) custom-call(s32[2]{0:T(128)S(1)} %copy-done.2, s32[2]{0:T(128)S(1)} %collective-permute-done.2._, ...), custom_call_target="tpu_custom_call" | custom-call | bytes 1048576 | tf_op jit(solution)/shard_map/pallas_call | solution.py:113
  9.0 0.0 copy-start
  9.0 0.6 collective-permute-start.3
  9.6 3.8 %collective-permute-done.3.refs_1_.refs_9_ = bf16[144,256]{1,0:T(8,128)(2,1)S(1)} collective-permute-done((bf16[144,256]{1,0:T(8,128)(2,1)S(1)}, bf16[144,256]{1,0:T(8,128)(2,1)S(1)}, u32[]{:S(2)}, u32[]{:S(2)}) %collective-permute-start.3) | collective-permute-done | bytes 73760 | tf_op jit(solution)/shard_map/ppermute | solution.py:146
  13.5 0.0 collective-permute-done.1.refs_2_
  13.5 0.0 collective-permute-done.refs_1_
  13.5 2.6 %collective-permute-start.5 = (bf16[2,256,256]{2,1,0:T(8,128)(2,1)S(1)}, bf16[2,256,256]{2,1,0:T(8,128)(2,1)S(1)}, u32[]{:S(2)}, u32[]{:S(2)}) collective-permute-start(bf16[2,256,256]{2,1,0:T(8,128)(2,1)S(1)} %collective-permute-done.1.refs_2_), channel_id=1, source_target_pairs={{0,4},{4,12},{12,8},{8,0},{1,5},{5,13},{13,9},{9,1},{2,6},{6,14},{... | collective-permute-start | bytes 786440 | tf_op jit(solution)/shard_map/ppermute | solution.py:142
  16.1 1.3 %collective-permute-start.4 = (bf16[2,256,256]{2,1,0:T(8,128)(2,1)S(1)}, bf16[2,256,256]{2,1,0:T(8,128)(2,1)S(1)}, u32[]{:S(2)}, u32[]{:S(2)}) collective-permute-start(bf16[2,256,256]{2,1,0:T(8,128)(2,1)S(1)} %collective-permute-done.1.refs_2_), channel_id=1, source_target_pairs={{0,2},{1,3},{2,0},{3,1},{4,6},{5,7},{6,4},{7,5},{8,10},{9,11},{10,... | collective-permute-start | bytes 786440 | tf_op jit(solution)/shard_map/ppermute | solution.py:146
  17.4 0.4 collective-permute-start.6
  17.8 0.0 copy-start.1
  17.8 0.7 copy-done.1
  18.5 0.0 copy-start.3
  18.5 0.7 copy-done.3
  19.1 0.0 copy-start.4
  19.1 0.7 copy-done.4
  19.8 1.3 %shard_map.104 = (s32[16]{0:T(128)S(1)}, s32[4]{0:T(128)S(1)}, s32[4]{0:T(128)S(1)}, f32[4,256,128]{2,1,0:T(8,128)S(1)}) custom-call(s32[4]{0:T(128)S(1)} %copy-done.3, s32[4]{0:T(128)S(1)} %copy-done.4, f32[4,256]{1,0:T(4,128)S(1)} %copy-done.1, bf16[144,256]{1,0:T(8,128)(2,1)S(1)} %get-tuple-element.48.refs_0_.refs_8_, ...), custom_call_target="tpu_custom_call" | custom-call | tf_op jit(solution)/shard_map/pallas_call | solution.py:113
  21.2 2.2 %collective-permute-done.6.refs_11_ = bf16[256,128]{1,0:T(8,128)(2,1)S(1)} collective-permute-done((bf16[256,128]{1,0:T(8,128)(2,1)S(1)}, bf16[256,128]{1,0:T(8,128)(2,1)S(1)}, u32[]{:S(2)}, u32[]{:S(2)}) %collective-permute-start.6) | collective-permute-done | bytes 65568 | tf_op jit(solution)/shard_map/ppermute | solution.py:142
  23.4 0.0 collective-permute-done.5.refs_4_
  23.4 0.0 collective-permute-done.4.refs_3_
  23.4 1.7 %collective-permute-start.8 = (bf16[2,256,256]{2,1,0:T(8,128)(2,1)S(1)}, bf16[2,256,256]{2,1,0:T(8,128)(2,1)S(1)}, u32[]{:S(2)}, u32[]{:S(2)}) collective-permute-start(bf16[2,256,256]{2,1,0:T(8,128)(2,1)S(1)} %collective-permute-done.5.refs_4_), channel_id=1, source_target_pairs={{0,4},{4,12},{12,8},{8,0},{1,5},{5,13},{13,9},{9,1},{2,6},{6,14},{... | collective-permute-start | bytes 786440 | tf_op jit(solution)/shard_map/ppermute | solution.py:142
  25.1 1.3 %collective-permute-start.7 = (bf16[2,256,256]{2,1,0:T(8,128)(2,1)S(1)}, bf16[2,256,256]{2,1,0:T(8,128)(2,1)S(1)}, u32[]{:S(2)}, u32[]{:S(2)}) collective-permute-start(bf16[2,256,256]{2,1,0:T(8,128)(2,1)S(1)} %collective-permute-done.5.refs_4_), channel_id=1, source_target_pairs={{0,2},{1,3},{2,0},{3,1},{4,6},{5,7},{6,4},{7,5},{8,10},{9,11},{10,... | collective-permute-start | bytes 786440 | tf_op jit(solution)/shard_map/ppermute | solution.py:146
  26.4 1.2 %collective-permute-start.10 = (bf16[256,128]{1,0:T(8,128)(2,1)S(1)}, bf16[256,128]{1,0:T(8,128)(2,1)S(1)}, u32[]{:S(2)}, u32[]{:S(2)}) collective-permute-start(bf16[256,128]{1,0:T(8,128)(2,1)S(1)} %get-tuple-element.61), channel_id=1, source_target_pairs={{0,8},{4,0},{12,4},{8,12},{1,9},{5,1},{13,5},{9,13},{2,10},{6,2},{... | collective-permute-start | bytes 196616 | tf_op jit(solution)/shard_map/ppermute | solution.py:142
  27.7 0.0 collective-permute-start.9
  27.7 4.7 %collective-permute-done.10.refs_14_ = bf16[256,128]{1,0:T(8,128)(2,1)S(1)} collective-permute-done((bf16[256,128]{1,0:T(8,128)(2,1)S(1)}, bf16[256,128]{1,0:T(8,128)(2,1)S(1)}, u32[]{:S(2)}, u32[]{:S(2)}) %collective-permute-start.10) | collective-permute-done | bytes 65568 | tf_op jit(solution)/shard_map/ppermute | solution.py:142
  32.4 0.0 collective-permute-done.9.refs_12_
  32.4 0.0 collective-permute-done.8.refs_6_
  32.4 0.0 collective-permute-done.7.refs_5_
  32.4 1.4 %collective-permute-start.11 = (bf16[2,256,256]{2,1,0:T(8,128)(2,1)S(1)}, bf16[2,256,256]{2,1,0:T(8,128)(2,1)S(1)}, u32[]{:S(2)}, u32[]{:S(2)}) collective-permute-start(bf16[2,256,256]{2,1,0:T(8,128)(2,1)S(1)} %collective-permute-done.8.refs_6_), channel_id=1, source_target_pairs={{0,2},{1,3},{2,0},{3,1},{4,6},{5,7},{6,4},{7,5},{8,10},{9,11},{10,... | collective-permute-start | bytes 786440 | tf_op jit(solution)/shard_map/ppermute | solution.py:146
  33.8 2.0 %collective-permute-start.13 = (bf16[256,256]{1,0:T(8,128)(2,1)S(1)}, bf16[256,256]{1,0:T(8,128)(2,1)S(1)}, u32[]{:S(2)}, u32[]{:S(2)}) collective-permute-start(bf16[256,256]{1,0:T(8,128)(2,1)S(1)} %get-tuple-element.65), channel_id=1, source_target_pairs={{0,12},{4,8},{12,0},{8,4},{1,13},{5,9},{13,1},{9,5},{2,14},{6,10},... | collective-permute-start | bytes 393224 | tf_op jit(solution)/shard_map/ppermute | solution.py:142
  35.8 0.0 collective-permute-start.12
  35.8 4.8 %collective-permute-done.13.refs_13_ = bf16[256,256]{1,0:T(8,128)(2,1)S(1)} collective-permute-done((bf16[256,256]{1,0:T(8,128)(2,1)S(1)}, bf16[256,256]{1,0:T(8,128)(2,1)S(1)}, u32[]{:S(2)}, u32[]{:S(2)}) %collective-permute-start.13) | collective-permute-done | bytes 131104 | tf_op jit(solution)/shard_map/ppermute | solution.py:142
  40.6 0.0 collective-permute-done.12.refs_15_
  40.6 0.0 collective-permute-done.11.refs_7_
  40.6 0.0 copy-start.5
  40.6 0.9 %copy-done.5 = bf16[2,1,256,256]{3,2,1,0:T(8,128)(2,1)S(1)} copy-done((bf16[2,1,256,256]{3,2,1,0:T(8,128)(2,1)S(1)}, bf16[2,1,256,256]{3,2,1,0:T(8,128)(2,1)}, u32[]{:S(2)}) %copy-start.5) | copy-done | bytes 262168
  41.6 3.0 %shard_map.105 = (bf16[4,256,256]{2,1,0:T(8,128)(2,1)S(1)}, bf16[4,256,256]{2,1,0:T(8,128)(2,1)S(1)}, bf16[4,2,2,256,256]{4,3,2,1,0:T(8,128)(2,1)}) custom-call(s32[16]{0:T(128)S(1)} %get-tuple-element.55.src, s32[4]{0:T(128)S(1)} %get-tuple-element.56.widths, bf16[2,256,256]{2,1,0:T(8,128)(2,1)S(1)} %bitcast.7, ...), custom_call_target="tpu_custom_call" | custom-call | flops 1073741824 | bytes 6291456 | tf_op jit(solution)/shard_map/pallas_call | solution.py:113
  44.6 0.1 collective-permute-start.14
  44.7 1.9 %collective-permute-done.14.other = bf16[4,256,256]{2,1,0:T(8,128)(2,1)S(1)} collective-permute-done((bf16[4,256,256]{2,1,0:T(8,128)(2,1)S(1)}, bf16[4,256,256]{2,1,0:T(8,128)(2,1)S(1)}, u32[]{:S(2)}, u32[]{:S(2)}) %collective-permute-start.14) | collective-permute-done | bytes 524320 | tf_op jit(solution)/shard_map/ppermute | solution.py:146
  46.6 0.0 copy-done
  46.6 0.5 shard_map.106
  47.0 10.9 %all_to_all.10.refs_2_.parts.parts1 = f32[16,8,128]{2,1,0:T(8,128)S(1)} all-to-all(f32[16,8,128]{2,1,0:T(8,128)S(1)} %get-tuple-element.74), channel_id=1, replica_groups=mesh['grp'=2,'blk'=4,'op'=4] {'blk','op'}, dimensions={0} | all-to-all | bytes 131072 | tf_op jit(solution)/shard_map/all_to_all | solution.py:556
  57.9 3.5 %shard_map.107 = (bf16[4,256,256]{2,1,0:T(8,128)(2,1)S(1)}, bf16[4,256,256]{2,1,0:T(8,128)(2,1)S(1)}, f32[1,8,128]{2,1,0:T(8,128)S(1)}) custom-call(s32[16]{0:T(128)S(1)} %get-tuple-element.55.src, s32[4]{0:T(128)S(1)} %get-tuple-element.56.widths, bf16[4,2,2,256,256]{4,3,2,1,0:T(8,128)(2,1)} %get-tuple-element.75.left_in, ...), custom_call_target="tpu_custom_call" | custom-call | flops 1073741824 | bytes 6291456 | tf_op jit(solution)/shard_map/pallas_call | solution.py:113
  61.4 0.1 collective-permute-start.15
  61.5 0.2 collective-permute-start.16
  61.7 1.7 %collective-permute-done.15.other = bf16[4,256,256]{2,1,0:T(8,128)(2,1)S(1)} collective-permute-done((bf16[4,256,256]{2,1,0:T(8,128)(2,1)S(1)}, bf16[4,256,256]{2,1,0:T(8,128)(2,1)S(1)}, u32[]{:S(2)}, u32[]{:S(2)}) %collective-permute-start.15) | collective-permute-done | bytes 524320 | tf_op jit(solution)/shard_map/ppermute | solution.py:146
  63.4 1.4 %shard_map.108 = (f32[16,16,128]{2,1,0:T(8,128)}, bf16[2,4,64,256]{3,2,1,0:T(8,128)(2,1)S(1)}, bf16[2,4,64,256]{3,2,1,0:T(8,128)(2,1)S(1)}) custom-call(f32[1,8,128]{2,1,0:T(8,128)S(1)} %get-tuple-element.77.half, f32[16,8,128]{2,1,0:T(8,128)S(1)} %all_to_all.10.refs_2_.parts.parts1, bf16[4,256,256]{2,1,0:T(8,128)(2,1)S(1)} %get-tuple-element.78.mine, ...), custom_call_target="tpu_custom_call" | custom-call | bytes 4194304 | tf_op jit(solution)/shard_map/pallas_call | solution.py:113
  64.8 0.2 collective-permute-start.17
  65.0 3.5 %all-to-all-start.1 = ((f32[16,16,128]{2,1,0:T(8,128)}), f32[16,16,128]{2,1,0:T(8,128)S(1)}, u32[]{:S(2)}, u32[]{:S(2)}) async-start(f32[16,16,128]{2,1,0:T(8,128)} %get-tuple-element.80), calls=%async_computation.1 | async-start | bytes 262144 | tf_op jit(solution)/shard_map/all_to_all | solution.py:556
  68.5 2.2 %collective-permute-done.16.refs_1_ = bf16[2,4,64,256]{3,2,1,0:T(8,128)(2,1)S(1)} collective-permute-done((bf16[2,4,64,256]{3,2,1,0:T(8,128)(2,1)S(1)}, bf16[2,4,64,256]{3,2,1,0:T(8,128)(2,1)S(1)}, u32[]{:S(2)}, u32[]{:S(2)}) %collective-permute-start.16) | collective-permute-done | bytes 262176 | tf_op jit(solution)/shard_map/ppermute | solution.py:146
  70.7 6.5 %all-to-all-done.1.parts2 = f32[16,16,128]{2,1,0:T(8,128)S(1)} async-done(((f32[16,16,128]{2,1,0:T(8,128)}), f32[16,16,128]{2,1,0:T(8,128)S(1)}, u32[]{:S(2)}, u32[]{:S(2)}) %all-to-all-start.1) | async-done | bytes 131104 | tf_op jit(solution)/shard_map/all_to_all | solution.py:556
  77.2 0.0 collective-permute-done.17.refs_3_
  77.2 1.7 %shard_map.109 = (bf16[4,64,512]{2,1,0:T(8,128)(2,1)}, bf16[4,64,512]{2,1,0:T(8,128)(2,1)}, f32[1]{0:T(128)}) custom-call(s32[4]{0:T(128)S(1)} %get-tuple-element.54.slots, f32[16,8,128]{2,1,0:T(8,128)S(1)} %all_to_all.10.refs_2_.parts.parts1, f32[16,16,128]{2,1,0:T(8,128)S(1)} %all-to-all-done.1.parts2, ...), custom_call_target="tpu_custom_call" | custom-call | bytes 4194304 | tf_op jit(solution)/shard_map/pallas_call | solution.py:113
Async XLA Ops:
  0.6 12.9 %collective-permute-start.1 = (bf16[2,256,256]{2,1,0:T(8,128)(2,1)}, bf16[2,256,256]{2,1,0:T(8,128)(2,1)S(1)}, u32[]{:S(2)}, u32[]{:S(2)}) collective-permute-start(bf16[2,256,256]{2,1,0:T(8,128)(2,1)} %bitcast.5), channel_id=1, source_target_pairs={{0,4},{4,12},{12,8},{8,0},{1,5},{5,13},{13,9},{9,1},{2,6},{6,14},{... | collective-permute-start | bytes 786440 | tf_op jit(solution)/shard_map/ppermute | solution.py:142
  3.7 9.8 %collective-permute-start = (bf16[2,256,256]{2,1,0:T(8,128)(2,1)}, bf16[2,256,256]{2,1,0:T(8,128)(2,1)S(1)}, u32[]{:S(2)}, u32[]{:S(2)}) collective-permute-start(bf16[2,256,256]{2,1,0:T(8,128)(2,1)} %bitcast.6), channel_id=1, source_target_pairs={{0,2},{1,3},{2,0},{3,1},{4,6},{5,7},{6,4},{7,5},{8,10},{9,11},{10,... | collective-permute-start | bytes 786440 | tf_op jit(solution)/shard_map/ppermute | solution.py:146
  5.2 1.3 %collective-permute-start.2 = (s32[2]{0:T(128)}, s32[2]{0:T(128)S(1)}, u32[]{:S(2)}, u32[]{:S(2)}) collective-permute-start(s32[2]{0:T(128)} %shift.1), channel_id=1, source_target_pairs={{0,1},{1,0},{2,3},{3,2},{4,5},{5,4},{6,7},{7,6},{8,9},{9,8},{10,11... | collective-permute-start | bytes 32 | tf_op jit(solution)/shard_map/ppermute | solution.py:146
  6.5 0.7 copy-start.2
  9.0 37.5 %copy-start = (f32[512]{0:T(512)S(1)}, f32[512]{0:T(512)}, u32[]{:S(2)}) copy-start(f32[512]{0:T(512)} %param.15) | copy-start | bytes 6148
  9.0 4.4 %collective-permute-start.3 = (bf16[144,256]{1,0:T(8,128)(2,1)S(1)}, bf16[144,256]{1,0:T(8,128)(2,1)S(1)}, u32[]{:S(2)}, u32[]{:S(2)}) collective-permute-start(bf16[144,256]{1,0:T(8,128)(2,1)S(1)} %get-tuple-element.45), channel_id=1, source_target_pairs={{0,2},{1,3},{2,0},{3,1},{4,6},{5,7},{6,4},{7,5},{8,10},{9,11},{10,... | collective-permute-start | bytes 221192 | tf_op jit(solution)/shard_map/ppermute | solution.py:146
  13.5 9.9 %collective-permute-start.5 = (bf16[2,256,256]{2,1,0:T(8,128)(2,1)S(1)}, bf16[2,256,256]{2,1,0:T(8,128)(2,1)S(1)}, u32[]{:S(2)}, u32[]{:S(2)}) collective-permute-start(bf16[2,256,256]{2,1,0:T(8,128)(2,1)S(1)} %collective-permute-done.1.refs_2_), channel_id=1, source_target_pairs={{0,4},{4,12},{12,8},{8,0},{1,5},{5,13},{13,9},{9,1},{2,6},{6,14},{... | collective-permute-start | bytes 786440 | tf_op jit(solution)/shard_map/ppermute | solution.py:142
  16.1 7.3 %collective-permute-start.4 = (bf16[2,256,256]{2,1,0:T(8,128)(2,1)S(1)}, bf16[2,256,256]{2,1,0:T(8,128)(2,1)S(1)}, u32[]{:S(2)}, u32[]{:S(2)}) collective-permute-start(bf16[2,256,256]{2,1,0:T(8,128)(2,1)S(1)} %collective-permute-done.1.refs_2_), channel_id=1, source_target_pairs={{0,2},{1,3},{2,0},{3,1},{4,6},{5,7},{6,4},{7,5},{8,10},{9,11},{10,... | collective-permute-start | bytes 786440 | tf_op jit(solution)/shard_map/ppermute | solution.py:146
  17.4 6.0 %collective-permute-start.6 = (bf16[256,128]{1,0:T(8,128)(2,1)S(1)}, bf16[256,128]{1,0:T(8,128)(2,1)S(1)}, u32[]{:S(2)}, u32[]{:S(2)}) collective-permute-start(bf16[256,128]{1,0:T(8,128)(2,1)S(1)} %get-tuple-element.47), channel_id=1, source_target_pairs={{0,4},{4,12},{12,8},{8,0},{1,5},{5,13},{13,9},{9,1},{2,6},{6,14},{... | collective-permute-start | bytes 196616 | tf_op jit(solution)/shard_map/ppermute | solution.py:142
  17.8 0.7 copy-start.1
  18.5 0.7 copy-start.3
  19.1 0.7 copy-start.4
  23.4 9.0 %collective-permute-start.8 = (bf16[2,256,256]{2,1,0:T(8,128)(2,1)S(1)}, bf16[2,256,256]{2,1,0:T(8,128)(2,1)S(1)}, u32[]{:S(2)}, u32[]{:S(2)}) collective-permute-start(bf16[2,256,256]{2,1,0:T(8,128)(2,1)S(1)} %collective-permute-done.5.refs_4_), channel_id=1, source_target_pairs={{0,4},{4,12},{12,8},{8,0},{1,5},{5,13},{13,9},{9,1},{2,6},{6,14},{... | collective-permute-start | bytes 786440 | tf_op jit(solution)/shard_map/ppermute | solution.py:142
  25.1 7.3 %collective-permute-start.7 = (bf16[2,256,256]{2,1,0:T(8,128)(2,1)S(1)}, bf16[2,256,256]{2,1,0:T(8,128)(2,1)S(1)}, u32[]{:S(2)}, u32[]{:S(2)}) collective-permute-start(bf16[2,256,256]{2,1,0:T(8,128)(2,1)S(1)} %collective-permute-done.5.refs_4_), channel_id=1, source_target_pairs={{0,2},{1,3},{2,0},{3,1},{4,6},{5,7},{6,4},{7,5},{8,10},{9,11},{10,... | collective-permute-start | bytes 786440 | tf_op jit(solution)/shard_map/ppermute | solution.py:146
  26.4 5.9 %collective-permute-start.10 = (bf16[256,128]{1,0:T(8,128)(2,1)S(1)}, bf16[256,128]{1,0:T(8,128)(2,1)S(1)}, u32[]{:S(2)}, u32[]{:S(2)}) collective-permute-start(bf16[256,128]{1,0:T(8,128)(2,1)S(1)} %get-tuple-element.61), channel_id=1, source_target_pairs={{0,8},{4,0},{12,4},{8,12},{1,9},{5,1},{13,5},{9,13},{2,10},{6,2},{... | collective-permute-start | bytes 196616 | tf_op jit(solution)/shard_map/ppermute | solution.py:142
  27.7 4.7 %collective-permute-start.9 = (bf16[256,128]{1,0:T(8,128)(2,1)S(1)}, bf16[256,128]{1,0:T(8,128)(2,1)S(1)}, u32[]{:S(2)}, u32[]{:S(2)}) collective-permute-start(bf16[256,128]{1,0:T(8,128)(2,1)S(1)} %collective-permute-done.6.refs_11_), channel_id=1, source_target_pairs={{0,1},{1,0},{2,3},{3,2},{4,5},{5,4},{6,7},{7,6},{8,9},{9,8},{10,11... | collective-permute-start | bytes 196616 | tf_op jit(solution)/shard_map/ppermute | solution.py:146
  32.4 8.3 %collective-permute-start.11 = (bf16[2,256,256]{2,1,0:T(8,128)(2,1)S(1)}, bf16[2,256,256]{2,1,0:T(8,128)(2,1)S(1)}, u32[]{:S(2)}, u32[]{:S(2)}) collective-permute-start(bf16[2,256,256]{2,1,0:T(8,128)(2,1)S(1)} %collective-permute-done.8.refs_6_), channel_id=1, source_target_pairs={{0,2},{1,3},{2,0},{3,1},{4,6},{5,7},{6,4},{7,5},{8,10},{9,11},{10,... | collective-permute-start | bytes 786440 | tf_op jit(solution)/shard_map/ppermute | solution.py:146
  33.8 6.8 %collective-permute-start.13 = (bf16[256,256]{1,0:T(8,128)(2,1)S(1)}, bf16[256,256]{1,0:T(8,128)(2,1)S(1)}, u32[]{:S(2)}, u32[]{:S(2)}) collective-permute-start(bf16[256,256]{1,0:T(8,128)(2,1)S(1)} %get-tuple-element.65), channel_id=1, source_target_pairs={{0,12},{4,8},{12,0},{8,4},{1,13},{5,9},{13,1},{9,5},{2,14},{6,10},... | collective-permute-start | bytes 393224 | tf_op jit(solution)/shard_map/ppermute | solution.py:142
  35.8 4.8 %collective-permute-start.12 = (bf16[256,128]{1,0:T(8,128)(2,1)S(1)}, bf16[256,128]{1,0:T(8,128)(2,1)S(1)}, u32[]{:S(2)}, u32[]{:S(2)}) collective-permute-start(bf16[256,128]{1,0:T(8,128)(2,1)S(1)} %collective-permute-done.10.refs_14_), channel_id=1, source_target_pairs={{0,1},{1,0},{2,3},{3,2},{4,5},{5,4},{6,7},{7,6},{8,9},{9,8},{10,11... | collective-permute-start | bytes 196616 | tf_op jit(solution)/shard_map/ppermute | solution.py:146
  40.6 1.0 %copy-start.5 = (bf16[2,1,256,256]{3,2,1,0:T(8,128)(2,1)S(1)}, bf16[2,1,256,256]{3,2,1,0:T(8,128)(2,1)}, u32[]{:S(2)}) copy-start(bf16[2,1,256,256]{3,2,1,0:T(8,128)(2,1)} %param.9) | copy-start | bytes 786436
  44.6 2.0 %collective-permute-start.14 = (bf16[4,256,256]{2,1,0:T(8,128)(2,1)S(1)}, bf16[4,256,256]{2,1,0:T(8,128)(2,1)S(1)}, u32[]{:S(2)}, u32[]{:S(2)}) collective-permute-start(bf16[4,256,256]{2,1,0:T(8,128)(2,1)S(1)} %get-tuple-element.71.mine), channel_id=1, source_target_pairs={{0,1},{1,0},{2,3},{3,2},{4,5},{5,4},{6,7},{7,6},{8,9},{9,8},{10,11... | collective-permute-start | bytes 1572872 | tf_op jit(solution)/shard_map/ppermute | solution.py:146
  61.4 2.0 %collective-permute-start.15 = (bf16[4,256,256]{2,1,0:T(8,128)(2,1)S(1)}, bf16[4,256,256]{2,1,0:T(8,128)(2,1)S(1)}, u32[]{:S(2)}, u32[]{:S(2)}) collective-permute-start(bf16[4,256,256]{2,1,0:T(8,128)(2,1)S(1)} %get-tuple-element.78.mine), channel_id=1, source_target_pairs={{0,1},{1,0},{2,3},{3,2},{4,5},{5,4},{6,7},{7,6},{8,9},{9,8},{10,11... | collective-permute-start | bytes 1572872 | tf_op jit(solution)/shard_map/ppermute | solution.py:146
  61.5 9.2 %collective-permute-start.16 = (bf16[2,4,64,256]{3,2,1,0:T(8,128)(2,1)S(1)}, bf16[2,4,64,256]{3,2,1,0:T(8,128)(2,1)S(1)}, u32[]{:S(2)}, u32[]{:S(2)}) collective-permute-start(bf16[2,4,64,256]{3,2,1,0:T(8,128)(2,1)S(1)} %get-tuple-element.82), channel_id=1, source_target_pairs={{0,2},{1,3},{2,0},{3,1},{4,6},{5,7},{6,4},{7,5},{8,10},{9,11},{10,... | collective-permute-start | bytes 786440 | tf_op jit(solution)/shard_map/ppermute | solution.py:146
  64.8 12.4 %collective-permute-start.17 = (bf16[2,4,64,256]{3,2,1,0:T(8,128)(2,1)S(1)}, bf16[2,4,64,256]{3,2,1,0:T(8,128)(2,1)S(1)}, u32[]{:S(2)}, u32[]{:S(2)}) collective-permute-start(bf16[2,4,64,256]{3,2,1,0:T(8,128)(2,1)S(1)} %get-tuple-element.84), channel_id=1, source_target_pairs={{0,2},{1,3},{2,0},{3,1},{4,6},{5,7},{6,4},{7,5},{8,10},{9,11},{10,... | collective-permute-start | bytes 786440 | tf_op jit(solution)/shard_map/ppermute | solution.py:146
  65.0 12.2 %all-to-all-start.1 = ((f32[16,16,128]{2,1,0:T(8,128)}), f32[16,16,128]{2,1,0:T(8,128)S(1)}, u32[]{:S(2)}, u32[]{:S(2)}) async-start(f32[16,16,128]{2,1,0:T(8,128)} %get-tuple-element.80), calls=%async_computation.1 | async-start | bytes 262144 | tf_op jit(solution)/shard_map/all_to_all | solution.py:556

commit v10 on v9

--- a/solution.py
+++ b/solution.py
@@ -146,11 +146,11 @@
     return lax.ppermute(block, "op", [(i, i ^ e) for i in range(n_op)])
 
 
-def gather(own, n_blk, n_op, pack, table):
+def gather(own, n_blk, n_op, pack, table, early):
     bits = [1 << b for b in reversed(range(1, n_op.bit_length() - 1))]
     order = sorted(range(1, n_blk), key=lambda d: min(d, n_blk - d))
     left, psi, right, tables, columns = {(0, 0): own}, {}, None, None, None
-    waiting, late = {(0, 0): 0}, None
+    waiting, late, made = {(0, 0): 0}, None, None
     for j in range(n_blk + len(bits)):
         new, moved = {}, {}
         for (d, e), done in waiting.items():
@@ -167,6 +167,10 @@
             moved["right"] += [swap(part, 2 * e, n_op) for e, part in enumerate(packed[1:], 1)]
         if j == 1:
             moved["tables"] = table(right)
+        if j == n_blk - 1 and j >= len(bits) + 1:
+            n_early = min(2, n_blk - 1)
+            psi[0] = [columns[0]]
+            moved["early"] = early(left, psi, n_early, tables)
         if 2 <= j < n_blk:
             moved["other"] = swap(psi[order[j - 2]][0], 1, n_op)
         late = onward(columns[order[j]], order[j], n_blk) if j < n_blk - 1 else None
@@ -176,12 +180,12 @@
         kept, moved = lax.optimization_barrier((kept, moved))
         left.update(kept)
         right, tables = moved.get("right", right), moved.get("tables", tables)
+        made = moved.get("early", made)
         if "psi" in moved:
             psi[order[j - 1]] = [moved["psi"]]
         if "other" in moved:
             psi[order[j - 2]].append(moved["other"])
-    psi[0] = [columns[0]]
-    return left, psi, right, tables
+    return left, psi, right, tables, made
 
 
 def place_of():
@@ -326,33 +330,67 @@
         out[t] = jnp.where(row_mask(widths[t], total.shape), total, 0.0).astype(jnp.bfloat16)
 
 
-def first_body(n_blk, n_pair, src, widths, *refs):
-    left = [refs[d * n_pair : (d + 1) * n_pair] for d in range(n_blk)]
-    refs = refs[n_blk * n_pair :]
-    right, refs = refs[:n_pair], refs[n_pair:]
-    psi, part_out, raw_out, left_out, inter, sems = refs[:-5], *refs[-5:]
+def keep(left, left_out, sems):
     copies = []
-    for d in range(n_blk):
-        for e in range(n_pair):
-            copies.append(
-                pltpu.make_async_copy(left[d][e], left_out.at[d, e], sems.at[d * n_pair + e])
-            )
+    for d, line in enumerate(left):
+        for e, ref in enumerate(line):
+            copies.append(pltpu.make_async_copy(ref, left_out.at[d, e], sems.at[d * len(line) + e]))
             copies[-1].start()
-    inter[n_blk] = jnp.zeros_like(inter[n_blk])
-    cols = raw_out.shape[2] // 2
-    for d in range(n_blk):
-        at = 0
-        while at < 2 * cols:
-            block = psi[0][...].astype(jnp.float32)
-            psi = psi[1:]
-            block = jnp.where(row_mask(widths[d], block.shape), block, 0.0)
-            raw_out[d, :, at : at + block.shape[1]] = block.astype(jnp.bfloat16)
-            at += block.shape[1]
-        terms = left[d][0].shape[0]
-        left_products(raw_out[d], lambda at: left[d][at // terms][...], inter.at[d])
-    sum_terms(src, widths, inter, right, part_out)
+    return copies
+
+
+def masked(psi, width, out):
+    at = 0
+    for ref in psi:
+        block = ref[...].astype(jnp.float32)
+        block = jnp.where(row_mask(width, block.shape), block, 0.0)
+        out[:, at : at + block.shape[1]] = block.astype(jnp.bfloat16)
+        at += block.shape[1]
+
+
+def take(refs, counts):
+    out = []
+    for count in counts:
+        out.append(refs[:count])
+        refs = refs[count:]
+    return out, refs
+
+
+def products_of(psi, left, widths, first, raw_out, inter):
+    for d, line in enumerate(left):
+        masked(psi[d], widths[first + d], raw_out.at[d])
+        terms = line[0].shape[0]
+        left_products(raw_out[d], lambda at: line[at // terms][...], inter.at[d])
+
+
+def early_body(n_pair, counts, widths, *refs):
+    left, refs = take(refs, [n_pair] * len(counts))
+    psi, (raw_out, inter_out, left_out, sems) = take(refs, counts)
+    copies = keep(left, left_out, sems)
+    products_of(psi, left, widths, 0, raw_out, inter_out)
     for copy in copies:
         copy.wait()
+
+
+def first_body(n_blk, n_pair, counts, src, widths, *refs):
+    n_late = len(counts)
+    n_early = n_blk - n_late
+    left, refs = take(refs, [n_pair] * n_late)
+    (right,), refs = take(refs, [n_pair])
+    psi, (raw_in, inter_in, part_out, raw_out, left_out, inter, sems) = take(refs, counts)
+    copies = keep(left, left_out, sems)
+    for j, (given, own) in enumerate(((inter_in, inter), (raw_in, raw_out))):
+        copies.append(
+            pltpu.make_async_copy(given, own.at[:n_early], sems.at[n_late * n_pair + j])
+        )
+        copies[-1].start()
+    inter[n_blk] = jnp.zeros_like(inter[n_blk])
+    products_of(
+        psi, left, widths, n_early, raw_out.at[n_early:], inter.at[n_early:n_blk]
+    )
+    for copy in copies:
+        copy.wait()
+    sum_terms(src, widths, inter, right, part_out)
 
 
 def send_rows(sends, j, d, h, block):
@@ -392,13 +430,15 @@
     return scale, tot[1:2] * scale * scale
 
 
-def second_body(n_blk, n_pair, count, src, widths, left_in, *refs):
+def second_body(n_blk, n_pair, count, src, widths, left_early, left_late, *refs):
     right, refs = refs[:n_pair], refs[n_pair:]
     parts, raw_in, sig_in, diag, right_diag, f_out, part_out, half_out = refs[:8]
     inter, corr, held, sems = refs[8:]
     copies = []
+    n_early = left_early.shape[0]
     for d in range(n_blk):
-        copies.append(pltpu.make_async_copy(left_in.at[d], held.at[d], sems.at[d]))
+        kept = left_early.at[d] if d < n_early else left_late.at[d - n_early]
+        copies.append(pltpu.make_async_copy(kept, held.at[d], sems.at[d]))
         copies[-1].start()
     inter[n_blk] = jnp.zeros_like(inter[n_blk])
     scale, theta = norm_theta(parts[...], count)
@@ -538,10 +578,33 @@
             + [((n_blk, rows, LANES), f32, VMEM)],
         )
 
-    left, psi_by, right, (src, widths, slots, diag) = gather(left_ops[:, 0], n_blk, n_op, pack, table)
-    left_ins = [(left[d, 2 * e], VMEM) for d in range(n_blk) for e in range(n_pair)]
+    def inputs(left, psi, those):
+        blocks = [left[d, 2 * e] for d in those for e in range(n_pair)]
+        halves = [half for d in those for half in psi[d]]
+        return [(x, VMEM) for x in blocks], [(x, VMEM) for x in halves], [len(psi[d]) for d in those]
+
+    def early(left, psi, n_early, tables):
+        left_ins, psi_ins, counts = inputs(left, psi, range(n_early))
+        return kernel(
+            functools.partial(early_body, n_pair, counts),
+            [(tables[1], SMEM)] + left_ins + psi_ins,
+            [
+                ((n_early, rows, 2 * cols), bf16, VMEM),
+                ((n_early, n_pair * terms, rows, 2 * cols), bf16, VMEM),
+                ((n_early, n_pair, terms, rows, rows), bf16, HBM),
+            ],
+            [pltpu.SemaphoreType.DMA((n_early * n_pair,))],
+            flops=2 * n_early * rows * rows * 2 * cols * terms * n_pair,
+            nbytes=4 << 20,
+        )
+
+    left, psi_by, right, (src, widths, slots, diag), (raw_early, inter_early, left_early) = gather(
+        left_ops[:, 0], n_blk, n_op, pack, table, early
+    )
+    n_early = raw_early.shape[0]
+    n_late = n_blk - n_early
+    left_ins, psi_ins, counts = inputs(left, psi_by, range(n_early, n_blk))
     right_ins = [(block, VMEM) for block in right]
-    psi_ins = [(block, VMEM) for d in range(n_blk) for block in psi_by[d]]
     diags = [(diag, VMEM), (diag_right[None], VMEM)]
 
     tables = [(src, SMEM), (widths, SMEM)]
@@ -549,7 +612,7 @@
     wide = ((n_blk, rows, 2 * cols), f32, VMEM)
     sends = [((2, n_blk, step, 2 * cols), bf16, VMEM)] * n_pair
     inter = pltpu.VMEM((n_blk + 1, n_pair * terms, rows, 2 * cols), bf16)
-    left_all = (n_blk, n_pair, terms, rows, rows)
+    left_late = (n_late, n_pair, terms, rows, rows)
     cost = dict(flops=2 * n_blk * rows * 2 * cols * terms * n_pair * (rows + 2 * cols), nbytes=6 << 20)
 
     def totals(parts):
@@ -559,10 +622,10 @@
         return [out[0]] + [swap(block, 2 * e, n_op) for e, block in enumerate(out[1:], 1)]
 
     part1, raw, kept = kernel(
-        functools.partial(first_body, n_blk, n_pair),
-        tables + left_ins + right_ins + psi_ins,
-        [narrow, narrow, (left_all, bf16, HBM)],
-        [inter, pltpu.SemaphoreType.DMA((n_blk * n_pair,))],
+        functools.partial(first_body, n_blk, n_pair, counts),
+        tables + left_ins + right_ins + psi_ins + [(raw_early, VMEM), (inter_early, VMEM)],
+        [narrow, narrow, (left_late, bf16, HBM)],
+        [inter, pltpu.SemaphoreType.DMA((n_late * n_pair + 2,))],
         **cost,
     )
     sig, dots1, *out1 = kernel(
@@ -571,16 +634,15 @@
         [wide, ((n_dev, 8, LANES), f32, VMEM)] + sends,
         nbytes=4 << 20,
     )
-    parts1 = totals(dots1)
-    got1 = exchange(out1)
+    parts1, got1 = lax.optimization_barrier((totals(dots1), exchange(out1)))
     fld, part2, half = kernel(
         functools.partial(second_body, n_blk, n_pair, count),
-        tables + [(kept, HBM)] + right_ins + [(x, VMEM) for x in (parts1, raw, sig)] + diags,
+        tables + [(left_early, HBM), (kept, HBM)] + right_ins + [(x, VMEM) for x in (parts1, raw, sig)] + diags,
         [narrow, narrow, ((1, 8, LANES), f32, VMEM)],
         [
             inter,
             pltpu.VMEM((n_blk, rows, 2 * cols), f32),
-            pltpu.VMEM(left_all, bf16),
+            pltpu.VMEM((n_blk, *left_late[1:]), bf16),
             pltpu.SemaphoreType.DMA((n_blk,)),
         ],
         **cost,
@@ -629,7 +691,7 @@
             and cols // right_ops.shape[2] * n_op == right_ops.shape[1]
             and psi.shape[1] % (16 * n_op) == 0
             and n_op & (n_op - 1) == 0
-            and mesh.shape["blk"] > 1
+            and mesh.shape["blk"] > n_op.bit_length() - 1
         )
         return (per_device if fits else per_device_general)(*args)
 

time: 79.2 us -> 76.2 us (0.962)
  blocking collectives: 10.9 us -> 20.8 us
  waiting for transfers between devices: 29.1 us -> 23.7 us
  starting transfers between devices: 21.3 us -> 16.6 us
  local copies, waits for them, and re-layouts: 3.61 us -> 0.03 us
  Pallas kernels: 13.3 us -> 14.2 us
    all_to_all x1 -> x2, blocking collectives: 10.9 us -> 20.8 us  [totals(): return lax.all_to_all(parts, ('blk', 'op'), 0, 0, tiled=True)]
    all_to_all x1 -> x0, waiting for transfers between devices: 6.48 us -> none  [totals(): return lax.all_to_all(parts, ('blk', 'op'), 0, 0, tiled=True)]
    unnamed x12, local copies, waits for them, and re-layouts: 3.61 us -> 0.03 us
    all_to_all x1 -> x0, starting transfers between devices: 3.51 us -> none  [totals(): return lax.all_to_all(parts, ('blk', 'op'), 0, 0, tiled=True)]
    ppermute x6, waiting for transfers between devices: 11.7 us -> 13.5 us  [onward(): return lax.ppermute(block, 'blk', pairs)]
    ppermute x12, starting transfers between devices: 6.7 us -> 5.36 us  [swap(): return lax.ppermute(block, 'op', [(i, i ^ e) for i in range(n_op)])]
    pallas_call x7 -> x8, Pallas kernels: 13.3 us -> 14.2 us  [kernel(): pl.pallas_call(body, out_shape=[HBM(shape, dtype) if space == HBM else ja...]
  transfers between devices with their start and end apart: 19 -> 18, of which waited for: 9 -> 9; matrix products, arithmetic and copies ran while one was open for 0% -> 0% of each run, Pallas kernels for 6% -> 6%
where the time goes in v10:
time: 76.2 us; the launch traced here: 76 us
  waiting for transfers between devices  23.7 us (31%)
  blocking collectives  20.8 us (27%)
  starting transfers between devices  16.6 us (22%)
  Pallas kernels  14.2 us (19%)
    all_to_all x2, blocking collectives, totals(): return lax.all_to_all(parts, ('blk', 'op'), 0, 0, tiled=True)  20.8 us
    pallas_call x8, Pallas kernels, kernel(): pl.pallas_call(body, out_shape=[HBM(shape, dtype) if space == HBM else ja...  14.2 us
    ppermute x6, waiting for transfers between devices, onward(): return lax.ppermute(block, 'blk', pairs)  13.5 us
    ppermute x6, starting transfers between devices, onward(): return lax.ppermute(block, 'blk', pairs)  11.2 us
    ppermute x12, waiting for transfers between devices, swap(): return lax.ppermute(block, 'op', [(i, i ^ e) for i in range(n_op)])  10.2 us
    ppermute x12, starting transfers between devices, swap(): return lax.ppermute(block, 'op', [(i, i ^ e) for i in range(n_op)])  5.36 us
  transfers between devices with their start and end apart: 18, of which 9 were waited for; matrix products, arithmetic and copies ran while one was open for 0% of the time, Pallas kernels for 6%

profile of v10, /device:TPU:0, one launch (start us, length us, event | category | flops | bytes accessed | tf_op | source)
XLA Modules:
  0.0 76.0 jit_solution(10115811494184507991)
XLA Ops:
  0.6 0.0 copy-start.3
  0.6 3.1 %collective-permute-start.1 = (bf16[2,256,256]{2,1,0:T(8,128)(2,1)}, bf16[2,256,256]{2,1,0:T(8,128)(2,1)S(1)}, u32[]{:S(2)}, u32[]{:S(2)}) collective-permute-start(bf16[2,256,256]{2,1,0:T(8,128)(2,1)} %bitcast.2), channel_id=1, source_target_pairs={{0,4},{4,12},{12,8},{8,0},{1,5},{5,13},{13,9},{9,1},{2,6},{6,14},{... | collective-permute-start | bytes 786440 | tf_op jit(solution)/shard_map/ppermute | solution.py:142
  3.7 1.5 %collective-permute-start = (bf16[2,256,256]{2,1,0:T(8,128)(2,1)}, bf16[2,256,256]{2,1,0:T(8,128)(2,1)S(1)}, u32[]{:S(2)}, u32[]{:S(2)}) collective-permute-start(bf16[2,256,256]{2,1,0:T(8,128)(2,1)} %bitcast.3), channel_id=1, source_target_pairs={{0,2},{1,3},{2,0},{3,1},{4,6},{5,7},{6,4},{7,5},{8,10},{9,11},{10,... | collective-permute-start | bytes 786440 | tf_op jit(solution)/shard_map/ppermute | solution.py:146
  5.2 0.0 copy-done.3
  5.2 0.0 collective-permute-start.2
  5.2 1.1 %collective-permute-done.2._ = s32[2]{0:T(128)S(1)} collective-permute-done((s32[2]{0:T(128)S(1)}, s32[2]{0:T(128)S(1)}, u32[]{:S(2)}, u32[]{:S(2)}) %collective-permute-start.2) | collective-permute-done | bytes 40 | tf_op jit(solution)/shard_map/ppermute | solution.py:146
  6.3 0.0 copy-start
  6.3 1.9 %shard_map.103 = (bf16[256,256]{1,0:T(8,128)(2,1)S(1)}, bf16[256,128]{1,0:T(8,128)(2,1)S(1)}, bf16[256,256]{1,0:T(8,128)(2,1)S(1)}, bf16[256,128]{1,0:T(8,128)(2...) custom-call(s32[2]{0:T(128)S(1)} %copy-done.3, s32[2]{0:T(128)S(1)} %collective-permute-done.2._, ...), custom_call_target="tpu_custom_call" | custom-call | bytes 1048576 | tf_op jit(solution)/shard_map/pallas_call | solution.py:113
  8.2 0.0 copy-start.2
  8.3 0.6 collective-permute-start.3
  8.9 4.4 %collective-permute-done.3.refs_1_.refs_5_ = bf16[144,256]{1,0:T(8,128)(2,1)S(1)} collective-permute-done((bf16[144,256]{1,0:T(8,128)(2,1)S(1)}, bf16[144,256]{1,0:T(8,128)(2,1)S(1)}, u32[]{:S(2)}, u32[]{:S(2)}) %collective-permute-start.3) | collective-permute-done | bytes 73760 | tf_op jit(solution)/shard_map/ppermute | solution.py:146
  13.3 0.0 collective-permute-done.1.refs_2_
  13.3 0.0 collective-permute-done.refs_1_
  13.3 0.0 copy-start.4
  13.3 0.0 copy-start.5
  13.3 2.6 %collective-permute-start.5 = (bf16[2,256,256]{2,1,0:T(8,128)(2,1)S(1)}, bf16[2,256,256]{2,1,0:T(8,128)(2,1)S(1)}, u32[]{:S(2)}, u32[]{:S(2)}) collective-permute-start(bf16[2,256,256]{2,1,0:T(8,128)(2,1)S(1)} %collective-permute-done.1.refs_2_), channel_id=1, source_target_pairs={{0,4},{4,12},{12,8},{8,0},{1,5},{5,13},{13,9},{9,1},{2,6},{6,14},{... | collective-permute-start | bytes 786440 | tf_op jit(solution)/shard_map/ppermute | solution.py:142
  15.9 1.5 %collective-permute-start.4 = (bf16[2,256,256]{2,1,0:T(8,128)(2,1)S(1)}, bf16[2,256,256]{2,1,0:T(8,128)(2,1)S(1)}, u32[]{:S(2)}, u32[]{:S(2)}) collective-permute-start(bf16[2,256,256]{2,1,0:T(8,128)(2,1)S(1)} %collective-permute-done.1.refs_2_), channel_id=1, source_target_pairs={{0,2},{1,3},{2,0},{3,1},{4,6},{5,7},{6,4},{7,5},{8,10},{9,11},{10,... | collective-permute-start | bytes 786440 | tf_op jit(solution)/shard_map/ppermute | solution.py:146
  17.4 0.4 collective-permute-start.6
  17.9 0.0 copy-done.2
  17.9 0.0 copy-done.4
  17.9 0.0 copy-done.5
  17.9 1.3 %shard_map.104 = (s32[16]{0:T(128)S(1)}, s32[4]{0:T(128)S(1)}, s32[4]{0:T(128)S(1)}, f32[4,256,128]{2,1,0:T(8,128)S(1)}) custom-call(s32[4]{0:T(128)S(1)} %copy-done.4, s32[4]{0:T(128)S(1)} %copy-done.5, f32[4,256]{1,0:T(4,128)S(1)} %copy-done.2, bf16[144,256]{1,0:T(8,128)(2,1)S(1)} %get-tuple-element.57.refs_0_.refs_4_, ...), custom_call_target="tpu_custom_call" | custom-call | tf_op jit(solution)/shard_map/pallas_call | solution.py:113
  19.2 4.2 %collective-permute-done.6.refs_5_ = bf16[256,128]{1,0:T(8,128)(2,1)S(1)} collective-permute-done((bf16[256,128]{1,0:T(8,128)(2,1)S(1)}, bf16[256,128]{1,0:T(8,128)(2,1)S(1)}, u32[]{:S(2)}, u32[]{:S(2)}) %collective-permute-start.6) | collective-permute-done | bytes 65568 | tf_op jit(solution)/shard_map/ppermute | solution.py:142
  23.5 0.0 collective-permute-done.5.refs_0_
  23.5 0.0 collective-permute-done.4.refs_3_
  23.5 1.7 %collective-permute-start.8 = (bf16[2,256,256]{2,1,0:T(8,128)(2,1)S(1)}, bf16[2,256,256]{2,1,0:T(8,128)(2,1)S(1)}, u32[]{:S(2)}, u32[]{:S(2)}) collective-permute-start(bf16[2,256,256]{2,1,0:T(8,128)(2,1)S(1)} %collective-permute-done.5.refs_0_), channel_id=1, source_target_pairs={{0,4},{4,12},{12,8},{8,0},{1,5},{5,13},{13,9},{9,1},{2,6},{6,14},{... | collective-permute-start | bytes 786440 | tf_op jit(solution)/shard_map/ppermute | solution.py:142
  25.2 0.5 collective-permute-start.7
  25.7 1.2 %collective-permute-start.10 = (bf16[256,128]{1,0:T(8,128)(2,1)S(1)}, bf16[256,128]{1,0:T(8,128)(2,1)S(1)}, u32[]{:S(2)}, u32[]{:S(2)}) collective-permute-start(bf16[256,128]{1,0:T(8,128)(2,1)S(1)} %get-tuple-element.68), channel_id=1, source_target_pairs={{0,8},{4,0},{12,4},{8,12},{1,9},{5,1},{13,5},{9,13},{2,10},{6,2},{... | collective-permute-start | bytes 196616 | tf_op jit(solution)/shard_map/ppermute | solution.py:142
  26.9 0.0 collective-permute-start.9
  26.9 5.7 %collective-permute-done.10.refs_7_ = bf16[256,128]{1,0:T(8,128)(2,1)S(1)} collective-permute-done((bf16[256,128]{1,0:T(8,128)(2,1)S(1)}, bf16[256,128]{1,0:T(8,128)(2,1)S(1)}, u32[]{:S(2)}, u32[]{:S(2)}) %collective-permute-start.10) | collective-permute-done | bytes 65568 | tf_op jit(solution)/shard_map/ppermute | solution.py:142
  32.6 0.0 collective-permute-done.9.refs_6_
  32.6 0.1 collective-permute-done.8.refs_2_
  32.7 0.0 collective-permute-done.7.refs_1_
  32.8 0.0 collective-permute-start.11
  32.8 2.2 %collective-permute-start.13 = (bf16[256,256]{1,0:T(8,128)(2,1)S(1)}, bf16[256,256]{1,0:T(8,128)(2,1)S(1)}, u32[]{:S(2)}, u32[]{:S(2)}) collective-permute-start(bf16[256,256]{1,0:T(8,128)(2,1)S(1)} %get-tuple-element.79), channel_id=1, source_target_pairs={{0,12},{4,8},{12,0},{8,4},{1,13},{5,9},{13,1},{9,5},{2,14},{6,10},... | collective-permute-start | bytes 393224 | tf_op jit(solution)/shard_map/ppermute | solution.py:142
  34.9 0.0 collective-permute-start.12
  34.9 0.0 copy-done
  34.9 1.7 %shard_map.105 = (bf16[2,256,256]{2,1,0:T(8,128)(2,1)S(1)}, bf16[2,4,256,256]{3,2,1,0:T(8,128)(2,1)S(1)}, bf16[2,2,2,256,256]{4,3,2,1,0:T(8,128)(2,1)}) custom-call(s32[4]{0:T(128)S(1)} %get-tuple-element.65.widths, bf16[2,256,256]{2,1,0:T(8,128)(2,1)S(1)} %bitcast.4, bf16[2,256,256]{2,1,0:T(8,128)(2,1)S(1)} %collective-permute-done.refs_1_, ...), custom_call_target="tpu_custom_call" | custom-call | flops 268435456 | bytes 4194304 | tf_op jit(solution)/shard_map/pallas_call | solution.py:113
  36.6 3.5 %collective-permute-done.13.refs_6_ = bf16[256,256]{1,0:T(8,128)(2,1)S(1)} collective-permute-done((bf16[256,256]{1,0:T(8,128)(2,1)S(1)}, bf16[256,256]{1,0:T(8,128)(2,1)S(1)}, u32[]{:S(2)}, u32[]{:S(2)}) %collective-permute-start.13) | collective-permute-done | bytes 131104 | tf_op jit(solution)/shard_map/ppermute | solution.py:142
  40.0 0.0 collective-permute-done.12.refs_8_
  40.0 0.8 %collective-permute-done.11.refs_3_ = bf16[2,256,256]{2,1,0:T(8,128)(2,1)S(1)} collective-permute-done((bf16[2,256,256]{2,1,0:T(8,128)(2,1)S(1)}, bf16[2,256,256]{2,1,0:T(8,128)(2,1)S(1)}, u32[]{:S(2)}, u32[]{:S(2)}) %collective-permute-start.11) | collective-permute-done | bytes 262176 | tf_op jit(solution)/shard_map/ppermute | solution.py:146
  40.9 2.3 %shard_map.106 = (bf16[4,256,256]{2,1,0:T(8,128)(2,1)S(1)}, bf16[4,256,256]{2,1,0:T(8,128)(2,1)S(1)}, bf16[2,2,2,256,256]{4,3,2,1,0:T(8,128)(2,1)}) custom-call(s32[16]{0:T(128)S(1)} %get-tuple-element.64.src, s32[4]{0:T(128)S(1)} %get-tuple-element.65.widths, bf16[2,256,256]{2,1,0:T(8,128)(2,1)S(1)} %collective-permute-done.5.refs_0_, ...), custom_call_target="tpu_custom_call" | custom-call | flops 1073741824 | bytes 6291456 | tf_op jit(solution)/shard_map/pallas_call | solution.py:113
  43.1 0.0 copy-start.1
  43.2 0.1 collective-permute-start.14
  43.2 1.9 %collective-permute-done.14.other = bf16[4,256,256]{2,1,0:T(8,128)(2,1)S(1)} collective-permute-done((bf16[4,256,256]{2,1,0:T(8,128)(2,1)S(1)}, bf16[4,256,256]{2,1,0:T(8,128)(2,1)S(1)}, u32[]{:S(2)}, u32[]{:S(2)}) %collective-permute-start.14) | collective-permute-done | bytes 524320 | tf_op jit(solution)/shard_map/ppermute | solution.py:146
  45.1 0.0 copy-done.1
  45.1 0.5 shard_map.107
  45.6 0.9 %collective-permute-start.15 = (bf16[2,4,64,256]{3,2,1,0:T(8,128)(2,1)S(1)}, bf16[2,4,64,256]{3,2,1,0:T(8,128)(2,1)S(1)}, u32[]{:S(2)}, u32[]{:S(2)}) collective-permute-start(bf16[2,4,64,256]{3,2,1,0:T(8,128)(2,1)S(1)} %get-tuple-element.90), channel_id=1, source_target_pairs={{0,2},{1,3},{2,0},{3,1},{4,6},{5,7},{6,4},{7,5},{8,10},{9,11},{10,... | collective-permute-start | bytes 786440 | tf_op jit(solution)/shard_map/ppermute | solution.py:146
  46.5 9.7 %all_to_all.10.refs_2_.parts.parts1 = f32[16,8,128]{2,1,0:T(8,128)S(1)} all-to-all(f32[16,8,128]{2,1,0:T(8,128)S(1)} %get-tuple-element.88), channel_id=1, replica_groups=mesh['grp'=2,'blk'=4,'op'=4] {'blk','op'}, dimensions={0} | all-to-all | bytes 131072 | tf_op jit(solution)/shard_map/all_to_all | solution.py:619
  56.3 0.0 collective-permute-done.15.refs_1_
  56.3 4.1 %shard_map.108 = (bf16[4,256,256]{2,1,0:T(8,128)(2,1)S(1)}, bf16[4,256,256]{2,1,0:T(8,128)(2,1)S(1)}, f32[1,8,128]{2,1,0:T(8,128)S(1)}) custom-call(s32[16]{0:T(128)S(1)} %get-tuple-element.64.src, s32[4]{0:T(128)S(1)} %get-tuple-element.65.widths, bf16[2,2,2,256,256]{4,3,2,1,0:T(8,128)(2,1)} %get-tuple-element.92.left_early, ...), custom_call_target="tpu_custom_call" | custom-call | flops 1073741824 | bytes 6291456 | tf_op jit(solution)/shard_map/pallas_call | solution.py:113
  60.4 0.1 collective-permute-start.16
  60.5 1.9 %collective-permute-done.16.other = bf16[4,256,256]{2,1,0:T(8,128)(2,1)S(1)} collective-permute-done((bf16[4,256,256]{2,1,0:T(8,128)(2,1)S(1)}, bf16[4,256,256]{2,1,0:T(8,128)(2,1)S(1)}, u32[]{:S(2)}, u32[]{:S(2)}) %collective-permute-start.16) | collective-permute-done | bytes 524320 | tf_op jit(solution)/shard_map/ppermute | solution.py:146
  62.4 0.7 shard_map.109
  63.1 0.2 collective-permute-start.17
  63.3 11.0 %all_to_all.11.parts2 = f32[16,16,128]{2,1,0:T(8,128)S(1)} all-to-all(f32[16,16,128]{2,1,0:T(8,128)S(1)} %get-tuple-element.98), channel_id=1, replica_groups=mesh['grp'=2,'blk'=4,'op'=4] {'blk','op'}, dimensions={0} | all-to-all | bytes 262144 | tf_op jit(solution)/shard_map/all_to_all | solution.py:619
  74.3 0.0 collective-permute-done.17.refs_3_
  74.3 1.7 %shard_map.110 = (bf16[4,64,512]{2,1,0:T(8,128)(2,1)}, bf16[4,64,512]{2,1,0:T(8,128)(2,1)}, f32[1]{0:T(128)}) custom-call(s32[4]{0:T(128)S(1)} %get-tuple-element.63.slots, f32[16,8,128]{2,1,0:T(8,128)S(1)} %all_to_all.10.refs_2_.parts.parts1, f32[16,16,128]{2,1,0:T(8,128)S(1)} %all_to_all.11.parts2, bf16[2,4,64,256]{3,2,1,0:T(8,128)(2,1)S(1)} %get-tuple-element.99.refs_0_, ...), custom_call_target="tpu_custom_call" | custom-call | bytes 4194304 | tf_op jit(solution)/shard_map/pallas_call | solution.py:113
Async XLA Ops:
  0.6 4.6 %copy-start.3 = (s32[2]{0:T(128)S(1)}, s32[2]{0:T(128)}, u32[]{:S(2)}) copy-start(s32[2]{0:T(128)} %shift.1) | copy-start | bytes 28
  0.6 12.6 %collective-permute-start.1 = (bf16[2,256,256]{2,1,0:T(8,128)(2,1)}, bf16[2,256,256]{2,1,0:T(8,128)(2,1)S(1)}, u32[]{:S(2)}, u32[]{:S(2)}) collective-permute-start(bf16[2,256,256]{2,1,0:T(8,128)(2,1)} %bitcast.2), channel_id=1, source_target_pairs={{0,4},{4,12},{12,8},{8,0},{1,5},{5,13},{13,9},{9,1},{2,6},{6,14},{... | collective-permute-start | bytes 786440 | tf_op jit(solution)/shard_map/ppermute | solution.py:142
  3.7 9.6 %collective-permute-start = (bf16[2,256,256]{2,1,0:T(8,128)(2,1)}, bf16[2,256,256]{2,1,0:T(8,128)(2,1)S(1)}, u32[]{:S(2)}, u32[]{:S(2)}) collective-permute-start(bf16[2,256,256]{2,1,0:T(8,128)(2,1)} %bitcast.3), channel_id=1, source_target_pairs={{0,2},{1,3},{2,0},{3,1},{4,6},{5,7},{6,4},{7,5},{8,10},{9,11},{10,... | collective-permute-start | bytes 786440 | tf_op jit(solution)/shard_map/ppermute | solution.py:146
  5.2 1.1 %collective-permute-start.2 = (s32[2]{0:T(128)S(1)}, s32[2]{0:T(128)S(1)}, u32[]{:S(2)}, u32[]{:S(2)}) collective-permute-start(s32[2]{0:T(128)S(1)} %copy-done.3), channel_id=1, source_target_pairs={{0,1},{1,0},{2,3},{3,2},{4,5},{5,4},{6,7},{7,6},{8,9},{9,8},{10,11... | collective-permute-start | bytes 32 | tf_op jit(solution)/shard_map/ppermute | solution.py:146
  6.3 28.6 %copy-start = (bf16[2,1,256,256]{3,2,1,0:T(8,128)(2,1)S(1)}, bf16[2,1,256,256]{3,2,1,0:T(8,128)(2,1)}, u32[]{:S(2)}) copy-start(bf16[2,1,256,256]{3,2,1,0:T(8,128)(2,1)} %param.9) | copy-start | bytes 786436
  8.2 9.6 %copy-start.2 = (f32[4,256]{1,0:T(4,128)S(1)}, f32[4,256]{1,0:T(4,128)}, u32[]{:S(2)}) copy-start(f32[4,256]{1,0:T(4,128)} %left_diag.1) | copy-start | bytes 12292
  8.3 5.0 %collective-permute-start.3 = (bf16[144,256]{1,0:T(8,128)(2,1)S(1)}, bf16[144,256]{1,0:T(8,128)(2,1)S(1)}, u32[]{:S(2)}, u32[]{:S(2)}) collective-permute-start(bf16[144,256]{1,0:T(8,128)(2,1)S(1)} %get-tuple-element.54), channel_id=1, source_target_pairs={{0,2},{1,3},{2,0},{3,1},{4,6},{5,7},{6,4},{7,5},{8,10},{9,11},{10,... | collective-permute-start | bytes 221192 | tf_op jit(solution)/shard_map/ppermute | solution.py:146
  13.3 4.6 %copy-start.4 = (s32[4]{0:T(128)S(1)}, s32[4]{0:T(128)}, u32[]{:S(2)}) copy-start(s32[4]{0:T(128)} %sector.1) | copy-start | bytes 52
  13.3 4.6 %copy-start.5 = (s32[4]{0:T(128)S(1)}, s32[4]{0:T(128)}, u32[]{:S(2)}) copy-start(s32[4]{0:T(128)} %width.1) | copy-start | bytes 52
  13.3 10.2 %collective-permute-start.5 = (bf16[2,256,256]{2,1,0:T(8,128)(2,1)S(1)}, bf16[2,256,256]{2,1,0:T(8,128)(2,1)S(1)}, u32[]{:S(2)}, u32[]{:S(2)}) collective-permute-start(bf16[2,256,256]{2,1,0:T(8,128)(2,1)S(1)} %collective-permute-done.1.refs_2_), channel_id=1, source_target_pairs={{0,4},{4,12},{12,8},{8,0},{1,5},{5,13},{13,9},{9,1},{2,6},{6,14},{... | collective-permute-start | bytes 786440 | tf_op jit(solution)/shard_map/ppermute | solution.py:142
  15.9 7.5 %collective-permute-start.4 = (bf16[2,256,256]{2,1,0:T(8,128)(2,1)S(1)}, bf16[2,256,256]{2,1,0:T(8,128)(2,1)S(1)}, u32[]{:S(2)}, u32[]{:S(2)}) collective-permute-start(bf16[2,256,256]{2,1,0:T(8,128)(2,1)S(1)} %collective-permute-done.1.refs_2_), channel_id=1, source_target_pairs={{0,2},{1,3},{2,0},{3,1},{4,6},{5,7},{6,4},{7,5},{8,10},{9,11},{10,... | collective-permute-start | bytes 786440 | tf_op jit(solution)/shard_map/ppermute | solution.py:146
  17.4 6.0 %collective-permute-start.6 = (bf16[256,128]{1,0:T(8,128)(2,1)S(1)}, bf16[256,128]{1,0:T(8,128)(2,1)S(1)}, u32[]{:S(2)}, u32[]{:S(2)}) collective-permute-start(bf16[256,128]{1,0:T(8,128)(2,1)S(1)} %get-tuple-element.56), channel_id=1, source_target_pairs={{0,4},{4,12},{12,8},{8,0},{1,5},{5,13},{13,9},{9,1},{2,6},{6,14},{... | collective-permute-start | bytes 196616 | tf_op jit(solution)/shard_map/ppermute | solution.py:142
  23.5 9.3 %collective-permute-start.8 = (bf16[2,256,256]{2,1,0:T(8,128)(2,1)S(1)}, bf16[2,256,256]{2,1,0:T(8,128)(2,1)S(1)}, u32[]{:S(2)}, u32[]{:S(2)}) collective-permute-start(bf16[2,256,256]{2,1,0:T(8,128)(2,1)S(1)} %collective-permute-done.5.refs_0_), channel_id=1, source_target_pairs={{0,4},{4,12},{12,8},{8,0},{1,5},{5,13},{13,9},{9,1},{2,6},{6,14},{... | collective-permute-start | bytes 786440 | tf_op jit(solution)/shard_map/ppermute | solution.py:142
  25.2 7.6 %collective-permute-start.7 = (bf16[2,256,256]{2,1,0:T(8,128)(2,1)S(1)}, bf16[2,256,256]{2,1,0:T(8,128)(2,1)S(1)}, u32[]{:S(2)}, u32[]{:S(2)}) collective-permute-start(bf16[2,256,256]{2,1,0:T(8,128)(2,1)S(1)} %collective-permute-done.5.refs_0_), channel_id=1, source_target_pairs={{0,2},{1,3},{2,0},{3,1},{4,6},{5,7},{6,4},{7,5},{8,10},{9,11},{10,... | collective-permute-start | bytes 786440 | tf_op jit(solution)/shard_map/ppermute | solution.py:146
  25.7 6.9 %collective-permute-start.10 = (bf16[256,128]{1,0:T(8,128)(2,1)S(1)}, bf16[256,128]{1,0:T(8,128)(2,1)S(1)}, u32[]{:S(2)}, u32[]{:S(2)}) collective-permute-start(bf16[256,128]{1,0:T(8,128)(2,1)S(1)} %get-tuple-element.68), channel_id=1, source_target_pairs={{0,8},{4,0},{12,4},{8,12},{1,9},{5,1},{13,5},{9,13},{2,10},{6,2},{... | collective-permute-start | bytes 196616 | tf_op jit(solution)/shard_map/ppermute | solution.py:142
  26.9 5.7 %collective-permute-start.9 = (bf16[256,128]{1,0:T(8,128)(2,1)S(1)}, bf16[256,128]{1,0:T(8,128)(2,1)S(1)}, u32[]{:S(2)}, u32[]{:S(2)}) collective-permute-start(bf16[256,128]{1,0:T(8,128)(2,1)S(1)} %collective-permute-done.6.refs_5_), channel_id=1, source_target_pairs={{0,1},{1,0},{2,3},{3,2},{4,5},{5,4},{6,7},{7,6},{8,9},{9,8},{10,11... | collective-permute-start | bytes 196616 | tf_op jit(solution)/shard_map/ppermute | solution.py:146
  32.8 8.1 %collective-permute-start.11 = (bf16[2,256,256]{2,1,0:T(8,128)(2,1)S(1)}, bf16[2,256,256]{2,1,0:T(8,128)(2,1)S(1)}, u32[]{:S(2)}, u32[]{:S(2)}) collective-permute-start(bf16[2,256,256]{2,1,0:T(8,128)(2,1)S(1)} %collective-permute-done.8.refs_2_), channel_id=1, source_target_pairs={{0,2},{1,3},{2,0},{3,1},{4,6},{5,7},{6,4},{7,5},{8,10},{9,11},{10,... | collective-permute-start | bytes 786440 | tf_op jit(solution)/shard_map/ppermute | solution.py:146
  32.8 7.3 %collective-permute-start.13 = (bf16[256,256]{1,0:T(8,128)(2,1)S(1)}, bf16[256,256]{1,0:T(8,128)(2,1)S(1)}, u32[]{:S(2)}, u32[]{:S(2)}) collective-permute-start(bf16[256,256]{1,0:T(8,128)(2,1)S(1)} %get-tuple-element.79), channel_id=1, source_target_pairs={{0,12},{4,8},{12,0},{8,4},{1,13},{5,9},{13,1},{9,5},{2,14},{6,10},... | collective-permute-start | bytes 393224 | tf_op jit(solution)/shard_map/ppermute | solution.py:142
  34.9 5.1 %collective-permute-start.12 = (bf16[256,128]{1,0:T(8,128)(2,1)S(1)}, bf16[256,128]{1,0:T(8,128)(2,1)S(1)}, u32[]{:S(2)}, u32[]{:S(2)}) collective-permute-start(bf16[256,128]{1,0:T(8,128)(2,1)S(1)} %collective-permute-done.10.refs_7_), channel_id=1, source_target_pairs={{0,1},{1,0},{2,3},{3,2},{4,5},{5,4},{6,7},{7,6},{8,9},{9,8},{10,11... | collective-permute-start | bytes 196616 | tf_op jit(solution)/shard_map/ppermute | solution.py:146
  43.1 2.0 %copy-start.1 = (f32[512]{0:T(512)S(1)}, f32[512]{0:T(512)}, u32[]{:S(2)}) copy-start(f32[512]{0:T(512)} %param.15) | copy-start | bytes 6148
  43.2 2.0 %collective-permute-start.14 = (bf16[4,256,256]{2,1,0:T(8,128)(2,1)S(1)}, bf16[4,256,256]{2,1,0:T(8,128)(2,1)S(1)}, u32[]{:S(2)}, u32[]{:S(2)}) collective-permute-start(bf16[4,256,256]{2,1,0:T(8,128)(2,1)S(1)} %get-tuple-element.85.mine), channel_id=1, source_target_pairs={{0,1},{1,0},{2,3},{3,2},{4,5},{5,4},{6,7},{7,6},{8,9},{9,8},{10,11... | collective-permute-start | bytes 1572872 | tf_op jit(solution)/shard_map/ppermute | solution.py:146
  45.6 10.7 %collective-permute-start.15 = (bf16[2,4,64,256]{3,2,1,0:T(8,128)(2,1)S(1)}, bf16[2,4,64,256]{3,2,1,0:T(8,128)(2,1)S(1)}, u32[]{:S(2)}, u32[]{:S(2)}) collective-permute-start(bf16[2,4,64,256]{3,2,1,0:T(8,128)(2,1)S(1)} %get-tuple-element.90), channel_id=1, source_target_pairs={{0,2},{1,3},{2,0},{3,1},{4,6},{5,7},{6,4},{7,5},{8,10},{9,11},{10,... | collective-permute-start | bytes 786440 | tf_op jit(solution)/shard_map/ppermute | solution.py:146
  60.4 2.0 %collective-permute-start.16 = (bf16[4,256,256]{2,1,0:T(8,128)(2,1)S(1)}, bf16[4,256,256]{2,1,0:T(8,128)(2,1)S(1)}, u32[]{:S(2)}, u32[]{:S(2)}) collective-permute-start(bf16[4,256,256]{2,1,0:T(8,128)(2,1)S(1)} %get-tuple-element.96.mine), channel_id=1, source_target_pairs={{0,1},{1,0},{2,3},{3,2},{4,5},{5,4},{6,7},{7,6},{8,9},{9,8},{10,11... | collective-permute-start | bytes 1572872 | tf_op jit(solution)/shard_map/ppermute | solution.py:146
  63.1 11.2 %collective-permute-start.17 = (bf16[2,4,64,256]{3,2,1,0:T(8,128)(2,1)S(1)}, bf16[2,4,64,256]{3,2,1,0:T(8,128)(2,1)S(1)}, u32[]{:S(2)}, u32[]{:S(2)}) collective-permute-start(bf16[2,4,64,256]{3,2,1,0:T(8,128)(2,1)S(1)} %get-tuple-element.102), channel_id=1, source_target_pairs={{0,2},{1,3},{2,0},{3,1},{4,6},{5,7},{6,4},{7,5},{8,10},{9,11},{10,... | collective-permute-start | bytes 786440 | tf_op jit(solution)/shard_map/ppermute | solution.py:146

commit v11 on v10

--- a/solution.py
+++ b/solution.py
@@ -408,20 +408,19 @@
 
 def sigma_body(mine, other, raw_in, diag, right_diag, sig_out, dots_out, *sends):
     n_blk, _, cols = diag.shape
-    sums = [jnp.zeros((8, cols), jnp.float32) for _ in range(2)]
+    sums = [[jnp.zeros((8, cols), jnp.float32) for _ in range(2)] for _ in range(2)]
     for d in range(n_blk):
         for h in range(2):
             part = slice(h * cols, (h + 1) * cols)
             raw = raw_in[d, :, part].astype(jnp.float32)
             sigma = total_of(mine, other, d, h, cols) + diagonal(diag, right_diag, d, h) * raw
             sig_out[d, :, part] = sigma
-            if h == 0:
-                sums = [sums[0] + fold(raw * raw), sums[1] + fold(raw * sigma)]
+            sums[h] = [sums[h][0] + fold(raw * raw), sums[h][1] + fold(raw * sigma)]
     for d in range(n_blk):
         for h in range(2):
             send_rows(sends, 0, d, h, raw_in.at[d, :, h * cols : (h + 1) * cols])
             send_rows(sends, 1, d, h, sig_out.at[d, :, h * cols : (h + 1) * cols])
-    spread([whole(x) for x in sums], dots_out)
+    spread([whole(x) + whole(y) for x, y in zip(*sums)], dots_out)
 
 
 def norm_theta(parts, count):
@@ -432,7 +431,7 @@
 
 def second_body(n_blk, n_pair, count, src, widths, left_early, left_late, *refs):
     right, refs = refs[:n_pair], refs[n_pair:]
-    parts, raw_in, sig_in, diag, right_diag, f_out, part_out, half_out = refs[:8]
+    parts, raw_in, sig_in, diag, right_diag, f_out, part_out, pair_out = refs[:8]
     inter, corr, held, sems = refs[8:]
     copies = []
     n_early = left_early.shape[0]
@@ -455,7 +454,8 @@
             corr[d, :, part] = item
             vv, vc, vs = vv + fold(vec * vec), vc + fold(vec * item), vs + fold(vec * sigma)
         halves.append((whole(vv), whole(vc), whole(vs)))
-    along = (halves[0][1] + halves[1][1]) / jnp.maximum(halves[0][0] + halves[1][0], 1e-30)
+    vv, vc, vs = (x + y for x, y in zip(*halves))
+    along = vc / jnp.maximum(vv, 1e-30)
     terms = held.shape[2]
     for d in range(n_blk):
         for h in range(2):
@@ -465,13 +465,13 @@
         copies[d].wait()
         left_products(f_out[d], lambda at: held[d, at // terms], inter.at[d])
     sum_terms(src, widths, inter, right, part_out)
-    spread(halves[0] + (along,), half_out)
-
-
-def image_body(count, half, parts, mine, other, raw_in, sig_in, f_in, diag, right_diag, dots_out, *sends):
+    spread((vv, vc, vs, along), pair_out)
+
+
+def image_body(count, pair, parts, mine, other, raw_in, sig_in, f_in, diag, right_diag, dots_out, *sends):
     n_blk, _, cols = diag.shape
     scale, _ = norm_theta(parts[...], count)
-    sums = [jnp.zeros((8, cols), jnp.float32) for _ in range(5)]
+    sums = [[jnp.zeros((8, cols), jnp.float32) for _ in range(5)] for _ in range(2)]
     for d in range(n_blk):
         for h in range(2):
             part = slice(h * cols, (h + 1) * cols)
@@ -480,13 +480,12 @@
             sends[-1][h] = image
             send_rows(sends[:-1], 0, d, h, f_in.at[d, :, part])
             send_rows(sends[:-1], 1, d, h, sends[-1].at[h])
-            if h == 0:
-                vec = raw_in[d, :, part].astype(jnp.float32) * scale
-                sigma = sig_in[d, :, part] * scale
-                prods = (fld * fld, vec * fld, vec * image, fld * sigma, fld * image)
-                sums = [one + fold(prod) for one, prod in zip(sums, prods)]
-    known = [half[0, j : j + 1] for j in range(4)]
-    spread(known + [whole(x) for x in sums], dots_out)
+            vec = raw_in[d, :, part].astype(jnp.float32) * scale
+            sigma = sig_in[d, :, part] * scale
+            prods = (fld * fld, vec * fld, vec * image, fld * sigma, fld * image)
+            sums[h] = [one + fold(prod) for one, prod in zip(sums[h], prods)]
+    known = [pair[0, j : j + 1] for j in range(4)]
+    spread(known + [whole(x) + whole(y) for x, y in zip(*sums)], dots_out)
 
 
 def ritz_pair(theta, h_mix, h_two):
@@ -528,7 +527,7 @@
     cu = cu * unit
     for e in range(n_pair):
         there = own_op ^ (2 * e)
-        back = parts2[own_blk * n_op + there][3:4] - along
+        back = parts2[own_blk * n_pair + there // 2][3:4] - along
         on_vec = (cv + cu * back) * scale
         for h in range(2):
             at = pl.multiple_of((there ^ h) * cols, LANES)
@@ -552,7 +551,7 @@
     cols = diag_right.shape[0] // n_op
     step = rows // n_op
     count = float(n_blk * rows * ncols)
-    n_dev = n_blk * n_op
+    n_sum = n_blk * n_pair
     bf16, f32, i32 = jnp.bfloat16, jnp.float32, jnp.int32
     last = sorted(range(1, n_blk), key=lambda d: min(d, n_blk - d))[-1]
 
@@ -616,7 +615,8 @@
     cost = dict(flops=2 * n_blk * rows * 2 * cols * terms * n_pair * (rows + 2 * cols), nbytes=6 << 20)
 
     def totals(parts):
-        return lax.all_to_all(parts, ("blk", "op"), 0, 0, tiled=True)
+        groups = [list(range(bit, n_blk * n_op, 2)) for bit in range(2)]
+        return lax.all_to_all(parts, ("blk", "op"), 0, 0, axis_index_groups=groups, tiled=True)
 
     def exchange(out):
         return [out[0]] + [swap(block, 2 * e, n_op) for e, block in enumerate(out[1:], 1)]
@@ -631,11 +631,11 @@
     sig, dots1, *out1 = kernel(
         sigma_body,
         [(x, VMEM) for x in (part1, swap(part1, 1, n_op), raw)] + diags,
-        [wide, ((n_dev, 8, LANES), f32, VMEM)] + sends,
+        [wide, ((n_sum, 8, LANES), f32, VMEM)] + sends,
         nbytes=4 << 20,
     )
     parts1, got1 = lax.optimization_barrier((totals(dots1), exchange(out1)))
-    fld, part2, half = kernel(
+    fld, part2, pair = kernel(
         functools.partial(second_body, n_blk, n_pair, count),
         tables + [(left_early, HBM), (kept, HBM)] + right_ins + [(x, VMEM) for x in (parts1, raw, sig)] + diags,
         [narrow, narrow, ((1, 8, LANES), f32, VMEM)],
@@ -649,8 +649,8 @@
     )
     dots2, *out2 = kernel(
         functools.partial(image_body, count),
-        [(x, VMEM) for x in (half, parts1, part2, swap(part2, 1, n_op), raw, sig, fld)] + diags,
-        [((n_dev, 16, LANES), f32, VMEM)] + sends,
+        [(x, VMEM) for x in (pair, parts1, part2, swap(part2, 1, n_op), raw, sig, fld)] + diags,
+        [((n_sum, 16, LANES), f32, VMEM)] + sends,
         [pltpu.VMEM((2, rows, cols), f32)],
         nbytes=4 << 20,
     )

time: 76.2 us -> 74.6 us (0.979)
  blocking collectives: 20.8 us -> 19 us
    all_to_all x2, blocking collectives: 20.8 us -> 19 us  [totals(): lax.all_to_all(parts, ('blk', 'op'), 0, 0, axis_index_groups=groups, tile...]
  transfers between devices with their start and end apart: 18 -> 18, of which waited for: 9 -> 9; matrix products, arithmetic and copies ran while one was open for 0% -> 0% of each run, Pallas kernels for 6% -> 7%
where the time goes in v11:
time: 74.6 us; the launch traced here: 74.3 us
  waiting for transfers between devices  23.7 us (32%)
  blocking collectives  19 us (25%)
  starting transfers between devices  16.9 us (23%)
  Pallas kernels  14 us (19%)
  between operations  0.76 us (1%)
    all_to_all x2, blocking collectives, totals(): lax.all_to_all(parts, ('blk', 'op'), 0, 0, axis_index_groups=groups, tile...  19 us
    pallas_call x8, Pallas kernels, kernel(): pl.pallas_call(body, out_shape=[HBM(shape, dtype) if space == HBM else ja...  14 us
    ppermute x6, waiting for transfers between devices, onward(): return lax.ppermute(block, 'blk', pairs)  13.5 us
    ppermute x6, starting transfers between devices, onward(): return lax.ppermute(block, 'blk', pairs)  11.2 us
    ppermute x12, waiting for transfers between devices, swap(): return lax.ppermute(block, 'op', [(i, i ^ e) for i in range(n_op)])  10.2 us
    ppermute x12, starting transfers between devices, swap(): return lax.ppermute(block, 'op', [(i, i ^ e) for i in range(n_op)])  5.7 us
  transfers between devices with their start and end apart: 18, of which 9 were waited for; matrix products, arithmetic and copies ran while one was open for 0% of the time, Pallas kernels for 7%

profile of v11, /device:TPU:0, one launch (start us, length us, event | category | flops | bytes accessed | tf_op | source)
XLA Modules:
  0.0 74.3 jit_solution(6010998207462224034)
XLA Ops:
  0.6 0.0 copy-start.3
  0.6 3.1 %collective-permute-start.1 = (bf16[2,256,256]{2,1,0:T(8,128)(2,1)}, bf16[2,256,256]{2,1,0:T(8,128)(2,1)S(1)}, u32[]{:S(2)}, u32[]{:S(2)}) collective-permute-start(bf16[2,256,256]{2,1,0:T(8,128)(2,1)} %bitcast.2), channel_id=1, source_target_pairs={{0,4},{4,12},{12,8},{8,0},{1,5},{5,13},{13,9},{9,1},{2,6},{6,14},{... | collective-permute-start | bytes 786440 | tf_op jit(solution)/shard_map/ppermute | solution.py:142
  3.7 1.5 %collective-permute-start = (bf16[2,256,256]{2,1,0:T(8,128)(2,1)}, bf16[2,256,256]{2,1,0:T(8,128)(2,1)S(1)}, u32[]{:S(2)}, u32[]{:S(2)}) collective-permute-start(bf16[2,256,256]{2,1,0:T(8,128)(2,1)} %bitcast.3), channel_id=1, source_target_pairs={{0,2},{1,3},{2,0},{3,1},{4,6},{5,7},{6,4},{7,5},{8,10},{9,11},{10,... | collective-permute-start | bytes 786440 | tf_op jit(solution)/shard_map/ppermute | solution.py:146
  5.2 0.0 copy-done.3
  5.2 0.0 collective-permute-start.2
  5.2 1.1 %collective-permute-done.2._ = s32[2]{0:T(128)S(1)} collective-permute-done((s32[2]{0:T(128)S(1)}, s32[2]{0:T(128)S(1)}, u32[]{:S(2)}, u32[]{:S(2)}) %collective-permute-start.2) | collective-permute-done | bytes 40 | tf_op jit(solution)/shard_map/ppermute | solution.py:146
  6.3 0.0 copy-start
  6.3 1.9 %shard_map.103 = (bf16[256,256]{1,0:T(8,128)(2,1)S(1)}, bf16[256,128]{1,0:T(8,128)(2,1)S(1)}, bf16[256,256]{1,0:T(8,128)(2,1)S(1)}, bf16[256,128]{1,0:T(8,128)(2...) custom-call(s32[2]{0:T(128)S(1)} %copy-done.3, s32[2]{0:T(128)S(1)} %collective-permute-done.2._, ...), custom_call_target="tpu_custom_call" | custom-call | bytes 1048576 | tf_op jit(solution)/shard_map/pallas_call | solution.py:113
  8.2 0.0 copy-start.2
  8.3 0.6 collective-permute-start.3
  8.9 4.4 %collective-permute-done.3.refs_1_.refs_5_ = bf16[144,256]{1,0:T(8,128)(2,1)S(1)} collective-permute-done((bf16[144,256]{1,0:T(8,128)(2,1)S(1)}, bf16[144,256]{1,0:T(8,128)(2,1)S(1)}, u32[]{:S(2)}, u32[]{:S(2)}) %collective-permute-start.3) | collective-permute-done | bytes 73760 | tf_op jit(solution)/shard_map/ppermute | solution.py:146
  13.3 0.0 collective-permute-done.1.refs_2_
  13.3 0.0 collective-permute-done.refs_1_
  13.3 0.0 copy-start.4
  13.3 0.0 copy-start.5
  13.3 2.6 %collective-permute-start.5 = (bf16[2,256,256]{2,1,0:T(8,128)(2,1)S(1)}, bf16[2,256,256]{2,1,0:T(8,128)(2,1)S(1)}, u32[]{:S(2)}, u32[]{:S(2)}) collective-permute-start(bf16[2,256,256]{2,1,0:T(8,128)(2,1)S(1)} %collective-permute-done.1.refs_2_), channel_id=1, source_target_pairs={{0,4},{4,12},{12,8},{8,0},{1,5},{5,13},{13,9},{9,1},{2,6},{6,14},{... | collective-permute-start | bytes 786440 | tf_op jit(solution)/shard_map/ppermute | solution.py:142
  15.9 1.5 %collective-permute-start.4 = (bf16[2,256,256]{2,1,0:T(8,128)(2,1)S(1)}, bf16[2,256,256]{2,1,0:T(8,128)(2,1)S(1)}, u32[]{:S(2)}, u32[]{:S(2)}) collective-permute-start(bf16[2,256,256]{2,1,0:T(8,128)(2,1)S(1)} %collective-permute-done.1.refs_2_), channel_id=1, source_target_pairs={{0,2},{1,3},{2,0},{3,1},{4,6},{5,7},{6,4},{7,5},{8,10},{9,11},{10,... | collective-permute-start | bytes 786440 | tf_op jit(solution)/shard_map/ppermute | solution.py:146
  17.4 0.4 collective-permute-start.6
  17.9 0.0 copy-done.2
  17.9 0.0 copy-done.4
  17.9 0.0 copy-done.5
  17.9 1.3 %shard_map.104 = (s32[16]{0:T(128)S(1)}, s32[4]{0:T(128)S(1)}, s32[4]{0:T(128)S(1)}, f32[4,256,128]{2,1,0:T(8,128)S(1)}) custom-call(s32[4]{0:T(128)S(1)} %copy-done.4, s32[4]{0:T(128)S(1)} %copy-done.5, f32[4,256]{1,0:T(4,128)S(1)} %copy-done.2, bf16[144,256]{1,0:T(8,128)(2,1)S(1)} %get-tuple-element.57.refs_0_.refs_4_, ...), custom_call_target="tpu_custom_call" | custom-call | tf_op jit(solution)/shard_map/pallas_call | solution.py:113
  19.2 4.2 %collective-permute-done.6.refs_5_ = bf16[256,128]{1,0:T(8,128)(2,1)S(1)} collective-permute-done((bf16[256,128]{1,0:T(8,128)(2,1)S(1)}, bf16[256,128]{1,0:T(8,128)(2,1)S(1)}, u32[]{:S(2)}, u32[]{:S(2)}) %collective-permute-start.6) | collective-permute-done | bytes 65568 | tf_op jit(solution)/shard_map/ppermute | solution.py:142
  23.5 0.0 collective-permute-done.5.refs_0_
  23.5 0.0 collective-permute-done.4.refs_3_
  23.5 1.7 %collective-permute-start.8 = (bf16[2,256,256]{2,1,0:T(8,128)(2,1)S(1)}, bf16[2,256,256]{2,1,0:T(8,128)(2,1)S(1)}, u32[]{:S(2)}, u32[]{:S(2)}) collective-permute-start(bf16[2,256,256]{2,1,0:T(8,128)(2,1)S(1)} %collective-permute-done.5.refs_0_), channel_id=1, source_target_pairs={{0,4},{4,12},{12,8},{8,0},{1,5},{5,13},{13,9},{9,1},{2,6},{6,14},{... | collective-permute-start | bytes 786440 | tf_op jit(solution)/shard_map/ppermute | solution.py:142
  25.2 0.5 collective-permute-start.7
  25.7 1.2 %collective-permute-start.10 = (bf16[256,128]{1,0:T(8,128)(2,1)S(1)}, bf16[256,128]{1,0:T(8,128)(2,1)S(1)}, u32[]{:S(2)}, u32[]{:S(2)}) collective-permute-start(bf16[256,128]{1,0:T(8,128)(2,1)S(1)} %get-tuple-element.68), channel_id=1, source_target_pairs={{0,8},{4,0},{12,4},{8,12},{1,9},{5,1},{13,5},{9,13},{2,10},{6,2},{... | collective-permute-start | bytes 196616 | tf_op jit(solution)/shard_map/ppermute | solution.py:142
  26.9 0.0 collective-permute-start.9
  26.9 5.7 %collective-permute-done.10.refs_7_ = bf16[256,128]{1,0:T(8,128)(2,1)S(1)} collective-permute-done((bf16[256,128]{1,0:T(8,128)(2,1)S(1)}, bf16[256,128]{1,0:T(8,128)(2,1)S(1)}, u32[]{:S(2)}, u32[]{:S(2)}) %collective-permute-start.10) | collective-permute-done | bytes 65568 | tf_op jit(solution)/shard_map/ppermute | solution.py:142
  32.6 0.0 collective-permute-done.9.refs_6_
  32.6 0.1 collective-permute-done.8.refs_2_
  32.7 0.0 collective-permute-done.7.refs_1_
  32.8 0.0 collective-permute-start.11
  32.8 2.2 %collective-permute-start.13 = (bf16[256,256]{1,0:T(8,128)(2,1)S(1)}, bf16[256,256]{1,0:T(8,128)(2,1)S(1)}, u32[]{:S(2)}, u32[]{:S(2)}) collective-permute-start(bf16[256,256]{1,0:T(8,128)(2,1)S(1)} %get-tuple-element.79), channel_id=1, source_target_pairs={{0,12},{4,8},{12,0},{8,4},{1,13},{5,9},{13,1},{9,5},{2,14},{6,10},... | collective-permute-start | bytes 393224 | tf_op jit(solution)/shard_map/ppermute | solution.py:142
  34.9 0.0 collective-permute-start.12
  34.9 0.0 copy-done
  34.9 1.7 %shard_map.105 = (bf16[2,256,256]{2,1,0:T(8,128)(2,1)S(1)}, bf16[2,4,256,256]{3,2,1,0:T(8,128)(2,1)S(1)}, bf16[2,2,2,256,256]{4,3,2,1,0:T(8,128)(2,1)}) custom-call(s32[4]{0:T(128)S(1)} %get-tuple-element.65.widths, bf16[2,256,256]{2,1,0:T(8,128)(2,1)S(1)} %bitcast.4, bf16[2,256,256]{2,1,0:T(8,128)(2,1)S(1)} %collective-permute-done.refs_1_, ...), custom_call_target="tpu_custom_call" | custom-call | flops 268435456 | bytes 4194304 | tf_op jit(solution)/shard_map/pallas_call | solution.py:113
  36.6 3.5 %collective-permute-done.13.refs_6_ = bf16[256,256]{1,0:T(8,128)(2,1)S(1)} collective-permute-done((bf16[256,256]{1,0:T(8,128)(2,1)S(1)}, bf16[256,256]{1,0:T(8,128)(2,1)S(1)}, u32[]{:S(2)}, u32[]{:S(2)}) %collective-permute-start.13) | collective-permute-done | bytes 131104 | tf_op jit(solution)/shard_map/ppermute | solution.py:142
  40.0 0.0 collective-permute-done.12.refs_8_
  40.0 0.8 %collective-permute-done.11.refs_3_ = bf16[2,256,256]{2,1,0:T(8,128)(2,1)S(1)} collective-permute-done((bf16[2,256,256]{2,1,0:T(8,128)(2,1)S(1)}, bf16[2,256,256]{2,1,0:T(8,128)(2,1)S(1)}, u32[]{:S(2)}, u32[]{:S(2)}) %collective-permute-start.11) | collective-permute-done | bytes 262176 | tf_op jit(solution)/shard_map/ppermute | solution.py:146
  40.9 2.3 %shard_map.106 = (bf16[4,256,256]{2,1,0:T(8,128)(2,1)S(1)}, bf16[4,256,256]{2,1,0:T(8,128)(2,1)S(1)}, bf16[2,2,2,256,256]{4,3,2,1,0:T(8,128)(2,1)}) custom-call(s32[16]{0:T(128)S(1)} %get-tuple-element.64.src, s32[4]{0:T(128)S(1)} %get-tuple-element.65.widths, bf16[2,256,256]{2,1,0:T(8,128)(2,1)S(1)} %collective-permute-done.5.refs_0_, ...), custom_call_target="tpu_custom_call" | custom-call | flops 1073741824 | bytes 6291456 | tf_op jit(solution)/shard_map/pallas_call | solution.py:113
  43.1 0.0 copy-start.1
  43.2 0.1 collective-permute-start.14
  43.2 1.9 %collective-permute-done.14.other = bf16[4,256,256]{2,1,0:T(8,128)(2,1)S(1)} collective-permute-done((bf16[4,256,256]{2,1,0:T(8,128)(2,1)S(1)}, bf16[4,256,256]{2,1,0:T(8,128)(2,1)S(1)}, u32[]{:S(2)}, u32[]{:S(2)}) %collective-permute-start.14) | collective-permute-done | bytes 524320 | tf_op jit(solution)/shard_map/ppermute | solution.py:146
  45.1 0.0 copy-done.1
  45.1 0.5 shard_map.107
  45.7 0.9 %collective-permute-start.15 = (bf16[2,4,64,256]{3,2,1,0:T(8,128)(2,1)S(1)}, bf16[2,4,64,256]{3,2,1,0:T(8,128)(2,1)S(1)}, u32[]{:S(2)}, u32[]{:S(2)}) collective-permute-start(bf16[2,4,64,256]{3,2,1,0:T(8,128)(2,1)S(1)} %get-tuple-element.90), channel_id=1, source_target_pairs={{0,2},{1,3},{2,0},{3,1},{4,6},{5,7},{6,4},{7,5},{8,10},{9,11},{10,... | collective-permute-start | bytes 786440 | tf_op jit(solution)/shard_map/ppermute | solution.py:146
  46.6 9.4 %all_to_all.10.refs_2_.parts.parts1 = f32[8,8,128]{2,1,0:T(8,128)S(1)} all-to-all(f32[8,8,128]{2,1,0:T(8,128)S(1)} %get-tuple-element.88), channel_id=1, replica_groups={{0,2,4,6,8,10,12,14},{1,3,5,7,9,11,13,15},{16,18,20,22,24,26,28,30},{17..., dimensions={0} | all-to-all | bytes 65536 | tf_op jit(solution)/shard_map/all_to_all | solution.py:619
  56.0 0.0 collective-permute-done.15.refs_1_
  56.0 3.6 %shard_map.108 = (bf16[4,256,256]{2,1,0:T(8,128)(2,1)S(1)}, bf16[4,256,256]{2,1,0:T(8,128)(2,1)S(1)}, f32[1,8,128]{2,1,0:T(8,128)S(1)}) custom-call(s32[16]{0:T(128)S(1)} %get-tuple-element.64.src, s32[4]{0:T(128)S(1)} %get-tuple-element.65.widths, bf16[2,2,2,256,256]{4,3,2,1,0:T(8,128)(2,1)} %get-tuple-element.92.left_early, ...), custom_call_target="tpu_custom_call" | custom-call | flops 1073741824 | bytes 6291456 | tf_op jit(solution)/shard_map/pallas_call | solution.py:113
  59.6 0.1 collective-permute-start.16
  59.7 1.9 %collective-permute-done.16.other = bf16[4,256,256]{2,1,0:T(8,128)(2,1)S(1)} collective-permute-done((bf16[4,256,256]{2,1,0:T(8,128)(2,1)S(1)}, bf16[4,256,256]{2,1,0:T(8,128)(2,1)S(1)}, u32[]{:S(2)}, u32[]{:S(2)}) %collective-permute-start.16) | collective-permute-done | bytes 524320 | tf_op jit(solution)/shard_map/ppermute | solution.py:146
  61.6 1.0 %shard_map.109 = (f32[8,16,128]{2,1,0:T(8,128)S(1)}, bf16[2,4,64,256]{3,2,1,0:T(8,128)(2,1)S(1)}, bf16[2,4,64,256]{3,2,1,0:T(8,128)(2,1)S(1)}) custom-call(f32[1,8,128]{2,1,0:T(8,128)S(1)} %get-tuple-element.95.pair, f32[8,8,128]{2,1,0:T(8,128)S(1)} %all_to_all.10.refs_2_.parts.parts1, bf16[4,256,256]{2,1,0:T(8,128)(2,1)S(1)} %get-tuple-element.96.mine, ...), custom_call_target="tpu_custom_call" | custom-call | bytes 4194304 | tf_op jit(solution)/shard_map/pallas_call | solution.py:113
  62.6 0.5 collective-permute-start.17
  63.1 9.5 %all_to_all.11.parts2 = f32[8,16,128]{2,1,0:T(8,128)S(1)} all-to-all(f32[8,16,128]{2,1,0:T(8,128)S(1)} %get-tuple-element.98), channel_id=1, replica_groups={{0,2,4,6,8,10,12,14},{1,3,5,7,9,11,13,15},{16,18,20,22,24,26,28,30},{17..., dimensions={0} | all-to-all | bytes 131072 | tf_op jit(solution)/shard_map/all_to_all | solution.py:619
  72.6 0.0 collective-permute-done.17.refs_3_
  72.6 1.7 %shard_map.110 = (bf16[4,64,512]{2,1,0:T(8,128)(2,1)}, bf16[4,64,512]{2,1,0:T(8,128)(2,1)}, f32[1]{0:T(128)}) custom-call(s32[4]{0:T(128)S(1)} %get-tuple-element.63.slots, f32[8,8,128]{2,1,0:T(8,128)S(1)} %all_to_all.10.refs_2_.parts.parts1, f32[8,16,128]{2,1,0:T(8,128)S(1)} %all_to_all.11.parts2, bf16[2,4,64,256]{3,2,1,0:T(8,128)(2,1)S(1)} %get-tuple-element.99.refs_0_, ...), custom_call_target="tpu_custom_call" | custom-call | bytes 4194304 | tf_op jit(solution)/shard_map/pallas_call | solution.py:113
Async XLA Ops:
  0.6 4.6 %copy-start.3 = (s32[2]{0:T(128)S(1)}, s32[2]{0:T(128)}, u32[]{:S(2)}) copy-start(s32[2]{0:T(128)} %shift.1) | copy-start | bytes 28
  0.6 12.6 %collective-permute-start.1 = (bf16[2,256,256]{2,1,0:T(8,128)(2,1)}, bf16[2,256,256]{2,1,0:T(8,128)(2,1)S(1)}, u32[]{:S(2)}, u32[]{:S(2)}) collective-permute-start(bf16[2,256,256]{2,1,0:T(8,128)(2,1)} %bitcast.2), channel_id=1, source_target_pairs={{0,4},{4,12},{12,8},{8,0},{1,5},{5,13},{13,9},{9,1},{2,6},{6,14},{... | collective-permute-start | bytes 786440 | tf_op jit(solution)/shard_map/ppermute | solution.py:142
  3.7 9.6 %collective-permute-start = (bf16[2,256,256]{2,1,0:T(8,128)(2,1)}, bf16[2,256,256]{2,1,0:T(8,128)(2,1)S(1)}, u32[]{:S(2)}, u32[]{:S(2)}) collective-permute-start(bf16[2,256,256]{2,1,0:T(8,128)(2,1)} %bitcast.3), channel_id=1, source_target_pairs={{0,2},{1,3},{2,0},{3,1},{4,6},{5,7},{6,4},{7,5},{8,10},{9,11},{10,... | collective-permute-start | bytes 786440 | tf_op jit(solution)/shard_map/ppermute | solution.py:146
  5.2 1.1 %collective-permute-start.2 = (s32[2]{0:T(128)S(1)}, s32[2]{0:T(128)S(1)}, u32[]{:S(2)}, u32[]{:S(2)}) collective-permute-start(s32[2]{0:T(128)S(1)} %copy-done.3), channel_id=1, source_target_pairs={{0,1},{1,0},{2,3},{3,2},{4,5},{5,4},{6,7},{7,6},{8,9},{9,8},{10,11... | collective-permute-start | bytes 32 | tf_op jit(solution)/shard_map/ppermute | solution.py:146
  6.3 28.6 %copy-start = (bf16[2,1,256,256]{3,2,1,0:T(8,128)(2,1)S(1)}, bf16[2,1,256,256]{3,2,1,0:T(8,128)(2,1)}, u32[]{:S(2)}) copy-start(bf16[2,1,256,256]{3,2,1,0:T(8,128)(2,1)} %param.9) | copy-start | bytes 786436
  8.2 9.6 %copy-start.2 = (f32[4,256]{1,0:T(4,128)S(1)}, f32[4,256]{1,0:T(4,128)}, u32[]{:S(2)}) copy-start(f32[4,256]{1,0:T(4,128)} %left_diag.1) | copy-start | bytes 12292
  8.3 5.0 %collective-permute-start.3 = (bf16[144,256]{1,0:T(8,128)(2,1)S(1)}, bf16[144,256]{1,0:T(8,128)(2,1)S(1)}, u32[]{:S(2)}, u32[]{:S(2)}) collective-permute-start(bf16[144,256]{1,0:T(8,128)(2,1)S(1)} %get-tuple-element.54), channel_id=1, source_target_pairs={{0,2},{1,3},{2,0},{3,1},{4,6},{5,7},{6,4},{7,5},{8,10},{9,11},{10,... | collective-permute-start | bytes 221192 | tf_op jit(solution)/shard_map/ppermute | solution.py:146
  13.3 4.6 %copy-start.4 = (s32[4]{0:T(128)S(1)}, s32[4]{0:T(128)}, u32[]{:S(2)}) copy-start(s32[4]{0:T(128)} %sector.1) | copy-start | bytes 52
  13.3 4.6 %copy-start.5 = (s32[4]{0:T(128)S(1)}, s32[4]{0:T(128)}, u32[]{:S(2)}) copy-start(s32[4]{0:T(128)} %width.1) | copy-start | bytes 52
  13.3 10.2 %collective-permute-start.5 = (bf16[2,256,256]{2,1,0:T(8,128)(2,1)S(1)}, bf16[2,256,256]{2,1,0:T(8,128)(2,1)S(1)}, u32[]{:S(2)}, u32[]{:S(2)}) collective-permute-start(bf16[2,256,256]{2,1,0:T(8,128)(2,1)S(1)} %collective-permute-done.1.refs_2_), channel_id=1, source_target_pairs={{0,4},{4,12},{12,8},{8,0},{1,5},{5,13},{13,9},{9,1},{2,6},{6,14},{... | collective-permute-start | bytes 786440 | tf_op jit(solution)/shard_map/ppermute | solution.py:142
  15.9 7.5 %collective-permute-start.4 = (bf16[2,256,256]{2,1,0:T(8,128)(2,1)S(1)}, bf16[2,256,256]{2,1,0:T(8,128)(2,1)S(1)}, u32[]{:S(2)}, u32[]{:S(2)}) collective-permute-start(bf16[2,256,256]{2,1,0:T(8,128)(2,1)S(1)} %collective-permute-done.1.refs_2_), channel_id=1, source_target_pairs={{0,2},{1,3},{2,0},{3,1},{4,6},{5,7},{6,4},{7,5},{8,10},{9,11},{10,... | collective-permute-start | bytes 786440 | tf_op jit(solution)/shard_map/ppermute | solution.py:146
  17.4 6.0 %collective-permute-start.6 = (bf16[256,128]{1,0:T(8,128)(2,1)S(1)}, bf16[256,128]{1,0:T(8,128)(2,1)S(1)}, u32[]{:S(2)}, u32[]{:S(2)}) collective-permute-start(bf16[256,128]{1,0:T(8,128)(2,1)S(1)} %get-tuple-element.56), channel_id=1, source_target_pairs={{0,4},{4,12},{12,8},{8,0},{1,5},{5,13},{13,9},{9,1},{2,6},{6,14},{... | collective-permute-start | bytes 196616 | tf_op jit(solution)/shard_map/ppermute | solution.py:142
  23.5 9.3 %collective-permute-start.8 = (bf16[2,256,256]{2,1,0:T(8,128)(2,1)S(1)}, bf16[2,256,256]{2,1,0:T(8,128)(2,1)S(1)}, u32[]{:S(2)}, u32[]{:S(2)}) collective-permute-start(bf16[2,256,256]{2,1,0:T(8,128)(2,1)S(1)} %collective-permute-done.5.refs_0_), channel_id=1, source_target_pairs={{0,4},{4,12},{12,8},{8,0},{1,5},{5,13},{13,9},{9,1},{2,6},{6,14},{... | collective-permute-start | bytes 786440 | tf_op jit(solution)/shard_map/ppermute | solution.py:142
  25.2 7.6 %collective-permute-start.7 = (bf16[2,256,256]{2,1,0:T(8,128)(2,1)S(1)}, bf16[2,256,256]{2,1,0:T(8,128)(2,1)S(1)}, u32[]{:S(2)}, u32[]{:S(2)}) collective-permute-start(bf16[2,256,256]{2,1,0:T(8,128)(2,1)S(1)} %collective-permute-done.5.refs_0_), channel_id=1, source_target_pairs={{0,2},{1,3},{2,0},{3,1},{4,6},{5,7},{6,4},{7,5},{8,10},{9,11},{10,... | collective-permute-start | bytes 786440 | tf_op jit(solution)/shard_map/ppermute | solution.py:146
  25.7 6.9 %collective-permute-start.10 = (bf16[256,128]{1,0:T(8,128)(2,1)S(1)}, bf16[256,128]{1,0:T(8,128)(2,1)S(1)}, u32[]{:S(2)}, u32[]{:S(2)}) collective-permute-start(bf16[256,128]{1,0:T(8,128)(2,1)S(1)} %get-tuple-element.68), channel_id=1, source_target_pairs={{0,8},{4,0},{12,4},{8,12},{1,9},{5,1},{13,5},{9,13},{2,10},{6,2},{... | collective-permute-start | bytes 196616 | tf_op jit(solution)/shard_map/ppermute | solution.py:142
  26.9 5.7 %collective-permute-start.9 = (bf16[256,128]{1,0:T(8,128)(2,1)S(1)}, bf16[256,128]{1,0:T(8,128)(2,1)S(1)}, u32[]{:S(2)}, u32[]{:S(2)}) collective-permute-start(bf16[256,128]{1,0:T(8,128)(2,1)S(1)} %collective-permute-done.6.refs_5_), channel_id=1, source_target_pairs={{0,1},{1,0},{2,3},{3,2},{4,5},{5,4},{6,7},{7,6},{8,9},{9,8},{10,11... | collective-permute-start | bytes 196616 | tf_op jit(solution)/shard_map/ppermute | solution.py:146
  32.8 8.1 %collective-permute-start.11 = (bf16[2,256,256]{2,1,0:T(8,128)(2,1)S(1)}, bf16[2,256,256]{2,1,0:T(8,128)(2,1)S(1)}, u32[]{:S(2)}, u32[]{:S(2)}) collective-permute-start(bf16[2,256,256]{2,1,0:T(8,128)(2,1)S(1)} %collective-permute-done.8.refs_2_), channel_id=1, source_target_pairs={{0,2},{1,3},{2,0},{3,1},{4,6},{5,7},{6,4},{7,5},{8,10},{9,11},{10,... | collective-permute-start | bytes 786440 | tf_op jit(solution)/shard_map/ppermute | solution.py:146
  32.8 7.3 %collective-permute-start.13 = (bf16[256,256]{1,0:T(8,128)(2,1)S(1)}, bf16[256,256]{1,0:T(8,128)(2,1)S(1)}, u32[]{:S(2)}, u32[]{:S(2)}) collective-permute-start(bf16[256,256]{1,0:T(8,128)(2,1)S(1)} %get-tuple-element.79), channel_id=1, source_target_pairs={{0,12},{4,8},{12,0},{8,4},{1,13},{5,9},{13,1},{9,5},{2,14},{6,10},... | collective-permute-start | bytes 393224 | tf_op jit(solution)/shard_map/ppermute | solution.py:142
  34.9 5.1 %collective-permute-start.12 = (bf16[256,128]{1,0:T(8,128)(2,1)S(1)}, bf16[256,128]{1,0:T(8,128)(2,1)S(1)}, u32[]{:S(2)}, u32[]{:S(2)}) collective-permute-start(bf16[256,128]{1,0:T(8,128)(2,1)S(1)} %collective-permute-done.10.refs_7_), channel_id=1, source_target_pairs={{0,1},{1,0},{2,3},{3,2},{4,5},{5,4},{6,7},{7,6},{8,9},{9,8},{10,11... | collective-permute-start | bytes 196616 | tf_op jit(solution)/shard_map/ppermute | solution.py:146
  43.1 2.0 %copy-start.1 = (f32[512]{0:T(512)S(1)}, f32[512]{0:T(512)}, u32[]{:S(2)}) copy-start(f32[512]{0:T(512)} %param.15) | copy-start | bytes 6148
  43.2 2.0 %collective-permute-start.14 = (bf16[4,256,256]{2,1,0:T(8,128)(2,1)S(1)}, bf16[4,256,256]{2,1,0:T(8,128)(2,1)S(1)}, u32[]{:S(2)}, u32[]{:S(2)}) collective-permute-start(bf16[4,256,256]{2,1,0:T(8,128)(2,1)S(1)} %get-tuple-element.85.mine), channel_id=1, source_target_pairs={{0,1},{1,0},{2,3},{3,2},{4,5},{5,4},{6,7},{7,6},{8,9},{9,8},{10,11... | collective-permute-start | bytes 1572872 | tf_op jit(solution)/shard_map/ppermute | solution.py:146
  45.7 10.3 %collective-permute-start.15 = (bf16[2,4,64,256]{3,2,1,0:T(8,128)(2,1)S(1)}, bf16[2,4,64,256]{3,2,1,0:T(8,128)(2,1)S(1)}, u32[]{:S(2)}, u32[]{:S(2)}) collective-permute-start(bf16[2,4,64,256]{3,2,1,0:T(8,128)(2,1)S(1)} %get-tuple-element.90), channel_id=1, source_target_pairs={{0,2},{1,3},{2,0},{3,1},{4,6},{5,7},{6,4},{7,5},{8,10},{9,11},{10,... | collective-permute-start | bytes 786440 | tf_op jit(solution)/shard_map/ppermute | solution.py:146
  59.6 2.0 %collective-permute-start.16 = (bf16[4,256,256]{2,1,0:T(8,128)(2,1)S(1)}, bf16[4,256,256]{2,1,0:T(8,128)(2,1)S(1)}, u32[]{:S(2)}, u32[]{:S(2)}) collective-permute-start(bf16[4,256,256]{2,1,0:T(8,128)(2,1)S(1)} %get-tuple-element.96.mine), channel_id=1, source_target_pairs={{0,1},{1,0},{2,3},{3,2},{4,5},{5,4},{6,7},{7,6},{8,9},{9,8},{10,11... | collective-permute-start | bytes 1572872 | tf_op jit(solution)/shard_map/ppermute | solution.py:146
  62.6 10.1 %collective-permute-start.17 = (bf16[2,4,64,256]{3,2,1,0:T(8,128)(2,1)S(1)}, bf16[2,4,64,256]{3,2,1,0:T(8,128)(2,1)S(1)}, u32[]{:S(2)}, u32[]{:S(2)}) collective-permute-start(bf16[2,4,64,256]{3,2,1,0:T(8,128)(2,1)S(1)} %get-tuple-element.102), channel_id=1, source_target_pairs={{0,2},{1,3},{2,0},{3,1},{4,6},{5,7},{6,4},{7,5},{8,10},{9,11},{10,... | collective-permute-start | bytes 786440 | tf_op jit(solution)/shard_map/ppermute | solution.py:146

commit v12 on v10

--- a/solution.py
+++ b/solution.py
@@ -315,7 +315,7 @@
         at += terms
 
 
-def sum_terms(src, widths, inter, right, out):
+def sum_terms(src, widths, inter, right, out, emit):
     n_blk, n_terms, _, _ = inter.shape
     n_blk -= 1
     terms = n_terms // len(right)
@@ -327,7 +327,9 @@
                 inter[src[t * n_terms + j], j], turned[j], preferred_element_type=jnp.float32
             )
             total = part if total is None else total + part
-        out[t] = jnp.where(row_mask(widths[t], total.shape), total, 0.0).astype(jnp.bfloat16)
+        total = jnp.where(row_mask(widths[t], total.shape), total, 0.0)
+        out[t] = total.astype(jnp.bfloat16)
+        emit(t, total)
 
 
 def keep(left, left_out, sems):
@@ -377,7 +379,8 @@
     n_early = n_blk - n_late
     left, refs = take(refs, [n_pair] * n_late)
     (right,), refs = take(refs, [n_pair])
-    psi, (raw_in, inter_in, part_out, raw_out, left_out, inter, sems) = take(refs, counts)
+    psi, refs = take(refs, counts)
+    raw_in, inter_in, diag, right_diag, part_out, raw_out, left_out, dots_out, inter, sems = refs
     copies = keep(left, left_out, sems)
     for j, (given, own) in enumerate(((inter_in, inter), (raw_in, raw_out))):
         copies.append(
@@ -390,7 +393,22 @@
     )
     for copy in copies:
         copy.wait()
-    sum_terms(src, widths, inter, right, part_out)
+    cols = diag.shape[2]
+    zero = jnp.zeros((8, cols), jnp.float32)
+    sums = [zero, zero]
+
+    def emit(d, total):
+        for h in range(2):
+            part = slice(h * cols, (h + 1) * cols)
+            raw = raw_out[d, :, part].astype(jnp.float32)
+            image = total[:, part]
+            if h == 0:
+                image = image + diagonal(diag, right_diag, d, h) * raw
+                sums[0] = sums[0] + fold(raw * raw)
+            sums[1] = sums[1] + fold(raw * image)
+
+    sum_terms(src, widths, inter, right, part_out, emit)
+    spread([whole(x) for x in sums], dots_out)
 
 
 def send_rows(sends, j, d, h, block):
@@ -406,22 +424,16 @@
     return own + other[d, :, (1 - h) * cols : (2 - h) * cols].astype(jnp.float32)
 
 
-def sigma_body(mine, other, raw_in, diag, right_diag, sig_out, dots_out, *sends):
+def sigma_body(mine, other, raw_in, diag, right_diag, sig_out, *sends):
     n_blk, _, cols = diag.shape
-    sums = [jnp.zeros((8, cols), jnp.float32) for _ in range(2)]
     for d in range(n_blk):
         for h in range(2):
             part = slice(h * cols, (h + 1) * cols)
             raw = raw_in[d, :, part].astype(jnp.float32)
             sigma = total_of(mine, other, d, h, cols) + diagonal(diag, right_diag, d, h) * raw
             sig_out[d, :, part] = sigma
-            if h == 0:
-                sums = [sums[0] + fold(raw * raw), sums[1] + fold(raw * sigma)]
-    for d in range(n_blk):
-        for h in range(2):
-            send_rows(sends, 0, d, h, raw_in.at[d, :, h * cols : (h + 1) * cols])
-            send_rows(sends, 1, d, h, sig_out.at[d, :, h * cols : (h + 1) * cols])
-    spread([whole(x) for x in sums], dots_out)
+            send_rows(sends, 0, d, h, raw_in.at[d, :, part])
+            send_rows(sends, 1, d, h, sig_out.at[d, :, part])
 
 
 def norm_theta(parts, count):
@@ -432,7 +444,7 @@
 
 def second_body(n_blk, n_pair, count, src, widths, left_early, left_late, *refs):
     right, refs = refs[:n_pair], refs[n_pair:]
-    parts, raw_in, sig_in, diag, right_diag, f_out, part_out, half_out = refs[:8]
+    parts, raw_in, sig_in, diag, right_diag, f_out, part_out, dots_out = refs[:8]
     inter, corr, held, sems = refs[8:]
     copies = []
     n_early = left_early.shape[0]
@@ -464,29 +476,36 @@
             f_out[d, :, part] = (corr[d, :, part] - along * vec).astype(jnp.bfloat16)
         copies[d].wait()
         left_products(f_out[d], lambda at: held[d, at // terms], inter.at[d])
-    sum_terms(src, widths, inter, right, part_out)
-    spread(halves[0] + (along,), half_out)
-
-
-def image_body(count, half, parts, mine, other, raw_in, sig_in, f_in, diag, right_diag, dots_out, *sends):
+    zero = jnp.zeros((8, cols), jnp.float32)
+    sums = [zero for _ in range(5)]
+
+    def emit(d, total):
+        for h in range(2):
+            part = slice(h * cols, (h + 1) * cols)
+            fld = f_out[d, :, part].astype(jnp.float32)
+            vec = raw_in[d, :, part].astype(jnp.float32) * scale
+            image = total[:, part]
+            if h == 0:
+                image = image + diagonal(diag, right_diag, d, h) * fld
+                for j, prod in enumerate((fld * fld, vec * fld, fld * sig_in[d, :, part] * scale)):
+                    sums[j] = sums[j] + fold(prod)
+            sums[3] = sums[3] + fold(vec * image)
+            sums[4] = sums[4] + fold(fld * image)
+
+    sum_terms(src, widths, inter, right, part_out, emit)
+    spread(list(halves[0]) + [along] + [whole(x) for x in sums], dots_out)
+
+
+def image_body(mine, other, f_in, diag, right_diag, *sends):
     n_blk, _, cols = diag.shape
-    scale, _ = norm_theta(parts[...], count)
-    sums = [jnp.zeros((8, cols), jnp.float32) for _ in range(5)]
+    sends, image = sends[:-1], sends[-1]
     for d in range(n_blk):
         for h in range(2):
             part = slice(h * cols, (h + 1) * cols)
             fld = f_in[d, :, part].astype(jnp.float32)
-            image = total_of(mine, other, d, h, cols) + diagonal(diag, right_diag, d, h) * fld
-            sends[-1][h] = image
-            send_rows(sends[:-1], 0, d, h, f_in.at[d, :, part])
-            send_rows(sends[:-1], 1, d, h, sends[-1].at[h])
-            if h == 0:
-                vec = raw_in[d, :, part].astype(jnp.float32) * scale
-                sigma = sig_in[d, :, part] * scale
-                prods = (fld * fld, vec * fld, vec * image, fld * sigma, fld * image)
-                sums = [one + fold(prod) for one, prod in zip(sums, prods)]
-    known = [half[0, j : j + 1] for j in range(4)]
-    spread(known + [whole(x) for x in sums], dots_out)
+            image[h] = total_of(mine, other, d, h, cols) + diagonal(diag, right_diag, d, h) * fld
+            send_rows(sends, 0, d, h, f_in.at[d, :, part])
+            send_rows(sends, 1, d, h, image.at[h])
 
 
 def ritz_pair(theta, h_mix, h_two):
@@ -511,7 +530,7 @@
     cols = new_out.shape[2] // n_op
     own_blk, own_op = place_of()
     scale, theta = norm_theta(parts1[...], count)
-    vv, vc, vs, local, ff, vf, vt, fs, ft = (parts2[:, j, :] for j in range(9))
+    vv, vc, vs, local, ff, vf, fs, vt, ft = (parts2[:, j, :] for j in range(9))
 
     def mean(x):
         return jnp.sum(x, axis=0, keepdims=True) * (1.0 / count)
@@ -621,24 +640,26 @@
     def exchange(out):
         return [out[0]] + [swap(block, 2 * e, n_op) for e, block in enumerate(out[1:], 1)]
 
-    part1, raw, kept = kernel(
+    part1, raw, kept, dots1 = kernel(
         functools.partial(first_body, n_blk, n_pair, counts),
-        tables + left_ins + right_ins + psi_ins + [(raw_early, VMEM), (inter_early, VMEM)],
-        [narrow, narrow, (left_late, bf16, HBM)],
+        tables + left_ins + right_ins + psi_ins + [(raw_early, VMEM), (inter_early, VMEM)] + diags,
+        [narrow, narrow, (left_late, bf16, HBM), ((n_dev, 8, LANES), f32, VMEM)],
         [inter, pltpu.SemaphoreType.DMA((n_late * n_pair + 2,))],
         **cost,
     )
-    sig, dots1, *out1 = kernel(
+    parts1 = totals(dots1)
+    sig, *out1 = kernel(
         sigma_body,
         [(x, VMEM) for x in (part1, swap(part1, 1, n_op), raw)] + diags,
-        [wide, ((n_dev, 8, LANES), f32, VMEM)] + sends,
+        [wide] + sends,
         nbytes=4 << 20,
     )
-    parts1, got1 = lax.optimization_barrier((totals(dots1), exchange(out1)))
-    fld, part2, half = kernel(
+    parts1, sig, got1 = lax.optimization_barrier((parts1, sig, exchange(out1)))
+    fld, part2, dots2 = kernel(
         functools.partial(second_body, n_blk, n_pair, count),
-        tables + [(left_early, HBM), (kept, HBM)] + right_ins + [(x, VMEM) for x in (parts1, raw, sig)] + diags,
-        [narrow, narrow, ((1, 8, LANES), f32, VMEM)],
+        tables + [(left_early, HBM), (kept, HBM)] + right_ins
+        + [(x, VMEM) for x in (parts1, raw, sig)] + diags,
+        [narrow, narrow, ((n_dev, 16, LANES), f32, VMEM)],
         [
             inter,
             pltpu.VMEM((n_blk, rows, 2 * cols), f32),
@@ -647,14 +668,14 @@
         ],
         **cost,
     )
-    dots2, *out2 = kernel(
-        functools.partial(image_body, count),
-        [(x, VMEM) for x in (half, parts1, part2, swap(part2, 1, n_op), raw, sig, fld)] + diags,
-        [((n_dev, 16, LANES), f32, VMEM)] + sends,
+    parts2 = totals(dots2)
+    out2 = kernel(
+        image_body,
+        [(x, VMEM) for x in (part2, swap(part2, 1, n_op), fld)] + diags,
+        sends,
         [pltpu.VMEM((2, rows, cols), f32)],
         nbytes=4 << 20,
     )
-    parts2 = totals(dots2)
     got2 = exchange(out2)
     final = ((n_blk, step, n_op * cols), bf16, VMEM)
     new, res, energy = kernel(

time: 76.2 us -> 76.4 us (level)
  no operation moved by 1% of the time
where the time goes in v12:
time: 76.4 us; the launch traced here: 76.1 us
  waiting for transfers between devices  23.7 us (31%)
  blocking collectives  20.7 us (27%)
  starting transfers between devices  16.6 us (22%)
  Pallas kernels  13.7 us (18%)
    all_to_all x2, blocking collectives, totals(): return lax.all_to_all(parts, ('blk', 'op'), 0, 0, tiled=True)  20.7 us
    pallas_call x8, Pallas kernels, kernel(): pl.pallas_call(body, out_shape=[HBM(shape, dtype) if space == HBM else ja...  13.7 us
    ppermute x6, waiting for transfers between devices, onward(): return lax.ppermute(block, 'blk', pairs)  13.5 us
    ppermute x6, starting transfers between devices, onward(): return lax.ppermute(block, 'blk', pairs)  11.2 us
    ppermute x12, waiting for transfers between devices, swap(): return lax.ppermute(block, 'op', [(i, i ^ e) for i in range(n_op)])  10.2 us
    ppermute x12, starting transfers between devices, swap(): return lax.ppermute(block, 'op', [(i, i ^ e) for i in range(n_op)])  5.37 us
  transfers between devices with their start and end apart: 18, of which 9 were waited for; matrix products, arithmetic and copies ran while one was open for 0% of the time, Pallas kernels for 6%

profile of v12, /device:TPU:0, one launch (start us, length us, event | category | flops | bytes accessed | tf_op | source)
XLA Modules:
  0.0 76.1 jit_solution(11132076439258231700)
XLA Ops:
  0.6 0.0 copy-start.3
  0.6 3.1 %collective-permute-start.1 = (bf16[2,256,256]{2,1,0:T(8,128)(2,1)}, bf16[2,256,256]{2,1,0:T(8,128)(2,1)S(1)}, u32[]{:S(2)}, u32[]{:S(2)}) collective-permute-start(bf16[2,256,256]{2,1,0:T(8,128)(2,1)} %bitcast.2), channel_id=1, source_target_pairs={{0,4},{4,12},{12,8},{8,0},{1,5},{5,13},{13,9},{9,1},{2,6},{6,14},{... | collective-permute-start | bytes 786440 | tf_op jit(solution)/shard_map/ppermute | solution.py:142
  3.7 1.5 %collective-permute-start = (bf16[2,256,256]{2,1,0:T(8,128)(2,1)}, bf16[2,256,256]{2,1,0:T(8,128)(2,1)S(1)}, u32[]{:S(2)}, u32[]{:S(2)}) collective-permute-start(bf16[2,256,256]{2,1,0:T(8,128)(2,1)} %bitcast.3), channel_id=1, source_target_pairs={{0,2},{1,3},{2,0},{3,1},{4,6},{5,7},{6,4},{7,5},{8,10},{9,11},{10,... | collective-permute-start | bytes 786440 | tf_op jit(solution)/shard_map/ppermute | solution.py:146
  5.2 0.0 copy-done.3
  5.2 0.0 collective-permute-start.2
  5.2 1.1 %collective-permute-done.2._ = s32[2]{0:T(128)S(1)} collective-permute-done((s32[2]{0:T(128)S(1)}, s32[2]{0:T(128)S(1)}, u32[]{:S(2)}, u32[]{:S(2)}) %collective-permute-start.2) | collective-permute-done | bytes 40 | tf_op jit(solution)/shard_map/ppermute | solution.py:146
  6.3 0.0 copy-start
  6.3 1.9 %shard_map.103 = (bf16[256,256]{1,0:T(8,128)(2,1)S(1)}, bf16[256,128]{1,0:T(8,128)(2,1)S(1)}, bf16[256,256]{1,0:T(8,128)(2,1)S(1)}, bf16[256,128]{1,0:T(8,128)(2...) custom-call(s32[2]{0:T(128)S(1)} %copy-done.3, s32[2]{0:T(128)S(1)} %collective-permute-done.2._, ...), custom_call_target="tpu_custom_call" | custom-call | bytes 1048576 | tf_op jit(solution)/shard_map/pallas_call | solution.py:113
  8.2 0.0 copy-start.2
  8.3 0.6 collective-permute-start.3
  8.9 4.4 %collective-permute-done.3.refs_1_.refs_5_ = bf16[144,256]{1,0:T(8,128)(2,1)S(1)} collective-permute-done((bf16[144,256]{1,0:T(8,128)(2,1)S(1)}, bf16[144,256]{1,0:T(8,128)(2,1)S(1)}, u32[]{:S(2)}, u32[]{:S(2)}) %collective-permute-start.3) | collective-permute-done | bytes 73760 | tf_op jit(solution)/shard_map/ppermute | solution.py:146
  13.3 0.0 collective-permute-done.1.refs_2_
  13.3 0.0 collective-permute-done.refs_1_
  13.3 0.0 copy-start.4
  13.3 0.0 copy-start.5
  13.3 2.6 %collective-permute-start.5 = (bf16[2,256,256]{2,1,0:T(8,128)(2,1)S(1)}, bf16[2,256,256]{2,1,0:T(8,128)(2,1)S(1)}, u32[]{:S(2)}, u32[]{:S(2)}) collective-permute-start(bf16[2,256,256]{2,1,0:T(8,128)(2,1)S(1)} %collective-permute-done.1.refs_2_), channel_id=1, source_target_pairs={{0,4},{4,12},{12,8},{8,0},{1,5},{5,13},{13,9},{9,1},{2,6},{6,14},{... | collective-permute-start | bytes 786440 | tf_op jit(solution)/shard_map/ppermute | solution.py:142
  15.9 1.5 %collective-permute-start.4 = (bf16[2,256,256]{2,1,0:T(8,128)(2,1)S(1)}, bf16[2,256,256]{2,1,0:T(8,128)(2,1)S(1)}, u32[]{:S(2)}, u32[]{:S(2)}) collective-permute-start(bf16[2,256,256]{2,1,0:T(8,128)(2,1)S(1)} %collective-permute-done.1.refs_2_), channel_id=1, source_target_pairs={{0,2},{1,3},{2,0},{3,1},{4,6},{5,7},{6,4},{7,5},{8,10},{9,11},{10,... | collective-permute-start | bytes 786440 | tf_op jit(solution)/shard_map/ppermute | solution.py:146
  17.4 0.4 collective-permute-start.6
  17.9 0.0 copy-done.2
  17.9 0.0 copy-done.4
  17.9 0.0 copy-done.5
  17.9 1.3 %shard_map.104 = (s32[16]{0:T(128)S(1)}, s32[4]{0:T(128)S(1)}, s32[4]{0:T(128)S(1)}, f32[4,256,128]{2,1,0:T(8,128)S(1)}) custom-call(s32[4]{0:T(128)S(1)} %copy-done.4, s32[4]{0:T(128)S(1)} %copy-done.5, f32[4,256]{1,0:T(4,128)S(1)} %copy-done.2, bf16[144,256]{1,0:T(8,128)(2,1)S(1)} %get-tuple-element.57.refs_0_.refs_4_, ...), custom_call_target="tpu_custom_call" | custom-call | tf_op jit(solution)/shard_map/pallas_call | solution.py:113
  19.2 4.2 %collective-permute-done.6.refs_5_ = bf16[256,128]{1,0:T(8,128)(2,1)S(1)} collective-permute-done((bf16[256,128]{1,0:T(8,128)(2,1)S(1)}, bf16[256,128]{1,0:T(8,128)(2,1)S(1)}, u32[]{:S(2)}, u32[]{:S(2)}) %collective-permute-start.6) | collective-permute-done | bytes 65568 | tf_op jit(solution)/shard_map/ppermute | solution.py:142
  23.5 0.0 collective-permute-done.5.refs_0_
  23.5 0.0 collective-permute-done.4.refs_3_
  23.5 1.7 %collective-permute-start.8 = (bf16[2,256,256]{2,1,0:T(8,128)(2,1)S(1)}, bf16[2,256,256]{2,1,0:T(8,128)(2,1)S(1)}, u32[]{:S(2)}, u32[]{:S(2)}) collective-permute-start(bf16[2,256,256]{2,1,0:T(8,128)(2,1)S(1)} %collective-permute-done.5.refs_0_), channel_id=1, source_target_pairs={{0,4},{4,12},{12,8},{8,0},{1,5},{5,13},{13,9},{9,1},{2,6},{6,14},{... | collective-permute-start | bytes 786440 | tf_op jit(solution)/shard_map/ppermute | solution.py:142
  25.2 0.5 collective-permute-start.7
  25.7 1.2 %collective-permute-start.10 = (bf16[256,128]{1,0:T(8,128)(2,1)S(1)}, bf16[256,128]{1,0:T(8,128)(2,1)S(1)}, u32[]{:S(2)}, u32[]{:S(2)}) collective-permute-start(bf16[256,128]{1,0:T(8,128)(2,1)S(1)} %get-tuple-element.68), channel_id=1, source_target_pairs={{0,8},{4,0},{12,4},{8,12},{1,9},{5,1},{13,5},{9,13},{2,10},{6,2},{... | collective-permute-start | bytes 196616 | tf_op jit(solution)/shard_map/ppermute | solution.py:142
  26.9 0.0 collective-permute-start.9
  26.9 5.7 %collective-permute-done.10.refs_7_ = bf16[256,128]{1,0:T(8,128)(2,1)S(1)} collective-permute-done((bf16[256,128]{1,0:T(8,128)(2,1)S(1)}, bf16[256,128]{1,0:T(8,128)(2,1)S(1)}, u32[]{:S(2)}, u32[]{:S(2)}) %collective-permute-start.10) | collective-permute-done | bytes 65568 | tf_op jit(solution)/shard_map/ppermute | solution.py:142
  32.6 0.0 collective-permute-done.9.refs_6_
  32.6 0.1 collective-permute-done.8.refs_2_
  32.7 0.0 collective-permute-done.7.refs_1_
  32.8 0.0 collective-permute-start.11
  32.8 2.2 %collective-permute-start.13 = (bf16[256,256]{1,0:T(8,128)(2,1)S(1)}, bf16[256,256]{1,0:T(8,128)(2,1)S(1)}, u32[]{:S(2)}, u32[]{:S(2)}) collective-permute-start(bf16[256,256]{1,0:T(8,128)(2,1)S(1)} %get-tuple-element.79), channel_id=1, source_target_pairs={{0,12},{4,8},{12,0},{8,4},{1,13},{5,9},{13,1},{9,5},{2,14},{6,10},... | collective-permute-start | bytes 393224 | tf_op jit(solution)/shard_map/ppermute | solution.py:142
  34.9 0.0 collective-permute-start.12
  34.9 0.0 copy-done
  34.9 1.7 %shard_map.105 = (bf16[2,256,256]{2,1,0:T(8,128)(2,1)S(1)}, bf16[2,4,256,256]{3,2,1,0:T(8,128)(2,1)S(1)}, bf16[2,2,2,256,256]{4,3,2,1,0:T(8,128)(2,1)}) custom-call(s32[4]{0:T(128)S(1)} %get-tuple-element.65.widths, bf16[2,256,256]{2,1,0:T(8,128)(2,1)S(1)} %bitcast.4, bf16[2,256,256]{2,1,0:T(8,128)(2,1)S(1)} %collective-permute-done.refs_1_, ...), custom_call_target="tpu_custom_call" | custom-call | flops 268435456 | bytes 4194304 | tf_op jit(solution)/shard_map/pallas_call | solution.py:113
  36.6 3.5 %collective-permute-done.13.refs_6_ = bf16[256,256]{1,0:T(8,128)(2,1)S(1)} collective-permute-done((bf16[256,256]{1,0:T(8,128)(2,1)S(1)}, bf16[256,256]{1,0:T(8,128)(2,1)S(1)}, u32[]{:S(2)}, u32[]{:S(2)}) %collective-permute-start.13) | collective-permute-done | bytes 131104 | tf_op jit(solution)/shard_map/ppermute | solution.py:142
  40.0 0.0 collective-permute-done.12.refs_8_
  40.0 0.8 %collective-permute-done.11.refs_3_ = bf16[2,256,256]{2,1,0:T(8,128)(2,1)S(1)} collective-permute-done((bf16[2,256,256]{2,1,0:T(8,128)(2,1)S(1)}, bf16[2,256,256]{2,1,0:T(8,128)(2,1)S(1)}, u32[]{:S(2)}, u32[]{:S(2)}) %collective-permute-start.11) | collective-permute-done | bytes 262176 | tf_op jit(solution)/shard_map/ppermute | solution.py:146
  40.9 0.0 copy-start.1
  40.9 0.7 copy-done.1
  41.5 2.4 %shard_map.106 = (bf16[4,256,256]{2,1,0:T(8,128)(2,1)S(1)}, bf16[4,256,256]{2,1,0:T(8,128)(2,1)S(1)}, bf16[2,2,2,256,256]{4,3,2,1,0:T(8,128)(2,1)}, f32[16,8,128]{2,1,0:T(8,128)S(1)}) custom-call(s32[16]{0:T(128)S(1)} %get-tuple-element.64.src, s32[4]{0:T(128)S(1)} %get-tuple-element.65.widths, bf16[2,256,256]{2,1,0:T(8,128)(2,1)S(1)} %collective-permute-done.5.refs_0_, ...), custom_call_target="tpu_custom_call" | custom-call | flops 1073741824 | bytes 6291456 | tf_op jit(solution)/shard_map/pallas_call | solution.py:113
  44.0 0.1 collective-permute-start.14
  44.1 1.9 %collective-permute-done.14.other = bf16[4,256,256]{2,1,0:T(8,128)(2,1)S(1)} collective-permute-done((bf16[4,256,256]{2,1,0:T(8,128)(2,1)S(1)}, bf16[4,256,256]{2,1,0:T(8,128)(2,1)S(1)}, u32[]{:S(2)}, u32[]{:S(2)}) %collective-permute-start.14) | collective-permute-done | bytes 524320 | tf_op jit(solution)/shard_map/ppermute | solution.py:146
  46.0 0.4 shard_map.107
  46.4 0.9 %collective-permute-start.15 = (bf16[2,4,64,256]{3,2,1,0:T(8,128)(2,1)S(1)}, bf16[2,4,64,256]{3,2,1,0:T(8,128)(2,1)S(1)}, u32[]{:S(2)}, u32[]{:S(2)}) collective-permute-start(bf16[2,4,64,256]{3,2,1,0:T(8,128)(2,1)S(1)} %get-tuple-element.91), channel_id=1, source_target_pairs={{0,2},{1,3},{2,0},{3,1},{4,6},{5,7},{6,4},{7,5},{8,10},{9,11},{10,... | collective-permute-start | bytes 786440 | tf_op jit(solution)/shard_map/ppermute | solution.py:146
  47.3 9.7 %all_to_all.10.refs_2_.parts1 = f32[16,8,128]{2,1,0:T(8,128)S(1)} all-to-all(f32[16,8,128]{2,1,0:T(8,128)S(1)} %get-tuple-element.86), channel_id=1, replica_groups=mesh['grp'=2,'blk'=4,'op'=4] {'blk','op'}, dimensions={0} | all-to-all | bytes 131072 | tf_op jit(solution)/shard_map/all_to_all | solution.py:638
  57.0 0.0 collective-permute-done.15.refs_1_
  57.0 3.8 %shard_map.108 = (bf16[4,256,256]{2,1,0:T(8,128)(2,1)S(1)}, bf16[4,256,256]{2,1,0:T(8,128)(2,1)S(1)}, f32[16,16,128]{2,1,0:T(8,128)S(1)}) custom-call(s32[16]{0:T(128)S(1)} %get-tuple-element.64.src, s32[4]{0:T(128)S(1)} %get-tuple-element.65.widths, bf16[2,2,2,256,256]{4,3,2,1,0:T(8,128)(2,1)} %get-tuple-element.93.left_early, ...), custom_call_target="tpu_custom_call" | custom-call | flops 1073741824 | bytes 6291456 | tf_op jit(solution)/shard_map/pallas_call | solution.py:113
  60.9 0.1 collective-permute-start.16
  61.0 1.9 %collective-permute-done.16.other = bf16[4,256,256]{2,1,0:T(8,128)(2,1)S(1)} collective-permute-done((bf16[4,256,256]{2,1,0:T(8,128)(2,1)S(1)}, bf16[4,256,256]{2,1,0:T(8,128)(2,1)S(1)}, u32[]{:S(2)}, u32[]{:S(2)}) %collective-permute-start.16) | collective-permute-done | bytes 524320 | tf_op jit(solution)/shard_map/ppermute | solution.py:146
  62.9 0.4 shard_map.109
  63.3 0.2 collective-permute-start.17
  63.4 11.0 %all_to_all.11.parts2 = f32[16,16,128]{2,1,0:T(8,128)S(1)} all-to-all(f32[16,16,128]{2,1,0:T(8,128)S(1)} %get-tuple-element.96), channel_id=1, replica_groups=mesh['grp'=2,'blk'=4,'op'=4] {'blk','op'}, dimensions={0} | all-to-all | bytes 262144 | tf_op jit(solution)/shard_map/all_to_all | solution.py:638
  74.4 0.0 collective-permute-done.17.refs_3_
  74.5 1.7 %shard_map.110 = (bf16[4,64,512]{2,1,0:T(8,128)(2,1)}, bf16[4,64,512]{2,1,0:T(8,128)(2,1)}, f32[1]{0:T(128)}) custom-call(s32[4]{0:T(128)S(1)} %get-tuple-element.63.slots, f32[16,8,128]{2,1,0:T(8,128)S(1)} %all_to_all.10.refs_2_.parts1, f32[16,16,128]{2,1,0:T(8,128)S(1)} %all_to_all.11.parts2, bf16[2,4,64,256]{3,2,1,0:T(8,128)(2,1)S(1)} %get-tuple-element.97.refs_0_, ...), custom_call_target="tpu_custom_call" | custom-call | bytes 4194304 | tf_op jit(solution)/shard_map/pallas_call | solution.py:113
Async XLA Ops:
  0.6 4.6 %copy-start.3 = (s32[2]{0:T(128)S(1)}, s32[2]{0:T(128)}, u32[]{:S(2)}) copy-start(s32[2]{0:T(128)} %shift.1) | copy-start | bytes 28
  0.6 12.6 %collective-permute-start.1 = (bf16[2,256,256]{2,1,0:T(8,128)(2,1)}, bf16[2,256,256]{2,1,0:T(8,128)(2,1)S(1)}, u32[]{:S(2)}, u32[]{:S(2)}) collective-permute-start(bf16[2,256,256]{2,1,0:T(8,128)(2,1)} %bitcast.2), channel_id=1, source_target_pairs={{0,4},{4,12},{12,8},{8,0},{1,5},{5,13},{13,9},{9,1},{2,6},{6,14},{... | collective-permute-start | bytes 786440 | tf_op jit(solution)/shard_map/ppermute | solution.py:142
  3.7 9.6 %collective-permute-start = (bf16[2,256,256]{2,1,0:T(8,128)(2,1)}, bf16[2,256,256]{2,1,0:T(8,128)(2,1)S(1)}, u32[]{:S(2)}, u32[]{:S(2)}) collective-permute-start(bf16[2,256,256]{2,1,0:T(8,128)(2,1)} %bitcast.3), channel_id=1, source_target_pairs={{0,2},{1,3},{2,0},{3,1},{4,6},{5,7},{6,4},{7,5},{8,10},{9,11},{10,... | collective-permute-start | bytes 786440 | tf_op jit(solution)/shard_map/ppermute | solution.py:146
  5.2 1.1 %collective-permute-start.2 = (s32[2]{0:T(128)S(1)}, s32[2]{0:T(128)S(1)}, u32[]{:S(2)}, u32[]{:S(2)}) collective-permute-start(s32[2]{0:T(128)S(1)} %copy-done.3), channel_id=1, source_target_pairs={{0,1},{1,0},{2,3},{3,2},{4,5},{5,4},{6,7},{7,6},{8,9},{9,8},{10,11... | collective-permute-start | bytes 32 | tf_op jit(solution)/shard_map/ppermute | solution.py:146
  6.3 28.6 %copy-start = (bf16[2,1,256,256]{3,2,1,0:T(8,128)(2,1)S(1)}, bf16[2,1,256,256]{3,2,1,0:T(8,128)(2,1)}, u32[]{:S(2)}) copy-start(bf16[2,1,256,256]{3,2,1,0:T(8,128)(2,1)} %param.9) | copy-start | bytes 786436
  8.2 9.6 %copy-start.2 = (f32[4,256]{1,0:T(4,128)S(1)}, f32[4,256]{1,0:T(4,128)}, u32[]{:S(2)}) copy-start(f32[4,256]{1,0:T(4,128)} %left_diag.1) | copy-start | bytes 12292
  8.3 5.0 %collective-permute-start.3 = (bf16[144,256]{1,0:T(8,128)(2,1)S(1)}, bf16[144,256]{1,0:T(8,128)(2,1)S(1)}, u32[]{:S(2)}, u32[]{:S(2)}) collective-permute-start(bf16[144,256]{1,0:T(8,128)(2,1)S(1)} %get-tuple-element.54), channel_id=1, source_target_pairs={{0,2},{1,3},{2,0},{3,1},{4,6},{5,7},{6,4},{7,5},{8,10},{9,11},{10,... | collective-permute-start | bytes 221192 | tf_op jit(solution)/shard_map/ppermute | solution.py:146
  13.3 4.6 %copy-start.4 = (s32[4]{0:T(128)S(1)}, s32[4]{0:T(128)}, u32[]{:S(2)}) copy-start(s32[4]{0:T(128)} %sector.1) | copy-start | bytes 52
  13.3 4.6 %copy-start.5 = (s32[4]{0:T(128)S(1)}, s32[4]{0:T(128)}, u32[]{:S(2)}) copy-start(s32[4]{0:T(128)} %width.1) | copy-start | bytes 52
  13.3 10.2 %collective-permute-start.5 = (bf16[2,256,256]{2,1,0:T(8,128)(2,1)S(1)}, bf16[2,256,256]{2,1,0:T(8,128)(2,1)S(1)}, u32[]{:S(2)}, u32[]{:S(2)}) collective-permute-start(bf16[2,256,256]{2,1,0:T(8,128)(2,1)S(1)} %collective-permute-done.1.refs_2_), channel_id=1, source_target_pairs={{0,4},{4,12},{12,8},{8,0},{1,5},{5,13},{13,9},{9,1},{2,6},{6,14},{... | collective-permute-start | bytes 786440 | tf_op jit(solution)/shard_map/ppermute | solution.py:142
  15.9 7.5 %collective-permute-start.4 = (bf16[2,256,256]{2,1,0:T(8,128)(2,1)S(1)}, bf16[2,256,256]{2,1,0:T(8,128)(2,1)S(1)}, u32[]{:S(2)}, u32[]{:S(2)}) collective-permute-start(bf16[2,256,256]{2,1,0:T(8,128)(2,1)S(1)} %collective-permute-done.1.refs_2_), channel_id=1, source_target_pairs={{0,2},{1,3},{2,0},{3,1},{4,6},{5,7},{6,4},{7,5},{8,10},{9,11},{10,... | collective-permute-start | bytes 786440 | tf_op jit(solution)/shard_map/ppermute | solution.py:146
  17.4 6.0 %collective-permute-start.6 = (bf16[256,128]{1,0:T(8,128)(2,1)S(1)}, bf16[256,128]{1,0:T(8,128)(2,1)S(1)}, u32[]{:S(2)}, u32[]{:S(2)}) collective-permute-start(bf16[256,128]{1,0:T(8,128)(2,1)S(1)} %get-tuple-element.56), channel_id=1, source_target_pairs={{0,4},{4,12},{12,8},{8,0},{1,5},{5,13},{13,9},{9,1},{2,6},{6,14},{... | collective-permute-start | bytes 196616 | tf_op jit(solution)/shard_map/ppermute | solution.py:142
  23.5 9.3 %collective-permute-start.8 = (bf16[2,256,256]{2,1,0:T(8,128)(2,1)S(1)}, bf16[2,256,256]{2,1,0:T(8,128)(2,1)S(1)}, u32[]{:S(2)}, u32[]{:S(2)}) collective-permute-start(bf16[2,256,256]{2,1,0:T(8,128)(2,1)S(1)} %collective-permute-done.5.refs_0_), channel_id=1, source_target_pairs={{0,4},{4,12},{12,8},{8,0},{1,5},{5,13},{13,9},{9,1},{2,6},{6,14},{... | collective-permute-start | bytes 786440 | tf_op jit(solution)/shard_map/ppermute | solution.py:142
  25.2 7.6 %collective-permute-start.7 = (bf16[2,256,256]{2,1,0:T(8,128)(2,1)S(1)}, bf16[2,256,256]{2,1,0:T(8,128)(2,1)S(1)}, u32[]{:S(2)}, u32[]{:S(2)}) collective-permute-start(bf16[2,256,256]{2,1,0:T(8,128)(2,1)S(1)} %collective-permute-done.5.refs_0_), channel_id=1, source_target_pairs={{0,2},{1,3},{2,0},{3,1},{4,6},{5,7},{6,4},{7,5},{8,10},{9,11},{10,... | collective-permute-start | bytes 786440 | tf_op jit(solution)/shard_map/ppermute | solution.py:146
  25.7 6.9 %collective-permute-start.10 = (bf16[256,128]{1,0:T(8,128)(2,1)S(1)}, bf16[256,128]{1,0:T(8,128)(2,1)S(1)}, u32[]{:S(2)}, u32[]{:S(2)}) collective-permute-start(bf16[256,128]{1,0:T(8,128)(2,1)S(1)} %get-tuple-element.68), channel_id=1, source_target_pairs={{0,8},{4,0},{12,4},{8,12},{1,9},{5,1},{13,5},{9,13},{2,10},{6,2},{... | collective-permute-start | bytes 196616 | tf_op jit(solution)/shard_map/ppermute | solution.py:142
  26.9 5.7 %collective-permute-start.9 = (bf16[256,128]{1,0:T(8,128)(2,1)S(1)}, bf16[256,128]{1,0:T(8,128)(2,1)S(1)}, u32[]{:S(2)}, u32[]{:S(2)}) collective-permute-start(bf16[256,128]{1,0:T(8,128)(2,1)S(1)} %collective-permute-done.6.refs_5_), channel_id=1, source_target_pairs={{0,1},{1,0},{2,3},{3,2},{4,5},{5,4},{6,7},{7,6},{8,9},{9,8},{10,11... | collective-permute-start | bytes 196616 | tf_op jit(solution)/shard_map/ppermute | solution.py:146
  32.8 8.1 %collective-permute-start.11 = (bf16[2,256,256]{2,1,0:T(8,128)(2,1)S(1)}, bf16[2,256,256]{2,1,0:T(8,128)(2,1)S(1)}, u32[]{:S(2)}, u32[]{:S(2)}) collective-permute-start(bf16[2,256,256]{2,1,0:T(8,128)(2,1)S(1)} %collective-permute-done.8.refs_2_), channel_id=1, source_target_pairs={{0,2},{1,3},{2,0},{3,1},{4,6},{5,7},{6,4},{7,5},{8,10},{9,11},{10,... | collective-permute-start | bytes 786440 | tf_op jit(solution)/shard_map/ppermute | solution.py:146
  32.8 7.3 %collective-permute-start.13 = (bf16[256,256]{1,0:T(8,128)(2,1)S(1)}, bf16[256,256]{1,0:T(8,128)(2,1)S(1)}, u32[]{:S(2)}, u32[]{:S(2)}) collective-permute-start(bf16[256,256]{1,0:T(8,128)(2,1)S(1)} %get-tuple-element.79), channel_id=1, source_target_pairs={{0,12},{4,8},{12,0},{8,4},{1,13},{5,9},{13,1},{9,5},{2,14},{6,10},... | collective-permute-start | bytes 393224 | tf_op jit(solution)/shard_map/ppermute | solution.py:142
  34.9 5.1 %collective-permute-start.12 = (bf16[256,128]{1,0:T(8,128)(2,1)S(1)}, bf16[256,128]{1,0:T(8,128)(2,1)S(1)}, u32[]{:S(2)}, u32[]{:S(2)}) collective-permute-start(bf16[256,128]{1,0:T(8,128)(2,1)S(1)} %collective-permute-done.10.refs_7_), channel_id=1, source_target_pairs={{0,1},{1,0},{2,3},{3,2},{4,5},{5,4},{6,7},{7,6},{8,9},{9,8},{10,11... | collective-permute-start | bytes 196616 | tf_op jit(solution)/shard_map/ppermute | solution.py:146
  40.9 0.7 copy-start.1
  44.0 2.0 %collective-permute-start.14 = (bf16[4,256,256]{2,1,0:T(8,128)(2,1)S(1)}, bf16[4,256,256]{2,1,0:T(8,128)(2,1)S(1)}, u32[]{:S(2)}, u32[]{:S(2)}) collective-permute-start(bf16[4,256,256]{2,1,0:T(8,128)(2,1)S(1)} %get-tuple-element.87.mine), channel_id=1, source_target_pairs={{0,1},{1,0},{2,3},{3,2},{4,5},{5,4},{6,7},{7,6},{8,9},{9,8},{10,11... | collective-permute-start | bytes 1572872 | tf_op jit(solution)/shard_map/ppermute | solution.py:146
  46.4 10.7 %collective-permute-start.15 = (bf16[2,4,64,256]{3,2,1,0:T(8,128)(2,1)S(1)}, bf16[2,4,64,256]{3,2,1,0:T(8,128)(2,1)S(1)}, u32[]{:S(2)}, u32[]{:S(2)}) collective-permute-start(bf16[2,4,64,256]{3,2,1,0:T(8,128)(2,1)S(1)} %get-tuple-element.91), channel_id=1, source_target_pairs={{0,2},{1,3},{2,0},{3,1},{4,6},{5,7},{6,4},{7,5},{8,10},{9,11},{10,... | collective-permute-start | bytes 786440 | tf_op jit(solution)/shard_map/ppermute | solution.py:146
  60.9 2.0 %collective-permute-start.16 = (bf16[4,256,256]{2,1,0:T(8,128)(2,1)S(1)}, bf16[4,256,256]{2,1,0:T(8,128)(2,1)S(1)}, u32[]{:S(2)}, u32[]{:S(2)}) collective-permute-start(bf16[4,256,256]{2,1,0:T(8,128)(2,1)S(1)} %get-tuple-element.99.mine), channel_id=1, source_target_pairs={{0,1},{1,0},{2,3},{3,2},{4,5},{5,4},{6,7},{7,6},{8,9},{9,8},{10,11... | collective-permute-start | bytes 1572872 | tf_op jit(solution)/shard_map/ppermute | solution.py:146
  63.3 11.2 %collective-permute-start.17 = (bf16[2,4,64,256]{3,2,1,0:T(8,128)(2,1)S(1)}, bf16[2,4,64,256]{3,2,1,0:T(8,128)(2,1)S(1)}, u32[]{:S(2)}, u32[]{:S(2)}) collective-permute-start(bf16[2,4,64,256]{3,2,1,0:T(8,128)(2,1)S(1)} %get-tuple-element.102), channel_id=1, source_target_pairs={{0,2},{1,3},{2,0},{3,1},{4,6},{5,7},{6,4},{7,5},{8,10},{9,11},{10,... | collective-permute-start | bytes 786440 | tf_op jit(solution)/shard_map/ppermute | solution.py:146

commit v13 on v12

--- a/solution.py
+++ b/solution.py
@@ -239,8 +239,9 @@
         copy.wait()
 
 
-def table_body(n_blk, terms, sector, width, left_diag, *refs):
-    tails, src, widths, slots, diag = refs[:-4], *refs[-4:]
+def table_body(n_blk, terms, sector, width, left_diag, right_diag, *refs):
+    tails, src, widths, slots, diag, right_out = refs[:-5], *refs[-5:]
+    right_out[...] = right_diag[...]
     n_pair = len(tails)
     rows, cols = tails[0].shape
     own_blk, _ = place_of()
@@ -380,7 +381,8 @@
     left, refs = take(refs, [n_pair] * n_late)
     (right,), refs = take(refs, [n_pair])
     psi, refs = take(refs, counts)
-    raw_in, inter_in, diag, right_diag, part_out, raw_out, left_out, dots_out, inter, sems = refs
+    raw_in, inter_in, diag, right_diag, part_out, raw_out, left_out, dots_out = refs[:8]
+    sends, (inter, sems) = refs[8:-2], refs[-2:]
     copies = keep(left, left_out, sems)
     for j, (given, own) in enumerate(((inter_in, inter), (raw_in, raw_out))):
         copies.append(
@@ -406,34 +408,25 @@
                 image = image + diagonal(diag, right_diag, d, h) * raw
                 sums[0] = sums[0] + fold(raw * raw)
             sums[1] = sums[1] + fold(raw * image)
+        for e, send in enumerate(sends, 2):
+            send_rows(e, send, d, raw_out, part_out)
 
     sum_terms(src, widths, inter, right, part_out, emit)
     spread([whole(x) for x in sums], dots_out)
 
 
-def send_rows(sends, j, d, h, block):
+def send_rows(e, send, d, field, part):
     _, own_op = place_of()
-    step, cols = sends[0].shape[2], block.shape[1]
-    for e, send in enumerate(sends):
-        start = pl.multiple_of((own_op ^ (2 * e)) * step, step)
-        send[j, d, :, h * cols : (h + 1) * cols] = block[pl.ds(start, step)].astype(send.dtype)
+    step = send.shape[2]
+    rows = pl.ds(pl.multiple_of((own_op ^ e) * step, step), step)
+    if e % 2 == 0:
+        send[0, d] = field[d, rows].astype(send.dtype)
+    send[send.shape[0] - 1, d] = part[d, rows]
 
 
 def total_of(mine, other, d, h, cols):
     own = mine[d, :, h * cols : (h + 1) * cols].astype(jnp.float32)
     return own + other[d, :, (1 - h) * cols : (2 - h) * cols].astype(jnp.float32)
-
-
-def sigma_body(mine, other, raw_in, diag, right_diag, sig_out, *sends):
-    n_blk, _, cols = diag.shape
-    for d in range(n_blk):
-        for h in range(2):
-            part = slice(h * cols, (h + 1) * cols)
-            raw = raw_in[d, :, part].astype(jnp.float32)
-            sigma = total_of(mine, other, d, h, cols) + diagonal(diag, right_diag, d, h) * raw
-            sig_out[d, :, part] = sigma
-            send_rows(sends, 0, d, h, raw_in.at[d, :, part])
-            send_rows(sends, 1, d, h, sig_out.at[d, :, part])
 
 
 def norm_theta(parts, count):
@@ -444,8 +437,8 @@
 
 def second_body(n_blk, n_pair, count, src, widths, left_early, left_late, *refs):
     right, refs = refs[:n_pair], refs[n_pair:]
-    parts, raw_in, sig_in, diag, right_diag, f_out, part_out, dots_out = refs[:8]
-    inter, corr, held, sems = refs[8:]
+    parts, raw_in, part_in, other_in, diag, right_diag, dots_out, own_out = refs[:8]
+    sends, (inter, corr, sig, fld, part_out, held, sems) = refs[8:-7], refs[-7:]
     copies = []
     n_early = left_early.shape[0]
     for d in range(n_blk):
@@ -461,7 +454,9 @@
         vv = vc = vs = jnp.zeros((8, cols), jnp.float32)
         for d in range(n_blk):
             vec = raw_in[d, :, part].astype(jnp.float32) * scale
-            sigma = sig_in[d, :, part] * scale
+            sigma = total_of(part_in, other_in, d, h, cols)
+            sigma = (sigma + diagonal(diag, right_diag, d, h) * raw_in[d, :, part].astype(jnp.float32)) * scale
+            sig[d, :, part] = sigma
             den = diagonal(diag, right_diag, d, h) - theta
             item = (sigma - theta * vec) * den / jnp.maximum(den * den, 0.25)
             corr[d, :, part] = item
@@ -473,39 +468,34 @@
         for h in range(2):
             part = slice(h * cols, (h + 1) * cols)
             vec = raw_in[d, :, part].astype(jnp.float32) * scale
-            f_out[d, :, part] = (corr[d, :, part] - along * vec).astype(jnp.bfloat16)
+            fld[d, :, part] = (corr[d, :, part] - along * vec).astype(jnp.bfloat16)
         copies[d].wait()
-        left_products(f_out[d], lambda at: held[d, at // terms], inter.at[d])
+        left_products(fld[d], lambda at: held[d, at // terms], inter.at[d])
     zero = jnp.zeros((8, cols), jnp.float32)
     sums = [zero for _ in range(5)]
 
     def emit(d, total):
         for h in range(2):
             part = slice(h * cols, (h + 1) * cols)
-            fld = f_out[d, :, part].astype(jnp.float32)
+            field = fld[d, :, part].astype(jnp.float32)
             vec = raw_in[d, :, part].astype(jnp.float32) * scale
             image = total[:, part]
             if h == 0:
-                image = image + diagonal(diag, right_diag, d, h) * fld
-                for j, prod in enumerate((fld * fld, vec * fld, fld * sig_in[d, :, part] * scale)):
+                image = image + diagonal(diag, right_diag, d, h) * field
+                for j, prod in enumerate((field * field, vec * field, field * sig[d, :, part])):
                     sums[j] = sums[j] + fold(prod)
             sums[3] = sums[3] + fold(vec * image)
-            sums[4] = sums[4] + fold(fld * image)
-
+            sums[4] = sums[4] + fold(field * image)
+        for e, send in enumerate(sends, 1):
+            send_rows(e, send, d, fld, part_out)
+        rows = pl.ds(pl.multiple_of(own_op * step, step), step)
+        for j, ref in enumerate((raw_in, sig, fld, part_out)):
+            own_out[j, d] = ref[d, rows].astype(own_out.dtype)
+
+    _, own_op = place_of()
+    step = own_out.shape[2]
     sum_terms(src, widths, inter, right, part_out, emit)
-    spread(list(halves[0]) + [along] + [whole(x) for x in sums], dots_out)
-
-
-def image_body(mine, other, f_in, diag, right_diag, *sends):
-    n_blk, _, cols = diag.shape
-    sends, image = sends[:-1], sends[-1]
-    for d in range(n_blk):
-        for h in range(2):
-            part = slice(h * cols, (h + 1) * cols)
-            fld = f_in[d, :, part].astype(jnp.float32)
-            image[h] = total_of(mine, other, d, h, cols) + diagonal(diag, right_diag, d, h) * fld
-            send_rows(sends, 0, d, h, f_in.at[d, :, part])
-            send_rows(sends, 1, d, h, image.at[h])
+    spread(list(halves[0]) + [whole(x) for x in sums], dots_out)
 
 
 def ritz_pair(theta, h_mix, h_two):
@@ -523,20 +513,24 @@
     return sine, jnp.where(upward, -cosine, cosine), 0.5 * (theta + h_two) - 0.5 * size
 
 
-def third_body(n_blk, n_op, count, slots, parts1, parts2, *refs):
-    n_pair = n_op // 2
-    got1, got2 = refs[:n_pair], refs[n_pair : 2 * n_pair]
-    new_out, res_out, energy_out = refs[2 * n_pair :]
-    cols = new_out.shape[2] // n_op
+def third_body(n_blk, n_op, count, slots, parts1, parts2, diag, right_diag, own, *refs):
+    got1, got2 = refs[: n_op - 2], refs[n_op - 2 : 2 * n_op - 3]
+    new_out, res_out, energy_out = refs[2 * n_op - 3 :]
+    step, cols = new_out.shape[1], new_out.shape[2] // n_op
     own_blk, own_op = place_of()
     scale, theta = norm_theta(parts1[...], count)
-    vv, vc, vs, local, ff, vf, fs, vt, ft = (parts2[:, j, :] for j in range(9))
+    pairs = parts2[...].reshape(n_blk * n_op // 2, 2, *parts2.shape[1:])
+    pairs = pairs[:, 0] + pairs[:, 1]
+    vv, vc, vs, ff, vf, fs, vt, ft = (pairs[:, j, :] for j in range(8))
 
     def mean(x):
         return jnp.sum(x, axis=0, keepdims=True) * (1.0 / count)
 
+    def nearest(vv, vc):
+        return vc / jnp.maximum(vv, 1e-30)
+
     along = mean(vc)
-    beta = local - along
+    beta = nearest(vv, vc) - along
     norm_sq = mean(ff + 2.0 * beta * vf + beta * beta * vv)
     unit = lax.rsqrt(jnp.maximum(norm_sq, 0.0) + EPS)
     v_s1 = unit * mean(vt + beta * vs)
@@ -545,17 +539,29 @@
     cv, cu, energy = ritz_pair(theta, 0.5 * (v_s1 + u_s0), u_s1)
     energy_out[0] = jnp.max(energy)
     cu = cu * unit
-    for e in range(n_pair):
-        there = own_op ^ (2 * e)
-        back = parts2[own_blk * n_op + there][3:4] - along
-        on_vec = (cv + cu * back) * scale
+    mine = pl.ds(pl.multiple_of(own_op * step, step), step)
+    for e in range(0, n_op, 2):
+        there = own_blk * n_op + (own_op ^ e)
+        pair = parts2[there] + parts2[own_blk * n_op + (own_op ^ e ^ 1)]
+        on_vec = cv + cu * (nearest(pair[0:1], pair[1:2]) - along)
         for h in range(2):
-            at = pl.multiple_of((there ^ h) * cols, LANES)
-            part = slice(h * cols, (h + 1) * cols)
+            at = pl.multiple_of((own_op ^ e ^ h) * cols, LANES)
+            part, crossed = slice(h * cols, (h + 1) * cols), slice((1 - h) * cols, (2 - h) * cols)
             for d in range(n_blk):
-                blocks = (got[e][j, d, :, part] for got in (got1, got2) for j in range(2))
-                raw, sigma, fld, image = (block.astype(jnp.float32) for block in blocks)
-                newvec = on_vec * raw + cu * fld
+                dmat = diag[d, mine] + right_diag[:, pl.ds(at, cols)]
+                if e:
+                    raw, fld = got1[e - 2][0, d, :, part], got2[e - 1][0, d, :, part]
+                    vec = raw.astype(jnp.float32) * scale
+                    sigma = got1[e - 2][1, d, :, part].astype(jnp.float32)
+                    sigma = sigma + got1[e - 1][0, d, :, crossed].astype(jnp.float32)
+                    sigma = sigma * scale + dmat * vec
+                    image = got2[e - 1][1, d, :, part].astype(jnp.float32)
+                else:
+                    raw, sigma, fld, image = (own[j, d, :, part].astype(jnp.float32) for j in range(4))
+                    vec = raw * scale
+                fld = fld.astype(jnp.float32)
+                image = image + got2[e][0, d, :, crossed].astype(jnp.float32) + dmat * fld
+                newvec = on_vec * vec + cu * fld
                 res = on_vec * sigma + cu * image - energy * newvec
                 new_out[slots[d], :, pl.ds(at, cols)] = newvec.astype(jnp.bfloat16)
                 res_out[slots[d], :, pl.ds(at, cols)] = res.astype(jnp.bfloat16)
@@ -590,11 +596,11 @@
     def table(right):
         return kernel(
             functools.partial(table_body, n_blk, terms),
-            [(slot_sector, SMEM), (sector_width, SMEM), (diag_left, VMEM)]
+            [(slot_sector, SMEM), (sector_width, SMEM), (diag_left, VMEM), (diag_right[None], VMEM)]
             + [(block, VMEM) for block in right],
             [((n_blk * n_pair * terms,), i32, SMEM)]
             + [((n_blk,), i32, SMEM)] * 2
-            + [((n_blk, rows, LANES), f32, VMEM)],
+            + [((n_blk, rows, LANES), f32, VMEM), ((1, n_op * cols), f32, VMEM)],
         )
 
     def inputs(left, psi, those):
@@ -617,19 +623,19 @@
             nbytes=4 << 20,
         )
 
-    left, psi_by, right, (src, widths, slots, diag), (raw_early, inter_early, left_early) = gather(
+    left, psi_by, right, (src, widths, slots, *both), (raw_early, inter_early, left_early) = gather(
         left_ops[:, 0], n_blk, n_op, pack, table, early
     )
     n_early = raw_early.shape[0]
     n_late = n_blk - n_early
     left_ins, psi_ins, counts = inputs(left, psi_by, range(n_early, n_blk))
     right_ins = [(block, VMEM) for block in right]
-    diags = [(diag, VMEM), (diag_right[None], VMEM)]
+    diags = [(x, VMEM) for x in both]
 
     tables = [(src, SMEM), (widths, SMEM)]
     narrow = ((n_blk, rows, 2 * cols), bf16, VMEM)
-    wide = ((n_blk, rows, 2 * cols), f32, VMEM)
-    sends = [((2, n_blk, step, 2 * cols), bf16, VMEM)] * n_pair
+    dots = ((n_dev, 8, LANES), f32, VMEM)
+    sends = [((2 - e % 2, n_blk, step, 2 * cols), bf16, VMEM) for e in range(1, n_op)]
     inter = pltpu.VMEM((n_blk + 1, n_pair * terms, rows, 2 * cols), bf16)
     left_late = (n_late, n_pair, terms, rows, rows)
     cost = dict(flops=2 * n_blk * rows * 2 * cols * terms * n_pair * (rows + 2 * cols), nbytes=6 << 20)
@@ -637,50 +643,43 @@
     def totals(parts):
         return lax.all_to_all(parts, ("blk", "op"), 0, 0, tiled=True)
 
-    def exchange(out):
-        return [out[0]] + [swap(block, 2 * e, n_op) for e, block in enumerate(out[1:], 1)]
-
-    part1, raw, kept, dots1 = kernel(
+    part1, raw, kept, dots1, *out1 = kernel(
         functools.partial(first_body, n_blk, n_pair, counts),
         tables + left_ins + right_ins + psi_ins + [(raw_early, VMEM), (inter_early, VMEM)] + diags,
-        [narrow, narrow, (left_late, bf16, HBM), ((n_dev, 8, LANES), f32, VMEM)],
+        [narrow, narrow, (left_late, bf16, HBM), dots] + sends[1:],
         [inter, pltpu.SemaphoreType.DMA((n_late * n_pair + 2,))],
         **cost,
     )
-    parts1 = totals(dots1)
-    sig, *out1 = kernel(
-        sigma_body,
-        [(x, VMEM) for x in (part1, swap(part1, 1, n_op), raw)] + diags,
-        [wide] + sends,
-        nbytes=4 << 20,
-    )
-    parts1, sig, got1 = lax.optimization_barrier((parts1, sig, exchange(out1)))
-    fld, part2, dots2 = kernel(
+    parts1, other1, got1 = lax.optimization_barrier(
+        (
+            totals(dots1),
+            swap(part1, 1, n_op),
+            [swap(block, e, n_op) for e, block in enumerate(out1, 2)],
+        )
+    )
+    dots2, own, *out2 = kernel(
         functools.partial(second_body, n_blk, n_pair, count),
         tables + [(left_early, HBM), (kept, HBM)] + right_ins
-        + [(x, VMEM) for x in (parts1, raw, sig)] + diags,
-        [narrow, narrow, ((n_dev, 16, LANES), f32, VMEM)],
+        + [(x, VMEM) for x in (parts1, raw, part1, other1)] + diags,
+        [dots, ((4, n_blk, step, 2 * cols), bf16, VMEM)] + sends,
         [
             inter,
             pltpu.VMEM((n_blk, rows, 2 * cols), f32),
+            pltpu.VMEM((n_blk, rows, 2 * cols), f32),
+            pltpu.VMEM((n_blk, rows, 2 * cols), bf16),
+            pltpu.VMEM((n_blk, rows, 2 * cols), bf16),
             pltpu.VMEM((n_blk, *left_late[1:]), bf16),
             pltpu.SemaphoreType.DMA((n_blk,)),
         ],
         **cost,
     )
     parts2 = totals(dots2)
-    out2 = kernel(
-        image_body,
-        [(x, VMEM) for x in (part2, swap(part2, 1, n_op), fld)] + diags,
-        sends,
-        [pltpu.VMEM((2, rows, cols), f32)],
-        nbytes=4 << 20,
-    )
-    got2 = exchange(out2)
+    got2 = [swap(block, e, n_op) for e, block in enumerate(out2, 1)]
     final = ((n_blk, step, n_op * cols), bf16, VMEM)
     new, res, energy = kernel(
         functools.partial(third_body, n_blk, n_op, count),
-        [(slots, SMEM)] + [(x, VMEM) for x in (parts1, parts2, *got1, *got2)],
+        [(slots, SMEM)] + [(x, VMEM) for x in (parts1, parts2)] + diags
+        + [(x, VMEM) for x in (own, *got1, *got2)],
         [final, final, ((1,), f32, SMEM)],
         nbytes=4 << 20,
     )

time: 76.4 us -> 74.7 us (0.978)
  waiting for transfers between devices: 23.7 us -> 19.7 us
  starting transfers between devices: 16.6 us -> 19.5 us
    ppermute x12 -> x14, waiting for transfers between devices: 10.2 us -> 6.38 us  [swap(): return lax.ppermute(block, 'op', [(i, i ^ e) for i in range(n_op)])]
    ppermute x12 -> x14, starting transfers between devices: 5.37 us -> 8.26 us  [swap(): return lax.ppermute(block, 'op', [(i, i ^ e) for i in range(n_op)])]
    pallas_call x8 -> x6, Pallas kernels: 13.7 us -> 13.9 us  [kernel(): pl.pallas_call(body, out_shape=[HBM(shape, dtype) if space == HBM else ja...]
  transfers between devices with their start and end apart: 18 -> 20, of which waited for: 9 -> 7; matrix products, arithmetic and copies ran while one was open for 0% -> 0% of each run, Pallas kernels for 6% -> 7%
where the time goes in v13:
time: 74.7 us; the launch traced here: 74.4 us
  blocking collectives  20.4 us (27%)
  waiting for transfers between devices  19.7 us (26%)
  starting transfers between devices  19.5 us (26%)
  Pallas kernels  13.9 us (19%)
    all_to_all x2, blocking collectives, totals(): return lax.all_to_all(parts, ('blk', 'op'), 0, 0, tiled=True)  20.4 us
    pallas_call x6, Pallas kernels, kernel(): pl.pallas_call(body, out_shape=[HBM(shape, dtype) if space == HBM else ja...  13.9 us
    ppermute x6, waiting for transfers between devices, onward(): return lax.ppermute(block, 'blk', pairs)  13.3 us
    ppermute x6, starting transfers between devices, onward(): return lax.ppermute(block, 'blk', pairs)  11.2 us
    ppermute x14, starting transfers between devices, swap(): return lax.ppermute(block, 'op', [(i, i ^ e) for i in range(n_op)])  8.26 us
    ppermute x14, waiting for transfers between devices, swap(): return lax.ppermute(block, 'op', [(i, i ^ e) for i in range(n_op)])  6.38 us
  transfers between devices with their start and end apart: 20, of which 7 were waited for; matrix products, arithmetic and copies ran while one was open for 0% of the time, Pallas kernels for 7%

profile of v13, /device:TPU:0, one launch (start us, length us, event | category | flops | bytes accessed | tf_op | source)
XLA Modules:
  0.0 74.4 jit_solution(17778500210887415005)
XLA Ops:
  0.6 0.0 copy-start.3
  0.6 3.1 %collective-permute-start.1 = (bf16[2,256,256]{2,1,0:T(8,128)(2,1)}, bf16[2,256,256]{2,1,0:T(8,128)(2,1)S(1)}, u32[]{:S(2)}, u32[]{:S(2)}) collective-permute-start(bf16[2,256,256]{2,1,0:T(8,128)(2,1)} %bitcast.2), channel_id=1, source_target_pairs={{0,4},{4,12},{12,8},{8,0},{1,5},{5,13},{13,9},{9,1},{2,6},{6,14},{... | collective-permute-start | bytes 786440 | tf_op jit(solution)/shard_map/ppermute | solution.py:142
  3.7 1.5 %collective-permute-start = (bf16[2,256,256]{2,1,0:T(8,128)(2,1)}, bf16[2,256,256]{2,1,0:T(8,128)(2,1)S(1)}, u32[]{:S(2)}, u32[]{:S(2)}) collective-permute-start(bf16[2,256,256]{2,1,0:T(8,128)(2,1)} %bitcast.3), channel_id=1, source_target_pairs={{0,2},{1,3},{2,0},{3,1},{4,6},{5,7},{6,4},{7,5},{8,10},{9,11},{10,... | collective-permute-start | bytes 786440 | tf_op jit(solution)/shard_map/ppermute | solution.py:146
  5.2 0.0 copy-done.3
  5.2 0.0 collective-permute-start.2
  5.2 1.1 %collective-permute-done.2._ = s32[2]{0:T(128)S(1)} collective-permute-done((s32[2]{0:T(128)S(1)}, s32[2]{0:T(128)S(1)}, u32[]{:S(2)}, u32[]{:S(2)}) %collective-permute-start.2) | collective-permute-done | bytes 40 | tf_op jit(solution)/shard_map/ppermute | solution.py:146
  6.3 0.0 copy-start
  6.3 1.9 %shard_map.103 = (bf16[256,256]{1,0:T(8,128)(2,1)S(1)}, bf16[256,128]{1,0:T(8,128)(2,1)S(1)}, bf16[256,256]{1,0:T(8,128)(2,1)S(1)}, bf16[256,128]{1,0:T(8,128)(2...) custom-call(s32[2]{0:T(128)S(1)} %copy-done.3, s32[2]{0:T(128)S(1)} %collective-permute-done.2._, ...), custom_call_target="tpu_custom_call" | custom-call | bytes 1048576 | tf_op jit(solution)/shard_map/pallas_call | solution.py:113
  8.2 0.0 copy-start.1
  8.3 0.6 collective-permute-start.3
  8.9 4.4 %collective-permute-done.3.refs_1_.refs_5_ = bf16[144,256]{1,0:T(8,128)(2,1)S(1)} collective-permute-done((bf16[144,256]{1,0:T(8,128)(2,1)S(1)}, bf16[144,256]{1,0:T(8,128)(2,1)S(1)}, u32[]{:S(2)}, u32[]{:S(2)}) %collective-permute-start.3) | collective-permute-done | bytes 73760 | tf_op jit(solution)/shard_map/ppermute | solution.py:146
  13.3 0.0 collective-permute-done.1.refs_2_
  13.3 0.0 collective-permute-done.refs_1_
  13.3 0.0 copy-start.2
  13.3 2.6 %collective-permute-start.5 = (bf16[2,256,256]{2,1,0:T(8,128)(2,1)S(1)}, bf16[2,256,256]{2,1,0:T(8,128)(2,1)S(1)}, u32[]{:S(2)}, u32[]{:S(2)}) collective-permute-start(bf16[2,256,256]{2,1,0:T(8,128)(2,1)S(1)} %collective-permute-done.1.refs_2_), channel_id=1, source_target_pairs={{0,4},{4,12},{12,8},{8,0},{1,5},{5,13},{13,9},{9,1},{2,6},{6,14},{... | collective-permute-start | bytes 786440 | tf_op jit(solution)/shard_map/ppermute | solution.py:142
  15.9 1.5 %collective-permute-start.4 = (bf16[2,256,256]{2,1,0:T(8,128)(2,1)S(1)}, bf16[2,256,256]{2,1,0:T(8,128)(2,1)S(1)}, u32[]{:S(2)}, u32[]{:S(2)}) collective-permute-start(bf16[2,256,256]{2,1,0:T(8,128)(2,1)S(1)} %collective-permute-done.1.refs_2_), channel_id=1, source_target_pairs={{0,2},{1,3},{2,0},{3,1},{4,6},{5,7},{6,4},{7,5},{8,10},{9,11},{10,... | collective-permute-start | bytes 786440 | tf_op jit(solution)/shard_map/ppermute | solution.py:146
  17.4 0.0 copy-start.4
  17.4 0.0 copy-start.5
  17.4 0.4 collective-permute-start.6
  17.9 0.0 copy-done.1
  17.9 0.0 copy-done.2
  17.9 0.2 copy-done.4
  18.1 0.0 copy-done.5
  18.1 1.3 %shard_map.104 = (s32[16]{0:T(128)S(1)}, s32[4]{0:T(128)S(1)}, s32[4]{0:T(128)S(1)}, f32[4,256,128]{2,1,0:T(8,128)S(1)}, f32[1,512]{1,0:T(1,128)S(1)}) custom-call(s32[4]{0:T(128)S(1)} %copy-done.4, s32[4]{0:T(128)S(1)} %copy-done.5, f32[4,256]{1,0:T(4,128)S(1)} %copy-done.1, f32[1,512]{1,0:T(1,128)S(1)} %bitcast.5, ...), custom_call_target="tpu_custom_call" | custom-call | tf_op jit(solution)/shard_map/pallas_call | solution.py:113
  19.4 4.0 %collective-permute-done.6.refs_5_ = bf16[256,128]{1,0:T(8,128)(2,1)S(1)} collective-permute-done((bf16[256,128]{1,0:T(8,128)(2,1)S(1)}, bf16[256,128]{1,0:T(8,128)(2,1)S(1)}, u32[]{:S(2)}, u32[]{:S(2)}) %collective-permute-start.6) | collective-permute-done | bytes 65568 | tf_op jit(solution)/shard_map/ppermute | solution.py:142
  23.5 0.0 collective-permute-done.5.refs_0_
  23.5 0.0 collective-permute-done.4.refs_3_
  23.5 1.7 %collective-permute-start.8 = (bf16[2,256,256]{2,1,0:T(8,128)(2,1)S(1)}, bf16[2,256,256]{2,1,0:T(8,128)(2,1)S(1)}, u32[]{:S(2)}, u32[]{:S(2)}) collective-permute-start(bf16[2,256,256]{2,1,0:T(8,128)(2,1)S(1)} %collective-permute-done.5.refs_0_), channel_id=1, source_target_pairs={{0,4},{4,12},{12,8},{8,0},{1,5},{5,13},{13,9},{9,1},{2,6},{6,14},{... | collective-permute-start | bytes 786440 | tf_op jit(solution)/shard_map/ppermute | solution.py:142
  25.2 0.5 collective-permute-start.7
  25.7 1.2 %collective-permute-start.10 = (bf16[256,128]{1,0:T(8,128)(2,1)S(1)}, bf16[256,128]{1,0:T(8,128)(2,1)S(1)}, u32[]{:S(2)}, u32[]{:S(2)}) collective-permute-start(bf16[256,128]{1,0:T(8,128)(2,1)S(1)} %get-tuple-element.70), channel_id=1, source_target_pairs={{0,8},{4,0},{12,4},{8,12},{1,9},{5,1},{13,5},{9,13},{2,10},{6,2},{... | collective-permute-start | bytes 196616 | tf_op jit(solution)/shard_map/ppermute | solution.py:142
  26.9 0.0 collective-permute-start.9
  26.9 5.7 %collective-permute-done.10.refs_7_ = bf16[256,128]{1,0:T(8,128)(2,1)S(1)} collective-permute-done((bf16[256,128]{1,0:T(8,128)(2,1)S(1)}, bf16[256,128]{1,0:T(8,128)(2,1)S(1)}, u32[]{:S(2)}, u32[]{:S(2)}) %collective-permute-start.10) | collective-permute-done | bytes 65568 | tf_op jit(solution)/shard_map/ppermute | solution.py:142
  32.6 0.0 collective-permute-done.9.refs_6_
  32.6 0.1 collective-permute-done.8.refs_2_
  32.7 0.0 collective-permute-done.7.refs_1_
  32.7 0.0 collective-permute-start.11
  32.7 2.2 %collective-permute-start.13 = (bf16[256,256]{1,0:T(8,128)(2,1)S(1)}, bf16[256,256]{1,0:T(8,128)(2,1)S(1)}, u32[]{:S(2)}, u32[]{:S(2)}) collective-permute-start(bf16[256,256]{1,0:T(8,128)(2,1)S(1)} %get-tuple-element.81), channel_id=1, source_target_pairs={{0,12},{4,8},{12,0},{8,4},{1,13},{5,9},{13,1},{9,5},{2,14},{6,10},... | collective-permute-start | bytes 393224 | tf_op jit(solution)/shard_map/ppermute | solution.py:142
  34.9 0.0 collective-permute-start.12
  34.9 0.0 copy-done
  34.9 1.7 %shard_map.105 = (bf16[2,256,256]{2,1,0:T(8,128)(2,1)S(1)}, bf16[2,4,256,256]{3,2,1,0:T(8,128)(2,1)S(1)}, bf16[2,2,2,256,256]{4,3,2,1,0:T(8,128)(2,1)}) custom-call(s32[4]{0:T(128)S(1)} %get-tuple-element.67.widths, bf16[2,256,256]{2,1,0:T(8,128)(2,1)S(1)} %bitcast.4, bf16[2,256,256]{2,1,0:T(8,128)(2,1)S(1)} %collective-permute-done.refs_1_, ...), custom_call_target="tpu_custom_call" | custom-call | flops 268435456 | bytes 4194304 | tf_op jit(solution)/shard_map/pallas_call | solution.py:113
  36.6 3.5 %collective-permute-done.13.refs_6_ = bf16[256,256]{1,0:T(8,128)(2,1)S(1)} collective-permute-done((bf16[256,256]{1,0:T(8,128)(2,1)S(1)}, bf16[256,256]{1,0:T(8,128)(2,1)S(1)}, u32[]{:S(2)}, u32[]{:S(2)}) %collective-permute-start.13) | collective-permute-done | bytes 131104 | tf_op jit(solution)/shard_map/ppermute | solution.py:142
  40.0 0.0 collective-permute-done.12.refs_8_
  40.0 0.8 %collective-permute-done.11.refs_3_ = bf16[2,256,256]{2,1,0:T(8,128)(2,1)S(1)} collective-permute-done((bf16[2,256,256]{2,1,0:T(8,128)(2,1)S(1)}, bf16[2,256,256]{2,1,0:T(8,128)(2,1)S(1)}, u32[]{:S(2)}, u32[]{:S(2)}) %collective-permute-start.11) | collective-permute-done | bytes 262176 | tf_op jit(solution)/shard_map/ppermute | solution.py:146
  40.8 2.4 %shard_map.106 = (bf16[4,256,256]{2,1,0:T(8,128)(2,1)S(1)}, bf16[4,256,256]{2,1,0:T(8,128)(2,1)S(1)}, bf16[2,2,2,256,256]{4,3,2,1,0:T(8,128)(2,1)}, f32[16,8,128...) custom-call(s32[16]{0:T(128)S(1)} %get-tuple-element.66.src, ...), custom_call_target="tpu_custom_call" | custom-call | flops 1073741824 | bytes 6291456 | tf_op jit(solution)/shard_map/pallas_call | solution.py:113
  43.3 0.1 collective-permute-start.14
  43.4 0.9 %collective-permute-start.15 = (bf16[2,4,64,256]{3,2,1,0:T(8,128)(2,1)S(1)}, bf16[2,4,64,256]{3,2,1,0:T(8,128)(2,1)S(1)}, u32[]{:S(2)}, u32[]{:S(2)}) collective-permute-start(bf16[2,4,64,256]{3,2,1,0:T(8,128)(2,1)S(1)} %get-tuple-element.91), channel_id=1, source_target_pairs={{0,2},{1,3},{2,0},{3,1},{4,6},{5,7},{6,4},{7,5},{8,10},{9,11},{10,... | collective-permute-start | bytes 786440 | tf_op jit(solution)/shard_map/ppermute | solution.py:146
  44.3 0.9 %collective-permute-start.16 = (bf16[1,4,64,256]{3,2,1,0:T(8,128)(2,1)S(1)}, bf16[1,4,64,256]{3,2,1,0:T(8,128)(2,1)S(1)}, u32[]{:S(2)}, u32[]{:S(2)}) collective-permute-start(bf16[1,4,64,256]{3,2,1,0:T(8,128)(2,1)S(1)} %get-tuple-element.92), channel_id=1, source_target_pairs={{0,3},{1,2},{2,1},{3,0},{4,7},{5,6},{6,5},{7,4},{8,11},{9,10},{10,... | collective-permute-start | bytes 393224 | tf_op jit(solution)/shard_map/ppermute | solution.py:146
  45.2 10.3 %all_to_all.10.refs_2_.parts1 = f32[16,8,128]{2,1,0:T(8,128)S(1)} all-to-all(f32[16,8,128]{2,1,0:T(8,128)S(1)} %get-tuple-element.89), channel_id=1, replica_groups=mesh['grp'=2,'blk'=4,'op'=4] {'blk','op'}, dimensions={0} | all-to-all | bytes 131072 | tf_op jit(solution)/shard_map/all_to_all | solution.py:644
  55.6 0.0 collective-permute-done.16.refs_1_
  55.6 0.0 collective-permute-done.15.refs_0_
  55.6 0.0 collective-permute-done.14.refs_5_
  55.6 4.7 %shard_map.107 = (f32[16,8,128]{2,1,0:T(8,128)S(1)}, bf16[4,4,64,256]{3,2,1,0:T(8,128)(2,1)S(1)}, bf16[1,4,64,256]{3,2,1,0:T(8,128)(2,1)S(1)}, bf16[2,4,64,256]{...) custom-call(s32[16]{0:T(128)S(1)} %get-tuple-element.66.src, s32[4]{0:T(128)S(1)} %get-tuple-element.67.widths, ...), custom_call_target="tpu_custom_call" | custom-call | flops 1073741824 | bytes 6291456 | tf_op jit(solution)/shard_map/pallas_call | solution.py:113
  60.3 1.0 %collective-permute-start.18 = (bf16[2,4,64,256]{3,2,1,0:T(8,128)(2,1)S(1)}, bf16[2,4,64,256]{3,2,1,0:T(8,128)(2,1)S(1)}, u32[]{:S(2)}, u32[]{:S(2)}) collective-permute-start(bf16[2,4,64,256]{3,2,1,0:T(8,128)(2,1)S(1)} %get-tuple-element.103), channel_id=1, source_target_pairs={{0,2},{1,3},{2,0},{3,1},{4,6},{5,7},{6,4},{7,5},{8,10},{9,11},{10,... | collective-permute-start | bytes 786440 | tf_op jit(solution)/shard_map/ppermute | solution.py:146
  61.3 0.0 collective-permute-start.17
  61.3 1.3 %collective-permute-start.19 = (bf16[1,4,64,256]{3,2,1,0:T(8,128)(2,1)S(1)}, bf16[1,4,64,256]{3,2,1,0:T(8,128)(2,1)S(1)}, u32[]{:S(2)}, u32[]{:S(2)}) collective-permute-start(bf16[1,4,64,256]{3,2,1,0:T(8,128)(2,1)S(1)} %get-tuple-element.104), channel_id=1, source_target_pairs={{0,3},{1,2},{2,1},{3,0},{4,7},{5,6},{6,5},{7,4},{8,11},{9,10},{10,... | collective-permute-start | bytes 393224 | tf_op jit(solution)/shard_map/ppermute | solution.py:146
  62.5 10.1 %all_to_all.11.parts2 = f32[16,8,128]{2,1,0:T(8,128)S(1)} all-to-all(f32[16,8,128]{2,1,0:T(8,128)S(1)} %get-tuple-element.98), channel_id=1, replica_groups=mesh['grp'=2,'blk'=4,'op'=4] {'blk','op'}, dimensions={0} | all-to-all | bytes 131072 | tf_op jit(solution)/shard_map/all_to_all | solution.py:644
  72.6 0.0 collective-permute-done.17.refs_2_
  72.6 0.0 collective-permute-done.19.refs_4_
  72.6 0.0 collective-permute-done.18.refs_3_
  72.6 1.8 %shard_map.108 = (bf16[4,64,512]{2,1,0:T(8,128)(2,1)}, bf16[4,64,512]{2,1,0:T(8,128)(2,1)}, f32[1]{0:T(128)}) custom-call(s32[4]{0:T(128)S(1)} %get-tuple-element.65.slots, f32[16,8,128]{2,1,0:T(8,128)S(1)} %all_to_all.10.refs_2_.parts1, f32[16,8,128]{2,1,0:T(8,128)S(1)} %all_to_all.11.parts2, f32[4,256,128]{2,1,0:T(8,128)S(1)} %get-tuple-element.87.refs_11_.refs_6_.diag, ...), custom_call_target="tpu_custom_call" | custom-call | bytes 4194304 | tf_op jit(solution)/shard_map/pallas_call | solution.py:113
Async XLA Ops:
  0.6 4.6 %copy-start.3 = (s32[2]{0:T(128)S(1)}, s32[2]{0:T(128)}, u32[]{:S(2)}) copy-start(s32[2]{0:T(128)} %shift.1) | copy-start | bytes 28
  0.6 12.6 %collective-permute-start.1 = (bf16[2,256,256]{2,1,0:T(8,128)(2,1)}, bf16[2,256,256]{2,1,0:T(8,128)(2,1)S(1)}, u32[]{:S(2)}, u32[]{:S(2)}) collective-permute-start(bf16[2,256,256]{2,1,0:T(8,128)(2,1)} %bitcast.2), channel_id=1, source_target_pairs={{0,4},{4,12},{12,8},{8,0},{1,5},{5,13},{13,9},{9,1},{2,6},{6,14},{... | collective-permute-start | bytes 786440 | tf_op jit(solution)/shard_map/ppermute | solution.py:142
  3.7 9.6 %collective-permute-start = (bf16[2,256,256]{2,1,0:T(8,128)(2,1)}, bf16[2,256,256]{2,1,0:T(8,128)(2,1)S(1)}, u32[]{:S(2)}, u32[]{:S(2)}) collective-permute-start(bf16[2,256,256]{2,1,0:T(8,128)(2,1)} %bitcast.3), channel_id=1, source_target_pairs={{0,2},{1,3},{2,0},{3,1},{4,6},{5,7},{6,4},{7,5},{8,10},{9,11},{10,... | collective-permute-start | bytes 786440 | tf_op jit(solution)/shard_map/ppermute | solution.py:146
  5.2 1.1 %collective-permute-start.2 = (s32[2]{0:T(128)S(1)}, s32[2]{0:T(128)S(1)}, u32[]{:S(2)}, u32[]{:S(2)}) collective-permute-start(s32[2]{0:T(128)S(1)} %copy-done.3), channel_id=1, source_target_pairs={{0,1},{1,0},{2,3},{3,2},{4,5},{5,4},{6,7},{7,6},{8,9},{9,8},{10,11... | collective-permute-start | bytes 32 | tf_op jit(solution)/shard_map/ppermute | solution.py:146
  6.3 28.6 %copy-start = (bf16[2,1,256,256]{3,2,1,0:T(8,128)(2,1)S(1)}, bf16[2,1,256,256]{3,2,1,0:T(8,128)(2,1)}, u32[]{:S(2)}) copy-start(bf16[2,1,256,256]{3,2,1,0:T(8,128)(2,1)} %param.9) | copy-start | bytes 786436
  8.2 9.6 %copy-start.1 = (f32[4,256]{1,0:T(4,128)S(1)}, f32[4,256]{1,0:T(4,128)}, u32[]{:S(2)}) copy-start(f32[4,256]{1,0:T(4,128)} %left_diag.1) | copy-start | bytes 12292
  8.3 5.0 %collective-permute-start.3 = (bf16[144,256]{1,0:T(8,128)(2,1)S(1)}, bf16[144,256]{1,0:T(8,128)(2,1)S(1)}, u32[]{:S(2)}, u32[]{:S(2)}) collective-permute-start(bf16[144,256]{1,0:T(8,128)(2,1)S(1)} %get-tuple-element.55), channel_id=1, source_target_pairs={{0,2},{1,3},{2,0},{3,1},{4,6},{5,7},{6,4},{7,5},{8,10},{9,11},{10,... | collective-permute-start | bytes 221192 | tf_op jit(solution)/shard_map/ppermute | solution.py:146
  13.3 4.6 %copy-start.2 = (f32[512]{0:T(512)S(1)}, f32[512]{0:T(512)}, u32[]{:S(2)}) copy-start(f32[512]{0:T(512)} %param.15) | copy-start | bytes 6148
  13.3 10.2 %collective-permute-start.5 = (bf16[2,256,256]{2,1,0:T(8,128)(2,1)S(1)}, bf16[2,256,256]{2,1,0:T(8,128)(2,1)S(1)}, u32[]{:S(2)}, u32[]{:S(2)}) collective-permute-start(bf16[2,256,256]{2,1,0:T(8,128)(2,1)S(1)} %collective-permute-done.1.refs_2_), channel_id=1, source_target_pairs={{0,4},{4,12},{12,8},{8,0},{1,5},{5,13},{13,9},{9,1},{2,6},{6,14},{... | collective-permute-start | bytes 786440 | tf_op jit(solution)/shard_map/ppermute | solution.py:142
  15.9 7.5 %collective-permute-start.4 = (bf16[2,256,256]{2,1,0:T(8,128)(2,1)S(1)}, bf16[2,256,256]{2,1,0:T(8,128)(2,1)S(1)}, u32[]{:S(2)}, u32[]{:S(2)}) collective-permute-start(bf16[2,256,256]{2,1,0:T(8,128)(2,1)S(1)} %collective-permute-done.1.refs_2_), channel_id=1, source_target_pairs={{0,2},{1,3},{2,0},{3,1},{4,6},{5,7},{6,4},{7,5},{8,10},{9,11},{10,... | collective-permute-start | bytes 786440 | tf_op jit(solution)/shard_map/ppermute | solution.py:146
  17.4 0.7 copy-start.4
  17.4 0.7 copy-start.5
  17.4 6.0 %collective-permute-start.6 = (bf16[256,128]{1,0:T(8,128)(2,1)S(1)}, bf16[256,128]{1,0:T(8,128)(2,1)S(1)}, u32[]{:S(2)}, u32[]{:S(2)}) collective-permute-start(bf16[256,128]{1,0:T(8,128)(2,1)S(1)} %get-tuple-element.57), channel_id=1, source_target_pairs={{0,4},{4,12},{12,8},{8,0},{1,5},{5,13},{13,9},{9,1},{2,6},{6,14},{... | collective-permute-start | bytes 196616 | tf_op jit(solution)/shard_map/ppermute | solution.py:142
  23.5 9.3 %collective-permute-start.8 = (bf16[2,256,256]{2,1,0:T(8,128)(2,1)S(1)}, bf16[2,256,256]{2,1,0:T(8,128)(2,1)S(1)}, u32[]{:S(2)}, u32[]{:S(2)}) collective-permute-start(bf16[2,256,256]{2,1,0:T(8,128)(2,1)S(1)} %collective-permute-done.5.refs_0_), channel_id=1, source_target_pairs={{0,4},{4,12},{12,8},{8,0},{1,5},{5,13},{13,9},{9,1},{2,6},{6,14},{... | collective-permute-start | bytes 786440 | tf_op jit(solution)/shard_map/ppermute | solution.py:142
  25.2 7.6 %collective-permute-start.7 = (bf16[2,256,256]{2,1,0:T(8,128)(2,1)S(1)}, bf16[2,256,256]{2,1,0:T(8,128)(2,1)S(1)}, u32[]{:S(2)}, u32[]{:S(2)}) collective-permute-start(bf16[2,256,256]{2,1,0:T(8,128)(2,1)S(1)} %collective-permute-done.5.refs_0_), channel_id=1, source_target_pairs={{0,2},{1,3},{2,0},{3,1},{4,6},{5,7},{6,4},{7,5},{8,10},{9,11},{10,... | collective-permute-start | bytes 786440 | tf_op jit(solution)/shard_map/ppermute | solution.py:146
  25.7 6.9 %collective-permute-start.10 = (bf16[256,128]{1,0:T(8,128)(2,1)S(1)}, bf16[256,128]{1,0:T(8,128)(2,1)S(1)}, u32[]{:S(2)}, u32[]{:S(2)}) collective-permute-start(bf16[256,128]{1,0:T(8,128)(2,1)S(1)} %get-tuple-element.70), channel_id=1, source_target_pairs={{0,8},{4,0},{12,4},{8,12},{1,9},{5,1},{13,5},{9,13},{2,10},{6,2},{... | collective-permute-start | bytes 196616 | tf_op jit(solution)/shard_map/ppermute | solution.py:142
  26.9 5.7 %collective-permute-start.9 = (bf16[256,128]{1,0:T(8,128)(2,1)S(1)}, bf16[256,128]{1,0:T(8,128)(2,1)S(1)}, u32[]{:S(2)}, u32[]{:S(2)}) collective-permute-start(bf16[256,128]{1,0:T(8,128)(2,1)S(1)} %collective-permute-done.6.refs_5_), channel_id=1, source_target_pairs={{0,1},{1,0},{2,3},{3,2},{4,5},{5,4},{6,7},{7,6},{8,9},{9,8},{10,11... | collective-permute-start | bytes 196616 | tf_op jit(solution)/shard_map/ppermute | solution.py:146
  32.7 8.1 %collective-permute-start.11 = (bf16[2,256,256]{2,1,0:T(8,128)(2,1)S(1)}, bf16[2,256,256]{2,1,0:T(8,128)(2,1)S(1)}, u32[]{:S(2)}, u32[]{:S(2)}) collective-permute-start(bf16[2,256,256]{2,1,0:T(8,128)(2,1)S(1)} %collective-permute-done.8.refs_2_), channel_id=1, source_target_pairs={{0,2},{1,3},{2,0},{3,1},{4,6},{5,7},{6,4},{7,5},{8,10},{9,11},{10,... | collective-permute-start | bytes 786440 | tf_op jit(solution)/shard_map/ppermute | solution.py:146
  32.7 7.3 %collective-permute-start.13 = (bf16[256,256]{1,0:T(8,128)(2,1)S(1)}, bf16[256,256]{1,0:T(8,128)(2,1)S(1)}, u32[]{:S(2)}, u32[]{:S(2)}) collective-permute-start(bf16[256,256]{1,0:T(8,128)(2,1)S(1)} %get-tuple-element.81), channel_id=1, source_target_pairs={{0,12},{4,8},{12,0},{8,4},{1,13},{5,9},{13,1},{9,5},{2,14},{6,10},... | collective-permute-start | bytes 393224 | tf_op jit(solution)/shard_map/ppermute | solution.py:142
  34.9 5.1 %collective-permute-start.12 = (bf16[256,128]{1,0:T(8,128)(2,1)S(1)}, bf16[256,128]{1,0:T(8,128)(2,1)S(1)}, u32[]{:S(2)}, u32[]{:S(2)}) collective-permute-start(bf16[256,128]{1,0:T(8,128)(2,1)S(1)} %collective-permute-done.10.refs_7_), channel_id=1, source_target_pairs={{0,1},{1,0},{2,3},{3,2},{4,5},{5,4},{6,7},{7,6},{8,9},{9,8},{10,11... | collective-permute-start | bytes 196616 | tf_op jit(solution)/shard_map/ppermute | solution.py:146
  43.3 12.3 %collective-permute-start.14 = (bf16[4,256,256]{2,1,0:T(8,128)(2,1)S(1)}, bf16[4,256,256]{2,1,0:T(8,128)(2,1)S(1)}, u32[]{:S(2)}, u32[]{:S(2)}) collective-permute-start(bf16[4,256,256]{2,1,0:T(8,128)(2,1)S(1)} %get-tuple-element.90.refs_4_), channel_id=1, source_target_pairs={{0,1},{1,0},{2,3},{3,2},{4,5},{5,4},{6,7},{7,6},{8,9},{9,8},{10,11... | collective-permute-start | bytes 1572872 | tf_op jit(solution)/shard_map/ppermute | solution.py:146
  43.4 12.2 %collective-permute-start.15 = (bf16[2,4,64,256]{3,2,1,0:T(8,128)(2,1)S(1)}, bf16[2,4,64,256]{3,2,1,0:T(8,128)(2,1)S(1)}, u32[]{:S(2)}, u32[]{:S(2)}) collective-permute-start(bf16[2,4,64,256]{3,2,1,0:T(8,128)(2,1)S(1)} %get-tuple-element.91), channel_id=1, source_target_pairs={{0,2},{1,3},{2,0},{3,1},{4,6},{5,7},{6,4},{7,5},{8,10},{9,11},{10,... | collective-permute-start | bytes 786440 | tf_op jit(solution)/shard_map/ppermute | solution.py:146
  44.3 11.3 %collective-permute-start.16 = (bf16[1,4,64,256]{3,2,1,0:T(8,128)(2,1)S(1)}, bf16[1,4,64,256]{3,2,1,0:T(8,128)(2,1)S(1)}, u32[]{:S(2)}, u32[]{:S(2)}) collective-permute-start(bf16[1,4,64,256]{3,2,1,0:T(8,128)(2,1)S(1)} %get-tuple-element.92), channel_id=1, source_target_pairs={{0,3},{1,2},{2,1},{3,0},{4,7},{5,6},{6,5},{7,4},{8,11},{9,10},{10,... | collective-permute-start | bytes 393224 | tf_op jit(solution)/shard_map/ppermute | solution.py:146
  60.3 12.3 %collective-permute-start.18 = (bf16[2,4,64,256]{3,2,1,0:T(8,128)(2,1)S(1)}, bf16[2,4,64,256]{3,2,1,0:T(8,128)(2,1)S(1)}, u32[]{:S(2)}, u32[]{:S(2)}) collective-permute-start(bf16[2,4,64,256]{3,2,1,0:T(8,128)(2,1)S(1)} %get-tuple-element.103), channel_id=1, source_target_pairs={{0,2},{1,3},{2,0},{3,1},{4,6},{5,7},{6,4},{7,5},{8,10},{9,11},{10,... | collective-permute-start | bytes 786440 | tf_op jit(solution)/shard_map/ppermute | solution.py:146
  61.3 11.3 %collective-permute-start.17 = (bf16[1,4,64,256]{3,2,1,0:T(8,128)(2,1)S(1)}, bf16[1,4,64,256]{3,2,1,0:T(8,128)(2,1)S(1)}, u32[]{:S(2)}, u32[]{:S(2)}) collective-permute-start(bf16[1,4,64,256]{3,2,1,0:T(8,128)(2,1)S(1)} %get-tuple-element.102), channel_id=1, source_target_pairs={{0,1},{1,0},{2,3},{3,2},{4,5},{5,4},{6,7},{7,6},{8,9},{9,8},{10,11... | collective-permute-start | bytes 393224 | tf_op jit(solution)/shard_map/ppermute | solution.py:146
  61.3 11.3 %collective-permute-start.19 = (bf16[1,4,64,256]{3,2,1,0:T(8,128)(2,1)S(1)}, bf16[1,4,64,256]{3,2,1,0:T(8,128)(2,1)S(1)}, u32[]{:S(2)}, u32[]{:S(2)}) collective-permute-start(bf16[1,4,64,256]{3,2,1,0:T(8,128)(2,1)S(1)} %get-tuple-element.104), channel_id=1, source_target_pairs={{0,3},{1,2},{2,1},{3,0},{4,7},{5,6},{6,5},{7,4},{8,11},{9,10},{10,... | collective-permute-start | bytes 393224 | tf_op jit(solution)/shard_map/ppermute | solution.py:146

commit v14 on v13

--- a/solution.py
+++ b/solution.py
@@ -149,42 +149,42 @@
 def gather(own, n_blk, n_op, pack, table, early):
     bits = [1 << b for b in reversed(range(1, n_op.bit_length() - 1))]
     order = sorted(range(1, n_blk), key=lambda d: min(d, n_blk - d))
-    left, psi, right, tables, columns = {(0, 0): own}, {}, None, None, None
-    waiting, late, made = {(0, 0): 0}, None, None
-    for j in range(n_blk + len(bits)):
-        new, moved = {}, {}
-        for (d, e), done in waiting.items():
-            if e == 0 and d + 1 < n_blk:
-                new[d + 1, 0] = onward(left[d, 0], 1, n_blk), 0
-            for b in range(done, len(bits)):
-                new[d, e ^ bits[b]] = swap(left[d, e], bits[b], n_op), b + 1
-        kept = {key: block for key, (block, _) in new.items()}
-        if late is not None:
-            moved["psi"] = late
-        if j == 0:
-            columns, packed = pack()
-            moved["right"] = [packed[0]]
-            moved["right"] += [swap(part, 2 * e, n_op) for e, part in enumerate(packed[1:], 1)]
-        if j == 1:
-            moved["tables"] = table(right)
-        if j == n_blk - 1 and j >= len(bits) + 1:
-            n_early = min(2, n_blk - 1)
-            psi[0] = [columns[0]]
-            moved["early"] = early(left, psi, n_early, tables)
-        if 2 <= j < n_blk:
-            moved["other"] = swap(psi[order[j - 2]][0], 1, n_op)
-        late = onward(columns[order[j]], order[j], n_blk) if j < n_blk - 1 else None
-        if not kept and not moved:
-            break
-        waiting = {key: done for key, (_, done) in new.items()}
-        kept, moved = lax.optimization_barrier((kept, moved))
-        left.update(kept)
-        right, tables = moved.get("right", right), moved.get("tables", tables)
-        made = moved.get("early", made)
-        if "psi" in moved:
-            psi[order[j - 1]] = [moved["psi"]]
-        if "other" in moved:
-            psi[order[j - 2]].append(moved["other"])
+    columns, packed = pack()
+    (came, swapped), columns, right = lax.optimization_barrier(
+        (
+            (onward(own, 1, n_blk), [swap(own, bit, n_op) for bit in bits[:1]]),
+            columns,
+            [packed[0]] + [swap(part, 2 * e, n_op) for e, part in enumerate(packed[1:], 1)],
+        )
+    )
+    left, psi = {(0, 0): [own], (1, 0): [came]}, {0: columns[0]}
+    for bit in bits[:1]:
+        left[0, bit] = swapped
+    half = max(own.shape[0] // 2, 1)
+    parts = [came[at : at + half] for at in range(0, own.shape[0], half)]
+    tables = made = None
+    for j in range(1, n_blk):
+        kept, extra = [], {}
+        for c, part in enumerate(parts):
+            ring = [onward(part, 1, n_blk)] if j < n_blk - 1 else []
+            new = (ring, [swap(part, bit, n_op) for bit in bits[:1]])
+            if c == len(parts) - 1:
+                extra["psi"] = onward(columns[order[j - 1]], order[j - 1], n_blk)
+                if j == n_blk - 1:
+                    extra["tables"] = table(right)
+                    extra["made"] = early(left, psi, extra["tables"])
+            new, extra, _ = lax.optimization_barrier((new, extra, kept))
+            kept.append(new)
+        psi[order[j - 1]] = extra["psi"]
+        for bit in bits[:1]:
+            left[j, bit] = [swaps[0] for _, swaps in kept]
+        if j < n_blk - 1:
+            parts = [ring[0] for ring, _ in kept]
+            left[j + 1, 0] = parts
+        tables, made = extra.get("tables", tables), extra.get("made", made)
+    for bit in bits[1:]:
+        more = {(d, e ^ bit): [swap(x, bit, n_op) for x in parts] for (d, e), parts in left.items()}
+        left.update(more)
     return left, psi, right, tables, made
 
 
@@ -204,7 +204,7 @@
     copies = []
     for d in range(n_blk):
         there = ring_at(ring_place(own_blk, n_blk) + d, n_blk) * n_op
-        for h in range(psi_out[d].shape[1] // cols):
+        for h in range(2):
             start = pl.multiple_of((there + (own_op ^ h)) * cols, LANES)
             copy = pltpu.make_async_copy(
                 psi.at[0, :, pl.ds(start, cols)],
@@ -306,12 +306,12 @@
 
 
 def left_products(block, left, inter):
-    n_terms, rows, cols = inter.shape
+    _, rows, cols = inter.shape
     at = 0
-    while at < n_terms:
-        ops = left(at)
-        terms = ops.shape[0]
-        prod = jnp.dot(ops.reshape(terms * rows, rows), block, preferred_element_type=jnp.float32)
+    for ref in left:
+        terms = ref.shape[0]
+        ops = ref[...].reshape(terms * rows, rows)
+        prod = jnp.dot(ops, block, preferred_element_type=jnp.float32)
         inter[at : at + terms] = prod.astype(jnp.bfloat16).reshape(terms, rows, cols)
         at += terms
 
@@ -336,19 +336,13 @@
 def keep(left, left_out, sems):
     copies = []
     for d, line in enumerate(left):
-        for e, ref in enumerate(line):
-            copies.append(pltpu.make_async_copy(ref, left_out.at[d, e], sems.at[d * len(line) + e]))
+        at = 0
+        for ref in line:
+            there = left_out.at[d, at : at + ref.shape[0]]
+            copies.append(pltpu.make_async_copy(ref, there, sems.at[len(copies)]))
             copies[-1].start()
+            at += ref.shape[0]
     return copies
-
-
-def masked(psi, width, out):
-    at = 0
-    for ref in psi:
-        block = ref[...].astype(jnp.float32)
-        block = jnp.where(row_mask(width, block.shape), block, 0.0)
-        out[:, at : at + block.shape[1]] = block.astype(jnp.bfloat16)
-        at += block.shape[1]
 
 
 def take(refs, counts):
@@ -361,14 +355,15 @@
 
 def products_of(psi, left, widths, first, raw_out, inter):
     for d, line in enumerate(left):
-        masked(psi[d], widths[first + d], raw_out.at[d])
-        terms = line[0].shape[0]
-        left_products(raw_out[d], lambda at: line[at // terms][...], inter.at[d])
-
-
-def early_body(n_pair, counts, widths, *refs):
-    left, refs = take(refs, [n_pair] * len(counts))
-    psi, (raw_out, inter_out, left_out, sems) = take(refs, counts)
+        block = psi[d][...].astype(jnp.float32)
+        block = jnp.where(row_mask(widths[first + d], block.shape), block, 0.0)
+        raw_out[d] = block.astype(jnp.bfloat16)
+        left_products(raw_out[d], line, inter.at[d])
+
+
+def early_body(counts, widths, *refs):
+    left, refs = take(refs, counts)
+    (psi,), (raw_out, inter_out, left_out, sems) = take(refs, [len(counts)])
     copies = keep(left, left_out, sems)
     products_of(psi, left, widths, 0, raw_out, inter_out)
     for copy in copies:
@@ -378,21 +373,18 @@
 def first_body(n_blk, n_pair, counts, src, widths, *refs):
     n_late = len(counts)
     n_early = n_blk - n_late
-    left, refs = take(refs, [n_pair] * n_late)
-    (right,), refs = take(refs, [n_pair])
-    psi, refs = take(refs, counts)
+    left, refs = take(refs, counts)
+    (right, psi), refs = take(refs, [n_pair, n_late])
     raw_in, inter_in, diag, right_diag, part_out, raw_out, left_out, dots_out = refs[:8]
     sends, (inter, sems) = refs[8:-2], refs[-2:]
     copies = keep(left, left_out, sems)
-    for j, (given, own) in enumerate(((inter_in, inter), (raw_in, raw_out))):
+    for given, own in ((inter_in, inter), (raw_in, raw_out)):
         copies.append(
-            pltpu.make_async_copy(given, own.at[:n_early], sems.at[n_late * n_pair + j])
+            pltpu.make_async_copy(given, own.at[:n_early], sems.at[len(copies)])
         )
         copies[-1].start()
     inter[n_blk] = jnp.zeros_like(inter[n_blk])
-    products_of(
-        psi, left, widths, n_early, raw_out.at[n_early:], inter.at[n_early:n_blk]
-    )
+    products_of(psi, left, widths, n_early, raw_out.at[n_early:], inter.at[n_early:n_blk])
     for copy in copies:
         copy.wait()
     cols = diag.shape[2]
@@ -463,14 +455,14 @@
             vv, vc, vs = vv + fold(vec * vec), vc + fold(vec * item), vs + fold(vec * sigma)
         halves.append((whole(vv), whole(vc), whole(vs)))
     along = (halves[0][1] + halves[1][1]) / jnp.maximum(halves[0][0] + halves[1][0], 1e-30)
-    terms = held.shape[2]
+    for copy in copies:
+        copy.wait()
     for d in range(n_blk):
         for h in range(2):
             part = slice(h * cols, (h + 1) * cols)
             vec = raw_in[d, :, part].astype(jnp.float32) * scale
             fld[d, :, part] = (corr[d, :, part] - along * vec).astype(jnp.bfloat16)
-        copies[d].wait()
-        left_products(fld[d], lambda at: held[d, at // terms], inter.at[d])
+        left_products(fld[d], [held.at[d]], inter.at[d])
     zero = jnp.zeros((8, cols), jnp.float32)
     sums = [zero for _ in range(5)]
 
@@ -579,14 +571,13 @@
     count = float(n_blk * rows * ncols)
     n_dev = n_blk * n_op
     bf16, f32, i32 = jnp.bfloat16, jnp.float32, jnp.int32
-    last = sorted(range(1, n_blk), key=lambda d: min(d, n_blk - d))[-1]
 
     def pack():
         first = swap(term_shift, 1, n_op)
         sent = kernel(
             functools.partial(pack_body, n_blk, n_op),
             [(term_shift, SMEM), (first, SMEM), (psi, HBM), (right_ops, HBM)],
-            [((rows, 2 * cols if d in (0, last) else cols), bf16, VMEM) for d in range(n_blk)]
+            [((rows, 2 * cols), bf16, VMEM)] * n_blk
             + [((terms * width + 16, 2 * cols), bf16, VMEM)] * n_pair,
             [pltpu.VMEM(right_ops.shape, bf16), pltpu.SemaphoreType.DMA((2 * n_blk + 1,))],
             nbytes=1 << 20,
@@ -603,22 +594,24 @@
             + [((n_blk, rows, LANES), f32, VMEM), ((1, n_op * cols), f32, VMEM)],
         )
 
+    n_early = min(2, n_blk - 1)
+
     def inputs(left, psi, those):
-        blocks = [left[d, 2 * e] for d in those for e in range(n_pair)]
-        halves = [half for d in those for half in psi[d]]
-        return [(x, VMEM) for x in blocks], [(x, VMEM) for x in halves], [len(psi[d]) for d in those]
-
-    def early(left, psi, n_early, tables):
-        left_ins, psi_ins, counts = inputs(left, psi, range(n_early))
+        lines = [[x for e in range(n_pair) for x in left[d, 2 * e]] for d in those]
+        blocks = [x for line in lines for x in line] + [psi[d] for d in those]
+        return [(x, VMEM) for x in blocks], [len(line) for line in lines]
+
+    def early(left, psi, tables):
+        ins, counts = inputs(left, psi, range(n_early))
         return kernel(
-            functools.partial(early_body, n_pair, counts),
-            [(tables[1], SMEM)] + left_ins + psi_ins,
+            functools.partial(early_body, counts),
+            [(tables[1], SMEM)] + ins,
             [
                 ((n_early, rows, 2 * cols), bf16, VMEM),
                 ((n_early, n_pair * terms, rows, 2 * cols), bf16, VMEM),
-                ((n_early, n_pair, terms, rows, rows), bf16, HBM),
+                ((n_early, n_pair * terms, rows, rows), bf16, HBM),
             ],
-            [pltpu.SemaphoreType.DMA((n_early * n_pair,))],
+            [pltpu.SemaphoreType.DMA((sum(counts),))],
             flops=2 * n_early * rows * rows * 2 * cols * terms * n_pair,
             nbytes=4 << 20,
         )
@@ -626,9 +619,9 @@
     left, psi_by, right, (src, widths, slots, *both), (raw_early, inter_early, left_early) = gather(
         left_ops[:, 0], n_blk, n_op, pack, table, early
     )
-    n_early = raw_early.shape[0]
     n_late = n_blk - n_early
-    left_ins, psi_ins, counts = inputs(left, psi_by, range(n_early, n_blk))
+    late_ins, counts = inputs(left, psi_by, range(n_early, n_blk))
+    left_ins, psi_ins = late_ins[: sum(counts)], late_ins[sum(counts) :]
     right_ins = [(block, VMEM) for block in right]
     diags = [(x, VMEM) for x in both]
 
@@ -637,7 +630,7 @@
     dots = ((n_dev, 8, LANES), f32, VMEM)
     sends = [((2 - e % 2, n_blk, step, 2 * cols), bf16, VMEM) for e in range(1, n_op)]
     inter = pltpu.VMEM((n_blk + 1, n_pair * terms, rows, 2 * cols), bf16)
-    left_late = (n_late, n_pair, terms, rows, rows)
+    left_late = (n_late, n_pair * terms, rows, rows)
     cost = dict(flops=2 * n_blk * rows * 2 * cols * terms * n_pair * (rows + 2 * cols), nbytes=6 << 20)
 
     def totals(parts):
@@ -647,7 +640,7 @@
         functools.partial(first_body, n_blk, n_pair, counts),
         tables + left_ins + right_ins + psi_ins + [(raw_early, VMEM), (inter_early, VMEM)] + diags,
         [narrow, narrow, (left_late, bf16, HBM), dots] + sends[1:],
-        [inter, pltpu.SemaphoreType.DMA((n_late * n_pair + 2,))],
+        [inter, pltpu.SemaphoreType.DMA((sum(counts) + 2,))],
         **cost,
     )
     parts1, other1, got1 = lax.optimization_barrier(
@@ -711,7 +704,8 @@
             and cols // right_ops.shape[2] * n_op == right_ops.shape[1]
             and psi.shape[1] % (16 * n_op) == 0
             and n_op & (n_op - 1) == 0
-            and mesh.shape["blk"] > n_op.bit_length() - 1
+            and n_op <= 4
+            and mesh.shape["blk"] > 2
         )
         return (per_device if fits else per_device_general)(*args)
 

time: 74.7 us -> 78.2 us (1.047)
  starting transfers between devices: 19.5 us -> 28.4 us
  waiting for transfers between devices: 19.7 us -> 12.8 us
  blocking collectives: 20.4 us -> 22 us
    ppermute x14 -> x15, starting transfers between devices: 8.26 us -> 14.4 us  [swap(): return lax.ppermute(block, 'op', [(i, i ^ e) for i in range(n_op)])]
    ppermute x6 -> x8, waiting for transfers between devices: 13.3 us -> 7.16 us  [onward(): return lax.ppermute(block, 'blk', pairs)]
    ppermute x6 -> x8, starting transfers between devices: 11.2 us -> 14 us  [onward(): return lax.ppermute(block, 'blk', pairs)]
    all_to_all x2, blocking collectives: 20.4 us -> 22 us  [totals(): return lax.all_to_all(parts, ('blk', 'op'), 0, 0, tiled=True)]
    ppermute x14 -> x15, waiting for transfers between devices: 6.38 us -> 5.61 us  [swap(): return lax.ppermute(block, 'op', [(i, i ^ e) for i in range(n_op)])]
  transfers between devices with their start and end apart: 20 -> 23, of which waited for: 7 -> 6; matrix products, arithmetic and copies ran while one was open for 0% -> 0% of each run, Pallas kernels for 7% -> 6%
where the time goes in v14:
time: 78.2 us; the launch traced here: 78 us
  starting transfers between devices  28.4 us (36%)
  blocking collectives  22 us (28%)
  Pallas kernels  14 us (18%)
  waiting for transfers between devices  12.8 us (16%)
    all_to_all x2, blocking collectives, totals(): return lax.all_to_all(parts, ('blk', 'op'), 0, 0, tiled=True)  22 us
    ppermute x15, starting transfers between devices, swap(): return lax.ppermute(block, 'op', [(i, i ^ e) for i in range(n_op)])  14.4 us
    pallas_call x6, Pallas kernels, kernel(): pl.pallas_call(body, out_shape=[HBM(shape, dtype) if space == HBM else ja...  14 us
    ppermute x8, starting transfers between devices, onward(): return lax.ppermute(block, 'blk', pairs)  14 us
    ppermute x8, waiting for transfers between devices, onward(): return lax.ppermute(block, 'blk', pairs)  7.16 us
    ppermute x15, waiting for transfers between devices, swap(): return lax.ppermute(block, 'op', [(i, i ^ e) for i in range(n_op)])  5.61 us
  transfers between devices with their start and end apart: 23, of which 6 were waited for; matrix products, arithmetic and copies ran while one was open for 0% of the time, Pallas kernels for 6%

profile of v14, /device:TPU:0, one launch (start us, length us, event | category | flops | bytes accessed | tf_op | source)
XLA Modules:
  0.0 78.0 jit_solution(14138151962535263171)
XLA Ops:
  0.6 0.0 copy-start.3
  0.6 3.0 %collective-permute-start.1 = (bf16[2,256,256]{2,1,0:T(8,128)(2,1)}, bf16[2,256,256]{2,1,0:T(8,128)(2,1)S(1)}, u32[]{:S(2)}, u32[]{:S(2)}) collective-permute-start(bf16[2,256,256]{2,1,0:T(8,128)(2,1)} %bitcast.2), channel_id=1, source_target_pairs={{0,2},{1,3},{2,0},{3,1},{4,6},{5,7},{6,4},{7,5},{8,10},{9,11},{10,... | collective-permute-start | bytes 786440 | tf_op jit(solution)/shard_map/ppermute | solution.py:146
  3.6 1.6 %collective-permute-start = (bf16[2,256,256]{2,1,0:T(8,128)(2,1)}, bf16[2,256,256]{2,1,0:T(8,128)(2,1)S(1)}, u32[]{:S(2)}, u32[]{:S(2)}) collective-permute-start(bf16[2,256,256]{2,1,0:T(8,128)(2,1)} %bitcast.3), channel_id=1, source_target_pairs={{0,4},{4,12},{12,8},{8,0},{1,5},{5,13},{13,9},{9,1},{2,6},{6,14},{... | collective-permute-start | bytes 786440 | tf_op jit(solution)/shard_map/ppermute | solution.py:142
  5.2 0.0 copy-done.3
  5.2 0.0 collective-permute-start.2
  5.2 1.1 %collective-permute-done.2._ = s32[2]{0:T(128)S(1)} collective-permute-done((s32[2]{0:T(128)S(1)}, s32[2]{0:T(128)S(1)}, u32[]{:S(2)}, u32[]{:S(2)}) %collective-permute-start.2) | collective-permute-done | bytes 40 | tf_op jit(solution)/shard_map/ppermute | solution.py:146
  6.3 1.9 %shard_map.103 = (bf16[256,256]{1,0:T(8,128)(2,1)S(1)}, bf16[256,256]{1,0:T(8,128)(2,1)S(1)}, bf16[256,256]{1,0:T(8,128)(2,1)S(1)}, bf16[256,256]{1,0:T(8,128)(2...) custom-call(s32[2]{0:T(128)S(1)} %copy-done.3, s32[2]{0:T(128)S(1)} %collective-permute-done.2._, ...), custom_call_target="tpu_custom_call" | custom-call | bytes 1048576 | tf_op jit(solution)/shard_map/pallas_call | solution.py:113
  8.3 0.6 collective-permute-start.3
  8.9 3.8 %collective-permute-done.3.refs_1_.refs_9_ = bf16[144,256]{1,0:T(8,128)(2,1)S(1)} collective-permute-done((bf16[144,256]{1,0:T(8,128)(2,1)S(1)}, bf16[144,256]{1,0:T(8,128)(2,1)S(1)}, u32[]{:S(2)}, u32[]{:S(2)}) %collective-permute-start.3) | collective-permute-done | bytes 73760 | tf_op jit(solution)/shard_map/ppermute | solution.py:146
  12.7 0.0 collective-permute-done.1.refs_1_
  12.7 0.0 collective-permute-done.refs_2_
  12.7 0.0 copy-start.2
  12.7 0.0 copy-start
  12.8 0.0 copy-start.1
  12.8 0.8 %collective-permute-start.8 = (bf16[1,256,256]{2,1,0:T(8,128)(2,1)S(1)}, bf16[1,256,256]{2,1,0:T(8,128)(2,1)S(1)}, u32[]{:S(2)}, u32[]{:S(2)}) collective-permute-start(bf16[1,256,256]{2,1,0:T(8,128)(2,1)S(1)} %get-tuple-element.117), channel_id=1, source_target_pairs={{0,2},{1,3},{2,0},{3,1},{4,6},{5,7},{6,4},{7,5},{8,10},{9,11},{10,... | collective-permute-start | bytes 393224 | tf_op jit(solution)/shard_map/ppermute | solution.py:146
  13.6 2.3 %collective-permute-start.7 = (bf16[1,256,256]{2,1,0:T(8,128)(2,1)S(1)}, bf16[1,256,256]{2,1,0:T(8,128)(2,1)S(1)}, u32[]{:S(2)}, u32[]{:S(2)}) collective-permute-start(bf16[1,256,256]{2,1,0:T(8,128)(2,1)S(1)} %get-tuple-element.117), channel_id=1, source_target_pairs={{0,4},{4,12},{12,8},{8,0},{1,5},{5,13},{13,9},{9,1},{2,6},{6,14},{... | collective-permute-start | bytes 393224 | tf_op jit(solution)/shard_map/ppermute | solution.py:142
  16.0 1.8 %collective-permute-start.6 = (bf16[256,256]{1,0:T(8,128)(2,1)S(1)}, bf16[256,256]{1,0:T(8,128)(2,1)S(1)}, u32[]{:S(2)}, u32[]{:S(2)}) collective-permute-start(bf16[256,256]{1,0:T(8,128)(2,1)S(1)} %get-tuple-element.67), channel_id=1, source_target_pairs={{0,4},{4,12},{12,8},{8,0},{1,5},{5,13},{13,9},{9,1},{2,6},{6,14},{... | collective-permute-start | bytes 393224 | tf_op jit(solution)/shard_map/ppermute | solution.py:142
  17.8 1.0 %collective-permute-start.5 = (bf16[1,256,256]{2,1,0:T(8,128)(2,1)S(1)}, bf16[1,256,256]{2,1,0:T(8,128)(2,1)S(1)}, u32[]{:S(2)}, u32[]{:S(2)}) collective-permute-start(bf16[1,256,256]{2,1,0:T(8,128)(2,1)S(1)} %get-tuple-element.118), channel_id=1, source_target_pairs={{0,2},{1,3},{2,0},{3,1},{4,6},{5,7},{6,4},{7,5},{8,10},{9,11},{10,... | collective-permute-start | bytes 393224 | tf_op jit(solution)/shard_map/ppermute | solution.py:146
  18.8 0.0 collective-permute-start.4
  18.9 0.0 collective-permute-done.8.refs_3_
  18.9 2.9 %collective-permute-start.11 = (bf16[256,256]{1,0:T(8,128)(2,1)S(1)}, bf16[256,256]{1,0:T(8,128)(2,1)S(1)}, u32[]{:S(2)}, u32[]{:S(2)}) collective-permute-start(bf16[256,256]{1,0:T(8,128)(2,1)S(1)} %get-tuple-element.71), channel_id=1, source_target_pairs={{0,8},{4,0},{12,4},{8,12},{1,9},{5,1},{13,5},{9,13},{2,10},{6,2},{... | collective-permute-start | bytes 393224 | tf_op jit(solution)/shard_map/ppermute | solution.py:142
  21.8 0.0 collective-permute-done.7.refs_0_
  21.8 1.0 %collective-permute-start.13 = (bf16[1,256,256]{2,1,0:T(8,128)(2,1)S(1)}, bf16[1,256,256]{2,1,0:T(8,128)(2,1)S(1)}, u32[]{:S(2)}, u32[]{:S(2)}) collective-permute-start(bf16[1,256,256]{2,1,0:T(8,128)(2,1)S(1)} %collective-permute-done.7.refs_0_), channel_id=1, source_target_pairs={{0,2},{1,3},{2,0},{3,1},{4,6},{5,7},{6,4},{7,5},{8,10},{9,11},{10,... | collective-permute-start | bytes 393224 | tf_op jit(solution)/shard_map/ppermute | solution.py:146
  22.7 0.8 %collective-permute-done.6.refs_6_ = bf16[256,256]{1,0:T(8,128)(2,1)S(1)} collective-permute-done((bf16[256,256]{1,0:T(8,128)(2,1)S(1)}, bf16[256,256]{1,0:T(8,128)(2,1)S(1)}, u32[]{:S(2)}, u32[]{:S(2)}) %collective-permute-start.6) | collective-permute-done | bytes 131104 | tf_op jit(solution)/shard_map/ppermute | solution.py:142
  23.6 1.6 %collective-permute-start.12 = (bf16[1,256,256]{2,1,0:T(8,128)(2,1)S(1)}, bf16[1,256,256]{2,1,0:T(8,128)(2,1)S(1)}, u32[]{:S(2)}, u32[]{:S(2)}) collective-permute-start(bf16[1,256,256]{2,1,0:T(8,128)(2,1)S(1)} %collective-permute-done.7.refs_0_), channel_id=1, source_target_pairs={{0,4},{4,12},{12,8},{8,0},{1,5},{5,13},{13,9},{9,1},{2,6},{6,14},{... | collective-permute-start | bytes 393224 | tf_op jit(solution)/shard_map/ppermute | solution.py:142
  25.2 0.0 collective-permute-done.5.refs_4_
  25.2 2.7 %collective-permute-done.4.refs_1_ = bf16[1,256,256]{2,1,0:T(8,128)(2,1)S(1)} collective-permute-done((bf16[1,256,256]{2,1,0:T(8,128)(2,1)S(1)}, bf16[1,256,256]{2,1,0:T(8,128)(2,1)S(1)}, u32[]{:S(2)}, u32[]{:S(2)}) %collective-permute-start.4) | collective-permute-done | bytes 131104 | tf_op jit(solution)/shard_map/ppermute | solution.py:142
  27.9 1.3 %collective-permute-start.10 = (bf16[1,256,256]{2,1,0:T(8,128)(2,1)S(1)}, bf16[1,256,256]{2,1,0:T(8,128)(2,1)S(1)}, u32[]{:S(2)}, u32[]{:S(2)}) collective-permute-start(bf16[1,256,256]{2,1,0:T(8,128)(2,1)S(1)} %collective-permute-done.4.refs_1_), channel_id=1, source_target_pairs={{0,2},{1,3},{2,0},{3,1},{4,6},{5,7},{6,4},{7,5},{8,10},{9,11},{10,... | collective-permute-start | bytes 393224 | tf_op jit(solution)/shard_map/ppermute | solution.py:146
  29.2 0.4 collective-permute-start.9
  29.6 0.0 collective-permute-done.13.refs_2_
  29.6 3.3 %collective-permute-start.15 = (bf16[256,256]{1,0:T(8,128)(2,1)S(1)}, bf16[256,256]{1,0:T(8,128)(2,1)S(1)}, u32[]{:S(2)}, u32[]{:S(2)}) collective-permute-start(bf16[256,256]{1,0:T(8,128)(2,1)S(1)} %get-tuple-element.85), channel_id=1, source_target_pairs={{0,12},{4,8},{12,0},{8,4},{1,13},{5,9},{13,1},{9,5},{2,14},{6,10},... | collective-permute-start | bytes 393224 | tf_op jit(solution)/shard_map/ppermute | solution.py:142
  32.9 0.0 collective-permute-done.12.refs_4_
  32.9 1.2 %collective-permute-start.16 = (bf16[1,256,256]{2,1,0:T(8,128)(2,1)S(1)}, bf16[1,256,256]{2,1,0:T(8,128)(2,1)S(1)}, u32[]{:S(2)}, u32[]{:S(2)}) collective-permute-start(bf16[1,256,256]{2,1,0:T(8,128)(2,1)S(1)} %collective-permute-done.12.refs_4_), channel_id=1, source_target_pairs={{0,2},{1,3},{2,0},{3,1},{4,6},{5,7},{6,4},{7,5},{8,10},{9,11},{10,... | collective-permute-start | bytes 393224 | tf_op jit(solution)/shard_map/ppermute | solution.py:146
  34.1 0.0 collective-permute-done.11.refs_11_
  34.1 0.0 collective-permute-done.10.refs_3_
  34.1 3.6 %collective-permute-done.9.refs_5_ = bf16[1,256,256]{2,1,0:T(8,128)(2,1)S(1)} collective-permute-done((bf16[1,256,256]{2,1,0:T(8,128)(2,1)S(1)}, bf16[1,256,256]{2,1,0:T(8,128)(2,1)S(1)}, u32[]{:S(2)}, u32[]{:S(2)}) %collective-permute-start.9) | collective-permute-done | bytes 131104 | tf_op jit(solution)/shard_map/ppermute | solution.py:142
  37.8 1.3 %collective-permute-start.14 = (bf16[1,256,256]{2,1,0:T(8,128)(2,1)S(1)}, bf16[1,256,256]{2,1,0:T(8,128)(2,1)S(1)}, u32[]{:S(2)}, u32[]{:S(2)}) collective-permute-start(bf16[1,256,256]{2,1,0:T(8,128)(2,1)S(1)} %collective-permute-done.9.refs_5_), channel_id=1, source_target_pairs={{0,2},{1,3},{2,0},{3,1},{4,6},{5,7},{6,4},{7,5},{8,10},{9,11},{10,... | collective-permute-start | bytes 393224 | tf_op jit(solution)/shard_map/ppermute | solution.py:146
  39.0 0.0 copy-done.2
  39.0 0.0 copy-done.1
  39.0 0.0 copy-done.4
  39.0 0.0 copy-done.5
  39.0 1.4 %shard_map.104 = (s32[16]{0:T(128)S(1)}, s32[4]{0:T(128)S(1)}, s32[4]{0:T(128)S(1)}, f32[4,256,128]{2,1,0:T(8,128)S(1)}, f32[1,512]{1,0:T(1,128)S(1)}) custom-call(s32[4]{0:T(128)S(1)} %copy-done.4, s32[4]{0:T(128)S(1)} %copy-done.5, f32[4,256]{1,0:T(4,128)S(1)} %copy-done.1, f32[1,512]{1,0:T(1,128)S(1)} %bitcast.5, ...), custom_call_target="tpu_custom_call" | custom-call | tf_op jit(solution)/shard_map/pallas_call | solution.py:113
  40.4 0.0 copy-done
  40.4 1.7 %shard_map.105 = (bf16[2,256,256]{2,1,0:T(8,128)(2,1)S(1)}, bf16[2,4,256,256]{3,2,1,0:T(8,128)(2,1)S(1)}, bf16[2,4,256,256]{3,2,1,0:T(8,128)(2,1)}) custom-call(s32[4]{0:T(128)S(1)} %get-tuple-element.92.widths, bf16[2,256,256]{2,1,0:T(8,128)(2,1)S(1)} %bitcast.4, bf16[2,256,256]{2,1,0:T(8,128)(2,1)S(1)} %collective-permute-done.1.refs_1_, ...), custom_call_target="tpu_custom_call" | custom-call | flops 268435456 | bytes 4194304 | tf_op jit(solution)/shard_map/pallas_call | solution.py:113
  42.1 0.0 collective-permute-done.16.refs_6_
  42.1 0.0 collective-permute-done.15.refs_10_
  42.1 0.6 collective-permute-done.14.refs_7_
  42.7 2.5 %shard_map.106 = (bf16[4,256,256]{2,1,0:T(8,128)(2,1)S(1)}, bf16[4,256,256]{2,1,0:T(8,128)(2,1)S(1)}, bf16[2,4,256,256]{3,2,1,0:T(8,128)(2,1)}, f32[16,8,128]{2,...) custom-call(s32[16]{0:T(128)S(1)} %get-tuple-element.91.src, ...), custom_call_target="tpu_custom_call" | custom-call | flops 1073741824 | bytes 6291456 | tf_op jit(solution)/shard_map/pallas_call | solution.py:113
  45.2 0.1 collective-permute-start.17
  45.3 1.3 %collective-permute-start.18 = (bf16[2,4,64,256]{3,2,1,0:T(8,128)(2,1)S(1)}, bf16[2,4,64,256]{3,2,1,0:T(8,128)(2,1)S(1)}, u32[]{:S(2)}, u32[]{:S(2)}) collective-permute-start(bf16[2,4,64,256]{3,2,1,0:T(8,128)(2,1)S(1)} %get-tuple-element.103), channel_id=1, source_target_pairs={{0,2},{1,3},{2,0},{3,1},{4,6},{5,7},{6,4},{7,5},{8,10},{9,11},{10,... | collective-permute-start | bytes 786440 | tf_op jit(solution)/shard_map/ppermute | solution.py:146
  46.6 0.5 collective-permute-start.19
  47.2 11.6 %all_to_all.10.refs_2_.parts1 = f32[16,8,128]{2,1,0:T(8,128)S(1)} all-to-all(f32[16,8,128]{2,1,0:T(8,128)S(1)} %get-tuple-element.101), channel_id=1, replica_groups=mesh['grp'=2,'blk'=4,'op'=4] {'blk','op'}, dimensions={0} | all-to-all | bytes 131072 | tf_op jit(solution)/shard_map/all_to_all | solution.py:637
  58.8 0.0 collective-permute-done.19.refs_1_
  58.8 0.0 collective-permute-done.18.refs_0_
  58.8 0.0 collective-permute-done.17.refs_5_
  58.8 4.8 %shard_map.107 = (f32[16,8,128]{2,1,0:T(8,128)S(1)}, bf16[4,4,64,256]{3,2,1,0:T(8,128)(2,1)S(1)}, bf16[1,4,64,256]{3,2,1,0:T(8,128)(2,1)S(1)}, bf16[2,4,64,256]{...) custom-call(s32[16]{0:T(128)S(1)} %get-tuple-element.91.src, s32[4]{0:T(128)S(1)} %get-tuple-element.92.widths, ...), custom_call_target="tpu_custom_call" | custom-call | flops 1073741824 | bytes 6291456 | tf_op jit(solution)/shard_map/pallas_call | solution.py:113
  63.6 0.2 collective-permute-start.21
  63.7 0.0 collective-permute-start.20
  63.7 2.0 %collective-permute-start.22 = (bf16[1,4,64,256]{3,2,1,0:T(8,128)(2,1)S(1)}, bf16[1,4,64,256]{3,2,1,0:T(8,128)(2,1)S(1)}, u32[]{:S(2)}, u32[]{:S(2)}) collective-permute-start(bf16[1,4,64,256]{3,2,1,0:T(8,128)(2,1)S(1)} %get-tuple-element.116), channel_id=1, source_target_pairs={{0,3},{1,2},{2,1},{3,0},{4,7},{5,6},{6,5},{7,4},{8,11},{9,10},{10,... | collective-permute-start | bytes 393224 | tf_op jit(solution)/shard_map/ppermute | solution.py:146
  65.8 10.4 %all_to_all.11.parts2 = f32[16,8,128]{2,1,0:T(8,128)S(1)} all-to-all(f32[16,8,128]{2,1,0:T(8,128)S(1)} %get-tuple-element.110), channel_id=1, replica_groups=mesh['grp'=2,'blk'=4,'op'=4] {'blk','op'}, dimensions={0} | all-to-all | bytes 131072 | tf_op jit(solution)/shard_map/all_to_all | solution.py:637
  76.1 0.0 collective-permute-done.20.refs_2_
  76.1 0.0 collective-permute-done.22.refs_4_
  76.1 0.0 collective-permute-done.21.refs_3_
  76.1 1.8 %shard_map.108 = (bf16[4,64,512]{2,1,0:T(8,128)(2,1)}, bf16[4,64,512]{2,1,0:T(8,128)(2,1)}, f32[1]{0:T(128)}) custom-call(s32[4]{0:T(128)S(1)} %get-tuple-element.90.slots, f32[16,8,128]{2,1,0:T(8,128)S(1)} %all_to_all.10.refs_2_.parts1, f32[16,8,128]{2,1,0:T(8,128)S(1)} %all_to_all.11.parts2, f32[4,256,128]{2,1,0:T(8,128)S(1)} %get-tuple-element.99.refs_14_.refs_6_.diag, ...), custom_call_target="tpu_custom_call" | custom-call | bytes 4194304 | tf_op jit(solution)/shard_map/pallas_call | solution.py:113
  (3 shorter events, 0.0 us)
Async XLA Ops:
  0.6 4.6 %copy-start.3 = (s32[2]{0:T(128)S(1)}, s32[2]{0:T(128)}, u32[]{:S(2)}) copy-start(s32[2]{0:T(128)} %shift.1) | copy-start | bytes 28
  0.6 12.1 %collective-permute-start.1 = (bf16[2,256,256]{2,1,0:T(8,128)(2,1)}, bf16[2,256,256]{2,1,0:T(8,128)(2,1)S(1)}, u32[]{:S(2)}, u32[]{:S(2)}) collective-permute-start(bf16[2,256,256]{2,1,0:T(8,128)(2,1)} %bitcast.2), channel_id=1, source_target_pairs={{0,2},{1,3},{2,0},{3,1},{4,6},{5,7},{6,4},{7,5},{8,10},{9,11},{10,... | collective-permute-start | bytes 786440 | tf_op jit(solution)/shard_map/ppermute | solution.py:146
  3.6 9.1 %collective-permute-start = (bf16[2,256,256]{2,1,0:T(8,128)(2,1)}, bf16[2,256,256]{2,1,0:T(8,128)(2,1)S(1)}, u32[]{:S(2)}, u32[]{:S(2)}) collective-permute-start(bf16[2,256,256]{2,1,0:T(8,128)(2,1)} %bitcast.3), channel_id=1, source_target_pairs={{0,4},{4,12},{12,8},{8,0},{1,5},{5,13},{13,9},{9,1},{2,6},{6,14},{... | collective-permute-start | bytes 786440 | tf_op jit(solution)/shard_map/ppermute | solution.py:142
  5.2 1.1 %collective-permute-start.2 = (s32[2]{0:T(128)S(1)}, s32[2]{0:T(128)S(1)}, u32[]{:S(2)}, u32[]{:S(2)}) collective-permute-start(s32[2]{0:T(128)S(1)} %copy-done.3), channel_id=1, source_target_pairs={{0,1},{1,0},{2,3},{3,2},{4,5},{5,4},{6,7},{7,6},{8,9},{9,8},{10,11... | collective-permute-start | bytes 32 | tf_op jit(solution)/shard_map/ppermute | solution.py:146
  8.3 4.4 %collective-permute-start.3 = (bf16[144,256]{1,0:T(8,128)(2,1)S(1)}, bf16[144,256]{1,0:T(8,128)(2,1)S(1)}, u32[]{:S(2)}, u32[]{:S(2)}) collective-permute-start(bf16[144,256]{1,0:T(8,128)(2,1)S(1)} %get-tuple-element.65), channel_id=1, source_target_pairs={{0,2},{1,3},{2,0},{3,1},{4,6},{5,7},{6,4},{7,5},{8,10},{9,11},{10,... | collective-permute-start | bytes 221192 | tf_op jit(solution)/shard_map/ppermute | solution.py:146
  12.7 26.3 %copy-start.2 = (f32[512]{0:T(512)S(1)}, f32[512]{0:T(512)}, u32[]{:S(2)}) copy-start(f32[512]{0:T(512)} %param.15) | copy-start | bytes 6148
  12.7 27.7 %copy-start = (bf16[2,1,256,256]{3,2,1,0:T(8,128)(2,1)S(1)}, bf16[2,1,256,256]{3,2,1,0:T(8,128)(2,1)}, u32[]{:S(2)}) copy-start(bf16[2,1,256,256]{3,2,1,0:T(8,128)(2,1)} %param.9) | copy-start | bytes 786436
  12.8 26.3 %copy-start.1 = (f32[4,256]{1,0:T(4,128)S(1)}, f32[4,256]{1,0:T(4,128)}, u32[]{:S(2)}) copy-start(f32[4,256]{1,0:T(4,128)} %left_diag.1) | copy-start | bytes 12292
  12.8 6.1 %collective-permute-start.8 = (bf16[1,256,256]{2,1,0:T(8,128)(2,1)S(1)}, bf16[1,256,256]{2,1,0:T(8,128)(2,1)S(1)}, u32[]{:S(2)}, u32[]{:S(2)}) collective-permute-start(bf16[1,256,256]{2,1,0:T(8,128)(2,1)S(1)} %get-tuple-element.117), channel_id=1, source_target_pairs={{0,2},{1,3},{2,0},{3,1},{4,6},{5,7},{6,4},{7,5},{8,10},{9,11},{10,... | collective-permute-start | bytes 393224 | tf_op jit(solution)/shard_map/ppermute | solution.py:146
  13.6 8.1 %collective-permute-start.7 = (bf16[1,256,256]{2,1,0:T(8,128)(2,1)S(1)}, bf16[1,256,256]{2,1,0:T(8,128)(2,1)S(1)}, u32[]{:S(2)}, u32[]{:S(2)}) collective-permute-start(bf16[1,256,256]{2,1,0:T(8,128)(2,1)S(1)} %get-tuple-element.117), channel_id=1, source_target_pairs={{0,4},{4,12},{12,8},{8,0},{1,5},{5,13},{13,9},{9,1},{2,6},{6,14},{... | collective-permute-start | bytes 393224 | tf_op jit(solution)/shard_map/ppermute | solution.py:142
  16.0 7.6 %collective-permute-start.6 = (bf16[256,256]{1,0:T(8,128)(2,1)S(1)}, bf16[256,256]{1,0:T(8,128)(2,1)S(1)}, u32[]{:S(2)}, u32[]{:S(2)}) collective-permute-start(bf16[256,256]{1,0:T(8,128)(2,1)S(1)} %get-tuple-element.67), channel_id=1, source_target_pairs={{0,4},{4,12},{12,8},{8,0},{1,5},{5,13},{13,9},{9,1},{2,6},{6,14},{... | collective-permute-start | bytes 393224 | tf_op jit(solution)/shard_map/ppermute | solution.py:142
  17.8 21.3 %copy-start.4 = (s32[4]{0:T(128)S(1)}, s32[4]{0:T(128)}, u32[]{:S(2)}) copy-start(s32[4]{0:T(128)} %sector.1) | copy-start | bytes 52
  17.8 21.3 %copy-start.5 = (s32[4]{0:T(128)S(1)}, s32[4]{0:T(128)}, u32[]{:S(2)}) copy-start(s32[4]{0:T(128)} %width.1) | copy-start | bytes 52
  17.8 7.4 %collective-permute-start.5 = (bf16[1,256,256]{2,1,0:T(8,128)(2,1)S(1)}, bf16[1,256,256]{2,1,0:T(8,128)(2,1)S(1)}, u32[]{:S(2)}, u32[]{:S(2)}) collective-permute-start(bf16[1,256,256]{2,1,0:T(8,128)(2,1)S(1)} %get-tuple-element.118), channel_id=1, source_target_pairs={{0,2},{1,3},{2,0},{3,1},{4,6},{5,7},{6,4},{7,5},{8,10},{9,11},{10,... | collective-permute-start | bytes 393224 | tf_op jit(solution)/shard_map/ppermute | solution.py:146
  18.8 9.0 %collective-permute-start.4 = (bf16[1,256,256]{2,1,0:T(8,128)(2,1)S(1)}, bf16[1,256,256]{2,1,0:T(8,128)(2,1)S(1)}, u32[]{:S(2)}, u32[]{:S(2)}) collective-permute-start(bf16[1,256,256]{2,1,0:T(8,128)(2,1)S(1)} %get-tuple-element.118), channel_id=1, source_target_pairs={{0,4},{4,12},{12,8},{8,0},{1,5},{5,13},{13,9},{9,1},{2,6},{6,14},{... | collective-permute-start | bytes 393224 | tf_op jit(solution)/shard_map/ppermute | solution.py:142
  18.9 15.3 %collective-permute-start.11 = (bf16[256,256]{1,0:T(8,128)(2,1)S(1)}, bf16[256,256]{1,0:T(8,128)(2,1)S(1)}, u32[]{:S(2)}, u32[]{:S(2)}) collective-permute-start(bf16[256,256]{1,0:T(8,128)(2,1)S(1)} %get-tuple-element.71), channel_id=1, source_target_pairs={{0,8},{4,0},{12,4},{8,12},{1,9},{5,1},{13,5},{9,13},{2,10},{6,2},{... | collective-permute-start | bytes 393224 | tf_op jit(solution)/shard_map/ppermute | solution.py:142
  21.8 7.8 %collective-permute-start.13 = (bf16[1,256,256]{2,1,0:T(8,128)(2,1)S(1)}, bf16[1,256,256]{2,1,0:T(8,128)(2,1)S(1)}, u32[]{:S(2)}, u32[]{:S(2)}) collective-permute-start(bf16[1,256,256]{2,1,0:T(8,128)(2,1)S(1)} %collective-permute-done.7.refs_0_), channel_id=1, source_target_pairs={{0,2},{1,3},{2,0},{3,1},{4,6},{5,7},{6,4},{7,5},{8,10},{9,11},{10,... | collective-permute-start | bytes 393224 | tf_op jit(solution)/shard_map/ppermute | solution.py:146
  23.6 9.3 %collective-permute-start.12 = (bf16[1,256,256]{2,1,0:T(8,128)(2,1)S(1)}, bf16[1,256,256]{2,1,0:T(8,128)(2,1)S(1)}, u32[]{:S(2)}, u32[]{:S(2)}) collective-permute-start(bf16[1,256,256]{2,1,0:T(8,128)(2,1)S(1)} %collective-permute-done.7.refs_0_), channel_id=1, source_target_pairs={{0,4},{4,12},{12,8},{8,0},{1,5},{5,13},{13,9},{9,1},{2,6},{6,14},{... | collective-permute-start | bytes 393224 | tf_op jit(solution)/shard_map/ppermute | solution.py:142
  27.9 6.3 %collective-permute-start.10 = (bf16[1,256,256]{2,1,0:T(8,128)(2,1)S(1)}, bf16[1,256,256]{2,1,0:T(8,128)(2,1)S(1)}, u32[]{:S(2)}, u32[]{:S(2)}) collective-permute-start(bf16[1,256,256]{2,1,0:T(8,128)(2,1)S(1)} %collective-permute-done.4.refs_1_), channel_id=1, source_target_pairs={{0,2},{1,3},{2,0},{3,1},{4,6},{5,7},{6,4},{7,5},{8,10},{9,11},{10,... | collective-permute-start | bytes 393224 | tf_op jit(solution)/shard_map/ppermute | solution.py:146
  29.2 8.6 %collective-permute-start.9 = (bf16[1,256,256]{2,1,0:T(8,128)(2,1)S(1)}, bf16[1,256,256]{2,1,0:T(8,128)(2,1)S(1)}, u32[]{:S(2)}, u32[]{:S(2)}) collective-permute-start(bf16[1,256,256]{2,1,0:T(8,128)(2,1)S(1)} %collective-permute-done.4.refs_1_), channel_id=1, source_target_pairs={{0,4},{4,12},{12,8},{8,0},{1,5},{5,13},{13,9},{9,1},{2,6},{6,14},{... | collective-permute-start | bytes 393224 | tf_op jit(solution)/shard_map/ppermute | solution.py:142
  29.6 12.6 %collective-permute-start.15 = (bf16[256,256]{1,0:T(8,128)(2,1)S(1)}, bf16[256,256]{1,0:T(8,128)(2,1)S(1)}, u32[]{:S(2)}, u32[]{:S(2)}) collective-permute-start(bf16[256,256]{1,0:T(8,128)(2,1)S(1)} %get-tuple-element.85), channel_id=1, source_target_pairs={{0,12},{4,8},{12,0},{8,4},{1,13},{5,9},{13,1},{9,5},{2,14},{6,10},... | collective-permute-start | bytes 393224 | tf_op jit(solution)/shard_map/ppermute | solution.py:142
  32.9 9.2 %collective-permute-start.16 = (bf16[1,256,256]{2,1,0:T(8,128)(2,1)S(1)}, bf16[1,256,256]{2,1,0:T(8,128)(2,1)S(1)}, u32[]{:S(2)}, u32[]{:S(2)}) collective-permute-start(bf16[1,256,256]{2,1,0:T(8,128)(2,1)S(1)} %collective-permute-done.12.refs_4_), channel_id=1, source_target_pairs={{0,2},{1,3},{2,0},{3,1},{4,6},{5,7},{6,4},{7,5},{8,10},{9,11},{10,... | collective-permute-start | bytes 393224 | tf_op jit(solution)/shard_map/ppermute | solution.py:146
  37.8 5.0 %collective-permute-start.14 = (bf16[1,256,256]{2,1,0:T(8,128)(2,1)S(1)}, bf16[1,256,256]{2,1,0:T(8,128)(2,1)S(1)}, u32[]{:S(2)}, u32[]{:S(2)}) collective-permute-start(bf16[1,256,256]{2,1,0:T(8,128)(2,1)S(1)} %collective-permute-done.9.refs_5_), channel_id=1, source_target_pairs={{0,2},{1,3},{2,0},{3,1},{4,6},{5,7},{6,4},{7,5},{8,10},{9,11},{10,... | collective-permute-start | bytes 393224 | tf_op jit(solution)/shard_map/ppermute | solution.py:146
  45.2 13.5 %collective-permute-start.17 = (bf16[4,256,256]{2,1,0:T(8,128)(2,1)S(1)}, bf16[4,256,256]{2,1,0:T(8,128)(2,1)S(1)}, u32[]{:S(2)}, u32[]{:S(2)}) collective-permute-start(bf16[4,256,256]{2,1,0:T(8,128)(2,1)S(1)} %get-tuple-element.102.refs_4_), channel_id=1, source_target_pairs={{0,1},{1,0},{2,3},{3,2},{4,5},{5,4},{6,7},{7,6},{8,9},{9,8},{10,11... | collective-permute-start | bytes 1572872 | tf_op jit(solution)/shard_map/ppermute | solution.py:146
  45.3 13.5 %collective-permute-start.18 = (bf16[2,4,64,256]{3,2,1,0:T(8,128)(2,1)S(1)}, bf16[2,4,64,256]{3,2,1,0:T(8,128)(2,1)S(1)}, u32[]{:S(2)}, u32[]{:S(2)}) collective-permute-start(bf16[2,4,64,256]{3,2,1,0:T(8,128)(2,1)S(1)} %get-tuple-element.103), channel_id=1, source_target_pairs={{0,2},{1,3},{2,0},{3,1},{4,6},{5,7},{6,4},{7,5},{8,10},{9,11},{10,... | collective-permute-start | bytes 786440 | tf_op jit(solution)/shard_map/ppermute | solution.py:146
  46.6 12.1 %collective-permute-start.19 = (bf16[1,4,64,256]{3,2,1,0:T(8,128)(2,1)S(1)}, bf16[1,4,64,256]{3,2,1,0:T(8,128)(2,1)S(1)}, u32[]{:S(2)}, u32[]{:S(2)}) collective-permute-start(bf16[1,4,64,256]{3,2,1,0:T(8,128)(2,1)S(1)} %get-tuple-element.104), channel_id=1, source_target_pairs={{0,3},{1,2},{2,1},{3,0},{4,7},{5,6},{6,5},{7,4},{8,11},{9,10},{10,... | collective-permute-start | bytes 393224 | tf_op jit(solution)/shard_map/ppermute | solution.py:146
  63.6 12.6 %collective-permute-start.21 = (bf16[2,4,64,256]{3,2,1,0:T(8,128)(2,1)S(1)}, bf16[2,4,64,256]{3,2,1,0:T(8,128)(2,1)S(1)}, u32[]{:S(2)}, u32[]{:S(2)}) collective-permute-start(bf16[2,4,64,256]{3,2,1,0:T(8,128)(2,1)S(1)} %get-tuple-element.115), channel_id=1, source_target_pairs={{0,2},{1,3},{2,0},{3,1},{4,6},{5,7},{6,4},{7,5},{8,10},{9,11},{10,... | collective-permute-start | bytes 786440 | tf_op jit(solution)/shard_map/ppermute | solution.py:146
  63.7 12.4 %collective-permute-start.20 = (bf16[1,4,64,256]{3,2,1,0:T(8,128)(2,1)S(1)}, bf16[1,4,64,256]{3,2,1,0:T(8,128)(2,1)S(1)}, u32[]{:S(2)}, u32[]{:S(2)}) collective-permute-start(bf16[1,4,64,256]{3,2,1,0:T(8,128)(2,1)S(1)} %get-tuple-element.114), channel_id=1, source_target_pairs={{0,1},{1,0},{2,3},{3,2},{4,5},{5,4},{6,7},{7,6},{8,9},{9,8},{10,11... | collective-permute-start | bytes 393224 | tf_op jit(solution)/shard_map/ppermute | solution.py:146
  63.7 12.4 %collective-permute-start.22 = (bf16[1,4,64,256]{3,2,1,0:T(8,128)(2,1)S(1)}, bf16[1,4,64,256]{3,2,1,0:T(8,128)(2,1)S(1)}, u32[]{:S(2)}, u32[]{:S(2)}) collective-permute-start(bf16[1,4,64,256]{3,2,1,0:T(8,128)(2,1)S(1)} %get-tuple-element.116), channel_id=1, source_target_pairs={{0,3},{1,2},{2,1},{3,0},{4,7},{5,6},{6,5},{7,4},{8,11},{9,10},{10,... | collective-permute-start | bytes 393224 | tf_op jit(solution)/shard_map/ppermute | solution.py:146

commit v15 on v14

--- a/solution.py
+++ b/solution.py
@@ -150,14 +150,17 @@
     bits = [1 << b for b in reversed(range(1, n_op.bit_length() - 1))]
     order = sorted(range(1, n_blk), key=lambda d: min(d, n_blk - d))
     columns, packed = pack()
-    (came, swapped), columns, right = lax.optimization_barrier(
+    (came, swapped), columns, right, near = lax.optimization_barrier(
         (
             (onward(own, 1, n_blk), [swap(own, bit, n_op) for bit in bits[:1]]),
             columns,
             [packed[0]] + [swap(part, 2 * e, n_op) for e, part in enumerate(packed[1:], 1)],
+            [onward(columns[d], d, n_blk) for d in order[:2]],
         )
     )
-    left, psi = {(0, 0): [own], (1, 0): [came]}, {0: columns[0]}
+    left, psi = {(0, 0): [own], (1, 0): [came]}, {0: [columns[0]]}
+    for d, block in zip(order[:2], near):
+        psi[d] = [block]
     for bit in bits[:1]:
         left[0, bit] = swapped
     half = max(own.shape[0] // 2, 1)
@@ -169,19 +172,24 @@
             ring = [onward(part, 1, n_blk)] if j < n_blk - 1 else []
             new = (ring, [swap(part, bit, n_op) for bit in bits[:1]])
             if c == len(parts) - 1:
-                extra["psi"] = onward(columns[order[j - 1]], order[j - 1], n_blk)
+                if j == 1:
+                    extra["tables"] = table(right)
+                    extra["psi"] = {d: onward(columns[d], d, n_blk) for d in order[2:]}
+                due = order[:1] if j == 2 else order[1:] if j == n_blk - 1 else []
+                extra["other"] = {d: swap(psi[d][0], 1, n_op) for d in due}
                 if j == n_blk - 1:
-                    extra["tables"] = table(right)
-                    extra["made"] = early(left, psi, extra["tables"])
+                    extra["made"] = early(left, psi, tables)
             new, extra, _ = lax.optimization_barrier((new, extra, kept))
             kept.append(new)
-        psi[order[j - 1]] = extra["psi"]
         for bit in bits[:1]:
             left[j, bit] = [swaps[0] for _, swaps in kept]
         if j < n_blk - 1:
             parts = [ring[0] for ring, _ in kept]
             left[j + 1, 0] = parts
         tables, made = extra.get("tables", tables), extra.get("made", made)
+        psi.update({d: [block] for d, block in extra.get("psi", {}).items()})
+        for d, block in extra["other"].items():
+            psi[d].append(block)
     for bit in bits[1:]:
         more = {(d, e ^ bit): [swap(x, bit, n_op) for x in parts] for (d, e), parts in left.items()}
         left.update(more)
@@ -204,7 +212,7 @@
     copies = []
     for d in range(n_blk):
         there = ring_at(ring_place(own_blk, n_blk) + d, n_blk) * n_op
-        for h in range(2):
+        for h in range(psi_out[d].shape[1] // cols):
             start = pl.multiple_of((there + (own_op ^ h)) * cols, LANES)
             copy = pltpu.make_async_copy(
                 psi.at[0, :, pl.ds(start, cols)],
@@ -355,26 +363,30 @@
 
 def products_of(psi, left, widths, first, raw_out, inter):
     for d, line in enumerate(left):
-        block = psi[d][...].astype(jnp.float32)
-        block = jnp.where(row_mask(widths[first + d], block.shape), block, 0.0)
-        raw_out[d] = block.astype(jnp.bfloat16)
+        at = 0
+        for ref in psi[d]:
+            block = ref[...].astype(jnp.float32)
+            block = jnp.where(row_mask(widths[first + d], block.shape), block, 0.0)
+            raw_out[d, :, at : at + block.shape[1]] = block.astype(jnp.bfloat16)
+            at += block.shape[1]
         left_products(raw_out[d], line, inter.at[d])
 
 
-def early_body(counts, widths, *refs):
+def early_body(counts, halves, widths, *refs):
     left, refs = take(refs, counts)
-    (psi,), (raw_out, inter_out, left_out, sems) = take(refs, [len(counts)])
+    psi, (raw_out, inter_out, left_out, sems) = take(refs, halves)
     copies = keep(left, left_out, sems)
     products_of(psi, left, widths, 0, raw_out, inter_out)
     for copy in copies:
         copy.wait()
 
 
-def first_body(n_blk, n_pair, counts, src, widths, *refs):
+def first_body(n_blk, n_pair, counts, halves, src, widths, *refs):
     n_late = len(counts)
     n_early = n_blk - n_late
     left, refs = take(refs, counts)
-    (right, psi), refs = take(refs, [n_pair, n_late])
+    (right,), refs = take(refs, [n_pair])
+    psi, refs = take(refs, halves)
     raw_in, inter_in, diag, right_diag, part_out, raw_out, left_out, dots_out = refs[:8]
     sends, (inter, sems) = refs[8:-2], refs[-2:]
     copies = keep(left, left_out, sems)
@@ -577,7 +589,7 @@
         sent = kernel(
             functools.partial(pack_body, n_blk, n_op),
             [(term_shift, SMEM), (first, SMEM), (psi, HBM), (right_ops, HBM)],
-            [((rows, 2 * cols), bf16, VMEM)] * n_blk
+            [((rows, 2 * cols if d == 0 else cols), bf16, VMEM) for d in range(n_blk)]
             + [((terms * width + 16, 2 * cols), bf16, VMEM)] * n_pair,
             [pltpu.VMEM(right_ops.shape, bf16), pltpu.SemaphoreType.DMA((2 * n_blk + 1,))],
             nbytes=1 << 20,
@@ -598,13 +610,13 @@
 
     def inputs(left, psi, those):
         lines = [[x for e in range(n_pair) for x in left[d, 2 * e]] for d in those]
-        blocks = [x for line in lines for x in line] + [psi[d] for d in those]
-        return [(x, VMEM) for x in blocks], [len(line) for line in lines]
+        blocks = [x for line in lines for x in line] + [x for d in those for x in psi[d]]
+        return [(x, VMEM) for x in blocks], [len(line) for line in lines], [len(psi[d]) for d in those]
 
     def early(left, psi, tables):
-        ins, counts = inputs(left, psi, range(n_early))
+        ins, counts, halves = inputs(left, psi, range(n_early))
         return kernel(
-            functools.partial(early_body, counts),
+            functools.partial(early_body, counts, halves),
             [(tables[1], SMEM)] + ins,
             [
                 ((n_early, rows, 2 * cols), bf16, VMEM),
@@ -620,7 +632,7 @@
         left_ops[:, 0], n_blk, n_op, pack, table, early
     )
     n_late = n_blk - n_early
-    late_ins, counts = inputs(left, psi_by, range(n_early, n_blk))
+    late_ins, counts, halves = inputs(left, psi_by, range(n_early, n_blk))
     left_ins, psi_ins = late_ins[: sum(counts)], late_ins[sum(counts) :]
     right_ins = [(block, VMEM) for block in right]
     diags = [(x, VMEM) for x in both]
@@ -637,7 +649,7 @@
         return lax.all_to_all(parts, ("blk", "op"), 0, 0, tiled=True)
 
     part1, raw, kept, dots1, *out1 = kernel(
-        functools.partial(first_body, n_blk, n_pair, counts),
+        functools.partial(first_body, n_blk, n_pair, counts, halves),
         tables + left_ins + right_ins + psi_ins + [(raw_early, VMEM), (inter_early, VMEM)] + diags,
         [narrow, narrow, (left_late, bf16, HBM), dots] + sends[1:],
         [inter, pltpu.SemaphoreType.DMA((sum(counts) + 2,))],
@@ -705,7 +717,7 @@
             and psi.shape[1] % (16 * n_op) == 0
             and n_op & (n_op - 1) == 0
             and n_op <= 4
-            and mesh.shape["blk"] > 2
+            and mesh.shape["blk"] > 3
         )
         return (per_device if fits else per_device_general)(*args)
 

time: 78.2 us -> 75.4 us (0.964)
  starting transfers between devices: 28.4 us -> 25.7 us
    ppermute x8, waiting for transfers between devices: 7.16 us -> 10.3 us  [onward(): return lax.ppermute(block, 'blk', pairs)]
    ppermute x15 -> x18, waiting for transfers between devices: 5.61 us -> 2.97 us  [swap(): return lax.ppermute(block, 'op', [(i, i ^ e) for i in range(n_op)])]
    ppermute x8, starting transfers between devices: 14 us -> 11.8 us  [onward(): return lax.ppermute(block, 'blk', pairs)]
    ppermute x15 -> x18, starting transfers between devices: 14.4 us -> 13.9 us  [swap(): return lax.ppermute(block, 'op', [(i, i ^ e) for i in range(n_op)])]
  transfers between devices with their start and end apart: 23 -> 26, of which waited for: 6 -> 8; matrix products, arithmetic and copies ran while one was open for 0% -> 0% of each run, Pallas kernels for 6% -> 7%
where the time goes in v15:
time: 75.4 us; the launch traced here: 75.2 us
  starting transfers between devices  25.7 us (34%)
  blocking collectives  21.4 us (28%)
  Pallas kernels  14 us (19%)
  waiting for transfers between devices  13.3 us (18%)
  between operations  0.79 us (1%)
    all_to_all x2, blocking collectives, totals(): return lax.all_to_all(parts, ('blk', 'op'), 0, 0, tiled=True)  21.4 us
    pallas_call x6, Pallas kernels, kernel(): pl.pallas_call(body, out_shape=[HBM(shape, dtype) if space == HBM else ja...  14 us
    ppermute x18, starting transfers between devices, swap(): return lax.ppermute(block, 'op', [(i, i ^ e) for i in range(n_op)])  13.9 us
    ppermute x8, starting transfers between devices, onward(): return lax.ppermute(block, 'blk', pairs)  11.8 us
    ppermute x8, waiting for transfers between devices, onward(): return lax.ppermute(block, 'blk', pairs)  10.3 us
    ppermute x18, waiting for transfers between devices, swap(): return lax.ppermute(block, 'op', [(i, i ^ e) for i in range(n_op)])  2.97 us
  transfers between devices with their start and end apart: 26, of which 8 were waited for; matrix products, arithmetic and copies ran while one was open for 0% of the time, Pallas kernels for 7%

profile of v15, /device:TPU:0, one launch (start us, length us, event | category | flops | bytes accessed | tf_op | source)
XLA Modules:
  0.0 75.2 jit_solution(12028980832272509546)
XLA Ops:
  0.6 3.0 %collective-permute-start.1 = (bf16[2,256,256]{2,1,0:T(8,128)(2,1)}, bf16[2,256,256]{2,1,0:T(8,128)(2,1)S(1)}, u32[]{:S(2)}, u32[]{:S(2)}) collective-permute-start(bf16[2,256,256]{2,1,0:T(8,128)(2,1)} %bitcast.2), channel_id=1, source_target_pairs={{0,2},{1,3},{2,0},{3,1},{4,6},{5,7},{6,4},{7,5},{8,10},{9,11},{10,... | collective-permute-start | bytes 786440 | tf_op jit(solution)/shard_map/ppermute | solution.py:146
  3.6 1.6 %collective-permute-start = (bf16[2,256,256]{2,1,0:T(8,128)(2,1)}, bf16[2,256,256]{2,1,0:T(8,128)(2,1)S(1)}, u32[]{:S(2)}, u32[]{:S(2)}) collective-permute-start(bf16[2,256,256]{2,1,0:T(8,128)(2,1)} %bitcast.3), channel_id=1, source_target_pairs={{0,4},{4,12},{12,8},{8,0},{1,5},{5,13},{13,9},{9,1},{2,6},{6,14},{... | collective-permute-start | bytes 786440 | tf_op jit(solution)/shard_map/ppermute | solution.py:142
  5.2 0.0 copy-done.3
  5.2 0.0 collective-permute-start.2
  5.2 1.1 %collective-permute-done.2._ = s32[2]{0:T(128)S(1)} collective-permute-done((s32[2]{0:T(128)S(1)}, s32[2]{0:T(128)S(1)}, u32[]{:S(2)}, u32[]{:S(2)}) %collective-permute-start.2) | collective-permute-done | bytes 40 | tf_op jit(solution)/shard_map/ppermute | solution.py:146
  6.3 1.9 %shard_map.103 = (bf16[256,256]{1,0:T(8,128)(2,1)S(1)}, bf16[256,128]{1,0:T(8,128)(2,1)S(1)}, bf16[256,128]{1,0:T(8,128)(2,1)S(1)}, bf16[256,128]{1,0:T(8,128)(2...) custom-call(s32[2]{0:T(128)S(1)} %copy-done.3, s32[2]{0:T(128)S(1)} %collective-permute-done.2._, ...), custom_call_target="tpu_custom_call" | custom-call | bytes 1048576 | tf_op jit(solution)/shard_map/pallas_call | solution.py:113
  8.3 0.6 collective-permute-start.3
  8.9 2.6 %collective-permute-start.4 = (bf16[256,128]{1,0:T(8,128)(2,1)S(1)}, bf16[256,128]{1,0:T(8,128)(2,1)S(1)}, u32[]{:S(2)}, u32[]{:S(2)}) collective-permute-start(bf16[256,128]{1,0:T(8,128)(2,1)S(1)} %get-tuple-element.62), channel_id=1, source_target_pairs={{0,4},{4,12},{12,8},{8,0},{1,5},{5,13},{13,9},{9,1},{2,6},{6,14},{... | collective-permute-start | bytes 196616 | tf_op jit(solution)/shard_map/ppermute | solution.py:142
  11.4 0.3 collective-permute-start.5
  11.8 2.3 %collective-permute-done.4.refs_6_ = bf16[256,128]{1,0:T(8,128)(2,1)S(1)} collective-permute-done((bf16[256,128]{1,0:T(8,128)(2,1)S(1)}, bf16[256,128]{1,0:T(8,128)(2,1)S(1)}, u32[]{:S(2)}, u32[]{:S(2)}) %collective-permute-start.4) | collective-permute-done | bytes 65568 | tf_op jit(solution)/shard_map/ppermute | solution.py:142
  14.1 1.7 %collective-permute-done.5.refs_12_ = bf16[256,128]{1,0:T(8,128)(2,1)S(1)} collective-permute-done((bf16[256,128]{1,0:T(8,128)(2,1)S(1)}, bf16[256,128]{1,0:T(8,128)(2,1)S(1)}, u32[]{:S(2)}, u32[]{:S(2)}) %collective-permute-start.5) | collective-permute-done | bytes 65568 | tf_op jit(solution)/shard_map/ppermute | solution.py:142
  15.7 0.0 collective-permute-done.3.refs_1_.refs_9_
  15.7 0.0 collective-permute-done.1.refs_1_
  15.7 0.0 collective-permute-done.refs_2_
  15.7 0.0 copy-start.2
  15.7 0.0 copy-start
  15.8 0.0 copy-start.1
  15.8 1.6 %collective-permute-start.10 = (bf16[1,256,256]{2,1,0:T(8,128)(2,1)S(1)}, bf16[1,256,256]{2,1,0:T(8,128)(2,1)S(1)}, u32[]{:S(2)}, u32[]{:S(2)}) collective-permute-start(bf16[1,256,256]{2,1,0:T(8,128)(2,1)S(1)} %get-tuple-element.119), channel_id=1, source_target_pairs={{0,2},{1,3},{2,0},{3,1},{4,6},{5,7},{6,4},{7,5},{8,10},{9,11},{10,... | collective-permute-start | bytes 393224 | tf_op jit(solution)/shard_map/ppermute | solution.py:146
  17.3 1.3 %collective-permute-start.9 = (bf16[1,256,256]{2,1,0:T(8,128)(2,1)S(1)}, bf16[1,256,256]{2,1,0:T(8,128)(2,1)S(1)}, u32[]{:S(2)}, u32[]{:S(2)}) collective-permute-start(bf16[1,256,256]{2,1,0:T(8,128)(2,1)S(1)} %get-tuple-element.119), channel_id=1, source_target_pairs={{0,4},{4,12},{12,8},{8,0},{1,5},{5,13},{13,9},{9,1},{2,6},{6,14},{... | collective-permute-start | bytes 393224 | tf_op jit(solution)/shard_map/ppermute | solution.py:142
  18.7 0.5 collective-permute-start.7
  19.2 2.5 %collective-permute-start.6 = (bf16[1,256,256]{2,1,0:T(8,128)(2,1)S(1)}, bf16[1,256,256]{2,1,0:T(8,128)(2,1)S(1)}, u32[]{:S(2)}, u32[]{:S(2)}) collective-permute-start(bf16[1,256,256]{2,1,0:T(8,128)(2,1)S(1)} %get-tuple-element.120), channel_id=1, source_target_pairs={{0,4},{4,12},{12,8},{8,0},{1,5},{5,13},{13,9},{9,1},{2,6},{6,14},{... | collective-permute-start | bytes 393224 | tf_op jit(solution)/shard_map/ppermute | solution.py:142
  21.7 0.6 collective-permute-start.8
  22.3 1.4 %shard_map.104 = (s32[16]{0:T(128)S(1)}, s32[4]{0:T(128)S(1)}, s32[4]{0:T(128)S(1)}, f32[4,256,128]{2,1,0:T(8,128)S(1)}, f32[1,512]{1,0:T(1,128)S(1)}) custom-call(s32[4]{0:T(128)S(1)} %copy-done.4, s32[4]{0:T(128)S(1)} %copy-done.5, f32[4,256]{1,0:T(4,128)S(1)} %copy-done.1, f32[1,512]{1,0:T(1,128)S(1)} %bitcast.5, ...), custom_call_target="tpu_custom_call" | custom-call | tf_op jit(solution)/shard_map/pallas_call | solution.py:113
  23.6 0.0 collective-permute-done.10.refs_3_
  23.7 0.8 %collective-permute-done.9.refs_0_ = bf16[1,256,256]{2,1,0:T(8,128)(2,1)S(1)} collective-permute-done((bf16[1,256,256]{2,1,0:T(8,128)(2,1)S(1)}, bf16[1,256,256]{2,1,0:T(8,128)(2,1)S(1)}, u32[]{:S(2)}, u32[]{:S(2)}) %collective-permute-start.9) | collective-permute-done | bytes 131104 | tf_op jit(solution)/shard_map/ppermute | solution.py:142
  24.5 0.7 collective-permute-start.12
  25.2 1.0 %collective-permute-start.11 = (bf16[1,256,256]{2,1,0:T(8,128)(2,1)S(1)}, bf16[1,256,256]{2,1,0:T(8,128)(2,1)S(1)}, u32[]{:S(2)}, u32[]{:S(2)}) collective-permute-start(bf16[1,256,256]{2,1,0:T(8,128)(2,1)S(1)} %collective-permute-done.9.refs_0_), channel_id=1, source_target_pairs={{0,4},{4,12},{12,8},{8,0},{1,5},{5,13},{13,9},{9,1},{2,6},{6,14},{... | collective-permute-start | bytes 393224 | tf_op jit(solution)/shard_map/ppermute | solution.py:142
  26.2 2.2 %collective-permute-done.8.refs_10_ = bf16[256,128]{1,0:T(8,128)(2,1)S(1)} collective-permute-done((bf16[256,128]{1,0:T(8,128)(2,1)S(1)}, bf16[256,128]{1,0:T(8,128)(2,1)S(1)}, u32[]{:S(2)}, u32[]{:S(2)}) %collective-permute-start.8) | collective-permute-done | bytes 65568 | tf_op jit(solution)/shard_map/ppermute | solution.py:142
  28.4 0.0 collective-permute-done.7.refs_4_
  28.4 0.0 collective-permute-done.6.refs_1_
  28.4 0.4 collective-permute-start.14
  28.8 1.9 %collective-permute-start.13 = (bf16[1,256,256]{2,1,0:T(8,128)(2,1)S(1)}, bf16[1,256,256]{2,1,0:T(8,128)(2,1)S(1)}, u32[]{:S(2)}, u32[]{:S(2)}) collective-permute-start(bf16[1,256,256]{2,1,0:T(8,128)(2,1)S(1)} %collective-permute-done.6.refs_1_), channel_id=1, source_target_pairs={{0,4},{4,12},{12,8},{8,0},{1,5},{5,13},{13,9},{9,1},{2,6},{6,14},{... | collective-permute-start | bytes 393224 | tf_op jit(solution)/shard_map/ppermute | solution.py:142
  30.7 0.0 collective-permute-start.15
  30.7 0.0 collective-permute-done.12.refs_2_
  30.7 1.4 %collective-permute-done.11.refs_4_ = bf16[1,256,256]{2,1,0:T(8,128)(2,1)S(1)} collective-permute-done((bf16[1,256,256]{2,1,0:T(8,128)(2,1)S(1)}, bf16[1,256,256]{2,1,0:T(8,128)(2,1)S(1)}, u32[]{:S(2)}, u32[]{:S(2)}) %collective-permute-start.11) | collective-permute-done | bytes 131104 | tf_op jit(solution)/shard_map/ppermute | solution.py:142
  32.2 1.5 %collective-permute-start.16 = (bf16[1,256,256]{2,1,0:T(8,128)(2,1)S(1)}, bf16[1,256,256]{2,1,0:T(8,128)(2,1)S(1)}, u32[]{:S(2)}, u32[]{:S(2)}) collective-permute-start(bf16[1,256,256]{2,1,0:T(8,128)(2,1)S(1)} %collective-permute-done.11.refs_4_), channel_id=1, source_target_pairs={{0,2},{1,3},{2,0},{3,1},{4,6},{5,7},{6,4},{7,5},{8,10},{9,11},{10,... | collective-permute-start | bytes 393224 | tf_op jit(solution)/shard_map/ppermute | solution.py:146
  33.7 0.0 collective-permute-done.15.refs_7_
  33.7 0.0 collective-permute-done.14.refs_3_
  33.7 1.9 %collective-permute-done.13.refs_5_ = bf16[1,256,256]{2,1,0:T(8,128)(2,1)S(1)} collective-permute-done((bf16[1,256,256]{2,1,0:T(8,128)(2,1)S(1)}, bf16[1,256,256]{2,1,0:T(8,128)(2,1)S(1)}, u32[]{:S(2)}, u32[]{:S(2)}) %collective-permute-start.13) | collective-permute-done | bytes 131104 | tf_op jit(solution)/shard_map/ppermute | solution.py:142
  35.6 0.9 %collective-permute-start.17 = (bf16[1,256,256]{2,1,0:T(8,128)(2,1)S(1)}, bf16[1,256,256]{2,1,0:T(8,128)(2,1)S(1)}, u32[]{:S(2)}, u32[]{:S(2)}) collective-permute-start(bf16[1,256,256]{2,1,0:T(8,128)(2,1)S(1)} %collective-permute-done.13.refs_5_), channel_id=1, source_target_pairs={{0,2},{1,3},{2,0},{3,1},{4,6},{5,7},{6,4},{7,5},{8,10},{9,11},{10,... | collective-permute-start | bytes 393224 | tf_op jit(solution)/shard_map/ppermute | solution.py:146
  36.5 0.0 collective-permute-start.19
  36.5 0.5 collective-permute-start.18
  37.0 1.7 %shard_map.105 = (bf16[2,256,256]{2,1,0:T(8,128)(2,1)S(1)}, bf16[2,4,256,256]{3,2,1,0:T(8,128)(2,1)S(1)}, bf16[2,4,256,256]{3,2,1,0:T(8,128)(2,1)}) custom-call(s32[4]{0:T(128)S(1)} %get-tuple-element.80.widths, bf16[2,256,256]{2,1,0:T(8,128)(2,1)S(1)} %bitcast.4, bf16[2,256,256]{2,1,0:T(8,128)(2,1)S(1)} %collective-permute-done.1.refs_1_, ...), custom_call_target="tpu_custom_call" | custom-call | flops 268435456 | bytes 4194304 | tf_op jit(solution)/shard_map/pallas_call | solution.py:113
  38.7 0.0 collective-permute-done.16.refs_6_
  38.7 0.0 collective-permute-done.19.refs_13_
  38.7 0.0 collective-permute-done.18.refs_11_
  38.7 1.8 %collective-permute-done.17.refs_7_ = bf16[1,256,256]{2,1,0:T(8,128)(2,1)S(1)} collective-permute-done((bf16[1,256,256]{2,1,0:T(8,128)(2,1)S(1)}, bf16[1,256,256]{2,1,0:T(8,128)(2,1)S(1)}, u32[]{:S(2)}, u32[]{:S(2)}) %collective-permute-start.17) | collective-permute-done | bytes 131104 | tf_op jit(solution)/shard_map/ppermute | solution.py:146
  40.6 2.5 %shard_map.106 = (bf16[4,256,256]{2,1,0:T(8,128)(2,1)S(1)}, bf16[4,256,256]{2,1,0:T(8,128)(2,1)S(1)}, bf16[2,4,256,256]{3,2,1,0:T(8,128)(2,1)}, f32[16,8,128]{2,...) custom-call(s32[16]{0:T(128)S(1)} %get-tuple-element.79.src, ...), custom_call_target="tpu_custom_call" | custom-call | flops 1073741824 | bytes 6291456 | tf_op jit(solution)/shard_map/pallas_call | solution.py:113
  43.0 0.1 collective-permute-start.20
  43.1 1.0 %collective-permute-start.21 = (bf16[2,4,64,256]{3,2,1,0:T(8,128)(2,1)S(1)}, bf16[2,4,64,256]{3,2,1,0:T(8,128)(2,1)S(1)}, u32[]{:S(2)}, u32[]{:S(2)}) collective-permute-start(bf16[2,4,64,256]{3,2,1,0:T(8,128)(2,1)S(1)} %get-tuple-element.105), channel_id=1, source_target_pairs={{0,2},{1,3},{2,0},{3,1},{4,6},{5,7},{6,4},{7,5},{8,10},{9,11},{10,... | collective-permute-start | bytes 786440 | tf_op jit(solution)/shard_map/ppermute | solution.py:146
  44.1 0.9 %collective-permute-start.22 = (bf16[1,4,64,256]{3,2,1,0:T(8,128)(2,1)S(1)}, bf16[1,4,64,256]{3,2,1,0:T(8,128)(2,1)S(1)}, u32[]{:S(2)}, u32[]{:S(2)}) collective-permute-start(bf16[1,4,64,256]{3,2,1,0:T(8,128)(2,1)S(1)} %get-tuple-element.106), channel_id=1, source_target_pairs={{0,3},{1,2},{2,1},{3,0},{4,7},{5,6},{6,5},{7,4},{8,11},{9,10},{10,... | collective-permute-start | bytes 393224 | tf_op jit(solution)/shard_map/ppermute | solution.py:146
  45.0 11.0 %all_to_all.10.refs_2_.parts1 = f32[16,8,128]{2,1,0:T(8,128)S(1)} all-to-all(f32[16,8,128]{2,1,0:T(8,128)S(1)} %get-tuple-element.103), channel_id=1, replica_groups=mesh['grp'=2,'blk'=4,'op'=4] {'blk','op'}, dimensions={0} | all-to-all | bytes 131072 | tf_op jit(solution)/shard_map/all_to_all | solution.py:649
  56.0 0.0 collective-permute-done.22.refs_1_
  56.0 0.0 collective-permute-done.21.refs_0_
  56.0 0.0 collective-permute-done.20.refs_5_
  56.0 4.8 %shard_map.107 = (f32[16,8,128]{2,1,0:T(8,128)S(1)}, bf16[4,4,64,256]{3,2,1,0:T(8,128)(2,1)S(1)}, bf16[1,4,64,256]{3,2,1,0:T(8,128)(2,1)S(1)}, bf16[2,4,64,256]{...) custom-call(s32[16]{0:T(128)S(1)} %get-tuple-element.79.src, s32[4]{0:T(128)S(1)} %get-tuple-element.80.widths, ...), custom_call_target="tpu_custom_call" | custom-call | flops 1073741824 | bytes 6291456 | tf_op jit(solution)/shard_map/pallas_call | solution.py:113
  60.8 0.3 collective-permute-start.24
  61.1 0.0 collective-permute-start.23
  61.1 1.9 %collective-permute-start.25 = (bf16[1,4,64,256]{3,2,1,0:T(8,128)(2,1)S(1)}, bf16[1,4,64,256]{3,2,1,0:T(8,128)(2,1)S(1)}, u32[]{:S(2)}, u32[]{:S(2)}) collective-permute-start(bf16[1,4,64,256]{3,2,1,0:T(8,128)(2,1)S(1)} %get-tuple-element.118), channel_id=1, source_target_pairs={{0,3},{1,2},{2,1},{3,0},{4,7},{5,6},{6,5},{7,4},{8,11},{9,10},{10,... | collective-permute-start | bytes 393224 | tf_op jit(solution)/shard_map/ppermute | solution.py:146
  63.0 10.4 %all_to_all.11.parts2 = f32[16,8,128]{2,1,0:T(8,128)S(1)} all-to-all(f32[16,8,128]{2,1,0:T(8,128)S(1)} %get-tuple-element.112), channel_id=1, replica_groups=mesh['grp'=2,'blk'=4,'op'=4] {'blk','op'}, dimensions={0} | all-to-all | bytes 131072 | tf_op jit(solution)/shard_map/all_to_all | solution.py:649
  73.4 0.0 collective-permute-done.23.refs_2_
  73.4 0.0 collective-permute-done.25.refs_4_
  73.4 0.0 collective-permute-done.24.refs_3_
  73.4 1.8 %shard_map.108 = (bf16[4,64,512]{2,1,0:T(8,128)(2,1)}, bf16[4,64,512]{2,1,0:T(8,128)(2,1)}, f32[1]{0:T(128)}) custom-call(s32[4]{0:T(128)S(1)} %get-tuple-element.78.slots, f32[16,8,128]{2,1,0:T(8,128)S(1)} %all_to_all.10.refs_2_.parts1, f32[16,8,128]{2,1,0:T(8,128)S(1)} %all_to_all.11.parts2, f32[4,256,128]{2,1,0:T(8,128)S(1)} %get-tuple-element.101.refs_16_.refs_6_.diag, ...), custom_call_target="tpu_custom_call" | custom-call | bytes 4194304 | tf_op jit(solution)/shard_map/pallas_call | solution.py:113
  (9 shorter events, 0.0 us)
Async XLA Ops:
  0.6 4.6 %copy-start.3 = (s32[2]{0:T(128)S(1)}, s32[2]{0:T(128)}, u32[]{:S(2)}) copy-start(s32[2]{0:T(128)} %shift.1) | copy-start | bytes 28
  0.6 15.1 %collective-permute-start.1 = (bf16[2,256,256]{2,1,0:T(8,128)(2,1)}, bf16[2,256,256]{2,1,0:T(8,128)(2,1)S(1)}, u32[]{:S(2)}, u32[]{:S(2)}) collective-permute-start(bf16[2,256,256]{2,1,0:T(8,128)(2,1)} %bitcast.2), channel_id=1, source_target_pairs={{0,2},{1,3},{2,0},{3,1},{4,6},{5,7},{6,4},{7,5},{8,10},{9,11},{10,... | collective-permute-start | bytes 786440 | tf_op jit(solution)/shard_map/ppermute | solution.py:146
  3.6 12.1 %collective-permute-start = (bf16[2,256,256]{2,1,0:T(8,128)(2,1)}, bf16[2,256,256]{2,1,0:T(8,128)(2,1)S(1)}, u32[]{:S(2)}, u32[]{:S(2)}) collective-permute-start(bf16[2,256,256]{2,1,0:T(8,128)(2,1)} %bitcast.3), channel_id=1, source_target_pairs={{0,4},{4,12},{12,8},{8,0},{1,5},{5,13},{13,9},{9,1},{2,6},{6,14},{... | collective-permute-start | bytes 786440 | tf_op jit(solution)/shard_map/ppermute | solution.py:142
  5.2 1.1 %collective-permute-start.2 = (s32[2]{0:T(128)S(1)}, s32[2]{0:T(128)S(1)}, u32[]{:S(2)}, u32[]{:S(2)}) collective-permute-start(s32[2]{0:T(128)S(1)} %copy-done.3), channel_id=1, source_target_pairs={{0,1},{1,0},{2,3},{3,2},{4,5},{5,4},{6,7},{7,6},{8,9},{9,8},{10,11... | collective-permute-start | bytes 32 | tf_op jit(solution)/shard_map/ppermute | solution.py:146
  8.3 7.5 %collective-permute-start.3 = (bf16[144,256]{1,0:T(8,128)(2,1)S(1)}, bf16[144,256]{1,0:T(8,128)(2,1)S(1)}, u32[]{:S(2)}, u32[]{:S(2)}) collective-permute-start(bf16[144,256]{1,0:T(8,128)(2,1)S(1)} %get-tuple-element.66), channel_id=1, source_target_pairs={{0,2},{1,3},{2,0},{3,1},{4,6},{5,7},{6,4},{7,5},{8,10},{9,11},{10,... | collective-permute-start | bytes 221192 | tf_op jit(solution)/shard_map/ppermute | solution.py:146
  8.9 5.2 %collective-permute-start.4 = (bf16[256,128]{1,0:T(8,128)(2,1)S(1)}, bf16[256,128]{1,0:T(8,128)(2,1)S(1)}, u32[]{:S(2)}, u32[]{:S(2)}) collective-permute-start(bf16[256,128]{1,0:T(8,128)(2,1)S(1)} %get-tuple-element.62), channel_id=1, source_target_pairs={{0,4},{4,12},{12,8},{8,0},{1,5},{5,13},{13,9},{9,1},{2,6},{6,14},{... | collective-permute-start | bytes 196616 | tf_op jit(solution)/shard_map/ppermute | solution.py:142
  11.4 4.3 %collective-permute-start.5 = (bf16[256,128]{1,0:T(8,128)(2,1)S(1)}, bf16[256,128]{1,0:T(8,128)(2,1)S(1)}, u32[]{:S(2)}, u32[]{:S(2)}) collective-permute-start(bf16[256,128]{1,0:T(8,128)(2,1)S(1)} %get-tuple-element.64), channel_id=1, source_target_pairs={{0,8},{4,0},{12,4},{8,12},{1,9},{5,1},{13,5},{9,13},{2,10},{6,2},{... | collective-permute-start | bytes 196616 | tf_op jit(solution)/shard_map/ppermute | solution.py:142
  15.7 6.6 %copy-start.2 = (f32[512]{0:T(512)S(1)}, f32[512]{0:T(512)}, u32[]{:S(2)}) copy-start(f32[512]{0:T(512)} %param.15) | copy-start | bytes 6148
  15.7 21.3 %copy-start = (bf16[2,1,256,256]{3,2,1,0:T(8,128)(2,1)S(1)}, bf16[2,1,256,256]{3,2,1,0:T(8,128)(2,1)}, u32[]{:S(2)}) copy-start(bf16[2,1,256,256]{3,2,1,0:T(8,128)(2,1)} %param.9) | copy-start | bytes 786436
  15.8 6.5 %copy-start.1 = (f32[4,256]{1,0:T(4,128)S(1)}, f32[4,256]{1,0:T(4,128)}, u32[]{:S(2)}) copy-start(f32[4,256]{1,0:T(4,128)} %left_diag.1) | copy-start | bytes 12292
  15.8 7.9 %collective-permute-start.10 = (bf16[1,256,256]{2,1,0:T(8,128)(2,1)S(1)}, bf16[1,256,256]{2,1,0:T(8,128)(2,1)S(1)}, u32[]{:S(2)}, u32[]{:S(2)}) collective-permute-start(bf16[1,256,256]{2,1,0:T(8,128)(2,1)S(1)} %get-tuple-element.119), channel_id=1, source_target_pairs={{0,2},{1,3},{2,0},{3,1},{4,6},{5,7},{6,4},{7,5},{8,10},{9,11},{10,... | collective-permute-start | bytes 393224 | tf_op jit(solution)/shard_map/ppermute | solution.py:146
  17.3 7.2 %collective-permute-start.9 = (bf16[1,256,256]{2,1,0:T(8,128)(2,1)S(1)}, bf16[1,256,256]{2,1,0:T(8,128)(2,1)S(1)}, u32[]{:S(2)}, u32[]{:S(2)}) collective-permute-start(bf16[1,256,256]{2,1,0:T(8,128)(2,1)S(1)} %get-tuple-element.119), channel_id=1, source_target_pairs={{0,4},{4,12},{12,8},{8,0},{1,5},{5,13},{13,9},{9,1},{2,6},{6,14},{... | collective-permute-start | bytes 393224 | tf_op jit(solution)/shard_map/ppermute | solution.py:142
  18.7 3.6 %copy-start.4 = (s32[4]{0:T(128)S(1)}, s32[4]{0:T(128)}, u32[]{:S(2)}) copy-start(s32[4]{0:T(128)} %sector.1) | copy-start | bytes 52
  18.7 3.6 %copy-start.5 = (s32[4]{0:T(128)S(1)}, s32[4]{0:T(128)}, u32[]{:S(2)}) copy-start(s32[4]{0:T(128)} %width.1) | copy-start | bytes 52
  18.7 9.7 %collective-permute-start.7 = (bf16[1,256,256]{2,1,0:T(8,128)(2,1)S(1)}, bf16[1,256,256]{2,1,0:T(8,128)(2,1)S(1)}, u32[]{:S(2)}, u32[]{:S(2)}) collective-permute-start(bf16[1,256,256]{2,1,0:T(8,128)(2,1)S(1)} %get-tuple-element.120), channel_id=1, source_target_pairs={{0,2},{1,3},{2,0},{3,1},{4,6},{5,7},{6,4},{7,5},{8,10},{9,11},{10,... | collective-permute-start | bytes 393224 | tf_op jit(solution)/shard_map/ppermute | solution.py:146
  19.2 9.2 %collective-permute-start.6 = (bf16[1,256,256]{2,1,0:T(8,128)(2,1)S(1)}, bf16[1,256,256]{2,1,0:T(8,128)(2,1)S(1)}, u32[]{:S(2)}, u32[]{:S(2)}) collective-permute-start(bf16[1,256,256]{2,1,0:T(8,128)(2,1)S(1)} %get-tuple-element.120), channel_id=1, source_target_pairs={{0,4},{4,12},{12,8},{8,0},{1,5},{5,13},{13,9},{9,1},{2,6},{6,14},{... | collective-permute-start | bytes 393224 | tf_op jit(solution)/shard_map/ppermute | solution.py:142
  21.7 6.7 %collective-permute-start.8 = (bf16[256,128]{1,0:T(8,128)(2,1)S(1)}, bf16[256,128]{1,0:T(8,128)(2,1)S(1)}, u32[]{:S(2)}, u32[]{:S(2)}) collective-permute-start(bf16[256,128]{1,0:T(8,128)(2,1)S(1)} %get-tuple-element.68), channel_id=1, source_target_pairs={{0,12},{4,8},{12,0},{8,4},{1,13},{5,9},{13,1},{9,5},{2,14},{6,10},... | collective-permute-start | bytes 196616 | tf_op jit(solution)/shard_map/ppermute | solution.py:142
  24.5 6.2 %collective-permute-start.12 = (bf16[1,256,256]{2,1,0:T(8,128)(2,1)S(1)}, bf16[1,256,256]{2,1,0:T(8,128)(2,1)S(1)}, u32[]{:S(2)}, u32[]{:S(2)}) collective-permute-start(bf16[1,256,256]{2,1,0:T(8,128)(2,1)S(1)} %collective-permute-done.9.refs_0_), channel_id=1, source_target_pairs={{0,2},{1,3},{2,0},{3,1},{4,6},{5,7},{6,4},{7,5},{8,10},{9,11},{10,... | collective-permute-start | bytes 393224 | tf_op jit(solution)/shard_map/ppermute | solution.py:146
  25.2 6.9 %collective-permute-start.11 = (bf16[1,256,256]{2,1,0:T(8,128)(2,1)S(1)}, bf16[1,256,256]{2,1,0:T(8,128)(2,1)S(1)}, u32[]{:S(2)}, u32[]{:S(2)}) collective-permute-start(bf16[1,256,256]{2,1,0:T(8,128)(2,1)S(1)} %collective-permute-done.9.refs_0_), channel_id=1, source_target_pairs={{0,4},{4,12},{12,8},{8,0},{1,5},{5,13},{13,9},{9,1},{2,6},{6,14},{... | collective-permute-start | bytes 393224 | tf_op jit(solution)/shard_map/ppermute | solution.py:142
  28.4 5.3 %collective-permute-start.14 = (bf16[1,256,256]{2,1,0:T(8,128)(2,1)S(1)}, bf16[1,256,256]{2,1,0:T(8,128)(2,1)S(1)}, u32[]{:S(2)}, u32[]{:S(2)}) collective-permute-start(bf16[1,256,256]{2,1,0:T(8,128)(2,1)S(1)} %collective-permute-done.6.refs_1_), channel_id=1, source_target_pairs={{0,2},{1,3},{2,0},{3,1},{4,6},{5,7},{6,4},{7,5},{8,10},{9,11},{10,... | collective-permute-start | bytes 393224 | tf_op jit(solution)/shard_map/ppermute | solution.py:146
  28.8 6.8 %collective-permute-start.13 = (bf16[1,256,256]{2,1,0:T(8,128)(2,1)S(1)}, bf16[1,256,256]{2,1,0:T(8,128)(2,1)S(1)}, u32[]{:S(2)}, u32[]{:S(2)}) collective-permute-start(bf16[1,256,256]{2,1,0:T(8,128)(2,1)S(1)} %collective-permute-done.6.refs_1_), channel_id=1, source_target_pairs={{0,4},{4,12},{12,8},{8,0},{1,5},{5,13},{13,9},{9,1},{2,6},{6,14},{... | collective-permute-start | bytes 393224 | tf_op jit(solution)/shard_map/ppermute | solution.py:142
  30.7 3.0 %collective-permute-start.15 = (bf16[256,128]{1,0:T(8,128)(2,1)S(1)}, bf16[256,128]{1,0:T(8,128)(2,1)S(1)}, u32[]{:S(2)}, u32[]{:S(2)}) collective-permute-start(bf16[256,128]{1,0:T(8,128)(2,1)S(1)} %collective-permute-done.4.refs_6_), channel_id=1, source_target_pairs={{0,1},{1,0},{2,3},{3,2},{4,5},{5,4},{6,7},{7,6},{8,9},{9,8},{10,11... | collective-permute-start | bytes 196616 | tf_op jit(solution)/shard_map/ppermute | solution.py:146
  32.2 6.5 %collective-permute-start.16 = (bf16[1,256,256]{2,1,0:T(8,128)(2,1)S(1)}, bf16[1,256,256]{2,1,0:T(8,128)(2,1)S(1)}, u32[]{:S(2)}, u32[]{:S(2)}) collective-permute-start(bf16[1,256,256]{2,1,0:T(8,128)(2,1)S(1)} %collective-permute-done.11.refs_4_), channel_id=1, source_target_pairs={{0,2},{1,3},{2,0},{3,1},{4,6},{5,7},{6,4},{7,5},{8,10},{9,11},{10,... | collective-permute-start | bytes 393224 | tf_op jit(solution)/shard_map/ppermute | solution.py:146
  35.6 5.0 %collective-permute-start.17 = (bf16[1,256,256]{2,1,0:T(8,128)(2,1)S(1)}, bf16[1,256,256]{2,1,0:T(8,128)(2,1)S(1)}, u32[]{:S(2)}, u32[]{:S(2)}) collective-permute-start(bf16[1,256,256]{2,1,0:T(8,128)(2,1)S(1)} %collective-permute-done.13.refs_5_), channel_id=1, source_target_pairs={{0,2},{1,3},{2,0},{3,1},{4,6},{5,7},{6,4},{7,5},{8,10},{9,11},{10,... | collective-permute-start | bytes 393224 | tf_op jit(solution)/shard_map/ppermute | solution.py:146
  36.5 2.2 %collective-permute-start.19 = (bf16[256,128]{1,0:T(8,128)(2,1)S(1)}, bf16[256,128]{1,0:T(8,128)(2,1)S(1)}, u32[]{:S(2)}, u32[]{:S(2)}) collective-permute-start(bf16[256,128]{1,0:T(8,128)(2,1)S(1)} %collective-permute-done.5.refs_12_), channel_id=1, source_target_pairs={{0,1},{1,0},{2,3},{3,2},{4,5},{5,4},{6,7},{7,6},{8,9},{9,8},{10,11... | collective-permute-start | bytes 196616 | tf_op jit(solution)/shard_map/ppermute | solution.py:146
  36.5 2.2 %collective-permute-start.18 = (bf16[256,128]{1,0:T(8,128)(2,1)S(1)}, bf16[256,128]{1,0:T(8,128)(2,1)S(1)}, u32[]{:S(2)}, u32[]{:S(2)}) collective-permute-start(bf16[256,128]{1,0:T(8,128)(2,1)S(1)} %collective-permute-done.8.refs_10_), channel_id=1, source_target_pairs={{0,1},{1,0},{2,3},{3,2},{4,5},{5,4},{6,7},{7,6},{8,9},{9,8},{10,11... | collective-permute-start | bytes 196616 | tf_op jit(solution)/shard_map/ppermute | solution.py:146
  43.0 12.9 %collective-permute-start.20 = (bf16[4,256,256]{2,1,0:T(8,128)(2,1)S(1)}, bf16[4,256,256]{2,1,0:T(8,128)(2,1)S(1)}, u32[]{:S(2)}, u32[]{:S(2)}) collective-permute-start(bf16[4,256,256]{2,1,0:T(8,128)(2,1)S(1)} %get-tuple-element.104.refs_4_), channel_id=1, source_target_pairs={{0,1},{1,0},{2,3},{3,2},{4,5},{5,4},{6,7},{7,6},{8,9},{9,8},{10,11... | collective-permute-start | bytes 1572872 | tf_op jit(solution)/shard_map/ppermute | solution.py:146
  43.1 12.9 %collective-permute-start.21 = (bf16[2,4,64,256]{3,2,1,0:T(8,128)(2,1)S(1)}, bf16[2,4,64,256]{3,2,1,0:T(8,128)(2,1)S(1)}, u32[]{:S(2)}, u32[]{:S(2)}) collective-permute-start(bf16[2,4,64,256]{3,2,1,0:T(8,128)(2,1)S(1)} %get-tuple-element.105), channel_id=1, source_target_pairs={{0,2},{1,3},{2,0},{3,1},{4,6},{5,7},{6,4},{7,5},{8,10},{9,11},{10,... | collective-permute-start | bytes 786440 | tf_op jit(solution)/shard_map/ppermute | solution.py:146
  44.1 11.9 %collective-permute-start.22 = (bf16[1,4,64,256]{3,2,1,0:T(8,128)(2,1)S(1)}, bf16[1,4,64,256]{3,2,1,0:T(8,128)(2,1)S(1)}, u32[]{:S(2)}, u32[]{:S(2)}) collective-permute-start(bf16[1,4,64,256]{3,2,1,0:T(8,128)(2,1)S(1)} %get-tuple-element.106), channel_id=1, source_target_pairs={{0,3},{1,2},{2,1},{3,0},{4,7},{5,6},{6,5},{7,4},{8,11},{9,10},{10,... | collective-permute-start | bytes 393224 | tf_op jit(solution)/shard_map/ppermute | solution.py:146
  60.8 12.6 %collective-permute-start.24 = (bf16[2,4,64,256]{3,2,1,0:T(8,128)(2,1)S(1)}, bf16[2,4,64,256]{3,2,1,0:T(8,128)(2,1)S(1)}, u32[]{:S(2)}, u32[]{:S(2)}) collective-permute-start(bf16[2,4,64,256]{3,2,1,0:T(8,128)(2,1)S(1)} %get-tuple-element.117), channel_id=1, source_target_pairs={{0,2},{1,3},{2,0},{3,1},{4,6},{5,7},{6,4},{7,5},{8,10},{9,11},{10,... | collective-permute-start | bytes 786440 | tf_op jit(solution)/shard_map/ppermute | solution.py:146
  61.1 12.2 %collective-permute-start.23 = (bf16[1,4,64,256]{3,2,1,0:T(8,128)(2,1)S(1)}, bf16[1,4,64,256]{3,2,1,0:T(8,128)(2,1)S(1)}, u32[]{:S(2)}, u32[]{:S(2)}) collective-permute-start(bf16[1,4,64,256]{3,2,1,0:T(8,128)(2,1)S(1)} %get-tuple-element.116), channel_id=1, source_target_pairs={{0,1},{1,0},{2,3},{3,2},{4,5},{5,4},{6,7},{7,6},{8,9},{9,8},{10,11... | collective-permute-start | bytes 393224 | tf_op jit(solution)/shard_map/ppermute | solution.py:146
  61.1 12.2 %collective-permute-start.25 = (bf16[1,4,64,256]{3,2,1,0:T(8,128)(2,1)S(1)}, bf16[1,4,64,256]{3,2,1,0:T(8,128)(2,1)S(1)}, u32[]{:S(2)}, u32[]{:S(2)}) collective-permute-start(bf16[1,4,64,256]{3,2,1,0:T(8,128)(2,1)S(1)} %get-tuple-element.118), channel_id=1, source_target_pairs={{0,3},{1,2},{2,1},{3,0},{4,7},{5,6},{6,5},{7,4},{8,11},{9,10},{10,... | collective-permute-start | bytes 393224 | tf_op jit(solution)/shard_map/ppermute | solution.py:146

commit v16 on v13

--- a/solution.py
+++ b/solution.py
@@ -285,12 +285,12 @@
 
 
 def spread(values, out):
-    line = lax.broadcasted_iota(jnp.int32, out.shape[1:], 0)
-    tile = jnp.zeros(out.shape[1:], jnp.float32)
+    lane = lax.broadcasted_iota(jnp.int32, out.shape[1:], 1)
+    row = jnp.zeros(out.shape[1:], jnp.float32)
     for j, value in enumerate(values):
-        tile = jnp.where(line == j, value, tile)
+        row = jnp.where(lane == j, value, row)
     for d in range(out.shape[0]):
-        out[d] = tile
+        out[d] = row
 
 
 def by_block(packed, terms, k):
@@ -431,8 +431,8 @@
 
 def norm_theta(parts, count):
     tot = jnp.sum(parts, axis=0) * (1.0 / count)
-    scale = lax.rsqrt(tot[0:1] + EPS)
-    return scale, tot[1:2] * scale * scale
+    scale = lax.rsqrt(tot[:, 0:1] + EPS)
+    return scale, tot[:, 1:2] * scale * scale
 
 
 def second_body(n_blk, n_pair, count, src, widths, left_early, left_late, *refs):
@@ -464,12 +464,13 @@
         halves.append((whole(vv), whole(vc), whole(vs)))
     along = (halves[0][1] + halves[1][1]) / jnp.maximum(halves[0][0] + halves[1][0], 1e-30)
     terms = held.shape[2]
+    for copy in copies:
+        copy.wait()
     for d in range(n_blk):
         for h in range(2):
             part = slice(h * cols, (h + 1) * cols)
             vec = raw_in[d, :, part].astype(jnp.float32) * scale
             fld[d, :, part] = (corr[d, :, part] - along * vec).astype(jnp.bfloat16)
-        copies[d].wait()
         left_products(fld[d], lambda at: held[d, at // terms], inter.at[d])
     zero = jnp.zeros((8, cols), jnp.float32)
     sums = [zero for _ in range(5)]
@@ -521,7 +522,7 @@
     scale, theta = norm_theta(parts1[...], count)
     pairs = parts2[...].reshape(n_blk * n_op // 2, 2, *parts2.shape[1:])
     pairs = pairs[:, 0] + pairs[:, 1]
-    vv, vc, vs, ff, vf, fs, vt, ft = (pairs[:, j, :] for j in range(8))
+    vv, vc, vs, ff, vf, fs, vt, ft = (pairs[:, 0, j : j + 1] for j in range(8))
 
     def mean(x):
         return jnp.sum(x, axis=0, keepdims=True) * (1.0 / count)
@@ -543,7 +544,7 @@
     for e in range(0, n_op, 2):
         there = own_blk * n_op + (own_op ^ e)
         pair = parts2[there] + parts2[own_blk * n_op + (own_op ^ e ^ 1)]
-        on_vec = cv + cu * (nearest(pair[0:1], pair[1:2]) - along)
+        on_vec = cv + cu * (nearest(pair[:, 0:1], pair[:, 1:2]) - along)
         for h in range(2):
             at = pl.multiple_of((own_op ^ e ^ h) * cols, LANES)
             part, crossed = slice(h * cols, (h + 1) * cols), slice((1 - h) * cols, (2 - h) * cols)
@@ -634,7 +635,7 @@
 
     tables = [(src, SMEM), (widths, SMEM)]
     narrow = ((n_blk, rows, 2 * cols), bf16, VMEM)
-    dots = ((n_dev, 8, LANES), f32, VMEM)
+    dots = ((n_dev, 1, LANES), f32, VMEM)
     sends = [((2 - e % 2, n_blk, step, 2 * cols), bf16, VMEM) for e in range(1, n_op)]
     inter = pltpu.VMEM((n_blk + 1, n_pair * terms, rows, 2 * cols), bf16)
     left_late = (n_late, n_pair, terms, rows, rows)

time: 74.7 us -> 73.8 us (0.988)
  blocking collectives: 20.4 us -> 19.3 us
    all_to_all x2, blocking collectives: 20.4 us -> 19.3 us  [totals(): return lax.all_to_all(parts, ('blk', 'op'), 0, 0, tiled=True)]
where the time goes in v16:
time: 73.8 us; the launch traced here: 73.6 us
  waiting for transfers between devices  19.7 us (27%)
  starting transfers between devices  19.5 us (26%)
  blocking collectives  19.3 us (26%)
  Pallas kernels  14.2 us (19%)
    all_to_all x2, blocking collectives, totals(): return lax.all_to_all(parts, ('blk', 'op'), 0, 0, tiled=True)  19.3 us
    pallas_call x6, Pallas kernels, kernel(): pl.pallas_call(body, out_shape=[HBM(shape, dtype) if space == HBM else ja...  14.2 us
    ppermute x6, waiting for transfers between devices, onward(): return lax.ppermute(block, 'blk', pairs)  13.3 us
    ppermute x6, starting transfers between devices, onward(): return lax.ppermute(block, 'blk', pairs)  11.2 us
    ppermute x14, starting transfers between devices, swap(): return lax.ppermute(block, 'op', [(i, i ^ e) for i in range(n_op)])  8.26 us
    ppermute x14, waiting for transfers between devices, swap(): return lax.ppermute(block, 'op', [(i, i ^ e) for i in range(n_op)])  6.38 us
  transfers between devices with their start and end apart: 20, of which 7 were waited for; matrix products, arithmetic and copies ran while one was open for 0% of the time, Pallas kernels for 7%

profile of v16, /device:TPU:0, one launch (start us, length us, event | category | flops | bytes accessed | tf_op | source)
XLA Modules:
  0.0 73.6 jit_solution(613028387404459783)
XLA Ops:
  0.6 0.0 copy-start.3
  0.6 3.1 %collective-permute-start.1 = (bf16[2,256,256]{2,1,0:T(8,128)(2,1)}, bf16[2,256,256]{2,1,0:T(8,128)(2,1)S(1)}, u32[]{:S(2)}, u32[]{:S(2)}) collective-permute-start(bf16[2,256,256]{2,1,0:T(8,128)(2,1)} %bitcast.2), channel_id=1, source_target_pairs={{0,4},{4,12},{12,8},{8,0},{1,5},{5,13},{13,9},{9,1},{2,6},{6,14},{... | collective-permute-start | bytes 786440 | tf_op jit(solution)/shard_map/ppermute | solution.py:142
  3.7 1.5 %collective-permute-start = (bf16[2,256,256]{2,1,0:T(8,128)(2,1)}, bf16[2,256,256]{2,1,0:T(8,128)(2,1)S(1)}, u32[]{:S(2)}, u32[]{:S(2)}) collective-permute-start(bf16[2,256,256]{2,1,0:T(8,128)(2,1)} %bitcast.3), channel_id=1, source_target_pairs={{0,2},{1,3},{2,0},{3,1},{4,6},{5,7},{6,4},{7,5},{8,10},{9,11},{10,... | collective-permute-start | bytes 786440 | tf_op jit(solution)/shard_map/ppermute | solution.py:146
  5.2 0.0 copy-done.3
  5.2 0.0 collective-permute-start.2
  5.2 1.1 %collective-permute-done.2._ = s32[2]{0:T(128)S(1)} collective-permute-done((s32[2]{0:T(128)S(1)}, s32[2]{0:T(128)S(1)}, u32[]{:S(2)}, u32[]{:S(2)}) %collective-permute-start.2) | collective-permute-done | bytes 40 | tf_op jit(solution)/shard_map/ppermute | solution.py:146
  6.3 0.0 copy-start
  6.3 1.9 %shard_map.103 = (bf16[256,256]{1,0:T(8,128)(2,1)S(1)}, bf16[256,128]{1,0:T(8,128)(2,1)S(1)}, bf16[256,256]{1,0:T(8,128)(2,1)S(1)}, bf16[256,128]{1,0:T(8,128)(2...) custom-call(s32[2]{0:T(128)S(1)} %copy-done.3, s32[2]{0:T(128)S(1)} %collective-permute-done.2._, ...), custom_call_target="tpu_custom_call" | custom-call | bytes 1048576 | tf_op jit(solution)/shard_map/pallas_call | solution.py:113
  8.2 0.0 copy-start.1
  8.3 0.6 collective-permute-start.3
  8.9 4.4 %collective-permute-done.3.refs_1_.refs_5_ = bf16[144,256]{1,0:T(8,128)(2,1)S(1)} collective-permute-done((bf16[144,256]{1,0:T(8,128)(2,1)S(1)}, bf16[144,256]{1,0:T(8,128)(2,1)S(1)}, u32[]{:S(2)}, u32[]{:S(2)}) %collective-permute-start.3) | collective-permute-done | bytes 73760 | tf_op jit(solution)/shard_map/ppermute | solution.py:146
  13.3 0.0 collective-permute-done.1.refs_2_
  13.3 0.0 collective-permute-done.refs_1_
  13.3 0.0 copy-start.2
  13.3 2.6 %collective-permute-start.5 = (bf16[2,256,256]{2,1,0:T(8,128)(2,1)S(1)}, bf16[2,256,256]{2,1,0:T(8,128)(2,1)S(1)}, u32[]{:S(2)}, u32[]{:S(2)}) collective-permute-start(bf16[2,256,256]{2,1,0:T(8,128)(2,1)S(1)} %collective-permute-done.1.refs_2_), channel_id=1, source_target_pairs={{0,4},{4,12},{12,8},{8,0},{1,5},{5,13},{13,9},{9,1},{2,6},{6,14},{... | collective-permute-start | bytes 786440 | tf_op jit(solution)/shard_map/ppermute | solution.py:142
  15.9 1.5 %collective-permute-start.4 = (bf16[2,256,256]{2,1,0:T(8,128)(2,1)S(1)}, bf16[2,256,256]{2,1,0:T(8,128)(2,1)S(1)}, u32[]{:S(2)}, u32[]{:S(2)}) collective-permute-start(bf16[2,256,256]{2,1,0:T(8,128)(2,1)S(1)} %collective-permute-done.1.refs_2_), channel_id=1, source_target_pairs={{0,2},{1,3},{2,0},{3,1},{4,6},{5,7},{6,4},{7,5},{8,10},{9,11},{10,... | collective-permute-start | bytes 786440 | tf_op jit(solution)/shard_map/ppermute | solution.py:146
  17.4 0.0 copy-start.4
  17.4 0.0 copy-start.5
  17.4 0.4 collective-permute-start.6
  17.9 0.0 copy-done.1
  17.9 0.0 copy-done.2
  17.9 0.2 copy-done.4
  18.1 0.0 copy-done.5
  18.1 1.3 %shard_map.104 = (s32[16]{0:T(128)S(1)}, s32[4]{0:T(128)S(1)}, s32[4]{0:T(128)S(1)}, f32[4,256,128]{2,1,0:T(8,128)S(1)}, f32[1,512]{1,0:T(1,128)S(1)}) custom-call(s32[4]{0:T(128)S(1)} %copy-done.4, s32[4]{0:T(128)S(1)} %copy-done.5, f32[4,256]{1,0:T(4,128)S(1)} %copy-done.1, f32[1,512]{1,0:T(1,128)S(1)} %bitcast.5, ...), custom_call_target="tpu_custom_call" | custom-call | tf_op jit(solution)/shard_map/pallas_call | solution.py:113
  19.4 4.0 %collective-permute-done.6.refs_5_ = bf16[256,128]{1,0:T(8,128)(2,1)S(1)} collective-permute-done((bf16[256,128]{1,0:T(8,128)(2,1)S(1)}, bf16[256,128]{1,0:T(8,128)(2,1)S(1)}, u32[]{:S(2)}, u32[]{:S(2)}) %collective-permute-start.6) | collective-permute-done | bytes 65568 | tf_op jit(solution)/shard_map/ppermute | solution.py:142
  23.5 0.0 collective-permute-done.5.refs_0_
  23.5 0.0 collective-permute-done.4.refs_3_
  23.5 1.7 %collective-permute-start.8 = (bf16[2,256,256]{2,1,0:T(8,128)(2,1)S(1)}, bf16[2,256,256]{2,1,0:T(8,128)(2,1)S(1)}, u32[]{:S(2)}, u32[]{:S(2)}) collective-permute-start(bf16[2,256,256]{2,1,0:T(8,128)(2,1)S(1)} %collective-permute-done.5.refs_0_), channel_id=1, source_target_pairs={{0,4},{4,12},{12,8},{8,0},{1,5},{5,13},{13,9},{9,1},{2,6},{6,14},{... | collective-permute-start | bytes 786440 | tf_op jit(solution)/shard_map/ppermute | solution.py:142
  25.2 0.5 collective-permute-start.7
  25.7 1.2 %collective-permute-start.10 = (bf16[256,128]{1,0:T(8,128)(2,1)S(1)}, bf16[256,128]{1,0:T(8,128)(2,1)S(1)}, u32[]{:S(2)}, u32[]{:S(2)}) collective-permute-start(bf16[256,128]{1,0:T(8,128)(2,1)S(1)} %get-tuple-element.70), channel_id=1, source_target_pairs={{0,8},{4,0},{12,4},{8,12},{1,9},{5,1},{13,5},{9,13},{2,10},{6,2},{... | collective-permute-start | bytes 196616 | tf_op jit(solution)/shard_map/ppermute | solution.py:142
  26.9 0.0 collective-permute-start.9
  26.9 5.7 %collective-permute-done.10.refs_7_ = bf16[256,128]{1,0:T(8,128)(2,1)S(1)} collective-permute-done((bf16[256,128]{1,0:T(8,128)(2,1)S(1)}, bf16[256,128]{1,0:T(8,128)(2,1)S(1)}, u32[]{:S(2)}, u32[]{:S(2)}) %collective-permute-start.10) | collective-permute-done | bytes 65568 | tf_op jit(solution)/shard_map/ppermute | solution.py:142
  32.6 0.0 collective-permute-done.9.refs_6_
  32.6 0.1 collective-permute-done.8.refs_2_
  32.7 0.0 collective-permute-done.7.refs_1_
  32.7 0.0 collective-permute-start.11
  32.7 2.2 %collective-permute-start.13 = (bf16[256,256]{1,0:T(8,128)(2,1)S(1)}, bf16[256,256]{1,0:T(8,128)(2,1)S(1)}, u32[]{:S(2)}, u32[]{:S(2)}) collective-permute-start(bf16[256,256]{1,0:T(8,128)(2,1)S(1)} %get-tuple-element.81), channel_id=1, source_target_pairs={{0,12},{4,8},{12,0},{8,4},{1,13},{5,9},{13,1},{9,5},{2,14},{6,10},... | collective-permute-start | bytes 393224 | tf_op jit(solution)/shard_map/ppermute | solution.py:142
  34.9 0.0 collective-permute-start.12
  34.9 0.0 copy-done
  34.9 1.7 %shard_map.105 = (bf16[2,256,256]{2,1,0:T(8,128)(2,1)S(1)}, bf16[2,4,256,256]{3,2,1,0:T(8,128)(2,1)S(1)}, bf16[2,2,2,256,256]{4,3,2,1,0:T(8,128)(2,1)}) custom-call(s32[4]{0:T(128)S(1)} %get-tuple-element.67.widths, bf16[2,256,256]{2,1,0:T(8,128)(2,1)S(1)} %bitcast.4, bf16[2,256,256]{2,1,0:T(8,128)(2,1)S(1)} %collective-permute-done.refs_1_, ...), custom_call_target="tpu_custom_call" | custom-call | flops 268435456 | bytes 4194304 | tf_op jit(solution)/shard_map/pallas_call | solution.py:113
  36.6 3.5 %collective-permute-done.13.refs_6_ = bf16[256,256]{1,0:T(8,128)(2,1)S(1)} collective-permute-done((bf16[256,256]{1,0:T(8,128)(2,1)S(1)}, bf16[256,256]{1,0:T(8,128)(2,1)S(1)}, u32[]{:S(2)}, u32[]{:S(2)}) %collective-permute-start.13) | collective-permute-done | bytes 131104 | tf_op jit(solution)/shard_map/ppermute | solution.py:142
  40.0 0.0 collective-permute-done.12.refs_8_
  40.0 0.8 %collective-permute-done.11.refs_3_ = bf16[2,256,256]{2,1,0:T(8,128)(2,1)S(1)} collective-permute-done((bf16[2,256,256]{2,1,0:T(8,128)(2,1)S(1)}, bf16[2,256,256]{2,1,0:T(8,128)(2,1)S(1)}, u32[]{:S(2)}, u32[]{:S(2)}) %collective-permute-start.11) | collective-permute-done | bytes 262176 | tf_op jit(solution)/shard_map/ppermute | solution.py:146
  40.8 2.4 %shard_map.106 = (bf16[4,256,256]{2,1,0:T(8,128)(2,1)S(1)}, bf16[4,256,256]{2,1,0:T(8,128)(2,1)S(1)}, bf16[2,2,2,256,256]{4,3,2,1,0:T(8,128)(2,1)}, f32[16,1,128...) custom-call(s32[16]{0:T(128)S(1)} %get-tuple-element.66.src, ...), custom_call_target="tpu_custom_call" | custom-call | flops 1073741824 | bytes 6291456 | tf_op jit(solution)/shard_map/pallas_call | solution.py:113
  43.3 0.1 collective-permute-start.14
  43.4 0.9 %collective-permute-start.15 = (bf16[2,4,64,256]{3,2,1,0:T(8,128)(2,1)S(1)}, bf16[2,4,64,256]{3,2,1,0:T(8,128)(2,1)S(1)}, u32[]{:S(2)}, u32[]{:S(2)}) collective-permute-start(bf16[2,4,64,256]{3,2,1,0:T(8,128)(2,1)S(1)} %get-tuple-element.91), channel_id=1, source_target_pairs={{0,2},{1,3},{2,0},{3,1},{4,6},{5,7},{6,4},{7,5},{8,10},{9,11},{10,... | collective-permute-start | bytes 786440 | tf_op jit(solution)/shard_map/ppermute | solution.py:146
  44.3 0.9 %collective-permute-start.16 = (bf16[1,4,64,256]{3,2,1,0:T(8,128)(2,1)S(1)}, bf16[1,4,64,256]{3,2,1,0:T(8,128)(2,1)S(1)}, u32[]{:S(2)}, u32[]{:S(2)}) collective-permute-start(bf16[1,4,64,256]{3,2,1,0:T(8,128)(2,1)S(1)} %get-tuple-element.92), channel_id=1, source_target_pairs={{0,3},{1,2},{2,1},{3,0},{4,7},{5,6},{6,5},{7,4},{8,11},{9,10},{10,... | collective-permute-start | bytes 393224 | tf_op jit(solution)/shard_map/ppermute | solution.py:146
  45.2 9.7 %all_to_all.10.refs_2_.parts1 = f32[16,1,128]{2,1,0:T(1,128)S(1)} all-to-all(f32[16,1,128]{2,1,0:T(1,128)S(1)} %get-tuple-element.89), channel_id=1, replica_groups=mesh['grp'=2,'blk'=4,'op'=4] {'blk','op'}, dimensions={0} | all-to-all | bytes 16384 | tf_op jit(solution)/shard_map/all_to_all | solution.py:645
  55.0 0.0 collective-permute-done.16.refs_1_
  55.0 0.0 collective-permute-done.15.refs_0_
  55.0 0.0 collective-permute-done.14.refs_5_
  55.0 4.8 %shard_map.107 = (f32[16,1,128]{2,1,0:T(1,128)S(1)}, bf16[4,4,64,256]{3,2,1,0:T(8,128)(2,1)S(1)}, bf16[1,4,64,256]{3,2,1,0:T(8,128)(2,1)S(1)}, bf16[2,4,64,256]{...) custom-call(s32[16]{0:T(128)S(1)} %get-tuple-element.66.src, s32[4]{0:T(128)S(1)} %get-tuple-element.67.widths, ...), custom_call_target="tpu_custom_call" | custom-call | flops 1073741824 | bytes 6291456 | tf_op jit(solution)/shard_map/pallas_call | solution.py:113
  59.8 0.9 %collective-permute-start.18 = (bf16[2,4,64,256]{3,2,1,0:T(8,128)(2,1)S(1)}, bf16[2,4,64,256]{3,2,1,0:T(8,128)(2,1)S(1)}, u32[]{:S(2)}, u32[]{:S(2)}) collective-permute-start(bf16[2,4,64,256]{3,2,1,0:T(8,128)(2,1)S(1)} %get-tuple-element.103), channel_id=1, source_target_pairs={{0,2},{1,3},{2,0},{3,1},{4,6},{5,7},{6,4},{7,5},{8,10},{9,11},{10,... | collective-permute-start | bytes 786440 | tf_op jit(solution)/shard_map/ppermute | solution.py:146
  60.7 0.0 collective-permute-start.17
  60.7 1.3 %collective-permute-start.19 = (bf16[1,4,64,256]{3,2,1,0:T(8,128)(2,1)S(1)}, bf16[1,4,64,256]{3,2,1,0:T(8,128)(2,1)S(1)}, u32[]{:S(2)}, u32[]{:S(2)}) collective-permute-start(bf16[1,4,64,256]{3,2,1,0:T(8,128)(2,1)S(1)} %get-tuple-element.104), channel_id=1, source_target_pairs={{0,3},{1,2},{2,1},{3,0},{4,7},{5,6},{6,5},{7,4},{8,11},{9,10},{10,... | collective-permute-start | bytes 393224 | tf_op jit(solution)/shard_map/ppermute | solution.py:146
  62.0 9.5 %all_to_all.11.parts2 = f32[16,1,128]{2,1,0:T(1,128)S(1)} all-to-all(f32[16,1,128]{2,1,0:T(1,128)S(1)} %get-tuple-element.98), channel_id=1, replica_groups=mesh['grp'=2,'blk'=4,'op'=4] {'blk','op'}, dimensions={0} | all-to-all | bytes 16384 | tf_op jit(solution)/shard_map/all_to_all | solution.py:645
  71.6 0.0 collective-permute-done.17.refs_2_
  71.6 0.0 collective-permute-done.19.refs_4_
  71.6 0.0 collective-permute-done.18.refs_3_
  71.6 2.0 %shard_map.108 = (bf16[4,64,512]{2,1,0:T(8,128)(2,1)}, bf16[4,64,512]{2,1,0:T(8,128)(2,1)}, f32[1]{0:T(128)}) custom-call(s32[4]{0:T(128)S(1)} %get-tuple-element.65.slots, f32[16,1,128]{2,1,0:T(1,128)S(1)} %all_to_all.10.refs_2_.parts1, f32[16,1,128]{2,1,0:T(1,128)S(1)} %all_to_all.11.parts2, f32[4,256,128]{2,1,0:T(8,128)S(1)} %get-tuple-element.87.refs_11_.refs_6_.diag, ...), custom_call_target="tpu_custom_call" | custom-call | bytes 4194304 | tf_op jit(solution)/shard_map/pallas_call | solution.py:113
Async XLA Ops:
  0.6 4.6 %copy-start.3 = (s32[2]{0:T(128)S(1)}, s32[2]{0:T(128)}, u32[]{:S(2)}) copy-start(s32[2]{0:T(128)} %shift.1) | copy-start | bytes 28
  0.6 12.6 %collective-permute-start.1 = (bf16[2,256,256]{2,1,0:T(8,128)(2,1)}, bf16[2,256,256]{2,1,0:T(8,128)(2,1)S(1)}, u32[]{:S(2)}, u32[]{:S(2)}) collective-permute-start(bf16[2,256,256]{2,1,0:T(8,128)(2,1)} %bitcast.2), channel_id=1, source_target_pairs={{0,4},{4,12},{12,8},{8,0},{1,5},{5,13},{13,9},{9,1},{2,6},{6,14},{... | collective-permute-start | bytes 786440 | tf_op jit(solution)/shard_map/ppermute | solution.py:142
  3.7 9.6 %collective-permute-start = (bf16[2,256,256]{2,1,0:T(8,128)(2,1)}, bf16[2,256,256]{2,1,0:T(8,128)(2,1)S(1)}, u32[]{:S(2)}, u32[]{:S(2)}) collective-permute-start(bf16[2,256,256]{2,1,0:T(8,128)(2,1)} %bitcast.3), channel_id=1, source_target_pairs={{0,2},{1,3},{2,0},{3,1},{4,6},{5,7},{6,4},{7,5},{8,10},{9,11},{10,... | collective-permute-start | bytes 786440 | tf_op jit(solution)/shard_map/ppermute | solution.py:146
  5.2 1.1 %collective-permute-start.2 = (s32[2]{0:T(128)S(1)}, s32[2]{0:T(128)S(1)}, u32[]{:S(2)}, u32[]{:S(2)}) collective-permute-start(s32[2]{0:T(128)S(1)} %copy-done.3), channel_id=1, source_target_pairs={{0,1},{1,0},{2,3},{3,2},{4,5},{5,4},{6,7},{7,6},{8,9},{9,8},{10,11... | collective-permute-start | bytes 32 | tf_op jit(solution)/shard_map/ppermute | solution.py:146
  6.3 28.6 %copy-start = (bf16[2,1,256,256]{3,2,1,0:T(8,128)(2,1)S(1)}, bf16[2,1,256,256]{3,2,1,0:T(8,128)(2,1)}, u32[]{:S(2)}) copy-start(bf16[2,1,256,256]{3,2,1,0:T(8,128)(2,1)} %param.9) | copy-start | bytes 786436
  8.2 9.6 %copy-start.1 = (f32[4,256]{1,0:T(4,128)S(1)}, f32[4,256]{1,0:T(4,128)}, u32[]{:S(2)}) copy-start(f32[4,256]{1,0:T(4,128)} %left_diag.1) | copy-start | bytes 12292
  8.3 5.0 %collective-permute-start.3 = (bf16[144,256]{1,0:T(8,128)(2,1)S(1)}, bf16[144,256]{1,0:T(8,128)(2,1)S(1)}, u32[]{:S(2)}, u32[]{:S(2)}) collective-permute-start(bf16[144,256]{1,0:T(8,128)(2,1)S(1)} %get-tuple-element.55), channel_id=1, source_target_pairs={{0,2},{1,3},{2,0},{3,1},{4,6},{5,7},{6,4},{7,5},{8,10},{9,11},{10,... | collective-permute-start | bytes 221192 | tf_op jit(solution)/shard_map/ppermute | solution.py:146
  13.3 4.6 %copy-start.2 = (f32[512]{0:T(512)S(1)}, f32[512]{0:T(512)}, u32[]{:S(2)}) copy-start(f32[512]{0:T(512)} %param.15) | copy-start | bytes 6148
  13.3 10.2 %collective-permute-start.5 = (bf16[2,256,256]{2,1,0:T(8,128)(2,1)S(1)}, bf16[2,256,256]{2,1,0:T(8,128)(2,1)S(1)}, u32[]{:S(2)}, u32[]{:S(2)}) collective-permute-start(bf16[2,256,256]{2,1,0:T(8,128)(2,1)S(1)} %collective-permute-done.1.refs_2_), channel_id=1, source_target_pairs={{0,4},{4,12},{12,8},{8,0},{1,5},{5,13},{13,9},{9,1},{2,6},{6,14},{... | collective-permute-start | bytes 786440 | tf_op jit(solution)/shard_map/ppermute | solution.py:142
  15.9 7.5 %collective-permute-start.4 = (bf16[2,256,256]{2,1,0:T(8,128)(2,1)S(1)}, bf16[2,256,256]{2,1,0:T(8,128)(2,1)S(1)}, u32[]{:S(2)}, u32[]{:S(2)}) collective-permute-start(bf16[2,256,256]{2,1,0:T(8,128)(2,1)S(1)} %collective-permute-done.1.refs_2_), channel_id=1, source_target_pairs={{0,2},{1,3},{2,0},{3,1},{4,6},{5,7},{6,4},{7,5},{8,10},{9,11},{10,... | collective-permute-start | bytes 786440 | tf_op jit(solution)/shard_map/ppermute | solution.py:146
  17.4 0.7 copy-start.4
  17.4 0.7 copy-start.5
  17.4 6.0 %collective-permute-start.6 = (bf16[256,128]{1,0:T(8,128)(2,1)S(1)}, bf16[256,128]{1,0:T(8,128)(2,1)S(1)}, u32[]{:S(2)}, u32[]{:S(2)}) collective-permute-start(bf16[256,128]{1,0:T(8,128)(2,1)S(1)} %get-tuple-element.57), channel_id=1, source_target_pairs={{0,4},{4,12},{12,8},{8,0},{1,5},{5,13},{13,9},{9,1},{2,6},{6,14},{... | collective-permute-start | bytes 196616 | tf_op jit(solution)/shard_map/ppermute | solution.py:142
  23.5 9.3 %collective-permute-start.8 = (bf16[2,256,256]{2,1,0:T(8,128)(2,1)S(1)}, bf16[2,256,256]{2,1,0:T(8,128)(2,1)S(1)}, u32[]{:S(2)}, u32[]{:S(2)}) collective-permute-start(bf16[2,256,256]{2,1,0:T(8,128)(2,1)S(1)} %collective-permute-done.5.refs_0_), channel_id=1, source_target_pairs={{0,4},{4,12},{12,8},{8,0},{1,5},{5,13},{13,9},{9,1},{2,6},{6,14},{... | collective-permute-start | bytes 786440 | tf_op jit(solution)/shard_map/ppermute | solution.py:142
  25.2 7.6 %collective-permute-start.7 = (bf16[2,256,256]{2,1,0:T(8,128)(2,1)S(1)}, bf16[2,256,256]{2,1,0:T(8,128)(2,1)S(1)}, u32[]{:S(2)}, u32[]{:S(2)}) collective-permute-start(bf16[2,256,256]{2,1,0:T(8,128)(2,1)S(1)} %collective-permute-done.5.refs_0_), channel_id=1, source_target_pairs={{0,2},{1,3},{2,0},{3,1},{4,6},{5,7},{6,4},{7,5},{8,10},{9,11},{10,... | collective-permute-start | bytes 786440 | tf_op jit(solution)/shard_map/ppermute | solution.py:146
  25.7 6.9 %collective-permute-start.10 = (bf16[256,128]{1,0:T(8,128)(2,1)S(1)}, bf16[256,128]{1,0:T(8,128)(2,1)S(1)}, u32[]{:S(2)}, u32[]{:S(2)}) collective-permute-start(bf16[256,128]{1,0:T(8,128)(2,1)S(1)} %get-tuple-element.70), channel_id=1, source_target_pairs={{0,8},{4,0},{12,4},{8,12},{1,9},{5,1},{13,5},{9,13},{2,10},{6,2},{... | collective-permute-start | bytes 196616 | tf_op jit(solution)/shard_map/ppermute | solution.py:142
  26.9 5.7 %collective-permute-start.9 = (bf16[256,128]{1,0:T(8,128)(2,1)S(1)}, bf16[256,128]{1,0:T(8,128)(2,1)S(1)}, u32[]{:S(2)}, u32[]{:S(2)}) collective-permute-start(bf16[256,128]{1,0:T(8,128)(2,1)S(1)} %collective-permute-done.6.refs_5_), channel_id=1, source_target_pairs={{0,1},{1,0},{2,3},{3,2},{4,5},{5,4},{6,7},{7,6},{8,9},{9,8},{10,11... | collective-permute-start | bytes 196616 | tf_op jit(solution)/shard_map/ppermute | solution.py:146
  32.7 8.1 %collective-permute-start.11 = (bf16[2,256,256]{2,1,0:T(8,128)(2,1)S(1)}, bf16[2,256,256]{2,1,0:T(8,128)(2,1)S(1)}, u32[]{:S(2)}, u32[]{:S(2)}) collective-permute-start(bf16[2,256,256]{2,1,0:T(8,128)(2,1)S(1)} %collective-permute-done.8.refs_2_), channel_id=1, source_target_pairs={{0,2},{1,3},{2,0},{3,1},{4,6},{5,7},{6,4},{7,5},{8,10},{9,11},{10,... | collective-permute-start | bytes 786440 | tf_op jit(solution)/shard_map/ppermute | solution.py:146
  32.7 7.3 %collective-permute-start.13 = (bf16[256,256]{1,0:T(8,128)(2,1)S(1)}, bf16[256,256]{1,0:T(8,128)(2,1)S(1)}, u32[]{:S(2)}, u32[]{:S(2)}) collective-permute-start(bf16[256,256]{1,0:T(8,128)(2,1)S(1)} %get-tuple-element.81), channel_id=1, source_target_pairs={{0,12},{4,8},{12,0},{8,4},{1,13},{5,9},{13,1},{9,5},{2,14},{6,10},... | collective-permute-start | bytes 393224 | tf_op jit(solution)/shard_map/ppermute | solution.py:142
  34.9 5.1 %collective-permute-start.12 = (bf16[256,128]{1,0:T(8,128)(2,1)S(1)}, bf16[256,128]{1,0:T(8,128)(2,1)S(1)}, u32[]{:S(2)}, u32[]{:S(2)}) collective-permute-start(bf16[256,128]{1,0:T(8,128)(2,1)S(1)} %collective-permute-done.10.refs_7_), channel_id=1, source_target_pairs={{0,1},{1,0},{2,3},{3,2},{4,5},{5,4},{6,7},{7,6},{8,9},{9,8},{10,11... | collective-permute-start | bytes 196616 | tf_op jit(solution)/shard_map/ppermute | solution.py:146
  43.3 11.7 %collective-permute-start.14 = (bf16[4,256,256]{2,1,0:T(8,128)(2,1)S(1)}, bf16[4,256,256]{2,1,0:T(8,128)(2,1)S(1)}, u32[]{:S(2)}, u32[]{:S(2)}) collective-permute-start(bf16[4,256,256]{2,1,0:T(8,128)(2,1)S(1)} %get-tuple-element.90.refs_4_), channel_id=1, source_target_pairs={{0,1},{1,0},{2,3},{3,2},{4,5},{5,4},{6,7},{7,6},{8,9},{9,8},{10,11... | collective-permute-start | bytes 1572872 | tf_op jit(solution)/shard_map/ppermute | solution.py:146
  43.4 11.6 %collective-permute-start.15 = (bf16[2,4,64,256]{3,2,1,0:T(8,128)(2,1)S(1)}, bf16[2,4,64,256]{3,2,1,0:T(8,128)(2,1)S(1)}, u32[]{:S(2)}, u32[]{:S(2)}) collective-permute-start(bf16[2,4,64,256]{3,2,1,0:T(8,128)(2,1)S(1)} %get-tuple-element.91), channel_id=1, source_target_pairs={{0,2},{1,3},{2,0},{3,1},{4,6},{5,7},{6,4},{7,5},{8,10},{9,11},{10,... | collective-permute-start | bytes 786440 | tf_op jit(solution)/shard_map/ppermute | solution.py:146
  44.3 10.7 %collective-permute-start.16 = (bf16[1,4,64,256]{3,2,1,0:T(8,128)(2,1)S(1)}, bf16[1,4,64,256]{3,2,1,0:T(8,128)(2,1)S(1)}, u32[]{:S(2)}, u32[]{:S(2)}) collective-permute-start(bf16[1,4,64,256]{3,2,1,0:T(8,128)(2,1)S(1)} %get-tuple-element.92), channel_id=1, source_target_pairs={{0,3},{1,2},{2,1},{3,0},{4,7},{5,6},{6,5},{7,4},{8,11},{9,10},{10,... | collective-permute-start | bytes 393224 | tf_op jit(solution)/shard_map/ppermute | solution.py:146
  59.8 11.8 %collective-permute-start.18 = (bf16[2,4,64,256]{3,2,1,0:T(8,128)(2,1)S(1)}, bf16[2,4,64,256]{3,2,1,0:T(8,128)(2,1)S(1)}, u32[]{:S(2)}, u32[]{:S(2)}) collective-permute-start(bf16[2,4,64,256]{3,2,1,0:T(8,128)(2,1)S(1)} %get-tuple-element.103), channel_id=1, source_target_pairs={{0,2},{1,3},{2,0},{3,1},{4,6},{5,7},{6,4},{7,5},{8,10},{9,11},{10,... | collective-permute-start | bytes 786440 | tf_op jit(solution)/shard_map/ppermute | solution.py:146
  60.7 10.8 %collective-permute-start.17 = (bf16[1,4,64,256]{3,2,1,0:T(8,128)(2,1)S(1)}, bf16[1,4,64,256]{3,2,1,0:T(8,128)(2,1)S(1)}, u32[]{:S(2)}, u32[]{:S(2)}) collective-permute-start(bf16[1,4,64,256]{3,2,1,0:T(8,128)(2,1)S(1)} %get-tuple-element.102), channel_id=1, source_target_pairs={{0,1},{1,0},{2,3},{3,2},{4,5},{5,4},{6,7},{7,6},{8,9},{9,8},{10,11... | collective-permute-start | bytes 393224 | tf_op jit(solution)/shard_map/ppermute | solution.py:146
  60.7 10.8 %collective-permute-start.19 = (bf16[1,4,64,256]{3,2,1,0:T(8,128)(2,1)S(1)}, bf16[1,4,64,256]{3,2,1,0:T(8,128)(2,1)S(1)}, u32[]{:S(2)}, u32[]{:S(2)}) collective-permute-start(bf16[1,4,64,256]{3,2,1,0:T(8,128)(2,1)S(1)} %get-tuple-element.104), channel_id=1, source_target_pairs={{0,3},{1,2},{2,1},{3,0},{4,7},{5,6},{6,5},{7,4},{8,11},{9,10},{10,... | collective-permute-start | bytes 393224 | tf_op jit(solution)/shard_map/ppermute | solution.py:146

commit v17 on v16

--- a/solution.py
+++ b/solution.py
@@ -109,7 +109,7 @@
 VMEM, SMEM, HBM = pltpu.VMEM, pltpu.SMEM, pltpu.HBM
 
 
-def kernel(body, ins, outs, scratch=(), flops=0, nbytes=0):
+def kernel(body, ins, outs, scratch=(), flops=0, nbytes=0, in_place=None):
     return pl.pallas_call(
         body,
         out_shape=[
@@ -119,6 +119,7 @@
         in_specs=[pl.BlockSpec(memory_space=space) for _, space in ins],
         out_specs=[pl.BlockSpec(memory_space=space) for _, _, space in outs],
         scratch_shapes=list(scratch),
+        input_output_aliases=in_place or {},
         compiler_params=pltpu.CompilerParams(vmem_limit_bytes=VMEM_LIMIT),
         cost_estimate=pl.CostEstimate(flops=flops, bytes_accessed=nbytes, transcendentals=0),
     )(*[pltpu.with_memory_space_constraint(x, HBM) if space == HBM else x for x, space in ins])
@@ -370,6 +371,7 @@
     left, refs = take(refs, [n_pair] * len(counts))
     psi, (raw_out, inter_out, left_out, sems) = take(refs, counts)
     copies = keep(left, left_out, sems)
+    inter_out[inter_out.shape[0] - 1] = jnp.zeros_like(inter_out[0])
     products_of(psi, left, widths, 0, raw_out, inter_out)
     for copy in copies:
         copy.wait()
@@ -381,20 +383,12 @@
     left, refs = take(refs, [n_pair] * n_late)
     (right,), refs = take(refs, [n_pair])
     psi, refs = take(refs, counts)
-    raw_in, inter_in, diag, right_diag, part_out, raw_out, left_out, dots_out = refs[:8]
-    sends, (inter, sems) = refs[8:-2], refs[-2:]
+    diag, right_diag, _, _, raw_out, inter, part_out, left_out, dots_out = refs[:9]
+    sends, sems = refs[9:-1], refs[-1]
     copies = keep(left, left_out, sems)
-    for j, (given, own) in enumerate(((inter_in, inter), (raw_in, raw_out))):
-        copies.append(
-            pltpu.make_async_copy(given, own.at[:n_early], sems.at[n_late * n_pair + j])
-        )
-        copies[-1].start()
-    inter[n_blk] = jnp.zeros_like(inter[n_blk])
     products_of(
         psi, left, widths, n_early, raw_out.at[n_early:], inter.at[n_early:n_blk]
     )
-    for copy in copies:
-        copy.wait()
     cols = diag.shape[2]
     zero = jnp.zeros((8, cols), jnp.float32)
     sums = [zero, zero]
@@ -408,20 +402,22 @@
                 image = image + diagonal(diag, right_diag, d, h) * raw
                 sums[0] = sums[0] + fold(raw * raw)
             sums[1] = sums[1] + fold(raw * image)
-        for e, send in enumerate(sends, 2):
-            send_rows(e, send, d, raw_out, part_out)
+        for e, send in enumerate(sends, 1):
+            send_rows(2 * e, send, d, raw_out, part_out, part_out)
 
     sum_terms(src, widths, inter, right, part_out, emit)
     spread([whole(x) for x in sums], dots_out)
-
-
-def send_rows(e, send, d, field, part):
+    for copy in copies:
+        copy.wait()
+
+
+def send_rows(e, send, d, *refs):
     _, own_op = place_of()
     step = send.shape[2]
-    rows = pl.ds(pl.multiple_of((own_op ^ e) * step, step), step)
-    if e % 2 == 0:
-        send[0, d] = field[d, rows].astype(send.dtype)
-    send[send.shape[0] - 1, d] = part[d, rows]
+    for j, ref in enumerate(refs):
+        other = e ^ 1 if j == 2 else e
+        rows = pl.ds(pl.multiple_of((own_op ^ other) * step, step), step)
+        send[j, d] = ref[d, rows].astype(send.dtype)
 
 
 def total_of(mine, other, d, h, cols):
@@ -479,16 +475,16 @@
         for h in range(2):
             part = slice(h * cols, (h + 1) * cols)
             field = fld[d, :, part].astype(jnp.float32)
-            vec = raw_in[d, :, part].astype(jnp.float32) * scale
+            raw = raw_in[d, :, part].astype(jnp.float32)
             image = total[:, part]
             if h == 0:
                 image = image + diagonal(diag, right_diag, d, h) * field
-                for j, prod in enumerate((field * field, vec * field, field * sig[d, :, part])):
+                for j, prod in enumerate((field * field, raw * field, field * sig[d, :, part])):
                     sums[j] = sums[j] + fold(prod)
-            sums[3] = sums[3] + fold(vec * image)
+            sums[3] = sums[3] + fold(raw * image)
             sums[4] = sums[4] + fold(field * image)
         for e, send in enumerate(sends, 1):
-            send_rows(e, send, d, fld, part_out)
+            send_rows(e, send, d, *((part_out,) if e % 2 else (fld, part_out)))
         rows = pl.ds(pl.multiple_of(own_op * step, step), step)
         for j, ref in enumerate((raw_in, sig, fld, part_out)):
             own_out[j, d] = ref[d, rows].astype(own_out.dtype)
@@ -496,7 +492,8 @@
     _, own_op = place_of()
     step = own_out.shape[2]
     sum_terms(src, widths, inter, right, part_out, emit)
-    spread(list(halves[0]) + [whole(x) for x in sums], dots_out)
+    ff, vf, fs, vt, ft = (whole(x) for x in sums)
+    spread(list(halves[0]) + [ff, vf * scale, fs, vt * scale, ft], dots_out)
 
 
 def ritz_pair(theta, h_mix, h_two):
@@ -515,8 +512,9 @@
 
 
 def third_body(n_blk, n_op, count, slots, parts1, parts2, diag, right_diag, own, *refs):
-    got1, got2 = refs[: n_op - 2], refs[n_op - 2 : 2 * n_op - 3]
-    new_out, res_out, energy_out = refs[2 * n_op - 3 :]
+    n_far = n_op - 2
+    got1, got2 = refs[:n_far], refs[n_far : n_far + n_op - 1]
+    new_out, res_out, energy_out = refs[n_far + n_op - 1 :]
     step, cols = new_out.shape[1], new_out.shape[2] // n_op
     own_blk, own_op = place_of()
     scale, theta = norm_theta(parts1[...], count)
@@ -604,6 +602,8 @@
             + [((n_blk, rows, LANES), f32, VMEM), ((1, n_op * cols), f32, VMEM)],
         )
 
+    narrow = ((n_blk, rows, 2 * cols), bf16, VMEM)
+
     def inputs(left, psi, those):
         blocks = [left[d, 2 * e] for d in those for e in range(n_pair)]
         halves = [half for d in those for half in psi[d]]
@@ -615,8 +615,8 @@
             functools.partial(early_body, n_pair, counts),
             [(tables[1], SMEM)] + left_ins + psi_ins,
             [
-                ((n_early, rows, 2 * cols), bf16, VMEM),
-                ((n_early, n_pair * terms, rows, 2 * cols), bf16, VMEM),
+                narrow,
+                ((n_blk + 1, n_pair * terms, rows, 2 * cols), bf16, VMEM),
                 ((n_early, n_pair, terms, rows, rows), bf16, HBM),
             ],
             [pltpu.SemaphoreType.DMA((n_early * n_pair,))],
@@ -627,16 +627,16 @@
     left, psi_by, right, (src, widths, slots, *both), (raw_early, inter_early, left_early) = gather(
         left_ops[:, 0], n_blk, n_op, pack, table, early
     )
-    n_early = raw_early.shape[0]
+    n_early = left_early.shape[0]
     n_late = n_blk - n_early
     left_ins, psi_ins, counts = inputs(left, psi_by, range(n_early, n_blk))
     right_ins = [(block, VMEM) for block in right]
     diags = [(x, VMEM) for x in both]
 
     tables = [(src, SMEM), (widths, SMEM)]
-    narrow = ((n_blk, rows, 2 * cols), bf16, VMEM)
     dots = ((n_dev, 1, LANES), f32, VMEM)
-    sends = [((2 - e % 2, n_blk, step, 2 * cols), bf16, VMEM) for e in range(1, n_op)]
+    sends1 = [((3, n_blk, step, 2 * cols), bf16, VMEM)] * (n_pair - 1)
+    sends2 = [((2 - e % 2, n_blk, step, 2 * cols), bf16, VMEM) for e in range(1, n_op)]
     inter = pltpu.VMEM((n_blk + 1, n_pair * terms, rows, 2 * cols), bf16)
     left_late = (n_late, n_pair, terms, rows, rows)
     cost = dict(flops=2 * n_blk * rows * 2 * cols * terms * n_pair * (rows + 2 * cols), nbytes=6 << 20)
@@ -644,25 +644,28 @@
     def totals(parts):
         return lax.all_to_all(parts, ("blk", "op"), 0, 0, tiled=True)
 
-    part1, raw, kept, dots1, *out1 = kernel(
+    first_ins = tables + left_ins + right_ins + psi_ins + diags
+    raw, _, part1, kept, dots1, *out1 = kernel(
         functools.partial(first_body, n_blk, n_pair, counts),
-        tables + left_ins + right_ins + psi_ins + [(raw_early, VMEM), (inter_early, VMEM)] + diags,
-        [narrow, narrow, (left_late, bf16, HBM), dots] + sends[1:],
-        [inter, pltpu.SemaphoreType.DMA((n_late * n_pair + 2,))],
+        first_ins + [(raw_early, VMEM), (inter_early, VMEM)],
+        [narrow, (inter_early.shape, bf16, VMEM), narrow, (left_late, bf16, HBM), dots] + sends1,
+        [pltpu.SemaphoreType.DMA((n_late * n_pair,))],
+        in_place={len(first_ins): 0, len(first_ins) + 1: 1},
         **cost,
     )
-    parts1, other1, got1 = lax.optimization_barrier(
+    parts1, other1, far = lax.optimization_barrier(
         (
             totals(dots1),
             swap(part1, 1, n_op),
-            [swap(block, e, n_op) for e, block in enumerate(out1, 2)],
+            [swap(block, 2 * e, n_op) for e, block in enumerate(out1, 1)],
         )
     )
+    got1 = [x for block in far for x in (block, swap(block[2:], 1, n_op))]
     dots2, own, *out2 = kernel(
         functools.partial(second_body, n_blk, n_pair, count),
         tables + [(left_early, HBM), (kept, HBM)] + right_ins
         + [(x, VMEM) for x in (parts1, raw, part1, other1)] + diags,
-        [dots, ((4, n_blk, step, 2 * cols), bf16, VMEM)] + sends,
+        [dots, ((4, n_blk, step, 2 * cols), bf16, VMEM)] + sends2,
         [
             inter,
             pltpu.VMEM((n_blk, rows, 2 * cols), f32),

time: 73.8 us -> 74.9 us (1.015)
  waiting for transfers between devices: 19.7 us -> 13.5 us
  local copies, waits for them, and re-layouts: 0.23 us -> 4.29 us
  blocking collectives: 19.3 us -> 21.1 us
  starting transfers between devices: 19.5 us -> 20.6 us
    ppermute x6, waiting for transfers between devices: 13.3 us -> 8.38 us  [onward(): return lax.ppermute(block, 'blk', pairs)]
    unnamed x12, local copies, waits for them, and re-layouts: 0.23 us -> 4.28 us
    all_to_all x2, blocking collectives: 19.3 us -> 21.1 us  [totals(): return lax.all_to_all(parts, ('blk', 'op'), 0, 0, tiled=True)]
    ppermute x14, starting transfers between devices: 8.26 us -> 9.52 us  [swap(): return lax.ppermute(block, 'op', [(i, i ^ e) for i in range(n_op)])]
    ppermute x14, waiting for transfers between devices: 6.38 us -> 5.13 us  [swap(): return lax.ppermute(block, 'op', [(i, i ^ e) for i in range(n_op)])]
  transfers between devices with their start and end apart: 20 -> 20, of which waited for: 7 -> 5; matrix products, arithmetic and copies ran while one was open for 0% -> 0% of each run, Pallas kernels for 7% -> 7%
where the time goes in v17:
time: 74.9 us; the launch traced here: 74.6 us
  blocking collectives  21.1 us (28%)
  starting transfers between devices  20.6 us (28%)
  Pallas kernels  14.3 us (19%)
  waiting for transfers between devices  13.5 us (18%)
  local copies, waits for them, and re-layouts  4.29 us (6%)
    all_to_all x2, blocking collectives, totals(): return lax.all_to_all(parts, ('blk', 'op'), 0, 0, tiled=True)  21.1 us
    pallas_call x6, Pallas kernels, kernel(): pl.pallas_call(body, out_shape=[HBM(shape, dtype) if space == HBM else ja...  14.3 us
    ppermute x6, starting transfers between devices, onward(): return lax.ppermute(block, 'blk', pairs)  11.1 us
    ppermute x14, starting transfers between devices, swap(): return lax.ppermute(block, 'op', [(i, i ^ e) for i in range(n_op)])  9.52 us
    ppermute x6, waiting for transfers between devices, onward(): return lax.ppermute(block, 'blk', pairs)  8.38 us
    ppermute x14, waiting for transfers between devices, swap(): return lax.ppermute(block, 'op', [(i, i ^ e) for i in range(n_op)])  5.13 us
    unnamed x12, local copies, waits for them, and re-layouts  4.28 us
  transfers between devices with their start and end apart: 20, of which 5 were waited for; matrix products, arithmetic and copies ran while one was open for 0% of the time, Pallas kernels for 7%

profile of v17, /device:TPU:0, one launch (start us, length us, event | category | flops | bytes accessed | tf_op | source)
XLA Modules:
  0.0 74.6 jit_solution(10293945661584742309)
XLA Ops:
  0.6 3.1 %collective-permute-start.1 = (bf16[2,256,256]{2,1,0:T(8,128)(2,1)}, bf16[2,256,256]{2,1,0:T(8,128)(2,1)S(1)}, u32[]{:S(2)}, u32[]{:S(2)}) collective-permute-start(bf16[2,256,256]{2,1,0:T(8,128)(2,1)} %bitcast.2), channel_id=1, source_target_pairs={{0,4},{4,12},{12,8},{8,0},{1,5},{5,13},{13,9},{9,1},{2,6},{6,14},{... | collective-permute-start | bytes 786440 | tf_op jit(solution)/shard_map/ppermute | solution.py:143
  3.7 1.5 %collective-permute-start = (bf16[2,256,256]{2,1,0:T(8,128)(2,1)}, bf16[2,256,256]{2,1,0:T(8,128)(2,1)S(1)}, u32[]{:S(2)}, u32[]{:S(2)}) collective-permute-start(bf16[2,256,256]{2,1,0:T(8,128)(2,1)} %bitcast.3), channel_id=1, source_target_pairs={{0,2},{1,3},{2,0},{3,1},{4,6},{5,7},{6,4},{7,5},{8,10},{9,11},{10,... | collective-permute-start | bytes 786440 | tf_op jit(solution)/shard_map/ppermute | solution.py:147
  5.2 0.0 collective-permute-start.2
  5.2 1.3 %collective-permute-done.2._ = s32[2]{0:T(128)S(1)} collective-permute-done((s32[2]{0:T(128)}, s32[2]{0:T(128)S(1)}, u32[]{:S(2)}, u32[]{:S(2)}) %collective-permute-start.2) | collective-permute-done | bytes 40 | tf_op jit(solution)/shard_map/ppermute | solution.py:147
  6.5 0.0 copy-start.3
  6.5 0.7 copy-done.3
  7.1 1.9 %shard_map.103 = (bf16[256,256]{1,0:T(8,128)(2,1)S(1)}, bf16[256,128]{1,0:T(8,128)(2,1)S(1)}, bf16[256,256]{1,0:T(8,128)(2,1)S(1)}, bf16[256,128]{1,0:T(8,128)(2...) custom-call(s32[2]{0:T(128)S(1)} %copy-done.3, s32[2]{0:T(128)S(1)} %collective-permute-done.2._, ...), custom_call_target="tpu_custom_call" | custom-call | bytes 1048576 | tf_op jit(solution)/shard_map/pallas_call | solution.py:113
  9.0 0.6 collective-permute-start.3
  9.6 3.8 %collective-permute-done.3.refs_1_.refs_5_ = bf16[144,256]{1,0:T(8,128)(2,1)S(1)} collective-permute-done((bf16[144,256]{1,0:T(8,128)(2,1)S(1)}, bf16[144,256]{1,0:T(8,128)(2,1)S(1)}, u32[]{:S(2)}, u32[]{:S(2)}) %collective-permute-start.3) | collective-permute-done | bytes 73760 | tf_op jit(solution)/shard_map/ppermute | solution.py:147
  13.5 0.0 collective-permute-done.1.refs_2_
  13.5 0.0 collective-permute-done.refs_1_
  13.5 2.6 %collective-permute-start.5 = (bf16[2,256,256]{2,1,0:T(8,128)(2,1)S(1)}, bf16[2,256,256]{2,1,0:T(8,128)(2,1)S(1)}, u32[]{:S(2)}, u32[]{:S(2)}) collective-permute-start(bf16[2,256,256]{2,1,0:T(8,128)(2,1)S(1)} %collective-permute-done.1.refs_2_), channel_id=1, source_target_pairs={{0,4},{4,12},{12,8},{8,0},{1,5},{5,13},{13,9},{9,1},{2,6},{6,14},{... | collective-permute-start | bytes 786440 | tf_op jit(solution)/shard_map/ppermute | solution.py:143
  16.1 1.3 %collective-permute-start.4 = (bf16[2,256,256]{2,1,0:T(8,128)(2,1)S(1)}, bf16[2,256,256]{2,1,0:T(8,128)(2,1)S(1)}, u32[]{:S(2)}, u32[]{:S(2)}) collective-permute-start(bf16[2,256,256]{2,1,0:T(8,128)(2,1)S(1)} %collective-permute-done.1.refs_2_), channel_id=1, source_target_pairs={{0,2},{1,3},{2,0},{3,1},{4,6},{5,7},{6,4},{7,5},{8,10},{9,11},{10,... | collective-permute-start | bytes 786440 | tf_op jit(solution)/shard_map/ppermute | solution.py:147
  17.4 0.4 collective-permute-start.6
  17.8 0.0 copy-start.1
  17.8 0.7 copy-done.1
  18.5 0.0 copy-start.2
  18.5 0.7 copy-done.2
  19.2 0.0 copy-start.4
  19.2 0.7 copy-done.4
  19.8 0.0 copy-start.5
  19.8 0.7 copy-done.5
  20.5 1.3 %shard_map.104 = (s32[16]{0:T(128)S(1)}, s32[4]{0:T(128)S(1)}, s32[4]{0:T(128)S(1)}, f32[4,256,128]{2,1,0:T(8,128)S(1)}, f32[1,512]{1,0:T(1,128)S(1)}) custom-call(s32[4]{0:T(128)S(1)} %copy-done.4, s32[4]{0:T(128)S(1)} %copy-done.5, f32[4,256]{1,0:T(4,128)S(1)} %copy-done.1, f32[1,512]{1,0:T(1,128)S(1)} %bitcast.5, ...), custom_call_target="tpu_custom_call" | custom-call | tf_op jit(solution)/shard_map/pallas_call | solution.py:113
  21.8 1.5 %collective-permute-done.6.refs_5_ = bf16[256,128]{1,0:T(8,128)(2,1)S(1)} collective-permute-done((bf16[256,128]{1,0:T(8,128)(2,1)S(1)}, bf16[256,128]{1,0:T(8,128)(2,1)S(1)}, u32[]{:S(2)}, u32[]{:S(2)}) %collective-permute-start.6) | collective-permute-done | bytes 65568 | tf_op jit(solution)/shard_map/ppermute | solution.py:143
  23.4 0.0 collective-permute-done.5.refs_0_
  23.4 0.0 collective-permute-done.4.refs_3_
  23.4 1.7 %collective-permute-start.8 = (bf16[2,256,256]{2,1,0:T(8,128)(2,1)S(1)}, bf16[2,256,256]{2,1,0:T(8,128)(2,1)S(1)}, u32[]{:S(2)}, u32[]{:S(2)}) collective-permute-start(bf16[2,256,256]{2,1,0:T(8,128)(2,1)S(1)} %collective-permute-done.5.refs_0_), channel_id=1, source_target_pairs={{0,4},{4,12},{12,8},{8,0},{1,5},{5,13},{13,9},{9,1},{2,6},{6,14},{... | collective-permute-start | bytes 786440 | tf_op jit(solution)/shard_map/ppermute | solution.py:143
  25.1 1.3 %collective-permute-start.7 = (bf16[2,256,256]{2,1,0:T(8,128)(2,1)S(1)}, bf16[2,256,256]{2,1,0:T(8,128)(2,1)S(1)}, u32[]{:S(2)}, u32[]{:S(2)}) collective-permute-start(bf16[2,256,256]{2,1,0:T(8,128)(2,1)S(1)} %collective-permute-done.5.refs_0_), channel_id=1, source_target_pairs={{0,2},{1,3},{2,0},{3,1},{4,6},{5,7},{6,4},{7,5},{8,10},{9,11},{10,... | collective-permute-start | bytes 786440 | tf_op jit(solution)/shard_map/ppermute | solution.py:147
  26.4 1.2 %collective-permute-start.10 = (bf16[256,128]{1,0:T(8,128)(2,1)S(1)}, bf16[256,128]{1,0:T(8,128)(2,1)S(1)}, u32[]{:S(2)}, u32[]{:S(2)}) collective-permute-start(bf16[256,128]{1,0:T(8,128)(2,1)S(1)} %get-tuple-element.68), channel_id=1, source_target_pairs={{0,8},{4,0},{12,4},{8,12},{1,9},{5,1},{13,5},{9,13},{2,10},{6,2},{... | collective-permute-start | bytes 196616 | tf_op jit(solution)/shard_map/ppermute | solution.py:143
  27.6 0.0 collective-permute-start.9
  27.6 4.7 %collective-permute-done.10.refs_7_ = bf16[256,128]{1,0:T(8,128)(2,1)S(1)} collective-permute-done((bf16[256,128]{1,0:T(8,128)(2,1)S(1)}, bf16[256,128]{1,0:T(8,128)(2,1)S(1)}, u32[]{:S(2)}, u32[]{:S(2)}) %collective-permute-start.10) | collective-permute-done | bytes 65568 | tf_op jit(solution)/shard_map/ppermute | solution.py:143
  32.4 0.0 collective-permute-done.9.refs_6_
  32.4 0.0 collective-permute-done.8.refs_2_
  32.4 0.0 collective-permute-done.7.refs_1_
  32.4 1.4 %collective-permute-start.11 = (bf16[2,256,256]{2,1,0:T(8,128)(2,1)S(1)}, bf16[2,256,256]{2,1,0:T(8,128)(2,1)S(1)}, u32[]{:S(2)}, u32[]{:S(2)}) collective-permute-start(bf16[2,256,256]{2,1,0:T(8,128)(2,1)S(1)} %collective-permute-done.8.refs_2_), channel_id=1, source_target_pairs={{0,2},{1,3},{2,0},{3,1},{4,6},{5,7},{6,4},{7,5},{8,10},{9,11},{10,... | collective-permute-start | bytes 786440 | tf_op jit(solution)/shard_map/ppermute | solution.py:147
  33.8 2.0 %collective-permute-start.13 = (bf16[256,256]{1,0:T(8,128)(2,1)S(1)}, bf16[256,256]{1,0:T(8,128)(2,1)S(1)}, u32[]{:S(2)}, u32[]{:S(2)}) collective-permute-start(bf16[256,256]{1,0:T(8,128)(2,1)S(1)} %get-tuple-element.79), channel_id=1, source_target_pairs={{0,12},{4,8},{12,0},{8,4},{1,13},{5,9},{13,1},{9,5},{2,14},{6,10},... | collective-permute-start | bytes 393224 | tf_op jit(solution)/shard_map/ppermute | solution.py:143
  35.8 0.0 collective-permute-start.12
  35.8 0.0 copy-start
  35.8 0.9 %copy-done = bf16[2,1,256,256]{3,2,1,0:T(8,128)(2,1)S(1)} copy-done((bf16[2,1,256,256]{3,2,1,0:T(8,128)(2,1)S(1)}, bf16[2,1,256,256]{3,2,1,0:T(8,128)(2,1)}, u32[]{:S(2)}) %copy-start) | copy-done | bytes 262168
  36.8 1.7 %shard_map.105 = (bf16[4,256,256]{2,1,0:T(8,128)(2,1)S(1)}, bf16[5,4,256,256]{3,2,1,0:T(8,128)(2,1)S(1)}, bf16[2,2,2,256,256]{4,3,2,1,0:T(8,128)(2,1)}) custom-call(s32[4]{0:T(128)S(1)} %get-tuple-element.65.widths, bf16[2,256,256]{2,1,0:T(8,128)(2,1)S(1)} %bitcast.4, bf16[2,256,256]{2,1,0:T(8,128)(2,1)S(1)} %collective-permute-done.refs_1_, ...), custom_call_target="tpu_custom_call" | custom-call | flops 268435456 | bytes 4194304 | tf_op jit(solution)/shard_map/pallas_call | solution.py:113
  38.5 2.1 %collective-permute-done.13.refs_6_ = bf16[256,256]{1,0:T(8,128)(2,1)S(1)} collective-permute-done((bf16[256,256]{1,0:T(8,128)(2,1)S(1)}, bf16[256,256]{1,0:T(8,128)(2,1)S(1)}, u32[]{:S(2)}, u32[]{:S(2)}) %collective-permute-start.13) | collective-permute-done | bytes 131104 | tf_op jit(solution)/shard_map/ppermute | solution.py:143
  40.6 0.0 collective-permute-done.12.refs_8_
  40.6 0.0 collective-permute-done.11.refs_3_
  40.6 2.5 %shard_map.106 = (bf16[4,256,256]{2,1,0:T(8,128)(2,1)S(1)}, bf16[5,4,256,256]{3,2,1,0:T(8,128)(2,1)S(1)}, bf16[4,256,256]{2,1,0:T(8,128)(2,1)S(1)}, bf16[2,2,2,2...) custom-call(s32[16]{0:T(128)S(1)} %get-tuple-element.64.src, ...), custom_call_target="tpu_custom_call", output_to_operand_aliasing={{0}: (13, {}), {1}: (14, {})} | custom-call | flops 1073741824 | bytes 6291456 | tf_op jit(solution)/shard_map/pallas_call | solution.py:113
  43.1 0.1 collective-permute-start.14
  43.2 1.0 %collective-permute-start.15 = (bf16[3,4,64,256]{3,2,1,0:T(8,128)(2,1)S(1)}, bf16[3,4,64,256]{3,2,1,0:T(8,128)(2,1)S(1)}, u32[]{:S(2)}, u32[]{:S(2)}) collective-permute-start(bf16[3,4,64,256]{3,2,1,0:T(8,128)(2,1)S(1)} %get-tuple-element.89), channel_id=1, source_target_pairs={{0,2},{1,3},{2,0},{3,1},{4,6},{5,7},{6,4},{7,5},{8,10},{9,11},{10,... | collective-permute-start | bytes 1179656 | tf_op jit(solution)/shard_map/ppermute | solution.py:147
  44.2 10.7 %all_to_all.10.refs_2_.parts1 = f32[16,1,128]{2,1,0:T(1,128)S(1)} all-to-all(f32[16,1,128]{2,1,0:T(1,128)S(1)} %get-tuple-element.87), channel_id=1, replica_groups=mesh['grp'=2,'blk'=4,'op'=4] {'blk','op'}, dimensions={0} | all-to-all | bytes 16384 | tf_op jit(solution)/shard_map/all_to_all | solution.py:645
  54.9 0.0 collective-permute-done.15.refs_0_
  54.9 0.0 collective-permute-done.14.refs_5_
  54.9 4.8 %shard_map.107 = (f32[16,1,128]{2,1,0:T(1,128)S(1)}, bf16[4,4,64,256]{3,2,1,0:T(8,128)(2,1)S(1)}, bf16[1,4,64,256]{3,2,1,0:T(8,128)(2,1)S(1)}, bf16[2,4,64,256]{...) custom-call(s32[16]{0:T(128)S(1)} %get-tuple-element.64.src, s32[4]{0:T(128)S(1)} %get-tuple-element.65.widths, ...), custom_call_target="tpu_custom_call" | custom-call | flops 1073741824 | bytes 6291456 | tf_op jit(solution)/shard_map/pallas_call | solution.py:113
  59.7 1.0 %collective-permute-start.18 = (bf16[2,4,64,256]{3,2,1,0:T(8,128)(2,1)S(1)}, bf16[2,4,64,256]{3,2,1,0:T(8,128)(2,1)S(1)}, u32[]{:S(2)}, u32[]{:S(2)}) collective-permute-start(bf16[2,4,64,256]{3,2,1,0:T(8,128)(2,1)S(1)} %get-tuple-element.99), channel_id=1, source_target_pairs={{0,2},{1,3},{2,0},{3,1},{4,6},{5,7},{6,4},{7,5},{8,10},{9,11},{10,... | collective-permute-start | bytes 786440 | tf_op jit(solution)/shard_map/ppermute | solution.py:147
  60.7 0.1 collective-permute-start.16
  60.8 0.5 collective-permute-start.17
  61.3 0.8 %collective-permute-start.19 = (bf16[1,4,64,256]{3,2,1,0:T(8,128)(2,1)S(1)}, bf16[1,4,64,256]{3,2,1,0:T(8,128)(2,1)S(1)}, u32[]{:S(2)}, u32[]{:S(2)}) collective-permute-start(bf16[1,4,64,256]{3,2,1,0:T(8,128)(2,1)S(1)} %get-tuple-element.100), channel_id=1, source_target_pairs={{0,3},{1,2},{2,1},{3,0},{4,7},{5,6},{6,5},{7,4},{8,11},{9,10},{10,... | collective-permute-start | bytes 393224 | tf_op jit(solution)/shard_map/ppermute | solution.py:147
  62.1 10.4 %all_to_all.11.parts2 = f32[16,1,128]{2,1,0:T(1,128)S(1)} all-to-all(f32[16,1,128]{2,1,0:T(1,128)S(1)} %get-tuple-element.95), channel_id=1, replica_groups=mesh['grp'=2,'blk'=4,'op'=4] {'blk','op'}, dimensions={0} | all-to-all | bytes 16384 | tf_op jit(solution)/shard_map/all_to_all | solution.py:645
  72.5 0.0 collective-permute-done.16.refs_1_
  72.5 0.0 collective-permute-done.17.refs_2_
  72.5 0.0 collective-permute-done.19.refs_4_
  72.5 0.0 collective-permute-done.18.refs_3_
  72.6 2.0 %shard_map.108 = (bf16[4,64,512]{2,1,0:T(8,128)(2,1)}, bf16[4,64,512]{2,1,0:T(8,128)(2,1)}, f32[1]{0:T(128)}) custom-call(s32[4]{0:T(128)S(1)} %get-tuple-element.63.slots, f32[16,1,128]{2,1,0:T(1,128)S(1)} %all_to_all.10.refs_2_.parts1, f32[16,1,128]{2,1,0:T(1,128)S(1)} %all_to_all.11.parts2, f32[4,256,128]{2,1,0:T(8,128)S(1)} %get-tuple-element.83.refs_9_.refs_6_.diag, ...), custom_call_target="tpu_custom_call" | custom-call | bytes 4194304 | tf_op jit(solution)/shard_map/pallas_call | solution.py:113
  (1 shorter events, 0.0 us)
Async XLA Ops:
  0.6 12.8 %collective-permute-start.1 = (bf16[2,256,256]{2,1,0:T(8,128)(2,1)}, bf16[2,256,256]{2,1,0:T(8,128)(2,1)S(1)}, u32[]{:S(2)}, u32[]{:S(2)}) collective-permute-start(bf16[2,256,256]{2,1,0:T(8,128)(2,1)} %bitcast.2), channel_id=1, source_target_pairs={{0,4},{4,12},{12,8},{8,0},{1,5},{5,13},{13,9},{9,1},{2,6},{6,14},{... | collective-permute-start | bytes 786440 | tf_op jit(solution)/shard_map/ppermute | solution.py:143
  3.7 9.8 %collective-permute-start = (bf16[2,256,256]{2,1,0:T(8,128)(2,1)}, bf16[2,256,256]{2,1,0:T(8,128)(2,1)S(1)}, u32[]{:S(2)}, u32[]{:S(2)}) collective-permute-start(bf16[2,256,256]{2,1,0:T(8,128)(2,1)} %bitcast.3), channel_id=1, source_target_pairs={{0,2},{1,3},{2,0},{3,1},{4,6},{5,7},{6,4},{7,5},{8,10},{9,11},{10,... | collective-permute-start | bytes 786440 | tf_op jit(solution)/shard_map/ppermute | solution.py:147
  5.2 1.3 %collective-permute-start.2 = (s32[2]{0:T(128)}, s32[2]{0:T(128)S(1)}, u32[]{:S(2)}, u32[]{:S(2)}) collective-permute-start(s32[2]{0:T(128)} %shift.1), channel_id=1, source_target_pairs={{0,1},{1,0},{2,3},{3,2},{4,5},{5,4},{6,7},{7,6},{8,9},{9,8},{10,11... | collective-permute-start | bytes 32 | tf_op jit(solution)/shard_map/ppermute | solution.py:147
  6.5 0.7 copy-start.3
  9.0 4.4 %collective-permute-start.3 = (bf16[144,256]{1,0:T(8,128)(2,1)S(1)}, bf16[144,256]{1,0:T(8,128)(2,1)S(1)}, u32[]{:S(2)}, u32[]{:S(2)}) collective-permute-start(bf16[144,256]{1,0:T(8,128)(2,1)S(1)} %get-tuple-element.53), channel_id=1, source_target_pairs={{0,2},{1,3},{2,0},{3,1},{4,6},{5,7},{6,4},{7,5},{8,10},{9,11},{10,... | collective-permute-start | bytes 221192 | tf_op jit(solution)/shard_map/ppermute | solution.py:147
  13.5 9.9 %collective-permute-start.5 = (bf16[2,256,256]{2,1,0:T(8,128)(2,1)S(1)}, bf16[2,256,256]{2,1,0:T(8,128)(2,1)S(1)}, u32[]{:S(2)}, u32[]{:S(2)}) collective-permute-start(bf16[2,256,256]{2,1,0:T(8,128)(2,1)S(1)} %collective-permute-done.1.refs_2_), channel_id=1, source_target_pairs={{0,4},{4,12},{12,8},{8,0},{1,5},{5,13},{13,9},{9,1},{2,6},{6,14},{... | collective-permute-start | bytes 786440 | tf_op jit(solution)/shard_map/ppermute | solution.py:143
  16.1 7.3 %collective-permute-start.4 = (bf16[2,256,256]{2,1,0:T(8,128)(2,1)S(1)}, bf16[2,256,256]{2,1,0:T(8,128)(2,1)S(1)}, u32[]{:S(2)}, u32[]{:S(2)}) collective-permute-start(bf16[2,256,256]{2,1,0:T(8,128)(2,1)S(1)} %collective-permute-done.1.refs_2_), channel_id=1, source_target_pairs={{0,2},{1,3},{2,0},{3,1},{4,6},{5,7},{6,4},{7,5},{8,10},{9,11},{10,... | collective-permute-start | bytes 786440 | tf_op jit(solution)/shard_map/ppermute | solution.py:147
  17.4 6.0 %collective-permute-start.6 = (bf16[256,128]{1,0:T(8,128)(2,1)S(1)}, bf16[256,128]{1,0:T(8,128)(2,1)S(1)}, u32[]{:S(2)}, u32[]{:S(2)}) collective-permute-start(bf16[256,128]{1,0:T(8,128)(2,1)S(1)} %get-tuple-element.55), channel_id=1, source_target_pairs={{0,4},{4,12},{12,8},{8,0},{1,5},{5,13},{13,9},{9,1},{2,6},{6,14},{... | collective-permute-start | bytes 196616 | tf_op jit(solution)/shard_map/ppermute | solution.py:143
  17.8 0.7 copy-start.1
  18.5 0.7 copy-start.2
  19.2 0.7 copy-start.4
  19.8 0.7 copy-start.5
  23.4 9.0 %collective-permute-start.8 = (bf16[2,256,256]{2,1,0:T(8,128)(2,1)S(1)}, bf16[2,256,256]{2,1,0:T(8,128)(2,1)S(1)}, u32[]{:S(2)}, u32[]{:S(2)}) collective-permute-start(bf16[2,256,256]{2,1,0:T(8,128)(2,1)S(1)} %collective-permute-done.5.refs_0_), channel_id=1, source_target_pairs={{0,4},{4,12},{12,8},{8,0},{1,5},{5,13},{13,9},{9,1},{2,6},{6,14},{... | collective-permute-start | bytes 786440 | tf_op jit(solution)/shard_map/ppermute | solution.py:143
  25.1 7.3 %collective-permute-start.7 = (bf16[2,256,256]{2,1,0:T(8,128)(2,1)S(1)}, bf16[2,256,256]{2,1,0:T(8,128)(2,1)S(1)}, u32[]{:S(2)}, u32[]{:S(2)}) collective-permute-start(bf16[2,256,256]{2,1,0:T(8,128)(2,1)S(1)} %collective-permute-done.5.refs_0_), channel_id=1, source_target_pairs={{0,2},{1,3},{2,0},{3,1},{4,6},{5,7},{6,4},{7,5},{8,10},{9,11},{10,... | collective-permute-start | bytes 786440 | tf_op jit(solution)/shard_map/ppermute | solution.py:147
  26.4 6.0 %collective-permute-start.10 = (bf16[256,128]{1,0:T(8,128)(2,1)S(1)}, bf16[256,128]{1,0:T(8,128)(2,1)S(1)}, u32[]{:S(2)}, u32[]{:S(2)}) collective-permute-start(bf16[256,128]{1,0:T(8,128)(2,1)S(1)} %get-tuple-element.68), channel_id=1, source_target_pairs={{0,8},{4,0},{12,4},{8,12},{1,9},{5,1},{13,5},{9,13},{2,10},{6,2},{... | collective-permute-start | bytes 196616 | tf_op jit(solution)/shard_map/ppermute | solution.py:143
  27.6 4.7 %collective-permute-start.9 = (bf16[256,128]{1,0:T(8,128)(2,1)S(1)}, bf16[256,128]{1,0:T(8,128)(2,1)S(1)}, u32[]{:S(2)}, u32[]{:S(2)}) collective-permute-start(bf16[256,128]{1,0:T(8,128)(2,1)S(1)} %collective-permute-done.6.refs_5_), channel_id=1, source_target_pairs={{0,1},{1,0},{2,3},{3,2},{4,5},{5,4},{6,7},{7,6},{8,9},{9,8},{10,11... | collective-permute-start | bytes 196616 | tf_op jit(solution)/shard_map/ppermute | solution.py:147
  32.4 8.3 %collective-permute-start.11 = (bf16[2,256,256]{2,1,0:T(8,128)(2,1)S(1)}, bf16[2,256,256]{2,1,0:T(8,128)(2,1)S(1)}, u32[]{:S(2)}, u32[]{:S(2)}) collective-permute-start(bf16[2,256,256]{2,1,0:T(8,128)(2,1)S(1)} %collective-permute-done.8.refs_2_), channel_id=1, source_target_pairs={{0,2},{1,3},{2,0},{3,1},{4,6},{5,7},{6,4},{7,5},{8,10},{9,11},{10,... | collective-permute-start | bytes 786440 | tf_op jit(solution)/shard_map/ppermute | solution.py:147
  33.8 6.8 %collective-permute-start.13 = (bf16[256,256]{1,0:T(8,128)(2,1)S(1)}, bf16[256,256]{1,0:T(8,128)(2,1)S(1)}, u32[]{:S(2)}, u32[]{:S(2)}) collective-permute-start(bf16[256,256]{1,0:T(8,128)(2,1)S(1)} %get-tuple-element.79), channel_id=1, source_target_pairs={{0,12},{4,8},{12,0},{8,4},{1,13},{5,9},{13,1},{9,5},{2,14},{6,10},... | collective-permute-start | bytes 393224 | tf_op jit(solution)/shard_map/ppermute | solution.py:143
  35.8 4.8 %collective-permute-start.12 = (bf16[256,128]{1,0:T(8,128)(2,1)S(1)}, bf16[256,128]{1,0:T(8,128)(2,1)S(1)}, u32[]{:S(2)}, u32[]{:S(2)}) collective-permute-start(bf16[256,128]{1,0:T(8,128)(2,1)S(1)} %collective-permute-done.10.refs_7_), channel_id=1, source_target_pairs={{0,1},{1,0},{2,3},{3,2},{4,5},{5,4},{6,7},{7,6},{8,9},{9,8},{10,11... | collective-permute-start | bytes 196616 | tf_op jit(solution)/shard_map/ppermute | solution.py:147
  35.8 1.0 %copy-start = (bf16[2,1,256,256]{3,2,1,0:T(8,128)(2,1)S(1)}, bf16[2,1,256,256]{3,2,1,0:T(8,128)(2,1)}, u32[]{:S(2)}) copy-start(bf16[2,1,256,256]{3,2,1,0:T(8,128)(2,1)} %param.9) | copy-start | bytes 786436
  43.1 11.7 %collective-permute-start.14 = (bf16[4,256,256]{2,1,0:T(8,128)(2,1)S(1)}, bf16[4,256,256]{2,1,0:T(8,128)(2,1)S(1)}, u32[]{:S(2)}, u32[]{:S(2)}) collective-permute-start(bf16[4,256,256]{2,1,0:T(8,128)(2,1)S(1)} %get-tuple-element.88.refs_4_), channel_id=1, source_target_pairs={{0,1},{1,0},{2,3},{3,2},{4,5},{5,4},{6,7},{7,6},{8,9},{9,8},{10,11... | collective-permute-start | bytes 1572872 | tf_op jit(solution)/shard_map/ppermute | solution.py:147
  43.2 11.7 %collective-permute-start.15 = (bf16[3,4,64,256]{3,2,1,0:T(8,128)(2,1)S(1)}, bf16[3,4,64,256]{3,2,1,0:T(8,128)(2,1)S(1)}, u32[]{:S(2)}, u32[]{:S(2)}) collective-permute-start(bf16[3,4,64,256]{3,2,1,0:T(8,128)(2,1)S(1)} %get-tuple-element.89), channel_id=1, source_target_pairs={{0,2},{1,3},{2,0},{3,1},{4,6},{5,7},{6,4},{7,5},{8,10},{9,11},{10,... | collective-permute-start | bytes 1179656 | tf_op jit(solution)/shard_map/ppermute | solution.py:147
  59.7 12.8 %collective-permute-start.18 = (bf16[2,4,64,256]{3,2,1,0:T(8,128)(2,1)S(1)}, bf16[2,4,64,256]{3,2,1,0:T(8,128)(2,1)S(1)}, u32[]{:S(2)}, u32[]{:S(2)}) collective-permute-start(bf16[2,4,64,256]{3,2,1,0:T(8,128)(2,1)S(1)} %get-tuple-element.99), channel_id=1, source_target_pairs={{0,2},{1,3},{2,0},{3,1},{4,6},{5,7},{6,4},{7,5},{8,10},{9,11},{10,... | collective-permute-start | bytes 786440 | tf_op jit(solution)/shard_map/ppermute | solution.py:147
  60.7 11.8 %collective-permute-start.16 = (bf16[1,4,64,256]{3,2,1,0:T(8,128)(2,1)S(1)}, bf16[1,4,64,256]{3,2,1,0:T(8,128)(2,1)S(1)}, u32[]{:S(2)}, u32[]{:S(2)}) collective-permute-start(bf16[1,4,64,256]{3,2,1,0:T(8,128)(2,1)S(1)} %slice.3), channel_id=1, source_target_pairs={{0,1},{1,0},{2,3},{3,2},{4,5},{5,4},{6,7},{7,6},{8,9},{9,8},{10,11... | collective-permute-start | bytes 393224 | tf_op jit(solution)/shard_map/ppermute | solution.py:147
  60.8 11.7 %collective-permute-start.17 = (bf16[1,4,64,256]{3,2,1,0:T(8,128)(2,1)S(1)}, bf16[1,4,64,256]{3,2,1,0:T(8,128)(2,1)S(1)}, u32[]{:S(2)}, u32[]{:S(2)}) collective-permute-start(bf16[1,4,64,256]{3,2,1,0:T(8,128)(2,1)S(1)} %get-tuple-element.98), channel_id=1, source_target_pairs={{0,1},{1,0},{2,3},{3,2},{4,5},{5,4},{6,7},{7,6},{8,9},{9,8},{10,11... | collective-permute-start | bytes 393224 | tf_op jit(solution)/shard_map/ppermute | solution.py:147
  61.3 11.2 %collective-permute-start.19 = (bf16[1,4,64,256]{3,2,1,0:T(8,128)(2,1)S(1)}, bf16[1,4,64,256]{3,2,1,0:T(8,128)(2,1)S(1)}, u32[]{:S(2)}, u32[]{:S(2)}) collective-permute-start(bf16[1,4,64,256]{3,2,1,0:T(8,128)(2,1)S(1)} %get-tuple-element.100), channel_id=1, source_target_pairs={{0,3},{1,2},{2,1},{3,0},{4,7},{5,6},{6,5},{7,4},{8,11},{9,10},{10,... | collective-permute-start | bytes 393224 | tf_op jit(solution)/shard_map/ppermute | solution.py:147

commit v18 on v16

--- a/solution.py
+++ b/solution.py
@@ -651,13 +651,8 @@
         [inter, pltpu.SemaphoreType.DMA((n_late * n_pair + 2,))],
         **cost,
     )
-    parts1, other1, got1 = lax.optimization_barrier(
-        (
-            totals(dots1),
-            swap(part1, 1, n_op),
-            [swap(block, e, n_op) for e, block in enumerate(out1, 2)],
-        )
-    )
+    parts1, other1 = lax.optimization_barrier((totals(dots1), swap(part1, 1, n_op)))
+    got1 = [swap(block, e, n_op) for e, block in enumerate(out1, 2)]
     dots2, own, *out2 = kernel(
         functools.partial(second_body, n_blk, n_pair, count),
         tables + [(left_early, HBM), (kept, HBM)] + right_ins
@@ -674,6 +669,7 @@
         ],
         **cost,
     )
+    dots2, out2, got1 = lax.optimization_barrier((dots2, out2, got1))
     parts2 = totals(dots2)
     got2 = [swap(block, e, n_op) for e, block in enumerate(out2, 1)]
     final = ((n_blk, step, n_op * cols), bf16, VMEM)

time: 73.8 us -> 73.8 us (level)
  transfers between devices with their start and end apart: 20 -> 20, of which waited for: 7 -> 7; matrix products, arithmetic and copies ran while one was open for 0% -> 0% of each run, Pallas kernels for 7% -> 13%
where the time goes in v18:
time: 73.8 us; the launch traced here: 73.6 us
  waiting for transfers between devices  19.7 us (27%)
  starting transfers between devices  19.5 us (26%)
  blocking collectives  19.3 us (26%)
  Pallas kernels  14.2 us (19%)
  between operations  0.74 us (1%)
    all_to_all x2, blocking collectives, totals(): return lax.all_to_all(parts, ('blk', 'op'), 0, 0, tiled=True)  19.3 us
    pallas_call x6, Pallas kernels, kernel(): pl.pallas_call(body, out_shape=[HBM(shape, dtype) if space == HBM else ja...  14.2 us
    ppermute x6, waiting for transfers between devices, onward(): return lax.ppermute(block, 'blk', pairs)  13.3 us
    ppermute x6, starting transfers between devices, onward(): return lax.ppermute(block, 'blk', pairs)  11.2 us
    ppermute x14, starting transfers between devices, swap(): return lax.ppermute(block, 'op', [(i, i ^ e) for i in range(n_op)])  8.26 us
    ppermute x14, waiting for transfers between devices, swap(): return lax.ppermute(block, 'op', [(i, i ^ e) for i in range(n_op)])  6.38 us
  transfers between devices with their start and end apart: 20, of which 7 were waited for; matrix products, arithmetic and copies ran while one was open for 0% of the time, Pallas kernels for 13%

profile of v18, /device:TPU:0, one launch (start us, length us, event | category | flops | bytes accessed | tf_op | source)
XLA Modules:
  0.0 73.6 jit_solution(12704212998043425976)
XLA Ops:
  0.6 0.0 copy-start.3
  0.6 3.1 %collective-permute-start.1 = (bf16[2,256,256]{2,1,0:T(8,128)(2,1)}, bf16[2,256,256]{2,1,0:T(8,128)(2,1)S(1)}, u32[]{:S(2)}, u32[]{:S(2)}) collective-permute-start(bf16[2,256,256]{2,1,0:T(8,128)(2,1)} %bitcast.2), channel_id=1, source_target_pairs={{0,4},{4,12},{12,8},{8,0},{1,5},{5,13},{13,9},{9,1},{2,6},{6,14},{... | collective-permute-start | bytes 786440 | tf_op jit(solution)/shard_map/ppermute | solution.py:142
  3.7 1.5 %collective-permute-start = (bf16[2,256,256]{2,1,0:T(8,128)(2,1)}, bf16[2,256,256]{2,1,0:T(8,128)(2,1)S(1)}, u32[]{:S(2)}, u32[]{:S(2)}) collective-permute-start(bf16[2,256,256]{2,1,0:T(8,128)(2,1)} %bitcast.3), channel_id=1, source_target_pairs={{0,2},{1,3},{2,0},{3,1},{4,6},{5,7},{6,4},{7,5},{8,10},{9,11},{10,... | collective-permute-start | bytes 786440 | tf_op jit(solution)/shard_map/ppermute | solution.py:146
  5.2 0.0 copy-done.3
  5.2 0.0 collective-permute-start.2
  5.2 1.1 %collective-permute-done.2._ = s32[2]{0:T(128)S(1)} collective-permute-done((s32[2]{0:T(128)S(1)}, s32[2]{0:T(128)S(1)}, u32[]{:S(2)}, u32[]{:S(2)}) %collective-permute-start.2) | collective-permute-done | bytes 40 | tf_op jit(solution)/shard_map/ppermute | solution.py:146
  6.3 0.0 copy-start
  6.3 1.9 %shard_map.103 = (bf16[256,256]{1,0:T(8,128)(2,1)S(1)}, bf16[256,128]{1,0:T(8,128)(2,1)S(1)}, bf16[256,256]{1,0:T(8,128)(2,1)S(1)}, bf16[256,128]{1,0:T(8,128)(2...) custom-call(s32[2]{0:T(128)S(1)} %copy-done.3, s32[2]{0:T(128)S(1)} %collective-permute-done.2._, ...), custom_call_target="tpu_custom_call" | custom-call | bytes 1048576 | tf_op jit(solution)/shard_map/pallas_call | solution.py:113
  8.2 0.0 copy-start.1
  8.3 0.6 collective-permute-start.3
  8.9 4.4 %collective-permute-done.3.refs_1_.refs_5_ = bf16[144,256]{1,0:T(8,128)(2,1)S(1)} collective-permute-done((bf16[144,256]{1,0:T(8,128)(2,1)S(1)}, bf16[144,256]{1,0:T(8,128)(2,1)S(1)}, u32[]{:S(2)}, u32[]{:S(2)}) %collective-permute-start.3) | collective-permute-done | bytes 73760 | tf_op jit(solution)/shard_map/ppermute | solution.py:146
  13.3 0.0 collective-permute-done.1.refs_2_
  13.3 0.0 collective-permute-done.refs_1_
  13.3 0.0 copy-start.2
  13.3 2.6 %collective-permute-start.5 = (bf16[2,256,256]{2,1,0:T(8,128)(2,1)S(1)}, bf16[2,256,256]{2,1,0:T(8,128)(2,1)S(1)}, u32[]{:S(2)}, u32[]{:S(2)}) collective-permute-start(bf16[2,256,256]{2,1,0:T(8,128)(2,1)S(1)} %collective-permute-done.1.refs_2_), channel_id=1, source_target_pairs={{0,4},{4,12},{12,8},{8,0},{1,5},{5,13},{13,9},{9,1},{2,6},{6,14},{... | collective-permute-start | bytes 786440 | tf_op jit(solution)/shard_map/ppermute | solution.py:142
  15.9 1.5 %collective-permute-start.4 = (bf16[2,256,256]{2,1,0:T(8,128)(2,1)S(1)}, bf16[2,256,256]{2,1,0:T(8,128)(2,1)S(1)}, u32[]{:S(2)}, u32[]{:S(2)}) collective-permute-start(bf16[2,256,256]{2,1,0:T(8,128)(2,1)S(1)} %collective-permute-done.1.refs_2_), channel_id=1, source_target_pairs={{0,2},{1,3},{2,0},{3,1},{4,6},{5,7},{6,4},{7,5},{8,10},{9,11},{10,... | collective-permute-start | bytes 786440 | tf_op jit(solution)/shard_map/ppermute | solution.py:146
  17.4 0.0 copy-start.4
  17.4 0.0 copy-start.5
  17.4 0.4 collective-permute-start.6
  17.9 0.0 copy-done.1
  17.9 0.0 copy-done.2
  17.9 0.2 copy-done.4
  18.1 0.0 copy-done.5
  18.1 1.3 %shard_map.104 = (s32[16]{0:T(128)S(1)}, s32[4]{0:T(128)S(1)}, s32[4]{0:T(128)S(1)}, f32[4,256,128]{2,1,0:T(8,128)S(1)}, f32[1,512]{1,0:T(1,128)S(1)}) custom-call(s32[4]{0:T(128)S(1)} %copy-done.4, s32[4]{0:T(128)S(1)} %copy-done.5, f32[4,256]{1,0:T(4,128)S(1)} %copy-done.1, f32[1,512]{1,0:T(1,128)S(1)} %bitcast.5, ...), custom_call_target="tpu_custom_call" | custom-call | tf_op jit(solution)/shard_map/pallas_call | solution.py:113
  19.4 4.0 %collective-permute-done.6.refs_5_ = bf16[256,128]{1,0:T(8,128)(2,1)S(1)} collective-permute-done((bf16[256,128]{1,0:T(8,128)(2,1)S(1)}, bf16[256,128]{1,0:T(8,128)(2,1)S(1)}, u32[]{:S(2)}, u32[]{:S(2)}) %collective-permute-start.6) | collective-permute-done | bytes 65568 | tf_op jit(solution)/shard_map/ppermute | solution.py:142
  23.5 0.0 collective-permute-done.5.refs_0_
  23.5 0.0 collective-permute-done.4.refs_3_
  23.5 1.7 %collective-permute-start.8 = (bf16[2,256,256]{2,1,0:T(8,128)(2,1)S(1)}, bf16[2,256,256]{2,1,0:T(8,128)(2,1)S(1)}, u32[]{:S(2)}, u32[]{:S(2)}) collective-permute-start(bf16[2,256,256]{2,1,0:T(8,128)(2,1)S(1)} %collective-permute-done.5.refs_0_), channel_id=1, source_target_pairs={{0,4},{4,12},{12,8},{8,0},{1,5},{5,13},{13,9},{9,1},{2,6},{6,14},{... | collective-permute-start | bytes 786440 | tf_op jit(solution)/shard_map/ppermute | solution.py:142
  25.2 0.5 collective-permute-start.7
  25.7 1.2 %collective-permute-start.10 = (bf16[256,128]{1,0:T(8,128)(2,1)S(1)}, bf16[256,128]{1,0:T(8,128)(2,1)S(1)}, u32[]{:S(2)}, u32[]{:S(2)}) collective-permute-start(bf16[256,128]{1,0:T(8,128)(2,1)S(1)} %get-tuple-element.74), channel_id=1, source_target_pairs={{0,8},{4,0},{12,4},{8,12},{1,9},{5,1},{13,5},{9,13},{2,10},{6,2},{... | collective-permute-start | bytes 196616 | tf_op jit(solution)/shard_map/ppermute | solution.py:142
  26.9 0.0 collective-permute-start.9
  26.9 5.7 %collective-permute-done.10.refs_7_ = bf16[256,128]{1,0:T(8,128)(2,1)S(1)} collective-permute-done((bf16[256,128]{1,0:T(8,128)(2,1)S(1)}, bf16[256,128]{1,0:T(8,128)(2,1)S(1)}, u32[]{:S(2)}, u32[]{:S(2)}) %collective-permute-start.10) | collective-permute-done | bytes 65568 | tf_op jit(solution)/shard_map/ppermute | solution.py:142
  32.6 0.0 collective-permute-done.9.refs_6_
  32.6 0.1 collective-permute-done.8.refs_2_
  32.7 0.0 collective-permute-done.7.refs_1_
  32.7 0.0 collective-permute-start.11
  32.7 2.2 %collective-permute-start.13 = (bf16[256,256]{1,0:T(8,128)(2,1)S(1)}, bf16[256,256]{1,0:T(8,128)(2,1)S(1)}, u32[]{:S(2)}, u32[]{:S(2)}) collective-permute-start(bf16[256,256]{1,0:T(8,128)(2,1)S(1)} %get-tuple-element.85), channel_id=1, source_target_pairs={{0,12},{4,8},{12,0},{8,4},{1,13},{5,9},{13,1},{9,5},{2,14},{6,10},... | collective-permute-start | bytes 393224 | tf_op jit(solution)/shard_map/ppermute | solution.py:142
  34.9 0.0 collective-permute-start.12
  34.9 0.0 copy-done
  34.9 1.7 %shard_map.105 = (bf16[2,256,256]{2,1,0:T(8,128)(2,1)S(1)}, bf16[2,4,256,256]{3,2,1,0:T(8,128)(2,1)S(1)}, bf16[2,2,2,256,256]{4,3,2,1,0:T(8,128)(2,1)}) custom-call(s32[4]{0:T(128)S(1)} %get-tuple-element.71.widths, bf16[2,256,256]{2,1,0:T(8,128)(2,1)S(1)} %bitcast.4, bf16[2,256,256]{2,1,0:T(8,128)(2,1)S(1)} %collective-permute-done.refs_1_, ...), custom_call_target="tpu_custom_call" | custom-call | flops 268435456 | bytes 4194304 | tf_op jit(solution)/shard_map/pallas_call | solution.py:113
  36.6 3.5 %collective-permute-done.13.refs_6_ = bf16[256,256]{1,0:T(8,128)(2,1)S(1)} collective-permute-done((bf16[256,256]{1,0:T(8,128)(2,1)S(1)}, bf16[256,256]{1,0:T(8,128)(2,1)S(1)}, u32[]{:S(2)}, u32[]{:S(2)}) %collective-permute-start.13) | collective-permute-done | bytes 131104 | tf_op jit(solution)/shard_map/ppermute | solution.py:142
  40.0 0.0 collective-permute-done.12.refs_8_
  40.0 0.8 %collective-permute-done.11.refs_3_ = bf16[2,256,256]{2,1,0:T(8,128)(2,1)S(1)} collective-permute-done((bf16[2,256,256]{2,1,0:T(8,128)(2,1)S(1)}, bf16[2,256,256]{2,1,0:T(8,128)(2,1)S(1)}, u32[]{:S(2)}, u32[]{:S(2)}) %collective-permute-start.11) | collective-permute-done | bytes 262176 | tf_op jit(solution)/shard_map/ppermute | solution.py:146
  40.8 2.4 %shard_map.106 = (bf16[4,256,256]{2,1,0:T(8,128)(2,1)S(1)}, bf16[4,256,256]{2,1,0:T(8,128)(2,1)S(1)}, bf16[2,2,2,256,256]{4,3,2,1,0:T(8,128)(2,1)}, f32[16,1,128...) custom-call(s32[16]{0:T(128)S(1)} %get-tuple-element.70.src, ...), custom_call_target="tpu_custom_call" | custom-call | flops 1073741824 | bytes 6291456 | tf_op jit(solution)/shard_map/pallas_call | solution.py:113
  43.3 0.1 collective-permute-start.14
  43.4 0.9 %collective-permute-start.15 = (bf16[2,4,64,256]{3,2,1,0:T(8,128)(2,1)S(1)}, bf16[2,4,64,256]{3,2,1,0:T(8,128)(2,1)S(1)}, u32[]{:S(2)}, u32[]{:S(2)}) collective-permute-start(bf16[2,4,64,256]{3,2,1,0:T(8,128)(2,1)S(1)} %get-tuple-element.104), channel_id=1, source_target_pairs={{0,2},{1,3},{2,0},{3,1},{4,6},{5,7},{6,4},{7,5},{8,10},{9,11},{10,... | collective-permute-start | bytes 786440 | tf_op jit(solution)/shard_map/ppermute | solution.py:146
  44.3 0.9 %collective-permute-start.16 = (bf16[1,4,64,256]{3,2,1,0:T(8,128)(2,1)S(1)}, bf16[1,4,64,256]{3,2,1,0:T(8,128)(2,1)S(1)}, u32[]{:S(2)}, u32[]{:S(2)}) collective-permute-start(bf16[1,4,64,256]{3,2,1,0:T(8,128)(2,1)S(1)} %get-tuple-element.105), channel_id=1, source_target_pairs={{0,3},{1,2},{2,1},{3,0},{4,7},{5,6},{6,5},{7,4},{8,11},{9,10},{10,... | collective-permute-start | bytes 393224 | tf_op jit(solution)/shard_map/ppermute | solution.py:146
  45.2 9.7 %all_to_all.10.refs_2_.parts1 = f32[16,1,128]{2,1,0:T(1,128)S(1)} all-to-all(f32[16,1,128]{2,1,0:T(1,128)S(1)} %get-tuple-element.93), channel_id=1, replica_groups=mesh['grp'=2,'blk'=4,'op'=4] {'blk','op'}, dimensions={0} | all-to-all | bytes 16384 | tf_op jit(solution)/shard_map/all_to_all | solution.py:645
  55.0 0.0 collective-permute-done.14.refs_5_
  55.0 4.8 %shard_map.107 = (f32[16,1,128]{2,1,0:T(1,128)S(1)}, bf16[4,4,64,256]{3,2,1,0:T(8,128)(2,1)S(1)}, bf16[1,4,64,256]{3,2,1,0:T(8,128)(2,1)S(1)}, bf16[2,4,64,256]{...) custom-call(s32[16]{0:T(128)S(1)} %get-tuple-element.70.src, s32[4]{0:T(128)S(1)} %get-tuple-element.71.widths, ...), custom_call_target="tpu_custom_call" | custom-call | flops 1073741824 | bytes 6291456 | tf_op jit(solution)/shard_map/pallas_call | solution.py:113
  59.8 0.0 collective-permute-done.16.refs_1_
  59.8 0.0 collective-permute-done.15.refs_0_
  59.8 0.9 %collective-permute-start.18 = (bf16[2,4,64,256]{3,2,1,0:T(8,128)(2,1)S(1)}, bf16[2,4,64,256]{3,2,1,0:T(8,128)(2,1)S(1)}, u32[]{:S(2)}, u32[]{:S(2)}) collective-permute-start(bf16[2,4,64,256]{3,2,1,0:T(8,128)(2,1)S(1)} %get-tuple-element.111), channel_id=1, source_target_pairs={{0,2},{1,3},{2,0},{3,1},{4,6},{5,7},{6,4},{7,5},{8,10},{9,11},{10,... | collective-permute-start | bytes 786440 | tf_op jit(solution)/shard_map/ppermute | solution.py:146
  60.7 0.0 collective-permute-start.17
  60.7 1.3 %collective-permute-start.19 = (bf16[1,4,64,256]{3,2,1,0:T(8,128)(2,1)S(1)}, bf16[1,4,64,256]{3,2,1,0:T(8,128)(2,1)S(1)}, u32[]{:S(2)}, u32[]{:S(2)}) collective-permute-start(bf16[1,4,64,256]{3,2,1,0:T(8,128)(2,1)S(1)} %get-tuple-element.112), channel_id=1, source_target_pairs={{0,3},{1,2},{2,1},{3,0},{4,7},{5,6},{6,5},{7,4},{8,11},{9,10},{10,... | collective-permute-start | bytes 393224 | tf_op jit(solution)/shard_map/ppermute | solution.py:146
  62.0 9.5 %all_to_all.11.parts2 = f32[16,1,128]{2,1,0:T(1,128)S(1)} all-to-all(f32[16,1,128]{2,1,0:T(1,128)S(1)} %get-tuple-element.106), channel_id=1, replica_groups=mesh['grp'=2,'blk'=4,'op'=4] {'blk','op'}, dimensions={0} | all-to-all | bytes 16384 | tf_op jit(solution)/shard_map/all_to_all | solution.py:645
  71.6 0.0 collective-permute-done.17.refs_2_
  71.6 0.0 collective-permute-done.19.refs_4_
  71.6 0.0 collective-permute-done.18.refs_3_
  71.6 2.0 %shard_map.108 = (bf16[4,64,512]{2,1,0:T(8,128)(2,1)}, bf16[4,64,512]{2,1,0:T(8,128)(2,1)}, f32[1]{0:T(128)}) custom-call(s32[4]{0:T(128)S(1)} %get-tuple-element.69.slots, f32[16,1,128]{2,1,0:T(1,128)S(1)} %all_to_all.10.refs_2_.parts1, f32[16,1,128]{2,1,0:T(1,128)S(1)} %all_to_all.11.parts2, f32[4,256,128]{2,1,0:T(8,128)S(1)} %get-tuple-element.91.refs_11_.refs_6_.diag, ...), custom_call_target="tpu_custom_call" | custom-call | bytes 4194304 | tf_op jit(solution)/shard_map/pallas_call | solution.py:113
Async XLA Ops:
  0.6 4.6 %copy-start.3 = (s32[2]{0:T(128)S(1)}, s32[2]{0:T(128)}, u32[]{:S(2)}) copy-start(s32[2]{0:T(128)} %shift.1) | copy-start | bytes 28
  0.6 12.6 %collective-permute-start.1 = (bf16[2,256,256]{2,1,0:T(8,128)(2,1)}, bf16[2,256,256]{2,1,0:T(8,128)(2,1)S(1)}, u32[]{:S(2)}, u32[]{:S(2)}) collective-permute-start(bf16[2,256,256]{2,1,0:T(8,128)(2,1)} %bitcast.2), channel_id=1, source_target_pairs={{0,4},{4,12},{12,8},{8,0},{1,5},{5,13},{13,9},{9,1},{2,6},{6,14},{... | collective-permute-start | bytes 786440 | tf_op jit(solution)/shard_map/ppermute | solution.py:142
  3.7 9.6 %collective-permute-start = (bf16[2,256,256]{2,1,0:T(8,128)(2,1)}, bf16[2,256,256]{2,1,0:T(8,128)(2,1)S(1)}, u32[]{:S(2)}, u32[]{:S(2)}) collective-permute-start(bf16[2,256,256]{2,1,0:T(8,128)(2,1)} %bitcast.3), channel_id=1, source_target_pairs={{0,2},{1,3},{2,0},{3,1},{4,6},{5,7},{6,4},{7,5},{8,10},{9,11},{10,... | collective-permute-start | bytes 786440 | tf_op jit(solution)/shard_map/ppermute | solution.py:146
  5.2 1.1 %collective-permute-start.2 = (s32[2]{0:T(128)S(1)}, s32[2]{0:T(128)S(1)}, u32[]{:S(2)}, u32[]{:S(2)}) collective-permute-start(s32[2]{0:T(128)S(1)} %copy-done.3), channel_id=1, source_target_pairs={{0,1},{1,0},{2,3},{3,2},{4,5},{5,4},{6,7},{7,6},{8,9},{9,8},{10,11... | collective-permute-start | bytes 32 | tf_op jit(solution)/shard_map/ppermute | solution.py:146
  6.3 28.6 %copy-start = (bf16[2,1,256,256]{3,2,1,0:T(8,128)(2,1)S(1)}, bf16[2,1,256,256]{3,2,1,0:T(8,128)(2,1)}, u32[]{:S(2)}) copy-start(bf16[2,1,256,256]{3,2,1,0:T(8,128)(2,1)} %param.9) | copy-start | bytes 786436
  8.2 9.6 %copy-start.1 = (f32[4,256]{1,0:T(4,128)S(1)}, f32[4,256]{1,0:T(4,128)}, u32[]{:S(2)}) copy-start(f32[4,256]{1,0:T(4,128)} %left_diag.1) | copy-start | bytes 12292
  8.3 5.0 %collective-permute-start.3 = (bf16[144,256]{1,0:T(8,128)(2,1)S(1)}, bf16[144,256]{1,0:T(8,128)(2,1)S(1)}, u32[]{:S(2)}, u32[]{:S(2)}) collective-permute-start(bf16[144,256]{1,0:T(8,128)(2,1)S(1)} %get-tuple-element.59), channel_id=1, source_target_pairs={{0,2},{1,3},{2,0},{3,1},{4,6},{5,7},{6,4},{7,5},{8,10},{9,11},{10,... | collective-permute-start | bytes 221192 | tf_op jit(solution)/shard_map/ppermute | solution.py:146
  13.3 4.6 %copy-start.2 = (f32[512]{0:T(512)S(1)}, f32[512]{0:T(512)}, u32[]{:S(2)}) copy-start(f32[512]{0:T(512)} %param.15) | copy-start | bytes 6148
  13.3 10.2 %collective-permute-start.5 = (bf16[2,256,256]{2,1,0:T(8,128)(2,1)S(1)}, bf16[2,256,256]{2,1,0:T(8,128)(2,1)S(1)}, u32[]{:S(2)}, u32[]{:S(2)}) collective-permute-start(bf16[2,256,256]{2,1,0:T(8,128)(2,1)S(1)} %collective-permute-done.1.refs_2_), channel_id=1, source_target_pairs={{0,4},{4,12},{12,8},{8,0},{1,5},{5,13},{13,9},{9,1},{2,6},{6,14},{... | collective-permute-start | bytes 786440 | tf_op jit(solution)/shard_map/ppermute | solution.py:142
  15.9 7.5 %collective-permute-start.4 = (bf16[2,256,256]{2,1,0:T(8,128)(2,1)S(1)}, bf16[2,256,256]{2,1,0:T(8,128)(2,1)S(1)}, u32[]{:S(2)}, u32[]{:S(2)}) collective-permute-start(bf16[2,256,256]{2,1,0:T(8,128)(2,1)S(1)} %collective-permute-done.1.refs_2_), channel_id=1, source_target_pairs={{0,2},{1,3},{2,0},{3,1},{4,6},{5,7},{6,4},{7,5},{8,10},{9,11},{10,... | collective-permute-start | bytes 786440 | tf_op jit(solution)/shard_map/ppermute | solution.py:146
  17.4 0.7 copy-start.4
  17.4 0.7 copy-start.5
  17.4 6.0 %collective-permute-start.6 = (bf16[256,128]{1,0:T(8,128)(2,1)S(1)}, bf16[256,128]{1,0:T(8,128)(2,1)S(1)}, u32[]{:S(2)}, u32[]{:S(2)}) collective-permute-start(bf16[256,128]{1,0:T(8,128)(2,1)S(1)} %get-tuple-element.61), channel_id=1, source_target_pairs={{0,4},{4,12},{12,8},{8,0},{1,5},{5,13},{13,9},{9,1},{2,6},{6,14},{... | collective-permute-start | bytes 196616 | tf_op jit(solution)/shard_map/ppermute | solution.py:142
  23.5 9.3 %collective-permute-start.8 = (bf16[2,256,256]{2,1,0:T(8,128)(2,1)S(1)}, bf16[2,256,256]{2,1,0:T(8,128)(2,1)S(1)}, u32[]{:S(2)}, u32[]{:S(2)}) collective-permute-start(bf16[2,256,256]{2,1,0:T(8,128)(2,1)S(1)} %collective-permute-done.5.refs_0_), channel_id=1, source_target_pairs={{0,4},{4,12},{12,8},{8,0},{1,5},{5,13},{13,9},{9,1},{2,6},{6,14},{... | collective-permute-start | bytes 786440 | tf_op jit(solution)/shard_map/ppermute | solution.py:142
  25.2 7.6 %collective-permute-start.7 = (bf16[2,256,256]{2,1,0:T(8,128)(2,1)S(1)}, bf16[2,256,256]{2,1,0:T(8,128)(2,1)S(1)}, u32[]{:S(2)}, u32[]{:S(2)}) collective-permute-start(bf16[2,256,256]{2,1,0:T(8,128)(2,1)S(1)} %collective-permute-done.5.refs_0_), channel_id=1, source_target_pairs={{0,2},{1,3},{2,0},{3,1},{4,6},{5,7},{6,4},{7,5},{8,10},{9,11},{10,... | collective-permute-start | bytes 786440 | tf_op jit(solution)/shard_map/ppermute | solution.py:146
  25.7 6.9 %collective-permute-start.10 = (bf16[256,128]{1,0:T(8,128)(2,1)S(1)}, bf16[256,128]{1,0:T(8,128)(2,1)S(1)}, u32[]{:S(2)}, u32[]{:S(2)}) collective-permute-start(bf16[256,128]{1,0:T(8,128)(2,1)S(1)} %get-tuple-element.74), channel_id=1, source_target_pairs={{0,8},{4,0},{12,4},{8,12},{1,9},{5,1},{13,5},{9,13},{2,10},{6,2},{... | collective-permute-start | bytes 196616 | tf_op jit(solution)/shard_map/ppermute | solution.py:142
  26.9 5.7 %collective-permute-start.9 = (bf16[256,128]{1,0:T(8,128)(2,1)S(1)}, bf16[256,128]{1,0:T(8,128)(2,1)S(1)}, u32[]{:S(2)}, u32[]{:S(2)}) collective-permute-start(bf16[256,128]{1,0:T(8,128)(2,1)S(1)} %collective-permute-done.6.refs_5_), channel_id=1, source_target_pairs={{0,1},{1,0},{2,3},{3,2},{4,5},{5,4},{6,7},{7,6},{8,9},{9,8},{10,11... | collective-permute-start | bytes 196616 | tf_op jit(solution)/shard_map/ppermute | solution.py:146
  32.7 8.1 %collective-permute-start.11 = (bf16[2,256,256]{2,1,0:T(8,128)(2,1)S(1)}, bf16[2,256,256]{2,1,0:T(8,128)(2,1)S(1)}, u32[]{:S(2)}, u32[]{:S(2)}) collective-permute-start(bf16[2,256,256]{2,1,0:T(8,128)(2,1)S(1)} %collective-permute-done.8.refs_2_), channel_id=1, source_target_pairs={{0,2},{1,3},{2,0},{3,1},{4,6},{5,7},{6,4},{7,5},{8,10},{9,11},{10,... | collective-permute-start | bytes 786440 | tf_op jit(solution)/shard_map/ppermute | solution.py:146
  32.7 7.3 %collective-permute-start.13 = (bf16[256,256]{1,0:T(8,128)(2,1)S(1)}, bf16[256,256]{1,0:T(8,128)(2,1)S(1)}, u32[]{:S(2)}, u32[]{:S(2)}) collective-permute-start(bf16[256,256]{1,0:T(8,128)(2,1)S(1)} %get-tuple-element.85), channel_id=1, source_target_pairs={{0,12},{4,8},{12,0},{8,4},{1,13},{5,9},{13,1},{9,5},{2,14},{6,10},... | collective-permute-start | bytes 393224 | tf_op jit(solution)/shard_map/ppermute | solution.py:142
  34.9 5.1 %collective-permute-start.12 = (bf16[256,128]{1,0:T(8,128)(2,1)S(1)}, bf16[256,128]{1,0:T(8,128)(2,1)S(1)}, u32[]{:S(2)}, u32[]{:S(2)}) collective-permute-start(bf16[256,128]{1,0:T(8,128)(2,1)S(1)} %collective-permute-done.10.refs_7_), channel_id=1, source_target_pairs={{0,1},{1,0},{2,3},{3,2},{4,5},{5,4},{6,7},{7,6},{8,9},{9,8},{10,11... | collective-permute-start | bytes 196616 | tf_op jit(solution)/shard_map/ppermute | solution.py:146
  43.3 11.7 %collective-permute-start.14 = (bf16[4,256,256]{2,1,0:T(8,128)(2,1)S(1)}, bf16[4,256,256]{2,1,0:T(8,128)(2,1)S(1)}, u32[]{:S(2)}, u32[]{:S(2)}) collective-permute-start(bf16[4,256,256]{2,1,0:T(8,128)(2,1)S(1)} %get-tuple-element.94.refs_4_), channel_id=1, source_target_pairs={{0,1},{1,0},{2,3},{3,2},{4,5},{5,4},{6,7},{7,6},{8,9},{9,8},{10,11... | collective-permute-start | bytes 1572872 | tf_op jit(solution)/shard_map/ppermute | solution.py:146
  43.4 16.4 %collective-permute-start.15 = (bf16[2,4,64,256]{3,2,1,0:T(8,128)(2,1)S(1)}, bf16[2,4,64,256]{3,2,1,0:T(8,128)(2,1)S(1)}, u32[]{:S(2)}, u32[]{:S(2)}) collective-permute-start(bf16[2,4,64,256]{3,2,1,0:T(8,128)(2,1)S(1)} %get-tuple-element.104), channel_id=1, source_target_pairs={{0,2},{1,3},{2,0},{3,1},{4,6},{5,7},{6,4},{7,5},{8,10},{9,11},{10,... | collective-permute-start | bytes 786440 | tf_op jit(solution)/shard_map/ppermute | solution.py:146
  44.3 15.5 %collective-permute-start.16 = (bf16[1,4,64,256]{3,2,1,0:T(8,128)(2,1)S(1)}, bf16[1,4,64,256]{3,2,1,0:T(8,128)(2,1)S(1)}, u32[]{:S(2)}, u32[]{:S(2)}) collective-permute-start(bf16[1,4,64,256]{3,2,1,0:T(8,128)(2,1)S(1)} %get-tuple-element.105), channel_id=1, source_target_pairs={{0,3},{1,2},{2,1},{3,0},{4,7},{5,6},{6,5},{7,4},{8,11},{9,10},{10,... | collective-permute-start | bytes 393224 | tf_op jit(solution)/shard_map/ppermute | solution.py:146
  59.8 11.8 %collective-permute-start.18 = (bf16[2,4,64,256]{3,2,1,0:T(8,128)(2,1)S(1)}, bf16[2,4,64,256]{3,2,1,0:T(8,128)(2,1)S(1)}, u32[]{:S(2)}, u32[]{:S(2)}) collective-permute-start(bf16[2,4,64,256]{3,2,1,0:T(8,128)(2,1)S(1)} %get-tuple-element.111), channel_id=1, source_target_pairs={{0,2},{1,3},{2,0},{3,1},{4,6},{5,7},{6,4},{7,5},{8,10},{9,11},{10,... | collective-permute-start | bytes 786440 | tf_op jit(solution)/shard_map/ppermute | solution.py:146
  60.7 10.8 %collective-permute-start.17 = (bf16[1,4,64,256]{3,2,1,0:T(8,128)(2,1)S(1)}, bf16[1,4,64,256]{3,2,1,0:T(8,128)(2,1)S(1)}, u32[]{:S(2)}, u32[]{:S(2)}) collective-permute-start(bf16[1,4,64,256]{3,2,1,0:T(8,128)(2,1)S(1)} %get-tuple-element.110), channel_id=1, source_target_pairs={{0,1},{1,0},{2,3},{3,2},{4,5},{5,4},{6,7},{7,6},{8,9},{9,8},{10,11... | collective-permute-start | bytes 393224 | tf_op jit(solution)/shard_map/ppermute | solution.py:146
  60.7 10.8 %collective-permute-start.19 = (bf16[1,4,64,256]{3,2,1,0:T(8,128)(2,1)S(1)}, bf16[1,4,64,256]{3,2,1,0:T(8,128)(2,1)S(1)}, u32[]{:S(2)}, u32[]{:S(2)}) collective-permute-start(bf16[1,4,64,256]{3,2,1,0:T(8,128)(2,1)S(1)} %get-tuple-element.112), channel_id=1, source_target_pairs={{0,3},{1,2},{2,1},{3,0},{4,7},{5,6},{6,5},{7,4},{8,11},{9,10},{10,... | collective-permute-start | bytes 393224 | tf_op jit(solution)/shard_map/ppermute | solution.py:146

commit v19 on v18

--- a/solution.py
+++ b/solution.py
@@ -321,13 +321,11 @@
     n_blk -= 1
     terms = n_terms // len(right)
     turned = [by_block(right[j // terms], terms, j % terms) for j in range(n_terms)]
+    turned = jnp.concatenate(turned, axis=0)
     for t in range(n_blk):
-        total = None
-        for j in range(n_terms):
-            part = jnp.dot(
-                inter[src[t * n_terms + j], j], turned[j], preferred_element_type=jnp.float32
-            )
-            total = part if total is None else total + part
+        moved = [inter[src[t * n_terms + j], j] for j in range(n_terms)]
+        moved = jnp.concatenate(moved, axis=1)
+        total = jnp.dot(moved, turned, preferred_element_type=jnp.float32)
         total = jnp.where(row_mask(widths[t], total.shape), total, 0.0)
         out[t] = total.astype(jnp.bfloat16)
         emit(t, total)
@@ -460,8 +458,10 @@
             den = diagonal(diag, right_diag, d, h) - theta
             item = (sigma - theta * vec) * den / jnp.maximum(den * den, 0.25)
             corr[d, :, part] = item
-            vv, vc, vs = vv + fold(vec * vec), vc + fold(vec * item), vs + fold(vec * sigma)
-        halves.append((whole(vv), whole(vc), whole(vs)))
+            vv, vc = vv + fold(vec * vec), vc + fold(vec * item)
+            if h == 0:
+                vs = vs + fold(vec * sigma)
+        halves.append((whole(vv), whole(vc), vs))
     along = (halves[0][1] + halves[1][1]) / jnp.maximum(halves[0][0] + halves[1][0], 1e-30)
     terms = held.shape[2]
     for copy in copies:
@@ -496,7 +496,8 @@
     _, own_op = place_of()
     step = own_out.shape[2]
     sum_terms(src, widths, inter, right, part_out, emit)
-    spread(list(halves[0]) + [whole(x) for x in sums], dots_out)
+    vv, vc, vs = halves[0]
+    spread([vv, vc] + [whole(x) for x in [vs] + sums], dots_out)
 
 
 def ritz_pair(theta, h_mix, h_two):
@@ -667,7 +668,8 @@
             pltpu.VMEM((n_blk, *left_late[1:]), bf16),
             pltpu.SemaphoreType.DMA((n_blk,)),
         ],
-        **cost,
+        flops=4 * cost["flops"],
+        nbytes=24 << 20,
     )
     dots2, out2, got1 = lax.optimization_barrier((dots2, out2, got1))
     parts2 = totals(dots2)

time: 73.8 us -> 75.5 us (1.023)
  blocking collectives: 19.3 us -> 12 us
  waiting for transfers between devices: 19.7 us -> 24.3 us
  starting transfers between devices: 19.5 us -> 23.1 us
    all_to_all x2 -> x1, blocking collectives: 19.3 us -> 12 us  [totals(): return lax.all_to_all(parts, ('blk', 'op'), 0, 0, tiled=True)]
    all_to_all x0 -> x1, waiting for transfers between devices: none -> 4.21 us  [totals(): return lax.all_to_all(parts, ('blk', 'op'), 0, 0, tiled=True)]
    all_to_all x0 -> x1, starting transfers between devices: none -> 3.48 us  [totals(): return lax.all_to_all(parts, ('blk', 'op'), 0, 0, tiled=True)]
  transfers between devices with their start and end apart: 20 -> 21, of which waited for: 7 -> 9; matrix products, arithmetic and copies ran while one was open for 0% -> 0% of each run, Pallas kernels for 13% -> 13%
where the time goes in v19:
time: 75.5 us; the launch traced here: 75.2 us
  waiting for transfers between devices  24.3 us (32%)
  starting transfers between devices  23.1 us (31%)
  Pallas kernels  14.8 us (20%)
  blocking collectives  12 us (16%)
    pallas_call x6, Pallas kernels, kernel(): pl.pallas_call(body, out_shape=[HBM(shape, dtype) if space == HBM else ja...  14.8 us
    ppermute x6, waiting for transfers between devices, onward(): return lax.ppermute(block, 'blk', pairs)  13.3 us
    all_to_all x1, blocking collectives, totals(): return lax.all_to_all(parts, ('blk', 'op'), 0, 0, tiled=True)  12 us
    ppermute x6, starting transfers between devices, onward(): return lax.ppermute(block, 'blk', pairs)  11.2 us
    ppermute x14, starting transfers between devices, swap(): return lax.ppermute(block, 'op', [(i, i ^ e) for i in range(n_op)])  8.41 us
    ppermute x14, waiting for transfers between devices, swap(): return lax.ppermute(block, 'op', [(i, i ^ e) for i in range(n_op)])  6.84 us
    all_to_all x1, waiting for transfers between devices, totals(): return lax.all_to_all(parts, ('blk', 'op'), 0, 0, tiled=True)  4.21 us
    all_to_all x1, starting transfers between devices, totals(): return lax.all_to_all(parts, ('blk', 'op'), 0, 0, tiled=True)  3.48 us
  transfers between devices with their start and end apart: 21, of which 9 were waited for; matrix products, arithmetic and copies ran while one was open for 0% of the time, Pallas kernels for 13%

profile of v19, /device:TPU:0, one launch (start us, length us, event | category | flops | bytes accessed | tf_op | source)
XLA Modules:
  0.0 75.2 jit_solution(8977811473784163768)
XLA Ops:
  0.6 0.0 copy-start.3
  0.6 3.1 %collective-permute-start.1 = (bf16[2,256,256]{2,1,0:T(8,128)(2,1)}, bf16[2,256,256]{2,1,0:T(8,128)(2,1)S(1)}, u32[]{:S(2)}, u32[]{:S(2)}) collective-permute-start(bf16[2,256,256]{2,1,0:T(8,128)(2,1)} %bitcast.2), channel_id=1, source_target_pairs={{0,4},{4,12},{12,8},{8,0},{1,5},{5,13},{13,9},{9,1},{2,6},{6,14},{... | collective-permute-start | bytes 786440 | tf_op jit(solution)/shard_map/ppermute | solution.py:142
  3.7 1.5 %collective-permute-start = (bf16[2,256,256]{2,1,0:T(8,128)(2,1)}, bf16[2,256,256]{2,1,0:T(8,128)(2,1)S(1)}, u32[]{:S(2)}, u32[]{:S(2)}) collective-permute-start(bf16[2,256,256]{2,1,0:T(8,128)(2,1)} %bitcast.3), channel_id=1, source_target_pairs={{0,2},{1,3},{2,0},{3,1},{4,6},{5,7},{6,4},{7,5},{8,10},{9,11},{10,... | collective-permute-start | bytes 786440 | tf_op jit(solution)/shard_map/ppermute | solution.py:146
  5.2 0.0 copy-done.3
  5.2 0.0 collective-permute-start.2
  5.2 1.1 %collective-permute-done.2._ = s32[2]{0:T(128)S(1)} collective-permute-done((s32[2]{0:T(128)S(1)}, s32[2]{0:T(128)S(1)}, u32[]{:S(2)}, u32[]{:S(2)}) %collective-permute-start.2) | collective-permute-done | bytes 40 | tf_op jit(solution)/shard_map/ppermute | solution.py:146
  6.3 0.0 copy-start
  6.3 1.9 %shard_map.103 = (bf16[256,256]{1,0:T(8,128)(2,1)S(1)}, bf16[256,128]{1,0:T(8,128)(2,1)S(1)}, bf16[256,256]{1,0:T(8,128)(2,1)S(1)}, bf16[256,128]{1,0:T(8,128)(2...) custom-call(s32[2]{0:T(128)S(1)} %copy-done.3, s32[2]{0:T(128)S(1)} %collective-permute-done.2._, ...), custom_call_target="tpu_custom_call" | custom-call | bytes 1048576 | tf_op jit(solution)/shard_map/pallas_call | solution.py:113
  8.2 0.0 copy-start.1
  8.3 0.6 collective-permute-start.3
  8.9 4.4 %collective-permute-done.3.refs_1_.refs_5_ = bf16[144,256]{1,0:T(8,128)(2,1)S(1)} collective-permute-done((bf16[144,256]{1,0:T(8,128)(2,1)S(1)}, bf16[144,256]{1,0:T(8,128)(2,1)S(1)}, u32[]{:S(2)}, u32[]{:S(2)}) %collective-permute-start.3) | collective-permute-done | bytes 73760 | tf_op jit(solution)/shard_map/ppermute | solution.py:146
  13.3 0.0 collective-permute-done.1.refs_2_
  13.3 0.0 collective-permute-done.refs_1_
  13.3 0.0 copy-start.2
  13.3 2.6 %collective-permute-start.5 = (bf16[2,256,256]{2,1,0:T(8,128)(2,1)S(1)}, bf16[2,256,256]{2,1,0:T(8,128)(2,1)S(1)}, u32[]{:S(2)}, u32[]{:S(2)}) collective-permute-start(bf16[2,256,256]{2,1,0:T(8,128)(2,1)S(1)} %collective-permute-done.1.refs_2_), channel_id=1, source_target_pairs={{0,4},{4,12},{12,8},{8,0},{1,5},{5,13},{13,9},{9,1},{2,6},{6,14},{... | collective-permute-start | bytes 786440 | tf_op jit(solution)/shard_map/ppermute | solution.py:142
  15.9 1.5 %collective-permute-start.4 = (bf16[2,256,256]{2,1,0:T(8,128)(2,1)S(1)}, bf16[2,256,256]{2,1,0:T(8,128)(2,1)S(1)}, u32[]{:S(2)}, u32[]{:S(2)}) collective-permute-start(bf16[2,256,256]{2,1,0:T(8,128)(2,1)S(1)} %collective-permute-done.1.refs_2_), channel_id=1, source_target_pairs={{0,2},{1,3},{2,0},{3,1},{4,6},{5,7},{6,4},{7,5},{8,10},{9,11},{10,... | collective-permute-start | bytes 786440 | tf_op jit(solution)/shard_map/ppermute | solution.py:146
  17.4 0.0 copy-start.4
  17.4 0.0 copy-start.5
  17.4 0.4 collective-permute-start.6
  17.9 0.0 copy-done.1
  17.9 0.0 copy-done.2
  17.9 0.2 copy-done.4
  18.1 0.0 copy-done.5
  18.1 1.3 %shard_map.104 = (s32[16]{0:T(128)S(1)}, s32[4]{0:T(128)S(1)}, s32[4]{0:T(128)S(1)}, f32[4,256,128]{2,1,0:T(8,128)S(1)}, f32[1,512]{1,0:T(1,128)S(1)}) custom-call(s32[4]{0:T(128)S(1)} %copy-done.4, s32[4]{0:T(128)S(1)} %copy-done.5, f32[4,256]{1,0:T(4,128)S(1)} %copy-done.1, f32[1,512]{1,0:T(1,128)S(1)} %bitcast.5, ...), custom_call_target="tpu_custom_call" | custom-call | tf_op jit(solution)/shard_map/pallas_call | solution.py:113
  19.4 4.0 %collective-permute-done.6.refs_5_ = bf16[256,128]{1,0:T(8,128)(2,1)S(1)} collective-permute-done((bf16[256,128]{1,0:T(8,128)(2,1)S(1)}, bf16[256,128]{1,0:T(8,128)(2,1)S(1)}, u32[]{:S(2)}, u32[]{:S(2)}) %collective-permute-start.6) | collective-permute-done | bytes 65568 | tf_op jit(solution)/shard_map/ppermute | solution.py:142
  23.5 0.0 collective-permute-done.5.refs_0_
  23.5 0.0 collective-permute-done.4.refs_3_
  23.5 1.7 %collective-permute-start.8 = (bf16[2,256,256]{2,1,0:T(8,128)(2,1)S(1)}, bf16[2,256,256]{2,1,0:T(8,128)(2,1)S(1)}, u32[]{:S(2)}, u32[]{:S(2)}) collective-permute-start(bf16[2,256,256]{2,1,0:T(8,128)(2,1)S(1)} %collective-permute-done.5.refs_0_), channel_id=1, source_target_pairs={{0,4},{4,12},{12,8},{8,0},{1,5},{5,13},{13,9},{9,1},{2,6},{6,14},{... | collective-permute-start | bytes 786440 | tf_op jit(solution)/shard_map/ppermute | solution.py:142
  25.2 0.5 collective-permute-start.7
  25.7 1.2 %collective-permute-start.10 = (bf16[256,128]{1,0:T(8,128)(2,1)S(1)}, bf16[256,128]{1,0:T(8,128)(2,1)S(1)}, u32[]{:S(2)}, u32[]{:S(2)}) collective-permute-start(bf16[256,128]{1,0:T(8,128)(2,1)S(1)} %get-tuple-element.74), channel_id=1, source_target_pairs={{0,8},{4,0},{12,4},{8,12},{1,9},{5,1},{13,5},{9,13},{2,10},{6,2},{... | collective-permute-start | bytes 196616 | tf_op jit(solution)/shard_map/ppermute | solution.py:142
  26.9 0.0 collective-permute-start.9
  26.9 5.7 %collective-permute-done.10.refs_7_ = bf16[256,128]{1,0:T(8,128)(2,1)S(1)} collective-permute-done((bf16[256,128]{1,0:T(8,128)(2,1)S(1)}, bf16[256,128]{1,0:T(8,128)(2,1)S(1)}, u32[]{:S(2)}, u32[]{:S(2)}) %collective-permute-start.10) | collective-permute-done | bytes 65568 | tf_op jit(solution)/shard_map/ppermute | solution.py:142
  32.6 0.0 collective-permute-done.9.refs_6_
  32.6 0.1 collective-permute-done.8.refs_2_
  32.7 0.0 collective-permute-done.7.refs_1_
  32.7 0.0 collective-permute-start.11
  32.7 2.2 %collective-permute-start.13 = (bf16[256,256]{1,0:T(8,128)(2,1)S(1)}, bf16[256,256]{1,0:T(8,128)(2,1)S(1)}, u32[]{:S(2)}, u32[]{:S(2)}) collective-permute-start(bf16[256,256]{1,0:T(8,128)(2,1)S(1)} %get-tuple-element.85), channel_id=1, source_target_pairs={{0,12},{4,8},{12,0},{8,4},{1,13},{5,9},{13,1},{9,5},{2,14},{6,10},... | collective-permute-start | bytes 393224 | tf_op jit(solution)/shard_map/ppermute | solution.py:142
  34.9 0.0 collective-permute-start.12
  34.9 0.0 copy-done
  34.9 1.7 %shard_map.105 = (bf16[2,256,256]{2,1,0:T(8,128)(2,1)S(1)}, bf16[2,4,256,256]{3,2,1,0:T(8,128)(2,1)S(1)}, bf16[2,2,2,256,256]{4,3,2,1,0:T(8,128)(2,1)}) custom-call(s32[4]{0:T(128)S(1)} %get-tuple-element.71.widths, bf16[2,256,256]{2,1,0:T(8,128)(2,1)S(1)} %bitcast.4, bf16[2,256,256]{2,1,0:T(8,128)(2,1)S(1)} %collective-permute-done.refs_1_, ...), custom_call_target="tpu_custom_call" | custom-call | flops 268435456 | bytes 4194304 | tf_op jit(solution)/shard_map/pallas_call | solution.py:113
  36.6 3.4 %collective-permute-done.13.refs_6_ = bf16[256,256]{1,0:T(8,128)(2,1)S(1)} collective-permute-done((bf16[256,256]{1,0:T(8,128)(2,1)S(1)}, bf16[256,256]{1,0:T(8,128)(2,1)S(1)}, u32[]{:S(2)}, u32[]{:S(2)}) %collective-permute-start.13) | collective-permute-done | bytes 131104 | tf_op jit(solution)/shard_map/ppermute | solution.py:142
  40.0 0.0 collective-permute-done.12.refs_8_
  40.0 0.8 %collective-permute-done.11.refs_3_ = bf16[2,256,256]{2,1,0:T(8,128)(2,1)S(1)} collective-permute-done((bf16[2,256,256]{2,1,0:T(8,128)(2,1)S(1)}, bf16[2,256,256]{2,1,0:T(8,128)(2,1)S(1)}, u32[]{:S(2)}, u32[]{:S(2)}) %collective-permute-start.11) | collective-permute-done | bytes 262176 | tf_op jit(solution)/shard_map/ppermute | solution.py:146
  40.8 3.1 %shard_map.106 = (bf16[4,256,256]{2,1,0:T(8,128)(2,1)S(1)}, bf16[4,256,256]{2,1,0:T(8,128)(2,1)S(1)}, bf16[2,2,2,256,256]{4,3,2,1,0:T(8,128)(2,1)}, f32[16,1,128...) custom-call(s32[16]{0:T(128)S(1)} %get-tuple-element.70.src, ...), custom_call_target="tpu_custom_call" | custom-call | flops 1073741824 | bytes 6291456 | tf_op jit(solution)/shard_map/pallas_call | solution.py:113
  43.9 0.1 collective-permute-start.14
  44.0 3.5 %all-to-all-start = ((f32[16,1,128]{2,1,0:T(1,128)}), f32[16,1,128]{2,1,0:T(1,128)S(1)}, u32[]{:S(2)}, u32[]{:S(2)}) async-start(f32[16,1,128]{2,1,0:T(1,128)} %get-tuple-element.93), calls=%async_computation | async-start | bytes 16384 | tf_op jit(solution)/shard_map/all_to_all | solution.py:646
  47.5 1.6 %collective-permute-start.16 = (bf16[1,4,64,256]{3,2,1,0:T(8,128)(2,1)S(1)}, bf16[1,4,64,256]{3,2,1,0:T(8,128)(2,1)S(1)}, u32[]{:S(2)}, u32[]{:S(2)}) collective-permute-start(bf16[1,4,64,256]{3,2,1,0:T(8,128)(2,1)S(1)} %get-tuple-element.105), channel_id=1, source_target_pairs={{0,3},{1,2},{2,1},{3,0},{4,7},{5,6},{6,5},{7,4},{8,11},{9,10},{10,... | collective-permute-start | bytes 393224 | tf_op jit(solution)/shard_map/ppermute | solution.py:146
  49.1 0.4 collective-permute-start.15
  49.6 4.2 %all-to-all-done.refs_2_.parts1 = f32[16,1,128]{2,1,0:T(1,128)S(1)} async-done(((f32[16,1,128]{2,1,0:T(1,128)}), f32[16,1,128]{2,1,0:T(1,128)S(1)}, u32[]{:S(2)}, u32[]{:S(2)}) %all-to-all-start) | async-done | bytes 8224 | tf_op jit(solution)/shard_map/all_to_all | solution.py:646
  53.8 0.0 collective-permute-done.14.refs_5_
  53.8 4.8 %shard_map.107 = (f32[16,1,128]{2,1,0:T(1,128)S(1)}, bf16[4,4,64,256]{3,2,1,0:T(8,128)(2,1)S(1)}, bf16[1,4,64,256]{3,2,1,0:T(8,128)(2,1)S(1)}, bf16[2,4,64,256]{...) custom-call(s32[16]{0:T(128)S(1)} %get-tuple-element.70.src, s32[4]{0:T(128)S(1)} %get-tuple-element.71.widths, ...), custom_call_target="tpu_custom_call" | custom-call | flops 4294967296 | bytes 25165824 | tf_op jit(solution)/shard_map/pallas_call | solution.py:113
  58.6 0.0 collective-permute-done.16.refs_1_
  58.6 0.5 collective-permute-done.15.refs_0_
  59.1 1.8 %collective-permute-start.18 = (bf16[2,4,64,256]{3,2,1,0:T(8,128)(2,1)S(1)}, bf16[2,4,64,256]{3,2,1,0:T(8,128)(2,1)S(1)}, u32[]{:S(2)}, u32[]{:S(2)}) collective-permute-start(bf16[2,4,64,256]{3,2,1,0:T(8,128)(2,1)S(1)} %get-tuple-element.111), channel_id=1, source_target_pairs={{0,2},{1,3},{2,0},{3,1},{4,6},{5,7},{6,4},{7,5},{8,10},{9,11},{10,... | collective-permute-start | bytes 786440 | tf_op jit(solution)/shard_map/ppermute | solution.py:146
  60.8 0.0 collective-permute-start.17
  60.8 0.4 collective-permute-start.19
  61.2 12.0 %all_to_all.10.parts2 = f32[16,1,128]{2,1,0:T(1,128)S(1)} all-to-all(f32[16,1,128]{2,1,0:T(1,128)S(1)} %get-tuple-element.106), channel_id=1, replica_groups=mesh['grp'=2,'blk'=4,'op'=4] {'blk','op'}, dimensions={0} | all-to-all | bytes 16384 | tf_op jit(solution)/shard_map/all_to_all | solution.py:646
  73.2 0.0 collective-permute-done.17.refs_2_
  73.2 0.0 collective-permute-done.19.refs_4_
  73.2 0.0 collective-permute-done.18.refs_3_
  73.2 2.0 %shard_map.108 = (bf16[4,64,512]{2,1,0:T(8,128)(2,1)}, bf16[4,64,512]{2,1,0:T(8,128)(2,1)}, f32[1]{0:T(128)}) custom-call(s32[4]{0:T(128)S(1)} %get-tuple-element.69.slots, f32[16,1,128]{2,1,0:T(1,128)S(1)} %all-to-all-done.refs_2_.parts1, f32[16,1,128]{2,1,0:T(1,128)S(1)} %all_to_all.10.parts2, f32[4,256,128]{2,1,0:T(8,128)S(1)} %get-tuple-element.91.refs_11_.refs_6_.diag, ...), custom_call_target="tpu_custom_call" | custom-call | bytes 4194304 | tf_op jit(solution)/shard_map/pallas_call | solution.py:113
Async XLA Ops:
  0.6 4.6 %copy-start.3 = (s32[2]{0:T(128)S(1)}, s32[2]{0:T(128)}, u32[]{:S(2)}) copy-start(s32[2]{0:T(128)} %shift.1) | copy-start | bytes 28
  0.6 12.6 %collective-permute-start.1 = (bf16[2,256,256]{2,1,0:T(8,128)(2,1)}, bf16[2,256,256]{2,1,0:T(8,128)(2,1)S(1)}, u32[]{:S(2)}, u32[]{:S(2)}) collective-permute-start(bf16[2,256,256]{2,1,0:T(8,128)(2,1)} %bitcast.2), channel_id=1, source_target_pairs={{0,4},{4,12},{12,8},{8,0},{1,5},{5,13},{13,9},{9,1},{2,6},{6,14},{... | collective-permute-start | bytes 786440 | tf_op jit(solution)/shard_map/ppermute | solution.py:142
  3.7 9.6 %collective-permute-start = (bf16[2,256,256]{2,1,0:T(8,128)(2,1)}, bf16[2,256,256]{2,1,0:T(8,128)(2,1)S(1)}, u32[]{:S(2)}, u32[]{:S(2)}) collective-permute-start(bf16[2,256,256]{2,1,0:T(8,128)(2,1)} %bitcast.3), channel_id=1, source_target_pairs={{0,2},{1,3},{2,0},{3,1},{4,6},{5,7},{6,4},{7,5},{8,10},{9,11},{10,... | collective-permute-start | bytes 786440 | tf_op jit(solution)/shard_map/ppermute | solution.py:146
  5.2 1.1 %collective-permute-start.2 = (s32[2]{0:T(128)S(1)}, s32[2]{0:T(128)S(1)}, u32[]{:S(2)}, u32[]{:S(2)}) collective-permute-start(s32[2]{0:T(128)S(1)} %copy-done.3), channel_id=1, source_target_pairs={{0,1},{1,0},{2,3},{3,2},{4,5},{5,4},{6,7},{7,6},{8,9},{9,8},{10,11... | collective-permute-start | bytes 32 | tf_op jit(solution)/shard_map/ppermute | solution.py:146
  6.3 28.6 %copy-start = (bf16[2,1,256,256]{3,2,1,0:T(8,128)(2,1)S(1)}, bf16[2,1,256,256]{3,2,1,0:T(8,128)(2,1)}, u32[]{:S(2)}) copy-start(bf16[2,1,256,256]{3,2,1,0:T(8,128)(2,1)} %param.9) | copy-start | bytes 786436
  8.2 9.6 %copy-start.1 = (f32[4,256]{1,0:T(4,128)S(1)}, f32[4,256]{1,0:T(4,128)}, u32[]{:S(2)}) copy-start(f32[4,256]{1,0:T(4,128)} %left_diag.1) | copy-start | bytes 12292
  8.3 5.0 %collective-permute-start.3 = (bf16[144,256]{1,0:T(8,128)(2,1)S(1)}, bf16[144,256]{1,0:T(8,128)(2,1)S(1)}, u32[]{:S(2)}, u32[]{:S(2)}) collective-permute-start(bf16[144,256]{1,0:T(8,128)(2,1)S(1)} %get-tuple-element.59), channel_id=1, source_target_pairs={{0,2},{1,3},{2,0},{3,1},{4,6},{5,7},{6,4},{7,5},{8,10},{9,11},{10,... | collective-permute-start | bytes 221192 | tf_op jit(solution)/shard_map/ppermute | solution.py:146
  13.3 4.6 %copy-start.2 = (f32[512]{0:T(512)S(1)}, f32[512]{0:T(512)}, u32[]{:S(2)}) copy-start(f32[512]{0:T(512)} %param.15) | copy-start | bytes 6148
  13.3 10.2 %collective-permute-start.5 = (bf16[2,256,256]{2,1,0:T(8,128)(2,1)S(1)}, bf16[2,256,256]{2,1,0:T(8,128)(2,1)S(1)}, u32[]{:S(2)}, u32[]{:S(2)}) collective-permute-start(bf16[2,256,256]{2,1,0:T(8,128)(2,1)S(1)} %collective-permute-done.1.refs_2_), channel_id=1, source_target_pairs={{0,4},{4,12},{12,8},{8,0},{1,5},{5,13},{13,9},{9,1},{2,6},{6,14},{... | collective-permute-start | bytes 786440 | tf_op jit(solution)/shard_map/ppermute | solution.py:142
  15.9 7.5 %collective-permute-start.4 = (bf16[2,256,256]{2,1,0:T(8,128)(2,1)S(1)}, bf16[2,256,256]{2,1,0:T(8,128)(2,1)S(1)}, u32[]{:S(2)}, u32[]{:S(2)}) collective-permute-start(bf16[2,256,256]{2,1,0:T(8,128)(2,1)S(1)} %collective-permute-done.1.refs_2_), channel_id=1, source_target_pairs={{0,2},{1,3},{2,0},{3,1},{4,6},{5,7},{6,4},{7,5},{8,10},{9,11},{10,... | collective-permute-start | bytes 786440 | tf_op jit(solution)/shard_map/ppermute | solution.py:146
  17.4 0.7 copy-start.4
  17.4 0.7 copy-start.5
  17.4 6.0 %collective-permute-start.6 = (bf16[256,128]{1,0:T(8,128)(2,1)S(1)}, bf16[256,128]{1,0:T(8,128)(2,1)S(1)}, u32[]{:S(2)}, u32[]{:S(2)}) collective-permute-start(bf16[256,128]{1,0:T(8,128)(2,1)S(1)} %get-tuple-element.61), channel_id=1, source_target_pairs={{0,4},{4,12},{12,8},{8,0},{1,5},{5,13},{13,9},{9,1},{2,6},{6,14},{... | collective-permute-start | bytes 196616 | tf_op jit(solution)/shard_map/ppermute | solution.py:142
  23.5 9.3 %collective-permute-start.8 = (bf16[2,256,256]{2,1,0:T(8,128)(2,1)S(1)}, bf16[2,256,256]{2,1,0:T(8,128)(2,1)S(1)}, u32[]{:S(2)}, u32[]{:S(2)}) collective-permute-start(bf16[2,256,256]{2,1,0:T(8,128)(2,1)S(1)} %collective-permute-done.5.refs_0_), channel_id=1, source_target_pairs={{0,4},{4,12},{12,8},{8,0},{1,5},{5,13},{13,9},{9,1},{2,6},{6,14},{... | collective-permute-start | bytes 786440 | tf_op jit(solution)/shard_map/ppermute | solution.py:142
  25.2 7.6 %collective-permute-start.7 = (bf16[2,256,256]{2,1,0:T(8,128)(2,1)S(1)}, bf16[2,256,256]{2,1,0:T(8,128)(2,1)S(1)}, u32[]{:S(2)}, u32[]{:S(2)}) collective-permute-start(bf16[2,256,256]{2,1,0:T(8,128)(2,1)S(1)} %collective-permute-done.5.refs_0_), channel_id=1, source_target_pairs={{0,2},{1,3},{2,0},{3,1},{4,6},{5,7},{6,4},{7,5},{8,10},{9,11},{10,... | collective-permute-start | bytes 786440 | tf_op jit(solution)/shard_map/ppermute | solution.py:146
  25.7 6.9 %collective-permute-start.10 = (bf16[256,128]{1,0:T(8,128)(2,1)S(1)}, bf16[256,128]{1,0:T(8,128)(2,1)S(1)}, u32[]{:S(2)}, u32[]{:S(2)}) collective-permute-start(bf16[256,128]{1,0:T(8,128)(2,1)S(1)} %get-tuple-element.74), channel_id=1, source_target_pairs={{0,8},{4,0},{12,4},{8,12},{1,9},{5,1},{13,5},{9,13},{2,10},{6,2},{... | collective-permute-start | bytes 196616 | tf_op jit(solution)/shard_map/ppermute | solution.py:142
  26.9 5.7 %collective-permute-start.9 = (bf16[256,128]{1,0:T(8,128)(2,1)S(1)}, bf16[256,128]{1,0:T(8,128)(2,1)S(1)}, u32[]{:S(2)}, u32[]{:S(2)}) collective-permute-start(bf16[256,128]{1,0:T(8,128)(2,1)S(1)} %collective-permute-done.6.refs_5_), channel_id=1, source_target_pairs={{0,1},{1,0},{2,3},{3,2},{4,5},{5,4},{6,7},{7,6},{8,9},{9,8},{10,11... | collective-permute-start | bytes 196616 | tf_op jit(solution)/shard_map/ppermute | solution.py:146
  32.7 8.1 %collective-permute-start.11 = (bf16[2,256,256]{2,1,0:T(8,128)(2,1)S(1)}, bf16[2,256,256]{2,1,0:T(8,128)(2,1)S(1)}, u32[]{:S(2)}, u32[]{:S(2)}) collective-permute-start(bf16[2,256,256]{2,1,0:T(8,128)(2,1)S(1)} %collective-permute-done.8.refs_2_), channel_id=1, source_target_pairs={{0,2},{1,3},{2,0},{3,1},{4,6},{5,7},{6,4},{7,5},{8,10},{9,11},{10,... | collective-permute-start | bytes 786440 | tf_op jit(solution)/shard_map/ppermute | solution.py:146
  32.7 7.3 %collective-permute-start.13 = (bf16[256,256]{1,0:T(8,128)(2,1)S(1)}, bf16[256,256]{1,0:T(8,128)(2,1)S(1)}, u32[]{:S(2)}, u32[]{:S(2)}) collective-permute-start(bf16[256,256]{1,0:T(8,128)(2,1)S(1)} %get-tuple-element.85), channel_id=1, source_target_pairs={{0,12},{4,8},{12,0},{8,4},{1,13},{5,9},{13,1},{9,5},{2,14},{6,10},... | collective-permute-start | bytes 393224 | tf_op jit(solution)/shard_map/ppermute | solution.py:142
  34.9 5.1 %collective-permute-start.12 = (bf16[256,128]{1,0:T(8,128)(2,1)S(1)}, bf16[256,128]{1,0:T(8,128)(2,1)S(1)}, u32[]{:S(2)}, u32[]{:S(2)}) collective-permute-start(bf16[256,128]{1,0:T(8,128)(2,1)S(1)} %collective-permute-done.10.refs_7_), channel_id=1, source_target_pairs={{0,1},{1,0},{2,3},{3,2},{4,5},{5,4},{6,7},{7,6},{8,9},{9,8},{10,11... | collective-permute-start | bytes 196616 | tf_op jit(solution)/shard_map/ppermute | solution.py:146
  43.9 9.9 %collective-permute-start.14 = (bf16[4,256,256]{2,1,0:T(8,128)(2,1)S(1)}, bf16[4,256,256]{2,1,0:T(8,128)(2,1)S(1)}, u32[]{:S(2)}, u32[]{:S(2)}) collective-permute-start(bf16[4,256,256]{2,1,0:T(8,128)(2,1)S(1)} %get-tuple-element.94.refs_4_), channel_id=1, source_target_pairs={{0,1},{1,0},{2,3},{3,2},{4,5},{5,4},{6,7},{7,6},{8,9},{9,8},{10,11... | collective-permute-start | bytes 1572872 | tf_op jit(solution)/shard_map/ppermute | solution.py:146
  44.0 9.8 %all-to-all-start = ((f32[16,1,128]{2,1,0:T(1,128)}), f32[16,1,128]{2,1,0:T(1,128)S(1)}, u32[]{:S(2)}, u32[]{:S(2)}) async-start(f32[16,1,128]{2,1,0:T(1,128)} %get-tuple-element.93), calls=%async_computation | async-start | bytes 16384 | tf_op jit(solution)/shard_map/all_to_all | solution.py:646
  47.5 11.1 %collective-permute-start.16 = (bf16[1,4,64,256]{3,2,1,0:T(8,128)(2,1)S(1)}, bf16[1,4,64,256]{3,2,1,0:T(8,128)(2,1)S(1)}, u32[]{:S(2)}, u32[]{:S(2)}) collective-permute-start(bf16[1,4,64,256]{3,2,1,0:T(8,128)(2,1)S(1)} %get-tuple-element.105), channel_id=1, source_target_pairs={{0,3},{1,2},{2,1},{3,0},{4,7},{5,6},{6,5},{7,4},{8,11},{9,10},{10,... | collective-permute-start | bytes 393224 | tf_op jit(solution)/shard_map/ppermute | solution.py:146
  49.1 9.9 %collective-permute-start.15 = (bf16[2,4,64,256]{3,2,1,0:T(8,128)(2,1)S(1)}, bf16[2,4,64,256]{3,2,1,0:T(8,128)(2,1)S(1)}, u32[]{:S(2)}, u32[]{:S(2)}) collective-permute-start(bf16[2,4,64,256]{3,2,1,0:T(8,128)(2,1)S(1)} %get-tuple-element.104), channel_id=1, source_target_pairs={{0,2},{1,3},{2,0},{3,1},{4,6},{5,7},{6,4},{7,5},{8,10},{9,11},{10,... | collective-permute-start | bytes 786440 | tf_op jit(solution)/shard_map/ppermute | solution.py:146
  59.1 14.2 %collective-permute-start.18 = (bf16[2,4,64,256]{3,2,1,0:T(8,128)(2,1)S(1)}, bf16[2,4,64,256]{3,2,1,0:T(8,128)(2,1)S(1)}, u32[]{:S(2)}, u32[]{:S(2)}) collective-permute-start(bf16[2,4,64,256]{3,2,1,0:T(8,128)(2,1)S(1)} %get-tuple-element.111), channel_id=1, source_target_pairs={{0,2},{1,3},{2,0},{3,1},{4,6},{5,7},{6,4},{7,5},{8,10},{9,11},{10,... | collective-permute-start | bytes 786440 | tf_op jit(solution)/shard_map/ppermute | solution.py:146
  60.8 12.4 %collective-permute-start.17 = (bf16[1,4,64,256]{3,2,1,0:T(8,128)(2,1)S(1)}, bf16[1,4,64,256]{3,2,1,0:T(8,128)(2,1)S(1)}, u32[]{:S(2)}, u32[]{:S(2)}) collective-permute-start(bf16[1,4,64,256]{3,2,1,0:T(8,128)(2,1)S(1)} %get-tuple-element.110), channel_id=1, source_target_pairs={{0,1},{1,0},{2,3},{3,2},{4,5},{5,4},{6,7},{7,6},{8,9},{9,8},{10,11... | collective-permute-start | bytes 393224 | tf_op jit(solution)/shard_map/ppermute | solution.py:146
  60.8 12.4 %collective-permute-start.19 = (bf16[1,4,64,256]{3,2,1,0:T(8,128)(2,1)S(1)}, bf16[1,4,64,256]{3,2,1,0:T(8,128)(2,1)S(1)}, u32[]{:S(2)}, u32[]{:S(2)}) collective-permute-start(bf16[1,4,64,256]{3,2,1,0:T(8,128)(2,1)S(1)} %get-tuple-element.112), channel_id=1, source_target_pairs={{0,3},{1,2},{2,1},{3,0},{4,7},{5,6},{6,5},{7,4},{8,11},{9,10},{10,... | collective-permute-start | bytes 393224 | tf_op jit(solution)/shard_map/ppermute | solution.py:146

commit v20 on v19

--- a/solution.py
+++ b/solution.py
@@ -321,11 +321,13 @@
     n_blk -= 1
     terms = n_terms // len(right)
     turned = [by_block(right[j // terms], terms, j % terms) for j in range(n_terms)]
-    turned = jnp.concatenate(turned, axis=0)
     for t in range(n_blk):
-        moved = [inter[src[t * n_terms + j], j] for j in range(n_terms)]
-        moved = jnp.concatenate(moved, axis=1)
-        total = jnp.dot(moved, turned, preferred_element_type=jnp.float32)
+        total = None
+        for j in range(n_terms):
+            part = jnp.dot(
+                inter[src[t * n_terms + j], j], turned[j], preferred_element_type=jnp.float32
+            )
+            total = part if total is None else total + part
         total = jnp.where(row_mask(widths[t], total.shape), total, 0.0)
         out[t] = total.astype(jnp.bfloat16)
         emit(t, total)
@@ -671,7 +673,7 @@
         flops=4 * cost["flops"],
         nbytes=24 << 20,
     )
-    dots2, out2, got1 = lax.optimization_barrier((dots2, out2, got1))
+    dots2, got1 = lax.optimization_barrier((dots2, got1))
     parts2 = totals(dots2)
     got2 = [swap(block, e, n_op) for e, block in enumerate(out2, 1)]
     final = ((n_blk, step, n_op * cols), bf16, VMEM)

time: 75.5 us -> 80.8 us (1.070)
  waiting for transfers between devices: 24.3 us -> 31.8 us
  blocking collectives: 12 us -> 9.83 us
    ppermute x14, waiting for transfers between devices: 6.84 us -> 14.1 us  [swap(): return lax.ppermute(block, 'op', [(i, i ^ e) for i in range(n_op)])]
    all_to_all x1, blocking collectives: 12 us -> 9.83 us  [totals(): return lax.all_to_all(parts, ('blk', 'op'), 0, 0, tiled=True)]
  transfers between devices with their start and end apart: 21 -> 21, of which waited for: 9 -> 9; matrix products, arithmetic and copies ran while one was open for 0% -> 0% of each run, Pallas kernels for 13% -> 12%
where the time goes in v20:
time: 80.8 us; the launch traced here: 80.5 us
  waiting for transfers between devices  31.8 us (39%)
  starting transfers between devices  23.1 us (29%)
  Pallas kernels  14.8 us (18%)
  blocking collectives  9.83 us (12%)
    pallas_call x6, Pallas kernels, kernel(): pl.pallas_call(body, out_shape=[HBM(shape, dtype) if space == HBM else ja...  14.8 us
    ppermute x14, waiting for transfers between devices, swap(): return lax.ppermute(block, 'op', [(i, i ^ e) for i in range(n_op)])  14.1 us
    ppermute x6, waiting for transfers between devices, onward(): return lax.ppermute(block, 'blk', pairs)  13.3 us
    ppermute x6, starting transfers between devices, onward(): return lax.ppermute(block, 'blk', pairs)  11.2 us
    all_to_all x1, blocking collectives, totals(): return lax.all_to_all(parts, ('blk', 'op'), 0, 0, tiled=True)  9.83 us
    ppermute x14, starting transfers between devices, swap(): return lax.ppermute(block, 'op', [(i, i ^ e) for i in range(n_op)])  8.39 us
    all_to_all x1, waiting for transfers between devices, totals(): return lax.all_to_all(parts, ('blk', 'op'), 0, 0, tiled=True)  4.41 us
    all_to_all x1, starting transfers between devices, totals(): return lax.all_to_all(parts, ('blk', 'op'), 0, 0, tiled=True)  3.48 us
  transfers between devices with their start and end apart: 21, of which 9 were waited for; matrix products, arithmetic and copies ran while one was open for 0% of the time, Pallas kernels for 12%

profile of v20, /device:TPU:0, one launch (start us, length us, event | category | flops | bytes accessed | tf_op | source)
XLA Modules:
  0.0 80.5 jit_solution(6876194979598197421)
XLA Ops:
  0.6 0.0 copy-start.3
  0.6 3.1 %collective-permute-start.1 = (bf16[2,256,256]{2,1,0:T(8,128)(2,1)}, bf16[2,256,256]{2,1,0:T(8,128)(2,1)S(1)}, u32[]{:S(2)}, u32[]{:S(2)}) collective-permute-start(bf16[2,256,256]{2,1,0:T(8,128)(2,1)} %bitcast.2), channel_id=1, source_target_pairs={{0,4},{4,12},{12,8},{8,0},{1,5},{5,13},{13,9},{9,1},{2,6},{6,14},{... | collective-permute-start | bytes 786440 | tf_op jit(solution)/shard_map/ppermute | solution.py:142
  3.7 1.5 %collective-permute-start = (bf16[2,256,256]{2,1,0:T(8,128)(2,1)}, bf16[2,256,256]{2,1,0:T(8,128)(2,1)S(1)}, u32[]{:S(2)}, u32[]{:S(2)}) collective-permute-start(bf16[2,256,256]{2,1,0:T(8,128)(2,1)} %bitcast.3), channel_id=1, source_target_pairs={{0,2},{1,3},{2,0},{3,1},{4,6},{5,7},{6,4},{7,5},{8,10},{9,11},{10,... | collective-permute-start | bytes 786440 | tf_op jit(solution)/shard_map/ppermute | solution.py:146
  5.2 0.0 copy-done.3
  5.2 0.0 collective-permute-start.2
  5.2 1.1 %collective-permute-done.2._ = s32[2]{0:T(128)S(1)} collective-permute-done((s32[2]{0:T(128)S(1)}, s32[2]{0:T(128)S(1)}, u32[]{:S(2)}, u32[]{:S(2)}) %collective-permute-start.2) | collective-permute-done | bytes 40 | tf_op jit(solution)/shard_map/ppermute | solution.py:146
  6.3 0.0 copy-start
  6.3 1.9 %shard_map.103 = (bf16[256,256]{1,0:T(8,128)(2,1)S(1)}, bf16[256,128]{1,0:T(8,128)(2,1)S(1)}, bf16[256,256]{1,0:T(8,128)(2,1)S(1)}, bf16[256,128]{1,0:T(8,128)(2...) custom-call(s32[2]{0:T(128)S(1)} %copy-done.3, s32[2]{0:T(128)S(1)} %collective-permute-done.2._, ...), custom_call_target="tpu_custom_call" | custom-call | bytes 1048576 | tf_op jit(solution)/shard_map/pallas_call | solution.py:113
  8.2 0.0 copy-start.1
  8.3 0.6 collective-permute-start.3
  8.9 4.4 %collective-permute-done.3.refs_1_.refs_5_ = bf16[144,256]{1,0:T(8,128)(2,1)S(1)} collective-permute-done((bf16[144,256]{1,0:T(8,128)(2,1)S(1)}, bf16[144,256]{1,0:T(8,128)(2,1)S(1)}, u32[]{:S(2)}, u32[]{:S(2)}) %collective-permute-start.3) | collective-permute-done | bytes 73760 | tf_op jit(solution)/shard_map/ppermute | solution.py:146
  13.3 0.0 collective-permute-done.1.refs_2_
  13.3 0.0 collective-permute-done.refs_1_
  13.3 0.0 copy-start.2
  13.3 2.6 %collective-permute-start.5 = (bf16[2,256,256]{2,1,0:T(8,128)(2,1)S(1)}, bf16[2,256,256]{2,1,0:T(8,128)(2,1)S(1)}, u32[]{:S(2)}, u32[]{:S(2)}) collective-permute-start(bf16[2,256,256]{2,1,0:T(8,128)(2,1)S(1)} %collective-permute-done.1.refs_2_), channel_id=1, source_target_pairs={{0,4},{4,12},{12,8},{8,0},{1,5},{5,13},{13,9},{9,1},{2,6},{6,14},{... | collective-permute-start | bytes 786440 | tf_op jit(solution)/shard_map/ppermute | solution.py:142
  15.9 1.5 %collective-permute-start.4 = (bf16[2,256,256]{2,1,0:T(8,128)(2,1)S(1)}, bf16[2,256,256]{2,1,0:T(8,128)(2,1)S(1)}, u32[]{:S(2)}, u32[]{:S(2)}) collective-permute-start(bf16[2,256,256]{2,1,0:T(8,128)(2,1)S(1)} %collective-permute-done.1.refs_2_), channel_id=1, source_target_pairs={{0,2},{1,3},{2,0},{3,1},{4,6},{5,7},{6,4},{7,5},{8,10},{9,11},{10,... | collective-permute-start | bytes 786440 | tf_op jit(solution)/shard_map/ppermute | solution.py:146
  17.4 0.0 copy-start.4
  17.4 0.0 copy-start.5
  17.4 0.4 collective-permute-start.6
  17.9 0.0 copy-done.1
  17.9 0.0 copy-done.2
  17.9 0.2 copy-done.4
  18.1 0.0 copy-done.5
  18.1 1.3 %shard_map.104 = (s32[16]{0:T(128)S(1)}, s32[4]{0:T(128)S(1)}, s32[4]{0:T(128)S(1)}, f32[4,256,128]{2,1,0:T(8,128)S(1)}, f32[1,512]{1,0:T(1,128)S(1)}) custom-call(s32[4]{0:T(128)S(1)} %copy-done.4, s32[4]{0:T(128)S(1)} %copy-done.5, f32[4,256]{1,0:T(4,128)S(1)} %copy-done.1, f32[1,512]{1,0:T(1,128)S(1)} %bitcast.5, ...), custom_call_target="tpu_custom_call" | custom-call | tf_op jit(solution)/shard_map/pallas_call | solution.py:113
  19.4 4.0 %collective-permute-done.6.refs_5_ = bf16[256,128]{1,0:T(8,128)(2,1)S(1)} collective-permute-done((bf16[256,128]{1,0:T(8,128)(2,1)S(1)}, bf16[256,128]{1,0:T(8,128)(2,1)S(1)}, u32[]{:S(2)}, u32[]{:S(2)}) %collective-permute-start.6) | collective-permute-done | bytes 65568 | tf_op jit(solution)/shard_map/ppermute | solution.py:142
  23.5 0.0 collective-permute-done.5.refs_0_
  23.5 0.0 collective-permute-done.4.refs_3_
  23.5 1.7 %collective-permute-start.8 = (bf16[2,256,256]{2,1,0:T(8,128)(2,1)S(1)}, bf16[2,256,256]{2,1,0:T(8,128)(2,1)S(1)}, u32[]{:S(2)}, u32[]{:S(2)}) collective-permute-start(bf16[2,256,256]{2,1,0:T(8,128)(2,1)S(1)} %collective-permute-done.5.refs_0_), channel_id=1, source_target_pairs={{0,4},{4,12},{12,8},{8,0},{1,5},{5,13},{13,9},{9,1},{2,6},{6,14},{... | collective-permute-start | bytes 786440 | tf_op jit(solution)/shard_map/ppermute | solution.py:142
  25.2 0.5 collective-permute-start.7
  25.7 1.2 %collective-permute-start.10 = (bf16[256,128]{1,0:T(8,128)(2,1)S(1)}, bf16[256,128]{1,0:T(8,128)(2,1)S(1)}, u32[]{:S(2)}, u32[]{:S(2)}) collective-permute-start(bf16[256,128]{1,0:T(8,128)(2,1)S(1)} %get-tuple-element.71), channel_id=1, source_target_pairs={{0,8},{4,0},{12,4},{8,12},{1,9},{5,1},{13,5},{9,13},{2,10},{6,2},{... | collective-permute-start | bytes 196616 | tf_op jit(solution)/shard_map/ppermute | solution.py:142
  26.9 0.0 collective-permute-start.9
  26.9 5.7 %collective-permute-done.10.refs_7_ = bf16[256,128]{1,0:T(8,128)(2,1)S(1)} collective-permute-done((bf16[256,128]{1,0:T(8,128)(2,1)S(1)}, bf16[256,128]{1,0:T(8,128)(2,1)S(1)}, u32[]{:S(2)}, u32[]{:S(2)}) %collective-permute-start.10) | collective-permute-done | bytes 65568 | tf_op jit(solution)/shard_map/ppermute | solution.py:142
  32.6 0.0 collective-permute-done.9.refs_6_
  32.6 0.1 collective-permute-done.8.refs_2_
  32.7 0.0 collective-permute-done.7.refs_1_
  32.7 0.0 collective-permute-start.11
  32.7 2.2 %collective-permute-start.13 = (bf16[256,256]{1,0:T(8,128)(2,1)S(1)}, bf16[256,256]{1,0:T(8,128)(2,1)S(1)}, u32[]{:S(2)}, u32[]{:S(2)}) collective-permute-start(bf16[256,256]{1,0:T(8,128)(2,1)S(1)} %get-tuple-element.82), channel_id=1, source_target_pairs={{0,12},{4,8},{12,0},{8,4},{1,13},{5,9},{13,1},{9,5},{2,14},{6,10},... | collective-permute-start | bytes 393224 | tf_op jit(solution)/shard_map/ppermute | solution.py:142
  34.9 0.0 collective-permute-start.12
  34.9 0.0 copy-done
  34.9 1.7 %shard_map.105 = (bf16[2,256,256]{2,1,0:T(8,128)(2,1)S(1)}, bf16[2,4,256,256]{3,2,1,0:T(8,128)(2,1)S(1)}, bf16[2,2,2,256,256]{4,3,2,1,0:T(8,128)(2,1)}) custom-call(s32[4]{0:T(128)S(1)} %get-tuple-element.68.widths, bf16[2,256,256]{2,1,0:T(8,128)(2,1)S(1)} %bitcast.4, bf16[2,256,256]{2,1,0:T(8,128)(2,1)S(1)} %collective-permute-done.refs_1_, ...), custom_call_target="tpu_custom_call" | custom-call | flops 268435456 | bytes 4194304 | tf_op jit(solution)/shard_map/pallas_call | solution.py:113
  36.6 3.4 %collective-permute-done.13.refs_6_ = bf16[256,256]{1,0:T(8,128)(2,1)S(1)} collective-permute-done((bf16[256,256]{1,0:T(8,128)(2,1)S(1)}, bf16[256,256]{1,0:T(8,128)(2,1)S(1)}, u32[]{:S(2)}, u32[]{:S(2)}) %collective-permute-start.13) | collective-permute-done | bytes 131104 | tf_op jit(solution)/shard_map/ppermute | solution.py:142
  40.0 0.0 collective-permute-done.12.refs_8_
  40.0 0.8 %collective-permute-done.11.refs_3_ = bf16[2,256,256]{2,1,0:T(8,128)(2,1)S(1)} collective-permute-done((bf16[2,256,256]{2,1,0:T(8,128)(2,1)S(1)}, bf16[2,256,256]{2,1,0:T(8,128)(2,1)S(1)}, u32[]{:S(2)}, u32[]{:S(2)}) %collective-permute-start.11) | collective-permute-done | bytes 262176 | tf_op jit(solution)/shard_map/ppermute | solution.py:146
  40.8 3.1 %shard_map.106 = (bf16[4,256,256]{2,1,0:T(8,128)(2,1)S(1)}, bf16[4,256,256]{2,1,0:T(8,128)(2,1)S(1)}, bf16[2,2,2,256,256]{4,3,2,1,0:T(8,128)(2,1)}, f32[16,1,128...) custom-call(s32[16]{0:T(128)S(1)} %get-tuple-element.67.src, ...), custom_call_target="tpu_custom_call" | custom-call | flops 1073741824 | bytes 6291456 | tf_op jit(solution)/shard_map/pallas_call | solution.py:113
  43.9 0.1 collective-permute-start.14
  44.0 3.5 %all-to-all-start = ((f32[16,1,128]{2,1,0:T(1,128)}), f32[16,1,128]{2,1,0:T(1,128)S(1)}, u32[]{:S(2)}, u32[]{:S(2)}) async-start(f32[16,1,128]{2,1,0:T(1,128)} %get-tuple-element.90), calls=%async_computation | async-start | bytes 16384 | tf_op jit(solution)/shard_map/all_to_all | solution.py:648
  47.5 1.9 %collective-permute-start.15 = (bf16[2,4,64,256]{3,2,1,0:T(8,128)(2,1)S(1)}, bf16[2,4,64,256]{3,2,1,0:T(8,128)(2,1)S(1)}, u32[]{:S(2)}, u32[]{:S(2)}) collective-permute-start(bf16[2,4,64,256]{3,2,1,0:T(8,128)(2,1)S(1)} %get-tuple-element.98), channel_id=1, source_target_pairs={{0,2},{1,3},{2,0},{3,1},{4,6},{5,7},{6,4},{7,5},{8,10},{9,11},{10,... | collective-permute-start | bytes 786440 | tf_op jit(solution)/shard_map/ppermute | solution.py:146
  49.4 4.4 %all-to-all-done.refs_2_.parts1 = f32[16,1,128]{2,1,0:T(1,128)S(1)} async-done(((f32[16,1,128]{2,1,0:T(1,128)}), f32[16,1,128]{2,1,0:T(1,128)S(1)}, u32[]{:S(2)}, u32[]{:S(2)}) %all-to-all-start) | async-done | bytes 8224 | tf_op jit(solution)/shard_map/all_to_all | solution.py:648
  53.8 0.0 collective-permute-done.14.refs_5_
  53.8 4.8 %shard_map.107 = (f32[16,1,128]{2,1,0:T(1,128)S(1)}, bf16[4,4,64,256]{3,2,1,0:T(8,128)(2,1)S(1)}, bf16[1,4,64,256]{3,2,1,0:T(8,128)(2,1)S(1)}, bf16[2,4,64,256]{...) custom-call(s32[16]{0:T(128)S(1)} %get-tuple-element.67.src, s32[4]{0:T(128)S(1)} %get-tuple-element.68.widths, ...), custom_call_target="tpu_custom_call" | custom-call | flops 4294967296 | bytes 25165824 | tf_op jit(solution)/shard_map/pallas_call | solution.py:113
  58.6 0.6 collective-permute-start.18
  59.2 0.6 collective-permute-start.16
  59.8 1.0 %collective-permute-start.17 = (bf16[1,4,64,256]{3,2,1,0:T(8,128)(2,1)S(1)}, bf16[1,4,64,256]{3,2,1,0:T(8,128)(2,1)S(1)}, u32[]{:S(2)}, u32[]{:S(2)}) collective-permute-start(bf16[1,4,64,256]{3,2,1,0:T(8,128)(2,1)S(1)} %get-tuple-element.104), channel_id=1, source_target_pairs={{0,1},{1,0},{2,3},{3,2},{4,5},{5,4},{6,7},{7,6},{8,9},{9,8},{10,11... | collective-permute-start | bytes 393224 | tf_op jit(solution)/shard_map/ppermute | solution.py:146
  60.8 0.1 collective-permute-start.19
  60.9 7.8 %collective-permute-done.16.refs_1_ = bf16[1,4,64,256]{3,2,1,0:T(8,128)(2,1)S(1)} collective-permute-done((bf16[1,4,64,256]{3,2,1,0:T(8,128)(2,1)S(1)}, bf16[1,4,64,256]{3,2,1,0:T(8,128)(2,1)S(1)}, u32[]{:S(2)}, u32[]{:S(2)}) %collective-permute-start.16) | collective-permute-done | bytes 131104 | tf_op jit(solution)/shard_map/ppermute | solution.py:146
  68.7 0.0 collective-permute-done.15.refs_0_
  68.7 9.8 %all_to_all.10.parts2 = f32[16,1,128]{2,1,0:T(1,128)S(1)} all-to-all(f32[16,1,128]{2,1,0:T(1,128)S(1)} %get-tuple-element.100), channel_id=1, replica_groups=mesh['grp'=2,'blk'=4,'op'=4] {'blk','op'}, dimensions={0} | all-to-all | bytes 16384 | tf_op jit(solution)/shard_map/all_to_all | solution.py:648
  78.5 0.0 collective-permute-done.17.refs_2_
  78.5 0.0 collective-permute-done.19.refs_4_
  78.5 0.0 collective-permute-done.18.refs_3_
  78.5 2.0 %shard_map.108 = (bf16[4,64,512]{2,1,0:T(8,128)(2,1)}, bf16[4,64,512]{2,1,0:T(8,128)(2,1)}, f32[1]{0:T(128)}) custom-call(s32[4]{0:T(128)S(1)} %get-tuple-element.66.slots, f32[16,1,128]{2,1,0:T(1,128)S(1)} %all-to-all-done.refs_2_.parts1, f32[16,1,128]{2,1,0:T(1,128)S(1)} %all_to_all.10.parts2, f32[4,256,128]{2,1,0:T(8,128)S(1)} %get-tuple-element.88.refs_11_.refs_6_.diag, ...), custom_call_target="tpu_custom_call" | custom-call | bytes 4194304 | tf_op jit(solution)/shard_map/pallas_call | solution.py:113
Async XLA Ops:
  0.6 4.6 %copy-start.3 = (s32[2]{0:T(128)S(1)}, s32[2]{0:T(128)}, u32[]{:S(2)}) copy-start(s32[2]{0:T(128)} %shift.1) | copy-start | bytes 28
  0.6 12.6 %collective-permute-start.1 = (bf16[2,256,256]{2,1,0:T(8,128)(2,1)}, bf16[2,256,256]{2,1,0:T(8,128)(2,1)S(1)}, u32[]{:S(2)}, u32[]{:S(2)}) collective-permute-start(bf16[2,256,256]{2,1,0:T(8,128)(2,1)} %bitcast.2), channel_id=1, source_target_pairs={{0,4},{4,12},{12,8},{8,0},{1,5},{5,13},{13,9},{9,1},{2,6},{6,14},{... | collective-permute-start | bytes 786440 | tf_op jit(solution)/shard_map/ppermute | solution.py:142
  3.7 9.6 %collective-permute-start = (bf16[2,256,256]{2,1,0:T(8,128)(2,1)}, bf16[2,256,256]{2,1,0:T(8,128)(2,1)S(1)}, u32[]{:S(2)}, u32[]{:S(2)}) collective-permute-start(bf16[2,256,256]{2,1,0:T(8,128)(2,1)} %bitcast.3), channel_id=1, source_target_pairs={{0,2},{1,3},{2,0},{3,1},{4,6},{5,7},{6,4},{7,5},{8,10},{9,11},{10,... | collective-permute-start | bytes 786440 | tf_op jit(solution)/shard_map/ppermute | solution.py:146
  5.2 1.1 %collective-permute-start.2 = (s32[2]{0:T(128)S(1)}, s32[2]{0:T(128)S(1)}, u32[]{:S(2)}, u32[]{:S(2)}) collective-permute-start(s32[2]{0:T(128)S(1)} %copy-done.3), channel_id=1, source_target_pairs={{0,1},{1,0},{2,3},{3,2},{4,5},{5,4},{6,7},{7,6},{8,9},{9,8},{10,11... | collective-permute-start | bytes 32 | tf_op jit(solution)/shard_map/ppermute | solution.py:146
  6.3 28.6 %copy-start = (bf16[2,1,256,256]{3,2,1,0:T(8,128)(2,1)S(1)}, bf16[2,1,256,256]{3,2,1,0:T(8,128)(2,1)}, u32[]{:S(2)}) copy-start(bf16[2,1,256,256]{3,2,1,0:T(8,128)(2,1)} %param.9) | copy-start | bytes 786436
  8.2 9.6 %copy-start.1 = (f32[4,256]{1,0:T(4,128)S(1)}, f32[4,256]{1,0:T(4,128)}, u32[]{:S(2)}) copy-start(f32[4,256]{1,0:T(4,128)} %left_diag.1) | copy-start | bytes 12292
  8.3 5.0 %collective-permute-start.3 = (bf16[144,256]{1,0:T(8,128)(2,1)S(1)}, bf16[144,256]{1,0:T(8,128)(2,1)S(1)}, u32[]{:S(2)}, u32[]{:S(2)}) collective-permute-start(bf16[144,256]{1,0:T(8,128)(2,1)S(1)} %get-tuple-element.56), channel_id=1, source_target_pairs={{0,2},{1,3},{2,0},{3,1},{4,6},{5,7},{6,4},{7,5},{8,10},{9,11},{10,... | collective-permute-start | bytes 221192 | tf_op jit(solution)/shard_map/ppermute | solution.py:146
  13.3 4.6 %copy-start.2 = (f32[512]{0:T(512)S(1)}, f32[512]{0:T(512)}, u32[]{:S(2)}) copy-start(f32[512]{0:T(512)} %param.15) | copy-start | bytes 6148
  13.3 10.2 %collective-permute-start.5 = (bf16[2,256,256]{2,1,0:T(8,128)(2,1)S(1)}, bf16[2,256,256]{2,1,0:T(8,128)(2,1)S(1)}, u32[]{:S(2)}, u32[]{:S(2)}) collective-permute-start(bf16[2,256,256]{2,1,0:T(8,128)(2,1)S(1)} %collective-permute-done.1.refs_2_), channel_id=1, source_target_pairs={{0,4},{4,12},{12,8},{8,0},{1,5},{5,13},{13,9},{9,1},{2,6},{6,14},{... | collective-permute-start | bytes 786440 | tf_op jit(solution)/shard_map/ppermute | solution.py:142
  15.9 7.5 %collective-permute-start.4 = (bf16[2,256,256]{2,1,0:T(8,128)(2,1)S(1)}, bf16[2,256,256]{2,1,0:T(8,128)(2,1)S(1)}, u32[]{:S(2)}, u32[]{:S(2)}) collective-permute-start(bf16[2,256,256]{2,1,0:T(8,128)(2,1)S(1)} %collective-permute-done.1.refs_2_), channel_id=1, source_target_pairs={{0,2},{1,3},{2,0},{3,1},{4,6},{5,7},{6,4},{7,5},{8,10},{9,11},{10,... | collective-permute-start | bytes 786440 | tf_op jit(solution)/shard_map/ppermute | solution.py:146
  17.4 0.7 copy-start.4
  17.4 0.7 copy-start.5
  17.4 6.0 %collective-permute-start.6 = (bf16[256,128]{1,0:T(8,128)(2,1)S(1)}, bf16[256,128]{1,0:T(8,128)(2,1)S(1)}, u32[]{:S(2)}, u32[]{:S(2)}) collective-permute-start(bf16[256,128]{1,0:T(8,128)(2,1)S(1)} %get-tuple-element.58), channel_id=1, source_target_pairs={{0,4},{4,12},{12,8},{8,0},{1,5},{5,13},{13,9},{9,1},{2,6},{6,14},{... | collective-permute-start | bytes 196616 | tf_op jit(solution)/shard_map/ppermute | solution.py:142
  23.5 9.3 %collective-permute-start.8 = (bf16[2,256,256]{2,1,0:T(8,128)(2,1)S(1)}, bf16[2,256,256]{2,1,0:T(8,128)(2,1)S(1)}, u32[]{:S(2)}, u32[]{:S(2)}) collective-permute-start(bf16[2,256,256]{2,1,0:T(8,128)(2,1)S(1)} %collective-permute-done.5.refs_0_), channel_id=1, source_target_pairs={{0,4},{4,12},{12,8},{8,0},{1,5},{5,13},{13,9},{9,1},{2,6},{6,14},{... | collective-permute-start | bytes 786440 | tf_op jit(solution)/shard_map/ppermute | solution.py:142
  25.2 7.6 %collective-permute-start.7 = (bf16[2,256,256]{2,1,0:T(8,128)(2,1)S(1)}, bf16[2,256,256]{2,1,0:T(8,128)(2,1)S(1)}, u32[]{:S(2)}, u32[]{:S(2)}) collective-permute-start(bf16[2,256,256]{2,1,0:T(8,128)(2,1)S(1)} %collective-permute-done.5.refs_0_), channel_id=1, source_target_pairs={{0,2},{1,3},{2,0},{3,1},{4,6},{5,7},{6,4},{7,5},{8,10},{9,11},{10,... | collective-permute-start | bytes 786440 | tf_op jit(solution)/shard_map/ppermute | solution.py:146
  25.7 6.9 %collective-permute-start.10 = (bf16[256,128]{1,0:T(8,128)(2,1)S(1)}, bf16[256,128]{1,0:T(8,128)(2,1)S(1)}, u32[]{:S(2)}, u32[]{:S(2)}) collective-permute-start(bf16[256,128]{1,0:T(8,128)(2,1)S(1)} %get-tuple-element.71), channel_id=1, source_target_pairs={{0,8},{4,0},{12,4},{8,12},{1,9},{5,1},{13,5},{9,13},{2,10},{6,2},{... | collective-permute-start | bytes 196616 | tf_op jit(solution)/shard_map/ppermute | solution.py:142
  26.9 5.7 %collective-permute-start.9 = (bf16[256,128]{1,0:T(8,128)(2,1)S(1)}, bf16[256,128]{1,0:T(8,128)(2,1)S(1)}, u32[]{:S(2)}, u32[]{:S(2)}) collective-permute-start(bf16[256,128]{1,0:T(8,128)(2,1)S(1)} %collective-permute-done.6.refs_5_), channel_id=1, source_target_pairs={{0,1},{1,0},{2,3},{3,2},{4,5},{5,4},{6,7},{7,6},{8,9},{9,8},{10,11... | collective-permute-start | bytes 196616 | tf_op jit(solution)/shard_map/ppermute | solution.py:146
  32.7 8.1 %collective-permute-start.11 = (bf16[2,256,256]{2,1,0:T(8,128)(2,1)S(1)}, bf16[2,256,256]{2,1,0:T(8,128)(2,1)S(1)}, u32[]{:S(2)}, u32[]{:S(2)}) collective-permute-start(bf16[2,256,256]{2,1,0:T(8,128)(2,1)S(1)} %collective-permute-done.8.refs_2_), channel_id=1, source_target_pairs={{0,2},{1,3},{2,0},{3,1},{4,6},{5,7},{6,4},{7,5},{8,10},{9,11},{10,... | collective-permute-start | bytes 786440 | tf_op jit(solution)/shard_map/ppermute | solution.py:146
  32.7 7.3 %collective-permute-start.13 = (bf16[256,256]{1,0:T(8,128)(2,1)S(1)}, bf16[256,256]{1,0:T(8,128)(2,1)S(1)}, u32[]{:S(2)}, u32[]{:S(2)}) collective-permute-start(bf16[256,256]{1,0:T(8,128)(2,1)S(1)} %get-tuple-element.82), channel_id=1, source_target_pairs={{0,12},{4,8},{12,0},{8,4},{1,13},{5,9},{13,1},{9,5},{2,14},{6,10},... | collective-permute-start | bytes 393224 | tf_op jit(solution)/shard_map/ppermute | solution.py:142
  34.9 5.1 %collective-permute-start.12 = (bf16[256,128]{1,0:T(8,128)(2,1)S(1)}, bf16[256,128]{1,0:T(8,128)(2,1)S(1)}, u32[]{:S(2)}, u32[]{:S(2)}) collective-permute-start(bf16[256,128]{1,0:T(8,128)(2,1)S(1)} %collective-permute-done.10.refs_7_), channel_id=1, source_target_pairs={{0,1},{1,0},{2,3},{3,2},{4,5},{5,4},{6,7},{7,6},{8,9},{9,8},{10,11... | collective-permute-start | bytes 196616 | tf_op jit(solution)/shard_map/ppermute | solution.py:146
  43.9 9.9 %collective-permute-start.14 = (bf16[4,256,256]{2,1,0:T(8,128)(2,1)S(1)}, bf16[4,256,256]{2,1,0:T(8,128)(2,1)S(1)}, u32[]{:S(2)}, u32[]{:S(2)}) collective-permute-start(bf16[4,256,256]{2,1,0:T(8,128)(2,1)S(1)} %get-tuple-element.91.refs_4_), channel_id=1, source_target_pairs={{0,1},{1,0},{2,3},{3,2},{4,5},{5,4},{6,7},{7,6},{8,9},{9,8},{10,11... | collective-permute-start | bytes 1572872 | tf_op jit(solution)/shard_map/ppermute | solution.py:146
  44.0 9.8 %all-to-all-start = ((f32[16,1,128]{2,1,0:T(1,128)}), f32[16,1,128]{2,1,0:T(1,128)S(1)}, u32[]{:S(2)}, u32[]{:S(2)}) async-start(f32[16,1,128]{2,1,0:T(1,128)} %get-tuple-element.90), calls=%async_computation | async-start | bytes 16384 | tf_op jit(solution)/shard_map/all_to_all | solution.py:648
  47.5 21.2 %collective-permute-start.15 = (bf16[2,4,64,256]{3,2,1,0:T(8,128)(2,1)S(1)}, bf16[2,4,64,256]{3,2,1,0:T(8,128)(2,1)S(1)}, u32[]{:S(2)}, u32[]{:S(2)}) collective-permute-start(bf16[2,4,64,256]{3,2,1,0:T(8,128)(2,1)S(1)} %get-tuple-element.98), channel_id=1, source_target_pairs={{0,2},{1,3},{2,0},{3,1},{4,6},{5,7},{6,4},{7,5},{8,10},{9,11},{10,... | collective-permute-start | bytes 786440 | tf_op jit(solution)/shard_map/ppermute | solution.py:146
  58.6 19.9 %collective-permute-start.18 = (bf16[2,4,64,256]{3,2,1,0:T(8,128)(2,1)S(1)}, bf16[2,4,64,256]{3,2,1,0:T(8,128)(2,1)S(1)}, u32[]{:S(2)}, u32[]{:S(2)}) collective-permute-start(bf16[2,4,64,256]{3,2,1,0:T(8,128)(2,1)S(1)} %get-tuple-element.105), channel_id=1, source_target_pairs={{0,2},{1,3},{2,0},{3,1},{4,6},{5,7},{6,4},{7,5},{8,10},{9,11},{10,... | collective-permute-start | bytes 786440 | tf_op jit(solution)/shard_map/ppermute | solution.py:146
  59.2 9.5 %collective-permute-start.16 = (bf16[1,4,64,256]{3,2,1,0:T(8,128)(2,1)S(1)}, bf16[1,4,64,256]{3,2,1,0:T(8,128)(2,1)S(1)}, u32[]{:S(2)}, u32[]{:S(2)}) collective-permute-start(bf16[1,4,64,256]{3,2,1,0:T(8,128)(2,1)S(1)} %get-tuple-element.99), channel_id=1, source_target_pairs={{0,3},{1,2},{2,1},{3,0},{4,7},{5,6},{6,5},{7,4},{8,11},{9,10},{10,... | collective-permute-start | bytes 393224 | tf_op jit(solution)/shard_map/ppermute | solution.py:146
  59.8 18.7 %collective-permute-start.17 = (bf16[1,4,64,256]{3,2,1,0:T(8,128)(2,1)S(1)}, bf16[1,4,64,256]{3,2,1,0:T(8,128)(2,1)S(1)}, u32[]{:S(2)}, u32[]{:S(2)}) collective-permute-start(bf16[1,4,64,256]{3,2,1,0:T(8,128)(2,1)S(1)} %get-tuple-element.104), channel_id=1, source_target_pairs={{0,1},{1,0},{2,3},{3,2},{4,5},{5,4},{6,7},{7,6},{8,9},{9,8},{10,11... | collective-permute-start | bytes 393224 | tf_op jit(solution)/shard_map/ppermute | solution.py:146
  60.8 17.7 %collective-permute-start.19 = (bf16[1,4,64,256]{3,2,1,0:T(8,128)(2,1)S(1)}, bf16[1,4,64,256]{3,2,1,0:T(8,128)(2,1)S(1)}, u32[]{:S(2)}, u32[]{:S(2)}) collective-permute-start(bf16[1,4,64,256]{3,2,1,0:T(8,128)(2,1)S(1)} %get-tuple-element.106), channel_id=1, source_target_pairs={{0,3},{1,2},{2,1},{3,0},{4,7},{5,6},{6,5},{7,4},{8,11},{9,10},{10,... | collective-permute-start | bytes 393224 | tf_op jit(solution)/shard_map/ppermute | solution.py:146

commit v21 on v20

--- a/solution.py
+++ b/solution.py
@@ -381,8 +381,7 @@
     left, refs = take(refs, [n_pair] * n_late)
     (right,), refs = take(refs, [n_pair])
     psi, refs = take(refs, counts)
-    raw_in, inter_in, diag, right_diag, part_out, raw_out, left_out, dots_out = refs[:8]
-    sends, (inter, sems) = refs[8:-2], refs[-2:]
+    raw_in, inter_in, diag, right_diag, part_out, raw_out, left_out, dots_out, inter, sems = refs
     copies = keep(left, left_out, sems)
     for j, (given, own) in enumerate(((inter_in, inter), (raw_in, raw_out))):
         copies.append(
@@ -408,25 +407,34 @@
                 image = image + diagonal(diag, right_diag, d, h) * raw
                 sums[0] = sums[0] + fold(raw * raw)
             sums[1] = sums[1] + fold(raw * image)
-        for e, send in enumerate(sends, 2):
-            send_rows(e, send, d, raw_out, part_out)
 
     sum_terms(src, widths, inter, right, part_out, emit)
     spread([whole(x) for x in sums], dots_out)
 
 
-def send_rows(e, send, d, field, part):
+def send_rows(e, send, d, *refs):
     _, own_op = place_of()
     step = send.shape[2]
     rows = pl.ds(pl.multiple_of((own_op ^ e) * step, step), step)
-    if e % 2 == 0:
-        send[0, d] = field[d, rows].astype(send.dtype)
-    send[send.shape[0] - 1, d] = part[d, rows]
+    for j, ref in enumerate(refs):
+        send[j, d] = ref[d, rows].astype(send.dtype)
 
 
 def total_of(mine, other, d, h, cols):
     own = mine[d, :, h * cols : (h + 1) * cols].astype(jnp.float32)
     return own + other[d, :, (1 - h) * cols : (2 - h) * cols].astype(jnp.float32)
+
+
+def sigma_body(mine, other, raw_in, diag, right_diag, sig_out, *sends):
+    n_blk, _, cols = diag.shape
+    for d in range(n_blk):
+        for h in range(2):
+            part = slice(h * cols, (h + 1) * cols)
+            raw = raw_in[d, :, part].astype(jnp.float32)
+            sigma = total_of(mine, other, d, h, cols) + diagonal(diag, right_diag, d, h) * raw
+            sig_out[d, :, part] = sigma
+        for e, send in enumerate(sends, 1):
+            send_rows(2 * e, send, d, raw_in, sig_out)
 
 
 def norm_theta(parts, count):
@@ -437,8 +445,8 @@
 
 def second_body(n_blk, n_pair, count, src, widths, left_early, left_late, *refs):
     right, refs = refs[:n_pair], refs[n_pair:]
-    parts, raw_in, part_in, other_in, diag, right_diag, dots_out, own_out = refs[:8]
-    sends, (inter, corr, sig, fld, part_out, held, sems) = refs[8:-7], refs[-7:]
+    parts, raw_in, sig, diag, right_diag, dots_out, own_out = refs[:7]
+    sends, (inter, corr, fld, part_out, held, sems) = refs[7:-6], refs[-6:]
     copies = []
     n_early = left_early.shape[0]
     for d in range(n_blk):
@@ -454,9 +462,7 @@
         vv = vc = vs = jnp.zeros((8, cols), jnp.float32)
         for d in range(n_blk):
             vec = raw_in[d, :, part].astype(jnp.float32) * scale
-            sigma = total_of(part_in, other_in, d, h, cols)
-            sigma = (sigma + diagonal(diag, right_diag, d, h) * raw_in[d, :, part].astype(jnp.float32)) * scale
-            sig[d, :, part] = sigma
+            sigma = sig[d, :, part] * scale
             den = diagonal(diag, right_diag, d, h) - theta
             item = (sigma - theta * vec) * den / jnp.maximum(den * den, 0.25)
             corr[d, :, part] = item
@@ -481,16 +487,16 @@
         for h in range(2):
             part = slice(h * cols, (h + 1) * cols)
             field = fld[d, :, part].astype(jnp.float32)
-            vec = raw_in[d, :, part].astype(jnp.float32) * scale
+            raw = raw_in[d, :, part].astype(jnp.float32)
             image = total[:, part]
             if h == 0:
                 image = image + diagonal(diag, right_diag, d, h) * field
-                for j, prod in enumerate((field * field, vec * field, field * sig[d, :, part])):
+                for j, prod in enumerate((field * field, raw * field, field * sig[d, :, part])):
                     sums[j] = sums[j] + fold(prod)
-            sums[3] = sums[3] + fold(vec * image)
+            sums[3] = sums[3] + fold(raw * image)
             sums[4] = sums[4] + fold(field * image)
         for e, send in enumerate(sends, 1):
-            send_rows(e, send, d, fld, part_out)
+            send_rows(e, send, d, *((part_out,) if e % 2 else (fld, part_out)))
         rows = pl.ds(pl.multiple_of(own_op * step, step), step)
         for j, ref in enumerate((raw_in, sig, fld, part_out)):
             own_out[j, d] = ref[d, rows].astype(own_out.dtype)
@@ -499,7 +505,8 @@
     step = own_out.shape[2]
     sum_terms(src, widths, inter, right, part_out, emit)
     vv, vc, vs = halves[0]
-    spread([vv, vc] + [whole(x) for x in [vs] + sums], dots_out)
+    ff, vf, fs, vt, ft = (whole(x) for x in sums)
+    spread([vv, vc, whole(vs), ff, vf * scale, fs * scale, vt * scale, ft], dots_out)
 
 
 def ritz_pair(theta, h_mix, h_two):
@@ -518,8 +525,9 @@
 
 
 def third_body(n_blk, n_op, count, slots, parts1, parts2, diag, right_diag, own, *refs):
-    got1, got2 = refs[: n_op - 2], refs[n_op - 2 : 2 * n_op - 3]
-    new_out, res_out, energy_out = refs[2 * n_op - 3 :]
+    n_far = n_op // 2 - 1
+    got1, got2 = refs[:n_far], refs[n_far : n_far + n_op - 1]
+    new_out, res_out, energy_out = refs[n_far + n_op - 1 :]
     step, cols = new_out.shape[1], new_out.shape[2] // n_op
     own_blk, own_op = place_of()
     scale, theta = norm_theta(parts1[...], count)
@@ -553,17 +561,12 @@
             part, crossed = slice(h * cols, (h + 1) * cols), slice((1 - h) * cols, (2 - h) * cols)
             for d in range(n_blk):
                 dmat = diag[d, mine] + right_diag[:, pl.ds(at, cols)]
+                blocks = [own.at[j] for j in range(4)]
                 if e:
-                    raw, fld = got1[e - 2][0, d, :, part], got2[e - 1][0, d, :, part]
-                    vec = raw.astype(jnp.float32) * scale
-                    sigma = got1[e - 2][1, d, :, part].astype(jnp.float32)
-                    sigma = sigma + got1[e - 1][0, d, :, crossed].astype(jnp.float32)
-                    sigma = sigma * scale + dmat * vec
-                    image = got2[e - 1][1, d, :, part].astype(jnp.float32)
-                else:
-                    raw, sigma, fld, image = (own[j, d, :, part].astype(jnp.float32) for j in range(4))
-                    vec = raw * scale
-                fld = fld.astype(jnp.float32)
+                    far, near = got1[e // 2 - 1], got2[e - 1]
+                    blocks = far.at[0], far.at[1], near.at[0], near.at[1]
+                raw, sigma, fld, image = (x[d, :, part].astype(jnp.float32) for x in blocks)
+                vec, sigma = raw * scale, sigma * scale
                 image = image + got2[e][0, d, :, crossed].astype(jnp.float32) + dmat * fld
                 newvec = on_vec * vec + cu * fld
                 res = on_vec * sigma + cu * image - energy * newvec
@@ -639,6 +642,7 @@
     tables = [(src, SMEM), (widths, SMEM)]
     narrow = ((n_blk, rows, 2 * cols), bf16, VMEM)
     dots = ((n_dev, 1, LANES), f32, VMEM)
+    wide = ((n_blk, rows, 2 * cols), f32, VMEM)
     sends = [((2 - e % 2, n_blk, step, 2 * cols), bf16, VMEM) for e in range(1, n_op)]
     inter = pltpu.VMEM((n_blk + 1, n_pair * terms, rows, 2 * cols), bf16)
     left_late = (n_late, n_pair, terms, rows, rows)
@@ -647,23 +651,28 @@
     def totals(parts):
         return lax.all_to_all(parts, ("blk", "op"), 0, 0, tiled=True)
 
-    part1, raw, kept, dots1, *out1 = kernel(
+    part1, raw, kept, dots1 = kernel(
         functools.partial(first_body, n_blk, n_pair, counts),
         tables + left_ins + right_ins + psi_ins + [(raw_early, VMEM), (inter_early, VMEM)] + diags,
-        [narrow, narrow, (left_late, bf16, HBM), dots] + sends[1:],
+        [narrow, narrow, (left_late, bf16, HBM), dots],
         [inter, pltpu.SemaphoreType.DMA((n_late * n_pair + 2,))],
         **cost,
     )
-    parts1, other1 = lax.optimization_barrier((totals(dots1), swap(part1, 1, n_op)))
-    got1 = [swap(block, e, n_op) for e, block in enumerate(out1, 2)]
+    parts1 = totals(dots1)
+    sig, *out1 = kernel(
+        sigma_body,
+        [(x, VMEM) for x in (part1, swap(part1, 1, n_op), raw)] + diags,
+        [wide] + sends[1::2],
+        nbytes=4 << 20,
+    )
+    got1 = [swap(block, 2 * e, n_op) for e, block in enumerate(out1, 1)]
     dots2, own, *out2 = kernel(
         functools.partial(second_body, n_blk, n_pair, count),
         tables + [(left_early, HBM), (kept, HBM)] + right_ins
-        + [(x, VMEM) for x in (parts1, raw, part1, other1)] + diags,
+        + [(x, VMEM) for x in (parts1, raw, sig)] + diags,
         [dots, ((4, n_blk, step, 2 * cols), bf16, VMEM)] + sends,
         [
             inter,
-            pltpu.VMEM((n_blk, rows, 2 * cols), f32),
             pltpu.VMEM((n_blk, rows, 2 * cols), f32),
             pltpu.VMEM((n_blk, rows, 2 * cols), bf16),
             pltpu.VMEM((n_blk, rows, 2 * cols), bf16),
@@ -673,7 +682,7 @@
         flops=4 * cost["flops"],
         nbytes=24 << 20,
     )
-    dots2, got1 = lax.optimization_barrier((dots2, got1))
+    dots2, out2, got1 = lax.optimization_barrier((dots2, out2, got1))
     parts2 = totals(dots2)
     got2 = [swap(block, e, n_op) for e, block in enumerate(out2, 1)]
     final = ((n_blk, step, n_op * cols), bf16, VMEM)

time: 80.8 us -> 73.7 us (0.912)
  waiting for transfers between devices: 31.8 us -> 23 us
  blocking collectives: 9.83 us -> 11.2 us
    ppermute x14 -> x13, waiting for transfers between devices: 14.1 us -> 6.38 us  [swap(): return lax.ppermute(block, 'op', [(i, i ^ e) for i in range(n_op)])]
    all_to_all x1, blocking collectives: 9.83 us -> 11.2 us  [totals(): return lax.all_to_all(parts, ('blk', 'op'), 0, 0, tiled=True)]
    all_to_all x1, waiting for transfers between devices: 4.41 us -> 3.36 us  [totals(): return lax.all_to_all(parts, ('blk', 'op'), 0, 0, tiled=True)]
    pallas_call x6 -> x7, Pallas kernels: 14.8 us -> 15.2 us  [kernel(): pl.pallas_call(body, out_shape=[HBM(shape, dtype) if space == HBM else ja...]
    ppermute x14 -> x13, starting transfers between devices: 8.39 us -> 8.28 us  [swap(): return lax.ppermute(block, 'op', [(i, i ^ e) for i in range(n_op)])]
  transfers between devices with their start and end apart: 21 -> 20, of which waited for: 9 -> 8; matrix products, arithmetic and copies ran while one was open for 0% -> 0% of each run, Pallas kernels for 12% -> 14%
where the time goes in v21:
time: 73.7 us; the launch traced here: 73.4 us
  starting transfers between devices  23 us (31%)
  waiting for transfers between devices  23 us (31%)
  Pallas kernels  15.2 us (21%)
  blocking collectives  11.2 us (15%)
  between operations  0.75 us (1%)
    pallas_call x7, Pallas kernels, kernel(): pl.pallas_call(body, out_shape=[HBM(shape, dtype) if space == HBM else ja...  15.2 us
    ppermute x6, waiting for transfers between devices, onward(): return lax.ppermute(block, 'blk', pairs)  13.3 us
    ppermute x6, starting transfers between devices, onward(): return lax.ppermute(block, 'blk', pairs)  11.2 us
    all_to_all x1, blocking collectives, totals(): return lax.all_to_all(parts, ('blk', 'op'), 0, 0, tiled=True)  11.2 us
    ppermute x13, starting transfers between devices, swap(): return lax.ppermute(block, 'op', [(i, i ^ e) for i in range(n_op)])  8.28 us
    ppermute x13, waiting for transfers between devices, swap(): return lax.ppermute(block, 'op', [(i, i ^ e) for i in range(n_op)])  6.38 us
    all_to_all x1, starting transfers between devices, totals(): return lax.all_to_all(parts, ('blk', 'op'), 0, 0, tiled=True)  3.48 us
    all_to_all x1, waiting for transfers between devices, totals(): return lax.all_to_all(parts, ('blk', 'op'), 0, 0, tiled=True)  3.36 us
  transfers between devices with their start and end apart: 20, of which 8 were waited for; matrix products, arithmetic and copies ran while one was open for 0% of the time, Pallas kernels for 14%

profile of v21, /device:TPU:0, one launch (start us, length us, event | category | flops | bytes accessed | tf_op | source)
XLA Modules:
  0.0 73.4 jit_solution(6828788353484170498)
XLA Ops:
  0.6 0.0 copy-start.3
  0.6 3.1 %collective-permute-start.1 = (bf16[2,256,256]{2,1,0:T(8,128)(2,1)}, bf16[2,256,256]{2,1,0:T(8,128)(2,1)S(1)}, u32[]{:S(2)}, u32[]{:S(2)}) collective-permute-start(bf16[2,256,256]{2,1,0:T(8,128)(2,1)} %bitcast.2), channel_id=1, source_target_pairs={{0,4},{4,12},{12,8},{8,0},{1,5},{5,13},{13,9},{9,1},{2,6},{6,14},{... | collective-permute-start | bytes 786440 | tf_op jit(solution)/shard_map/ppermute | solution.py:142
  3.7 1.5 %collective-permute-start = (bf16[2,256,256]{2,1,0:T(8,128)(2,1)}, bf16[2,256,256]{2,1,0:T(8,128)(2,1)S(1)}, u32[]{:S(2)}, u32[]{:S(2)}) collective-permute-start(bf16[2,256,256]{2,1,0:T(8,128)(2,1)} %bitcast.3), channel_id=1, source_target_pairs={{0,2},{1,3},{2,0},{3,1},{4,6},{5,7},{6,4},{7,5},{8,10},{9,11},{10,... | collective-permute-start | bytes 786440 | tf_op jit(solution)/shard_map/ppermute | solution.py:146
  5.2 0.0 copy-done.3
  5.2 0.0 collective-permute-start.2
  5.2 1.1 %collective-permute-done.2._ = s32[2]{0:T(128)S(1)} collective-permute-done((s32[2]{0:T(128)S(1)}, s32[2]{0:T(128)S(1)}, u32[]{:S(2)}, u32[]{:S(2)}) %collective-permute-start.2) | collective-permute-done | bytes 40 | tf_op jit(solution)/shard_map/ppermute | solution.py:146
  6.3 0.0 copy-start
  6.3 1.9 %shard_map.103 = (bf16[256,256]{1,0:T(8,128)(2,1)S(1)}, bf16[256,128]{1,0:T(8,128)(2,1)S(1)}, bf16[256,256]{1,0:T(8,128)(2,1)S(1)}, bf16[256,128]{1,0:T(8,128)(2...) custom-call(s32[2]{0:T(128)S(1)} %copy-done.3, s32[2]{0:T(128)S(1)} %collective-permute-done.2._, ...), custom_call_target="tpu_custom_call" | custom-call | bytes 1048576 | tf_op jit(solution)/shard_map/pallas_call | solution.py:113
  8.2 0.0 copy-start.1
  8.3 0.6 collective-permute-start.3
  8.9 4.4 %collective-permute-done.3.refs_1_.refs_5_ = bf16[144,256]{1,0:T(8,128)(2,1)S(1)} collective-permute-done((bf16[144,256]{1,0:T(8,128)(2,1)S(1)}, bf16[144,256]{1,0:T(8,128)(2,1)S(1)}, u32[]{:S(2)}, u32[]{:S(2)}) %collective-permute-start.3) | collective-permute-done | bytes 73760 | tf_op jit(solution)/shard_map/ppermute | solution.py:146
  13.3 0.0 collective-permute-done.1.refs_2_
  13.3 0.0 collective-permute-done.refs_1_
  13.3 0.0 copy-start.2
  13.3 2.6 %collective-permute-start.5 = (bf16[2,256,256]{2,1,0:T(8,128)(2,1)S(1)}, bf16[2,256,256]{2,1,0:T(8,128)(2,1)S(1)}, u32[]{:S(2)}, u32[]{:S(2)}) collective-permute-start(bf16[2,256,256]{2,1,0:T(8,128)(2,1)S(1)} %collective-permute-done.1.refs_2_), channel_id=1, source_target_pairs={{0,4},{4,12},{12,8},{8,0},{1,5},{5,13},{13,9},{9,1},{2,6},{6,14},{... | collective-permute-start | bytes 786440 | tf_op jit(solution)/shard_map/ppermute | solution.py:142
  15.9 1.5 %collective-permute-start.4 = (bf16[2,256,256]{2,1,0:T(8,128)(2,1)S(1)}, bf16[2,256,256]{2,1,0:T(8,128)(2,1)S(1)}, u32[]{:S(2)}, u32[]{:S(2)}) collective-permute-start(bf16[2,256,256]{2,1,0:T(8,128)(2,1)S(1)} %collective-permute-done.1.refs_2_), channel_id=1, source_target_pairs={{0,2},{1,3},{2,0},{3,1},{4,6},{5,7},{6,4},{7,5},{8,10},{9,11},{10,... | collective-permute-start | bytes 786440 | tf_op jit(solution)/shard_map/ppermute | solution.py:146
  17.4 0.0 copy-start.4
  17.4 0.0 copy-start.5
  17.4 0.4 collective-permute-start.6
  17.9 0.0 copy-done.1
  17.9 0.0 copy-done.2
  17.9 0.2 copy-done.4
  18.1 0.0 copy-done.5
  18.1 1.3 %shard_map.104 = (s32[16]{0:T(128)S(1)}, s32[4]{0:T(128)S(1)}, s32[4]{0:T(128)S(1)}, f32[4,256,128]{2,1,0:T(8,128)S(1)}, f32[1,512]{1,0:T(1,128)S(1)}) custom-call(s32[4]{0:T(128)S(1)} %copy-done.4, s32[4]{0:T(128)S(1)} %copy-done.5, f32[4,256]{1,0:T(4,128)S(1)} %copy-done.1, f32[1,512]{1,0:T(1,128)S(1)} %bitcast.5, ...), custom_call_target="tpu_custom_call" | custom-call | tf_op jit(solution)/shard_map/pallas_call | solution.py:113
  19.4 4.0 %collective-permute-done.6.refs_5_ = bf16[256,128]{1,0:T(8,128)(2,1)S(1)} collective-permute-done((bf16[256,128]{1,0:T(8,128)(2,1)S(1)}, bf16[256,128]{1,0:T(8,128)(2,1)S(1)}, u32[]{:S(2)}, u32[]{:S(2)}) %collective-permute-start.6) | collective-permute-done | bytes 65568 | tf_op jit(solution)/shard_map/ppermute | solution.py:142
  23.5 0.0 collective-permute-done.5.refs_0_
  23.5 0.0 collective-permute-done.4.refs_3_
  23.5 1.7 %collective-permute-start.8 = (bf16[2,256,256]{2,1,0:T(8,128)(2,1)S(1)}, bf16[2,256,256]{2,1,0:T(8,128)(2,1)S(1)}, u32[]{:S(2)}, u32[]{:S(2)}) collective-permute-start(bf16[2,256,256]{2,1,0:T(8,128)(2,1)S(1)} %collective-permute-done.5.refs_0_), channel_id=1, source_target_pairs={{0,4},{4,12},{12,8},{8,0},{1,5},{5,13},{13,9},{9,1},{2,6},{6,14},{... | collective-permute-start | bytes 786440 | tf_op jit(solution)/shard_map/ppermute | solution.py:142
  25.2 0.5 collective-permute-start.7
  25.7 1.2 %collective-permute-start.10 = (bf16[256,128]{1,0:T(8,128)(2,1)S(1)}, bf16[256,128]{1,0:T(8,128)(2,1)S(1)}, u32[]{:S(2)}, u32[]{:S(2)}) collective-permute-start(bf16[256,128]{1,0:T(8,128)(2,1)S(1)} %get-tuple-element.71), channel_id=1, source_target_pairs={{0,8},{4,0},{12,4},{8,12},{1,9},{5,1},{13,5},{9,13},{2,10},{6,2},{... | collective-permute-start | bytes 196616 | tf_op jit(solution)/shard_map/ppermute | solution.py:142
  26.9 0.0 collective-permute-start.9
  26.9 5.7 %collective-permute-done.10.refs_7_ = bf16[256,128]{1,0:T(8,128)(2,1)S(1)} collective-permute-done((bf16[256,128]{1,0:T(8,128)(2,1)S(1)}, bf16[256,128]{1,0:T(8,128)(2,1)S(1)}, u32[]{:S(2)}, u32[]{:S(2)}) %collective-permute-start.10) | collective-permute-done | bytes 65568 | tf_op jit(solution)/shard_map/ppermute | solution.py:142
  32.6 0.0 collective-permute-done.9.refs_6_
  32.6 0.1 collective-permute-done.8.refs_2_
  32.7 0.0 collective-permute-done.7.refs_1_
  32.7 0.0 collective-permute-start.11
  32.7 2.2 %collective-permute-start.13 = (bf16[256,256]{1,0:T(8,128)(2,1)S(1)}, bf16[256,256]{1,0:T(8,128)(2,1)S(1)}, u32[]{:S(2)}, u32[]{:S(2)}) collective-permute-start(bf16[256,256]{1,0:T(8,128)(2,1)S(1)} %get-tuple-element.82), channel_id=1, source_target_pairs={{0,12},{4,8},{12,0},{8,4},{1,13},{5,9},{13,1},{9,5},{2,14},{6,10},... | collective-permute-start | bytes 393224 | tf_op jit(solution)/shard_map/ppermute | solution.py:142
  34.9 0.0 collective-permute-start.12
  34.9 0.0 copy-done
  34.9 1.7 %shard_map.105 = (bf16[2,256,256]{2,1,0:T(8,128)(2,1)S(1)}, bf16[2,4,256,256]{3,2,1,0:T(8,128)(2,1)S(1)}, bf16[2,2,2,256,256]{4,3,2,1,0:T(8,128)(2,1)}) custom-call(s32[4]{0:T(128)S(1)} %get-tuple-element.68.widths, bf16[2,256,256]{2,1,0:T(8,128)(2,1)S(1)} %bitcast.4, bf16[2,256,256]{2,1,0:T(8,128)(2,1)S(1)} %collective-permute-done.refs_1_, ...), custom_call_target="tpu_custom_call" | custom-call | flops 268435456 | bytes 4194304 | tf_op jit(solution)/shard_map/pallas_call | solution.py:113
  36.6 3.4 %collective-permute-done.13.refs_6_ = bf16[256,256]{1,0:T(8,128)(2,1)S(1)} collective-permute-done((bf16[256,256]{1,0:T(8,128)(2,1)S(1)}, bf16[256,256]{1,0:T(8,128)(2,1)S(1)}, u32[]{:S(2)}, u32[]{:S(2)}) %collective-permute-start.13) | collective-permute-done | bytes 131104 | tf_op jit(solution)/shard_map/ppermute | solution.py:142
  40.0 0.0 collective-permute-done.12.refs_8_
  40.0 0.8 %collective-permute-done.11.refs_3_ = bf16[2,256,256]{2,1,0:T(8,128)(2,1)S(1)} collective-permute-done((bf16[2,256,256]{2,1,0:T(8,128)(2,1)S(1)}, bf16[2,256,256]{2,1,0:T(8,128)(2,1)S(1)}, u32[]{:S(2)}, u32[]{:S(2)}) %collective-permute-start.11) | collective-permute-done | bytes 262176 | tf_op jit(solution)/shard_map/ppermute | solution.py:146
  40.8 3.0 %shard_map.106 = (bf16[4,256,256]{2,1,0:T(8,128)(2,1)S(1)}, bf16[4,256,256]{2,1,0:T(8,128)(2,1)S(1)}, bf16[2,2,2,256,256]{4,3,2,1,0:T(8,128)(2,1)}, f32[16,1,128]{2,1,0:T(1,128)}) custom-call(s32[16]{0:T(128)S(1)} %get-tuple-element.67.src, s32[4]{0:T(128)S(1)} %get-tuple-element.68.widths, bf16[2,256,256]{2,1,0:T(8,128)(2,1)S(1)} %collective-permute-done.5.refs_0_, ...), custom_call_target="tpu_custom_call" | custom-call | flops 1073741824 | bytes 6291456 | tf_op jit(solution)/shard_map/pallas_call | solution.py:113
  43.9 0.1 collective-permute-start.14
  44.0 3.5 %all-to-all-start = ((f32[16,1,128]{2,1,0:T(1,128)}), f32[16,1,128]{2,1,0:T(1,128)S(1)}, u32[]{:S(2)}, u32[]{:S(2)}) async-start(f32[16,1,128]{2,1,0:T(1,128)} %get-tuple-element.90), calls=%async_computation | async-start | bytes 16384 | tf_op jit(solution)/shard_map/all_to_all | solution.py:652
  47.5 0.0 collective-permute-done.14.other
  47.5 1.0 %shard_map.107 = (f32[4,256,256]{2,1,0:T(8,128)S(1)}, bf16[2,4,64,256]{3,2,1,0:T(8,128)(2,1)}) custom-call(bf16[4,256,256]{2,1,0:T(8,128)(2,1)S(1)} %get-tuple-element.94.mine, bf16[4,256,256]{2,1,0:T(8,128)(2,1)S(1)} %collective-permute-done.14.other, bf16[4,256,256]{2,1,0:T(8,128)(2,1)S(1)} %get-tuple-element.93.raw_in.refs_3_, ...), custom_call_target="tpu_custom_call" | custom-call | bytes 4194304 | tf_op jit(solution)/shard_map/pallas_call | solution.py:113
  48.5 1.9 %collective-permute-start.15 = (bf16[2,4,64,256]{3,2,1,0:T(8,128)(2,1)}, bf16[2,4,64,256]{3,2,1,0:T(8,128)(2,1)S(1)}, u32[]{:S(2)}, u32[]{:S(2)}) collective-permute-start(bf16[2,4,64,256]{3,2,1,0:T(8,128)(2,1)} %get-tuple-element.100), channel_id=1, source_target_pairs={{0,2},{1,3},{2,0},{3,1},{4,6},{5,7},{6,4},{7,5},{8,10},{9,11},{10,... | collective-permute-start | bytes 786440 | tf_op jit(solution)/shard_map/ppermute | solution.py:146
  50.4 3.4 %all-to-all-done.refs_2_.parts1 = f32[16,1,128]{2,1,0:T(1,128)S(1)} async-done(((f32[16,1,128]{2,1,0:T(1,128)}), f32[16,1,128]{2,1,0:T(1,128)S(1)}, u32[]{:S(2)}, u32[]{:S(2)}) %all-to-all-start) | async-done | bytes 8224 | tf_op jit(solution)/shard_map/all_to_all | solution.py:652
  53.8 4.2 %shard_map.108 = (f32[16,1,128]{2,1,0:T(1,128)S(1)}, bf16[4,4,64,256]{3,2,1,0:T(8,128)(2,1)S(1)}, bf16[1,4,64,256]{3,2,1,0:T(8,128)(2,1)S(1)}, bf16[2,4,64,256]{...) custom-call(s32[16]{0:T(128)S(1)} %get-tuple-element.67.src, s32[4]{0:T(128)S(1)} %get-tuple-element.68.widths, ...), custom_call_target="tpu_custom_call" | custom-call | flops 4294967296 | bytes 25165824 | tf_op jit(solution)/shard_map/pallas_call | solution.py:113
  58.0 0.0 collective-permute-done.15.refs_0_
  58.0 1.0 %collective-permute-start.17 = (bf16[2,4,64,256]{3,2,1,0:T(8,128)(2,1)S(1)}, bf16[2,4,64,256]{3,2,1,0:T(8,128)(2,1)S(1)}, u32[]{:S(2)}, u32[]{:S(2)}) collective-permute-start(bf16[2,4,64,256]{3,2,1,0:T(8,128)(2,1)S(1)} %get-tuple-element.105), channel_id=1, source_target_pairs={{0,2},{1,3},{2,0},{3,1},{4,6},{5,7},{6,4},{7,5},{8,10},{9,11},{10,... | collective-permute-start | bytes 786440 | tf_op jit(solution)/shard_map/ppermute | solution.py:146
  59.0 0.0 collective-permute-start.16
  59.0 1.2 %collective-permute-start.18 = (bf16[1,4,64,256]{3,2,1,0:T(8,128)(2,1)S(1)}, bf16[1,4,64,256]{3,2,1,0:T(8,128)(2,1)S(1)}, u32[]{:S(2)}, u32[]{:S(2)}) collective-permute-start(bf16[1,4,64,256]{3,2,1,0:T(8,128)(2,1)S(1)} %get-tuple-element.106), channel_id=1, source_target_pairs={{0,3},{1,2},{2,1},{3,0},{4,7},{5,6},{6,5},{7,4},{8,11},{9,10},{10,... | collective-permute-start | bytes 393224 | tf_op jit(solution)/shard_map/ppermute | solution.py:146
  60.2 11.2 %all_to_all.10.parts2 = f32[16,1,128]{2,1,0:T(1,128)S(1)} all-to-all(f32[16,1,128]{2,1,0:T(1,128)S(1)} %get-tuple-element.101), channel_id=1, replica_groups=mesh['grp'=2,'blk'=4,'op'=4] {'blk','op'}, dimensions={0} | all-to-all | bytes 16384 | tf_op jit(solution)/shard_map/all_to_all | solution.py:652
  71.4 0.0 collective-permute-done.16.refs_1_
  71.4 0.0 collective-permute-done.18.refs_3_
  71.4 0.0 collective-permute-done.17.refs_2_
  71.4 2.0 %shard_map.109 = (bf16[4,64,512]{2,1,0:T(8,128)(2,1)}, bf16[4,64,512]{2,1,0:T(8,128)(2,1)}, f32[1]{0:T(128)}) custom-call(s32[4]{0:T(128)S(1)} %get-tuple-element.66.slots, f32[16,1,128]{2,1,0:T(1,128)S(1)} %all-to-all-done.refs_2_.parts1, f32[16,1,128]{2,1,0:T(1,128)S(1)} %all_to_all.10.parts2, f32[4,256,128]{2,1,0:T(8,128)S(1)} %get-tuple-element.88.refs_11_.diag.refs_5_, ...), custom_call_target="tpu_custom_call" | custom-call | bytes 4194304 | tf_op jit(solution)/shard_map/pallas_call | solution.py:113
Async XLA Ops:
  0.6 4.6 %copy-start.3 = (s32[2]{0:T(128)S(1)}, s32[2]{0:T(128)}, u32[]{:S(2)}) copy-start(s32[2]{0:T(128)} %shift.1) | copy-start | bytes 28
  0.6 12.6 %collective-permute-start.1 = (bf16[2,256,256]{2,1,0:T(8,128)(2,1)}, bf16[2,256,256]{2,1,0:T(8,128)(2,1)S(1)}, u32[]{:S(2)}, u32[]{:S(2)}) collective-permute-start(bf16[2,256,256]{2,1,0:T(8,128)(2,1)} %bitcast.2), channel_id=1, source_target_pairs={{0,4},{4,12},{12,8},{8,0},{1,5},{5,13},{13,9},{9,1},{2,6},{6,14},{... | collective-permute-start | bytes 786440 | tf_op jit(solution)/shard_map/ppermute | solution.py:142
  3.7 9.6 %collective-permute-start = (bf16[2,256,256]{2,1,0:T(8,128)(2,1)}, bf16[2,256,256]{2,1,0:T(8,128)(2,1)S(1)}, u32[]{:S(2)}, u32[]{:S(2)}) collective-permute-start(bf16[2,256,256]{2,1,0:T(8,128)(2,1)} %bitcast.3), channel_id=1, source_target_pairs={{0,2},{1,3},{2,0},{3,1},{4,6},{5,7},{6,4},{7,5},{8,10},{9,11},{10,... | collective-permute-start | bytes 786440 | tf_op jit(solution)/shard_map/ppermute | solution.py:146
  5.2 1.1 %collective-permute-start.2 = (s32[2]{0:T(128)S(1)}, s32[2]{0:T(128)S(1)}, u32[]{:S(2)}, u32[]{:S(2)}) collective-permute-start(s32[2]{0:T(128)S(1)} %copy-done.3), channel_id=1, source_target_pairs={{0,1},{1,0},{2,3},{3,2},{4,5},{5,4},{6,7},{7,6},{8,9},{9,8},{10,11... | collective-permute-start | bytes 32 | tf_op jit(solution)/shard_map/ppermute | solution.py:146
  6.3 28.6 %copy-start = (bf16[2,1,256,256]{3,2,1,0:T(8,128)(2,1)S(1)}, bf16[2,1,256,256]{3,2,1,0:T(8,128)(2,1)}, u32[]{:S(2)}) copy-start(bf16[2,1,256,256]{3,2,1,0:T(8,128)(2,1)} %param.9) | copy-start | bytes 786436
  8.2 9.6 %copy-start.1 = (f32[4,256]{1,0:T(4,128)S(1)}, f32[4,256]{1,0:T(4,128)}, u32[]{:S(2)}) copy-start(f32[4,256]{1,0:T(4,128)} %left_diag.1) | copy-start | bytes 12292
  8.3 5.0 %collective-permute-start.3 = (bf16[144,256]{1,0:T(8,128)(2,1)S(1)}, bf16[144,256]{1,0:T(8,128)(2,1)S(1)}, u32[]{:S(2)}, u32[]{:S(2)}) collective-permute-start(bf16[144,256]{1,0:T(8,128)(2,1)S(1)} %get-tuple-element.56), channel_id=1, source_target_pairs={{0,2},{1,3},{2,0},{3,1},{4,6},{5,7},{6,4},{7,5},{8,10},{9,11},{10,... | collective-permute-start | bytes 221192 | tf_op jit(solution)/shard_map/ppermute | solution.py:146
  13.3 4.6 %copy-start.2 = (f32[512]{0:T(512)S(1)}, f32[512]{0:T(512)}, u32[]{:S(2)}) copy-start(f32[512]{0:T(512)} %param.15) | copy-start | bytes 6148
  13.3 10.2 %collective-permute-start.5 = (bf16[2,256,256]{2,1,0:T(8,128)(2,1)S(1)}, bf16[2,256,256]{2,1,0:T(8,128)(2,1)S(1)}, u32[]{:S(2)}, u32[]{:S(2)}) collective-permute-start(bf16[2,256,256]{2,1,0:T(8,128)(2,1)S(1)} %collective-permute-done.1.refs_2_), channel_id=1, source_target_pairs={{0,4},{4,12},{12,8},{8,0},{1,5},{5,13},{13,9},{9,1},{2,6},{6,14},{... | collective-permute-start | bytes 786440 | tf_op jit(solution)/shard_map/ppermute | solution.py:142
  15.9 7.5 %collective-permute-start.4 = (bf16[2,256,256]{2,1,0:T(8,128)(2,1)S(1)}, bf16[2,256,256]{2,1,0:T(8,128)(2,1)S(1)}, u32[]{:S(2)}, u32[]{:S(2)}) collective-permute-start(bf16[2,256,256]{2,1,0:T(8,128)(2,1)S(1)} %collective-permute-done.1.refs_2_), channel_id=1, source_target_pairs={{0,2},{1,3},{2,0},{3,1},{4,6},{5,7},{6,4},{7,5},{8,10},{9,11},{10,... | collective-permute-start | bytes 786440 | tf_op jit(solution)/shard_map/ppermute | solution.py:146
  17.4 0.7 copy-start.4
  17.4 0.7 copy-start.5
  17.4 6.0 %collective-permute-start.6 = (bf16[256,128]{1,0:T(8,128)(2,1)S(1)}, bf16[256,128]{1,0:T(8,128)(2,1)S(1)}, u32[]{:S(2)}, u32[]{:S(2)}) collective-permute-start(bf16[256,128]{1,0:T(8,128)(2,1)S(1)} %get-tuple-element.58), channel_id=1, source_target_pairs={{0,4},{4,12},{12,8},{8,0},{1,5},{5,13},{13,9},{9,1},{2,6},{6,14},{... | collective-permute-start | bytes 196616 | tf_op jit(solution)/shard_map/ppermute | solution.py:142
  23.5 9.3 %collective-permute-start.8 = (bf16[2,256,256]{2,1,0:T(8,128)(2,1)S(1)}, bf16[2,256,256]{2,1,0:T(8,128)(2,1)S(1)}, u32[]{:S(2)}, u32[]{:S(2)}) collective-permute-start(bf16[2,256,256]{2,1,0:T(8,128)(2,1)S(1)} %collective-permute-done.5.refs_0_), channel_id=1, source_target_pairs={{0,4},{4,12},{12,8},{8,0},{1,5},{5,13},{13,9},{9,1},{2,6},{6,14},{... | collective-permute-start | bytes 786440 | tf_op jit(solution)/shard_map/ppermute | solution.py:142
  25.2 7.6 %collective-permute-start.7 = (bf16[2,256,256]{2,1,0:T(8,128)(2,1)S(1)}, bf16[2,256,256]{2,1,0:T(8,128)(2,1)S(1)}, u32[]{:S(2)}, u32[]{:S(2)}) collective-permute-start(bf16[2,256,256]{2,1,0:T(8,128)(2,1)S(1)} %collective-permute-done.5.refs_0_), channel_id=1, source_target_pairs={{0,2},{1,3},{2,0},{3,1},{4,6},{5,7},{6,4},{7,5},{8,10},{9,11},{10,... | collective-permute-start | bytes 786440 | tf_op jit(solution)/shard_map/ppermute | solution.py:146
  25.7 6.9 %collective-permute-start.10 = (bf16[256,128]{1,0:T(8,128)(2,1)S(1)}, bf16[256,128]{1,0:T(8,128)(2,1)S(1)}, u32[]{:S(2)}, u32[]{:S(2)}) collective-permute-start(bf16[256,128]{1,0:T(8,128)(2,1)S(1)} %get-tuple-element.71), channel_id=1, source_target_pairs={{0,8},{4,0},{12,4},{8,12},{1,9},{5,1},{13,5},{9,13},{2,10},{6,2},{... | collective-permute-start | bytes 196616 | tf_op jit(solution)/shard_map/ppermute | solution.py:142
  26.9 5.7 %collective-permute-start.9 = (bf16[256,128]{1,0:T(8,128)(2,1)S(1)}, bf16[256,128]{1,0:T(8,128)(2,1)S(1)}, u32[]{:S(2)}, u32[]{:S(2)}) collective-permute-start(bf16[256,128]{1,0:T(8,128)(2,1)S(1)} %collective-permute-done.6.refs_5_), channel_id=1, source_target_pairs={{0,1},{1,0},{2,3},{3,2},{4,5},{5,4},{6,7},{7,6},{8,9},{9,8},{10,11... | collective-permute-start | bytes 196616 | tf_op jit(solution)/shard_map/ppermute | solution.py:146
  32.7 8.1 %collective-permute-start.11 = (bf16[2,256,256]{2,1,0:T(8,128)(2,1)S(1)}, bf16[2,256,256]{2,1,0:T(8,128)(2,1)S(1)}, u32[]{:S(2)}, u32[]{:S(2)}) collective-permute-start(bf16[2,256,256]{2,1,0:T(8,128)(2,1)S(1)} %collective-permute-done.8.refs_2_), channel_id=1, source_target_pairs={{0,2},{1,3},{2,0},{3,1},{4,6},{5,7},{6,4},{7,5},{8,10},{9,11},{10,... | collective-permute-start | bytes 786440 | tf_op jit(solution)/shard_map/ppermute | solution.py:146
  32.7 7.3 %collective-permute-start.13 = (bf16[256,256]{1,0:T(8,128)(2,1)S(1)}, bf16[256,256]{1,0:T(8,128)(2,1)S(1)}, u32[]{:S(2)}, u32[]{:S(2)}) collective-permute-start(bf16[256,256]{1,0:T(8,128)(2,1)S(1)} %get-tuple-element.82), channel_id=1, source_target_pairs={{0,12},{4,8},{12,0},{8,4},{1,13},{5,9},{13,1},{9,5},{2,14},{6,10},... | collective-permute-start | bytes 393224 | tf_op jit(solution)/shard_map/ppermute | solution.py:142
  34.9 5.1 %collective-permute-start.12 = (bf16[256,128]{1,0:T(8,128)(2,1)S(1)}, bf16[256,128]{1,0:T(8,128)(2,1)S(1)}, u32[]{:S(2)}, u32[]{:S(2)}) collective-permute-start(bf16[256,128]{1,0:T(8,128)(2,1)S(1)} %collective-permute-done.10.refs_7_), channel_id=1, source_target_pairs={{0,1},{1,0},{2,3},{3,2},{4,5},{5,4},{6,7},{7,6},{8,9},{9,8},{10,11... | collective-permute-start | bytes 196616 | tf_op jit(solution)/shard_map/ppermute | solution.py:146
  43.9 3.6 %collective-permute-start.14 = (bf16[4,256,256]{2,1,0:T(8,128)(2,1)S(1)}, bf16[4,256,256]{2,1,0:T(8,128)(2,1)S(1)}, u32[]{:S(2)}, u32[]{:S(2)}) collective-permute-start(bf16[4,256,256]{2,1,0:T(8,128)(2,1)S(1)} %get-tuple-element.94.mine), channel_id=1, source_target_pairs={{0,1},{1,0},{2,3},{3,2},{4,5},{5,4},{6,7},{7,6},{8,9},{9,8},{10,11... | collective-permute-start | bytes 1572872 | tf_op jit(solution)/shard_map/ppermute | solution.py:146
  44.0 9.8 %all-to-all-start = ((f32[16,1,128]{2,1,0:T(1,128)}), f32[16,1,128]{2,1,0:T(1,128)S(1)}, u32[]{:S(2)}, u32[]{:S(2)}) async-start(f32[16,1,128]{2,1,0:T(1,128)} %get-tuple-element.90), calls=%async_computation | async-start | bytes 16384 | tf_op jit(solution)/shard_map/all_to_all | solution.py:652
  48.5 9.5 %collective-permute-start.15 = (bf16[2,4,64,256]{3,2,1,0:T(8,128)(2,1)}, bf16[2,4,64,256]{3,2,1,0:T(8,128)(2,1)S(1)}, u32[]{:S(2)}, u32[]{:S(2)}) collective-permute-start(bf16[2,4,64,256]{3,2,1,0:T(8,128)(2,1)} %get-tuple-element.100), channel_id=1, source_target_pairs={{0,2},{1,3},{2,0},{3,1},{4,6},{5,7},{6,4},{7,5},{8,10},{9,11},{10,... | collective-permute-start | bytes 786440 | tf_op jit(solution)/shard_map/ppermute | solution.py:146
  58.0 13.4 %collective-permute-start.17 = (bf16[2,4,64,256]{3,2,1,0:T(8,128)(2,1)S(1)}, bf16[2,4,64,256]{3,2,1,0:T(8,128)(2,1)S(1)}, u32[]{:S(2)}, u32[]{:S(2)}) collective-permute-start(bf16[2,4,64,256]{3,2,1,0:T(8,128)(2,1)S(1)} %get-tuple-element.105), channel_id=1, source_target_pairs={{0,2},{1,3},{2,0},{3,1},{4,6},{5,7},{6,4},{7,5},{8,10},{9,11},{10,... | collective-permute-start | bytes 786440 | tf_op jit(solution)/shard_map/ppermute | solution.py:146
  59.0 12.4 %collective-permute-start.16 = (bf16[1,4,64,256]{3,2,1,0:T(8,128)(2,1)S(1)}, bf16[1,4,64,256]{3,2,1,0:T(8,128)(2,1)S(1)}, u32[]{:S(2)}, u32[]{:S(2)}) collective-permute-start(bf16[1,4,64,256]{3,2,1,0:T(8,128)(2,1)S(1)} %get-tuple-element.104), channel_id=1, source_target_pairs={{0,1},{1,0},{2,3},{3,2},{4,5},{5,4},{6,7},{7,6},{8,9},{9,8},{10,11... | collective-permute-start | bytes 393224 | tf_op jit(solution)/shard_map/ppermute | solution.py:146
  59.0 12.4 %collective-permute-start.18 = (bf16[1,4,64,256]{3,2,1,0:T(8,128)(2,1)S(1)}, bf16[1,4,64,256]{3,2,1,0:T(8,128)(2,1)S(1)}, u32[]{:S(2)}, u32[]{:S(2)}) collective-permute-start(bf16[1,4,64,256]{3,2,1,0:T(8,128)(2,1)S(1)} %get-tuple-element.106), channel_id=1, source_target_pairs={{0,3},{1,2},{2,1},{3,0},{4,7},{5,6},{6,5},{7,4},{8,11},{9,10},{10,... | collective-permute-start | bytes 393224 | tf_op jit(solution)/shard_map/ppermute | solution.py:146

commit v22 on v21

--- a/solution.py
+++ b/solution.py
@@ -682,9 +682,9 @@
         flops=4 * cost["flops"],
         nbytes=24 << 20,
     )
-    dots2, out2, got1 = lax.optimization_barrier((dots2, out2, got1))
+    near, got1 = lax.optimization_barrier((out2[0], got1))
     parts2 = totals(dots2)
-    got2 = [swap(block, e, n_op) for e, block in enumerate(out2, 1)]
+    got2 = [swap(near, 1, n_op)] + [swap(block, e, n_op) for e, block in enumerate(out2[1:], 2)]
     final = ((n_blk, step, n_op * cols), bf16, VMEM)
     new, res, energy = kernel(
         functools.partial(third_body, n_blk, n_op, count),

time: 73.7 us -> 72.2 us (0.980)
  blocking collectives: 11.2 us -> 9.72 us
    all_to_all x1, blocking collectives: 11.2 us -> 9.72 us  [totals(): return lax.all_to_all(parts, ('blk', 'op'), 0, 0, tiled=True)]
where the time goes in v22:
time: 72.2 us; the launch traced here: 71.9 us
  starting transfers between devices  23 us (32%)
  waiting for transfers between devices  23 us (32%)
  Pallas kernels  15.2 us (21%)
  blocking collectives  9.72 us (13%)
  between operations  0.74 us (1%)
    pallas_call x7, Pallas kernels, kernel(): pl.pallas_call(body, out_shape=[HBM(shape, dtype) if space == HBM else ja...  15.2 us
    ppermute x6, waiting for transfers between devices, onward(): return lax.ppermute(block, 'blk', pairs)  13.3 us
    ppermute x6, starting transfers between devices, onward(): return lax.ppermute(block, 'blk', pairs)  11.2 us
    all_to_all x1, blocking collectives, totals(): return lax.all_to_all(parts, ('blk', 'op'), 0, 0, tiled=True)  9.72 us
    ppermute x13, starting transfers between devices, swap(): return lax.ppermute(block, 'op', [(i, i ^ e) for i in range(n_op)])  8.28 us
    ppermute x13, waiting for transfers between devices, swap(): return lax.ppermute(block, 'op', [(i, i ^ e) for i in range(n_op)])  6.38 us
    all_to_all x1, starting transfers between devices, totals(): return lax.all_to_all(parts, ('blk', 'op'), 0, 0, tiled=True)  3.48 us
    all_to_all x1, waiting for transfers between devices, totals(): return lax.all_to_all(parts, ('blk', 'op'), 0, 0, tiled=True)  3.36 us
  transfers between devices with their start and end apart: 20, of which 8 were waited for; matrix products, arithmetic and copies ran while one was open for 0% of the time, Pallas kernels for 14%

profile of v22, /device:TPU:0, one launch (start us, length us, event | category | flops | bytes accessed | tf_op | source)
XLA Modules:
  0.0 71.9 jit_solution(18278137559612943139)
XLA Ops:
  0.6 0.0 copy-start.3
  0.6 3.1 %collective-permute-start.1 = (bf16[2,256,256]{2,1,0:T(8,128)(2,1)}, bf16[2,256,256]{2,1,0:T(8,128)(2,1)S(1)}, u32[]{:S(2)}, u32[]{:S(2)}) collective-permute-start(bf16[2,256,256]{2,1,0:T(8,128)(2,1)} %bitcast.2), channel_id=1, source_target_pairs={{0,4},{4,12},{12,8},{8,0},{1,5},{5,13},{13,9},{9,1},{2,6},{6,14},{... | collective-permute-start | bytes 786440 | tf_op jit(solution)/shard_map/ppermute | solution.py:142
  3.7 1.5 %collective-permute-start = (bf16[2,256,256]{2,1,0:T(8,128)(2,1)}, bf16[2,256,256]{2,1,0:T(8,128)(2,1)S(1)}, u32[]{:S(2)}, u32[]{:S(2)}) collective-permute-start(bf16[2,256,256]{2,1,0:T(8,128)(2,1)} %bitcast.3), channel_id=1, source_target_pairs={{0,2},{1,3},{2,0},{3,1},{4,6},{5,7},{6,4},{7,5},{8,10},{9,11},{10,... | collective-permute-start | bytes 786440 | tf_op jit(solution)/shard_map/ppermute | solution.py:146
  5.2 0.0 copy-done.3
  5.2 0.0 collective-permute-start.2
  5.2 1.1 %collective-permute-done.2._ = s32[2]{0:T(128)S(1)} collective-permute-done((s32[2]{0:T(128)S(1)}, s32[2]{0:T(128)S(1)}, u32[]{:S(2)}, u32[]{:S(2)}) %collective-permute-start.2) | collective-permute-done | bytes 40 | tf_op jit(solution)/shard_map/ppermute | solution.py:146
  6.3 0.0 copy-start
  6.3 1.9 %shard_map.103 = (bf16[256,256]{1,0:T(8,128)(2,1)S(1)}, bf16[256,128]{1,0:T(8,128)(2,1)S(1)}, bf16[256,256]{1,0:T(8,128)(2,1)S(1)}, bf16[256,128]{1,0:T(8,128)(2...) custom-call(s32[2]{0:T(128)S(1)} %copy-done.3, s32[2]{0:T(128)S(1)} %collective-permute-done.2._, ...), custom_call_target="tpu_custom_call" | custom-call | bytes 1048576 | tf_op jit(solution)/shard_map/pallas_call | solution.py:113
  8.2 0.0 copy-start.1
  8.3 0.6 collective-permute-start.3
  8.9 4.4 %collective-permute-done.3.refs_1_.refs_5_ = bf16[144,256]{1,0:T(8,128)(2,1)S(1)} collective-permute-done((bf16[144,256]{1,0:T(8,128)(2,1)S(1)}, bf16[144,256]{1,0:T(8,128)(2,1)S(1)}, u32[]{:S(2)}, u32[]{:S(2)}) %collective-permute-start.3) | collective-permute-done | bytes 73760 | tf_op jit(solution)/shard_map/ppermute | solution.py:146
  13.3 0.0 collective-permute-done.1.refs_2_
  13.3 0.0 collective-permute-done.refs_1_
  13.3 0.0 copy-start.2
  13.3 2.6 %collective-permute-start.5 = (bf16[2,256,256]{2,1,0:T(8,128)(2,1)S(1)}, bf16[2,256,256]{2,1,0:T(8,128)(2,1)S(1)}, u32[]{:S(2)}, u32[]{:S(2)}) collective-permute-start(bf16[2,256,256]{2,1,0:T(8,128)(2,1)S(1)} %collective-permute-done.1.refs_2_), channel_id=1, source_target_pairs={{0,4},{4,12},{12,8},{8,0},{1,5},{5,13},{13,9},{9,1},{2,6},{6,14},{... | collective-permute-start | bytes 786440 | tf_op jit(solution)/shard_map/ppermute | solution.py:142
  15.9 1.5 %collective-permute-start.4 = (bf16[2,256,256]{2,1,0:T(8,128)(2,1)S(1)}, bf16[2,256,256]{2,1,0:T(8,128)(2,1)S(1)}, u32[]{:S(2)}, u32[]{:S(2)}) collective-permute-start(bf16[2,256,256]{2,1,0:T(8,128)(2,1)S(1)} %collective-permute-done.1.refs_2_), channel_id=1, source_target_pairs={{0,2},{1,3},{2,0},{3,1},{4,6},{5,7},{6,4},{7,5},{8,10},{9,11},{10,... | collective-permute-start | bytes 786440 | tf_op jit(solution)/shard_map/ppermute | solution.py:146
  17.4 0.0 copy-start.4
  17.4 0.0 copy-start.5
  17.4 0.4 collective-permute-start.6
  17.9 0.0 copy-done.1
  17.9 0.0 copy-done.2
  17.9 0.2 copy-done.4
  18.1 0.0 copy-done.5
  18.1 1.3 %shard_map.104 = (s32[16]{0:T(128)S(1)}, s32[4]{0:T(128)S(1)}, s32[4]{0:T(128)S(1)}, f32[4,256,128]{2,1,0:T(8,128)S(1)}, f32[1,512]{1,0:T(1,128)S(1)}) custom-call(s32[4]{0:T(128)S(1)} %copy-done.4, s32[4]{0:T(128)S(1)} %copy-done.5, f32[4,256]{1,0:T(4,128)S(1)} %copy-done.1, f32[1,512]{1,0:T(1,128)S(1)} %bitcast.5, ...), custom_call_target="tpu_custom_call" | custom-call | tf_op jit(solution)/shard_map/pallas_call | solution.py:113
  19.4 4.0 %collective-permute-done.6.refs_5_ = bf16[256,128]{1,0:T(8,128)(2,1)S(1)} collective-permute-done((bf16[256,128]{1,0:T(8,128)(2,1)S(1)}, bf16[256,128]{1,0:T(8,128)(2,1)S(1)}, u32[]{:S(2)}, u32[]{:S(2)}) %collective-permute-start.6) | collective-permute-done | bytes 65568 | tf_op jit(solution)/shard_map/ppermute | solution.py:142
  23.5 0.0 collective-permute-done.5.refs_0_
  23.5 0.0 collective-permute-done.4.refs_3_
  23.5 1.7 %collective-permute-start.8 = (bf16[2,256,256]{2,1,0:T(8,128)(2,1)S(1)}, bf16[2,256,256]{2,1,0:T(8,128)(2,1)S(1)}, u32[]{:S(2)}, u32[]{:S(2)}) collective-permute-start(bf16[2,256,256]{2,1,0:T(8,128)(2,1)S(1)} %collective-permute-done.5.refs_0_), channel_id=1, source_target_pairs={{0,4},{4,12},{12,8},{8,0},{1,5},{5,13},{13,9},{9,1},{2,6},{6,14},{... | collective-permute-start | bytes 786440 | tf_op jit(solution)/shard_map/ppermute | solution.py:142
  25.2 0.5 collective-permute-start.7
  25.7 1.2 %collective-permute-start.10 = (bf16[256,128]{1,0:T(8,128)(2,1)S(1)}, bf16[256,128]{1,0:T(8,128)(2,1)S(1)}, u32[]{:S(2)}, u32[]{:S(2)}) collective-permute-start(bf16[256,128]{1,0:T(8,128)(2,1)S(1)} %get-tuple-element.68), channel_id=1, source_target_pairs={{0,8},{4,0},{12,4},{8,12},{1,9},{5,1},{13,5},{9,13},{2,10},{6,2},{... | collective-permute-start | bytes 196616 | tf_op jit(solution)/shard_map/ppermute | solution.py:142
  26.9 0.0 collective-permute-start.9
  26.9 5.7 %collective-permute-done.10.refs_7_ = bf16[256,128]{1,0:T(8,128)(2,1)S(1)} collective-permute-done((bf16[256,128]{1,0:T(8,128)(2,1)S(1)}, bf16[256,128]{1,0:T(8,128)(2,1)S(1)}, u32[]{:S(2)}, u32[]{:S(2)}) %collective-permute-start.10) | collective-permute-done | bytes 65568 | tf_op jit(solution)/shard_map/ppermute | solution.py:142
  32.6 0.0 collective-permute-done.9.refs_6_
  32.6 0.1 collective-permute-done.8.refs_2_
  32.7 0.0 collective-permute-done.7.refs_1_
  32.7 0.0 collective-permute-start.11
  32.7 2.2 %collective-permute-start.13 = (bf16[256,256]{1,0:T(8,128)(2,1)S(1)}, bf16[256,256]{1,0:T(8,128)(2,1)S(1)}, u32[]{:S(2)}, u32[]{:S(2)}) collective-permute-start(bf16[256,256]{1,0:T(8,128)(2,1)S(1)} %get-tuple-element.79), channel_id=1, source_target_pairs={{0,12},{4,8},{12,0},{8,4},{1,13},{5,9},{13,1},{9,5},{2,14},{6,10},... | collective-permute-start | bytes 393224 | tf_op jit(solution)/shard_map/ppermute | solution.py:142
  34.9 0.0 collective-permute-start.12
  34.9 0.0 copy-done
  34.9 1.7 %shard_map.105 = (bf16[2,256,256]{2,1,0:T(8,128)(2,1)S(1)}, bf16[2,4,256,256]{3,2,1,0:T(8,128)(2,1)S(1)}, bf16[2,2,2,256,256]{4,3,2,1,0:T(8,128)(2,1)}) custom-call(s32[4]{0:T(128)S(1)} %get-tuple-element.65.widths, bf16[2,256,256]{2,1,0:T(8,128)(2,1)S(1)} %bitcast.4, bf16[2,256,256]{2,1,0:T(8,128)(2,1)S(1)} %collective-permute-done.refs_1_, ...), custom_call_target="tpu_custom_call" | custom-call | flops 268435456 | bytes 4194304 | tf_op jit(solution)/shard_map/pallas_call | solution.py:113
  36.6 3.4 %collective-permute-done.13.refs_6_ = bf16[256,256]{1,0:T(8,128)(2,1)S(1)} collective-permute-done((bf16[256,256]{1,0:T(8,128)(2,1)S(1)}, bf16[256,256]{1,0:T(8,128)(2,1)S(1)}, u32[]{:S(2)}, u32[]{:S(2)}) %collective-permute-start.13) | collective-permute-done | bytes 131104 | tf_op jit(solution)/shard_map/ppermute | solution.py:142
  40.0 0.0 collective-permute-done.12.refs_8_
  40.0 0.8 %collective-permute-done.11.refs_3_ = bf16[2,256,256]{2,1,0:T(8,128)(2,1)S(1)} collective-permute-done((bf16[2,256,256]{2,1,0:T(8,128)(2,1)S(1)}, bf16[2,256,256]{2,1,0:T(8,128)(2,1)S(1)}, u32[]{:S(2)}, u32[]{:S(2)}) %collective-permute-start.11) | collective-permute-done | bytes 262176 | tf_op jit(solution)/shard_map/ppermute | solution.py:146
  40.8 3.0 %shard_map.106 = (bf16[4,256,256]{2,1,0:T(8,128)(2,1)S(1)}, bf16[4,256,256]{2,1,0:T(8,128)(2,1)S(1)}, bf16[2,2,2,256,256]{4,3,2,1,0:T(8,128)(2,1)}, f32[16,1,128]{2,1,0:T(1,128)}) custom-call(s32[16]{0:T(128)S(1)} %get-tuple-element.64.src, s32[4]{0:T(128)S(1)} %get-tuple-element.65.widths, bf16[2,256,256]{2,1,0:T(8,128)(2,1)S(1)} %collective-permute-done.5.refs_0_, ...), custom_call_target="tpu_custom_call" | custom-call | flops 1073741824 | bytes 6291456 | tf_op jit(solution)/shard_map/pallas_call | solution.py:113
  43.9 0.1 collective-permute-start.14
  44.0 3.5 %all-to-all-start = ((f32[16,1,128]{2,1,0:T(1,128)}), f32[16,1,128]{2,1,0:T(1,128)S(1)}, u32[]{:S(2)}, u32[]{:S(2)}) async-start(f32[16,1,128]{2,1,0:T(1,128)} %get-tuple-element.87), calls=%async_computation | async-start | bytes 16384 | tf_op jit(solution)/shard_map/all_to_all | solution.py:652
  47.5 0.0 collective-permute-done.14.other
  47.5 1.0 %shard_map.107 = (f32[4,256,256]{2,1,0:T(8,128)S(1)}, bf16[2,4,64,256]{3,2,1,0:T(8,128)(2,1)}) custom-call(bf16[4,256,256]{2,1,0:T(8,128)(2,1)S(1)} %get-tuple-element.91.mine, bf16[4,256,256]{2,1,0:T(8,128)(2,1)S(1)} %collective-permute-done.14.other, bf16[4,256,256]{2,1,0:T(8,128)(2,1)S(1)} %get-tuple-element.90.raw_in.refs_3_, ...), custom_call_target="tpu_custom_call" | custom-call | bytes 4194304 | tf_op jit(solution)/shard_map/pallas_call | solution.py:113
  48.5 1.9 %collective-permute-start.15 = (bf16[2,4,64,256]{3,2,1,0:T(8,128)(2,1)}, bf16[2,4,64,256]{3,2,1,0:T(8,128)(2,1)S(1)}, u32[]{:S(2)}, u32[]{:S(2)}) collective-permute-start(bf16[2,4,64,256]{3,2,1,0:T(8,128)(2,1)} %get-tuple-element.96), channel_id=1, source_target_pairs={{0,2},{1,3},{2,0},{3,1},{4,6},{5,7},{6,4},{7,5},{8,10},{9,11},{10,... | collective-permute-start | bytes 786440 | tf_op jit(solution)/shard_map/ppermute | solution.py:146
  50.4 3.4 %all-to-all-done.refs_2_.parts1 = f32[16,1,128]{2,1,0:T(1,128)S(1)} async-done(((f32[16,1,128]{2,1,0:T(1,128)}), f32[16,1,128]{2,1,0:T(1,128)S(1)}, u32[]{:S(2)}, u32[]{:S(2)}) %all-to-all-start) | async-done | bytes 8224 | tf_op jit(solution)/shard_map/all_to_all | solution.py:652
  53.8 4.2 %shard_map.108 = (f32[16,1,128]{2,1,0:T(1,128)S(1)}, bf16[4,4,64,256]{3,2,1,0:T(8,128)(2,1)S(1)}, bf16[1,4,64,256]{3,2,1,0:T(8,128)(2,1)S(1)}, bf16[2,4,64,256]{...) custom-call(s32[16]{0:T(128)S(1)} %get-tuple-element.64.src, s32[4]{0:T(128)S(1)} %get-tuple-element.65.widths, ...), custom_call_target="tpu_custom_call" | custom-call | flops 4294967296 | bytes 25165824 | tf_op jit(solution)/shard_map/pallas_call | solution.py:113
  58.0 0.6 collective-permute-start.17
  58.5 0.6 collective-permute-start.18
  59.2 0.0 collective-permute-done.15.refs_0_
  59.2 1.0 %collective-permute-start.16 = (bf16[1,4,64,256]{3,2,1,0:T(8,128)(2,1)S(1)}, bf16[1,4,64,256]{3,2,1,0:T(8,128)(2,1)S(1)}, u32[]{:S(2)}, u32[]{:S(2)}) collective-permute-start(bf16[1,4,64,256]{3,2,1,0:T(8,128)(2,1)S(1)} %get-tuple-element.98), channel_id=1, source_target_pairs={{0,1},{1,0},{2,3},{3,2},{4,5},{5,4},{6,7},{7,6},{8,9},{9,8},{10,11... | collective-permute-start | bytes 393224 | tf_op jit(solution)/shard_map/ppermute | solution.py:146
  60.2 9.7 %all_to_all.10.parts2 = f32[16,1,128]{2,1,0:T(1,128)S(1)} all-to-all(f32[16,1,128]{2,1,0:T(1,128)S(1)} %get-tuple-element.93), channel_id=1, replica_groups=mesh['grp'=2,'blk'=4,'op'=4] {'blk','op'}, dimensions={0} | all-to-all | bytes 16384 | tf_op jit(solution)/shard_map/all_to_all | solution.py:652
  69.9 0.0 collective-permute-done.18.refs_3_
  69.9 0.0 collective-permute-done.17.refs_2_
  69.9 0.0 collective-permute-done.16.refs_1_
  69.9 2.0 %shard_map.109 = (bf16[4,64,512]{2,1,0:T(8,128)(2,1)}, bf16[4,64,512]{2,1,0:T(8,128)(2,1)}, f32[1]{0:T(128)}) custom-call(s32[4]{0:T(128)S(1)} %get-tuple-element.63.slots, f32[16,1,128]{2,1,0:T(1,128)S(1)} %all-to-all-done.refs_2_.parts1, f32[16,1,128]{2,1,0:T(1,128)S(1)} %all_to_all.10.parts2, f32[4,256,128]{2,1,0:T(8,128)S(1)} %get-tuple-element.85.refs_11_.diag.refs_5_, ...), custom_call_target="tpu_custom_call" | custom-call | bytes 4194304 | tf_op jit(solution)/shard_map/pallas_call | solution.py:113
Async XLA Ops:
  0.6 4.6 %copy-start.3 = (s32[2]{0:T(128)S(1)}, s32[2]{0:T(128)}, u32[]{:S(2)}) copy-start(s32[2]{0:T(128)} %shift.1) | copy-start | bytes 28
  0.6 12.6 %collective-permute-start.1 = (bf16[2,256,256]{2,1,0:T(8,128)(2,1)}, bf16[2,256,256]{2,1,0:T(8,128)(2,1)S(1)}, u32[]{:S(2)}, u32[]{:S(2)}) collective-permute-start(bf16[2,256,256]{2,1,0:T(8,128)(2,1)} %bitcast.2), channel_id=1, source_target_pairs={{0,4},{4,12},{12,8},{8,0},{1,5},{5,13},{13,9},{9,1},{2,6},{6,14},{... | collective-permute-start | bytes 786440 | tf_op jit(solution)/shard_map/ppermute | solution.py:142
  3.7 9.6 %collective-permute-start = (bf16[2,256,256]{2,1,0:T(8,128)(2,1)}, bf16[2,256,256]{2,1,0:T(8,128)(2,1)S(1)}, u32[]{:S(2)}, u32[]{:S(2)}) collective-permute-start(bf16[2,256,256]{2,1,0:T(8,128)(2,1)} %bitcast.3), channel_id=1, source_target_pairs={{0,2},{1,3},{2,0},{3,1},{4,6},{5,7},{6,4},{7,5},{8,10},{9,11},{10,... | collective-permute-start | bytes 786440 | tf_op jit(solution)/shard_map/ppermute | solution.py:146
  5.2 1.1 %collective-permute-start.2 = (s32[2]{0:T(128)S(1)}, s32[2]{0:T(128)S(1)}, u32[]{:S(2)}, u32[]{:S(2)}) collective-permute-start(s32[2]{0:T(128)S(1)} %copy-done.3), channel_id=1, source_target_pairs={{0,1},{1,0},{2,3},{3,2},{4,5},{5,4},{6,7},{7,6},{8,9},{9,8},{10,11... | collective-permute-start | bytes 32 | tf_op jit(solution)/shard_map/ppermute | solution.py:146
  6.3 28.6 %copy-start = (bf16[2,1,256,256]{3,2,1,0:T(8,128)(2,1)S(1)}, bf16[2,1,256,256]{3,2,1,0:T(8,128)(2,1)}, u32[]{:S(2)}) copy-start(bf16[2,1,256,256]{3,2,1,0:T(8,128)(2,1)} %param.9) | copy-start | bytes 786436
  8.2 9.6 %copy-start.1 = (f32[4,256]{1,0:T(4,128)S(1)}, f32[4,256]{1,0:T(4,128)}, u32[]{:S(2)}) copy-start(f32[4,256]{1,0:T(4,128)} %left_diag.1) | copy-start | bytes 12292
  8.3 5.0 %collective-permute-start.3 = (bf16[144,256]{1,0:T(8,128)(2,1)S(1)}, bf16[144,256]{1,0:T(8,128)(2,1)S(1)}, u32[]{:S(2)}, u32[]{:S(2)}) collective-permute-start(bf16[144,256]{1,0:T(8,128)(2,1)S(1)} %get-tuple-element.53), channel_id=1, source_target_pairs={{0,2},{1,3},{2,0},{3,1},{4,6},{5,7},{6,4},{7,5},{8,10},{9,11},{10,... | collective-permute-start | bytes 221192 | tf_op jit(solution)/shard_map/ppermute | solution.py:146
  13.3 4.6 %copy-start.2 = (f32[512]{0:T(512)S(1)}, f32[512]{0:T(512)}, u32[]{:S(2)}) copy-start(f32[512]{0:T(512)} %param.15) | copy-start | bytes 6148
  13.3 10.2 %collective-permute-start.5 = (bf16[2,256,256]{2,1,0:T(8,128)(2,1)S(1)}, bf16[2,256,256]{2,1,0:T(8,128)(2,1)S(1)}, u32[]{:S(2)}, u32[]{:S(2)}) collective-permute-start(bf16[2,256,256]{2,1,0:T(8,128)(2,1)S(1)} %collective-permute-done.1.refs_2_), channel_id=1, source_target_pairs={{0,4},{4,12},{12,8},{8,0},{1,5},{5,13},{13,9},{9,1},{2,6},{6,14},{... | collective-permute-start | bytes 786440 | tf_op jit(solution)/shard_map/ppermute | solution.py:142
  15.9 7.5 %collective-permute-start.4 = (bf16[2,256,256]{2,1,0:T(8,128)(2,1)S(1)}, bf16[2,256,256]{2,1,0:T(8,128)(2,1)S(1)}, u32[]{:S(2)}, u32[]{:S(2)}) collective-permute-start(bf16[2,256,256]{2,1,0:T(8,128)(2,1)S(1)} %collective-permute-done.1.refs_2_), channel_id=1, source_target_pairs={{0,2},{1,3},{2,0},{3,1},{4,6},{5,7},{6,4},{7,5},{8,10},{9,11},{10,... | collective-permute-start | bytes 786440 | tf_op jit(solution)/shard_map/ppermute | solution.py:146
  17.4 0.7 copy-start.4
  17.4 0.7 copy-start.5
  17.4 6.0 %collective-permute-start.6 = (bf16[256,128]{1,0:T(8,128)(2,1)S(1)}, bf16[256,128]{1,0:T(8,128)(2,1)S(1)}, u32[]{:S(2)}, u32[]{:S(2)}) collective-permute-start(bf16[256,128]{1,0:T(8,128)(2,1)S(1)} %get-tuple-element.55), channel_id=1, source_target_pairs={{0,4},{4,12},{12,8},{8,0},{1,5},{5,13},{13,9},{9,1},{2,6},{6,14},{... | collective-permute-start | bytes 196616 | tf_op jit(solution)/shard_map/ppermute | solution.py:142
  23.5 9.3 %collective-permute-start.8 = (bf16[2,256,256]{2,1,0:T(8,128)(2,1)S(1)}, bf16[2,256,256]{2,1,0:T(8,128)(2,1)S(1)}, u32[]{:S(2)}, u32[]{:S(2)}) collective-permute-start(bf16[2,256,256]{2,1,0:T(8,128)(2,1)S(1)} %collective-permute-done.5.refs_0_), channel_id=1, source_target_pairs={{0,4},{4,12},{12,8},{8,0},{1,5},{5,13},{13,9},{9,1},{2,6},{6,14},{... | collective-permute-start | bytes 786440 | tf_op jit(solution)/shard_map/ppermute | solution.py:142
  25.2 7.6 %collective-permute-start.7 = (bf16[2,256,256]{2,1,0:T(8,128)(2,1)S(1)}, bf16[2,256,256]{2,1,0:T(8,128)(2,1)S(1)}, u32[]{:S(2)}, u32[]{:S(2)}) collective-permute-start(bf16[2,256,256]{2,1,0:T(8,128)(2,1)S(1)} %collective-permute-done.5.refs_0_), channel_id=1, source_target_pairs={{0,2},{1,3},{2,0},{3,1},{4,6},{5,7},{6,4},{7,5},{8,10},{9,11},{10,... | collective-permute-start | bytes 786440 | tf_op jit(solution)/shard_map/ppermute | solution.py:146
  25.7 6.9 %collective-permute-start.10 = (bf16[256,128]{1,0:T(8,128)(2,1)S(1)}, bf16[256,128]{1,0:T(8,128)(2,1)S(1)}, u32[]{:S(2)}, u32[]{:S(2)}) collective-permute-start(bf16[256,128]{1,0:T(8,128)(2,1)S(1)} %get-tuple-element.68), channel_id=1, source_target_pairs={{0,8},{4,0},{12,4},{8,12},{1,9},{5,1},{13,5},{9,13},{2,10},{6,2},{... | collective-permute-start | bytes 196616 | tf_op jit(solution)/shard_map/ppermute | solution.py:142
  26.9 5.7 %collective-permute-start.9 = (bf16[256,128]{1,0:T(8,128)(2,1)S(1)}, bf16[256,128]{1,0:T(8,128)(2,1)S(1)}, u32[]{:S(2)}, u32[]{:S(2)}) collective-permute-start(bf16[256,128]{1,0:T(8,128)(2,1)S(1)} %collective-permute-done.6.refs_5_), channel_id=1, source_target_pairs={{0,1},{1,0},{2,3},{3,2},{4,5},{5,4},{6,7},{7,6},{8,9},{9,8},{10,11... | collective-permute-start | bytes 196616 | tf_op jit(solution)/shard_map/ppermute | solution.py:146
  32.7 8.1 %collective-permute-start.11 = (bf16[2,256,256]{2,1,0:T(8,128)(2,1)S(1)}, bf16[2,256,256]{2,1,0:T(8,128)(2,1)S(1)}, u32[]{:S(2)}, u32[]{:S(2)}) collective-permute-start(bf16[2,256,256]{2,1,0:T(8,128)(2,1)S(1)} %collective-permute-done.8.refs_2_), channel_id=1, source_target_pairs={{0,2},{1,3},{2,0},{3,1},{4,6},{5,7},{6,4},{7,5},{8,10},{9,11},{10,... | collective-permute-start | bytes 786440 | tf_op jit(solution)/shard_map/ppermute | solution.py:146
  32.7 7.3 %collective-permute-start.13 = (bf16[256,256]{1,0:T(8,128)(2,1)S(1)}, bf16[256,256]{1,0:T(8,128)(2,1)S(1)}, u32[]{:S(2)}, u32[]{:S(2)}) collective-permute-start(bf16[256,256]{1,0:T(8,128)(2,1)S(1)} %get-tuple-element.79), channel_id=1, source_target_pairs={{0,12},{4,8},{12,0},{8,4},{1,13},{5,9},{13,1},{9,5},{2,14},{6,10},... | collective-permute-start | bytes 393224 | tf_op jit(solution)/shard_map/ppermute | solution.py:142
  34.9 5.1 %collective-permute-start.12 = (bf16[256,128]{1,0:T(8,128)(2,1)S(1)}, bf16[256,128]{1,0:T(8,128)(2,1)S(1)}, u32[]{:S(2)}, u32[]{:S(2)}) collective-permute-start(bf16[256,128]{1,0:T(8,128)(2,1)S(1)} %collective-permute-done.10.refs_7_), channel_id=1, source_target_pairs={{0,1},{1,0},{2,3},{3,2},{4,5},{5,4},{6,7},{7,6},{8,9},{9,8},{10,11... | collective-permute-start | bytes 196616 | tf_op jit(solution)/shard_map/ppermute | solution.py:146
  43.9 3.6 %collective-permute-start.14 = (bf16[4,256,256]{2,1,0:T(8,128)(2,1)S(1)}, bf16[4,256,256]{2,1,0:T(8,128)(2,1)S(1)}, u32[]{:S(2)}, u32[]{:S(2)}) collective-permute-start(bf16[4,256,256]{2,1,0:T(8,128)(2,1)S(1)} %get-tuple-element.91.mine), channel_id=1, source_target_pairs={{0,1},{1,0},{2,3},{3,2},{4,5},{5,4},{6,7},{7,6},{8,9},{9,8},{10,11... | collective-permute-start | bytes 1572872 | tf_op jit(solution)/shard_map/ppermute | solution.py:146
  44.0 9.8 %all-to-all-start = ((f32[16,1,128]{2,1,0:T(1,128)}), f32[16,1,128]{2,1,0:T(1,128)S(1)}, u32[]{:S(2)}, u32[]{:S(2)}) async-start(f32[16,1,128]{2,1,0:T(1,128)} %get-tuple-element.87), calls=%async_computation | async-start | bytes 16384 | tf_op jit(solution)/shard_map/all_to_all | solution.py:652
  48.5 10.7 %collective-permute-start.15 = (bf16[2,4,64,256]{3,2,1,0:T(8,128)(2,1)}, bf16[2,4,64,256]{3,2,1,0:T(8,128)(2,1)S(1)}, u32[]{:S(2)}, u32[]{:S(2)}) collective-permute-start(bf16[2,4,64,256]{3,2,1,0:T(8,128)(2,1)} %get-tuple-element.96), channel_id=1, source_target_pairs={{0,2},{1,3},{2,0},{3,1},{4,6},{5,7},{6,4},{7,5},{8,10},{9,11},{10,... | collective-permute-start | bytes 786440 | tf_op jit(solution)/shard_map/ppermute | solution.py:146
  58.0 11.9 %collective-permute-start.17 = (bf16[2,4,64,256]{3,2,1,0:T(8,128)(2,1)S(1)}, bf16[2,4,64,256]{3,2,1,0:T(8,128)(2,1)S(1)}, u32[]{:S(2)}, u32[]{:S(2)}) collective-permute-start(bf16[2,4,64,256]{3,2,1,0:T(8,128)(2,1)S(1)} %get-tuple-element.99), channel_id=1, source_target_pairs={{0,2},{1,3},{2,0},{3,1},{4,6},{5,7},{6,4},{7,5},{8,10},{9,11},{10,... | collective-permute-start | bytes 786440 | tf_op jit(solution)/shard_map/ppermute | solution.py:146
  58.5 11.4 %collective-permute-start.18 = (bf16[1,4,64,256]{3,2,1,0:T(8,128)(2,1)S(1)}, bf16[1,4,64,256]{3,2,1,0:T(8,128)(2,1)S(1)}, u32[]{:S(2)}, u32[]{:S(2)}) collective-permute-start(bf16[1,4,64,256]{3,2,1,0:T(8,128)(2,1)S(1)} %get-tuple-element.100), channel_id=1, source_target_pairs={{0,3},{1,2},{2,1},{3,0},{4,7},{5,6},{6,5},{7,4},{8,11},{9,10},{10,... | collective-permute-start | bytes 393224 | tf_op jit(solution)/shard_map/ppermute | solution.py:146
  59.2 10.7 %collective-permute-start.16 = (bf16[1,4,64,256]{3,2,1,0:T(8,128)(2,1)S(1)}, bf16[1,4,64,256]{3,2,1,0:T(8,128)(2,1)S(1)}, u32[]{:S(2)}, u32[]{:S(2)}) collective-permute-start(bf16[1,4,64,256]{3,2,1,0:T(8,128)(2,1)S(1)} %get-tuple-element.98), channel_id=1, source_target_pairs={{0,1},{1,0},{2,3},{3,2},{4,5},{5,4},{6,7},{7,6},{8,9},{9,8},{10,11... | collective-permute-start | bytes 393224 | tf_op jit(solution)/shard_map/ppermute | solution.py:146

commit v23 on v22

--- a/solution.py
+++ b/solution.py
@@ -150,7 +150,7 @@
     bits = [1 << b for b in reversed(range(1, n_op.bit_length() - 1))]
     order = sorted(range(1, n_blk), key=lambda d: min(d, n_blk - d))
     left, psi, right, tables, columns = {(0, 0): own}, {}, None, None, None
-    waiting, late, made = {(0, 0): 0}, None, None
+    waiting, across, late, made = {(0, 0): 0}, {}, None, None
     for j in range(n_blk + len(bits)):
         new, moved = {}, {}
         for (d, e), done in waiting.items():
@@ -158,13 +158,19 @@
                 new[d + 1, 0] = onward(left[d, 0], 1, n_blk), 0
             for b in range(done, len(bits)):
                 new[d, e ^ bits[b]] = swap(left[d, e], bits[b], n_op), b + 1
-        kept = {key: block for key, (block, _) in new.items()}
+        left.update({key: block for key, (block, _) in new.items()})
+        kept = {key: block for key, (block, _) in new.items() if key[1] == 0}
+        kept.update(across)
+        across = {key: block for key, (block, _) in new.items() if key[1] != 0}
         if late is not None:
             moved["psi"] = late
         if j == 0:
             columns, packed = pack()
-            moved["right"] = [packed[0]]
-            moved["right"] += [swap(part, 2 * e, n_op) for e, part in enumerate(packed[1:], 1)]
+            right = [packed[0]]
+            right += [swap(part, 2 * e, n_op) for e, part in enumerate(packed[1:], 1)]
+            moved["columns"] = columns
+        if j == 0:
+            moved["right"] = right
         if j == 1:
             moved["tables"] = table(right)
         if j == n_blk - 1 and j >= len(bits) + 1:
@@ -174,12 +180,13 @@
         if 2 <= j < n_blk:
             moved["other"] = swap(psi[order[j - 2]][0], 1, n_op)
         late = onward(columns[order[j]], order[j], n_blk) if j < n_blk - 1 else None
-        if not kept and not moved:
+        if not kept:
             break
         waiting = {key: done for key, (_, done) in new.items()}
         kept, moved = lax.optimization_barrier((kept, moved))
         left.update(kept)
         right, tables = moved.get("right", right), moved.get("tables", tables)
+        columns = moved.get("columns", columns)
         made = moved.get("early", made)
         if "psi" in moved:
             psi[order[j - 1]] = [moved["psi"]]

time: 72.2 us -> 72 us (level)
  starting transfers between devices: 23 us -> 30.5 us
  waiting for transfers between devices: 23 us -> 15.5 us
    ppermute x6, waiting for transfers between devices: 13.3 us -> 8.22 us  [onward(): return lax.ppermute(block, 'blk', pairs)]
    ppermute x6, starting transfers between devices: 11.2 us -> 14.3 us  [onward(): return lax.ppermute(block, 'blk', pairs)]
    ppermute x13, waiting for transfers between devices: 6.38 us -> 3.97 us  [swap(): return lax.ppermute(block, 'op', [(i, i ^ e) for i in range(n_op)])]
    ppermute x13, starting transfers between devices: 8.28 us -> 10.5 us  [swap(): return lax.ppermute(block, 'op', [(i, i ^ e) for i in range(n_op)])]
    all_to_all x1, starting transfers between devices: 3.48 us -> 5.68 us  [totals(): return lax.all_to_all(parts, ('blk', 'op'), 0, 0, tiled=True)]
  transfers between devices with their start and end apart: 20 -> 20, of which waited for: 8 -> 6; matrix products, arithmetic and copies ran while one was open for 0% -> 0% of each run, Pallas kernels for 14% -> 14%
where the time goes in v23:
time: 72 us; the launch traced here: 71.7 us
  starting transfers between devices  30.5 us (42%)
  waiting for transfers between devices  15.5 us (22%)
  Pallas kernels  15.2 us (21%)
  blocking collectives  9.73 us (14%)
  between operations  0.76 us (1%)
    pallas_call x7, Pallas kernels, kernel(): pl.pallas_call(body, out_shape=[HBM(shape, dtype) if space == HBM else ja...  15.2 us
    ppermute x6, starting transfers between devices, onward(): return lax.ppermute(block, 'blk', pairs)  14.3 us
    ppermute x13, starting transfers between devices, swap(): return lax.ppermute(block, 'op', [(i, i ^ e) for i in range(n_op)])  10.5 us
    all_to_all x1, blocking collectives, totals(): return lax.all_to_all(parts, ('blk', 'op'), 0, 0, tiled=True)  9.73 us
    ppermute x6, waiting for transfers between devices, onward(): return lax.ppermute(block, 'blk', pairs)  8.22 us
    all_to_all x1, starting transfers between devices, totals(): return lax.all_to_all(parts, ('blk', 'op'), 0, 0, tiled=True)  5.68 us
    ppermute x13, waiting for transfers between devices, swap(): return lax.ppermute(block, 'op', [(i, i ^ e) for i in range(n_op)])  3.97 us
    all_to_all x1, waiting for transfers between devices, totals(): return lax.all_to_all(parts, ('blk', 'op'), 0, 0, tiled=True)  3.36 us
  transfers between devices with their start and end apart: 20, of which 6 were waited for; matrix products, arithmetic and copies ran while one was open for 0% of the time, Pallas kernels for 14%

profile of v23, /device:TPU:0, one launch (start us, length us, event | category | flops | bytes accessed | tf_op | source)
XLA Modules:
  0.0 71.7 jit_solution(6379679724076105969)
XLA Ops:
  0.6 0.0 copy-start.3
  0.6 0.0 copy-start
  0.7 3.1 %collective-permute-start.1 = (bf16[2,256,256]{2,1,0:T(8,128)(2,1)}, bf16[2,256,256]{2,1,0:T(8,128)(2,1)S(1)}, u32[]{:S(2)}, u32[]{:S(2)}) collective-permute-start(bf16[2,256,256]{2,1,0:T(8,128)(2,1)} %bitcast.2), channel_id=1, source_target_pairs={{0,4},{4,12},{12,8},{8,0},{1,5},{5,13},{13,9},{9,1},{2,6},{6,14},{... | collective-permute-start | bytes 786440 | tf_op jit(solution)/shard_map/ppermute | solution.py:142
  3.7 0.0 copy-done.3
  3.7 0.0 collective-permute-start.2
  3.7 1.1 %collective-permute-done.2._ = s32[2]{0:T(128)S(1)} collective-permute-done((s32[2]{0:T(128)S(1)}, s32[2]{0:T(128)S(1)}, u32[]{:S(2)}, u32[]{:S(2)}) %collective-permute-start.2) | collective-permute-done | bytes 40 | tf_op jit(solution)/shard_map/ppermute | solution.py:146
  4.9 1.9 %shard_map.103 = (bf16[256,256]{1,0:T(8,128)(2,1)S(1)}, bf16[256,128]{1,0:T(8,128)(2,1)S(1)}, bf16[256,256]{1,0:T(8,128)(2,1)S(1)}, bf16[256,128]{1,0:T(8,128)(2...) custom-call(s32[2]{0:T(128)S(1)} %copy-done.3, s32[2]{0:T(128)S(1)} %collective-permute-done.2._, ...), custom_call_target="tpu_custom_call" | custom-call | bytes 1048576 | tf_op jit(solution)/shard_map/pallas_call | solution.py:113
  6.8 1.6 %collective-permute-start.3 = (bf16[144,256]{1,0:T(8,128)(2,1)S(1)}, bf16[144,256]{1,0:T(8,128)(2,1)S(1)}, u32[]{:S(2)}, u32[]{:S(2)}) collective-permute-start(bf16[144,256]{1,0:T(8,128)(2,1)S(1)} %get-tuple-element.59), channel_id=1, source_target_pairs={{0,2},{1,3},{2,0},{3,1},{4,6},{5,7},{6,4},{7,5},{8,10},{9,11},{10,... | collective-permute-start | bytes 221192 | tf_op jit(solution)/shard_map/ppermute | solution.py:146
  8.3 0.0 copy-done
  8.3 0.5 collective-permute-start
  8.9 2.8 %collective-permute-done.3.refs_1_.refs_5_ = bf16[144,256]{1,0:T(8,128)(2,1)S(1)} collective-permute-done((bf16[144,256]{1,0:T(8,128)(2,1)S(1)}, bf16[144,256]{1,0:T(8,128)(2,1)S(1)}, u32[]{:S(2)}, u32[]{:S(2)}) %collective-permute-start.3) | collective-permute-done | bytes 73760 | tf_op jit(solution)/shard_map/ppermute | solution.py:146
  11.6 0.0 collective-permute-done.1.refs_2_
  11.7 0.0 copy-start.1
  11.7 0.0 copy-start.2
  11.7 0.0 copy-start.4
  11.7 0.0 copy-start.5
  11.7 2.6 %collective-permute-start.4 = (bf16[2,256,256]{2,1,0:T(8,128)(2,1)S(1)}, bf16[2,256,256]{2,1,0:T(8,128)(2,1)S(1)}, u32[]{:S(2)}, u32[]{:S(2)}) collective-permute-start(bf16[2,256,256]{2,1,0:T(8,128)(2,1)S(1)} %collective-permute-done.1.refs_2_), channel_id=1, source_target_pairs={{0,4},{4,12},{12,8},{8,0},{1,5},{5,13},{13,9},{9,1},{2,6},{6,14},{... | collective-permute-start | bytes 786440 | tf_op jit(solution)/shard_map/ppermute | solution.py:142
  14.3 1.2 %collective-permute-start.5 = (bf16[256,128]{1,0:T(8,128)(2,1)S(1)}, bf16[256,128]{1,0:T(8,128)(2,1)S(1)}, u32[]{:S(2)}, u32[]{:S(2)}) collective-permute-start(bf16[256,128]{1,0:T(8,128)(2,1)S(1)} %get-tuple-element.55), channel_id=1, source_target_pairs={{0,4},{4,12},{12,8},{8,0},{1,5},{5,13},{13,9},{9,1},{2,6},{6,14},{... | collective-permute-start | bytes 196616 | tf_op jit(solution)/shard_map/ppermute | solution.py:142
  15.5 1.5 %collective-permute-start.7 = (bf16[2,256,256]{2,1,0:T(8,128)(2,1)S(1)}, bf16[2,256,256]{2,1,0:T(8,128)(2,1)S(1)}, u32[]{:S(2)}, u32[]{:S(2)}) collective-permute-start(bf16[2,256,256]{2,1,0:T(8,128)(2,1)S(1)} %collective-permute-done.1.refs_2_), channel_id=1, source_target_pairs={{0,2},{1,3},{2,0},{3,1},{4,6},{5,7},{6,4},{7,5},{8,10},{9,11},{10,... | collective-permute-start | bytes 786440 | tf_op jit(solution)/shard_map/ppermute | solution.py:146
  17.0 0.0 copy-done.1
  17.0 0.0 copy-done.2
  17.0 0.0 copy-done.4
  17.0 0.0 copy-done.5
  17.0 1.4 %shard_map.104 = (s32[16]{0:T(128)S(1)}, s32[4]{0:T(128)S(1)}, s32[4]{0:T(128)S(1)}, f32[4,256,128]{2,1,0:T(8,128)S(1)}, f32[1,512]{1,0:T(1,128)S(1)}) custom-call(s32[4]{0:T(128)S(1)} %copy-done.4, s32[4]{0:T(128)S(1)} %copy-done.5, f32[4,256]{1,0:T(4,128)S(1)} %copy-done.1, f32[1,512]{1,0:T(1,128)S(1)} %bitcast.5, ...), custom_call_target="tpu_custom_call" | custom-call | tf_op jit(solution)/shard_map/pallas_call | solution.py:113
  18.4 2.8 %collective-permute-done.5.refs_5_ = bf16[256,128]{1,0:T(8,128)(2,1)S(1)} collective-permute-done((bf16[256,128]{1,0:T(8,128)(2,1)S(1)}, bf16[256,128]{1,0:T(8,128)(2,1)S(1)}, u32[]{:S(2)}, u32[]{:S(2)}) %collective-permute-start.5) | collective-permute-done | bytes 65568 | tf_op jit(solution)/shard_map/ppermute | solution.py:142
  21.2 0.0 collective-permute-done.refs_1_
  21.2 0.0 collective-permute-done.4.refs_0_
  21.2 1.7 %collective-permute-start.8 = (bf16[2,256,256]{2,1,0:T(8,128)(2,1)S(1)}, bf16[2,256,256]{2,1,0:T(8,128)(2,1)S(1)}, u32[]{:S(2)}, u32[]{:S(2)}) collective-permute-start(bf16[2,256,256]{2,1,0:T(8,128)(2,1)S(1)} %collective-permute-done.4.refs_0_), channel_id=1, source_target_pairs={{0,4},{4,12},{12,8},{8,0},{1,5},{5,13},{13,9},{9,1},{2,6},{6,14},{... | collective-permute-start | bytes 786440 | tf_op jit(solution)/shard_map/ppermute | solution.py:142
  22.9 1.2 %collective-permute-start.10 = (bf16[256,128]{1,0:T(8,128)(2,1)S(1)}, bf16[256,128]{1,0:T(8,128)(2,1)S(1)}, u32[]{:S(2)}, u32[]{:S(2)}) collective-permute-start(bf16[256,128]{1,0:T(8,128)(2,1)S(1)} %get-tuple-element.74), channel_id=1, source_target_pairs={{0,8},{4,0},{12,4},{8,12},{1,9},{5,1},{13,5},{9,13},{2,10},{6,2},{... | collective-permute-start | bytes 196616 | tf_op jit(solution)/shard_map/ppermute | solution.py:142
  24.1 0.0 collective-permute-start.9
  24.1 1.5 %collective-permute-start.6 = (bf16[2,256,256]{2,1,0:T(8,128)(2,1)S(1)}, bf16[2,256,256]{2,1,0:T(8,128)(2,1)S(1)}, u32[]{:S(2)}, u32[]{:S(2)}) collective-permute-start(bf16[2,256,256]{2,1,0:T(8,128)(2,1)S(1)} %collective-permute-done.4.refs_0_), channel_id=1, source_target_pairs={{0,2},{1,3},{2,0},{3,1},{4,6},{5,7},{6,4},{7,5},{8,10},{9,11},{10,... | collective-permute-start | bytes 786440 | tf_op jit(solution)/shard_map/ppermute | solution.py:146
  25.6 4.1 %collective-permute-done.10.refs_7_ = bf16[256,128]{1,0:T(8,128)(2,1)S(1)} collective-permute-done((bf16[256,128]{1,0:T(8,128)(2,1)S(1)}, bf16[256,128]{1,0:T(8,128)(2,1)S(1)}, u32[]{:S(2)}, u32[]{:S(2)}) %collective-permute-start.10) | collective-permute-done | bytes 65568 | tf_op jit(solution)/shard_map/ppermute | solution.py:142
  29.7 0.0 collective-permute-done.7.refs_3_
  29.7 0.0 collective-permute-done.9.refs_6_
  29.7 0.0 collective-permute-done.8.refs_2_
  29.7 1.3 %collective-permute-start.13 = (bf16[2,256,256]{2,1,0:T(8,128)(2,1)S(1)}, bf16[2,256,256]{2,1,0:T(8,128)(2,1)S(1)}, u32[]{:S(2)}, u32[]{:S(2)}) collective-permute-start(bf16[2,256,256]{2,1,0:T(8,128)(2,1)S(1)} %collective-permute-done.8.refs_2_), channel_id=1, source_target_pairs={{0,2},{1,3},{2,0},{3,1},{4,6},{5,7},{6,4},{7,5},{8,10},{9,11},{10,... | collective-permute-start | bytes 786440 | tf_op jit(solution)/shard_map/ppermute | solution.py:146
  31.0 4.4 %collective-permute-start.12 = (bf16[256,256]{1,0:T(8,128)(2,1)S(1)}, bf16[256,256]{1,0:T(8,128)(2,1)S(1)}, u32[]{:S(2)}, u32[]{:S(2)}) collective-permute-start(bf16[256,256]{1,0:T(8,128)(2,1)S(1)} %get-tuple-element.82), channel_id=1, source_target_pairs={{0,12},{4,8},{12,0},{8,4},{1,13},{5,9},{13,1},{9,5},{2,14},{6,10},... | collective-permute-start | bytes 393224 | tf_op jit(solution)/shard_map/ppermute | solution.py:142
  35.4 0.0 collective-permute-start.11
  35.4 1.7 %shard_map.105 = (bf16[2,256,256]{2,1,0:T(8,128)(2,1)S(1)}, bf16[2,4,256,256]{3,2,1,0:T(8,128)(2,1)S(1)}, bf16[2,2,2,256,256]{4,3,2,1,0:T(8,128)(2,1)}) custom-call(s32[4]{0:T(128)S(1)} %get-tuple-element.70.widths, bf16[2,256,256]{2,1,0:T(8,128)(2,1)S(1)} %bitcast.4, bf16[2,256,256]{2,1,0:T(8,128)(2,1)S(1)} %collective-permute-done.refs_1_, ...), custom_call_target="tpu_custom_call" | custom-call | flops 268435456 | bytes 4194304 | tf_op jit(solution)/shard_map/pallas_call | solution.py:113
  37.1 1.3 %collective-permute-done.12.refs_6_ = bf16[256,256]{1,0:T(8,128)(2,1)S(1)} collective-permute-done((bf16[256,256]{1,0:T(8,128)(2,1)S(1)}, bf16[256,256]{1,0:T(8,128)(2,1)S(1)}, u32[]{:S(2)}, u32[]{:S(2)}) %collective-permute-start.12) | collective-permute-done | bytes 131104 | tf_op jit(solution)/shard_map/ppermute | solution.py:142
  38.4 0.0 collective-permute-done.6.refs_1_
  38.4 0.0 collective-permute-done.11.refs_8_
  38.4 0.0 collective-permute-done.13.refs_3_
  38.5 3.0 %shard_map.106 = (bf16[4,256,256]{2,1,0:T(8,128)(2,1)S(1)}, bf16[4,256,256]{2,1,0:T(8,128)(2,1)S(1)}, bf16[2,2,2,256,256]{4,3,2,1,0:T(8,128)(2,1)}, f32[16,1,128]{2,1,0:T(1,128)}) custom-call(s32[16]{0:T(128)S(1)} %get-tuple-element.69.src, s32[4]{0:T(128)S(1)} %get-tuple-element.70.widths, bf16[2,256,256]{2,1,0:T(8,128)(2,1)S(1)} %collective-permute-done.4.refs_0_, ...), custom_call_target="tpu_custom_call" | custom-call | flops 1073741824 | bytes 6291456 | tf_op jit(solution)/shard_map/pallas_call | solution.py:113
  41.5 0.1 collective-permute-start.14
  41.6 5.7 %all-to-all-start = ((f32[16,1,128]{2,1,0:T(1,128)}), f32[16,1,128]{2,1,0:T(1,128)S(1)}, u32[]{:S(2)}, u32[]{:S(2)}) async-start(f32[16,1,128]{2,1,0:T(1,128)} %get-tuple-element.91), calls=%async_computation | async-start | bytes 16384 | tf_op jit(solution)/shard_map/all_to_all | solution.py:659
  47.3 0.0 collective-permute-done.14.other
  47.3 1.0 %shard_map.107 = (f32[4,256,256]{2,1,0:T(8,128)S(1)}, bf16[2,4,64,256]{3,2,1,0:T(8,128)(2,1)}) custom-call(bf16[4,256,256]{2,1,0:T(8,128)(2,1)S(1)} %get-tuple-element.95.mine, bf16[4,256,256]{2,1,0:T(8,128)(2,1)S(1)} %collective-permute-done.14.other, bf16[4,256,256]{2,1,0:T(8,128)(2,1)S(1)} %get-tuple-element.94.raw_in.refs_3_, ...), custom_call_target="tpu_custom_call" | custom-call | bytes 4194304 | tf_op jit(solution)/shard_map/pallas_call | solution.py:113
  48.3 1.9 %collective-permute-start.15 = (bf16[2,4,64,256]{3,2,1,0:T(8,128)(2,1)}, bf16[2,4,64,256]{3,2,1,0:T(8,128)(2,1)S(1)}, u32[]{:S(2)}, u32[]{:S(2)}) collective-permute-start(bf16[2,4,64,256]{3,2,1,0:T(8,128)(2,1)} %get-tuple-element.100), channel_id=1, source_target_pairs={{0,2},{1,3},{2,0},{3,1},{4,6},{5,7},{6,4},{7,5},{8,10},{9,11},{10,... | collective-permute-start | bytes 786440 | tf_op jit(solution)/shard_map/ppermute | solution.py:146
  50.2 3.4 %all-to-all-done.refs_2_.parts1 = f32[16,1,128]{2,1,0:T(1,128)S(1)} async-done(((f32[16,1,128]{2,1,0:T(1,128)}), f32[16,1,128]{2,1,0:T(1,128)S(1)}, u32[]{:S(2)}, u32[]{:S(2)}) %all-to-all-start) | async-done | bytes 8224 | tf_op jit(solution)/shard_map/all_to_all | solution.py:659
  53.6 4.2 %shard_map.108 = (f32[16,1,128]{2,1,0:T(1,128)S(1)}, bf16[4,4,64,256]{3,2,1,0:T(8,128)(2,1)S(1)}, bf16[1,4,64,256]{3,2,1,0:T(8,128)(2,1)S(1)}, bf16[2,4,64,256]{...) custom-call(s32[16]{0:T(128)S(1)} %get-tuple-element.69.src, s32[4]{0:T(128)S(1)} %get-tuple-element.70.widths, ...), custom_call_target="tpu_custom_call" | custom-call | flops 4294967296 | bytes 25165824 | tf_op jit(solution)/shard_map/pallas_call | solution.py:113
  57.8 0.6 collective-permute-start.17
  58.4 0.6 collective-permute-start.18
  59.0 0.0 collective-permute-done.15.refs_0_
  59.0 1.0 %collective-permute-start.16 = (bf16[1,4,64,256]{3,2,1,0:T(8,128)(2,1)S(1)}, bf16[1,4,64,256]{3,2,1,0:T(8,128)(2,1)S(1)}, u32[]{:S(2)}, u32[]{:S(2)}) collective-permute-start(bf16[1,4,64,256]{3,2,1,0:T(8,128)(2,1)S(1)} %get-tuple-element.102), channel_id=1, source_target_pairs={{0,1},{1,0},{2,3},{3,2},{4,5},{5,4},{6,7},{7,6},{8,9},{9,8},{10,11... | collective-permute-start | bytes 393224 | tf_op jit(solution)/shard_map/ppermute | solution.py:146
  60.0 9.7 %all_to_all.10.parts2 = f32[16,1,128]{2,1,0:T(1,128)S(1)} all-to-all(f32[16,1,128]{2,1,0:T(1,128)S(1)} %get-tuple-element.97), channel_id=1, replica_groups=mesh['grp'=2,'blk'=4,'op'=4] {'blk','op'}, dimensions={0} | all-to-all | bytes 16384 | tf_op jit(solution)/shard_map/all_to_all | solution.py:659
  69.7 0.0 collective-permute-done.18.refs_3_
  69.7 0.0 collective-permute-done.17.refs_2_
  69.8 0.0 collective-permute-done.16.refs_1_
  69.8 2.0 %shard_map.109 = (bf16[4,64,512]{2,1,0:T(8,128)(2,1)}, bf16[4,64,512]{2,1,0:T(8,128)(2,1)}, f32[1]{0:T(128)}) custom-call(s32[4]{0:T(128)S(1)} %get-tuple-element.68.slots, f32[16,1,128]{2,1,0:T(1,128)S(1)} %all-to-all-done.refs_2_.parts1, f32[16,1,128]{2,1,0:T(1,128)S(1)} %all_to_all.10.parts2, f32[4,256,128]{2,1,0:T(8,128)S(1)} %get-tuple-element.89.refs_11_.diag.refs_5_, ...), custom_call_target="tpu_custom_call" | custom-call | bytes 4194304 | tf_op jit(solution)/shard_map/pallas_call | solution.py:113
Async XLA Ops:
  0.6 3.1 %copy-start.3 = (s32[2]{0:T(128)S(1)}, s32[2]{0:T(128)}, u32[]{:S(2)}) copy-start(s32[2]{0:T(128)} %shift.1) | copy-start | bytes 28
  0.6 7.7 %copy-start = (bf16[2,1,256,256]{3,2,1,0:T(8,128)(2,1)S(1)}, bf16[2,1,256,256]{3,2,1,0:T(8,128)(2,1)}, u32[]{:S(2)}) copy-start(bf16[2,1,256,256]{3,2,1,0:T(8,128)(2,1)} %param.9) | copy-start | bytes 786436
  0.7 11.0 %collective-permute-start.1 = (bf16[2,256,256]{2,1,0:T(8,128)(2,1)}, bf16[2,256,256]{2,1,0:T(8,128)(2,1)S(1)}, u32[]{:S(2)}, u32[]{:S(2)}) collective-permute-start(bf16[2,256,256]{2,1,0:T(8,128)(2,1)} %bitcast.2), channel_id=1, source_target_pairs={{0,4},{4,12},{12,8},{8,0},{1,5},{5,13},{13,9},{9,1},{2,6},{6,14},{... | collective-permute-start | bytes 786440 | tf_op jit(solution)/shard_map/ppermute | solution.py:142
  3.7 1.1 %collective-permute-start.2 = (s32[2]{0:T(128)S(1)}, s32[2]{0:T(128)S(1)}, u32[]{:S(2)}, u32[]{:S(2)}) collective-permute-start(s32[2]{0:T(128)S(1)} %copy-done.3), channel_id=1, source_target_pairs={{0,1},{1,0},{2,3},{3,2},{4,5},{5,4},{6,7},{7,6},{8,9},{9,8},{10,11... | collective-permute-start | bytes 32 | tf_op jit(solution)/shard_map/ppermute | solution.py:146
  6.8 4.9 %collective-permute-start.3 = (bf16[144,256]{1,0:T(8,128)(2,1)S(1)}, bf16[144,256]{1,0:T(8,128)(2,1)S(1)}, u32[]{:S(2)}, u32[]{:S(2)}) collective-permute-start(bf16[144,256]{1,0:T(8,128)(2,1)S(1)} %get-tuple-element.59), channel_id=1, source_target_pairs={{0,2},{1,3},{2,0},{3,1},{4,6},{5,7},{6,4},{7,5},{8,10},{9,11},{10,... | collective-permute-start | bytes 221192 | tf_op jit(solution)/shard_map/ppermute | solution.py:146
  8.3 12.9 %collective-permute-start = (bf16[2,256,256]{2,1,0:T(8,128)(2,1)S(1)}, bf16[2,256,256]{2,1,0:T(8,128)(2,1)S(1)}, u32[]{:S(2)}, u32[]{:S(2)}) collective-permute-start(bf16[2,256,256]{2,1,0:T(8,128)(2,1)S(1)} %bitcast.3), channel_id=1, source_target_pairs={{0,2},{1,3},{2,0},{3,1},{4,6},{5,7},{6,4},{7,5},{8,10},{9,11},{10,... | collective-permute-start | bytes 786440 | tf_op jit(solution)/shard_map/ppermute | solution.py:146
  11.7 5.4 %copy-start.1 = (f32[4,256]{1,0:T(4,128)S(1)}, f32[4,256]{1,0:T(4,128)}, u32[]{:S(2)}) copy-start(f32[4,256]{1,0:T(4,128)} %left_diag.1) | copy-start | bytes 12292
  11.7 5.4 %copy-start.2 = (f32[512]{0:T(512)S(1)}, f32[512]{0:T(512)}, u32[]{:S(2)}) copy-start(f32[512]{0:T(512)} %param.15) | copy-start | bytes 6148
  11.7 5.4 %copy-start.4 = (s32[4]{0:T(128)S(1)}, s32[4]{0:T(128)}, u32[]{:S(2)}) copy-start(s32[4]{0:T(128)} %sector.1) | copy-start | bytes 52
  11.7 5.4 %copy-start.5 = (s32[4]{0:T(128)S(1)}, s32[4]{0:T(128)}, u32[]{:S(2)}) copy-start(s32[4]{0:T(128)} %width.1) | copy-start | bytes 52
  11.7 9.5 %collective-permute-start.4 = (bf16[2,256,256]{2,1,0:T(8,128)(2,1)S(1)}, bf16[2,256,256]{2,1,0:T(8,128)(2,1)S(1)}, u32[]{:S(2)}, u32[]{:S(2)}) collective-permute-start(bf16[2,256,256]{2,1,0:T(8,128)(2,1)S(1)} %collective-permute-done.1.refs_2_), channel_id=1, source_target_pairs={{0,4},{4,12},{12,8},{8,0},{1,5},{5,13},{13,9},{9,1},{2,6},{6,14},{... | collective-permute-start | bytes 786440 | tf_op jit(solution)/shard_map/ppermute | solution.py:142
  14.3 6.9 %collective-permute-start.5 = (bf16[256,128]{1,0:T(8,128)(2,1)S(1)}, bf16[256,128]{1,0:T(8,128)(2,1)S(1)}, u32[]{:S(2)}, u32[]{:S(2)}) collective-permute-start(bf16[256,128]{1,0:T(8,128)(2,1)S(1)} %get-tuple-element.55), channel_id=1, source_target_pairs={{0,4},{4,12},{12,8},{8,0},{1,5},{5,13},{13,9},{9,1},{2,6},{6,14},{... | collective-permute-start | bytes 196616 | tf_op jit(solution)/shard_map/ppermute | solution.py:142
  15.5 14.2 %collective-permute-start.7 = (bf16[2,256,256]{2,1,0:T(8,128)(2,1)S(1)}, bf16[2,256,256]{2,1,0:T(8,128)(2,1)S(1)}, u32[]{:S(2)}, u32[]{:S(2)}) collective-permute-start(bf16[2,256,256]{2,1,0:T(8,128)(2,1)S(1)} %collective-permute-done.1.refs_2_), channel_id=1, source_target_pairs={{0,2},{1,3},{2,0},{3,1},{4,6},{5,7},{6,4},{7,5},{8,10},{9,11},{10,... | collective-permute-start | bytes 786440 | tf_op jit(solution)/shard_map/ppermute | solution.py:146
  21.2 8.5 %collective-permute-start.8 = (bf16[2,256,256]{2,1,0:T(8,128)(2,1)S(1)}, bf16[2,256,256]{2,1,0:T(8,128)(2,1)S(1)}, u32[]{:S(2)}, u32[]{:S(2)}) collective-permute-start(bf16[2,256,256]{2,1,0:T(8,128)(2,1)S(1)} %collective-permute-done.4.refs_0_), channel_id=1, source_target_pairs={{0,4},{4,12},{12,8},{8,0},{1,5},{5,13},{13,9},{9,1},{2,6},{6,14},{... | collective-permute-start | bytes 786440 | tf_op jit(solution)/shard_map/ppermute | solution.py:142
  22.9 6.8 %collective-permute-start.10 = (bf16[256,128]{1,0:T(8,128)(2,1)S(1)}, bf16[256,128]{1,0:T(8,128)(2,1)S(1)}, u32[]{:S(2)}, u32[]{:S(2)}) collective-permute-start(bf16[256,128]{1,0:T(8,128)(2,1)S(1)} %get-tuple-element.74), channel_id=1, source_target_pairs={{0,8},{4,0},{12,4},{8,12},{1,9},{5,1},{13,5},{9,13},{2,10},{6,2},{... | collective-permute-start | bytes 196616 | tf_op jit(solution)/shard_map/ppermute | solution.py:142
  24.1 5.6 %collective-permute-start.9 = (bf16[256,128]{1,0:T(8,128)(2,1)S(1)}, bf16[256,128]{1,0:T(8,128)(2,1)S(1)}, u32[]{:S(2)}, u32[]{:S(2)}) collective-permute-start(bf16[256,128]{1,0:T(8,128)(2,1)S(1)} %collective-permute-done.5.refs_5_), channel_id=1, source_target_pairs={{0,1},{1,0},{2,3},{3,2},{4,5},{5,4},{6,7},{7,6},{8,9},{9,8},{10,11... | collective-permute-start | bytes 196616 | tf_op jit(solution)/shard_map/ppermute | solution.py:146
  24.1 14.3 %collective-permute-start.6 = (bf16[2,256,256]{2,1,0:T(8,128)(2,1)S(1)}, bf16[2,256,256]{2,1,0:T(8,128)(2,1)S(1)}, u32[]{:S(2)}, u32[]{:S(2)}) collective-permute-start(bf16[2,256,256]{2,1,0:T(8,128)(2,1)S(1)} %collective-permute-done.4.refs_0_), channel_id=1, source_target_pairs={{0,2},{1,3},{2,0},{3,1},{4,6},{5,7},{6,4},{7,5},{8,10},{9,11},{10,... | collective-permute-start | bytes 786440 | tf_op jit(solution)/shard_map/ppermute | solution.py:146
  29.7 8.7 %collective-permute-start.13 = (bf16[2,256,256]{2,1,0:T(8,128)(2,1)S(1)}, bf16[2,256,256]{2,1,0:T(8,128)(2,1)S(1)}, u32[]{:S(2)}, u32[]{:S(2)}) collective-permute-start(bf16[2,256,256]{2,1,0:T(8,128)(2,1)S(1)} %collective-permute-done.8.refs_2_), channel_id=1, source_target_pairs={{0,2},{1,3},{2,0},{3,1},{4,6},{5,7},{6,4},{7,5},{8,10},{9,11},{10,... | collective-permute-start | bytes 786440 | tf_op jit(solution)/shard_map/ppermute | solution.py:146
  31.0 7.4 %collective-permute-start.12 = (bf16[256,256]{1,0:T(8,128)(2,1)S(1)}, bf16[256,256]{1,0:T(8,128)(2,1)S(1)}, u32[]{:S(2)}, u32[]{:S(2)}) collective-permute-start(bf16[256,256]{1,0:T(8,128)(2,1)S(1)} %get-tuple-element.82), channel_id=1, source_target_pairs={{0,12},{4,8},{12,0},{8,4},{1,13},{5,9},{13,1},{9,5},{2,14},{6,10},... | collective-permute-start | bytes 393224 | tf_op jit(solution)/shard_map/ppermute | solution.py:142
  35.4 3.0 %collective-permute-start.11 = (bf16[256,128]{1,0:T(8,128)(2,1)S(1)}, bf16[256,128]{1,0:T(8,128)(2,1)S(1)}, u32[]{:S(2)}, u32[]{:S(2)}) collective-permute-start(bf16[256,128]{1,0:T(8,128)(2,1)S(1)} %collective-permute-done.10.refs_7_), channel_id=1, source_target_pairs={{0,1},{1,0},{2,3},{3,2},{4,5},{5,4},{6,7},{7,6},{8,9},{9,8},{10,11... | collective-permute-start | bytes 196616 | tf_op jit(solution)/shard_map/ppermute | solution.py:146
  41.5 5.8 %collective-permute-start.14 = (bf16[4,256,256]{2,1,0:T(8,128)(2,1)S(1)}, bf16[4,256,256]{2,1,0:T(8,128)(2,1)S(1)}, u32[]{:S(2)}, u32[]{:S(2)}) collective-permute-start(bf16[4,256,256]{2,1,0:T(8,128)(2,1)S(1)} %get-tuple-element.95.mine), channel_id=1, source_target_pairs={{0,1},{1,0},{2,3},{3,2},{4,5},{5,4},{6,7},{7,6},{8,9},{9,8},{10,11... | collective-permute-start | bytes 1572872 | tf_op jit(solution)/shard_map/ppermute | solution.py:146
  41.6 12.0 %all-to-all-start = ((f32[16,1,128]{2,1,0:T(1,128)}), f32[16,1,128]{2,1,0:T(1,128)S(1)}, u32[]{:S(2)}, u32[]{:S(2)}) async-start(f32[16,1,128]{2,1,0:T(1,128)} %get-tuple-element.91), calls=%async_computation | async-start | bytes 16384 | tf_op jit(solution)/shard_map/all_to_all | solution.py:659
  48.3 10.7 %collective-permute-start.15 = (bf16[2,4,64,256]{3,2,1,0:T(8,128)(2,1)}, bf16[2,4,64,256]{3,2,1,0:T(8,128)(2,1)S(1)}, u32[]{:S(2)}, u32[]{:S(2)}) collective-permute-start(bf16[2,4,64,256]{3,2,1,0:T(8,128)(2,1)} %get-tuple-element.100), channel_id=1, source_target_pairs={{0,2},{1,3},{2,0},{3,1},{4,6},{5,7},{6,4},{7,5},{8,10},{9,11},{10,... | collective-permute-start | bytes 786440 | tf_op jit(solution)/shard_map/ppermute | solution.py:146
  57.8 11.9 %collective-permute-start.17 = (bf16[2,4,64,256]{3,2,1,0:T(8,128)(2,1)S(1)}, bf16[2,4,64,256]{3,2,1,0:T(8,128)(2,1)S(1)}, u32[]{:S(2)}, u32[]{:S(2)}) collective-permute-start(bf16[2,4,64,256]{3,2,1,0:T(8,128)(2,1)S(1)} %get-tuple-element.103), channel_id=1, source_target_pairs={{0,2},{1,3},{2,0},{3,1},{4,6},{5,7},{6,4},{7,5},{8,10},{9,11},{10,... | collective-permute-start | bytes 786440 | tf_op jit(solution)/shard_map/ppermute | solution.py:146
  58.4 11.4 %collective-permute-start.18 = (bf16[1,4,64,256]{3,2,1,0:T(8,128)(2,1)S(1)}, bf16[1,4,64,256]{3,2,1,0:T(8,128)(2,1)S(1)}, u32[]{:S(2)}, u32[]{:S(2)}) collective-permute-start(bf16[1,4,64,256]{3,2,1,0:T(8,128)(2,1)S(1)} %get-tuple-element.104), channel_id=1, source_target_pairs={{0,3},{1,2},{2,1},{3,0},{4,7},{5,6},{6,5},{7,4},{8,11},{9,10},{10,... | collective-permute-start | bytes 393224 | tf_op jit(solution)/shard_map/ppermute | solution.py:146
  59.0 10.7 %collective-permute-start.16 = (bf16[1,4,64,256]{3,2,1,0:T(8,128)(2,1)S(1)}, bf16[1,4,64,256]{3,2,1,0:T(8,128)(2,1)S(1)}, u32[]{:S(2)}, u32[]{:S(2)}) collective-permute-start(bf16[1,4,64,256]{3,2,1,0:T(8,128)(2,1)S(1)} %get-tuple-element.102), channel_id=1, source_target_pairs={{0,1},{1,0},{2,3},{3,2},{4,5},{5,4},{6,7},{7,6},{8,9},{9,8},{10,11... | collective-permute-start | bytes 393224 | tf_op jit(solution)/shard_map/ppermute | solution.py:146

commit v24 on v22

--- a/solution.py
+++ b/solution.py
@@ -109,7 +109,7 @@
 VMEM, SMEM, HBM = pltpu.VMEM, pltpu.SMEM, pltpu.HBM
 
 
-def kernel(body, ins, outs, scratch=(), flops=0, nbytes=0):
+def kernel(body, ins, outs, scratch=(), flops=0, nbytes=0, in_place=None):
     return pl.pallas_call(
         body,
         out_shape=[
@@ -119,6 +119,7 @@
         in_specs=[pl.BlockSpec(memory_space=space) for _, space in ins],
         out_specs=[pl.BlockSpec(memory_space=space) for _, _, space in outs],
         scratch_shapes=list(scratch),
+        input_output_aliases=in_place or {},
         compiler_params=pltpu.CompilerParams(vmem_limit_bytes=VMEM_LIMIT),
         cost_estimate=pl.CostEstimate(flops=flops, bytes_accessed=nbytes, transcendentals=0),
     )(*[pltpu.with_memory_space_constraint(x, HBM) if space == HBM else x for x, space in ins])
@@ -170,7 +171,7 @@
         if j == n_blk - 1 and j >= len(bits) + 1:
             n_early = min(2, n_blk - 1)
             psi[0] = [columns[0]]
-            moved["early"] = early(left, psi, n_early, tables)
+            moved["early"] = early(left, psi, right, n_early, tables)
         if 2 <= j < n_blk:
             moved["other"] = swap(psi[order[j - 2]][0], 1, n_op)
         late = onward(columns[order[j]], order[j], n_blk) if j < n_blk - 1 else None
@@ -316,16 +317,14 @@
         at += terms
 
 
-def sum_terms(src, widths, inter, right, out, emit):
+def sum_terms(src, widths, inter, blocks, out, emit):
     n_blk, n_terms, _, _ = inter.shape
     n_blk -= 1
-    terms = n_terms // len(right)
-    turned = [by_block(right[j // terms], terms, j % terms) for j in range(n_terms)]
     for t in range(n_blk):
         total = None
         for j in range(n_terms):
             part = jnp.dot(
-                inter[src[t * n_terms + j], j], turned[j], preferred_element_type=jnp.float32
+                inter[src[t * n_terms + j], j], blocks[j], preferred_element_type=jnp.float32
             )
             total = part if total is None else total + part
         total = jnp.where(row_mask(widths[t], total.shape), total, 0.0)
@@ -366,11 +365,25 @@
         left_products(raw_out[d], lambda at: line[at // terms][...], inter.at[d])
 
 
+def right_products(inter, blocks, sums, d):
+    for j in range(blocks.shape[0]):
+        prod = jnp.dot(inter[d, j], blocks[j], preferred_element_type=jnp.float32)
+        sums[d, j] = prod.astype(sums.dtype)
+
+
 def early_body(n_pair, counts, widths, *refs):
     left, refs = take(refs, [n_pair] * len(counts))
-    psi, (raw_out, inter_out, left_out, sems) = take(refs, counts)
+    (right,), refs = take(refs, [n_pair])
+    psi, (raw_out, sums_out, blocks_out, left_out, inter, sems) = take(refs, counts)
     copies = keep(left, left_out, sems)
-    products_of(psi, left, widths, 0, raw_out, inter_out)
+    n_terms = blocks_out.shape[0]
+    terms = n_terms // n_pair
+    for j in range(n_terms):
+        blocks_out[j] = by_block(right[j // terms], terms, j % terms)
+    sums_out[sums_out.shape[0] - 1] = jnp.zeros_like(sums_out[0])
+    products_of(psi, left, widths, 0, raw_out, inter)
+    for d in range(len(counts)):
+        right_products(inter, blocks_out, sums_out, d)
     for copy in copies:
         copy.wait()
 
@@ -379,21 +392,13 @@
     n_late = len(counts)
     n_early = n_blk - n_late
     left, refs = take(refs, [n_pair] * n_late)
-    (right,), refs = take(refs, [n_pair])
     psi, refs = take(refs, counts)
-    raw_in, inter_in, diag, right_diag, part_out, raw_out, left_out, dots_out, inter, sems = refs
+    blocks, diag, right_diag, _, _, raw_out, held, part_out, left_out, dots_out, inter, sems = refs
+    n_terms = blocks.shape[0]
     copies = keep(left, left_out, sems)
-    for j, (given, own) in enumerate(((inter_in, inter), (raw_in, raw_out))):
-        copies.append(
-            pltpu.make_async_copy(given, own.at[:n_early], sems.at[n_late * n_pair + j])
-        )
-        copies[-1].start()
-    inter[n_blk] = jnp.zeros_like(inter[n_blk])
-    products_of(
-        psi, left, widths, n_early, raw_out.at[n_early:], inter.at[n_early:n_blk]
-    )
-    for copy in copies:
-        copy.wait()
+    products_of(psi, left, widths, n_early, raw_out.at[n_early:], inter)
+    for d in range(n_late):
+        right_products(inter, blocks, held.at[n_early:], d)
     cols = diag.shape[2]
     zero = jnp.zeros((8, cols), jnp.float32)
     sums = [zero, zero]
@@ -408,8 +413,17 @@
                 sums[0] = sums[0] + fold(raw * raw)
             sums[1] = sums[1] + fold(raw * image)
 
-    sum_terms(src, widths, inter, right, part_out, emit)
+    for t in range(n_blk):
+        total = None
+        for j in range(n_terms):
+            part = held[src[t * n_terms + j], j].astype(jnp.float32)
+            total = part if total is None else total + part
+        total = jnp.where(row_mask(widths[t], total.shape), total, 0.0)
+        part_out[t] = total.astype(jnp.bfloat16)
+        emit(t, total)
     spread([whole(x) for x in sums], dots_out)
+    for copy in copies:
+        copy.wait()
 
 
 def send_rows(e, send, d, *refs):
@@ -443,8 +457,8 @@
     return scale, tot[:, 1:2] * scale * scale
 
 
-def second_body(n_blk, n_pair, count, src, widths, left_early, left_late, *refs):
-    right, refs = refs[:n_pair], refs[n_pair:]
+def second_body(n_blk, count, src, widths, left_early, left_late, *refs):
+    blocks, refs = refs[0], refs[1:]
     parts, raw_in, sig, diag, right_diag, dots_out, own_out = refs[:7]
     sends, (inter, corr, fld, part_out, held, sems) = refs[7:-6], refs[-6:]
     copies = []
@@ -503,7 +517,7 @@
 
     _, own_op = place_of()
     step = own_out.shape[2]
-    sum_terms(src, widths, inter, right, part_out, emit)
+    sum_terms(src, widths, inter, blocks, part_out, emit)
     vv, vc, vs = halves[0]
     ff, vf, fs, vt, ft = (whole(x) for x in sums)
     spread([vv, vc, whole(vs), ff, vf * scale, fs * scale, vt * scale, ft], dots_out)
@@ -527,8 +541,8 @@
 def third_body(n_blk, n_op, count, slots, parts1, parts2, diag, right_diag, own, *refs):
     n_far = n_op // 2 - 1
     got1, got2 = refs[:n_far], refs[n_far : n_far + n_op - 1]
-    new_out, res_out, energy_out = refs[n_far + n_op - 1 :]
-    step, cols = new_out.shape[1], new_out.shape[2] // n_op
+    new_out, res_out, energy_out, new, res, sems = refs[n_far + n_op - 1 :]
+    step, cols = new.shape[1], new.shape[2] // n_op
     own_blk, own_op = place_of()
     scale, theta = norm_theta(parts1[...], count)
     pairs = parts2[...].reshape(n_blk * n_op // 2, 2, *parts2.shape[1:])
@@ -552,26 +566,33 @@
     energy_out[0] = jnp.max(energy)
     cu = cu * unit
     mine = pl.ds(pl.multiple_of(own_op * step, step), step)
+    on_vec = []
     for e in range(0, n_op, 2):
         there = own_blk * n_op + (own_op ^ e)
         pair = parts2[there] + parts2[own_blk * n_op + (own_op ^ e ^ 1)]
-        on_vec = cv + cu * (nearest(pair[:, 0:1], pair[:, 1:2]) - along)
-        for h in range(2):
-            at = pl.multiple_of((own_op ^ e ^ h) * cols, LANES)
-            part, crossed = slice(h * cols, (h + 1) * cols), slice((1 - h) * cols, (2 - h) * cols)
-            for d in range(n_blk):
+        on_vec.append(cv + cu * (nearest(pair[:, 0:1], pair[:, 1:2]) - along))
+    copies = []
+    for d in range(n_blk):
+        for e in range(0, n_op, 2):
+            blocks = [own.at[j] for j in range(4)]
+            if e:
+                far, near = got1[e // 2 - 1], got2[e - 1]
+                blocks = far.at[0], far.at[1], near.at[0], near.at[1]
+            for h in range(2):
+                at = pl.multiple_of((own_op ^ e ^ h) * cols, LANES)
+                part, crossed = slice(h * cols, (h + 1) * cols), slice((1 - h) * cols, (2 - h) * cols)
                 dmat = diag[d, mine] + right_diag[:, pl.ds(at, cols)]
-                blocks = [own.at[j] for j in range(4)]
-                if e:
-                    far, near = got1[e // 2 - 1], got2[e - 1]
-                    blocks = far.at[0], far.at[1], near.at[0], near.at[1]
                 raw, sigma, fld, image = (x[d, :, part].astype(jnp.float32) for x in blocks)
-                vec, sigma = raw * scale, sigma * scale
                 image = image + got2[e][0, d, :, crossed].astype(jnp.float32) + dmat * fld
-                newvec = on_vec * vec + cu * fld
-                res = on_vec * sigma + cu * image - energy * newvec
-                new_out[slots[d], :, pl.ds(at, cols)] = newvec.astype(jnp.bfloat16)
-                res_out[slots[d], :, pl.ds(at, cols)] = res.astype(jnp.bfloat16)
+                newvec = on_vec[e // 2] * (raw * scale) + cu * fld
+                rest = on_vec[e // 2] * (sigma * scale) + cu * image - energy * newvec
+                new[d, :, pl.ds(at, cols)] = newvec.astype(jnp.bfloat16)
+                res[d, :, pl.ds(at, cols)] = rest.astype(jnp.bfloat16)
+        for j, (held, out) in enumerate(((new, new_out), (res, res_out))):
+            copies.append(pltpu.make_async_copy(held.at[d], out.at[slots[d]], sems.at[2 * d + j]))
+            copies[-1].start()
+    for copy in copies:
+        copy.wait()
 
 
 def per_device(
@@ -615,32 +636,36 @@
         halves = [half for d in those for half in psi[d]]
         return [(x, VMEM) for x in blocks], [(x, VMEM) for x in halves], [len(psi[d]) for d in those]
 
-    def early(left, psi, n_early, tables):
+    narrow = ((n_blk, rows, 2 * cols), bf16, VMEM)
+
+    def early(left, psi, right, n_early, tables):
         left_ins, psi_ins, counts = inputs(left, psi, range(n_early))
         return kernel(
             functools.partial(early_body, n_pair, counts),
-            [(tables[1], SMEM)] + left_ins + psi_ins,
+            [(tables[1], SMEM)] + left_ins + [(x, VMEM) for x in right] + psi_ins,
             [
-                ((n_early, rows, 2 * cols), bf16, VMEM),
-                ((n_early, n_pair * terms, rows, 2 * cols), bf16, VMEM),
+                narrow,
+                ((n_blk + 1, n_pair * terms, rows, 2 * cols), bf16, VMEM),
+                ((n_pair * terms, 2 * cols, 2 * cols), bf16, VMEM),
                 ((n_early, n_pair, terms, rows, rows), bf16, HBM),
             ],
-            [pltpu.SemaphoreType.DMA((n_early * n_pair,))],
+            [
+                pltpu.VMEM((n_early, n_pair * terms, rows, 2 * cols), bf16),
+                pltpu.SemaphoreType.DMA((n_early * n_pair,)),
+            ],
             flops=2 * n_early * rows * rows * 2 * cols * terms * n_pair,
             nbytes=4 << 20,
         )
 
-    left, psi_by, right, (src, widths, slots, *both), (raw_early, inter_early, left_early) = gather(
+    left, psi_by, right, (src, widths, slots, *both), (raw_early, products, blocks, left_early) = gather(
         left_ops[:, 0], n_blk, n_op, pack, table, early
     )
-    n_early = raw_early.shape[0]
+    n_early = left_early.shape[0]
     n_late = n_blk - n_early
     left_ins, psi_ins, counts = inputs(left, psi_by, range(n_early, n_blk))
-    right_ins = [(block, VMEM) for block in right]
     diags = [(x, VMEM) for x in both]
 
     tables = [(src, SMEM), (widths, SMEM)]
-    narrow = ((n_blk, rows, 2 * cols), bf16, VMEM)
     dots = ((n_dev, 1, LANES), f32, VMEM)
     wide = ((n_blk, rows, 2 * cols), f32, VMEM)
     sends = [((2 - e % 2, n_blk, step, 2 * cols), bf16, VMEM) for e in range(1, n_op)]
@@ -651,11 +676,16 @@
     def totals(parts):
         return lax.all_to_all(parts, ("blk", "op"), 0, 0, tiled=True)
 
-    part1, raw, kept, dots1 = kernel(
+    first_ins = tables + left_ins + psi_ins + [(blocks, VMEM)] + diags
+    raw, _, part1, kept, dots1 = kernel(
         functools.partial(first_body, n_blk, n_pair, counts),
-        tables + left_ins + right_ins + psi_ins + [(raw_early, VMEM), (inter_early, VMEM)] + diags,
-        [narrow, narrow, (left_late, bf16, HBM), dots],
-        [inter, pltpu.SemaphoreType.DMA((n_late * n_pair + 2,))],
+        first_ins + [(raw_early, VMEM), (products, VMEM)],
+        [narrow, (products.shape, bf16, VMEM), narrow, (left_late, bf16, HBM), dots],
+        [
+            pltpu.VMEM((n_late, n_pair * terms, rows, 2 * cols), bf16),
+            pltpu.SemaphoreType.DMA((n_late * n_pair,)),
+        ],
+        in_place={len(first_ins): 0, len(first_ins) + 1: 1},
         **cost,
     )
     parts1 = totals(dots1)
@@ -667,8 +697,8 @@
     )
     got1 = [swap(block, 2 * e, n_op) for e, block in enumerate(out1, 1)]
     dots2, own, *out2 = kernel(
-        functools.partial(second_body, n_blk, n_pair, count),
-        tables + [(left_early, HBM), (kept, HBM)] + right_ins
+        functools.partial(second_body, n_blk, count),
+        tables + [(left_early, HBM), (kept, HBM), (blocks, VMEM)]
         + [(x, VMEM) for x in (parts1, raw, sig)] + diags,
         [dots, ((4, n_blk, step, 2 * cols), bf16, VMEM)] + sends,
         [
@@ -685,12 +715,13 @@
     near, got1 = lax.optimization_barrier((out2[0], got1))
     parts2 = totals(dots2)
     got2 = [swap(near, 1, n_op)] + [swap(block, e, n_op) for e, block in enumerate(out2[1:], 2)]
-    final = ((n_blk, step, n_op * cols), bf16, VMEM)
+    final = ((n_blk, step, n_op * cols), bf16, HBM)
     new, res, energy = kernel(
         functools.partial(third_body, n_blk, n_op, count),
         [(slots, SMEM)] + [(x, VMEM) for x in (parts1, parts2)] + diags
         + [(x, VMEM) for x in (own, *got1, *got2)],
         [final, final, ((1,), f32, SMEM)],
+        [pltpu.VMEM(final[0], bf16)] * 2 + [pltpu.SemaphoreType.DMA((2 * n_blk,))],
         nbytes=4 << 20,
     )
     return new, res, energy

time: 72.2 us -> 74.2 us (1.028)
  waiting for transfers between devices: 23 us -> 16.6 us
  local copies, waits for them, and re-layouts: 0.23 us -> 6.5 us
  starting transfers between devices: 23 us -> 25.7 us
  blocking collectives: 9.72 us -> 8.97 us
    unnamed x12 -> x16, local copies, waits for them, and re-layouts: 0.23 us -> 6.5 us
    ppermute x6, waiting for transfers between devices: 13.3 us -> 8.36 us  [onward(): return lax.ppermute(block, 'blk', pairs)]
    ppermute x13, starting transfers between devices: 8.28 us -> 10.3 us  [swap(): return lax.ppermute(block, 'op', [(i, i ^ e) for i in range(n_op)])]
    ppermute x13, waiting for transfers between devices: 6.38 us -> 5.13 us  [swap(): return lax.ppermute(block, 'op', [(i, i ^ e) for i in range(n_op)])]
    all_to_all x1, starting transfers between devices: 3.48 us -> 4.28 us  [totals(): return lax.all_to_all(parts, ('blk', 'op'), 0, 0, tiled=True)]
    all_to_all x1, blocking collectives: 9.72 us -> 8.97 us  [totals(): return lax.all_to_all(parts, ('blk', 'op'), 0, 0, tiled=True)]
  transfers between devices with their start and end apart: 20 -> 20, of which waited for: 8 -> 6; matrix products, arithmetic and copies ran while one was open for 0% -> 0% of each run, Pallas kernels for 14% -> 13%
where the time goes in v24:
time: 74.2 us; the launch traced here: 73.8 us
  starting transfers between devices  25.7 us (35%)
  waiting for transfers between devices  16.6 us (22%)
  Pallas kernels  15.3 us (21%)
  blocking collectives  8.97 us (12%)
  local copies, waits for them, and re-layouts  6.5 us (9%)
    pallas_call x7, Pallas kernels, kernel(): pl.pallas_call(body, out_shape=[HBM(shape, dtype) if space == HBM else ja...  15.3 us
    ppermute x6, starting transfers between devices, onward(): return lax.ppermute(block, 'blk', pairs)  11.1 us
    ppermute x13, starting transfers between devices, swap(): return lax.ppermute(block, 'op', [(i, i ^ e) for i in range(n_op)])  10.3 us
    all_to_all x1, blocking collectives, totals(): return lax.all_to_all(parts, ('blk', 'op'), 0, 0, tiled=True)  8.97 us
    ppermute x6, waiting for transfers between devices, onward(): return lax.ppermute(block, 'blk', pairs)  8.36 us
    unnamed x16, local copies, waits for them, and re-layouts  6.5 us
    ppermute x13, waiting for transfers between devices, swap(): return lax.ppermute(block, 'op', [(i, i ^ e) for i in range(n_op)])  5.13 us
    all_to_all x1, starting transfers between devices, totals(): return lax.all_to_all(parts, ('blk', 'op'), 0, 0, tiled=True)  4.28 us
  transfers between devices with their start and end apart: 20, of which 6 were waited for; matrix products, arithmetic and copies ran while one was open for 0% of the time, Pallas kernels for 13%

profile of v24, /device:TPU:0, one launch (start us, length us, event | category | flops | bytes accessed | tf_op | source)
XLA Modules:
  0.0 73.8 jit_solution(13089321863418897130)
XLA Ops:
  0.6 3.1 %collective-permute-start.1 = (bf16[2,256,256]{2,1,0:T(8,128)(2,1)}, bf16[2,256,256]{2,1,0:T(8,128)(2,1)S(1)}, u32[]{:S(2)}, u32[]{:S(2)}) collective-permute-start(bf16[2,256,256]{2,1,0:T(8,128)(2,1)} %bitcast.2), channel_id=1, source_target_pairs={{0,4},{4,12},{12,8},{8,0},{1,5},{5,13},{13,9},{9,1},{2,6},{6,14},{... | collective-permute-start | bytes 786440 | tf_op jit(solution)/shard_map/ppermute | solution.py:143
  3.7 1.5 %collective-permute-start = (bf16[2,256,256]{2,1,0:T(8,128)(2,1)}, bf16[2,256,256]{2,1,0:T(8,128)(2,1)S(1)}, u32[]{:S(2)}, u32[]{:S(2)}) collective-permute-start(bf16[2,256,256]{2,1,0:T(8,128)(2,1)} %bitcast.3), channel_id=1, source_target_pairs={{0,2},{1,3},{2,0},{3,1},{4,6},{5,7},{6,4},{7,5},{8,10},{9,11},{10,... | collective-permute-start | bytes 786440 | tf_op jit(solution)/shard_map/ppermute | solution.py:147
  5.2 0.0 collective-permute-start.2
  5.2 1.3 %collective-permute-done.2._ = s32[2]{0:T(128)S(1)} collective-permute-done((s32[2]{0:T(128)}, s32[2]{0:T(128)S(1)}, u32[]{:S(2)}, u32[]{:S(2)}) %collective-permute-start.2) | collective-permute-done | bytes 40 | tf_op jit(solution)/shard_map/ppermute | solution.py:147
  6.5 0.0 copy-start.3
  6.5 0.7 copy-done.3
  7.1 1.9 %shard_map.103 = (bf16[256,256]{1,0:T(8,128)(2,1)S(1)}, bf16[256,128]{1,0:T(8,128)(2,1)S(1)}, bf16[256,256]{1,0:T(8,128)(2,1)S(1)}, bf16[256,128]{1,0:T(8,128)(2...) custom-call(s32[2]{0:T(128)S(1)} %copy-done.3, s32[2]{0:T(128)S(1)} %collective-permute-done.2._, ...), custom_call_target="tpu_custom_call" | custom-call | bytes 1048576 | tf_op jit(solution)/shard_map/pallas_call | solution.py:113
  9.0 0.6 collective-permute-start.3
  9.6 3.8 %collective-permute-done.3.refs_1_.refs_5_ = bf16[144,256]{1,0:T(8,128)(2,1)S(1)} collective-permute-done((bf16[144,256]{1,0:T(8,128)(2,1)S(1)}, bf16[144,256]{1,0:T(8,128)(2,1)S(1)}, u32[]{:S(2)}, u32[]{:S(2)}) %collective-permute-start.3) | collective-permute-done | bytes 73760 | tf_op jit(solution)/shard_map/ppermute | solution.py:147
  13.5 0.0 collective-permute-done.1.refs_2_
  13.5 0.0 collective-permute-done.refs_1_
  13.5 2.6 %collective-permute-start.5 = (bf16[2,256,256]{2,1,0:T(8,128)(2,1)S(1)}, bf16[2,256,256]{2,1,0:T(8,128)(2,1)S(1)}, u32[]{:S(2)}, u32[]{:S(2)}) collective-permute-start(bf16[2,256,256]{2,1,0:T(8,128)(2,1)S(1)} %collective-permute-done.1.refs_2_), channel_id=1, source_target_pairs={{0,4},{4,12},{12,8},{8,0},{1,5},{5,13},{13,9},{9,1},{2,6},{6,14},{... | collective-permute-start | bytes 786440 | tf_op jit(solution)/shard_map/ppermute | solution.py:143
  16.1 1.3 %collective-permute-start.4 = (bf16[2,256,256]{2,1,0:T(8,128)(2,1)S(1)}, bf16[2,256,256]{2,1,0:T(8,128)(2,1)S(1)}, u32[]{:S(2)}, u32[]{:S(2)}) collective-permute-start(bf16[2,256,256]{2,1,0:T(8,128)(2,1)S(1)} %collective-permute-done.1.refs_2_), channel_id=1, source_target_pairs={{0,2},{1,3},{2,0},{3,1},{4,6},{5,7},{6,4},{7,5},{8,10},{9,11},{10,... | collective-permute-start | bytes 786440 | tf_op jit(solution)/shard_map/ppermute | solution.py:147
  17.4 0.4 collective-permute-start.6
  17.8 0.0 copy-start.1
  17.8 0.7 copy-done.1
  18.5 0.0 copy-start.2
  18.5 0.7 copy-done.2
  19.2 0.0 copy-start.4
  19.2 0.7 copy-done.4
  19.8 0.0 copy-start.5
  19.8 0.7 copy-done.5
  20.5 1.3 %shard_map.104 = (s32[16]{0:T(128)S(1)}, s32[4]{0:T(128)S(1)}, s32[4]{0:T(128)S(1)}, f32[4,256,128]{2,1,0:T(8,128)S(1)}, f32[1,512]{1,0:T(1,128)S(1)}) custom-call(s32[4]{0:T(128)S(1)} %copy-done.4, s32[4]{0:T(128)S(1)} %copy-done.5, f32[4,256]{1,0:T(4,128)S(1)} %copy-done.1, f32[1,512]{1,0:T(1,128)S(1)} %bitcast.5, ...), custom_call_target="tpu_custom_call" | custom-call | tf_op jit(solution)/shard_map/pallas_call | solution.py:113
  21.8 1.5 %collective-permute-done.6.refs_7_ = bf16[256,128]{1,0:T(8,128)(2,1)S(1)} collective-permute-done((bf16[256,128]{1,0:T(8,128)(2,1)S(1)}, bf16[256,128]{1,0:T(8,128)(2,1)S(1)}, u32[]{:S(2)}, u32[]{:S(2)}) %collective-permute-start.6) | collective-permute-done | bytes 65568 | tf_op jit(solution)/shard_map/ppermute | solution.py:143
  23.4 0.0 collective-permute-done.5.refs_0_
  23.4 0.0 collective-permute-done.4.refs_3_
  23.4 1.7 %collective-permute-start.8 = (bf16[2,256,256]{2,1,0:T(8,128)(2,1)S(1)}, bf16[2,256,256]{2,1,0:T(8,128)(2,1)S(1)}, u32[]{:S(2)}, u32[]{:S(2)}) collective-permute-start(bf16[2,256,256]{2,1,0:T(8,128)(2,1)S(1)} %collective-permute-done.5.refs_0_), channel_id=1, source_target_pairs={{0,4},{4,12},{12,8},{8,0},{1,5},{5,13},{13,9},{9,1},{2,6},{6,14},{... | collective-permute-start | bytes 786440 | tf_op jit(solution)/shard_map/ppermute | solution.py:143
  25.1 1.3 %collective-permute-start.7 = (bf16[2,256,256]{2,1,0:T(8,128)(2,1)S(1)}, bf16[2,256,256]{2,1,0:T(8,128)(2,1)S(1)}, u32[]{:S(2)}, u32[]{:S(2)}) collective-permute-start(bf16[2,256,256]{2,1,0:T(8,128)(2,1)S(1)} %collective-permute-done.5.refs_0_), channel_id=1, source_target_pairs={{0,2},{1,3},{2,0},{3,1},{4,6},{5,7},{6,4},{7,5},{8,10},{9,11},{10,... | collective-permute-start | bytes 786440 | tf_op jit(solution)/shard_map/ppermute | solution.py:147
  26.4 1.2 %collective-permute-start.10 = (bf16[256,128]{1,0:T(8,128)(2,1)S(1)}, bf16[256,128]{1,0:T(8,128)(2,1)S(1)}, u32[]{:S(2)}, u32[]{:S(2)}) collective-permute-start(bf16[256,128]{1,0:T(8,128)(2,1)S(1)} %get-tuple-element.70), channel_id=1, source_target_pairs={{0,8},{4,0},{12,4},{8,12},{1,9},{5,1},{13,5},{9,13},{2,10},{6,2},{... | collective-permute-start | bytes 196616 | tf_op jit(solution)/shard_map/ppermute | solution.py:143
  27.6 0.0 collective-permute-start.9
  27.6 4.7 %collective-permute-done.10.refs_5_ = bf16[256,128]{1,0:T(8,128)(2,1)S(1)} collective-permute-done((bf16[256,128]{1,0:T(8,128)(2,1)S(1)}, bf16[256,128]{1,0:T(8,128)(2,1)S(1)}, u32[]{:S(2)}, u32[]{:S(2)}) %collective-permute-start.10) | collective-permute-done | bytes 65568 | tf_op jit(solution)/shard_map/ppermute | solution.py:143
  32.4 0.0 collective-permute-done.9.refs_8_
  32.4 0.0 collective-permute-done.8.refs_2_
  32.4 0.0 collective-permute-done.7.refs_1_
  32.4 1.4 %collective-permute-start.11 = (bf16[2,256,256]{2,1,0:T(8,128)(2,1)S(1)}, bf16[2,256,256]{2,1,0:T(8,128)(2,1)S(1)}, u32[]{:S(2)}, u32[]{:S(2)}) collective-permute-start(bf16[2,256,256]{2,1,0:T(8,128)(2,1)S(1)} %collective-permute-done.8.refs_2_), channel_id=1, source_target_pairs={{0,2},{1,3},{2,0},{3,1},{4,6},{5,7},{6,4},{7,5},{8,10},{9,11},{10,... | collective-permute-start | bytes 786440 | tf_op jit(solution)/shard_map/ppermute | solution.py:147
  33.8 2.0 %collective-permute-start.13 = (bf16[256,256]{1,0:T(8,128)(2,1)S(1)}, bf16[256,256]{1,0:T(8,128)(2,1)S(1)}, u32[]{:S(2)}, u32[]{:S(2)}) collective-permute-start(bf16[256,256]{1,0:T(8,128)(2,1)S(1)} %get-tuple-element.82), channel_id=1, source_target_pairs={{0,12},{4,8},{12,0},{8,4},{1,13},{5,9},{13,1},{9,5},{2,14},{6,10},... | collective-permute-start | bytes 393224 | tf_op jit(solution)/shard_map/ppermute | solution.py:143
  35.8 0.0 collective-permute-start.12
  35.8 0.0 copy-start
  35.8 0.9 %copy-done = bf16[2,1,256,256]{3,2,1,0:T(8,128)(2,1)S(1)} copy-done((bf16[2,1,256,256]{3,2,1,0:T(8,128)(2,1)S(1)}, bf16[2,1,256,256]{3,2,1,0:T(8,128)(2,1)}, u32[]{:S(2)}) %copy-start) | copy-done | bytes 262168
  36.8 1.7 %shard_map.105 = (bf16[4,256,256]{2,1,0:T(8,128)(2,1)S(1)}, bf16[5,4,256,256]{3,2,1,0:T(8,128)(2,1)S(1)}, bf16[4,256,256]{2,1,0:T(8,128)(2,1)S(1)}, bf16[2,2,2,256,256]{4,3,2,1,0:T(8,128)(2,1)}) custom-call(s32[4]{0:T(128)S(1)} %get-tuple-element.67.widths, bf16[2,256,256]{2,1,0:T(8,128)(2,1)S(1)} %bitcast.4, ...), custom_call_target="tpu_custom_call" | custom-call | flops 268435456 | bytes 4194304 | tf_op jit(solution)/shard_map/pallas_call | solution.py:113
  38.5 2.1 %collective-permute-done.13.refs_4_ = bf16[256,256]{1,0:T(8,128)(2,1)S(1)} collective-permute-done((bf16[256,256]{1,0:T(8,128)(2,1)S(1)}, bf16[256,256]{1,0:T(8,128)(2,1)S(1)}, u32[]{:S(2)}, u32[]{:S(2)}) %collective-permute-start.13) | collective-permute-done | bytes 131104 | tf_op jit(solution)/shard_map/ppermute | solution.py:143
  40.6 0.0 collective-permute-done.12.refs_6_
  40.6 0.0 collective-permute-done.11.refs_3_
  40.6 3.5 %shard_map.106 = (bf16[4,256,256]{2,1,0:T(8,128)(2,1)S(1)}, bf16[5,4,256,256]{3,2,1,0:T(8,128)(2,1)S(1)}, bf16[4,256,256]{2,1,0:T(8,128)(2,1)S(1)}, bf16[2,2,2,256,256]{4,3,2,1,0:T(8,128)(2,1)}, f32[16,1,128]{2,1,0:T(1,128)}) custom-call(s32[16]{0:T(128)S(1)} %get-tuple-element.66.src, ...), custom_call_target="tpu_custom_call", output_to_operand_aliasing={{0}: (12, {}), {1}: (13, {})} | custom-call | flops 1073741824 | bytes 6291456 | tf_op jit(solution)/shard_map/pallas_call | solution.py:113
  44.1 0.1 collective-permute-start.14
  44.2 4.3 %all-to-all-start = ((f32[16,1,128]{2,1,0:T(1,128)}), f32[16,1,128]{2,1,0:T(1,128)S(1)}, u32[]{:S(2)}, u32[]{:S(2)}) async-start(f32[16,1,128]{2,1,0:T(1,128)} %get-tuple-element.91), calls=%async_computation | async-start | bytes 16384 | tf_op jit(solution)/shard_map/all_to_all | solution.py:677
  48.5 0.0 collective-permute-done.14.other
  48.5 0.3 shard_map.107
  48.8 0.0 copy-start.6
  48.8 1.0 %copy-done.6 = f32[4,256,256]{2,1,0:T(8,128)} copy-done((f32[4,256,256]{2,1,0:T(8,128)}, f32[4,256,256]{2,1,0:T(8,128)S(1)}, u32[]{:S(2)}) %copy-start.6) | copy-done | bytes 1048600
  49.8 1.9 %collective-permute-start.15 = (bf16[2,4,64,256]{3,2,1,0:T(8,128)(2,1)S(1)}, bf16[2,4,64,256]{3,2,1,0:T(8,128)(2,1)S(1)}, u32[]{:S(2)}, u32[]{:S(2)}) collective-permute-start(bf16[2,4,64,256]{3,2,1,0:T(8,128)(2,1)S(1)} %get-tuple-element.100), channel_id=1, source_target_pairs={{0,2},{1,3},{2,0},{3,1},{4,6},{5,7},{6,4},{7,5},{8,10},{9,11},{10,... | collective-permute-start | bytes 786440 | tf_op jit(solution)/shard_map/ppermute | solution.py:147
  51.7 3.1 %all-to-all-done.refs_1_.parts1 = f32[16,1,128]{2,1,0:T(1,128)S(1)} async-done(((f32[16,1,128]{2,1,0:T(1,128)}), f32[16,1,128]{2,1,0:T(1,128)S(1)}, u32[]{:S(2)}, u32[]{:S(2)}) %all-to-all-start) | async-done | bytes 8224 | tf_op jit(solution)/shard_map/all_to_all | solution.py:677
  54.8 0.0 copy-start.7
  54.8 1.2 %copy-done.7 = f32[4,256,256]{2,1,0:T(8,128)S(1)} copy-done((f32[4,256,256]{2,1,0:T(8,128)S(1)}, f32[4,256,256]{2,1,0:T(8,128)}, u32[]{:S(2)}) %copy-start.7) | copy-done | bytes 1048600
  56.0 4.0 %shard_map.108 = (f32[16,1,128]{2,1,0:T(1,128)S(1)}, bf16[4,4,64,256]{3,2,1,0:T(8,128)(2,1)S(1)}, bf16[1,4,64,256]{3,2,1,0:T(8,128)(2,1)S(1)}, bf16[2,4,64,256]{...) custom-call(s32[16]{0:T(128)S(1)} %get-tuple-element.66.src, s32[4]{0:T(128)S(1)} %get-tuple-element.67.widths, ...), custom_call_target="tpu_custom_call" | custom-call | flops 4294967296 | bytes 25165824 | tf_op jit(solution)/shard_map/pallas_call | solution.py:113
  60.1 0.6 collective-permute-start.17
  60.6 0.6 collective-permute-start.18
  61.3 0.0 collective-permute-done.15.refs_0_
  61.3 1.0 %collective-permute-start.16 = (bf16[1,4,64,256]{3,2,1,0:T(8,128)(2,1)S(1)}, bf16[1,4,64,256]{3,2,1,0:T(8,128)(2,1)S(1)}, u32[]{:S(2)}, u32[]{:S(2)}) collective-permute-start(bf16[1,4,64,256]{3,2,1,0:T(8,128)(2,1)S(1)} %get-tuple-element.102), channel_id=1, source_target_pairs={{0,1},{1,0},{2,3},{3,2},{4,5},{5,4},{6,7},{7,6},{8,9},{9,8},{10,11... | collective-permute-start | bytes 393224 | tf_op jit(solution)/shard_map/ppermute | solution.py:147
  62.3 9.0 %all_to_all.10.parts2 = f32[16,1,128]{2,1,0:T(1,128)S(1)} all-to-all(f32[16,1,128]{2,1,0:T(1,128)S(1)} %get-tuple-element.97), channel_id=1, replica_groups=mesh['grp'=2,'blk'=4,'op'=4] {'blk','op'}, dimensions={0} | all-to-all | bytes 16384 | tf_op jit(solution)/shard_map/all_to_all | solution.py:677
  71.2 0.0 collective-permute-done.18.refs_3_
  71.2 0.0 collective-permute-done.17.refs_2_
  71.2 0.0 collective-permute-done.16.refs_1_
  71.2 2.5 %shard_map.109 = (bf16[4,64,512]{2,1,0:T(8,128)(2,1)}, bf16[4,64,512]{2,1,0:T(8,128)(2,1)}, f32[1]{0:T(128)}) custom-call(s32[4]{0:T(128)S(1)} %get-tuple-element.65.slots, f32[16,1,128]{2,1,0:T(1,128)S(1)} %all-to-all-done.refs_1_.parts1, f32[16,1,128]{2,1,0:T(1,128)S(1)} %all_to_all.10.parts2, f32[4,256,128]{2,1,0:T(8,128)S(1)} %get-tuple-element.87.refs_8_.diag.refs_4_, ...), custom_call_target="tpu_custom_call" | custom-call | bytes 4194304 | tf_op jit(solution)/shard_map/pallas_call | solution.py:113
Async XLA Ops:
  0.6 12.8 %collective-permute-start.1 = (bf16[2,256,256]{2,1,0:T(8,128)(2,1)}, bf16[2,256,256]{2,1,0:T(8,128)(2,1)S(1)}, u32[]{:S(2)}, u32[]{:S(2)}) collective-permute-start(bf16[2,256,256]{2,1,0:T(8,128)(2,1)} %bitcast.2), channel_id=1, source_target_pairs={{0,4},{4,12},{12,8},{8,0},{1,5},{5,13},{13,9},{9,1},{2,6},{6,14},{... | collective-permute-start | bytes 786440 | tf_op jit(solution)/shard_map/ppermute | solution.py:143
  3.7 9.8 %collective-permute-start = (bf16[2,256,256]{2,1,0:T(8,128)(2,1)}, bf16[2,256,256]{2,1,0:T(8,128)(2,1)S(1)}, u32[]{:S(2)}, u32[]{:S(2)}) collective-permute-start(bf16[2,256,256]{2,1,0:T(8,128)(2,1)} %bitcast.3), channel_id=1, source_target_pairs={{0,2},{1,3},{2,0},{3,1},{4,6},{5,7},{6,4},{7,5},{8,10},{9,11},{10,... | collective-permute-start | bytes 786440 | tf_op jit(solution)/shard_map/ppermute | solution.py:147
  5.2 1.3 %collective-permute-start.2 = (s32[2]{0:T(128)}, s32[2]{0:T(128)S(1)}, u32[]{:S(2)}, u32[]{:S(2)}) collective-permute-start(s32[2]{0:T(128)} %shift.1), channel_id=1, source_target_pairs={{0,1},{1,0},{2,3},{3,2},{4,5},{5,4},{6,7},{7,6},{8,9},{9,8},{10,11... | collective-permute-start | bytes 32 | tf_op jit(solution)/shard_map/ppermute | solution.py:147
  6.5 0.7 copy-start.3
  9.0 4.4 %collective-permute-start.3 = (bf16[144,256]{1,0:T(8,128)(2,1)S(1)}, bf16[144,256]{1,0:T(8,128)(2,1)S(1)}, u32[]{:S(2)}, u32[]{:S(2)}) collective-permute-start(bf16[144,256]{1,0:T(8,128)(2,1)S(1)} %get-tuple-element.55), channel_id=1, source_target_pairs={{0,2},{1,3},{2,0},{3,1},{4,6},{5,7},{6,4},{7,5},{8,10},{9,11},{10,... | collective-permute-start | bytes 221192 | tf_op jit(solution)/shard_map/ppermute | solution.py:147
  13.5 9.9 %collective-permute-start.5 = (bf16[2,256,256]{2,1,0:T(8,128)(2,1)S(1)}, bf16[2,256,256]{2,1,0:T(8,128)(2,1)S(1)}, u32[]{:S(2)}, u32[]{:S(2)}) collective-permute-start(bf16[2,256,256]{2,1,0:T(8,128)(2,1)S(1)} %collective-permute-done.1.refs_2_), channel_id=1, source_target_pairs={{0,4},{4,12},{12,8},{8,0},{1,5},{5,13},{13,9},{9,1},{2,6},{6,14},{... | collective-permute-start | bytes 786440 | tf_op jit(solution)/shard_map/ppermute | solution.py:143
  16.1 7.3 %collective-permute-start.4 = (bf16[2,256,256]{2,1,0:T(8,128)(2,1)S(1)}, bf16[2,256,256]{2,1,0:T(8,128)(2,1)S(1)}, u32[]{:S(2)}, u32[]{:S(2)}) collective-permute-start(bf16[2,256,256]{2,1,0:T(8,128)(2,1)S(1)} %collective-permute-done.1.refs_2_), channel_id=1, source_target_pairs={{0,2},{1,3},{2,0},{3,1},{4,6},{5,7},{6,4},{7,5},{8,10},{9,11},{10,... | collective-permute-start | bytes 786440 | tf_op jit(solution)/shard_map/ppermute | solution.py:147
  17.4 6.0 %collective-permute-start.6 = (bf16[256,128]{1,0:T(8,128)(2,1)S(1)}, bf16[256,128]{1,0:T(8,128)(2,1)S(1)}, u32[]{:S(2)}, u32[]{:S(2)}) collective-permute-start(bf16[256,128]{1,0:T(8,128)(2,1)S(1)} %get-tuple-element.57), channel_id=1, source_target_pairs={{0,4},{4,12},{12,8},{8,0},{1,5},{5,13},{13,9},{9,1},{2,6},{6,14},{... | collective-permute-start | bytes 196616 | tf_op jit(solution)/shard_map/ppermute | solution.py:143
  17.8 0.7 copy-start.1
  18.5 0.7 copy-start.2
  19.2 0.7 copy-start.4
  19.8 0.7 copy-start.5
  23.4 9.0 %collective-permute-start.8 = (bf16[2,256,256]{2,1,0:T(8,128)(2,1)S(1)}, bf16[2,256,256]{2,1,0:T(8,128)(2,1)S(1)}, u32[]{:S(2)}, u32[]{:S(2)}) collective-permute-start(bf16[2,256,256]{2,1,0:T(8,128)(2,1)S(1)} %collective-permute-done.5.refs_0_), channel_id=1, source_target_pairs={{0,4},{4,12},{12,8},{8,0},{1,5},{5,13},{13,9},{9,1},{2,6},{6,14},{... | collective-permute-start | bytes 786440 | tf_op jit(solution)/shard_map/ppermute | solution.py:143
  25.1 7.3 %collective-permute-start.7 = (bf16[2,256,256]{2,1,0:T(8,128)(2,1)S(1)}, bf16[2,256,256]{2,1,0:T(8,128)(2,1)S(1)}, u32[]{:S(2)}, u32[]{:S(2)}) collective-permute-start(bf16[2,256,256]{2,1,0:T(8,128)(2,1)S(1)} %collective-permute-done.5.refs_0_), channel_id=1, source_target_pairs={{0,2},{1,3},{2,0},{3,1},{4,6},{5,7},{6,4},{7,5},{8,10},{9,11},{10,... | collective-permute-start | bytes 786440 | tf_op jit(solution)/shard_map/ppermute | solution.py:147
  26.4 6.0 %collective-permute-start.10 = (bf16[256,128]{1,0:T(8,128)(2,1)S(1)}, bf16[256,128]{1,0:T(8,128)(2,1)S(1)}, u32[]{:S(2)}, u32[]{:S(2)}) collective-permute-start(bf16[256,128]{1,0:T(8,128)(2,1)S(1)} %get-tuple-element.70), channel_id=1, source_target_pairs={{0,8},{4,0},{12,4},{8,12},{1,9},{5,1},{13,5},{9,13},{2,10},{6,2},{... | collective-permute-start | bytes 196616 | tf_op jit(solution)/shard_map/ppermute | solution.py:143
  27.6 4.7 %collective-permute-start.9 = (bf16[256,128]{1,0:T(8,128)(2,1)S(1)}, bf16[256,128]{1,0:T(8,128)(2,1)S(1)}, u32[]{:S(2)}, u32[]{:S(2)}) collective-permute-start(bf16[256,128]{1,0:T(8,128)(2,1)S(1)} %collective-permute-done.6.refs_7_), channel_id=1, source_target_pairs={{0,1},{1,0},{2,3},{3,2},{4,5},{5,4},{6,7},{7,6},{8,9},{9,8},{10,11... | collective-permute-start | bytes 196616 | tf_op jit(solution)/shard_map/ppermute | solution.py:147
  32.4 8.3 %collective-permute-start.11 = (bf16[2,256,256]{2,1,0:T(8,128)(2,1)S(1)}, bf16[2,256,256]{2,1,0:T(8,128)(2,1)S(1)}, u32[]{:S(2)}, u32[]{:S(2)}) collective-permute-start(bf16[2,256,256]{2,1,0:T(8,128)(2,1)S(1)} %collective-permute-done.8.refs_2_), channel_id=1, source_target_pairs={{0,2},{1,3},{2,0},{3,1},{4,6},{5,7},{6,4},{7,5},{8,10},{9,11},{10,... | collective-permute-start | bytes 786440 | tf_op jit(solution)/shard_map/ppermute | solution.py:147
  33.8 6.8 %collective-permute-start.13 = (bf16[256,256]{1,0:T(8,128)(2,1)S(1)}, bf16[256,256]{1,0:T(8,128)(2,1)S(1)}, u32[]{:S(2)}, u32[]{:S(2)}) collective-permute-start(bf16[256,256]{1,0:T(8,128)(2,1)S(1)} %get-tuple-element.82), channel_id=1, source_target_pairs={{0,12},{4,8},{12,0},{8,4},{1,13},{5,9},{13,1},{9,5},{2,14},{6,10},... | collective-permute-start | bytes 393224 | tf_op jit(solution)/shard_map/ppermute | solution.py:143
  35.8 4.8 %collective-permute-start.12 = (bf16[256,128]{1,0:T(8,128)(2,1)S(1)}, bf16[256,128]{1,0:T(8,128)(2,1)S(1)}, u32[]{:S(2)}, u32[]{:S(2)}) collective-permute-start(bf16[256,128]{1,0:T(8,128)(2,1)S(1)} %collective-permute-done.10.refs_5_), channel_id=1, source_target_pairs={{0,1},{1,0},{2,3},{3,2},{4,5},{5,4},{6,7},{7,6},{8,9},{9,8},{10,11... | collective-permute-start | bytes 196616 | tf_op jit(solution)/shard_map/ppermute | solution.py:147
  35.8 1.0 %copy-start = (bf16[2,1,256,256]{3,2,1,0:T(8,128)(2,1)S(1)}, bf16[2,1,256,256]{3,2,1,0:T(8,128)(2,1)}, u32[]{:S(2)}) copy-start(bf16[2,1,256,256]{3,2,1,0:T(8,128)(2,1)} %param.9) | copy-start | bytes 786436
  44.1 4.4 %collective-permute-start.14 = (bf16[4,256,256]{2,1,0:T(8,128)(2,1)S(1)}, bf16[4,256,256]{2,1,0:T(8,128)(2,1)S(1)}, u32[]{:S(2)}, u32[]{:S(2)}) collective-permute-start(bf16[4,256,256]{2,1,0:T(8,128)(2,1)S(1)} %get-tuple-element.95.mine), channel_id=1, source_target_pairs={{0,1},{1,0},{2,3},{3,2},{4,5},{5,4},{6,7},{7,6},{8,9},{9,8},{10,11... | collective-permute-start | bytes 1572872 | tf_op jit(solution)/shard_map/ppermute | solution.py:147
  44.2 10.6 %all-to-all-start = ((f32[16,1,128]{2,1,0:T(1,128)}), f32[16,1,128]{2,1,0:T(1,128)S(1)}, u32[]{:S(2)}, u32[]{:S(2)}) async-start(f32[16,1,128]{2,1,0:T(1,128)} %get-tuple-element.91), calls=%async_computation | async-start | bytes 16384 | tf_op jit(solution)/shard_map/all_to_all | solution.py:677
  48.8 1.0 %copy-start.6 = (f32[4,256,256]{2,1,0:T(8,128)}, f32[4,256,256]{2,1,0:T(8,128)S(1)}, u32[]{:S(2)}) copy-start(f32[4,256,256]{2,1,0:T(8,128)S(1)} %get-tuple-element.96.refs_3_) | copy-start | bytes 3145732
  49.8 11.4 %collective-permute-start.15 = (bf16[2,4,64,256]{3,2,1,0:T(8,128)(2,1)S(1)}, bf16[2,4,64,256]{3,2,1,0:T(8,128)(2,1)S(1)}, u32[]{:S(2)}, u32[]{:S(2)}) collective-permute-start(bf16[2,4,64,256]{3,2,1,0:T(8,128)(2,1)S(1)} %get-tuple-element.100), channel_id=1, source_target_pairs={{0,2},{1,3},{2,0},{3,1},{4,6},{5,7},{6,4},{7,5},{8,10},{9,11},{10,... | collective-permute-start | bytes 786440 | tf_op jit(solution)/shard_map/ppermute | solution.py:147
  54.8 1.2 %copy-start.7 = (f32[4,256,256]{2,1,0:T(8,128)S(1)}, f32[4,256,256]{2,1,0:T(8,128)}, u32[]{:S(2)}) copy-start(f32[4,256,256]{2,1,0:T(8,128)} %copy-done.6) | copy-start | bytes 3145732
  60.1 11.2 %collective-permute-start.17 = (bf16[2,4,64,256]{3,2,1,0:T(8,128)(2,1)S(1)}, bf16[2,4,64,256]{3,2,1,0:T(8,128)(2,1)S(1)}, u32[]{:S(2)}, u32[]{:S(2)}) collective-permute-start(bf16[2,4,64,256]{3,2,1,0:T(8,128)(2,1)S(1)} %get-tuple-element.103), channel_id=1, source_target_pairs={{0,2},{1,3},{2,0},{3,1},{4,6},{5,7},{6,4},{7,5},{8,10},{9,11},{10,... | collective-permute-start | bytes 786440 | tf_op jit(solution)/shard_map/ppermute | solution.py:147
  60.6 10.6 %collective-permute-start.18 = (bf16[1,4,64,256]{3,2,1,0:T(8,128)(2,1)S(1)}, bf16[1,4,64,256]{3,2,1,0:T(8,128)(2,1)S(1)}, u32[]{:S(2)}, u32[]{:S(2)}) collective-permute-start(bf16[1,4,64,256]{3,2,1,0:T(8,128)(2,1)S(1)} %get-tuple-element.104), channel_id=1, source_target_pairs={{0,3},{1,2},{2,1},{3,0},{4,7},{5,6},{6,5},{7,4},{8,11},{9,10},{10,... | collective-permute-start | bytes 393224 | tf_op jit(solution)/shard_map/ppermute | solution.py:147
  61.3 10.0 %collective-permute-start.16 = (bf16[1,4,64,256]{3,2,1,0:T(8,128)(2,1)S(1)}, bf16[1,4,64,256]{3,2,1,0:T(8,128)(2,1)S(1)}, u32[]{:S(2)}, u32[]{:S(2)}) collective-permute-start(bf16[1,4,64,256]{3,2,1,0:T(8,128)(2,1)S(1)} %get-tuple-element.102), channel_id=1, source_target_pairs={{0,1},{1,0},{2,3},{3,2},{4,5},{5,4},{6,7},{7,6},{8,9},{9,8},{10,11... | collective-permute-start | bytes 393224 | tf_op jit(solution)/shard_map/ppermute | solution.py:147

commit v25 on v23

--- a/solution.py
+++ b/solution.py
@@ -126,15 +126,14 @@
 
 def ring_at(place, n_blk):
     place = place % n_blk if isinstance(place, int) else lax.rem(place + n_blk, n_blk)
-    odd, even = 2 * place - 1, 2 * (n_blk - place)
+    even, odd = 2 * place, 2 * (n_blk - place) - 1
     if isinstance(place, int):
-        return 0 if place == 0 else odd if odd < n_blk else even
-    return jnp.where(place == 0, 0, jnp.where(odd < n_blk, odd, even))
+        return even if even < n_blk else odd
+    return jnp.where(even < n_blk, even, odd)
 
 
 def ring_place(index, n_blk):
-    odd, even = (index + 1) // 2, lax.rem(n_blk - index // 2, n_blk)
-    return jnp.where(lax.rem(index, 2) == 1, odd, even)
+    return jnp.where(lax.rem(index, 2) == 1, n_blk - (index + 1) // 2, index // 2)
 
 
 def onward(block, d, n_blk):
@@ -148,7 +147,7 @@
 
 def gather(own, n_blk, n_op, pack, table, early):
     bits = [1 << b for b in reversed(range(1, n_op.bit_length() - 1))]
-    order = sorted(range(1, n_blk), key=lambda d: min(d, n_blk - d))
+    order = sorted(range(1, n_blk), key=lambda d: (min(d, n_blk - d), -d))
     left, psi, right, tables, columns = {(0, 0): own}, {}, None, None, None
     waiting, across, late, made = {(0, 0): 0}, {}, None, None
     for j in range(n_blk + len(bits)):
@@ -176,8 +175,10 @@
         if j == n_blk - 1 and j >= len(bits) + 1:
             n_early = min(2, n_blk - 1)
             psi[0] = [columns[0]]
-            moved["early"] = early(left, psi, n_early, tables)
-        if 2 <= j < n_blk:
+            moved["other"] = swap(psi[order[j - 2]][0], 1, n_op)
+            at_hand = {**psi, order[j - 2]: psi[order[j - 2]] + [moved["other"]]}
+            moved["early"] = early(left, at_hand, n_early, tables)
+        elif 2 <= j < n_blk:
             moved["other"] = swap(psi[order[j - 2]][0], 1, n_op)
         late = onward(columns[order[j]], order[j], n_blk) if j < n_blk - 1 else None
         if not kept:
@@ -593,7 +594,7 @@
     count = float(n_blk * rows * ncols)
     n_dev = n_blk * n_op
     bf16, f32, i32 = jnp.bfloat16, jnp.float32, jnp.int32
-    last = sorted(range(1, n_blk), key=lambda d: min(d, n_blk - d))[-1]
+    last = sorted(range(1, n_blk), key=lambda d: (min(d, n_blk - d), -d))[-1]
 
     def pack():
         first = swap(term_shift, 1, n_op)

time: 72 us -> 71.8 us (level)
  starting transfers between devices: 30.5 us -> 27.4 us
  waiting for transfers between devices: 15.5 us -> 18.4 us
    ppermute x6, starting transfers between devices: 14.3 us -> 12.2 us  [onward(): return lax.ppermute(block, 'blk', pairs)]
    ppermute x6, waiting for transfers between devices: 8.22 us -> 9.89 us  [onward(): return lax.ppermute(block, 'blk', pairs)]
    all_to_all x1, starting transfers between devices: 5.68 us -> 4.29 us  [totals(): return lax.all_to_all(parts, ('blk', 'op'), 0, 0, tiled=True)]
    ppermute x13, waiting for transfers between devices: 3.97 us -> 5.2 us  [swap(): return lax.ppermute(block, 'op', [(i, i ^ e) for i in range(n_op)])]
  transfers between devices with their start and end apart: 20 -> 20, of which waited for: 6 -> 7; matrix products, arithmetic and copies ran while one was open for 0% -> 0% of each run, Pallas kernels for 14% -> 14%
where the time goes in v25:
time: 71.8 us; the launch traced here: 71.5 us
  starting transfers between devices  27.4 us (38%)
  waiting for transfers between devices  18.4 us (26%)
  Pallas kernels  15.2 us (21%)
  blocking collectives  9.72 us (14%)
  between operations  0.76 us (1%)
    pallas_call x7, Pallas kernels, kernel(): pl.pallas_call(body, out_shape=[HBM(shape, dtype) if space == HBM else ja...  15.2 us
    ppermute x6, starting transfers between devices, onward(): return lax.ppermute(block, 'blk', pairs)  12.2 us
    ppermute x13, starting transfers between devices, swap(): return lax.ppermute(block, 'op', [(i, i ^ e) for i in range(n_op)])  10.9 us
    ppermute x6, waiting for transfers between devices, onward(): return lax.ppermute(block, 'blk', pairs)  9.89 us
    all_to_all x1, blocking collectives, totals(): return lax.all_to_all(parts, ('blk', 'op'), 0, 0, tiled=True)  9.72 us
    ppermute x13, waiting for transfers between devices, swap(): return lax.ppermute(block, 'op', [(i, i ^ e) for i in range(n_op)])  5.2 us
    all_to_all x1, starting transfers between devices, totals(): return lax.all_to_all(parts, ('blk', 'op'), 0, 0, tiled=True)  4.29 us
    all_to_all x1, waiting for transfers between devices, totals(): return lax.all_to_all(parts, ('blk', 'op'), 0, 0, tiled=True)  3.36 us
  transfers between devices with their start and end apart: 20, of which 7 were waited for; matrix products, arithmetic and copies ran while one was open for 0% of the time, Pallas kernels for 14%

profile of v25, /device:TPU:0, one launch (start us, length us, event | category | flops | bytes accessed | tf_op | source)
XLA Modules:
  0.0 71.5 jit_solution(9516475917815413928)
XLA Ops:
  0.6 0.0 copy-start.3
  0.6 0.0 copy-start
  0.7 4.1 %collective-permute-start.1 = (bf16[2,256,256]{2,1,0:T(8,128)(2,1)}, bf16[2,256,256]{2,1,0:T(8,128)(2,1)S(1)}, u32[]{:S(2)}, u32[]{:S(2)}) collective-permute-start(bf16[2,256,256]{2,1,0:T(8,128)(2,1)} %bitcast.2), channel_id=1, source_target_pairs={{0,8},{8,12},{12,4},{4,0},{1,9},{9,13},{13,5},{5,1},{2,10},{10,14}... | collective-permute-start | bytes 786440 | tf_op jit(solution)/shard_map/ppermute | solution.py:141
  4.7 0.0 copy-done.3
  4.7 0.0 collective-permute-start.2
  4.7 1.1 %collective-permute-done.2._ = s32[2]{0:T(128)S(1)} collective-permute-done((s32[2]{0:T(128)S(1)}, s32[2]{0:T(128)S(1)}, u32[]{:S(2)}, u32[]{:S(2)}) %collective-permute-start.2) | collective-permute-done | bytes 40 | tf_op jit(solution)/shard_map/ppermute | solution.py:145
  5.9 1.9 %shard_map.103 = (bf16[256,256]{1,0:T(8,128)(2,1)S(1)}, bf16[256,128]{1,0:T(8,128)(2,1)S(1)}, bf16[256,256]{1,0:T(8,128)(2,1)S(1)}, bf16[256,128]{1,0:T(8,128)(2...) custom-call(s32[2]{0:T(128)S(1)} %copy-done.3, s32[2]{0:T(128)S(1)} %collective-permute-done.2._, ...), custom_call_target="tpu_custom_call" | custom-call | bytes 1048576 | tf_op jit(solution)/shard_map/pallas_call | solution.py:113
  7.8 1.6 %collective-permute-start.3 = (bf16[144,256]{1,0:T(8,128)(2,1)S(1)}, bf16[144,256]{1,0:T(8,128)(2,1)S(1)}, u32[]{:S(2)}, u32[]{:S(2)}) collective-permute-start(bf16[144,256]{1,0:T(8,128)(2,1)S(1)} %get-tuple-element.58), channel_id=1, source_target_pairs={{0,2},{1,3},{2,0},{3,1},{4,6},{5,7},{6,4},{7,5},{8,10},{9,11},{10,... | collective-permute-start | bytes 221192 | tf_op jit(solution)/shard_map/ppermute | solution.py:145
  9.3 0.0 copy-done
  9.3 0.5 collective-permute-start
  9.9 2.8 %collective-permute-done.3.refs_1_.refs_5_ = bf16[144,256]{1,0:T(8,128)(2,1)S(1)} collective-permute-done((bf16[144,256]{1,0:T(8,128)(2,1)S(1)}, bf16[144,256]{1,0:T(8,128)(2,1)S(1)}, u32[]{:S(2)}, u32[]{:S(2)}) %collective-permute-start.3) | collective-permute-done | bytes 73760 | tf_op jit(solution)/shard_map/ppermute | solution.py:145
  12.7 0.0 collective-permute-done.1.refs_2_
  12.7 0.0 copy-start.1
  12.7 0.0 copy-start.2
  12.7 0.0 copy-start.4
  12.7 0.0 copy-start.5
  12.7 1.6 %collective-permute-start.4 = (bf16[2,256,256]{2,1,0:T(8,128)(2,1)S(1)}, bf16[2,256,256]{2,1,0:T(8,128)(2,1)S(1)}, u32[]{:S(2)}, u32[]{:S(2)}) collective-permute-start(bf16[2,256,256]{2,1,0:T(8,128)(2,1)S(1)} %collective-permute-done.1.refs_2_), channel_id=1, source_target_pairs={{0,8},{8,12},{12,4},{4,0},{1,9},{9,13},{13,5},{5,1},{2,10},{10,14}... | collective-permute-start | bytes 786440 | tf_op jit(solution)/shard_map/ppermute | solution.py:141
  14.3 0.5 collective-permute-start.5
  14.8 1.8 %collective-permute-start.7 = (bf16[2,256,256]{2,1,0:T(8,128)(2,1)S(1)}, bf16[2,256,256]{2,1,0:T(8,128)(2,1)S(1)}, u32[]{:S(2)}, u32[]{:S(2)}) collective-permute-start(bf16[2,256,256]{2,1,0:T(8,128)(2,1)S(1)} %collective-permute-done.1.refs_2_), channel_id=1, source_target_pairs={{0,2},{1,3},{2,0},{3,1},{4,6},{5,7},{6,4},{7,5},{8,10},{9,11},{10,... | collective-permute-start | bytes 786440 | tf_op jit(solution)/shard_map/ppermute | solution.py:145
  16.6 0.0 copy-done.1
  16.6 0.0 copy-done.2
  16.6 0.0 copy-done.4
  16.6 0.0 copy-done.5
  16.6 1.3 %shard_map.104 = (s32[16]{0:T(128)S(1)}, s32[4]{0:T(128)S(1)}, s32[4]{0:T(128)S(1)}, f32[4,256,128]{2,1,0:T(8,128)S(1)}, f32[1,512]{1,0:T(1,128)S(1)}) custom-call(s32[4]{0:T(128)S(1)} %copy-done.4, s32[4]{0:T(128)S(1)} %copy-done.5, f32[4,256]{1,0:T(4,128)S(1)} %copy-done.1, f32[1,512]{1,0:T(1,128)S(1)} %bitcast.5, ...), custom_call_target="tpu_custom_call" | custom-call | tf_op jit(solution)/shard_map/pallas_call | solution.py:113
  17.9 3.9 %collective-permute-done.5.refs_7_ = bf16[256,128]{1,0:T(8,128)(2,1)S(1)} collective-permute-done((bf16[256,128]{1,0:T(8,128)(2,1)S(1)}, bf16[256,128]{1,0:T(8,128)(2,1)S(1)}, u32[]{:S(2)}, u32[]{:S(2)}) %collective-permute-start.5) | collective-permute-done | bytes 65568 | tf_op jit(solution)/shard_map/ppermute | solution.py:141
  21.9 0.0 collective-permute-done.refs_1_
  21.9 0.0 collective-permute-done.4.refs_0_
  21.9 1.3 %collective-permute-start.8 = (bf16[2,256,256]{2,1,0:T(8,128)(2,1)S(1)}, bf16[2,256,256]{2,1,0:T(8,128)(2,1)S(1)}, u32[]{:S(2)}, u32[]{:S(2)}) collective-permute-start(bf16[2,256,256]{2,1,0:T(8,128)(2,1)S(1)} %collective-permute-done.4.refs_0_), channel_id=1, source_target_pairs={{0,8},{8,12},{12,4},{4,0},{1,9},{9,13},{13,5},{5,1},{2,10},{10,14}... | collective-permute-start | bytes 786440 | tf_op jit(solution)/shard_map/ppermute | solution.py:141
  23.1 2.0 %collective-permute-start.10 = (bf16[256,128]{1,0:T(8,128)(2,1)S(1)}, bf16[256,128]{1,0:T(8,128)(2,1)S(1)}, u32[]{:S(2)}, u32[]{:S(2)}) collective-permute-start(bf16[256,128]{1,0:T(8,128)(2,1)S(1)} %get-tuple-element.73), channel_id=1, source_target_pairs={{0,8},{8,12},{12,4},{4,0},{1,9},{9,13},{13,5},{5,1},{2,10},{10,14}... | collective-permute-start | bytes 196616 | tf_op jit(solution)/shard_map/ppermute | solution.py:141
  25.1 0.0 collective-permute-start.9
  25.1 1.5 %collective-permute-start.6 = (bf16[2,256,256]{2,1,0:T(8,128)(2,1)S(1)}, bf16[2,256,256]{2,1,0:T(8,128)(2,1)S(1)}, u32[]{:S(2)}, u32[]{:S(2)}) collective-permute-start(bf16[2,256,256]{2,1,0:T(8,128)(2,1)S(1)} %collective-permute-done.4.refs_0_), channel_id=1, source_target_pairs={{0,2},{1,3},{2,0},{3,1},{4,6},{5,7},{6,4},{7,5},{8,10},{9,11},{10,... | collective-permute-start | bytes 786440 | tf_op jit(solution)/shard_map/ppermute | solution.py:145
  26.6 4.8 %collective-permute-done.10.refs_5_ = bf16[256,128]{1,0:T(8,128)(2,1)S(1)} collective-permute-done((bf16[256,128]{1,0:T(8,128)(2,1)S(1)}, bf16[256,128]{1,0:T(8,128)(2,1)S(1)}, u32[]{:S(2)}, u32[]{:S(2)}) %collective-permute-start.10) | collective-permute-done | bytes 65568 | tf_op jit(solution)/shard_map/ppermute | solution.py:141
  31.4 0.0 collective-permute-done.7.refs_3_
  31.4 0.0 collective-permute-done.9.refs_8_
  31.4 0.0 collective-permute-done.8.refs_2_
  31.4 1.3 %collective-permute-start.13 = (bf16[2,256,256]{2,1,0:T(8,128)(2,1)S(1)}, bf16[2,256,256]{2,1,0:T(8,128)(2,1)S(1)}, u32[]{:S(2)}, u32[]{:S(2)}) collective-permute-start(bf16[2,256,256]{2,1,0:T(8,128)(2,1)S(1)} %collective-permute-done.8.refs_2_), channel_id=1, source_target_pairs={{0,2},{1,3},{2,0},{3,1},{4,6},{5,7},{6,4},{7,5},{8,10},{9,11},{10,... | collective-permute-start | bytes 786440 | tf_op jit(solution)/shard_map/ppermute | solution.py:145
  32.7 2.8 %collective-permute-start.12 = (bf16[256,256]{1,0:T(8,128)(2,1)S(1)}, bf16[256,256]{1,0:T(8,128)(2,1)S(1)}, u32[]{:S(2)}, u32[]{:S(2)}) collective-permute-start(bf16[256,256]{1,0:T(8,128)(2,1)S(1)} %get-tuple-element.80), channel_id=1, source_target_pairs={{0,12},{8,4},{12,0},{4,8},{1,13},{9,5},{13,1},{5,9},{2,14},{10,6},... | collective-permute-start | bytes 393224 | tf_op jit(solution)/shard_map/ppermute | solution.py:141
  35.5 0.0 collective-permute-start.11
  35.5 1.3 %collective-permute-done.11.refs_6_ = bf16[256,128]{1,0:T(8,128)(2,1)S(1)} collective-permute-done((bf16[256,128]{1,0:T(8,128)(2,1)S(1)}, bf16[256,128]{1,0:T(8,128)(2,1)S(1)}, u32[]{:S(2)}, u32[]{:S(2)}) %collective-permute-start.11) | collective-permute-done | bytes 65568 | tf_op jit(solution)/shard_map/ppermute | solution.py:145
  36.8 1.7 %shard_map.105 = (bf16[2,256,256]{2,1,0:T(8,128)(2,1)S(1)}, bf16[2,4,256,256]{3,2,1,0:T(8,128)(2,1)S(1)}, bf16[2,2,2,256,256]{4,3,2,1,0:T(8,128)(2,1)}) custom-call(s32[4]{0:T(128)S(1)} %get-tuple-element.69.widths, bf16[2,256,256]{2,1,0:T(8,128)(2,1)S(1)} %bitcast.4, bf16[2,256,256]{2,1,0:T(8,128)(2,1)S(1)} %collective-permute-done.refs_1_, ...), custom_call_target="tpu_custom_call" | custom-call | flops 268435456 | bytes 4194304 | tf_op jit(solution)/shard_map/pallas_call | solution.py:113
  38.5 1.1 %collective-permute-done.12.refs_6_ = bf16[256,256]{1,0:T(8,128)(2,1)S(1)} collective-permute-done((bf16[256,256]{1,0:T(8,128)(2,1)S(1)}, bf16[256,256]{1,0:T(8,128)(2,1)S(1)}, u32[]{:S(2)}, u32[]{:S(2)}) %collective-permute-start.12) | collective-permute-done | bytes 131104 | tf_op jit(solution)/shard_map/ppermute | solution.py:141
  39.6 0.0 collective-permute-done.6.refs_1_
  39.6 0.0 collective-permute-done.13.refs_3_
  39.6 3.0 %shard_map.106 = (bf16[4,256,256]{2,1,0:T(8,128)(2,1)S(1)}, bf16[4,256,256]{2,1,0:T(8,128)(2,1)S(1)}, bf16[2,2,2,256,256]{4,3,2,1,0:T(8,128)(2,1)}, f32[16,1,128]{2,1,0:T(1,128)}) custom-call(s32[16]{0:T(128)S(1)} %get-tuple-element.68.src, s32[4]{0:T(128)S(1)} %get-tuple-element.69.widths, bf16[2,256,256]{2,1,0:T(8,128)(2,1)S(1)} %collective-permute-done.4.refs_0_, ...), custom_call_target="tpu_custom_call" | custom-call | flops 1073741824 | bytes 6291456 | tf_op jit(solution)/shard_map/pallas_call | solution.py:113
  42.7 0.1 collective-permute-start.14
  42.7 4.3 %all-to-all-start = ((f32[16,1,128]{2,1,0:T(1,128)}), f32[16,1,128]{2,1,0:T(1,128)S(1)}, u32[]{:S(2)}, u32[]{:S(2)}) async-start(f32[16,1,128]{2,1,0:T(1,128)} %get-tuple-element.89), calls=%async_computation | async-start | bytes 16384 | tf_op jit(solution)/shard_map/all_to_all | solution.py:660
  47.0 0.0 collective-permute-done.14.other
  47.0 1.0 %shard_map.107 = (f32[4,256,256]{2,1,0:T(8,128)S(1)}, bf16[2,4,64,256]{3,2,1,0:T(8,128)(2,1)}) custom-call(bf16[4,256,256]{2,1,0:T(8,128)(2,1)S(1)} %get-tuple-element.93.mine, bf16[4,256,256]{2,1,0:T(8,128)(2,1)S(1)} %collective-permute-done.14.other, bf16[4,256,256]{2,1,0:T(8,128)(2,1)S(1)} %get-tuple-element.92.raw_in.refs_3_, ...), custom_call_target="tpu_custom_call" | custom-call | bytes 4194304 | tf_op jit(solution)/shard_map/pallas_call | solution.py:113
  48.1 1.9 %collective-permute-start.15 = (bf16[2,4,64,256]{3,2,1,0:T(8,128)(2,1)}, bf16[2,4,64,256]{3,2,1,0:T(8,128)(2,1)S(1)}, u32[]{:S(2)}, u32[]{:S(2)}) collective-permute-start(bf16[2,4,64,256]{3,2,1,0:T(8,128)(2,1)} %get-tuple-element.98), channel_id=1, source_target_pairs={{0,2},{1,3},{2,0},{3,1},{4,6},{5,7},{6,4},{7,5},{8,10},{9,11},{10,... | collective-permute-start | bytes 786440 | tf_op jit(solution)/shard_map/ppermute | solution.py:145
  50.0 3.4 %all-to-all-done.refs_2_.parts1 = f32[16,1,128]{2,1,0:T(1,128)S(1)} async-done(((f32[16,1,128]{2,1,0:T(1,128)}), f32[16,1,128]{2,1,0:T(1,128)S(1)}, u32[]{:S(2)}, u32[]{:S(2)}) %all-to-all-start) | async-done | bytes 8224 | tf_op jit(solution)/shard_map/all_to_all | solution.py:660
  53.4 4.2 %shard_map.108 = (f32[16,1,128]{2,1,0:T(1,128)S(1)}, bf16[4,4,64,256]{3,2,1,0:T(8,128)(2,1)S(1)}, bf16[1,4,64,256]{3,2,1,0:T(8,128)(2,1)S(1)}, bf16[2,4,64,256]{...) custom-call(s32[16]{0:T(128)S(1)} %get-tuple-element.68.src, s32[4]{0:T(128)S(1)} %get-tuple-element.69.widths, ...), custom_call_target="tpu_custom_call" | custom-call | flops 4294967296 | bytes 25165824 | tf_op jit(solution)/shard_map/pallas_call | solution.py:113
  57.6 0.6 collective-permute-start.17
  58.2 0.6 collective-permute-start.18
  58.8 0.0 collective-permute-done.15.refs_0_
  58.8 1.0 %collective-permute-start.16 = (bf16[1,4,64,256]{3,2,1,0:T(8,128)(2,1)S(1)}, bf16[1,4,64,256]{3,2,1,0:T(8,128)(2,1)S(1)}, u32[]{:S(2)}, u32[]{:S(2)}) collective-permute-start(bf16[1,4,64,256]{3,2,1,0:T(8,128)(2,1)S(1)} %get-tuple-element.100), channel_id=1, source_target_pairs={{0,1},{1,0},{2,3},{3,2},{4,5},{5,4},{6,7},{7,6},{8,9},{9,8},{10,11... | collective-permute-start | bytes 393224 | tf_op jit(solution)/shard_map/ppermute | solution.py:145
  59.8 9.7 %all_to_all.10.parts2 = f32[16,1,128]{2,1,0:T(1,128)S(1)} all-to-all(f32[16,1,128]{2,1,0:T(1,128)S(1)} %get-tuple-element.95), channel_id=1, replica_groups=mesh['grp'=2,'blk'=4,'op'=4] {'blk','op'}, dimensions={0} | all-to-all | bytes 16384 | tf_op jit(solution)/shard_map/all_to_all | solution.py:660
  69.5 0.0 collective-permute-done.18.refs_3_
  69.5 0.0 collective-permute-done.17.refs_2_
  69.5 0.0 collective-permute-done.16.refs_1_
  69.5 2.0 %shard_map.109 = (bf16[4,64,512]{2,1,0:T(8,128)(2,1)}, bf16[4,64,512]{2,1,0:T(8,128)(2,1)}, f32[1]{0:T(128)}) custom-call(s32[4]{0:T(128)S(1)} %get-tuple-element.67.slots, f32[16,1,128]{2,1,0:T(1,128)S(1)} %all-to-all-done.refs_2_.parts1, f32[16,1,128]{2,1,0:T(1,128)S(1)} %all_to_all.10.parts2, f32[4,256,128]{2,1,0:T(8,128)S(1)} %get-tuple-element.87.refs_11_.diag.refs_5_, ...), custom_call_target="tpu_custom_call" | custom-call | bytes 4194304 | tf_op jit(solution)/shard_map/pallas_call | solution.py:113
Async XLA Ops:
  0.6 4.1 %copy-start.3 = (s32[2]{0:T(128)S(1)}, s32[2]{0:T(128)}, u32[]{:S(2)}) copy-start(s32[2]{0:T(128)} %shift.1) | copy-start | bytes 28
  0.6 8.7 %copy-start = (bf16[2,1,256,256]{3,2,1,0:T(8,128)(2,1)S(1)}, bf16[2,1,256,256]{3,2,1,0:T(8,128)(2,1)}, u32[]{:S(2)}) copy-start(bf16[2,1,256,256]{3,2,1,0:T(8,128)(2,1)} %param.9) | copy-start | bytes 786436
  0.7 12.0 %collective-permute-start.1 = (bf16[2,256,256]{2,1,0:T(8,128)(2,1)}, bf16[2,256,256]{2,1,0:T(8,128)(2,1)S(1)}, u32[]{:S(2)}, u32[]{:S(2)}) collective-permute-start(bf16[2,256,256]{2,1,0:T(8,128)(2,1)} %bitcast.2), channel_id=1, source_target_pairs={{0,8},{8,12},{12,4},{4,0},{1,9},{9,13},{13,5},{5,1},{2,10},{10,14}... | collective-permute-start | bytes 786440 | tf_op jit(solution)/shard_map/ppermute | solution.py:141
  4.7 1.1 %collective-permute-start.2 = (s32[2]{0:T(128)S(1)}, s32[2]{0:T(128)S(1)}, u32[]{:S(2)}, u32[]{:S(2)}) collective-permute-start(s32[2]{0:T(128)S(1)} %copy-done.3), channel_id=1, source_target_pairs={{0,1},{1,0},{2,3},{3,2},{4,5},{5,4},{6,7},{7,6},{8,9},{9,8},{10,11... | collective-permute-start | bytes 32 | tf_op jit(solution)/shard_map/ppermute | solution.py:145
  7.8 4.9 %collective-permute-start.3 = (bf16[144,256]{1,0:T(8,128)(2,1)S(1)}, bf16[144,256]{1,0:T(8,128)(2,1)S(1)}, u32[]{:S(2)}, u32[]{:S(2)}) collective-permute-start(bf16[144,256]{1,0:T(8,128)(2,1)S(1)} %get-tuple-element.58), channel_id=1, source_target_pairs={{0,2},{1,3},{2,0},{3,1},{4,6},{5,7},{6,4},{7,5},{8,10},{9,11},{10,... | collective-permute-start | bytes 221192 | tf_op jit(solution)/shard_map/ppermute | solution.py:145
  9.3 12.5 %collective-permute-start = (bf16[2,256,256]{2,1,0:T(8,128)(2,1)S(1)}, bf16[2,256,256]{2,1,0:T(8,128)(2,1)S(1)}, u32[]{:S(2)}, u32[]{:S(2)}) collective-permute-start(bf16[2,256,256]{2,1,0:T(8,128)(2,1)S(1)} %bitcast.3), channel_id=1, source_target_pairs={{0,2},{1,3},{2,0},{3,1},{4,6},{5,7},{6,4},{7,5},{8,10},{9,11},{10,... | collective-permute-start | bytes 786440 | tf_op jit(solution)/shard_map/ppermute | solution.py:145
  12.7 3.9 %copy-start.1 = (f32[4,256]{1,0:T(4,128)S(1)}, f32[4,256]{1,0:T(4,128)}, u32[]{:S(2)}) copy-start(f32[4,256]{1,0:T(4,128)} %left_diag.1) | copy-start | bytes 12292
  12.7 3.9 %copy-start.2 = (f32[512]{0:T(512)S(1)}, f32[512]{0:T(512)}, u32[]{:S(2)}) copy-start(f32[512]{0:T(512)} %param.15) | copy-start | bytes 6148
  12.7 3.9 %copy-start.4 = (s32[4]{0:T(128)S(1)}, s32[4]{0:T(128)}, u32[]{:S(2)}) copy-start(s32[4]{0:T(128)} %sector.1) | copy-start | bytes 52
  12.7 3.9 %copy-start.5 = (s32[4]{0:T(128)S(1)}, s32[4]{0:T(128)}, u32[]{:S(2)}) copy-start(s32[4]{0:T(128)} %width.1) | copy-start | bytes 52
  12.7 9.2 %collective-permute-start.4 = (bf16[2,256,256]{2,1,0:T(8,128)(2,1)S(1)}, bf16[2,256,256]{2,1,0:T(8,128)(2,1)S(1)}, u32[]{:S(2)}, u32[]{:S(2)}) collective-permute-start(bf16[2,256,256]{2,1,0:T(8,128)(2,1)S(1)} %collective-permute-done.1.refs_2_), channel_id=1, source_target_pairs={{0,8},{8,12},{12,4},{4,0},{1,9},{9,13},{13,5},{5,1},{2,10},{10,14}... | collective-permute-start | bytes 786440 | tf_op jit(solution)/shard_map/ppermute | solution.py:141
  14.3 7.5 %collective-permute-start.5 = (bf16[256,128]{1,0:T(8,128)(2,1)S(1)}, bf16[256,128]{1,0:T(8,128)(2,1)S(1)}, u32[]{:S(2)}, u32[]{:S(2)}) collective-permute-start(bf16[256,128]{1,0:T(8,128)(2,1)S(1)} %get-tuple-element.56), channel_id=1, source_target_pairs={{0,4},{8,0},{12,8},{4,12},{1,5},{9,1},{13,9},{5,13},{2,6},{10,2},{... | collective-permute-start | bytes 196616 | tf_op jit(solution)/shard_map/ppermute | solution.py:141
  14.8 16.6 %collective-permute-start.7 = (bf16[2,256,256]{2,1,0:T(8,128)(2,1)S(1)}, bf16[2,256,256]{2,1,0:T(8,128)(2,1)S(1)}, u32[]{:S(2)}, u32[]{:S(2)}) collective-permute-start(bf16[2,256,256]{2,1,0:T(8,128)(2,1)S(1)} %collective-permute-done.1.refs_2_), channel_id=1, source_target_pairs={{0,2},{1,3},{2,0},{3,1},{4,6},{5,7},{6,4},{7,5},{8,10},{9,11},{10,... | collective-permute-start | bytes 786440 | tf_op jit(solution)/shard_map/ppermute | solution.py:145
  21.9 9.5 %collective-permute-start.8 = (bf16[2,256,256]{2,1,0:T(8,128)(2,1)S(1)}, bf16[2,256,256]{2,1,0:T(8,128)(2,1)S(1)}, u32[]{:S(2)}, u32[]{:S(2)}) collective-permute-start(bf16[2,256,256]{2,1,0:T(8,128)(2,1)S(1)} %collective-permute-done.4.refs_0_), channel_id=1, source_target_pairs={{0,8},{8,12},{12,4},{4,0},{1,9},{9,13},{13,5},{5,1},{2,10},{10,14}... | collective-permute-start | bytes 786440 | tf_op jit(solution)/shard_map/ppermute | solution.py:141
  23.1 8.3 %collective-permute-start.10 = (bf16[256,128]{1,0:T(8,128)(2,1)S(1)}, bf16[256,128]{1,0:T(8,128)(2,1)S(1)}, u32[]{:S(2)}, u32[]{:S(2)}) collective-permute-start(bf16[256,128]{1,0:T(8,128)(2,1)S(1)} %get-tuple-element.73), channel_id=1, source_target_pairs={{0,8},{8,12},{12,4},{4,0},{1,9},{9,13},{13,5},{5,1},{2,10},{10,14}... | collective-permute-start | bytes 196616 | tf_op jit(solution)/shard_map/ppermute | solution.py:141
  25.1 6.3 %collective-permute-start.9 = (bf16[256,128]{1,0:T(8,128)(2,1)S(1)}, bf16[256,128]{1,0:T(8,128)(2,1)S(1)}, u32[]{:S(2)}, u32[]{:S(2)}) collective-permute-start(bf16[256,128]{1,0:T(8,128)(2,1)S(1)} %collective-permute-done.5.refs_7_), channel_id=1, source_target_pairs={{0,1},{1,0},{2,3},{3,2},{4,5},{5,4},{6,7},{7,6},{8,9},{9,8},{10,11... | collective-permute-start | bytes 196616 | tf_op jit(solution)/shard_map/ppermute | solution.py:145
  25.1 14.5 %collective-permute-start.6 = (bf16[2,256,256]{2,1,0:T(8,128)(2,1)S(1)}, bf16[2,256,256]{2,1,0:T(8,128)(2,1)S(1)}, u32[]{:S(2)}, u32[]{:S(2)}) collective-permute-start(bf16[2,256,256]{2,1,0:T(8,128)(2,1)S(1)} %collective-permute-done.4.refs_0_), channel_id=1, source_target_pairs={{0,2},{1,3},{2,0},{3,1},{4,6},{5,7},{6,4},{7,5},{8,10},{9,11},{10,... | collective-permute-start | bytes 786440 | tf_op jit(solution)/shard_map/ppermute | solution.py:145
  31.4 8.2 %collective-permute-start.13 = (bf16[2,256,256]{2,1,0:T(8,128)(2,1)S(1)}, bf16[2,256,256]{2,1,0:T(8,128)(2,1)S(1)}, u32[]{:S(2)}, u32[]{:S(2)}) collective-permute-start(bf16[2,256,256]{2,1,0:T(8,128)(2,1)S(1)} %collective-permute-done.8.refs_2_), channel_id=1, source_target_pairs={{0,2},{1,3},{2,0},{3,1},{4,6},{5,7},{6,4},{7,5},{8,10},{9,11},{10,... | collective-permute-start | bytes 786440 | tf_op jit(solution)/shard_map/ppermute | solution.py:145
  32.7 6.9 %collective-permute-start.12 = (bf16[256,256]{1,0:T(8,128)(2,1)S(1)}, bf16[256,256]{1,0:T(8,128)(2,1)S(1)}, u32[]{:S(2)}, u32[]{:S(2)}) collective-permute-start(bf16[256,256]{1,0:T(8,128)(2,1)S(1)} %get-tuple-element.80), channel_id=1, source_target_pairs={{0,12},{8,4},{12,0},{4,8},{1,13},{9,5},{13,1},{5,9},{2,14},{10,6},... | collective-permute-start | bytes 393224 | tf_op jit(solution)/shard_map/ppermute | solution.py:141
  35.5 1.3 %collective-permute-start.11 = (bf16[256,128]{1,0:T(8,128)(2,1)S(1)}, bf16[256,128]{1,0:T(8,128)(2,1)S(1)}, u32[]{:S(2)}, u32[]{:S(2)}) collective-permute-start(bf16[256,128]{1,0:T(8,128)(2,1)S(1)} %collective-permute-done.10.refs_5_), channel_id=1, source_target_pairs={{0,1},{1,0},{2,3},{3,2},{4,5},{5,4},{6,7},{7,6},{8,9},{9,8},{10,11... | collective-permute-start | bytes 196616 | tf_op jit(solution)/shard_map/ppermute | solution.py:145
  42.7 4.4 %collective-permute-start.14 = (bf16[4,256,256]{2,1,0:T(8,128)(2,1)S(1)}, bf16[4,256,256]{2,1,0:T(8,128)(2,1)S(1)}, u32[]{:S(2)}, u32[]{:S(2)}) collective-permute-start(bf16[4,256,256]{2,1,0:T(8,128)(2,1)S(1)} %get-tuple-element.93.mine), channel_id=1, source_target_pairs={{0,1},{1,0},{2,3},{3,2},{4,5},{5,4},{6,7},{7,6},{8,9},{9,8},{10,11... | collective-permute-start | bytes 1572872 | tf_op jit(solution)/shard_map/ppermute | solution.py:145
  42.7 10.6 %all-to-all-start = ((f32[16,1,128]{2,1,0:T(1,128)}), f32[16,1,128]{2,1,0:T(1,128)S(1)}, u32[]{:S(2)}, u32[]{:S(2)}) async-start(f32[16,1,128]{2,1,0:T(1,128)} %get-tuple-element.89), calls=%async_computation | async-start | bytes 16384 | tf_op jit(solution)/shard_map/all_to_all | solution.py:660
  48.1 10.7 %collective-permute-start.15 = (bf16[2,4,64,256]{3,2,1,0:T(8,128)(2,1)}, bf16[2,4,64,256]{3,2,1,0:T(8,128)(2,1)S(1)}, u32[]{:S(2)}, u32[]{:S(2)}) collective-permute-start(bf16[2,4,64,256]{3,2,1,0:T(8,128)(2,1)} %get-tuple-element.98), channel_id=1, source_target_pairs={{0,2},{1,3},{2,0},{3,1},{4,6},{5,7},{6,4},{7,5},{8,10},{9,11},{10,... | collective-permute-start | bytes 786440 | tf_op jit(solution)/shard_map/ppermute | solution.py:145
  57.6 11.9 %collective-permute-start.17 = (bf16[2,4,64,256]{3,2,1,0:T(8,128)(2,1)S(1)}, bf16[2,4,64,256]{3,2,1,0:T(8,128)(2,1)S(1)}, u32[]{:S(2)}, u32[]{:S(2)}) collective-permute-start(bf16[2,4,64,256]{3,2,1,0:T(8,128)(2,1)S(1)} %get-tuple-element.101), channel_id=1, source_target_pairs={{0,2},{1,3},{2,0},{3,1},{4,6},{5,7},{6,4},{7,5},{8,10},{9,11},{10,... | collective-permute-start | bytes 786440 | tf_op jit(solution)/shard_map/ppermute | solution.py:145
  58.2 11.4 %collective-permute-start.18 = (bf16[1,4,64,256]{3,2,1,0:T(8,128)(2,1)S(1)}, bf16[1,4,64,256]{3,2,1,0:T(8,128)(2,1)S(1)}, u32[]{:S(2)}, u32[]{:S(2)}) collective-permute-start(bf16[1,4,64,256]{3,2,1,0:T(8,128)(2,1)S(1)} %get-tuple-element.102), channel_id=1, source_target_pairs={{0,3},{1,2},{2,1},{3,0},{4,7},{5,6},{6,5},{7,4},{8,11},{9,10},{10,... | collective-permute-start | bytes 393224 | tf_op jit(solution)/shard_map/ppermute | solution.py:145
  58.8 10.7 %collective-permute-start.16 = (bf16[1,4,64,256]{3,2,1,0:T(8,128)(2,1)S(1)}, bf16[1,4,64,256]{3,2,1,0:T(8,128)(2,1)S(1)}, u32[]{:S(2)}, u32[]{:S(2)}) collective-permute-start(bf16[1,4,64,256]{3,2,1,0:T(8,128)(2,1)S(1)} %get-tuple-element.100), channel_id=1, source_target_pairs={{0,1},{1,0},{2,3},{3,2},{4,5},{5,4},{6,7},{7,6},{8,9},{9,8},{10,11... | collective-permute-start | bytes 393224 | tf_op jit(solution)/shard_map/ppermute | solution.py:145

commit v26 on v23

--- a/solution.py
+++ b/solution.py
@@ -126,15 +126,14 @@
 
 def ring_at(place, n_blk):
     place = place % n_blk if isinstance(place, int) else lax.rem(place + n_blk, n_blk)
-    odd, even = 2 * place - 1, 2 * (n_blk - place)
+    even, odd = 2 * place, 2 * (n_blk - place) - 1
     if isinstance(place, int):
-        return 0 if place == 0 else odd if odd < n_blk else even
-    return jnp.where(place == 0, 0, jnp.where(odd < n_blk, odd, even))
+        return even if even < n_blk else odd
+    return jnp.where(even < n_blk, even, odd)
 
 
 def ring_place(index, n_blk):
-    odd, even = (index + 1) // 2, lax.rem(n_blk - index // 2, n_blk)
-    return jnp.where(lax.rem(index, 2) == 1, odd, even)
+    return jnp.where(lax.rem(index, 2) == 1, n_blk - (index + 1) // 2, index // 2)
 
 
 def onward(block, d, n_blk):
@@ -169,9 +168,9 @@
             right = [packed[0]]
             right += [swap(part, 2 * e, n_op) for e, part in enumerate(packed[1:], 1)]
             moved["columns"] = columns
-        if j == 0:
+        if j == 1:
             moved["right"] = right
-        if j == 1:
+        if j == 2:
             moved["tables"] = table(right)
         if j == n_blk - 1 and j >= len(bits) + 1:
             n_early = min(2, n_blk - 1)
@@ -440,7 +439,7 @@
             raw = raw_in[d, :, part].astype(jnp.float32)
             sigma = total_of(mine, other, d, h, cols) + diagonal(diag, right_diag, d, h) * raw
             sig_out[d, :, part] = sigma
-        for e, send in enumerate(sends, 1):
+        for e, send in enumerate(sends):
             send_rows(2 * e, send, d, raw_in, sig_out)
 
 
@@ -504,12 +503,8 @@
             sums[4] = sums[4] + fold(field * image)
         for e, send in enumerate(sends, 1):
             send_rows(e, send, d, *((part_out,) if e % 2 else (fld, part_out)))
-        rows = pl.ds(pl.multiple_of(own_op * step, step), step)
-        for j, ref in enumerate((raw_in, sig, fld, part_out)):
-            own_out[j, d] = ref[d, rows].astype(own_out.dtype)
-
-    _, own_op = place_of()
-    step = own_out.shape[2]
+        send_rows(0, own_out, d, fld, part_out)
+
     sum_terms(src, widths, inter, right, part_out, emit)
     vv, vc, vs = halves[0]
     ff, vf, fs, vt, ft = (whole(x) for x in sums)
@@ -531,10 +526,10 @@
     return sine, jnp.where(upward, -cosine, cosine), 0.5 * (theta + h_two) - 0.5 * size
 
 
-def third_body(n_blk, n_op, count, slots, parts1, parts2, diag, right_diag, own, *refs):
-    n_far = n_op // 2 - 1
-    got1, got2 = refs[:n_far], refs[n_far : n_far + n_op - 1]
-    new_out, res_out, energy_out = refs[n_far + n_op - 1 :]
+def third_body(n_blk, n_op, count, slots, parts1, parts2, diag, right_diag, *refs):
+    n_far = n_op // 2
+    got1, got2 = refs[:n_far], refs[n_far : n_far + n_op]
+    new_out, res_out, energy_out = refs[n_far + n_op :]
     step, cols = new_out.shape[1], new_out.shape[2] // n_op
     own_blk, own_op = place_of()
     scale, theta = norm_theta(parts1[...], count)
@@ -568,13 +563,11 @@
             part, crossed = slice(h * cols, (h + 1) * cols), slice((1 - h) * cols, (2 - h) * cols)
             for d in range(n_blk):
                 dmat = diag[d, mine] + right_diag[:, pl.ds(at, cols)]
-                blocks = [own.at[j] for j in range(4)]
-                if e:
-                    far, near = got1[e // 2 - 1], got2[e - 1]
-                    blocks = far.at[0], far.at[1], near.at[0], near.at[1]
+                far, near = got1[e // 2], got2[e]
+                blocks = far.at[0], far.at[1], near.at[0], near.at[1]
                 raw, sigma, fld, image = (x[d, :, part].astype(jnp.float32) for x in blocks)
                 vec, sigma = raw * scale, sigma * scale
-                image = image + got2[e][0, d, :, crossed].astype(jnp.float32) + dmat * fld
+                image = image + got2[e + 1][0, d, :, crossed].astype(jnp.float32) + dmat * fld
                 newvec = on_vec * vec + cu * fld
                 res = on_vec * sigma + cu * image - energy * newvec
                 new_out[slots[d], :, pl.ds(at, cols)] = newvec.astype(jnp.bfloat16)
@@ -669,15 +662,15 @@
     sig, *out1 = kernel(
         sigma_body,
         [(x, VMEM) for x in (part1, swap(part1, 1, n_op), raw)] + diags,
-        [wide] + sends[1::2],
+        [wide] + sends[1:2] * n_pair,
         nbytes=4 << 20,
     )
-    got1 = [swap(block, 2 * e, n_op) for e, block in enumerate(out1, 1)]
+    got1 = [swap(block, 2 * e, n_op) for e, block in enumerate(out1[1:], 1)]
     dots2, own, *out2 = kernel(
         functools.partial(second_body, n_blk, n_pair, count),
         tables + [(left_early, HBM), (kept, HBM)] + right_ins
         + [(x, VMEM) for x in (parts1, raw, sig)] + diags,
-        [dots, ((4, n_blk, step, 2 * cols), bf16, VMEM)] + sends,
+        [dots, sends[1]] + sends,
         [
             inter,
             pltpu.VMEM((n_blk, rows, 2 * cols), f32),
@@ -696,7 +689,7 @@
     new, res, energy = kernel(
         functools.partial(third_body, n_blk, n_op, count),
         [(slots, SMEM)] + [(x, VMEM) for x in (parts1, parts2)] + diags
-        + [(x, VMEM) for x in (own, *got1, *got2)],
+        + [(x, VMEM) for x in (out1[0], *got1, own, *got2)],
         [final, final, ((1,), f32, SMEM)],
         nbytes=4 << 20,
     )

time: 72 us -> 71.6 us (level)
  local copies, waits for them, and re-layouts: 0.03 us -> 2.25 us
  starting transfers between devices: 30.5 us -> 29.1 us
  blocking collectives: 9.73 us -> 8.97 us
    ppermute x6, waiting for transfers between devices: 8.22 us -> 11.6 us  [onward(): return lax.ppermute(block, 'blk', pairs)]
    ppermute x13, waiting for transfers between devices: 3.97 us -> 1.15 us  [swap(): return lax.ppermute(block, 'op', [(i, i ^ e) for i in range(n_op)])]
    unnamed x12 -> x16, local copies, waits for them, and re-layouts: 0.03 us -> 2.25 us
    all_to_all x1, starting transfers between devices: 5.68 us -> 4.38 us  [totals(): return lax.all_to_all(parts, ('blk', 'op'), 0, 0, tiled=True)]
    all_to_all x1, blocking collectives: 9.73 us -> 8.97 us  [totals(): return lax.all_to_all(parts, ('blk', 'op'), 0, 0, tiled=True)]
  transfers between devices with their start and end apart: 20 -> 20, of which waited for: 6 -> 6; matrix products, arithmetic and copies ran while one was open for 0% -> 0% of each run, Pallas kernels for 14% -> 13%
where the time goes in v26:
time: 71.6 us; the launch traced here: 71.3 us
  starting transfers between devices  29.1 us (41%)
  waiting for transfers between devices  15.8 us (22%)
  Pallas kernels  14.5 us (20%)
  blocking collectives  8.97 us (13%)
  local copies, waits for them, and re-layouts  2.25 us (3%)
  between operations  0.77 us (1%)
    pallas_call x7, Pallas kernels, kernel(): pl.pallas_call(body, out_shape=[HBM(shape, dtype) if space == HBM else ja...  14.5 us
    ppermute x6, starting transfers between devices, onward(): return lax.ppermute(block, 'blk', pairs)  13.9 us
    ppermute x6, waiting for transfers between devices, onward(): return lax.ppermute(block, 'blk', pairs)  11.6 us
    ppermute x13, starting transfers between devices, swap(): return lax.ppermute(block, 'op', [(i, i ^ e) for i in range(n_op)])  10.8 us
    all_to_all x1, blocking collectives, totals(): return lax.all_to_all(parts, ('blk', 'op'), 0, 0, tiled=True)  8.97 us
    all_to_all x1, starting transfers between devices, totals(): return lax.all_to_all(parts, ('blk', 'op'), 0, 0, tiled=True)  4.38 us
    all_to_all x1, waiting for transfers between devices, totals(): return lax.all_to_all(parts, ('blk', 'op'), 0, 0, tiled=True)  3.04 us
    unnamed x16, local copies, waits for them, and re-layouts  2.25 us
  transfers between devices with their start and end apart: 20, of which 6 were waited for; matrix products, arithmetic and copies ran while one was open for 0% of the time, Pallas kernels for 13%

profile of v26, /device:TPU:0, one launch (start us, length us, event | category | flops | bytes accessed | tf_op | source)
XLA Modules:
  0.0 71.3 jit_solution(6396778012050055160)
XLA Ops:
  0.6 0.0 copy-start.3
  0.6 4.1 %collective-permute-start = (bf16[2,256,256]{2,1,0:T(8,128)(2,1)}, bf16[2,256,256]{2,1,0:T(8,128)(2,1)S(1)}, u32[]{:S(2)}, u32[]{:S(2)}) collective-permute-start(bf16[2,256,256]{2,1,0:T(8,128)(2,1)} %bitcast.2), channel_id=1, source_target_pairs={{0,8},{8,12},{12,4},{4,0},{1,9},{9,13},{13,5},{5,1},{2,10},{10,14}... | collective-permute-start | bytes 786440 | tf_op jit(solution)/shard_map/ppermute | solution.py:141
  4.7 1.5 %collective-permute-start.3 = (bf16[2,256,256]{2,1,0:T(8,128)(2,1)}, bf16[2,256,256]{2,1,0:T(8,128)(2,1)S(1)}, u32[]{:S(2)}, u32[]{:S(2)}) collective-permute-start(bf16[2,256,256]{2,1,0:T(8,128)(2,1)} %bitcast.3), channel_id=1, source_target_pairs={{0,2},{1,3},{2,0},{3,1},{4,6},{5,7},{6,4},{7,5},{8,10},{9,11},{10,... | collective-permute-start | bytes 786440 | tf_op jit(solution)/shard_map/ppermute | solution.py:145
  6.2 0.0 copy-done.3
  6.2 0.0 collective-permute-start.1
  6.2 1.1 %collective-permute-done.1._ = s32[2]{0:T(128)S(1)} collective-permute-done((s32[2]{0:T(128)S(1)}, s32[2]{0:T(128)S(1)}, u32[]{:S(2)}, u32[]{:S(2)}) %collective-permute-start.1) | collective-permute-done | bytes 40 | tf_op jit(solution)/shard_map/ppermute | solution.py:145
  7.3 0.0 copy-start
  7.3 1.9 %shard_map.103 = (bf16[256,256]{1,0:T(8,128)(2,1)S(1)}, bf16[256,128]{1,0:T(8,128)(2,1)S(1)}, bf16[256,256]{1,0:T(8,128)(2,1)S(1)}, bf16[256,128]{1,0:T(8,128)(2...) custom-call(s32[2]{0:T(128)S(1)} %copy-done.3, s32[2]{0:T(128)S(1)} %collective-permute-done.1._, ...), custom_call_target="tpu_custom_call" | custom-call | bytes 1048576 | tf_op jit(solution)/shard_map/pallas_call | solution.py:113
  9.3 1.4 %collective-permute-done.refs_2_ = bf16[2,256,256]{2,1,0:T(8,128)(2,1)S(1)} collective-permute-done((bf16[2,256,256]{2,1,0:T(8,128)(2,1)}, bf16[2,256,256]{2,1,0:T(8,128)(2,1)S(1)}, u32[]{:S(2)}, u32[]{:S(2)}) %collective-permute-start) | collective-permute-done | bytes 262176 | tf_op jit(solution)/shard_map/ppermute | solution.py:141
  10.6 0.0 copy-start.1
  10.6 3.3 %collective-permute-start.4 = (bf16[2,256,256]{2,1,0:T(8,128)(2,1)S(1)}, bf16[2,256,256]{2,1,0:T(8,128)(2,1)S(1)}, u32[]{:S(2)}, u32[]{:S(2)}) collective-permute-start(bf16[2,256,256]{2,1,0:T(8,128)(2,1)S(1)} %collective-permute-done.refs_2_), channel_id=1, source_target_pairs={{0,8},{8,12},{12,4},{4,0},{1,9},{9,13},{13,5},{5,1},{2,10},{10,14}... | collective-permute-start | bytes 786440 | tf_op jit(solution)/shard_map/ppermute | solution.py:141
  13.9 0.0 copy-start.2
  13.9 1.5 %collective-permute-start.6 = (bf16[144,256]{1,0:T(8,128)(2,1)S(1)}, bf16[144,256]{1,0:T(8,128)(2,1)S(1)}, u32[]{:S(2)}, u32[]{:S(2)}) collective-permute-start(bf16[144,256]{1,0:T(8,128)(2,1)S(1)} %get-tuple-element.61), channel_id=1, source_target_pairs={{0,2},{1,3},{2,0},{3,1},{4,6},{5,7},{6,4},{7,5},{8,10},{9,11},{10,... | collective-permute-start | bytes 221192 | tf_op jit(solution)/shard_map/ppermute | solution.py:145
  15.4 0.7 collective-permute-start.5
  16.1 0.5 collective-permute-start.2
  16.6 3.4 %collective-permute-done.5.refs_5_ = bf16[256,128]{1,0:T(8,128)(2,1)S(1)} collective-permute-done((bf16[256,128]{1,0:T(8,128)(2,1)S(1)}, bf16[256,128]{1,0:T(8,128)(2,1)S(1)}, u32[]{:S(2)}, u32[]{:S(2)}) %collective-permute-start.5) | collective-permute-done | bytes 65568 | tf_op jit(solution)/shard_map/ppermute | solution.py:141
  20.0 0.0 collective-permute-done.6.refs_1_.refs_5_
  20.0 0.0 collective-permute-done.3.refs_1_
  20.0 0.0 collective-permute-done.4.refs_0_
  20.0 0.0 copy-start.4
  20.0 0.0 copy-start.5
  20.0 3.4 %collective-permute-start.7 = (bf16[2,256,256]{2,1,0:T(8,128)(2,1)S(1)}, bf16[2,256,256]{2,1,0:T(8,128)(2,1)S(1)}, u32[]{:S(2)}, u32[]{:S(2)}) collective-permute-start(bf16[2,256,256]{2,1,0:T(8,128)(2,1)S(1)} %collective-permute-done.4.refs_0_), channel_id=1, source_target_pairs={{0,8},{8,12},{12,4},{4,0},{1,9},{9,13},{13,5},{5,1},{2,10},{10,14}... | collective-permute-start | bytes 786440 | tf_op jit(solution)/shard_map/ppermute | solution.py:141
  23.5 0.0 collective-permute-start.9
  23.5 0.0 collective-permute-start.8
  23.5 1.5 %collective-permute-start.10 = (bf16[2,256,256]{2,1,0:T(8,128)(2,1)S(1)}, bf16[2,256,256]{2,1,0:T(8,128)(2,1)S(1)}, u32[]{:S(2)}, u32[]{:S(2)}) collective-permute-start(bf16[2,256,256]{2,1,0:T(8,128)(2,1)S(1)} %collective-permute-done.4.refs_0_), channel_id=1, source_target_pairs={{0,2},{1,3},{2,0},{3,1},{4,6},{5,7},{6,4},{7,5},{8,10},{9,11},{10,... | collective-permute-start | bytes 786440 | tf_op jit(solution)/shard_map/ppermute | solution.py:145
  25.0 0.0 copy-done.1
  25.0 0.0 copy-done.2
  25.0 0.0 copy-done.4
  25.0 0.0 copy-done.5
  25.0 1.3 %shard_map.104 = (s32[16]{0:T(128)S(1)}, s32[4]{0:T(128)S(1)}, s32[4]{0:T(128)S(1)}, f32[4,256,128]{2,1,0:T(8,128)S(1)}, f32[1,512]{1,0:T(1,128)S(1)}) custom-call(s32[4]{0:T(128)S(1)} %copy-done.4, s32[4]{0:T(128)S(1)} %copy-done.5, f32[4,256]{1,0:T(4,128)S(1)} %copy-done.1, f32[1,512]{1,0:T(1,128)S(1)} %bitcast.5, ...), custom_call_target="tpu_custom_call" | custom-call | tf_op jit(solution)/shard_map/pallas_call | solution.py:113
  26.3 4.1 %collective-permute-done.9.refs_7_ = bf16[256,128]{1,0:T(8,128)(2,1)S(1)} collective-permute-done((bf16[256,128]{1,0:T(8,128)(2,1)S(1)}, bf16[256,128]{1,0:T(8,128)(2,1)S(1)}, u32[]{:S(2)}, u32[]{:S(2)}) %collective-permute-start.9) | collective-permute-done | bytes 65568 | tf_op jit(solution)/shard_map/ppermute | solution.py:141
  30.4 0.0 collective-permute-done.2.refs_3_
  30.4 0.0 collective-permute-done.8.refs_6_
  30.4 0.0 collective-permute-done.7.refs_2_
  30.5 1.6 %collective-permute-start.13 = (bf16[2,256,256]{2,1,0:T(8,128)(2,1)S(1)}, bf16[2,256,256]{2,1,0:T(8,128)(2,1)S(1)}, u32[]{:S(2)}, u32[]{:S(2)}) collective-permute-start(bf16[2,256,256]{2,1,0:T(8,128)(2,1)S(1)} %collective-permute-done.7.refs_2_), channel_id=1, source_target_pairs={{0,2},{1,3},{2,0},{3,1},{4,6},{5,7},{6,4},{7,5},{8,10},{9,11},{10,... | collective-permute-start | bytes 786440 | tf_op jit(solution)/shard_map/ppermute | solution.py:145
  32.0 2.5 %collective-permute-start.12 = (bf16[256,256]{1,0:T(8,128)(2,1)S(1)}, bf16[256,256]{1,0:T(8,128)(2,1)S(1)}, u32[]{:S(2)}, u32[]{:S(2)}) collective-permute-start(bf16[256,256]{1,0:T(8,128)(2,1)S(1)} %get-tuple-element.83), channel_id=1, source_target_pairs={{0,12},{8,4},{12,0},{4,8},{1,13},{9,5},{13,1},{5,9},{2,14},{10,6},... | collective-permute-start | bytes 393224 | tf_op jit(solution)/shard_map/ppermute | solution.py:141
  34.5 0.0 collective-permute-start.11
  34.5 0.0 copy-done
  34.5 1.7 %shard_map.105 = (bf16[2,256,256]{2,1,0:T(8,128)(2,1)S(1)}, bf16[2,4,256,256]{3,2,1,0:T(8,128)(2,1)S(1)}, bf16[2,2,2,256,256]{4,3,2,1,0:T(8,128)(2,1)}) custom-call(s32[4]{0:T(128)S(1)} %get-tuple-element.74.widths, bf16[2,256,256]{2,1,0:T(8,128)(2,1)S(1)} %bitcast.4, bf16[2,256,256]{2,1,0:T(8,128)(2,1)S(1)} %collective-permute-done.3.refs_1_, ...), custom_call_target="tpu_custom_call" | custom-call | flops 268435456 | bytes 4194304 | tf_op jit(solution)/shard_map/pallas_call | solution.py:113
  36.2 2.7 %collective-permute-done.12.refs_6_ = bf16[256,256]{1,0:T(8,128)(2,1)S(1)} collective-permute-done((bf16[256,256]{1,0:T(8,128)(2,1)S(1)}, bf16[256,256]{1,0:T(8,128)(2,1)S(1)}, u32[]{:S(2)}, u32[]{:S(2)}) %collective-permute-start.12) | collective-permute-done | bytes 131104 | tf_op jit(solution)/shard_map/ppermute | solution.py:141
  38.9 0.0 collective-permute-done.10.refs_1_
  38.9 0.0 collective-permute-done.11.refs_8_
  38.9 0.0 collective-permute-done.13.refs_3_
  38.9 3.0 %shard_map.106 = (bf16[4,256,256]{2,1,0:T(8,128)(2,1)S(1)}, bf16[4,256,256]{2,1,0:T(8,128)(2,1)S(1)}, bf16[2,2,2,256,256]{4,3,2,1,0:T(8,128)(2,1)}, f32[16,1,128]{2,1,0:T(1,128)}) custom-call(s32[16]{0:T(128)S(1)} %get-tuple-element.73.src, s32[4]{0:T(128)S(1)} %get-tuple-element.74.widths, bf16[2,256,256]{2,1,0:T(8,128)(2,1)S(1)} %collective-permute-done.4.refs_0_, ...), custom_call_target="tpu_custom_call" | custom-call | flops 1073741824 | bytes 6291456 | tf_op jit(solution)/shard_map/pallas_call | solution.py:113
  41.9 0.1 collective-permute-start.14
  42.0 4.4 %all-to-all-start = ((f32[16,1,128]{2,1,0:T(1,128)}), f32[16,1,128]{2,1,0:T(1,128)S(1)}, u32[]{:S(2)}, u32[]{:S(2)}) async-start(f32[16,1,128]{2,1,0:T(1,128)} %get-tuple-element.92), calls=%async_computation | async-start | bytes 16384 | tf_op jit(solution)/shard_map/all_to_all | solution.py:652
  46.4 0.0 collective-permute-done.14.other
  46.4 0.3 shard_map.107
  46.8 0.0 copy-start.6
  46.8 1.0 %copy-done.6 = f32[4,256,256]{2,1,0:T(8,128)} copy-done((f32[4,256,256]{2,1,0:T(8,128)}, f32[4,256,256]{2,1,0:T(8,128)S(1)}, u32[]{:S(2)}) %copy-start.6) | copy-done | bytes 1048600
  47.8 1.9 %collective-permute-start.15 = (bf16[2,4,64,256]{3,2,1,0:T(8,128)(2,1)S(1)}, bf16[2,4,64,256]{3,2,1,0:T(8,128)(2,1)S(1)}, u32[]{:S(2)}, u32[]{:S(2)}) collective-permute-start(bf16[2,4,64,256]{3,2,1,0:T(8,128)(2,1)S(1)} %get-tuple-element.101), channel_id=1, source_target_pairs={{0,2},{1,3},{2,0},{3,1},{4,6},{5,7},{6,4},{7,5},{8,10},{9,11},{10,... | collective-permute-start | bytes 786440 | tf_op jit(solution)/shard_map/ppermute | solution.py:145
  49.7 3.0 %all-to-all-done.refs_2_.parts1 = f32[16,1,128]{2,1,0:T(1,128)S(1)} async-done(((f32[16,1,128]{2,1,0:T(1,128)}), f32[16,1,128]{2,1,0:T(1,128)S(1)}, u32[]{:S(2)}, u32[]{:S(2)}) %all-to-all-start) | async-done | bytes 8224 | tf_op jit(solution)/shard_map/all_to_all | solution.py:652
  52.7 0.0 copy-start.7
  52.7 1.2 %copy-done.7 = f32[4,256,256]{2,1,0:T(8,128)S(1)} copy-done((f32[4,256,256]{2,1,0:T(8,128)S(1)}, f32[4,256,256]{2,1,0:T(8,128)}, u32[]{:S(2)}) %copy-start.7) | copy-done | bytes 1048600
  54.0 4.2 %shard_map.108 = (f32[16,1,128]{2,1,0:T(1,128)S(1)}, bf16[2,4,64,256]{3,2,1,0:T(8,128)(2,1)S(1)}, bf16[1,4,64,256]{3,2,1,0:T(8,128)(2,1)S(1)}, bf16[2,4,64,256]{...) custom-call(s32[16]{0:T(128)S(1)} %get-tuple-element.73.src, s32[4]{0:T(128)S(1)} %get-tuple-element.74.widths, ...), custom_call_target="tpu_custom_call" | custom-call | flops 4294967296 | bytes 25165824 | tf_op jit(solution)/shard_map/pallas_call | solution.py:113
  58.2 0.6 collective-permute-start.17
  58.7 0.6 collective-permute-start.18
  59.4 0.0 collective-permute-done.15.refs_1_
  59.4 1.0 %collective-permute-start.16 = (bf16[1,4,64,256]{3,2,1,0:T(8,128)(2,1)S(1)}, bf16[1,4,64,256]{3,2,1,0:T(8,128)(2,1)S(1)}, u32[]{:S(2)}, u32[]{:S(2)}) collective-permute-start(bf16[1,4,64,256]{3,2,1,0:T(8,128)(2,1)S(1)} %get-tuple-element.104), channel_id=1, source_target_pairs={{0,1},{1,0},{2,3},{3,2},{4,5},{5,4},{6,7},{7,6},{8,9},{9,8},{10,11... | collective-permute-start | bytes 393224 | tf_op jit(solution)/shard_map/ppermute | solution.py:145
  60.4 9.0 %all_to_all.10.parts2 = f32[16,1,128]{2,1,0:T(1,128)S(1)} all-to-all(f32[16,1,128]{2,1,0:T(1,128)S(1)} %get-tuple-element.98), channel_id=1, replica_groups=mesh['grp'=2,'blk'=4,'op'=4] {'blk','op'}, dimensions={0} | all-to-all | bytes 16384 | tf_op jit(solution)/shard_map/all_to_all | solution.py:652
  69.3 0.0 collective-permute-done.18.refs_5_
  69.3 0.0 collective-permute-done.17.refs_4_
  69.3 0.0 collective-permute-done.16.refs_3_
  69.4 2.0 %shard_map.109 = (bf16[4,64,512]{2,1,0:T(8,128)(2,1)}, bf16[4,64,512]{2,1,0:T(8,128)(2,1)}, f32[1]{0:T(128)}) custom-call(s32[4]{0:T(128)S(1)} %get-tuple-element.72.slots, f32[16,1,128]{2,1,0:T(1,128)S(1)} %all-to-all-done.refs_2_.parts1, f32[16,1,128]{2,1,0:T(1,128)S(1)} %all_to_all.10.parts2, f32[4,256,128]{2,1,0:T(8,128)S(1)} %get-tuple-element.90.refs_11_.diag.refs_5_, ...), custom_call_target="tpu_custom_call" | custom-call | bytes 4194304 | tf_op jit(solution)/shard_map/pallas_call | solution.py:113
Async XLA Ops:
  0.6 5.6 %copy-start.3 = (s32[2]{0:T(128)S(1)}, s32[2]{0:T(128)}, u32[]{:S(2)}) copy-start(s32[2]{0:T(128)} %shift.1) | copy-start | bytes 28
  0.6 10.0 %collective-permute-start = (bf16[2,256,256]{2,1,0:T(8,128)(2,1)}, bf16[2,256,256]{2,1,0:T(8,128)(2,1)S(1)}, u32[]{:S(2)}, u32[]{:S(2)}) collective-permute-start(bf16[2,256,256]{2,1,0:T(8,128)(2,1)} %bitcast.2), channel_id=1, source_target_pairs={{0,8},{8,12},{12,4},{4,0},{1,9},{9,13},{13,5},{5,1},{2,10},{10,14}... | collective-permute-start | bytes 786440 | tf_op jit(solution)/shard_map/ppermute | solution.py:141
  4.7 15.3 %collective-permute-start.3 = (bf16[2,256,256]{2,1,0:T(8,128)(2,1)}, bf16[2,256,256]{2,1,0:T(8,128)(2,1)S(1)}, u32[]{:S(2)}, u32[]{:S(2)}) collective-permute-start(bf16[2,256,256]{2,1,0:T(8,128)(2,1)} %bitcast.3), channel_id=1, source_target_pairs={{0,2},{1,3},{2,0},{3,1},{4,6},{5,7},{6,4},{7,5},{8,10},{9,11},{10,... | collective-permute-start | bytes 786440 | tf_op jit(solution)/shard_map/ppermute | solution.py:145
  6.2 1.1 %collective-permute-start.1 = (s32[2]{0:T(128)S(1)}, s32[2]{0:T(128)S(1)}, u32[]{:S(2)}, u32[]{:S(2)}) collective-permute-start(s32[2]{0:T(128)S(1)} %copy-done.3), channel_id=1, source_target_pairs={{0,1},{1,0},{2,3},{3,2},{4,5},{5,4},{6,7},{7,6},{8,9},{9,8},{10,11... | collective-permute-start | bytes 32 | tf_op jit(solution)/shard_map/ppermute | solution.py:145
  7.3 27.1 %copy-start = (bf16[2,1,256,256]{3,2,1,0:T(8,128)(2,1)S(1)}, bf16[2,1,256,256]{3,2,1,0:T(8,128)(2,1)}, u32[]{:S(2)}) copy-start(bf16[2,1,256,256]{3,2,1,0:T(8,128)(2,1)} %param.9) | copy-start | bytes 786436
  10.6 14.3 %copy-start.1 = (f32[4,256]{1,0:T(4,128)S(1)}, f32[4,256]{1,0:T(4,128)}, u32[]{:S(2)}) copy-start(f32[4,256]{1,0:T(4,128)} %left_diag.1) | copy-start | bytes 12292
  10.6 9.4 %collective-permute-start.4 = (bf16[2,256,256]{2,1,0:T(8,128)(2,1)S(1)}, bf16[2,256,256]{2,1,0:T(8,128)(2,1)S(1)}, u32[]{:S(2)}, u32[]{:S(2)}) collective-permute-start(bf16[2,256,256]{2,1,0:T(8,128)(2,1)S(1)} %collective-permute-done.refs_2_), channel_id=1, source_target_pairs={{0,8},{8,12},{12,4},{4,0},{1,9},{9,13},{13,5},{5,1},{2,10},{10,14}... | collective-permute-start | bytes 786440 | tf_op jit(solution)/shard_map/ppermute | solution.py:141
  13.9 11.1 %copy-start.2 = (f32[512]{0:T(512)S(1)}, f32[512]{0:T(512)}, u32[]{:S(2)}) copy-start(f32[512]{0:T(512)} %param.15) | copy-start | bytes 6148
  13.9 6.1 %collective-permute-start.6 = (bf16[144,256]{1,0:T(8,128)(2,1)S(1)}, bf16[144,256]{1,0:T(8,128)(2,1)S(1)}, u32[]{:S(2)}, u32[]{:S(2)}) collective-permute-start(bf16[144,256]{1,0:T(8,128)(2,1)S(1)} %get-tuple-element.61), channel_id=1, source_target_pairs={{0,2},{1,3},{2,0},{3,1},{4,6},{5,7},{6,4},{7,5},{8,10},{9,11},{10,... | collective-permute-start | bytes 221192 | tf_op jit(solution)/shard_map/ppermute | solution.py:145
  15.4 4.6 %collective-permute-start.5 = (bf16[256,128]{1,0:T(8,128)(2,1)S(1)}, bf16[256,128]{1,0:T(8,128)(2,1)S(1)}, u32[]{:S(2)}, u32[]{:S(2)}) collective-permute-start(bf16[256,128]{1,0:T(8,128)(2,1)S(1)} %get-tuple-element.56), channel_id=1, source_target_pairs={{0,8},{8,12},{12,4},{4,0},{1,9},{9,13},{13,5},{5,1},{2,10},{10,14}... | collective-permute-start | bytes 196616 | tf_op jit(solution)/shard_map/ppermute | solution.py:141
  16.1 14.4 %collective-permute-start.2 = (bf16[2,256,256]{2,1,0:T(8,128)(2,1)S(1)}, bf16[2,256,256]{2,1,0:T(8,128)(2,1)S(1)}, u32[]{:S(2)}, u32[]{:S(2)}) collective-permute-start(bf16[2,256,256]{2,1,0:T(8,128)(2,1)S(1)} %collective-permute-done.refs_2_), channel_id=1, source_target_pairs={{0,2},{1,3},{2,0},{3,1},{4,6},{5,7},{6,4},{7,5},{8,10},{9,11},{10,... | collective-permute-start | bytes 786440 | tf_op jit(solution)/shard_map/ppermute | solution.py:145
  20.0 5.0 %copy-start.4 = (s32[4]{0:T(128)S(1)}, s32[4]{0:T(128)}, u32[]{:S(2)}) copy-start(s32[4]{0:T(128)} %sector.1) | copy-start | bytes 52
  20.0 5.0 %copy-start.5 = (s32[4]{0:T(128)S(1)}, s32[4]{0:T(128)}, u32[]{:S(2)}) copy-start(s32[4]{0:T(128)} %width.1) | copy-start | bytes 52
  20.0 10.4 %collective-permute-start.7 = (bf16[2,256,256]{2,1,0:T(8,128)(2,1)S(1)}, bf16[2,256,256]{2,1,0:T(8,128)(2,1)S(1)}, u32[]{:S(2)}, u32[]{:S(2)}) collective-permute-start(bf16[2,256,256]{2,1,0:T(8,128)(2,1)S(1)} %collective-permute-done.4.refs_0_), channel_id=1, source_target_pairs={{0,8},{8,12},{12,4},{4,0},{1,9},{9,13},{13,5},{5,1},{2,10},{10,14}... | collective-permute-start | bytes 786440 | tf_op jit(solution)/shard_map/ppermute | solution.py:141
  23.5 7.0 %collective-permute-start.9 = (bf16[256,128]{1,0:T(8,128)(2,1)S(1)}, bf16[256,128]{1,0:T(8,128)(2,1)S(1)}, u32[]{:S(2)}, u32[]{:S(2)}) collective-permute-start(bf16[256,128]{1,0:T(8,128)(2,1)S(1)} %get-tuple-element.64), channel_id=1, source_target_pairs={{0,4},{8,0},{12,8},{4,12},{1,5},{9,1},{13,9},{5,13},{2,6},{10,2},{... | collective-permute-start | bytes 196616 | tf_op jit(solution)/shard_map/ppermute | solution.py:141
  23.5 7.0 %collective-permute-start.8 = (bf16[256,128]{1,0:T(8,128)(2,1)S(1)}, bf16[256,128]{1,0:T(8,128)(2,1)S(1)}, u32[]{:S(2)}, u32[]{:S(2)}) collective-permute-start(bf16[256,128]{1,0:T(8,128)(2,1)S(1)} %collective-permute-done.5.refs_5_), channel_id=1, source_target_pairs={{0,1},{1,0},{2,3},{3,2},{4,5},{5,4},{6,7},{7,6},{8,9},{9,8},{10,11... | collective-permute-start | bytes 196616 | tf_op jit(solution)/shard_map/ppermute | solution.py:145
  23.5 15.4 %collective-permute-start.10 = (bf16[2,256,256]{2,1,0:T(8,128)(2,1)S(1)}, bf16[2,256,256]{2,1,0:T(8,128)(2,1)S(1)}, u32[]{:S(2)}, u32[]{:S(2)}) collective-permute-start(bf16[2,256,256]{2,1,0:T(8,128)(2,1)S(1)} %collective-permute-done.4.refs_0_), channel_id=1, source_target_pairs={{0,2},{1,3},{2,0},{3,1},{4,6},{5,7},{6,4},{7,5},{8,10},{9,11},{10,... | collective-permute-start | bytes 786440 | tf_op jit(solution)/shard_map/ppermute | solution.py:145
  30.5 8.4 %collective-permute-start.13 = (bf16[2,256,256]{2,1,0:T(8,128)(2,1)S(1)}, bf16[2,256,256]{2,1,0:T(8,128)(2,1)S(1)}, u32[]{:S(2)}, u32[]{:S(2)}) collective-permute-start(bf16[2,256,256]{2,1,0:T(8,128)(2,1)S(1)} %collective-permute-done.7.refs_2_), channel_id=1, source_target_pairs={{0,2},{1,3},{2,0},{3,1},{4,6},{5,7},{6,4},{7,5},{8,10},{9,11},{10,... | collective-permute-start | bytes 786440 | tf_op jit(solution)/shard_map/ppermute | solution.py:145
  32.0 6.9 %collective-permute-start.12 = (bf16[256,256]{1,0:T(8,128)(2,1)S(1)}, bf16[256,256]{1,0:T(8,128)(2,1)S(1)}, u32[]{:S(2)}, u32[]{:S(2)}) collective-permute-start(bf16[256,256]{1,0:T(8,128)(2,1)S(1)} %get-tuple-element.83), channel_id=1, source_target_pairs={{0,12},{8,4},{12,0},{4,8},{1,13},{9,5},{13,1},{5,9},{2,14},{10,6},... | collective-permute-start | bytes 393224 | tf_op jit(solution)/shard_map/ppermute | solution.py:141
  34.5 4.4 %collective-permute-start.11 = (bf16[256,128]{1,0:T(8,128)(2,1)S(1)}, bf16[256,128]{1,0:T(8,128)(2,1)S(1)}, u32[]{:S(2)}, u32[]{:S(2)}) collective-permute-start(bf16[256,128]{1,0:T(8,128)(2,1)S(1)} %collective-permute-done.9.refs_7_), channel_id=1, source_target_pairs={{0,1},{1,0},{2,3},{3,2},{4,5},{5,4},{6,7},{7,6},{8,9},{9,8},{10,11... | collective-permute-start | bytes 196616 | tf_op jit(solution)/shard_map/ppermute | solution.py:145
  41.9 4.5 %collective-permute-start.14 = (bf16[4,256,256]{2,1,0:T(8,128)(2,1)S(1)}, bf16[4,256,256]{2,1,0:T(8,128)(2,1)S(1)}, u32[]{:S(2)}, u32[]{:S(2)}) collective-permute-start(bf16[4,256,256]{2,1,0:T(8,128)(2,1)S(1)} %get-tuple-element.96.mine), channel_id=1, source_target_pairs={{0,1},{1,0},{2,3},{3,2},{4,5},{5,4},{6,7},{7,6},{8,9},{9,8},{10,11... | collective-permute-start | bytes 1572872 | tf_op jit(solution)/shard_map/ppermute | solution.py:145
  42.0 10.7 %all-to-all-start = ((f32[16,1,128]{2,1,0:T(1,128)}), f32[16,1,128]{2,1,0:T(1,128)S(1)}, u32[]{:S(2)}, u32[]{:S(2)}) async-start(f32[16,1,128]{2,1,0:T(1,128)} %get-tuple-element.92), calls=%async_computation | async-start | bytes 16384 | tf_op jit(solution)/shard_map/all_to_all | solution.py:652
  46.8 1.0 %copy-start.6 = (f32[4,256,256]{2,1,0:T(8,128)}, f32[4,256,256]{2,1,0:T(8,128)S(1)}, u32[]{:S(2)}) copy-start(f32[4,256,256]{2,1,0:T(8,128)S(1)} %get-tuple-element.97.refs_4_) | copy-start | bytes 3145732
  47.8 11.6 %collective-permute-start.15 = (bf16[2,4,64,256]{3,2,1,0:T(8,128)(2,1)S(1)}, bf16[2,4,64,256]{3,2,1,0:T(8,128)(2,1)S(1)}, u32[]{:S(2)}, u32[]{:S(2)}) collective-permute-start(bf16[2,4,64,256]{3,2,1,0:T(8,128)(2,1)S(1)} %get-tuple-element.101), channel_id=1, source_target_pairs={{0,2},{1,3},{2,0},{3,1},{4,6},{5,7},{6,4},{7,5},{8,10},{9,11},{10,... | collective-permute-start | bytes 786440 | tf_op jit(solution)/shard_map/ppermute | solution.py:145
  52.7 1.2 %copy-start.7 = (f32[4,256,256]{2,1,0:T(8,128)S(1)}, f32[4,256,256]{2,1,0:T(8,128)}, u32[]{:S(2)}) copy-start(f32[4,256,256]{2,1,0:T(8,128)} %copy-done.6) | copy-start | bytes 3145732
  58.2 11.2 %collective-permute-start.17 = (bf16[2,4,64,256]{3,2,1,0:T(8,128)(2,1)S(1)}, bf16[2,4,64,256]{3,2,1,0:T(8,128)(2,1)S(1)}, u32[]{:S(2)}, u32[]{:S(2)}) collective-permute-start(bf16[2,4,64,256]{3,2,1,0:T(8,128)(2,1)S(1)} %get-tuple-element.105), channel_id=1, source_target_pairs={{0,2},{1,3},{2,0},{3,1},{4,6},{5,7},{6,4},{7,5},{8,10},{9,11},{10,... | collective-permute-start | bytes 786440 | tf_op jit(solution)/shard_map/ppermute | solution.py:145
  58.7 10.6 %collective-permute-start.18 = (bf16[1,4,64,256]{3,2,1,0:T(8,128)(2,1)S(1)}, bf16[1,4,64,256]{3,2,1,0:T(8,128)(2,1)S(1)}, u32[]{:S(2)}, u32[]{:S(2)}) collective-permute-start(bf16[1,4,64,256]{3,2,1,0:T(8,128)(2,1)S(1)} %get-tuple-element.106), channel_id=1, source_target_pairs={{0,3},{1,2},{2,1},{3,0},{4,7},{5,6},{6,5},{7,4},{8,11},{9,10},{10,... | collective-permute-start | bytes 393224 | tf_op jit(solution)/shard_map/ppermute | solution.py:145
  59.4 10.0 %collective-permute-start.16 = (bf16[1,4,64,256]{3,2,1,0:T(8,128)(2,1)S(1)}, bf16[1,4,64,256]{3,2,1,0:T(8,128)(2,1)S(1)}, u32[]{:S(2)}, u32[]{:S(2)}) collective-permute-start(bf16[1,4,64,256]{3,2,1,0:T(8,128)(2,1)S(1)} %get-tuple-element.104), channel_id=1, source_target_pairs={{0,1},{1,0},{2,3},{3,2},{4,5},{5,4},{6,7},{7,6},{8,9},{9,8},{10,11... | collective-permute-start | bytes 393224 | tf_op jit(solution)/shard_map/ppermute | solution.py:145

commit v27 on v23

--- a/solution.py
+++ b/solution.py
@@ -126,15 +126,14 @@
 
 def ring_at(place, n_blk):
     place = place % n_blk if isinstance(place, int) else lax.rem(place + n_blk, n_blk)
-    odd, even = 2 * place - 1, 2 * (n_blk - place)
+    even, odd = 2 * place, 2 * (n_blk - place) - 1
     if isinstance(place, int):
-        return 0 if place == 0 else odd if odd < n_blk else even
-    return jnp.where(place == 0, 0, jnp.where(odd < n_blk, odd, even))
+        return even if even < n_blk else odd
+    return jnp.where(even < n_blk, even, odd)
 
 
 def ring_place(index, n_blk):
-    odd, even = (index + 1) // 2, lax.rem(n_blk - index // 2, n_blk)
-    return jnp.where(lax.rem(index, 2) == 1, odd, even)
+    return jnp.where(lax.rem(index, 2) == 1, n_blk - (index + 1) // 2, index // 2)
 
 
 def onward(block, d, n_blk):
@@ -389,17 +388,18 @@
     (right,), refs = take(refs, [n_pair])
     psi, refs = take(refs, counts)
     raw_in, inter_in, diag, right_diag, part_out, raw_out, left_out, dots_out, inter, sems = refs
-    copies = keep(left, left_out, sems)
+    ready = []
     for j, (given, own) in enumerate(((inter_in, inter), (raw_in, raw_out))):
-        copies.append(
+        ready.append(
             pltpu.make_async_copy(given, own.at[:n_early], sems.at[n_late * n_pair + j])
         )
-        copies[-1].start()
+        ready[-1].start()
+    copies = keep(left, left_out, sems)
     inter[n_blk] = jnp.zeros_like(inter[n_blk])
     products_of(
         psi, left, widths, n_early, raw_out.at[n_early:], inter.at[n_early:n_blk]
     )
-    for copy in copies:
+    for copy in ready:
         copy.wait()
     cols = diag.shape[2]
     zero = jnp.zeros((8, cols), jnp.float32)
@@ -417,6 +417,8 @@
 
     sum_terms(src, widths, inter, right, part_out, emit)
     spread([whole(x) for x in sums], dots_out)
+    for copy in copies:
+        copy.wait()
 
 
 def send_rows(e, send, d, *refs):

time: 72 us -> 70.9 us (0.985)
  starting transfers between devices: 30.5 us -> 27.6 us
  waiting for transfers between devices: 15.5 us -> 17.8 us
    ppermute x6, starting transfers between devices: 14.3 us -> 11.8 us  [onward(): return lax.ppermute(block, 'blk', pairs)]
    ppermute x6, waiting for transfers between devices: 8.22 us -> 10.5 us  [onward(): return lax.ppermute(block, 'blk', pairs)]
    all_to_all x1, starting transfers between devices: 5.68 us -> 4.63 us  [totals(): return lax.all_to_all(parts, ('blk', 'op'), 0, 0, tiled=True)]
where the time goes in v27:
time: 70.9 us; the launch traced here: 70.7 us
  starting transfers between devices  27.6 us (39%)
  waiting for transfers between devices  17.8 us (25%)
  Pallas kernels  14.8 us (21%)
  blocking collectives  9.73 us (14%)
  between operations  0.76 us (1%)
    pallas_call x7, Pallas kernels, kernel(): pl.pallas_call(body, out_shape=[HBM(shape, dtype) if space == HBM else ja...  14.8 us
    ppermute x6, starting transfers between devices, onward(): return lax.ppermute(block, 'blk', pairs)  11.8 us
    ppermute x13, starting transfers between devices, swap(): return lax.ppermute(block, 'op', [(i, i ^ e) for i in range(n_op)])  11.1 us
    ppermute x6, waiting for transfers between devices, onward(): return lax.ppermute(block, 'blk', pairs)  10.5 us
    all_to_all x1, blocking collectives, totals(): return lax.all_to_all(parts, ('blk', 'op'), 0, 0, tiled=True)  9.73 us
    all_to_all x1, starting transfers between devices, totals(): return lax.all_to_all(parts, ('blk', 'op'), 0, 0, tiled=True)  4.63 us
    ppermute x13, waiting for transfers between devices, swap(): return lax.ppermute(block, 'op', [(i, i ^ e) for i in range(n_op)])  3.95 us
    all_to_all x1, waiting for transfers between devices, totals(): return lax.all_to_all(parts, ('blk', 'op'), 0, 0, tiled=True)  3.36 us
  transfers between devices with their start and end apart: 20, of which 6 were waited for; matrix products, arithmetic and copies ran while one was open for 0% of the time, Pallas kernels for 14%

profile of v27, /device:TPU:0, one launch (start us, length us, event | category | flops | bytes accessed | tf_op | source)
XLA Modules:
  0.0 70.7 jit_solution(11850206133679815162)
XLA Ops:
  0.6 0.0 copy-start.3
  0.6 0.0 copy-start
  0.7 4.1 %collective-permute-start.1 = (bf16[2,256,256]{2,1,0:T(8,128)(2,1)}, bf16[2,256,256]{2,1,0:T(8,128)(2,1)S(1)}, u32[]{:S(2)}, u32[]{:S(2)}) collective-permute-start(bf16[2,256,256]{2,1,0:T(8,128)(2,1)} %bitcast.2), channel_id=1, source_target_pairs={{0,8},{8,12},{12,4},{4,0},{1,9},{9,13},{13,5},{5,1},{2,10},{10,14}... | collective-permute-start | bytes 786440 | tf_op jit(solution)/shard_map/ppermute | solution.py:141
  4.7 0.0 copy-done.3
  4.7 0.0 collective-permute-start.2
  4.7 1.1 %collective-permute-done.2._ = s32[2]{0:T(128)S(1)} collective-permute-done((s32[2]{0:T(128)S(1)}, s32[2]{0:T(128)S(1)}, u32[]{:S(2)}, u32[]{:S(2)}) %collective-permute-start.2) | collective-permute-done | bytes 40 | tf_op jit(solution)/shard_map/ppermute | solution.py:145
  5.9 1.9 %shard_map.103 = (bf16[256,256]{1,0:T(8,128)(2,1)S(1)}, bf16[256,128]{1,0:T(8,128)(2,1)S(1)}, bf16[256,256]{1,0:T(8,128)(2,1)S(1)}, bf16[256,128]{1,0:T(8,128)(2...) custom-call(s32[2]{0:T(128)S(1)} %copy-done.3, s32[2]{0:T(128)S(1)} %collective-permute-done.2._, ...), custom_call_target="tpu_custom_call" | custom-call | bytes 1048576 | tf_op jit(solution)/shard_map/pallas_call | solution.py:113
  7.8 1.6 %collective-permute-start.3 = (bf16[144,256]{1,0:T(8,128)(2,1)S(1)}, bf16[144,256]{1,0:T(8,128)(2,1)S(1)}, u32[]{:S(2)}, u32[]{:S(2)}) collective-permute-start(bf16[144,256]{1,0:T(8,128)(2,1)S(1)} %get-tuple-element.59), channel_id=1, source_target_pairs={{0,2},{1,3},{2,0},{3,1},{4,6},{5,7},{6,4},{7,5},{8,10},{9,11},{10,... | collective-permute-start | bytes 221192 | tf_op jit(solution)/shard_map/ppermute | solution.py:145
  9.3 0.0 copy-done
  9.3 0.5 collective-permute-start
  9.9 2.8 %collective-permute-done.3.refs_1_.refs_5_ = bf16[144,256]{1,0:T(8,128)(2,1)S(1)} collective-permute-done((bf16[144,256]{1,0:T(8,128)(2,1)S(1)}, bf16[144,256]{1,0:T(8,128)(2,1)S(1)}, u32[]{:S(2)}, u32[]{:S(2)}) %collective-permute-start.3) | collective-permute-done | bytes 73760 | tf_op jit(solution)/shard_map/ppermute | solution.py:145
  12.7 0.0 collective-permute-done.1.refs_2_
  12.7 0.0 copy-start.1
  12.7 0.0 copy-start.2
  12.7 0.0 copy-start.4
  12.7 0.0 copy-start.5
  12.7 1.6 %collective-permute-start.4 = (bf16[2,256,256]{2,1,0:T(8,128)(2,1)S(1)}, bf16[2,256,256]{2,1,0:T(8,128)(2,1)S(1)}, u32[]{:S(2)}, u32[]{:S(2)}) collective-permute-start(bf16[2,256,256]{2,1,0:T(8,128)(2,1)S(1)} %collective-permute-done.1.refs_2_), channel_id=1, source_target_pairs={{0,8},{8,12},{12,4},{4,0},{1,9},{9,13},{13,5},{5,1},{2,10},{10,14}... | collective-permute-start | bytes 786440 | tf_op jit(solution)/shard_map/ppermute | solution.py:141
  14.3 0.6 collective-permute-start.5
  14.9 1.8 %collective-permute-start.7 = (bf16[2,256,256]{2,1,0:T(8,128)(2,1)S(1)}, bf16[2,256,256]{2,1,0:T(8,128)(2,1)S(1)}, u32[]{:S(2)}, u32[]{:S(2)}) collective-permute-start(bf16[2,256,256]{2,1,0:T(8,128)(2,1)S(1)} %collective-permute-done.1.refs_2_), channel_id=1, source_target_pairs={{0,2},{1,3},{2,0},{3,1},{4,6},{5,7},{6,4},{7,5},{8,10},{9,11},{10,... | collective-permute-start | bytes 786440 | tf_op jit(solution)/shard_map/ppermute | solution.py:145
  16.7 0.0 copy-done.1
  16.7 0.0 copy-done.2
  16.7 0.0 copy-done.4
  16.7 0.0 copy-done.5
  16.7 1.3 %shard_map.104 = (s32[16]{0:T(128)S(1)}, s32[4]{0:T(128)S(1)}, s32[4]{0:T(128)S(1)}, f32[4,256,128]{2,1,0:T(8,128)S(1)}, f32[1,512]{1,0:T(1,128)S(1)}) custom-call(s32[4]{0:T(128)S(1)} %copy-done.4, s32[4]{0:T(128)S(1)} %copy-done.5, f32[4,256]{1,0:T(4,128)S(1)} %copy-done.1, f32[1,512]{1,0:T(1,128)S(1)} %bitcast.5, ...), custom_call_target="tpu_custom_call" | custom-call | tf_op jit(solution)/shard_map/pallas_call | solution.py:113
  18.1 3.3 %collective-permute-done.5.refs_5_ = bf16[256,128]{1,0:T(8,128)(2,1)S(1)} collective-permute-done((bf16[256,128]{1,0:T(8,128)(2,1)S(1)}, bf16[256,128]{1,0:T(8,128)(2,1)S(1)}, u32[]{:S(2)}, u32[]{:S(2)}) %collective-permute-start.5) | collective-permute-done | bytes 65568 | tf_op jit(solution)/shard_map/ppermute | solution.py:141
  21.3 0.0 collective-permute-done.refs_1_
  21.3 0.0 collective-permute-done.4.refs_0_
  21.3 2.5 %collective-permute-start.8 = (bf16[2,256,256]{2,1,0:T(8,128)(2,1)S(1)}, bf16[2,256,256]{2,1,0:T(8,128)(2,1)S(1)}, u32[]{:S(2)}, u32[]{:S(2)}) collective-permute-start(bf16[2,256,256]{2,1,0:T(8,128)(2,1)S(1)} %collective-permute-done.4.refs_0_), channel_id=1, source_target_pairs={{0,8},{8,12},{12,4},{4,0},{1,9},{9,13},{13,5},{5,1},{2,10},{10,14}... | collective-permute-start | bytes 786440 | tf_op jit(solution)/shard_map/ppermute | solution.py:141
  23.8 0.0 collective-permute-start.10
  23.8 0.0 collective-permute-start.9
  23.8 1.5 %collective-permute-start.6 = (bf16[2,256,256]{2,1,0:T(8,128)(2,1)S(1)}, bf16[2,256,256]{2,1,0:T(8,128)(2,1)S(1)}, u32[]{:S(2)}, u32[]{:S(2)}) collective-permute-start(bf16[2,256,256]{2,1,0:T(8,128)(2,1)S(1)} %collective-permute-done.4.refs_0_), channel_id=1, source_target_pairs={{0,2},{1,3},{2,0},{3,1},{4,6},{5,7},{6,4},{7,5},{8,10},{9,11},{10,... | collective-permute-start | bytes 786440 | tf_op jit(solution)/shard_map/ppermute | solution.py:145
  25.3 5.1 %collective-permute-done.10.refs_7_ = bf16[256,128]{1,0:T(8,128)(2,1)S(1)} collective-permute-done((bf16[256,128]{1,0:T(8,128)(2,1)S(1)}, bf16[256,128]{1,0:T(8,128)(2,1)S(1)}, u32[]{:S(2)}, u32[]{:S(2)}) %collective-permute-start.10) | collective-permute-done | bytes 65568 | tf_op jit(solution)/shard_map/ppermute | solution.py:141
  30.4 0.0 collective-permute-done.7.refs_3_
  30.4 0.0 collective-permute-done.9.refs_6_
  30.4 0.0 collective-permute-done.8.refs_2_
  30.4 1.6 %collective-permute-start.13 = (bf16[2,256,256]{2,1,0:T(8,128)(2,1)S(1)}, bf16[2,256,256]{2,1,0:T(8,128)(2,1)S(1)}, u32[]{:S(2)}, u32[]{:S(2)}) collective-permute-start(bf16[2,256,256]{2,1,0:T(8,128)(2,1)S(1)} %collective-permute-done.8.refs_2_), channel_id=1, source_target_pairs={{0,2},{1,3},{2,0},{3,1},{4,6},{5,7},{6,4},{7,5},{8,10},{9,11},{10,... | collective-permute-start | bytes 786440 | tf_op jit(solution)/shard_map/ppermute | solution.py:145
  32.0 3.1 %collective-permute-start.12 = (bf16[256,256]{1,0:T(8,128)(2,1)S(1)}, bf16[256,256]{1,0:T(8,128)(2,1)S(1)}, u32[]{:S(2)}, u32[]{:S(2)}) collective-permute-start(bf16[256,256]{1,0:T(8,128)(2,1)S(1)} %get-tuple-element.82), channel_id=1, source_target_pairs={{0,12},{8,4},{12,0},{4,8},{1,13},{9,5},{13,1},{5,9},{2,14},{10,6},... | collective-permute-start | bytes 393224 | tf_op jit(solution)/shard_map/ppermute | solution.py:141
  35.1 0.0 collective-permute-start.11
  35.1 1.7 %shard_map.105 = (bf16[2,256,256]{2,1,0:T(8,128)(2,1)S(1)}, bf16[2,4,256,256]{3,2,1,0:T(8,128)(2,1)S(1)}, bf16[2,2,2,256,256]{4,3,2,1,0:T(8,128)(2,1)}) custom-call(s32[4]{0:T(128)S(1)} %get-tuple-element.70.widths, bf16[2,256,256]{2,1,0:T(8,128)(2,1)S(1)} %bitcast.4, bf16[2,256,256]{2,1,0:T(8,128)(2,1)S(1)} %collective-permute-done.refs_1_, ...), custom_call_target="tpu_custom_call" | custom-call | flops 268435456 | bytes 4194304 | tf_op jit(solution)/shard_map/pallas_call | solution.py:113
  36.8 2.0 %collective-permute-done.12.refs_6_ = bf16[256,256]{1,0:T(8,128)(2,1)S(1)} collective-permute-done((bf16[256,256]{1,0:T(8,128)(2,1)S(1)}, bf16[256,256]{1,0:T(8,128)(2,1)S(1)}, u32[]{:S(2)}, u32[]{:S(2)}) %collective-permute-start.12) | collective-permute-done | bytes 131104 | tf_op jit(solution)/shard_map/ppermute | solution.py:141
  38.8 0.0 collective-permute-done.6.refs_1_
  38.8 0.0 collective-permute-done.11.refs_8_
  38.8 0.0 collective-permute-done.13.refs_3_
  38.8 2.7 %shard_map.106 = (bf16[4,256,256]{2,1,0:T(8,128)(2,1)S(1)}, bf16[4,256,256]{2,1,0:T(8,128)(2,1)S(1)}, bf16[2,2,2,256,256]{4,3,2,1,0:T(8,128)(2,1)}, f32[16,1,128]{2,1,0:T(1,128)}) custom-call(s32[16]{0:T(128)S(1)} %get-tuple-element.69.src, s32[4]{0:T(128)S(1)} %get-tuple-element.70.widths, bf16[2,256,256]{2,1,0:T(8,128)(2,1)S(1)} %collective-permute-done.4.refs_0_, ...), custom_call_target="tpu_custom_call" | custom-call | flops 1073741824 | bytes 6291456 | tf_op jit(solution)/shard_map/pallas_call | solution.py:113
  41.5 0.1 collective-permute-start.14
  41.6 4.6 %all-to-all-start = ((f32[16,1,128]{2,1,0:T(1,128)}), f32[16,1,128]{2,1,0:T(1,128)S(1)}, u32[]{:S(2)}, u32[]{:S(2)}) async-start(f32[16,1,128]{2,1,0:T(1,128)} %get-tuple-element.91), calls=%async_computation | async-start | bytes 16384 | tf_op jit(solution)/shard_map/all_to_all | solution.py:661
  46.2 0.0 collective-permute-done.14.other
  46.2 1.0 %shard_map.107 = (f32[4,256,256]{2,1,0:T(8,128)S(1)}, bf16[2,4,64,256]{3,2,1,0:T(8,128)(2,1)}) custom-call(bf16[4,256,256]{2,1,0:T(8,128)(2,1)S(1)} %get-tuple-element.95.mine, bf16[4,256,256]{2,1,0:T(8,128)(2,1)S(1)} %collective-permute-done.14.other, bf16[4,256,256]{2,1,0:T(8,128)(2,1)S(1)} %get-tuple-element.94.raw_in.refs_3_, ...), custom_call_target="tpu_custom_call" | custom-call | bytes 4194304 | tf_op jit(solution)/shard_map/pallas_call | solution.py:113
  47.2 1.9 %collective-permute-start.15 = (bf16[2,4,64,256]{3,2,1,0:T(8,128)(2,1)}, bf16[2,4,64,256]{3,2,1,0:T(8,128)(2,1)S(1)}, u32[]{:S(2)}, u32[]{:S(2)}) collective-permute-start(bf16[2,4,64,256]{3,2,1,0:T(8,128)(2,1)} %get-tuple-element.100), channel_id=1, source_target_pairs={{0,2},{1,3},{2,0},{3,1},{4,6},{5,7},{6,4},{7,5},{8,10},{9,11},{10,... | collective-permute-start | bytes 786440 | tf_op jit(solution)/shard_map/ppermute | solution.py:145
  49.2 3.4 %all-to-all-done.refs_2_.parts1 = f32[16,1,128]{2,1,0:T(1,128)S(1)} async-done(((f32[16,1,128]{2,1,0:T(1,128)}), f32[16,1,128]{2,1,0:T(1,128)S(1)}, u32[]{:S(2)}, u32[]{:S(2)}) %all-to-all-start) | async-done | bytes 8224 | tf_op jit(solution)/shard_map/all_to_all | solution.py:661
  52.5 4.2 %shard_map.108 = (f32[16,1,128]{2,1,0:T(1,128)S(1)}, bf16[4,4,64,256]{3,2,1,0:T(8,128)(2,1)S(1)}, bf16[1,4,64,256]{3,2,1,0:T(8,128)(2,1)S(1)}, bf16[2,4,64,256]{...) custom-call(s32[16]{0:T(128)S(1)} %get-tuple-element.69.src, s32[4]{0:T(128)S(1)} %get-tuple-element.70.widths, ...), custom_call_target="tpu_custom_call" | custom-call | flops 4294967296 | bytes 25165824 | tf_op jit(solution)/shard_map/pallas_call | solution.py:113
  56.7 0.6 collective-permute-start.17
  57.3 0.6 collective-permute-start.18
  57.9 0.0 collective-permute-done.15.refs_0_
  58.0 1.0 %collective-permute-start.16 = (bf16[1,4,64,256]{3,2,1,0:T(8,128)(2,1)S(1)}, bf16[1,4,64,256]{3,2,1,0:T(8,128)(2,1)S(1)}, u32[]{:S(2)}, u32[]{:S(2)}) collective-permute-start(bf16[1,4,64,256]{3,2,1,0:T(8,128)(2,1)S(1)} %get-tuple-element.102), channel_id=1, source_target_pairs={{0,1},{1,0},{2,3},{3,2},{4,5},{5,4},{6,7},{7,6},{8,9},{9,8},{10,11... | collective-permute-start | bytes 393224 | tf_op jit(solution)/shard_map/ppermute | solution.py:145
  59.0 9.7 %all_to_all.10.parts2 = f32[16,1,128]{2,1,0:T(1,128)S(1)} all-to-all(f32[16,1,128]{2,1,0:T(1,128)S(1)} %get-tuple-element.97), channel_id=1, replica_groups=mesh['grp'=2,'blk'=4,'op'=4] {'blk','op'}, dimensions={0} | all-to-all | bytes 16384 | tf_op jit(solution)/shard_map/all_to_all | solution.py:661
  68.7 0.0 collective-permute-done.18.refs_3_
  68.7 0.0 collective-permute-done.17.refs_2_
  68.7 0.0 collective-permute-done.16.refs_1_
  68.7 2.0 %shard_map.109 = (bf16[4,64,512]{2,1,0:T(8,128)(2,1)}, bf16[4,64,512]{2,1,0:T(8,128)(2,1)}, f32[1]{0:T(128)}) custom-call(s32[4]{0:T(128)S(1)} %get-tuple-element.68.slots, f32[16,1,128]{2,1,0:T(1,128)S(1)} %all-to-all-done.refs_2_.parts1, f32[16,1,128]{2,1,0:T(1,128)S(1)} %all_to_all.10.parts2, f32[4,256,128]{2,1,0:T(8,128)S(1)} %get-tuple-element.89.refs_11_.diag.refs_5_, ...), custom_call_target="tpu_custom_call" | custom-call | bytes 4194304 | tf_op jit(solution)/shard_map/pallas_call | solution.py:113
Async XLA Ops:
  0.6 4.1 %copy-start.3 = (s32[2]{0:T(128)S(1)}, s32[2]{0:T(128)}, u32[]{:S(2)}) copy-start(s32[2]{0:T(128)} %shift.1) | copy-start | bytes 28
  0.6 8.7 %copy-start = (bf16[2,1,256,256]{3,2,1,0:T(8,128)(2,1)S(1)}, bf16[2,1,256,256]{3,2,1,0:T(8,128)(2,1)}, u32[]{:S(2)}) copy-start(bf16[2,1,256,256]{3,2,1,0:T(8,128)(2,1)} %param.9) | copy-start | bytes 786436
  0.7 12.0 %collective-permute-start.1 = (bf16[2,256,256]{2,1,0:T(8,128)(2,1)}, bf16[2,256,256]{2,1,0:T(8,128)(2,1)S(1)}, u32[]{:S(2)}, u32[]{:S(2)}) collective-permute-start(bf16[2,256,256]{2,1,0:T(8,128)(2,1)} %bitcast.2), channel_id=1, source_target_pairs={{0,8},{8,12},{12,4},{4,0},{1,9},{9,13},{13,5},{5,1},{2,10},{10,14}... | collective-permute-start | bytes 786440 | tf_op jit(solution)/shard_map/ppermute | solution.py:141
  4.7 1.1 %collective-permute-start.2 = (s32[2]{0:T(128)S(1)}, s32[2]{0:T(128)S(1)}, u32[]{:S(2)}, u32[]{:S(2)}) collective-permute-start(s32[2]{0:T(128)S(1)} %copy-done.3), channel_id=1, source_target_pairs={{0,1},{1,0},{2,3},{3,2},{4,5},{5,4},{6,7},{7,6},{8,9},{9,8},{10,11... | collective-permute-start | bytes 32 | tf_op jit(solution)/shard_map/ppermute | solution.py:145
  7.8 4.9 %collective-permute-start.3 = (bf16[144,256]{1,0:T(8,128)(2,1)S(1)}, bf16[144,256]{1,0:T(8,128)(2,1)S(1)}, u32[]{:S(2)}, u32[]{:S(2)}) collective-permute-start(bf16[144,256]{1,0:T(8,128)(2,1)S(1)} %get-tuple-element.59), channel_id=1, source_target_pairs={{0,2},{1,3},{2,0},{3,1},{4,6},{5,7},{6,4},{7,5},{8,10},{9,11},{10,... | collective-permute-start | bytes 221192 | tf_op jit(solution)/shard_map/ppermute | solution.py:145
  9.3 12.0 %collective-permute-start = (bf16[2,256,256]{2,1,0:T(8,128)(2,1)S(1)}, bf16[2,256,256]{2,1,0:T(8,128)(2,1)S(1)}, u32[]{:S(2)}, u32[]{:S(2)}) collective-permute-start(bf16[2,256,256]{2,1,0:T(8,128)(2,1)S(1)} %bitcast.3), channel_id=1, source_target_pairs={{0,2},{1,3},{2,0},{3,1},{4,6},{5,7},{6,4},{7,5},{8,10},{9,11},{10,... | collective-permute-start | bytes 786440 | tf_op jit(solution)/shard_map/ppermute | solution.py:145
  12.7 4.0 %copy-start.1 = (f32[4,256]{1,0:T(4,128)S(1)}, f32[4,256]{1,0:T(4,128)}, u32[]{:S(2)}) copy-start(f32[4,256]{1,0:T(4,128)} %left_diag.1) | copy-start | bytes 12292
  12.7 4.0 %copy-start.2 = (f32[512]{0:T(512)S(1)}, f32[512]{0:T(512)}, u32[]{:S(2)}) copy-start(f32[512]{0:T(512)} %param.15) | copy-start | bytes 6148
  12.7 4.0 %copy-start.4 = (s32[4]{0:T(128)S(1)}, s32[4]{0:T(128)}, u32[]{:S(2)}) copy-start(s32[4]{0:T(128)} %sector.1) | copy-start | bytes 52
  12.7 4.0 %copy-start.5 = (s32[4]{0:T(128)S(1)}, s32[4]{0:T(128)}, u32[]{:S(2)}) copy-start(s32[4]{0:T(128)} %width.1) | copy-start | bytes 52
  12.7 8.6 %collective-permute-start.4 = (bf16[2,256,256]{2,1,0:T(8,128)(2,1)S(1)}, bf16[2,256,256]{2,1,0:T(8,128)(2,1)S(1)}, u32[]{:S(2)}, u32[]{:S(2)}) collective-permute-start(bf16[2,256,256]{2,1,0:T(8,128)(2,1)S(1)} %collective-permute-done.1.refs_2_), channel_id=1, source_target_pairs={{0,8},{8,12},{12,4},{4,0},{1,9},{9,13},{13,5},{5,1},{2,10},{10,14}... | collective-permute-start | bytes 786440 | tf_op jit(solution)/shard_map/ppermute | solution.py:141
  14.3 7.0 %collective-permute-start.5 = (bf16[256,128]{1,0:T(8,128)(2,1)S(1)}, bf16[256,128]{1,0:T(8,128)(2,1)S(1)}, u32[]{:S(2)}, u32[]{:S(2)}) collective-permute-start(bf16[256,128]{1,0:T(8,128)(2,1)S(1)} %get-tuple-element.55), channel_id=1, source_target_pairs={{0,8},{8,12},{12,4},{4,0},{1,9},{9,13},{13,5},{5,1},{2,10},{10,14}... | collective-permute-start | bytes 196616 | tf_op jit(solution)/shard_map/ppermute | solution.py:141
  14.9 15.5 %collective-permute-start.7 = (bf16[2,256,256]{2,1,0:T(8,128)(2,1)S(1)}, bf16[2,256,256]{2,1,0:T(8,128)(2,1)S(1)}, u32[]{:S(2)}, u32[]{:S(2)}) collective-permute-start(bf16[2,256,256]{2,1,0:T(8,128)(2,1)S(1)} %collective-permute-done.1.refs_2_), channel_id=1, source_target_pairs={{0,2},{1,3},{2,0},{3,1},{4,6},{5,7},{6,4},{7,5},{8,10},{9,11},{10,... | collective-permute-start | bytes 786440 | tf_op jit(solution)/shard_map/ppermute | solution.py:145
  21.3 9.1 %collective-permute-start.8 = (bf16[2,256,256]{2,1,0:T(8,128)(2,1)S(1)}, bf16[2,256,256]{2,1,0:T(8,128)(2,1)S(1)}, u32[]{:S(2)}, u32[]{:S(2)}) collective-permute-start(bf16[2,256,256]{2,1,0:T(8,128)(2,1)S(1)} %collective-permute-done.4.refs_0_), channel_id=1, source_target_pairs={{0,8},{8,12},{12,4},{4,0},{1,9},{9,13},{13,5},{5,1},{2,10},{10,14}... | collective-permute-start | bytes 786440 | tf_op jit(solution)/shard_map/ppermute | solution.py:141
  23.8 6.6 %collective-permute-start.10 = (bf16[256,128]{1,0:T(8,128)(2,1)S(1)}, bf16[256,128]{1,0:T(8,128)(2,1)S(1)}, u32[]{:S(2)}, u32[]{:S(2)}) collective-permute-start(bf16[256,128]{1,0:T(8,128)(2,1)S(1)} %get-tuple-element.74), channel_id=1, source_target_pairs={{0,4},{8,0},{12,8},{4,12},{1,5},{9,1},{13,9},{5,13},{2,6},{10,2},{... | collective-permute-start | bytes 196616 | tf_op jit(solution)/shard_map/ppermute | solution.py:141
  23.8 6.6 %collective-permute-start.9 = (bf16[256,128]{1,0:T(8,128)(2,1)S(1)}, bf16[256,128]{1,0:T(8,128)(2,1)S(1)}, u32[]{:S(2)}, u32[]{:S(2)}) collective-permute-start(bf16[256,128]{1,0:T(8,128)(2,1)S(1)} %collective-permute-done.5.refs_5_), channel_id=1, source_target_pairs={{0,1},{1,0},{2,3},{3,2},{4,5},{5,4},{6,7},{7,6},{8,9},{9,8},{10,11... | collective-permute-start | bytes 196616 | tf_op jit(solution)/shard_map/ppermute | solution.py:145
  23.8 15.0 %collective-permute-start.6 = (bf16[2,256,256]{2,1,0:T(8,128)(2,1)S(1)}, bf16[2,256,256]{2,1,0:T(8,128)(2,1)S(1)}, u32[]{:S(2)}, u32[]{:S(2)}) collective-permute-start(bf16[2,256,256]{2,1,0:T(8,128)(2,1)S(1)} %collective-permute-done.4.refs_0_), channel_id=1, source_target_pairs={{0,2},{1,3},{2,0},{3,1},{4,6},{5,7},{6,4},{7,5},{8,10},{9,11},{10,... | collective-permute-start | bytes 786440 | tf_op jit(solution)/shard_map/ppermute | solution.py:145
  30.4 8.4 %collective-permute-start.13 = (bf16[2,256,256]{2,1,0:T(8,128)(2,1)S(1)}, bf16[2,256,256]{2,1,0:T(8,128)(2,1)S(1)}, u32[]{:S(2)}, u32[]{:S(2)}) collective-permute-start(bf16[2,256,256]{2,1,0:T(8,128)(2,1)S(1)} %collective-permute-done.8.refs_2_), channel_id=1, source_target_pairs={{0,2},{1,3},{2,0},{3,1},{4,6},{5,7},{6,4},{7,5},{8,10},{9,11},{10,... | collective-permute-start | bytes 786440 | tf_op jit(solution)/shard_map/ppermute | solution.py:145
  32.0 6.8 %collective-permute-start.12 = (bf16[256,256]{1,0:T(8,128)(2,1)S(1)}, bf16[256,256]{1,0:T(8,128)(2,1)S(1)}, u32[]{:S(2)}, u32[]{:S(2)}) collective-permute-start(bf16[256,256]{1,0:T(8,128)(2,1)S(1)} %get-tuple-element.82), channel_id=1, source_target_pairs={{0,12},{8,4},{12,0},{4,8},{1,13},{9,5},{13,1},{5,9},{2,14},{10,6},... | collective-permute-start | bytes 393224 | tf_op jit(solution)/shard_map/ppermute | solution.py:141
  35.1 3.7 %collective-permute-start.11 = (bf16[256,128]{1,0:T(8,128)(2,1)S(1)}, bf16[256,128]{1,0:T(8,128)(2,1)S(1)}, u32[]{:S(2)}, u32[]{:S(2)}) collective-permute-start(bf16[256,128]{1,0:T(8,128)(2,1)S(1)} %collective-permute-done.10.refs_7_), channel_id=1, source_target_pairs={{0,1},{1,0},{2,3},{3,2},{4,5},{5,4},{6,7},{7,6},{8,9},{9,8},{10,11... | collective-permute-start | bytes 196616 | tf_op jit(solution)/shard_map/ppermute | solution.py:145
  41.5 4.7 %collective-permute-start.14 = (bf16[4,256,256]{2,1,0:T(8,128)(2,1)S(1)}, bf16[4,256,256]{2,1,0:T(8,128)(2,1)S(1)}, u32[]{:S(2)}, u32[]{:S(2)}) collective-permute-start(bf16[4,256,256]{2,1,0:T(8,128)(2,1)S(1)} %get-tuple-element.95.mine), channel_id=1, source_target_pairs={{0,1},{1,0},{2,3},{3,2},{4,5},{5,4},{6,7},{7,6},{8,9},{9,8},{10,11... | collective-permute-start | bytes 1572872 | tf_op jit(solution)/shard_map/ppermute | solution.py:145
  41.6 11.0 %all-to-all-start = ((f32[16,1,128]{2,1,0:T(1,128)}), f32[16,1,128]{2,1,0:T(1,128)S(1)}, u32[]{:S(2)}, u32[]{:S(2)}) async-start(f32[16,1,128]{2,1,0:T(1,128)} %get-tuple-element.91), calls=%async_computation | async-start | bytes 16384 | tf_op jit(solution)/shard_map/all_to_all | solution.py:661
  47.2 10.7 %collective-permute-start.15 = (bf16[2,4,64,256]{3,2,1,0:T(8,128)(2,1)}, bf16[2,4,64,256]{3,2,1,0:T(8,128)(2,1)S(1)}, u32[]{:S(2)}, u32[]{:S(2)}) collective-permute-start(bf16[2,4,64,256]{3,2,1,0:T(8,128)(2,1)} %get-tuple-element.100), channel_id=1, source_target_pairs={{0,2},{1,3},{2,0},{3,1},{4,6},{5,7},{6,4},{7,5},{8,10},{9,11},{10,... | collective-permute-start | bytes 786440 | tf_op jit(solution)/shard_map/ppermute | solution.py:145
  56.7 11.9 %collective-permute-start.17 = (bf16[2,4,64,256]{3,2,1,0:T(8,128)(2,1)S(1)}, bf16[2,4,64,256]{3,2,1,0:T(8,128)(2,1)S(1)}, u32[]{:S(2)}, u32[]{:S(2)}) collective-permute-start(bf16[2,4,64,256]{3,2,1,0:T(8,128)(2,1)S(1)} %get-tuple-element.103), channel_id=1, source_target_pairs={{0,2},{1,3},{2,0},{3,1},{4,6},{5,7},{6,4},{7,5},{8,10},{9,11},{10,... | collective-permute-start | bytes 786440 | tf_op jit(solution)/shard_map/ppermute | solution.py:145
  57.3 11.4 %collective-permute-start.18 = (bf16[1,4,64,256]{3,2,1,0:T(8,128)(2,1)S(1)}, bf16[1,4,64,256]{3,2,1,0:T(8,128)(2,1)S(1)}, u32[]{:S(2)}, u32[]{:S(2)}) collective-permute-start(bf16[1,4,64,256]{3,2,1,0:T(8,128)(2,1)S(1)} %get-tuple-element.104), channel_id=1, source_target_pairs={{0,3},{1,2},{2,1},{3,0},{4,7},{5,6},{6,5},{7,4},{8,11},{9,10},{10,... | collective-permute-start | bytes 393224 | tf_op jit(solution)/shard_map/ppermute | solution.py:145
  58.0 10.7 %collective-permute-start.16 = (bf16[1,4,64,256]{3,2,1,0:T(8,128)(2,1)S(1)}, bf16[1,4,64,256]{3,2,1,0:T(8,128)(2,1)S(1)}, u32[]{:S(2)}, u32[]{:S(2)}) collective-permute-start(bf16[1,4,64,256]{3,2,1,0:T(8,128)(2,1)S(1)} %get-tuple-element.102), channel_id=1, source_target_pairs={{0,1},{1,0},{2,3},{3,2},{4,5},{5,4},{6,7},{7,6},{8,9},{9,8},{10,11... | collective-permute-start | bytes 393224 | tf_op jit(solution)/shard_map/ppermute | solution.py:145

commit v28 on v27

--- a/solution.py
+++ b/solution.py
@@ -109,7 +109,7 @@
 VMEM, SMEM, HBM = pltpu.VMEM, pltpu.SMEM, pltpu.HBM
 
 
-def kernel(body, ins, outs, scratch=(), flops=0, nbytes=0):
+def kernel(body, ins, outs, scratch=(), flops=0, nbytes=0, in_place=None):
     return pl.pallas_call(
         body,
         out_shape=[
@@ -119,6 +119,7 @@
         in_specs=[pl.BlockSpec(memory_space=space) for _, space in ins],
         out_specs=[pl.BlockSpec(memory_space=space) for _, _, space in outs],
         scratch_shapes=list(scratch),
+        input_output_aliases=in_place or {},
         compiler_params=pltpu.CompilerParams(vmem_limit_bytes=VMEM_LIMIT),
         cost_estimate=pl.CostEstimate(flops=flops, bytes_accessed=nbytes, transcendentals=0),
     )(*[pltpu.with_memory_space_constraint(x, HBM) if space == HBM else x for x, space in ins])
@@ -376,6 +377,7 @@
     left, refs = take(refs, [n_pair] * len(counts))
     psi, (raw_out, inter_out, left_out, sems) = take(refs, counts)
     copies = keep(left, left_out, sems)
+    inter_out[inter_out.shape[0] - 1] = jnp.zeros_like(inter_out[0])
     products_of(psi, left, widths, 0, raw_out, inter_out)
     for copy in copies:
         copy.wait()
@@ -387,20 +389,11 @@
     left, refs = take(refs, [n_pair] * n_late)
     (right,), refs = take(refs, [n_pair])
     psi, refs = take(refs, counts)
-    raw_in, inter_in, diag, right_diag, part_out, raw_out, left_out, dots_out, inter, sems = refs
-    ready = []
-    for j, (given, own) in enumerate(((inter_in, inter), (raw_in, raw_out))):
-        ready.append(
-            pltpu.make_async_copy(given, own.at[:n_early], sems.at[n_late * n_pair + j])
-        )
-        ready[-1].start()
+    diag, right_diag, _, _, raw_out, inter, part_out, left_out, dots_out, sems = refs
     copies = keep(left, left_out, sems)
-    inter[n_blk] = jnp.zeros_like(inter[n_blk])
     products_of(
         psi, left, widths, n_early, raw_out.at[n_early:], inter.at[n_early:n_blk]
     )
-    for copy in ready:
-        copy.wait()
     cols = diag.shape[2]
     zero = jnp.zeros((8, cols), jnp.float32)
     sums = [zero, zero]
@@ -630,8 +623,8 @@
             functools.partial(early_body, n_pair, counts),
             [(tables[1], SMEM)] + left_ins + psi_ins,
             [
-                ((n_early, rows, 2 * cols), bf16, VMEM),
-                ((n_early, n_pair * terms, rows, 2 * cols), bf16, VMEM),
+                ((n_blk, rows, 2 * cols), bf16, VMEM),
+                ((n_blk + 1, n_pair * terms, rows, 2 * cols), bf16, VMEM),
                 ((n_early, n_pair, terms, rows, rows), bf16, HBM),
             ],
             [pltpu.SemaphoreType.DMA((n_early * n_pair,))],
@@ -642,7 +635,7 @@
     left, psi_by, right, (src, widths, slots, *both), (raw_early, inter_early, left_early) = gather(
         left_ops[:, 0], n_blk, n_op, pack, table, early
     )
-    n_early = raw_early.shape[0]
+    n_early = left_early.shape[0]
     n_late = n_blk - n_early
     left_ins, psi_ins, counts = inputs(left, psi_by, range(n_early, n_blk))
     right_ins = [(block, VMEM) for block in right]
@@ -660,11 +653,13 @@
     def totals(parts):
         return lax.all_to_all(parts, ("blk", "op"), 0, 0, tiled=True)
 
-    part1, raw, kept, dots1 = kernel(
+    first_ins = tables + left_ins + right_ins + psi_ins + diags
+    raw, _, part1, kept, dots1 = kernel(
         functools.partial(first_body, n_blk, n_pair, counts),
-        tables + left_ins + right_ins + psi_ins + [(raw_early, VMEM), (inter_early, VMEM)] + diags,
-        [narrow, narrow, (left_late, bf16, HBM), dots],
-        [inter, pltpu.SemaphoreType.DMA((n_late * n_pair + 2,))],
+        first_ins + [(raw_early, VMEM), (inter_early, VMEM)],
+        [narrow, (inter_early.shape, bf16, VMEM), narrow, (left_late, bf16, HBM), dots],
+        [pltpu.SemaphoreType.DMA((n_late * n_pair,))],
+        in_place={len(first_ins): 0, len(first_ins) + 1: 1},
         **cost,
     )
     parts1 = totals(dots1)

time: 70.9 us -> 72.3 us (1.020)
  local copies, waits for them, and re-layouts: 0.03 us -> 4.28 us
  waiting for transfers between devices: 17.8 us -> 15.9 us
  starting transfers between devices: 27.6 us -> 25.9 us
    unnamed x12, local copies, waits for them, and re-layouts: 0.03 us -> 4.28 us
    ppermute x6, waiting for transfers between devices: 10.5 us -> 8.36 us  [onward(): return lax.ppermute(block, 'blk', pairs)]
    ppermute x6, starting transfers between devices: 11.8 us -> 9.9 us  [onward(): return lax.ppermute(block, 'blk', pairs)]
  transfers between devices with their start and end apart: 20 -> 20, of which waited for: 6 -> 7; matrix products, arithmetic and copies ran while one was open for 0% -> 0% of each run, Pallas kernels for 14% -> 14%
where the time goes in v28:
time: 72.3 us; the launch traced here: 72 us
  starting transfers between devices  25.9 us (36%)
  waiting for transfers between devices  15.9 us (22%)
  Pallas kernels  15.5 us (21%)
  blocking collectives  9.69 us (13%)
  local copies, waits for them, and re-layouts  4.28 us (6%)
  between operations  0.73 us (1%)
    pallas_call x7, Pallas kernels, kernel(): pl.pallas_call(body, out_shape=[HBM(shape, dtype) if space == HBM else ja...  15.5 us
    ppermute x13, starting transfers between devices, swap(): return lax.ppermute(block, 'op', [(i, i ^ e) for i in range(n_op)])  10.7 us
    ppermute x6, starting transfers between devices, onward(): return lax.ppermute(block, 'blk', pairs)  9.9 us
    all_to_all x1, blocking collectives, totals(): return lax.all_to_all(parts, ('blk', 'op'), 0, 0, tiled=True)  9.69 us
    ppermute x6, waiting for transfers between devices, onward(): return lax.ppermute(block, 'blk', pairs)  8.36 us
    all_to_all x1, starting transfers between devices, totals(): return lax.all_to_all(parts, ('blk', 'op'), 0, 0, tiled=True)  5.33 us
    unnamed x12, local copies, waits for them, and re-layouts  4.28 us
    ppermute x13, waiting for transfers between devices, swap(): return lax.ppermute(block, 'op', [(i, i ^ e) for i in range(n_op)])  4.16 us
  transfers between devices with their start and end apart: 20, of which 7 were waited for; matrix products, arithmetic and copies ran while one was open for 0% of the time, Pallas kernels for 14%

profile of v28, /device:TPU:0, one launch (start us, length us, event | category | flops | bytes accessed | tf_op | source)
XLA Modules:
  0.0 72.0 jit_solution(15241630203000820484)
XLA Ops:
  0.6 4.1 %collective-permute-start.1 = (bf16[2,256,256]{2,1,0:T(8,128)(2,1)}, bf16[2,256,256]{2,1,0:T(8,128)(2,1)S(1)}, u32[]{:S(2)}, u32[]{:S(2)}) collective-permute-start(bf16[2,256,256]{2,1,0:T(8,128)(2,1)} %bitcast.2), channel_id=1, source_target_pairs={{0,8},{8,12},{12,4},{4,0},{1,9},{9,13},{13,5},{5,1},{2,10},{10,14}... | collective-permute-start | bytes 786440 | tf_op jit(solution)/shard_map/ppermute | solution.py:142
  4.7 0.0 collective-permute-start.2
  4.7 1.3 %collective-permute-done.2._ = s32[2]{0:T(128)S(1)} collective-permute-done((s32[2]{0:T(128)}, s32[2]{0:T(128)S(1)}, u32[]{:S(2)}, u32[]{:S(2)}) %collective-permute-start.2) | collective-permute-done | bytes 40 | tf_op jit(solution)/shard_map/ppermute | solution.py:146
  6.0 0.0 copy-start.3
  6.0 0.7 copy-done.3
  6.6 1.9 %shard_map.103 = (bf16[256,256]{1,0:T(8,128)(2,1)S(1)}, bf16[256,128]{1,0:T(8,128)(2,1)S(1)}, bf16[256,256]{1,0:T(8,128)(2,1)S(1)}, bf16[256,128]{1,0:T(8,128)(2...) custom-call(s32[2]{0:T(128)S(1)} %copy-done.3, s32[2]{0:T(128)S(1)} %collective-permute-done.2._, ...), custom_call_target="tpu_custom_call" | custom-call | bytes 1048576 | tf_op jit(solution)/shard_map/pallas_call | solution.py:113
  8.5 1.6 %collective-permute-start.3 = (bf16[144,256]{1,0:T(8,128)(2,1)S(1)}, bf16[144,256]{1,0:T(8,128)(2,1)S(1)}, u32[]{:S(2)}, u32[]{:S(2)}) collective-permute-start(bf16[144,256]{1,0:T(8,128)(2,1)S(1)} %get-tuple-element.59), channel_id=1, source_target_pairs={{0,2},{1,3},{2,0},{3,1},{4,6},{5,7},{6,4},{7,5},{8,10},{9,11},{10,... | collective-permute-start | bytes 221192 | tf_op jit(solution)/shard_map/ppermute | solution.py:146
  10.1 0.5 collective-permute-start
  10.6 2.6 %collective-permute-done.3.refs_1_.refs_5_ = bf16[144,256]{1,0:T(8,128)(2,1)S(1)} collective-permute-done((bf16[144,256]{1,0:T(8,128)(2,1)S(1)}, bf16[144,256]{1,0:T(8,128)(2,1)S(1)}, u32[]{:S(2)}, u32[]{:S(2)}) %collective-permute-start.3) | collective-permute-done | bytes 73760 | tf_op jit(solution)/shard_map/ppermute | solution.py:146
  13.2 0.0 collective-permute-done.1.refs_2_
  13.2 1.6 %collective-permute-start.4 = (bf16[2,256,256]{2,1,0:T(8,128)(2,1)S(1)}, bf16[2,256,256]{2,1,0:T(8,128)(2,1)S(1)}, u32[]{:S(2)}, u32[]{:S(2)}) collective-permute-start(bf16[2,256,256]{2,1,0:T(8,128)(2,1)S(1)} %collective-permute-done.1.refs_2_), channel_id=1, source_target_pairs={{0,8},{8,12},{12,4},{4,0},{1,9},{9,13},{13,5},{5,1},{2,10},{10,14}... | collective-permute-start | bytes 786440 | tf_op jit(solution)/shard_map/ppermute | solution.py:142
  14.8 0.3 collective-permute-start.5
  15.1 2.0 %collective-permute-start.7 = (bf16[2,256,256]{2,1,0:T(8,128)(2,1)S(1)}, bf16[2,256,256]{2,1,0:T(8,128)(2,1)S(1)}, u32[]{:S(2)}, u32[]{:S(2)}) collective-permute-start(bf16[2,256,256]{2,1,0:T(8,128)(2,1)S(1)} %collective-permute-done.1.refs_2_), channel_id=1, source_target_pairs={{0,2},{1,3},{2,0},{3,1},{4,6},{5,7},{6,4},{7,5},{8,10},{9,11},{10,... | collective-permute-start | bytes 786440 | tf_op jit(solution)/shard_map/ppermute | solution.py:146
  17.1 0.0 copy-start.1
  17.1 0.7 copy-done.1
  17.8 0.0 copy-start.2
  17.8 0.7 copy-done.2
  18.5 0.0 copy-start.4
  18.5 0.7 copy-done.4
  19.2 0.0 copy-start.5
  19.2 0.7 copy-done.5
  19.8 1.3 %shard_map.104 = (s32[16]{0:T(128)S(1)}, s32[4]{0:T(128)S(1)}, s32[4]{0:T(128)S(1)}, f32[4,256,128]{2,1,0:T(8,128)S(1)}, f32[1,512]{1,0:T(1,128)S(1)}) custom-call(s32[4]{0:T(128)S(1)} %copy-done.4, s32[4]{0:T(128)S(1)} %copy-done.5, f32[4,256]{1,0:T(4,128)S(1)} %copy-done.1, f32[1,512]{1,0:T(1,128)S(1)} %bitcast.5, ...), custom_call_target="tpu_custom_call" | custom-call | tf_op jit(solution)/shard_map/pallas_call | solution.py:113
  21.2 0.8 %collective-permute-done.5.refs_5_ = bf16[256,128]{1,0:T(8,128)(2,1)S(1)} collective-permute-done((bf16[256,128]{1,0:T(8,128)(2,1)S(1)}, bf16[256,128]{1,0:T(8,128)(2,1)S(1)}, u32[]{:S(2)}, u32[]{:S(2)}) %collective-permute-start.5) | collective-permute-done | bytes 65568 | tf_op jit(solution)/shard_map/ppermute | solution.py:142
  22.0 0.0 collective-permute-done.refs_1_
  22.0 0.0 collective-permute-done.4.refs_0_
  22.0 2.5 %collective-permute-start.8 = (bf16[2,256,256]{2,1,0:T(8,128)(2,1)S(1)}, bf16[2,256,256]{2,1,0:T(8,128)(2,1)S(1)}, u32[]{:S(2)}, u32[]{:S(2)}) collective-permute-start(bf16[2,256,256]{2,1,0:T(8,128)(2,1)S(1)} %collective-permute-done.4.refs_0_), channel_id=1, source_target_pairs={{0,8},{8,12},{12,4},{4,0},{1,9},{9,13},{13,5},{5,1},{2,10},{10,14}... | collective-permute-start | bytes 786440 | tf_op jit(solution)/shard_map/ppermute | solution.py:142
  24.5 0.0 collective-permute-start.10
  24.5 0.0 collective-permute-start.9
  24.5 1.5 %collective-permute-start.6 = (bf16[2,256,256]{2,1,0:T(8,128)(2,1)S(1)}, bf16[2,256,256]{2,1,0:T(8,128)(2,1)S(1)}, u32[]{:S(2)}, u32[]{:S(2)}) collective-permute-start(bf16[2,256,256]{2,1,0:T(8,128)(2,1)S(1)} %collective-permute-done.4.refs_0_), channel_id=1, source_target_pairs={{0,2},{1,3},{2,0},{3,1},{4,6},{5,7},{6,4},{7,5},{8,10},{9,11},{10,... | collective-permute-start | bytes 786440 | tf_op jit(solution)/shard_map/ppermute | solution.py:146
  26.0 4.7 %collective-permute-done.10.refs_7_ = bf16[256,128]{1,0:T(8,128)(2,1)S(1)} collective-permute-done((bf16[256,128]{1,0:T(8,128)(2,1)S(1)}, bf16[256,128]{1,0:T(8,128)(2,1)S(1)}, u32[]{:S(2)}, u32[]{:S(2)}) %collective-permute-start.10) | collective-permute-done | bytes 65568 | tf_op jit(solution)/shard_map/ppermute | solution.py:142
  30.7 0.0 collective-permute-done.7.refs_3_
  30.7 0.0 collective-permute-done.9.refs_6_
  30.7 0.0 collective-permute-done.8.refs_2_
  30.7 0.9 %collective-permute-start.13 = (bf16[2,256,256]{2,1,0:T(8,128)(2,1)S(1)}, bf16[2,256,256]{2,1,0:T(8,128)(2,1)S(1)}, u32[]{:S(2)}, u32[]{:S(2)}) collective-permute-start(bf16[2,256,256]{2,1,0:T(8,128)(2,1)S(1)} %collective-permute-done.8.refs_2_), channel_id=1, source_target_pairs={{0,2},{1,3},{2,0},{3,1},{4,6},{5,7},{6,4},{7,5},{8,10},{9,11},{10,... | collective-permute-start | bytes 786440 | tf_op jit(solution)/shard_map/ppermute | solution.py:146
  31.6 1.4 %collective-permute-start.12 = (bf16[256,256]{1,0:T(8,128)(2,1)S(1)}, bf16[256,256]{1,0:T(8,128)(2,1)S(1)}, u32[]{:S(2)}, u32[]{:S(2)}) collective-permute-start(bf16[256,256]{1,0:T(8,128)(2,1)S(1)} %get-tuple-element.82), channel_id=1, source_target_pairs={{0,12},{8,4},{12,0},{4,8},{1,13},{9,5},{13,1},{5,9},{2,14},{10,6},... | collective-permute-start | bytes 393224 | tf_op jit(solution)/shard_map/ppermute | solution.py:142
  33.0 0.0 collective-permute-start.11
  33.0 0.0 copy-start
  33.0 0.9 %copy-done = bf16[2,1,256,256]{3,2,1,0:T(8,128)(2,1)S(1)} copy-done((bf16[2,1,256,256]{3,2,1,0:T(8,128)(2,1)S(1)}, bf16[2,1,256,256]{3,2,1,0:T(8,128)(2,1)}, u32[]{:S(2)}) %copy-start) | copy-done | bytes 262168
  34.0 1.7 %shard_map.105 = (bf16[4,256,256]{2,1,0:T(8,128)(2,1)S(1)}, bf16[5,4,256,256]{3,2,1,0:T(8,128)(2,1)S(1)}, bf16[2,2,2,256,256]{4,3,2,1,0:T(8,128)(2,1)}) custom-call(s32[4]{0:T(128)S(1)} %get-tuple-element.70.widths, bf16[2,256,256]{2,1,0:T(8,128)(2,1)S(1)} %bitcast.4, bf16[2,256,256]{2,1,0:T(8,128)(2,1)S(1)} %collective-permute-done.refs_1_, ...), custom_call_target="tpu_custom_call" | custom-call | flops 268435456 | bytes 4194304 | tf_op jit(solution)/shard_map/pallas_call | solution.py:113
  35.7 2.8 %collective-permute-done.12.refs_6_ = bf16[256,256]{1,0:T(8,128)(2,1)S(1)} collective-permute-done((bf16[256,256]{1,0:T(8,128)(2,1)S(1)}, bf16[256,256]{1,0:T(8,128)(2,1)S(1)}, u32[]{:S(2)}, u32[]{:S(2)}) %collective-permute-start.12) | collective-permute-done | bytes 131104 | tf_op jit(solution)/shard_map/ppermute | solution.py:142
  38.5 0.0 collective-permute-done.6.refs_1_
  38.5 0.0 collective-permute-done.11.refs_8_
  38.5 0.3 collective-permute-done.13.refs_3_
  38.8 3.3 %shard_map.106 = (bf16[4,256,256]{2,1,0:T(8,128)(2,1)S(1)}, bf16[5,4,256,256]{3,2,1,0:T(8,128)(2,1)S(1)}, bf16[4,256,256]{2,1,0:T(8,128)(2,1)S(1)}, bf16[2,2,2,256,256]{4,3,2,1,0:T(8,128)(2,1)}, f32[16,1,128]{2,1,0:T(1,128)}) custom-call(s32[16]{0:T(128)S(1)} %get-tuple-element.69.src, ...), custom_call_target="tpu_custom_call", output_to_operand_aliasing={{0}: (13, {}), {1}: (14, {})} | custom-call | flops 1073741824 | bytes 6291456 | tf_op jit(solution)/shard_map/pallas_call | solution.py:113
  42.1 0.1 collective-permute-start.14
  42.2 5.3 %all-to-all-start = ((f32[16,1,128]{2,1,0:T(1,128)}), f32[16,1,128]{2,1,0:T(1,128)S(1)}, u32[]{:S(2)}, u32[]{:S(2)}) async-start(f32[16,1,128]{2,1,0:T(1,128)} %get-tuple-element.91), calls=%async_computation | async-start | bytes 16384 | tf_op jit(solution)/shard_map/all_to_all | solution.py:654
  47.5 0.0 collective-permute-done.14.other
  47.5 1.0 %shard_map.107 = (f32[4,256,256]{2,1,0:T(8,128)S(1)}, bf16[2,4,64,256]{3,2,1,0:T(8,128)(2,1)}) custom-call(bf16[4,256,256]{2,1,0:T(8,128)(2,1)S(1)} %get-tuple-element.95.mine, bf16[4,256,256]{2,1,0:T(8,128)(2,1)S(1)} %collective-permute-done.14.other, bf16[4,256,256]{2,1,0:T(8,128)(2,1)S(1)} %get-tuple-element.94.raw_in.refs_3_, ...), custom_call_target="tpu_custom_call" | custom-call | bytes 4194304 | tf_op jit(solution)/shard_map/pallas_call | solution.py:113
  48.6 1.9 %collective-permute-start.15 = (bf16[2,4,64,256]{3,2,1,0:T(8,128)(2,1)}, bf16[2,4,64,256]{3,2,1,0:T(8,128)(2,1)S(1)}, u32[]{:S(2)}, u32[]{:S(2)}) collective-permute-start(bf16[2,4,64,256]{3,2,1,0:T(8,128)(2,1)} %get-tuple-element.100), channel_id=1, source_target_pairs={{0,2},{1,3},{2,0},{3,1},{4,6},{5,7},{6,4},{7,5},{8,10},{9,11},{10,... | collective-permute-start | bytes 786440 | tf_op jit(solution)/shard_map/ppermute | solution.py:146
  50.5 3.4 %all-to-all-done.refs_2_.parts1 = f32[16,1,128]{2,1,0:T(1,128)S(1)} async-done(((f32[16,1,128]{2,1,0:T(1,128)}), f32[16,1,128]{2,1,0:T(1,128)S(1)}, u32[]{:S(2)}, u32[]{:S(2)}) %all-to-all-start) | async-done | bytes 8224 | tf_op jit(solution)/shard_map/all_to_all | solution.py:654
  53.8 4.2 %shard_map.108 = (f32[16,1,128]{2,1,0:T(1,128)S(1)}, bf16[4,4,64,256]{3,2,1,0:T(8,128)(2,1)S(1)}, bf16[1,4,64,256]{3,2,1,0:T(8,128)(2,1)S(1)}, bf16[2,4,64,256]{...) custom-call(s32[16]{0:T(128)S(1)} %get-tuple-element.69.src, s32[4]{0:T(128)S(1)} %get-tuple-element.70.widths, ...), custom_call_target="tpu_custom_call" | custom-call | flops 4294967296 | bytes 25165824 | tf_op jit(solution)/shard_map/pallas_call | solution.py:113
  58.1 0.6 collective-permute-start.17
  58.6 0.6 collective-permute-start.18
  59.3 0.0 collective-permute-done.15.refs_0_
  59.3 1.0 %collective-permute-start.16 = (bf16[1,4,64,256]{3,2,1,0:T(8,128)(2,1)S(1)}, bf16[1,4,64,256]{3,2,1,0:T(8,128)(2,1)S(1)}, u32[]{:S(2)}, u32[]{:S(2)}) collective-permute-start(bf16[1,4,64,256]{3,2,1,0:T(8,128)(2,1)S(1)} %get-tuple-element.102), channel_id=1, source_target_pairs={{0,1},{1,0},{2,3},{3,2},{4,5},{5,4},{6,7},{7,6},{8,9},{9,8},{10,11... | collective-permute-start | bytes 393224 | tf_op jit(solution)/shard_map/ppermute | solution.py:146
  60.3 9.7 %all_to_all.10.parts2 = f32[16,1,128]{2,1,0:T(1,128)S(1)} all-to-all(f32[16,1,128]{2,1,0:T(1,128)S(1)} %get-tuple-element.97), channel_id=1, replica_groups=mesh['grp'=2,'blk'=4,'op'=4] {'blk','op'}, dimensions={0} | all-to-all | bytes 16384 | tf_op jit(solution)/shard_map/all_to_all | solution.py:654
  70.0 0.0 collective-permute-done.18.refs_3_
  70.0 0.0 collective-permute-done.17.refs_2_
  70.0 0.0 collective-permute-done.16.refs_1_
  70.0 2.0 %shard_map.109 = (bf16[4,64,512]{2,1,0:T(8,128)(2,1)}, bf16[4,64,512]{2,1,0:T(8,128)(2,1)}, f32[1]{0:T(128)}) custom-call(s32[4]{0:T(128)S(1)} %get-tuple-element.68.slots, f32[16,1,128]{2,1,0:T(1,128)S(1)} %all-to-all-done.refs_2_.parts1, f32[16,1,128]{2,1,0:T(1,128)S(1)} %all_to_all.10.parts2, f32[4,256,128]{2,1,0:T(8,128)S(1)} %get-tuple-element.87.refs_9_.diag.refs_5_, ...), custom_call_target="tpu_custom_call" | custom-call | bytes 4194304 | tf_op jit(solution)/shard_map/pallas_call | solution.py:113
Async XLA Ops:
  0.6 12.6 %collective-permute-start.1 = (bf16[2,256,256]{2,1,0:T(8,128)(2,1)}, bf16[2,256,256]{2,1,0:T(8,128)(2,1)S(1)}, u32[]{:S(2)}, u32[]{:S(2)}) collective-permute-start(bf16[2,256,256]{2,1,0:T(8,128)(2,1)} %bitcast.2), channel_id=1, source_target_pairs={{0,8},{8,12},{12,4},{4,0},{1,9},{9,13},{13,5},{5,1},{2,10},{10,14}... | collective-permute-start | bytes 786440 | tf_op jit(solution)/shard_map/ppermute | solution.py:142
  4.7 1.3 %collective-permute-start.2 = (s32[2]{0:T(128)}, s32[2]{0:T(128)S(1)}, u32[]{:S(2)}, u32[]{:S(2)}) collective-permute-start(s32[2]{0:T(128)} %shift.1), channel_id=1, source_target_pairs={{0,1},{1,0},{2,3},{3,2},{4,5},{5,4},{6,7},{7,6},{8,9},{9,8},{10,11... | collective-permute-start | bytes 32 | tf_op jit(solution)/shard_map/ppermute | solution.py:146
  6.0 0.7 copy-start.3
  8.5 4.6 %collective-permute-start.3 = (bf16[144,256]{1,0:T(8,128)(2,1)S(1)}, bf16[144,256]{1,0:T(8,128)(2,1)S(1)}, u32[]{:S(2)}, u32[]{:S(2)}) collective-permute-start(bf16[144,256]{1,0:T(8,128)(2,1)S(1)} %get-tuple-element.59), channel_id=1, source_target_pairs={{0,2},{1,3},{2,0},{3,1},{4,6},{5,7},{6,4},{7,5},{8,10},{9,11},{10,... | collective-permute-start | bytes 221192 | tf_op jit(solution)/shard_map/ppermute | solution.py:146
  10.1 11.9 %collective-permute-start = (bf16[2,256,256]{2,1,0:T(8,128)(2,1)}, bf16[2,256,256]{2,1,0:T(8,128)(2,1)S(1)}, u32[]{:S(2)}, u32[]{:S(2)}) collective-permute-start(bf16[2,256,256]{2,1,0:T(8,128)(2,1)} %bitcast.3), channel_id=1, source_target_pairs={{0,2},{1,3},{2,0},{3,1},{4,6},{5,7},{6,4},{7,5},{8,10},{9,11},{10,... | collective-permute-start | bytes 786440 | tf_op jit(solution)/shard_map/ppermute | solution.py:146
  13.2 8.8 %collective-permute-start.4 = (bf16[2,256,256]{2,1,0:T(8,128)(2,1)S(1)}, bf16[2,256,256]{2,1,0:T(8,128)(2,1)S(1)}, u32[]{:S(2)}, u32[]{:S(2)}) collective-permute-start(bf16[2,256,256]{2,1,0:T(8,128)(2,1)S(1)} %collective-permute-done.1.refs_2_), channel_id=1, source_target_pairs={{0,8},{8,12},{12,4},{4,0},{1,9},{9,13},{13,5},{5,1},{2,10},{10,14}... | collective-permute-start | bytes 786440 | tf_op jit(solution)/shard_map/ppermute | solution.py:142
  14.8 7.2 %collective-permute-start.5 = (bf16[256,128]{1,0:T(8,128)(2,1)S(1)}, bf16[256,128]{1,0:T(8,128)(2,1)S(1)}, u32[]{:S(2)}, u32[]{:S(2)}) collective-permute-start(bf16[256,128]{1,0:T(8,128)(2,1)S(1)} %get-tuple-element.55), channel_id=1, source_target_pairs={{0,8},{8,12},{12,4},{4,0},{1,9},{9,13},{13,5},{5,1},{2,10},{10,14}... | collective-permute-start | bytes 196616 | tf_op jit(solution)/shard_map/ppermute | solution.py:142
  15.1 15.6 %collective-permute-start.7 = (bf16[2,256,256]{2,1,0:T(8,128)(2,1)S(1)}, bf16[2,256,256]{2,1,0:T(8,128)(2,1)S(1)}, u32[]{:S(2)}, u32[]{:S(2)}) collective-permute-start(bf16[2,256,256]{2,1,0:T(8,128)(2,1)S(1)} %collective-permute-done.1.refs_2_), channel_id=1, source_target_pairs={{0,2},{1,3},{2,0},{3,1},{4,6},{5,7},{6,4},{7,5},{8,10},{9,11},{10,... | collective-permute-start | bytes 786440 | tf_op jit(solution)/shard_map/ppermute | solution.py:146
  17.1 0.7 copy-start.1
  17.8 0.7 copy-start.2
  18.5 0.7 copy-start.4
  19.2 0.7 copy-start.5
  22.0 8.7 %collective-permute-start.8 = (bf16[2,256,256]{2,1,0:T(8,128)(2,1)S(1)}, bf16[2,256,256]{2,1,0:T(8,128)(2,1)S(1)}, u32[]{:S(2)}, u32[]{:S(2)}) collective-permute-start(bf16[2,256,256]{2,1,0:T(8,128)(2,1)S(1)} %collective-permute-done.4.refs_0_), channel_id=1, source_target_pairs={{0,8},{8,12},{12,4},{4,0},{1,9},{9,13},{13,5},{5,1},{2,10},{10,14}... | collective-permute-start | bytes 786440 | tf_op jit(solution)/shard_map/ppermute | solution.py:142
  24.5 6.2 %collective-permute-start.10 = (bf16[256,128]{1,0:T(8,128)(2,1)S(1)}, bf16[256,128]{1,0:T(8,128)(2,1)S(1)}, u32[]{:S(2)}, u32[]{:S(2)}) collective-permute-start(bf16[256,128]{1,0:T(8,128)(2,1)S(1)} %get-tuple-element.74), channel_id=1, source_target_pairs={{0,4},{8,0},{12,8},{4,12},{1,5},{9,1},{13,9},{5,13},{2,6},{10,2},{... | collective-permute-start | bytes 196616 | tf_op jit(solution)/shard_map/ppermute | solution.py:142
  24.5 6.2 %collective-permute-start.9 = (bf16[256,128]{1,0:T(8,128)(2,1)S(1)}, bf16[256,128]{1,0:T(8,128)(2,1)S(1)}, u32[]{:S(2)}, u32[]{:S(2)}) collective-permute-start(bf16[256,128]{1,0:T(8,128)(2,1)S(1)} %collective-permute-done.5.refs_5_), channel_id=1, source_target_pairs={{0,1},{1,0},{2,3},{3,2},{4,5},{5,4},{6,7},{7,6},{8,9},{9,8},{10,11... | collective-permute-start | bytes 196616 | tf_op jit(solution)/shard_map/ppermute | solution.py:146
  24.5 14.0 %collective-permute-start.6 = (bf16[2,256,256]{2,1,0:T(8,128)(2,1)S(1)}, bf16[2,256,256]{2,1,0:T(8,128)(2,1)S(1)}, u32[]{:S(2)}, u32[]{:S(2)}) collective-permute-start(bf16[2,256,256]{2,1,0:T(8,128)(2,1)S(1)} %collective-permute-done.4.refs_0_), channel_id=1, source_target_pairs={{0,2},{1,3},{2,0},{3,1},{4,6},{5,7},{6,4},{7,5},{8,10},{9,11},{10,... | collective-permute-start | bytes 786440 | tf_op jit(solution)/shard_map/ppermute | solution.py:146
  30.7 8.1 %collective-permute-start.13 = (bf16[2,256,256]{2,1,0:T(8,128)(2,1)S(1)}, bf16[2,256,256]{2,1,0:T(8,128)(2,1)S(1)}, u32[]{:S(2)}, u32[]{:S(2)}) collective-permute-start(bf16[2,256,256]{2,1,0:T(8,128)(2,1)S(1)} %collective-permute-done.8.refs_2_), channel_id=1, source_target_pairs={{0,2},{1,3},{2,0},{3,1},{4,6},{5,7},{6,4},{7,5},{8,10},{9,11},{10,... | collective-permute-start | bytes 786440 | tf_op jit(solution)/shard_map/ppermute | solution.py:146
  31.6 6.9 %collective-permute-start.12 = (bf16[256,256]{1,0:T(8,128)(2,1)S(1)}, bf16[256,256]{1,0:T(8,128)(2,1)S(1)}, u32[]{:S(2)}, u32[]{:S(2)}) collective-permute-start(bf16[256,256]{1,0:T(8,128)(2,1)S(1)} %get-tuple-element.82), channel_id=1, source_target_pairs={{0,12},{8,4},{12,0},{4,8},{1,13},{9,5},{13,1},{5,9},{2,14},{10,6},... | collective-permute-start | bytes 393224 | tf_op jit(solution)/shard_map/ppermute | solution.py:142
  33.0 5.5 %collective-permute-start.11 = (bf16[256,128]{1,0:T(8,128)(2,1)S(1)}, bf16[256,128]{1,0:T(8,128)(2,1)S(1)}, u32[]{:S(2)}, u32[]{:S(2)}) collective-permute-start(bf16[256,128]{1,0:T(8,128)(2,1)S(1)} %collective-permute-done.10.refs_7_), channel_id=1, source_target_pairs={{0,1},{1,0},{2,3},{3,2},{4,5},{5,4},{6,7},{7,6},{8,9},{9,8},{10,11... | collective-permute-start | bytes 196616 | tf_op jit(solution)/shard_map/ppermute | solution.py:146
  33.0 1.0 %copy-start = (bf16[2,1,256,256]{3,2,1,0:T(8,128)(2,1)S(1)}, bf16[2,1,256,256]{3,2,1,0:T(8,128)(2,1)}, u32[]{:S(2)}) copy-start(bf16[2,1,256,256]{3,2,1,0:T(8,128)(2,1)} %param.9) | copy-start | bytes 786436
  42.1 5.4 %collective-permute-start.14 = (bf16[4,256,256]{2,1,0:T(8,128)(2,1)S(1)}, bf16[4,256,256]{2,1,0:T(8,128)(2,1)S(1)}, u32[]{:S(2)}, u32[]{:S(2)}) collective-permute-start(bf16[4,256,256]{2,1,0:T(8,128)(2,1)S(1)} %get-tuple-element.95.mine), channel_id=1, source_target_pairs={{0,1},{1,0},{2,3},{3,2},{4,5},{5,4},{6,7},{7,6},{8,9},{9,8},{10,11... | collective-permute-start | bytes 1572872 | tf_op jit(solution)/shard_map/ppermute | solution.py:146
  42.2 11.7 %all-to-all-start = ((f32[16,1,128]{2,1,0:T(1,128)}), f32[16,1,128]{2,1,0:T(1,128)S(1)}, u32[]{:S(2)}, u32[]{:S(2)}) async-start(f32[16,1,128]{2,1,0:T(1,128)} %get-tuple-element.91), calls=%async_computation | async-start | bytes 16384 | tf_op jit(solution)/shard_map/all_to_all | solution.py:654
  48.6 10.7 %collective-permute-start.15 = (bf16[2,4,64,256]{3,2,1,0:T(8,128)(2,1)}, bf16[2,4,64,256]{3,2,1,0:T(8,128)(2,1)S(1)}, u32[]{:S(2)}, u32[]{:S(2)}) collective-permute-start(bf16[2,4,64,256]{3,2,1,0:T(8,128)(2,1)} %get-tuple-element.100), channel_id=1, source_target_pairs={{0,2},{1,3},{2,0},{3,1},{4,6},{5,7},{6,4},{7,5},{8,10},{9,11},{10,... | collective-permute-start | bytes 786440 | tf_op jit(solution)/shard_map/ppermute | solution.py:146
  58.1 11.9 %collective-permute-start.17 = (bf16[2,4,64,256]{3,2,1,0:T(8,128)(2,1)S(1)}, bf16[2,4,64,256]{3,2,1,0:T(8,128)(2,1)S(1)}, u32[]{:S(2)}, u32[]{:S(2)}) collective-permute-start(bf16[2,4,64,256]{3,2,1,0:T(8,128)(2,1)S(1)} %get-tuple-element.103), channel_id=1, source_target_pairs={{0,2},{1,3},{2,0},{3,1},{4,6},{5,7},{6,4},{7,5},{8,10},{9,11},{10,... | collective-permute-start | bytes 786440 | tf_op jit(solution)/shard_map/ppermute | solution.py:146
  58.6 11.3 %collective-permute-start.18 = (bf16[1,4,64,256]{3,2,1,0:T(8,128)(2,1)S(1)}, bf16[1,4,64,256]{3,2,1,0:T(8,128)(2,1)S(1)}, u32[]{:S(2)}, u32[]{:S(2)}) collective-permute-start(bf16[1,4,64,256]{3,2,1,0:T(8,128)(2,1)S(1)} %get-tuple-element.104), channel_id=1, source_target_pairs={{0,3},{1,2},{2,1},{3,0},{4,7},{5,6},{6,5},{7,4},{8,11},{9,10},{10,... | collective-permute-start | bytes 393224 | tf_op jit(solution)/shard_map/ppermute | solution.py:146
  59.3 10.7 %collective-permute-start.16 = (bf16[1,4,64,256]{3,2,1,0:T(8,128)(2,1)S(1)}, bf16[1,4,64,256]{3,2,1,0:T(8,128)(2,1)S(1)}, u32[]{:S(2)}, u32[]{:S(2)}) collective-permute-start(bf16[1,4,64,256]{3,2,1,0:T(8,128)(2,1)S(1)} %get-tuple-element.102), channel_id=1, source_target_pairs={{0,1},{1,0},{2,3},{3,2},{4,5},{5,4},{6,7},{7,6},{8,9},{9,8},{10,11... | collective-permute-start | bytes 393224 | tf_op jit(solution)/shard_map/ppermute | solution.py:146

commit v29 on v27

--- a/solution.py
+++ b/solution.py
@@ -394,11 +394,11 @@
             pltpu.make_async_copy(given, own.at[:n_early], sems.at[n_late * n_pair + j])
         )
         ready[-1].start()
-    copies = keep(left, left_out, sems)
     inter[n_blk] = jnp.zeros_like(inter[n_blk])
     products_of(
         psi, left, widths, n_early, raw_out.at[n_early:], inter.at[n_early:n_blk]
     )
+    copies = keep(left, left_out, sems)
     for copy in ready:
         copy.wait()
     cols = diag.shape[2]

time: 70.9 us -> 70.9 us (level)
  no operation moved by 1% of the time
where the time goes in v29:
time: 70.9 us; the launch traced here: 70.7 us
  starting transfers between devices  27.6 us (39%)
  waiting for transfers between devices  17.8 us (25%)
  Pallas kernels  14.8 us (21%)
  blocking collectives  9.73 us (14%)
  between operations  0.76 us (1%)
    pallas_call x7, Pallas kernels, kernel(): pl.pallas_call(body, out_shape=[HBM(shape, dtype) if space == HBM else ja...  14.8 us
    ppermute x6, starting transfers between devices, onward(): return lax.ppermute(block, 'blk', pairs)  11.8 us
    ppermute x13, starting transfers between devices, swap(): return lax.ppermute(block, 'op', [(i, i ^ e) for i in range(n_op)])  11.1 us
    ppermute x6, waiting for transfers between devices, onward(): return lax.ppermute(block, 'blk', pairs)  10.5 us
    all_to_all x1, blocking collectives, totals(): return lax.all_to_all(parts, ('blk', 'op'), 0, 0, tiled=True)  9.73 us
    all_to_all x1, starting transfers between devices, totals(): return lax.all_to_all(parts, ('blk', 'op'), 0, 0, tiled=True)  4.63 us
    ppermute x13, waiting for transfers between devices, swap(): return lax.ppermute(block, 'op', [(i, i ^ e) for i in range(n_op)])  3.95 us
    all_to_all x1, waiting for transfers between devices, totals(): return lax.all_to_all(parts, ('blk', 'op'), 0, 0, tiled=True)  3.36 us
  transfers between devices with their start and end apart: 20, of which 6 were waited for; matrix products, arithmetic and copies ran while one was open for 0% of the time, Pallas kernels for 14%

profile of v29, /device:TPU:0, one launch (start us, length us, event | category | flops | bytes accessed | tf_op | source)
XLA Modules:
  0.0 70.7 jit_solution(11850206133679815162)
XLA Ops:
  0.6 0.0 copy-start.3
  0.6 0.0 copy-start
  0.7 4.1 %collective-permute-start.1 = (bf16[2,256,256]{2,1,0:T(8,128)(2,1)}, bf16[2,256,256]{2,1,0:T(8,128)(2,1)S(1)}, u32[]{:S(2)}, u32[]{:S(2)}) collective-permute-start(bf16[2,256,256]{2,1,0:T(8,128)(2,1)} %bitcast.2), channel_id=1, source_target_pairs={{0,8},{8,12},{12,4},{4,0},{1,9},{9,13},{13,5},{5,1},{2,10},{10,14}... | collective-permute-start | bytes 786440 | tf_op jit(solution)/shard_map/ppermute | solution.py:141
  4.7 0.0 copy-done.3
  4.7 0.0 collective-permute-start.2
  4.7 1.1 %collective-permute-done.2._ = s32[2]{0:T(128)S(1)} collective-permute-done((s32[2]{0:T(128)S(1)}, s32[2]{0:T(128)S(1)}, u32[]{:S(2)}, u32[]{:S(2)}) %collective-permute-start.2) | collective-permute-done | bytes 40 | tf_op jit(solution)/shard_map/ppermute | solution.py:145
  5.9 1.9 %shard_map.103 = (bf16[256,256]{1,0:T(8,128)(2,1)S(1)}, bf16[256,128]{1,0:T(8,128)(2,1)S(1)}, bf16[256,256]{1,0:T(8,128)(2,1)S(1)}, bf16[256,128]{1,0:T(8,128)(2...) custom-call(s32[2]{0:T(128)S(1)} %copy-done.3, s32[2]{0:T(128)S(1)} %collective-permute-done.2._, ...), custom_call_target="tpu_custom_call" | custom-call | bytes 1048576 | tf_op jit(solution)/shard_map/pallas_call | solution.py:113
  7.8 1.6 %collective-permute-start.3 = (bf16[144,256]{1,0:T(8,128)(2,1)S(1)}, bf16[144,256]{1,0:T(8,128)(2,1)S(1)}, u32[]{:S(2)}, u32[]{:S(2)}) collective-permute-start(bf16[144,256]{1,0:T(8,128)(2,1)S(1)} %get-tuple-element.59), channel_id=1, source_target_pairs={{0,2},{1,3},{2,0},{3,1},{4,6},{5,7},{6,4},{7,5},{8,10},{9,11},{10,... | collective-permute-start | bytes 221192 | tf_op jit(solution)/shard_map/ppermute | solution.py:145
  9.3 0.0 copy-done
  9.3 0.5 collective-permute-start
  9.9 2.8 %collective-permute-done.3.refs_1_.refs_5_ = bf16[144,256]{1,0:T(8,128)(2,1)S(1)} collective-permute-done((bf16[144,256]{1,0:T(8,128)(2,1)S(1)}, bf16[144,256]{1,0:T(8,128)(2,1)S(1)}, u32[]{:S(2)}, u32[]{:S(2)}) %collective-permute-start.3) | collective-permute-done | bytes 73760 | tf_op jit(solution)/shard_map/ppermute | solution.py:145
  12.7 0.0 collective-permute-done.1.refs_2_
  12.7 0.0 copy-start.1
  12.7 0.0 copy-start.2
  12.7 0.0 copy-start.4
  12.7 0.0 copy-start.5
  12.7 1.6 %collective-permute-start.4 = (bf16[2,256,256]{2,1,0:T(8,128)(2,1)S(1)}, bf16[2,256,256]{2,1,0:T(8,128)(2,1)S(1)}, u32[]{:S(2)}, u32[]{:S(2)}) collective-permute-start(bf16[2,256,256]{2,1,0:T(8,128)(2,1)S(1)} %collective-permute-done.1.refs_2_), channel_id=1, source_target_pairs={{0,8},{8,12},{12,4},{4,0},{1,9},{9,13},{13,5},{5,1},{2,10},{10,14}... | collective-permute-start | bytes 786440 | tf_op jit(solution)/shard_map/ppermute | solution.py:141
  14.3 0.6 collective-permute-start.5
  14.9 1.8 %collective-permute-start.7 = (bf16[2,256,256]{2,1,0:T(8,128)(2,1)S(1)}, bf16[2,256,256]{2,1,0:T(8,128)(2,1)S(1)}, u32[]{:S(2)}, u32[]{:S(2)}) collective-permute-start(bf16[2,256,256]{2,1,0:T(8,128)(2,1)S(1)} %collective-permute-done.1.refs_2_), channel_id=1, source_target_pairs={{0,2},{1,3},{2,0},{3,1},{4,6},{5,7},{6,4},{7,5},{8,10},{9,11},{10,... | collective-permute-start | bytes 786440 | tf_op jit(solution)/shard_map/ppermute | solution.py:145
  16.7 0.0 copy-done.1
  16.7 0.0 copy-done.2
  16.7 0.0 copy-done.4
  16.7 0.0 copy-done.5
  16.7 1.3 %shard_map.104 = (s32[16]{0:T(128)S(1)}, s32[4]{0:T(128)S(1)}, s32[4]{0:T(128)S(1)}, f32[4,256,128]{2,1,0:T(8,128)S(1)}, f32[1,512]{1,0:T(1,128)S(1)}) custom-call(s32[4]{0:T(128)S(1)} %copy-done.4, s32[4]{0:T(128)S(1)} %copy-done.5, f32[4,256]{1,0:T(4,128)S(1)} %copy-done.1, f32[1,512]{1,0:T(1,128)S(1)} %bitcast.5, ...), custom_call_target="tpu_custom_call" | custom-call | tf_op jit(solution)/shard_map/pallas_call | solution.py:113
  18.1 3.3 %collective-permute-done.5.refs_5_ = bf16[256,128]{1,0:T(8,128)(2,1)S(1)} collective-permute-done((bf16[256,128]{1,0:T(8,128)(2,1)S(1)}, bf16[256,128]{1,0:T(8,128)(2,1)S(1)}, u32[]{:S(2)}, u32[]{:S(2)}) %collective-permute-start.5) | collective-permute-done | bytes 65568 | tf_op jit(solution)/shard_map/ppermute | solution.py:141
  21.3 0.0 collective-permute-done.refs_1_
  21.3 0.0 collective-permute-done.4.refs_0_
  21.3 2.5 %collective-permute-start.8 = (bf16[2,256,256]{2,1,0:T(8,128)(2,1)S(1)}, bf16[2,256,256]{2,1,0:T(8,128)(2,1)S(1)}, u32[]{:S(2)}, u32[]{:S(2)}) collective-permute-start(bf16[2,256,256]{2,1,0:T(8,128)(2,1)S(1)} %collective-permute-done.4.refs_0_), channel_id=1, source_target_pairs={{0,8},{8,12},{12,4},{4,0},{1,9},{9,13},{13,5},{5,1},{2,10},{10,14}... | collective-permute-start | bytes 786440 | tf_op jit(solution)/shard_map/ppermute | solution.py:141
  23.8 0.0 collective-permute-start.10
  23.8 0.0 collective-permute-start.9
  23.8 1.5 %collective-permute-start.6 = (bf16[2,256,256]{2,1,0:T(8,128)(2,1)S(1)}, bf16[2,256,256]{2,1,0:T(8,128)(2,1)S(1)}, u32[]{:S(2)}, u32[]{:S(2)}) collective-permute-start(bf16[2,256,256]{2,1,0:T(8,128)(2,1)S(1)} %collective-permute-done.4.refs_0_), channel_id=1, source_target_pairs={{0,2},{1,3},{2,0},{3,1},{4,6},{5,7},{6,4},{7,5},{8,10},{9,11},{10,... | collective-permute-start | bytes 786440 | tf_op jit(solution)/shard_map/ppermute | solution.py:145
  25.3 5.1 %collective-permute-done.10.refs_7_ = bf16[256,128]{1,0:T(8,128)(2,1)S(1)} collective-permute-done((bf16[256,128]{1,0:T(8,128)(2,1)S(1)}, bf16[256,128]{1,0:T(8,128)(2,1)S(1)}, u32[]{:S(2)}, u32[]{:S(2)}) %collective-permute-start.10) | collective-permute-done | bytes 65568 | tf_op jit(solution)/shard_map/ppermute | solution.py:141
  30.4 0.0 collective-permute-done.7.refs_3_
  30.4 0.0 collective-permute-done.9.refs_6_
  30.4 0.0 collective-permute-done.8.refs_2_
  30.4 1.6 %collective-permute-start.13 = (bf16[2,256,256]{2,1,0:T(8,128)(2,1)S(1)}, bf16[2,256,256]{2,1,0:T(8,128)(2,1)S(1)}, u32[]{:S(2)}, u32[]{:S(2)}) collective-permute-start(bf16[2,256,256]{2,1,0:T(8,128)(2,1)S(1)} %collective-permute-done.8.refs_2_), channel_id=1, source_target_pairs={{0,2},{1,3},{2,0},{3,1},{4,6},{5,7},{6,4},{7,5},{8,10},{9,11},{10,... | collective-permute-start | bytes 786440 | tf_op jit(solution)/shard_map/ppermute | solution.py:145
  32.0 3.1 %collective-permute-start.12 = (bf16[256,256]{1,0:T(8,128)(2,1)S(1)}, bf16[256,256]{1,0:T(8,128)(2,1)S(1)}, u32[]{:S(2)}, u32[]{:S(2)}) collective-permute-start(bf16[256,256]{1,0:T(8,128)(2,1)S(1)} %get-tuple-element.82), channel_id=1, source_target_pairs={{0,12},{8,4},{12,0},{4,8},{1,13},{9,5},{13,1},{5,9},{2,14},{10,6},... | collective-permute-start | bytes 393224 | tf_op jit(solution)/shard_map/ppermute | solution.py:141
  35.1 0.0 collective-permute-start.11
  35.1 1.7 %shard_map.105 = (bf16[2,256,256]{2,1,0:T(8,128)(2,1)S(1)}, bf16[2,4,256,256]{3,2,1,0:T(8,128)(2,1)S(1)}, bf16[2,2,2,256,256]{4,3,2,1,0:T(8,128)(2,1)}) custom-call(s32[4]{0:T(128)S(1)} %get-tuple-element.70.widths, bf16[2,256,256]{2,1,0:T(8,128)(2,1)S(1)} %bitcast.4, bf16[2,256,256]{2,1,0:T(8,128)(2,1)S(1)} %collective-permute-done.refs_1_, ...), custom_call_target="tpu_custom_call" | custom-call | flops 268435456 | bytes 4194304 | tf_op jit(solution)/shard_map/pallas_call | solution.py:113
  36.8 2.0 %collective-permute-done.12.refs_6_ = bf16[256,256]{1,0:T(8,128)(2,1)S(1)} collective-permute-done((bf16[256,256]{1,0:T(8,128)(2,1)S(1)}, bf16[256,256]{1,0:T(8,128)(2,1)S(1)}, u32[]{:S(2)}, u32[]{:S(2)}) %collective-permute-start.12) | collective-permute-done | bytes 131104 | tf_op jit(solution)/shard_map/ppermute | solution.py:141
  38.8 0.0 collective-permute-done.6.refs_1_
  38.8 0.0 collective-permute-done.11.refs_8_
  38.8 0.0 collective-permute-done.13.refs_3_
  38.8 2.7 %shard_map.106 = (bf16[4,256,256]{2,1,0:T(8,128)(2,1)S(1)}, bf16[4,256,256]{2,1,0:T(8,128)(2,1)S(1)}, bf16[2,2,2,256,256]{4,3,2,1,0:T(8,128)(2,1)}, f32[16,1,128]{2,1,0:T(1,128)}) custom-call(s32[16]{0:T(128)S(1)} %get-tuple-element.69.src, s32[4]{0:T(128)S(1)} %get-tuple-element.70.widths, bf16[2,256,256]{2,1,0:T(8,128)(2,1)S(1)} %collective-permute-done.4.refs_0_, ...), custom_call_target="tpu_custom_call" | custom-call | flops 1073741824 | bytes 6291456 | tf_op jit(solution)/shard_map/pallas_call | solution.py:113
  41.5 0.1 collective-permute-start.14
  41.6 4.6 %all-to-all-start = ((f32[16,1,128]{2,1,0:T(1,128)}), f32[16,1,128]{2,1,0:T(1,128)S(1)}, u32[]{:S(2)}, u32[]{:S(2)}) async-start(f32[16,1,128]{2,1,0:T(1,128)} %get-tuple-element.91), calls=%async_computation | async-start | bytes 16384 | tf_op jit(solution)/shard_map/all_to_all | solution.py:661
  46.2 0.0 collective-permute-done.14.other
  46.2 1.0 %shard_map.107 = (f32[4,256,256]{2,1,0:T(8,128)S(1)}, bf16[2,4,64,256]{3,2,1,0:T(8,128)(2,1)}) custom-call(bf16[4,256,256]{2,1,0:T(8,128)(2,1)S(1)} %get-tuple-element.95.mine, bf16[4,256,256]{2,1,0:T(8,128)(2,1)S(1)} %collective-permute-done.14.other, bf16[4,256,256]{2,1,0:T(8,128)(2,1)S(1)} %get-tuple-element.94.raw_in.refs_3_, ...), custom_call_target="tpu_custom_call" | custom-call | bytes 4194304 | tf_op jit(solution)/shard_map/pallas_call | solution.py:113
  47.2 1.9 %collective-permute-start.15 = (bf16[2,4,64,256]{3,2,1,0:T(8,128)(2,1)}, bf16[2,4,64,256]{3,2,1,0:T(8,128)(2,1)S(1)}, u32[]{:S(2)}, u32[]{:S(2)}) collective-permute-start(bf16[2,4,64,256]{3,2,1,0:T(8,128)(2,1)} %get-tuple-element.100), channel_id=1, source_target_pairs={{0,2},{1,3},{2,0},{3,1},{4,6},{5,7},{6,4},{7,5},{8,10},{9,11},{10,... | collective-permute-start | bytes 786440 | tf_op jit(solution)/shard_map/ppermute | solution.py:145
  49.2 3.4 %all-to-all-done.refs_2_.parts1 = f32[16,1,128]{2,1,0:T(1,128)S(1)} async-done(((f32[16,1,128]{2,1,0:T(1,128)}), f32[16,1,128]{2,1,0:T(1,128)S(1)}, u32[]{:S(2)}, u32[]{:S(2)}) %all-to-all-start) | async-done | bytes 8224 | tf_op jit(solution)/shard_map/all_to_all | solution.py:661
  52.5 4.2 %shard_map.108 = (f32[16,1,128]{2,1,0:T(1,128)S(1)}, bf16[4,4,64,256]{3,2,1,0:T(8,128)(2,1)S(1)}, bf16[1,4,64,256]{3,2,1,0:T(8,128)(2,1)S(1)}, bf16[2,4,64,256]{...) custom-call(s32[16]{0:T(128)S(1)} %get-tuple-element.69.src, s32[4]{0:T(128)S(1)} %get-tuple-element.70.widths, ...), custom_call_target="tpu_custom_call" | custom-call | flops 4294967296 | bytes 25165824 | tf_op jit(solution)/shard_map/pallas_call | solution.py:113
  56.7 0.6 collective-permute-start.17
  57.3 0.6 collective-permute-start.18
  57.9 0.0 collective-permute-done.15.refs_0_
  58.0 1.0 %collective-permute-start.16 = (bf16[1,4,64,256]{3,2,1,0:T(8,128)(2,1)S(1)}, bf16[1,4,64,256]{3,2,1,0:T(8,128)(2,1)S(1)}, u32[]{:S(2)}, u32[]{:S(2)}) collective-permute-start(bf16[1,4,64,256]{3,2,1,0:T(8,128)(2,1)S(1)} %get-tuple-element.102), channel_id=1, source_target_pairs={{0,1},{1,0},{2,3},{3,2},{4,5},{5,4},{6,7},{7,6},{8,9},{9,8},{10,11... | collective-permute-start | bytes 393224 | tf_op jit(solution)/shard_map/ppermute | solution.py:145
  59.0 9.7 %all_to_all.10.parts2 = f32[16,1,128]{2,1,0:T(1,128)S(1)} all-to-all(f32[16,1,128]{2,1,0:T(1,128)S(1)} %get-tuple-element.97), channel_id=1, replica_groups=mesh['grp'=2,'blk'=4,'op'=4] {'blk','op'}, dimensions={0} | all-to-all | bytes 16384 | tf_op jit(solution)/shard_map/all_to_all | solution.py:661
  68.7 0.0 collective-permute-done.18.refs_3_
  68.7 0.0 collective-permute-done.17.refs_2_
  68.7 0.0 collective-permute-done.16.refs_1_
  68.7 2.0 %shard_map.109 = (bf16[4,64,512]{2,1,0:T(8,128)(2,1)}, bf16[4,64,512]{2,1,0:T(8,128)(2,1)}, f32[1]{0:T(128)}) custom-call(s32[4]{0:T(128)S(1)} %get-tuple-element.68.slots, f32[16,1,128]{2,1,0:T(1,128)S(1)} %all-to-all-done.refs_2_.parts1, f32[16,1,128]{2,1,0:T(1,128)S(1)} %all_to_all.10.parts2, f32[4,256,128]{2,1,0:T(8,128)S(1)} %get-tuple-element.89.refs_11_.diag.refs_5_, ...), custom_call_target="tpu_custom_call" | custom-call | bytes 4194304 | tf_op jit(solution)/shard_map/pallas_call | solution.py:113
Async XLA Ops:
  0.6 4.1 %copy-start.3 = (s32[2]{0:T(128)S(1)}, s32[2]{0:T(128)}, u32[]{:S(2)}) copy-start(s32[2]{0:T(128)} %shift.1) | copy-start | bytes 28
  0.6 8.7 %copy-start = (bf16[2,1,256,256]{3,2,1,0:T(8,128)(2,1)S(1)}, bf16[2,1,256,256]{3,2,1,0:T(8,128)(2,1)}, u32[]{:S(2)}) copy-start(bf16[2,1,256,256]{3,2,1,0:T(8,128)(2,1)} %param.9) | copy-start | bytes 786436
  0.7 12.0 %collective-permute-start.1 = (bf16[2,256,256]{2,1,0:T(8,128)(2,1)}, bf16[2,256,256]{2,1,0:T(8,128)(2,1)S(1)}, u32[]{:S(2)}, u32[]{:S(2)}) collective-permute-start(bf16[2,256,256]{2,1,0:T(8,128)(2,1)} %bitcast.2), channel_id=1, source_target_pairs={{0,8},{8,12},{12,4},{4,0},{1,9},{9,13},{13,5},{5,1},{2,10},{10,14}... | collective-permute-start | bytes 786440 | tf_op jit(solution)/shard_map/ppermute | solution.py:141
  4.7 1.1 %collective-permute-start.2 = (s32[2]{0:T(128)S(1)}, s32[2]{0:T(128)S(1)}, u32[]{:S(2)}, u32[]{:S(2)}) collective-permute-start(s32[2]{0:T(128)S(1)} %copy-done.3), channel_id=1, source_target_pairs={{0,1},{1,0},{2,3},{3,2},{4,5},{5,4},{6,7},{7,6},{8,9},{9,8},{10,11... | collective-permute-start | bytes 32 | tf_op jit(solution)/shard_map/ppermute | solution.py:145
  7.8 4.9 %collective-permute-start.3 = (bf16[144,256]{1,0:T(8,128)(2,1)S(1)}, bf16[144,256]{1,0:T(8,128)(2,1)S(1)}, u32[]{:S(2)}, u32[]{:S(2)}) collective-permute-start(bf16[144,256]{1,0:T(8,128)(2,1)S(1)} %get-tuple-element.59), channel_id=1, source_target_pairs={{0,2},{1,3},{2,0},{3,1},{4,6},{5,7},{6,4},{7,5},{8,10},{9,11},{10,... | collective-permute-start | bytes 221192 | tf_op jit(solution)/shard_map/ppermute | solution.py:145
  9.3 12.0 %collective-permute-start = (bf16[2,256,256]{2,1,0:T(8,128)(2,1)S(1)}, bf16[2,256,256]{2,1,0:T(8,128)(2,1)S(1)}, u32[]{:S(2)}, u32[]{:S(2)}) collective-permute-start(bf16[2,256,256]{2,1,0:T(8,128)(2,1)S(1)} %bitcast.3), channel_id=1, source_target_pairs={{0,2},{1,3},{2,0},{3,1},{4,6},{5,7},{6,4},{7,5},{8,10},{9,11},{10,... | collective-permute-start | bytes 786440 | tf_op jit(solution)/shard_map/ppermute | solution.py:145
  12.7 4.0 %copy-start.1 = (f32[4,256]{1,0:T(4,128)S(1)}, f32[4,256]{1,0:T(4,128)}, u32[]{:S(2)}) copy-start(f32[4,256]{1,0:T(4,128)} %left_diag.1) | copy-start | bytes 12292
  12.7 4.0 %copy-start.2 = (f32[512]{0:T(512)S(1)}, f32[512]{0:T(512)}, u32[]{:S(2)}) copy-start(f32[512]{0:T(512)} %param.15) | copy-start | bytes 6148
  12.7 4.0 %copy-start.4 = (s32[4]{0:T(128)S(1)}, s32[4]{0:T(128)}, u32[]{:S(2)}) copy-start(s32[4]{0:T(128)} %sector.1) | copy-start | bytes 52
  12.7 4.0 %copy-start.5 = (s32[4]{0:T(128)S(1)}, s32[4]{0:T(128)}, u32[]{:S(2)}) copy-start(s32[4]{0:T(128)} %width.1) | copy-start | bytes 52
  12.7 8.6 %collective-permute-start.4 = (bf16[2,256,256]{2,1,0:T(8,128)(2,1)S(1)}, bf16[2,256,256]{2,1,0:T(8,128)(2,1)S(1)}, u32[]{:S(2)}, u32[]{:S(2)}) collective-permute-start(bf16[2,256,256]{2,1,0:T(8,128)(2,1)S(1)} %collective-permute-done.1.refs_2_), channel_id=1, source_target_pairs={{0,8},{8,12},{12,4},{4,0},{1,9},{9,13},{13,5},{5,1},{2,10},{10,14}... | collective-permute-start | bytes 786440 | tf_op jit(solution)/shard_map/ppermute | solution.py:141
  14.3 7.0 %collective-permute-start.5 = (bf16[256,128]{1,0:T(8,128)(2,1)S(1)}, bf16[256,128]{1,0:T(8,128)(2,1)S(1)}, u32[]{:S(2)}, u32[]{:S(2)}) collective-permute-start(bf16[256,128]{1,0:T(8,128)(2,1)S(1)} %get-tuple-element.55), channel_id=1, source_target_pairs={{0,8},{8,12},{12,4},{4,0},{1,9},{9,13},{13,5},{5,1},{2,10},{10,14}... | collective-permute-start | bytes 196616 | tf_op jit(solution)/shard_map/ppermute | solution.py:141
  14.9 15.5 %collective-permute-start.7 = (bf16[2,256,256]{2,1,0:T(8,128)(2,1)S(1)}, bf16[2,256,256]{2,1,0:T(8,128)(2,1)S(1)}, u32[]{:S(2)}, u32[]{:S(2)}) collective-permute-start(bf16[2,256,256]{2,1,0:T(8,128)(2,1)S(1)} %collective-permute-done.1.refs_2_), channel_id=1, source_target_pairs={{0,2},{1,3},{2,0},{3,1},{4,6},{5,7},{6,4},{7,5},{8,10},{9,11},{10,... | collective-permute-start | bytes 786440 | tf_op jit(solution)/shard_map/ppermute | solution.py:145
  21.3 9.1 %collective-permute-start.8 = (bf16[2,256,256]{2,1,0:T(8,128)(2,1)S(1)}, bf16[2,256,256]{2,1,0:T(8,128)(2,1)S(1)}, u32[]{:S(2)}, u32[]{:S(2)}) collective-permute-start(bf16[2,256,256]{2,1,0:T(8,128)(2,1)S(1)} %collective-permute-done.4.refs_0_), channel_id=1, source_target_pairs={{0,8},{8,12},{12,4},{4,0},{1,9},{9,13},{13,5},{5,1},{2,10},{10,14}... | collective-permute-start | bytes 786440 | tf_op jit(solution)/shard_map/ppermute | solution.py:141
  23.8 6.6 %collective-permute-start.10 = (bf16[256,128]{1,0:T(8,128)(2,1)S(1)}, bf16[256,128]{1,0:T(8,128)(2,1)S(1)}, u32[]{:S(2)}, u32[]{:S(2)}) collective-permute-start(bf16[256,128]{1,0:T(8,128)(2,1)S(1)} %get-tuple-element.74), channel_id=1, source_target_pairs={{0,4},{8,0},{12,8},{4,12},{1,5},{9,1},{13,9},{5,13},{2,6},{10,2},{... | collective-permute-start | bytes 196616 | tf_op jit(solution)/shard_map/ppermute | solution.py:141
  23.8 6.6 %collective-permute-start.9 = (bf16[256,128]{1,0:T(8,128)(2,1)S(1)}, bf16[256,128]{1,0:T(8,128)(2,1)S(1)}, u32[]{:S(2)}, u32[]{:S(2)}) collective-permute-start(bf16[256,128]{1,0:T(8,128)(2,1)S(1)} %collective-permute-done.5.refs_5_), channel_id=1, source_target_pairs={{0,1},{1,0},{2,3},{3,2},{4,5},{5,4},{6,7},{7,6},{8,9},{9,8},{10,11... | collective-permute-start | bytes 196616 | tf_op jit(solution)/shard_map/ppermute | solution.py:145
  23.8 15.0 %collective-permute-start.6 = (bf16[2,256,256]{2,1,0:T(8,128)(2,1)S(1)}, bf16[2,256,256]{2,1,0:T(8,128)(2,1)S(1)}, u32[]{:S(2)}, u32[]{:S(2)}) collective-permute-start(bf16[2,256,256]{2,1,0:T(8,128)(2,1)S(1)} %collective-permute-done.4.refs_0_), channel_id=1, source_target_pairs={{0,2},{1,3},{2,0},{3,1},{4,6},{5,7},{6,4},{7,5},{8,10},{9,11},{10,... | collective-permute-start | bytes 786440 | tf_op jit(solution)/shard_map/ppermute | solution.py:145
  30.4 8.4 %collective-permute-start.13 = (bf16[2,256,256]{2,1,0:T(8,128)(2,1)S(1)}, bf16[2,256,256]{2,1,0:T(8,128)(2,1)S(1)}, u32[]{:S(2)}, u32[]{:S(2)}) collective-permute-start(bf16[2,256,256]{2,1,0:T(8,128)(2,1)S(1)} %collective-permute-done.8.refs_2_), channel_id=1, source_target_pairs={{0,2},{1,3},{2,0},{3,1},{4,6},{5,7},{6,4},{7,5},{8,10},{9,11},{10,... | collective-permute-start | bytes 786440 | tf_op jit(solution)/shard_map/ppermute | solution.py:145
  32.0 6.8 %collective-permute-start.12 = (bf16[256,256]{1,0:T(8,128)(2,1)S(1)}, bf16[256,256]{1,0:T(8,128)(2,1)S(1)}, u32[]{:S(2)}, u32[]{:S(2)}) collective-permute-start(bf16[256,256]{1,0:T(8,128)(2,1)S(1)} %get-tuple-element.82), channel_id=1, source_target_pairs={{0,12},{8,4},{12,0},{4,8},{1,13},{9,5},{13,1},{5,9},{2,14},{10,6},... | collective-permute-start | bytes 393224 | tf_op jit(solution)/shard_map/ppermute | solution.py:141
  35.1 3.7 %collective-permute-start.11 = (bf16[256,128]{1,0:T(8,128)(2,1)S(1)}, bf16[256,128]{1,0:T(8,128)(2,1)S(1)}, u32[]{:S(2)}, u32[]{:S(2)}) collective-permute-start(bf16[256,128]{1,0:T(8,128)(2,1)S(1)} %collective-permute-done.10.refs_7_), channel_id=1, source_target_pairs={{0,1},{1,0},{2,3},{3,2},{4,5},{5,4},{6,7},{7,6},{8,9},{9,8},{10,11... | collective-permute-start | bytes 196616 | tf_op jit(solution)/shard_map/ppermute | solution.py:145
  41.5 4.7 %collective-permute-start.14 = (bf16[4,256,256]{2,1,0:T(8,128)(2,1)S(1)}, bf16[4,256,256]{2,1,0:T(8,128)(2,1)S(1)}, u32[]{:S(2)}, u32[]{:S(2)}) collective-permute-start(bf16[4,256,256]{2,1,0:T(8,128)(2,1)S(1)} %get-tuple-element.95.mine), channel_id=1, source_target_pairs={{0,1},{1,0},{2,3},{3,2},{4,5},{5,4},{6,7},{7,6},{8,9},{9,8},{10,11... | collective-permute-start | bytes 1572872 | tf_op jit(solution)/shard_map/ppermute | solution.py:145
  41.6 11.0 %all-to-all-start = ((f32[16,1,128]{2,1,0:T(1,128)}), f32[16,1,128]{2,1,0:T(1,128)S(1)}, u32[]{:S(2)}, u32[]{:S(2)}) async-start(f32[16,1,128]{2,1,0:T(1,128)} %get-tuple-element.91), calls=%async_computation | async-start | bytes 16384 | tf_op jit(solution)/shard_map/all_to_all | solution.py:661
  47.2 10.7 %collective-permute-start.15 = (bf16[2,4,64,256]{3,2,1,0:T(8,128)(2,1)}, bf16[2,4,64,256]{3,2,1,0:T(8,128)(2,1)S(1)}, u32[]{:S(2)}, u32[]{:S(2)}) collective-permute-start(bf16[2,4,64,256]{3,2,1,0:T(8,128)(2,1)} %get-tuple-element.100), channel_id=1, source_target_pairs={{0,2},{1,3},{2,0},{3,1},{4,6},{5,7},{6,4},{7,5},{8,10},{9,11},{10,... | collective-permute-start | bytes 786440 | tf_op jit(solution)/shard_map/ppermute | solution.py:145
  56.7 11.9 %collective-permute-start.17 = (bf16[2,4,64,256]{3,2,1,0:T(8,128)(2,1)S(1)}, bf16[2,4,64,256]{3,2,1,0:T(8,128)(2,1)S(1)}, u32[]{:S(2)}, u32[]{:S(2)}) collective-permute-start(bf16[2,4,64,256]{3,2,1,0:T(8,128)(2,1)S(1)} %get-tuple-element.103), channel_id=1, source_target_pairs={{0,2},{1,3},{2,0},{3,1},{4,6},{5,7},{6,4},{7,5},{8,10},{9,11},{10,... | collective-permute-start | bytes 786440 | tf_op jit(solution)/shard_map/ppermute | solution.py:145
  57.3 11.4 %collective-permute-start.18 = (bf16[1,4,64,256]{3,2,1,0:T(8,128)(2,1)S(1)}, bf16[1,4,64,256]{3,2,1,0:T(8,128)(2,1)S(1)}, u32[]{:S(2)}, u32[]{:S(2)}) collective-permute-start(bf16[1,4,64,256]{3,2,1,0:T(8,128)(2,1)S(1)} %get-tuple-element.104), channel_id=1, source_target_pairs={{0,3},{1,2},{2,1},{3,0},{4,7},{5,6},{6,5},{7,4},{8,11},{9,10},{10,... | collective-permute-start | bytes 393224 | tf_op jit(solution)/shard_map/ppermute | solution.py:145
  58.0 10.7 %collective-permute-start.16 = (bf16[1,4,64,256]{3,2,1,0:T(8,128)(2,1)S(1)}, bf16[1,4,64,256]{3,2,1,0:T(8,128)(2,1)S(1)}, u32[]{:S(2)}, u32[]{:S(2)}) collective-permute-start(bf16[1,4,64,256]{3,2,1,0:T(8,128)(2,1)S(1)} %get-tuple-element.102), channel_id=1, source_target_pairs={{0,1},{1,0},{2,3},{3,2},{4,5},{5,4},{6,7},{7,6},{8,9},{9,8},{10,11... | collective-permute-start | bytes 393224 | tf_op jit(solution)/shard_map/ppermute | solution.py:145

commit v30 on v27

--- a/solution.py
+++ b/solution.py
@@ -149,7 +149,7 @@
     bits = [1 << b for b in reversed(range(1, n_op.bit_length() - 1))]
     order = sorted(range(1, n_blk), key=lambda d: min(d, n_blk - d))
     left, psi, right, tables, columns = {(0, 0): own}, {}, None, None, None
-    waiting, across, late, made = {(0, 0): 0}, {}, None, None
+    waiting, across, made = {(0, 0): 0}, {}, None
     for j in range(n_blk + len(bits)):
         new, moved = {}, {}
         for (d, e), done in waiting.items():
@@ -161,8 +161,8 @@
         kept = {key: block for key, (block, _) in new.items() if key[1] == 0}
         kept.update(across)
         across = {key: block for key, (block, _) in new.items() if key[1] != 0}
-        if late is not None:
-            moved["psi"] = late
+        due = order[:2] if j == 1 else order[2:] if j == n_blk - 1 else []
+        moved["psi"] = {d: onward(columns[d], d, n_blk) for d in due}
         if j == 0:
             columns, packed = pack()
             right = [packed[0]]
@@ -176,9 +176,8 @@
             n_early = min(2, n_blk - 1)
             psi[0] = [columns[0]]
             moved["early"] = early(left, psi, n_early, tables)
-        if 2 <= j < n_blk:
-            moved["other"] = swap(psi[order[j - 2]][0], 1, n_op)
-        late = onward(columns[order[j]], order[j], n_blk) if j < n_blk - 1 else None
+        if j == 2:
+            moved["other"] = {d: swap(psi[d][0], 1, n_op) for d in order[:2]}
         if not kept:
             break
         waiting = {key: done for key, (_, done) in new.items()}
@@ -187,10 +186,9 @@
         right, tables = moved.get("right", right), moved.get("tables", tables)
         columns = moved.get("columns", columns)
         made = moved.get("early", made)
-        if "psi" in moved:
-            psi[order[j - 1]] = [moved["psi"]]
-        if "other" in moved:
-            psi[order[j - 2]].append(moved["other"])
+        psi.update({d: [block] for d, block in moved["psi"].items()})
+        for d, block in moved.get("other", {}).items():
+            psi[d].append(block)
     return left, psi, right, tables, made
 
 
@@ -595,14 +593,14 @@
     count = float(n_blk * rows * ncols)
     n_dev = n_blk * n_op
     bf16, f32, i32 = jnp.bfloat16, jnp.float32, jnp.int32
-    last = sorted(range(1, n_blk), key=lambda d: min(d, n_blk - d))[-1]
+    far = sorted(range(1, n_blk), key=lambda d: min(d, n_blk - d))[2:]
 
     def pack():
         first = swap(term_shift, 1, n_op)
         sent = kernel(
             functools.partial(pack_body, n_blk, n_op),
             [(term_shift, SMEM), (first, SMEM), (psi, HBM), (right_ops, HBM)],
-            [((rows, 2 * cols if d in (0, last) else cols), bf16, VMEM) for d in range(n_blk)]
+            [((rows, 2 * cols if d in (0, *far) else cols), bf16, VMEM) for d in range(n_blk)]
             + [((terms * width + 16, 2 * cols), bf16, VMEM)] * n_pair,
             [pltpu.VMEM(right_ops.shape, bf16), pltpu.SemaphoreType.DMA((2 * n_blk + 1,))],
             nbytes=1 << 20,

time: 70.9 us -> 71.6 us (level)
  transfers between devices with their start and end apart: 20 -> 20, of which waited for: 6 -> 7; matrix products, arithmetic and copies ran while one was open for 0% -> 0% of each run, Pallas kernels for 14% -> 14%
where the time goes in v30:
time: 71.6 us; the launch traced here: 71.4 us
  starting transfers between devices  27.7 us (39%)
  waiting for transfers between devices  18.4 us (26%)
  Pallas kernels  14.8 us (21%)
  blocking collectives  9.73 us (14%)
  between operations  0.76 us (1%)
    pallas_call x7, Pallas kernels, kernel(): pl.pallas_call(body, out_shape=[HBM(shape, dtype) if space == HBM else ja...  14.8 us
    ppermute x6, starting transfers between devices, onward(): return lax.ppermute(block, 'blk', pairs)  11.8 us
    ppermute x13, starting transfers between devices, swap(): return lax.ppermute(block, 'op', [(i, i ^ e) for i in range(n_op)])  11.6 us
    ppermute x6, waiting for transfers between devices, onward(): return lax.ppermute(block, 'blk', pairs)  11.1 us
    all_to_all x1, blocking collectives, totals(): return lax.all_to_all(parts, ('blk', 'op'), 0, 0, tiled=True)  9.73 us
    all_to_all x1, starting transfers between devices, totals(): return lax.all_to_all(parts, ('blk', 'op'), 0, 0, tiled=True)  4.29 us
    ppermute x13, waiting for transfers between devices, swap(): return lax.ppermute(block, 'op', [(i, i ^ e) for i in range(n_op)])  3.95 us
    all_to_all x1, waiting for transfers between devices, totals(): return lax.all_to_all(parts, ('blk', 'op'), 0, 0, tiled=True)  3.36 us
  transfers between devices with their start and end apart: 20, of which 7 were waited for; matrix products, arithmetic and copies ran while one was open for 0% of the time, Pallas kernels for 14%

profile of v30, /device:TPU:0, one launch (start us, length us, event | category | flops | bytes accessed | tf_op | source)
XLA Modules:
  0.0 71.4 jit_solution(12868792260789119899)
XLA Ops:
  0.6 0.0 copy-start.3
  0.6 0.0 copy-start
  0.7 4.1 %collective-permute-start.1 = (bf16[2,256,256]{2,1,0:T(8,128)(2,1)}, bf16[2,256,256]{2,1,0:T(8,128)(2,1)S(1)}, u32[]{:S(2)}, u32[]{:S(2)}) collective-permute-start(bf16[2,256,256]{2,1,0:T(8,128)(2,1)} %bitcast.2), channel_id=1, source_target_pairs={{0,8},{8,12},{12,4},{4,0},{1,9},{9,13},{13,5},{5,1},{2,10},{10,14}... | collective-permute-start | bytes 786440 | tf_op jit(solution)/shard_map/ppermute | solution.py:141
  4.7 0.0 copy-done.3
  4.7 0.0 collective-permute-start.2
  4.7 1.1 %collective-permute-done.2._ = s32[2]{0:T(128)S(1)} collective-permute-done((s32[2]{0:T(128)S(1)}, s32[2]{0:T(128)S(1)}, u32[]{:S(2)}, u32[]{:S(2)}) %collective-permute-start.2) | collective-permute-done | bytes 40 | tf_op jit(solution)/shard_map/ppermute | solution.py:145
  5.9 1.9 %shard_map.103 = (bf16[256,256]{1,0:T(8,128)(2,1)S(1)}, bf16[256,128]{1,0:T(8,128)(2,1)S(1)}, bf16[256,256]{1,0:T(8,128)(2,1)S(1)}, bf16[256,128]{1,0:T(8,128)(2...) custom-call(s32[2]{0:T(128)S(1)} %copy-done.3, s32[2]{0:T(128)S(1)} %collective-permute-done.2._, ...), custom_call_target="tpu_custom_call" | custom-call | bytes 1048576 | tf_op jit(solution)/shard_map/pallas_call | solution.py:113
  7.8 1.6 %collective-permute-start.3 = (bf16[144,256]{1,0:T(8,128)(2,1)S(1)}, bf16[144,256]{1,0:T(8,128)(2,1)S(1)}, u32[]{:S(2)}, u32[]{:S(2)}) collective-permute-start(bf16[144,256]{1,0:T(8,128)(2,1)S(1)} %get-tuple-element.60), channel_id=1, source_target_pairs={{0,2},{1,3},{2,0},{3,1},{4,6},{5,7},{6,4},{7,5},{8,10},{9,11},{10,... | collective-permute-start | bytes 221192 | tf_op jit(solution)/shard_map/ppermute | solution.py:145
  9.3 0.0 copy-done
  9.3 0.5 collective-permute-start
  9.9 2.8 %collective-permute-done.3.refs_1_.refs_5_ = bf16[144,256]{1,0:T(8,128)(2,1)S(1)} collective-permute-done((bf16[144,256]{1,0:T(8,128)(2,1)S(1)}, bf16[144,256]{1,0:T(8,128)(2,1)S(1)}, u32[]{:S(2)}, u32[]{:S(2)}) %collective-permute-start.3) | collective-permute-done | bytes 73760 | tf_op jit(solution)/shard_map/ppermute | solution.py:145
  12.7 0.0 collective-permute-done.1.refs_2_
  12.7 0.0 copy-start.1
  12.7 0.0 copy-start.2
  12.7 0.0 copy-start.4
  12.7 0.0 copy-start.5
  12.7 1.6 %collective-permute-start.4 = (bf16[2,256,256]{2,1,0:T(8,128)(2,1)S(1)}, bf16[2,256,256]{2,1,0:T(8,128)(2,1)S(1)}, u32[]{:S(2)}, u32[]{:S(2)}) collective-permute-start(bf16[2,256,256]{2,1,0:T(8,128)(2,1)S(1)} %collective-permute-done.1.refs_2_), channel_id=1, source_target_pairs={{0,8},{8,12},{12,4},{4,0},{1,9},{9,13},{13,5},{5,1},{2,10},{10,14}... | collective-permute-start | bytes 786440 | tf_op jit(solution)/shard_map/ppermute | solution.py:141
  14.3 0.6 collective-permute-start.5
  14.9 1.4 %collective-permute-start.6 = (bf16[256,128]{1,0:T(8,128)(2,1)S(1)}, bf16[256,128]{1,0:T(8,128)(2,1)S(1)}, u32[]{:S(2)}, u32[]{:S(2)}) collective-permute-start(bf16[256,128]{1,0:T(8,128)(2,1)S(1)} %get-tuple-element.63), channel_id=1, source_target_pairs={{0,4},{8,0},{12,8},{4,12},{1,5},{9,1},{13,9},{5,13},{2,6},{10,2},{... | collective-permute-start | bytes 196616 | tf_op jit(solution)/shard_map/ppermute | solution.py:141
  16.3 1.8 %collective-permute-start.8 = (bf16[2,256,256]{2,1,0:T(8,128)(2,1)S(1)}, bf16[2,256,256]{2,1,0:T(8,128)(2,1)S(1)}, u32[]{:S(2)}, u32[]{:S(2)}) collective-permute-start(bf16[2,256,256]{2,1,0:T(8,128)(2,1)S(1)} %collective-permute-done.1.refs_2_), channel_id=1, source_target_pairs={{0,2},{1,3},{2,0},{3,1},{4,6},{5,7},{6,4},{7,5},{8,10},{9,11},{10,... | collective-permute-start | bytes 786440 | tf_op jit(solution)/shard_map/ppermute | solution.py:145
  18.1 0.0 copy-done.1
  18.1 0.0 copy-done.2
  18.1 0.0 copy-done.4
  18.1 0.0 copy-done.5
  18.1 1.3 %shard_map.104 = (s32[16]{0:T(128)S(1)}, s32[4]{0:T(128)S(1)}, s32[4]{0:T(128)S(1)}, f32[4,256,128]{2,1,0:T(8,128)S(1)}, f32[1,512]{1,0:T(1,128)S(1)}) custom-call(s32[4]{0:T(128)S(1)} %copy-done.4, s32[4]{0:T(128)S(1)} %copy-done.5, f32[4,256]{1,0:T(4,128)S(1)} %copy-done.1, f32[1,512]{1,0:T(1,128)S(1)} %bitcast.5, ...), custom_call_target="tpu_custom_call" | custom-call | tf_op jit(solution)/shard_map/pallas_call | solution.py:113
  19.5 0.0 collective-permute-done.refs_1_
  19.5 2.6 %collective-permute-done.5.refs_5_ = bf16[256,128]{1,0:T(8,128)(2,1)S(1)} collective-permute-done((bf16[256,128]{1,0:T(8,128)(2,1)S(1)}, bf16[256,128]{1,0:T(8,128)(2,1)S(1)}, u32[]{:S(2)}, u32[]{:S(2)}) %collective-permute-start.5) | collective-permute-done | bytes 65568 | tf_op jit(solution)/shard_map/ppermute | solution.py:141
  22.1 1.2 %collective-permute-done.6.refs_7_ = bf16[256,128]{1,0:T(8,128)(2,1)S(1)} collective-permute-done((bf16[256,128]{1,0:T(8,128)(2,1)S(1)}, bf16[256,128]{1,0:T(8,128)(2,1)S(1)}, u32[]{:S(2)}, u32[]{:S(2)}) %collective-permute-start.6) | collective-permute-done | bytes 65568 | tf_op jit(solution)/shard_map/ppermute | solution.py:141
  23.3 0.0 collective-permute-done.4.refs_0_
  23.3 1.3 %collective-permute-start.9 = (bf16[2,256,256]{2,1,0:T(8,128)(2,1)S(1)}, bf16[2,256,256]{2,1,0:T(8,128)(2,1)S(1)}, u32[]{:S(2)}, u32[]{:S(2)}) collective-permute-start(bf16[2,256,256]{2,1,0:T(8,128)(2,1)S(1)} %collective-permute-done.4.refs_0_), channel_id=1, source_target_pairs={{0,8},{8,12},{12,4},{4,0},{1,9},{9,13},{13,5},{5,1},{2,10},{10,14}... | collective-permute-start | bytes 786440 | tf_op jit(solution)/shard_map/ppermute | solution.py:141
  24.5 0.0 collective-permute-start.10
  24.5 0.5 collective-permute-start.11
  25.0 1.5 %collective-permute-start.7 = (bf16[2,256,256]{2,1,0:T(8,128)(2,1)S(1)}, bf16[2,256,256]{2,1,0:T(8,128)(2,1)S(1)}, u32[]{:S(2)}, u32[]{:S(2)}) collective-permute-start(bf16[2,256,256]{2,1,0:T(8,128)(2,1)S(1)} %collective-permute-done.4.refs_0_), channel_id=1, source_target_pairs={{0,2},{1,3},{2,0},{3,1},{4,6},{5,7},{6,4},{7,5},{8,10},{9,11},{10,... | collective-permute-start | bytes 786440 | tf_op jit(solution)/shard_map/ppermute | solution.py:145
  26.5 0.0 collective-permute-done.8.refs_3_
  26.5 0.0 collective-permute-done.10.refs_6_
  26.5 0.0 collective-permute-done.11.refs_8_
  26.5 5.0 %collective-permute-done.9.refs_2_ = bf16[2,256,256]{2,1,0:T(8,128)(2,1)S(1)} collective-permute-done((bf16[2,256,256]{2,1,0:T(8,128)(2,1)S(1)}, bf16[2,256,256]{2,1,0:T(8,128)(2,1)S(1)}, u32[]{:S(2)}, u32[]{:S(2)}) %collective-permute-start.9) | collective-permute-done | bytes 262176 | tf_op jit(solution)/shard_map/ppermute | solution.py:141
  31.5 1.5 %collective-permute-start.13 = (bf16[2,256,256]{2,1,0:T(8,128)(2,1)S(1)}, bf16[2,256,256]{2,1,0:T(8,128)(2,1)S(1)}, u32[]{:S(2)}, u32[]{:S(2)}) collective-permute-start(bf16[2,256,256]{2,1,0:T(8,128)(2,1)S(1)} %collective-permute-done.9.refs_2_), channel_id=1, source_target_pairs={{0,2},{1,3},{2,0},{3,1},{4,6},{5,7},{6,4},{7,5},{8,10},{9,11},{10,... | collective-permute-start | bytes 786440 | tf_op jit(solution)/shard_map/ppermute | solution.py:145
  33.0 2.8 %collective-permute-start.12 = (bf16[256,256]{1,0:T(8,128)(2,1)S(1)}, bf16[256,256]{1,0:T(8,128)(2,1)S(1)}, u32[]{:S(2)}, u32[]{:S(2)}) collective-permute-start(bf16[256,256]{1,0:T(8,128)(2,1)S(1)} %get-tuple-element.84), channel_id=1, source_target_pairs={{0,12},{8,4},{12,0},{4,8},{1,13},{9,5},{13,1},{5,9},{2,14},{10,6},... | collective-permute-start | bytes 393224 | tf_op jit(solution)/shard_map/ppermute | solution.py:141
  35.8 1.7 %shard_map.105 = (bf16[2,256,256]{2,1,0:T(8,128)(2,1)S(1)}, bf16[2,4,256,256]{3,2,1,0:T(8,128)(2,1)S(1)}, bf16[2,2,2,256,256]{4,3,2,1,0:T(8,128)(2,1)}) custom-call(s32[4]{0:T(128)S(1)} %get-tuple-element.73.widths, bf16[2,256,256]{2,1,0:T(8,128)(2,1)S(1)} %bitcast.4, bf16[2,256,256]{2,1,0:T(8,128)(2,1)S(1)} %collective-permute-done.refs_1_, ...), custom_call_target="tpu_custom_call" | custom-call | flops 268435456 | bytes 4194304 | tf_op jit(solution)/shard_map/pallas_call | solution.py:113
  37.5 2.4 %collective-permute-done.12.refs_6_ = bf16[256,256]{1,0:T(8,128)(2,1)S(1)} collective-permute-done((bf16[256,256]{1,0:T(8,128)(2,1)S(1)}, bf16[256,256]{1,0:T(8,128)(2,1)S(1)}, u32[]{:S(2)}, u32[]{:S(2)}) %collective-permute-start.12) | collective-permute-done | bytes 131104 | tf_op jit(solution)/shard_map/ppermute | solution.py:141
  39.9 0.0 collective-permute-done.7.refs_1_
  39.9 0.0 collective-permute-done.13.refs_3_
  39.9 2.6 %shard_map.106 = (bf16[4,256,256]{2,1,0:T(8,128)(2,1)S(1)}, bf16[4,256,256]{2,1,0:T(8,128)(2,1)S(1)}, bf16[2,2,2,256,256]{4,3,2,1,0:T(8,128)(2,1)}, f32[16,1,128]{2,1,0:T(1,128)}) custom-call(s32[16]{0:T(128)S(1)} %get-tuple-element.72.src, s32[4]{0:T(128)S(1)} %get-tuple-element.73.widths, bf16[2,256,256]{2,1,0:T(8,128)(2,1)S(1)} %collective-permute-done.4.refs_0_, ...), custom_call_target="tpu_custom_call" | custom-call | flops 1073741824 | bytes 6291456 | tf_op jit(solution)/shard_map/pallas_call | solution.py:113
  42.5 0.1 collective-permute-start.14
  42.6 4.3 %all-to-all-start = ((f32[16,1,128]{2,1,0:T(1,128)}), f32[16,1,128]{2,1,0:T(1,128)S(1)}, u32[]{:S(2)}, u32[]{:S(2)}) async-start(f32[16,1,128]{2,1,0:T(1,128)} %get-tuple-element.93), calls=%async_computation | async-start | bytes 16384 | tf_op jit(solution)/shard_map/all_to_all | solution.py:659
  46.9 0.0 collective-permute-done.14.other
  46.9 1.0 %shard_map.107 = (f32[4,256,256]{2,1,0:T(8,128)S(1)}, bf16[2,4,64,256]{3,2,1,0:T(8,128)(2,1)}) custom-call(bf16[4,256,256]{2,1,0:T(8,128)(2,1)S(1)} %get-tuple-element.97.mine, bf16[4,256,256]{2,1,0:T(8,128)(2,1)S(1)} %collective-permute-done.14.other, bf16[4,256,256]{2,1,0:T(8,128)(2,1)S(1)} %get-tuple-element.96.raw_in.refs_3_, ...), custom_call_target="tpu_custom_call" | custom-call | bytes 4194304 | tf_op jit(solution)/shard_map/pallas_call | solution.py:113
  48.0 1.9 %collective-permute-start.15 = (bf16[2,4,64,256]{3,2,1,0:T(8,128)(2,1)}, bf16[2,4,64,256]{3,2,1,0:T(8,128)(2,1)S(1)}, u32[]{:S(2)}, u32[]{:S(2)}) collective-permute-start(bf16[2,4,64,256]{3,2,1,0:T(8,128)(2,1)} %get-tuple-element.102), channel_id=1, source_target_pairs={{0,2},{1,3},{2,0},{3,1},{4,6},{5,7},{6,4},{7,5},{8,10},{9,11},{10,... | collective-permute-start | bytes 786440 | tf_op jit(solution)/shard_map/ppermute | solution.py:145
  49.9 3.4 %all-to-all-done.refs_2_.parts1 = f32[16,1,128]{2,1,0:T(1,128)S(1)} async-done(((f32[16,1,128]{2,1,0:T(1,128)}), f32[16,1,128]{2,1,0:T(1,128)S(1)}, u32[]{:S(2)}, u32[]{:S(2)}) %all-to-all-start) | async-done | bytes 8224 | tf_op jit(solution)/shard_map/all_to_all | solution.py:659
  53.2 4.2 %shard_map.108 = (f32[16,1,128]{2,1,0:T(1,128)S(1)}, bf16[4,4,64,256]{3,2,1,0:T(8,128)(2,1)S(1)}, bf16[1,4,64,256]{3,2,1,0:T(8,128)(2,1)S(1)}, bf16[2,4,64,256]{...) custom-call(s32[16]{0:T(128)S(1)} %get-tuple-element.72.src, s32[4]{0:T(128)S(1)} %get-tuple-element.73.widths, ...), custom_call_target="tpu_custom_call" | custom-call | flops 4294967296 | bytes 25165824 | tf_op jit(solution)/shard_map/pallas_call | solution.py:113
  57.5 0.6 collective-permute-start.17
  58.0 0.6 collective-permute-start.18
  58.7 0.0 collective-permute-done.15.refs_0_
  58.7 1.0 %collective-permute-start.16 = (bf16[1,4,64,256]{3,2,1,0:T(8,128)(2,1)S(1)}, bf16[1,4,64,256]{3,2,1,0:T(8,128)(2,1)S(1)}, u32[]{:S(2)}, u32[]{:S(2)}) collective-permute-start(bf16[1,4,64,256]{3,2,1,0:T(8,128)(2,1)S(1)} %get-tuple-element.104), channel_id=1, source_target_pairs={{0,1},{1,0},{2,3},{3,2},{4,5},{5,4},{6,7},{7,6},{8,9},{9,8},{10,11... | collective-permute-start | bytes 393224 | tf_op jit(solution)/shard_map/ppermute | solution.py:145
  59.7 9.7 %all_to_all.10.parts2 = f32[16,1,128]{2,1,0:T(1,128)S(1)} all-to-all(f32[16,1,128]{2,1,0:T(1,128)S(1)} %get-tuple-element.99), channel_id=1, replica_groups=mesh['grp'=2,'blk'=4,'op'=4] {'blk','op'}, dimensions={0} | all-to-all | bytes 16384 | tf_op jit(solution)/shard_map/all_to_all | solution.py:659
  69.4 0.0 collective-permute-done.18.refs_3_
  69.4 0.0 collective-permute-done.17.refs_2_
  69.4 0.0 collective-permute-done.16.refs_1_
  69.4 2.0 %shard_map.109 = (bf16[4,64,512]{2,1,0:T(8,128)(2,1)}, bf16[4,64,512]{2,1,0:T(8,128)(2,1)}, f32[1]{0:T(128)}) custom-call(s32[4]{0:T(128)S(1)} %get-tuple-element.71.slots, f32[16,1,128]{2,1,0:T(1,128)S(1)} %all-to-all-done.refs_2_.parts1, f32[16,1,128]{2,1,0:T(1,128)S(1)} %all_to_all.10.parts2, f32[4,256,128]{2,1,0:T(8,128)S(1)} %get-tuple-element.91.refs_11_.diag.refs_5_, ...), custom_call_target="tpu_custom_call" | custom-call | bytes 4194304 | tf_op jit(solution)/shard_map/pallas_call | solution.py:113
Async XLA Ops:
  0.6 4.1 %copy-start.3 = (s32[2]{0:T(128)S(1)}, s32[2]{0:T(128)}, u32[]{:S(2)}) copy-start(s32[2]{0:T(128)} %shift.1) | copy-start | bytes 28
  0.6 8.7 %copy-start = (bf16[2,1,256,256]{3,2,1,0:T(8,128)(2,1)S(1)}, bf16[2,1,256,256]{3,2,1,0:T(8,128)(2,1)}, u32[]{:S(2)}) copy-start(bf16[2,1,256,256]{3,2,1,0:T(8,128)(2,1)} %param.9) | copy-start | bytes 786436
  0.7 12.0 %collective-permute-start.1 = (bf16[2,256,256]{2,1,0:T(8,128)(2,1)}, bf16[2,256,256]{2,1,0:T(8,128)(2,1)S(1)}, u32[]{:S(2)}, u32[]{:S(2)}) collective-permute-start(bf16[2,256,256]{2,1,0:T(8,128)(2,1)} %bitcast.2), channel_id=1, source_target_pairs={{0,8},{8,12},{12,4},{4,0},{1,9},{9,13},{13,5},{5,1},{2,10},{10,14}... | collective-permute-start | bytes 786440 | tf_op jit(solution)/shard_map/ppermute | solution.py:141
  4.7 1.1 %collective-permute-start.2 = (s32[2]{0:T(128)S(1)}, s32[2]{0:T(128)S(1)}, u32[]{:S(2)}, u32[]{:S(2)}) collective-permute-start(s32[2]{0:T(128)S(1)} %copy-done.3), channel_id=1, source_target_pairs={{0,1},{1,0},{2,3},{3,2},{4,5},{5,4},{6,7},{7,6},{8,9},{9,8},{10,11... | collective-permute-start | bytes 32 | tf_op jit(solution)/shard_map/ppermute | solution.py:145
  7.8 4.9 %collective-permute-start.3 = (bf16[144,256]{1,0:T(8,128)(2,1)S(1)}, bf16[144,256]{1,0:T(8,128)(2,1)S(1)}, u32[]{:S(2)}, u32[]{:S(2)}) collective-permute-start(bf16[144,256]{1,0:T(8,128)(2,1)S(1)} %get-tuple-element.60), channel_id=1, source_target_pairs={{0,2},{1,3},{2,0},{3,1},{4,6},{5,7},{6,4},{7,5},{8,10},{9,11},{10,... | collective-permute-start | bytes 221192 | tf_op jit(solution)/shard_map/ppermute | solution.py:145
  9.3 10.2 %collective-permute-start = (bf16[2,256,256]{2,1,0:T(8,128)(2,1)S(1)}, bf16[2,256,256]{2,1,0:T(8,128)(2,1)S(1)}, u32[]{:S(2)}, u32[]{:S(2)}) collective-permute-start(bf16[2,256,256]{2,1,0:T(8,128)(2,1)S(1)} %bitcast.3), channel_id=1, source_target_pairs={{0,2},{1,3},{2,0},{3,1},{4,6},{5,7},{6,4},{7,5},{8,10},{9,11},{10,... | collective-permute-start | bytes 786440 | tf_op jit(solution)/shard_map/ppermute | solution.py:145
  12.7 5.5 %copy-start.1 = (f32[4,256]{1,0:T(4,128)S(1)}, f32[4,256]{1,0:T(4,128)}, u32[]{:S(2)}) copy-start(f32[4,256]{1,0:T(4,128)} %left_diag.1) | copy-start | bytes 12292
  12.7 5.5 %copy-start.2 = (f32[512]{0:T(512)S(1)}, f32[512]{0:T(512)}, u32[]{:S(2)}) copy-start(f32[512]{0:T(512)} %param.15) | copy-start | bytes 6148
  12.7 5.5 %copy-start.4 = (s32[4]{0:T(128)S(1)}, s32[4]{0:T(128)}, u32[]{:S(2)}) copy-start(s32[4]{0:T(128)} %sector.1) | copy-start | bytes 52
  12.7 5.5 %copy-start.5 = (s32[4]{0:T(128)S(1)}, s32[4]{0:T(128)}, u32[]{:S(2)}) copy-start(s32[4]{0:T(128)} %width.1) | copy-start | bytes 52
  12.7 10.6 %collective-permute-start.4 = (bf16[2,256,256]{2,1,0:T(8,128)(2,1)S(1)}, bf16[2,256,256]{2,1,0:T(8,128)(2,1)S(1)}, u32[]{:S(2)}, u32[]{:S(2)}) collective-permute-start(bf16[2,256,256]{2,1,0:T(8,128)(2,1)S(1)} %collective-permute-done.1.refs_2_), channel_id=1, source_target_pairs={{0,8},{8,12},{12,4},{4,0},{1,9},{9,13},{13,5},{5,1},{2,10},{10,14}... | collective-permute-start | bytes 786440 | tf_op jit(solution)/shard_map/ppermute | solution.py:141
  14.3 7.7 %collective-permute-start.5 = (bf16[256,128]{1,0:T(8,128)(2,1)S(1)}, bf16[256,128]{1,0:T(8,128)(2,1)S(1)}, u32[]{:S(2)}, u32[]{:S(2)}) collective-permute-start(bf16[256,128]{1,0:T(8,128)(2,1)S(1)} %get-tuple-element.62), channel_id=1, source_target_pairs={{0,8},{8,12},{12,4},{4,0},{1,9},{9,13},{13,5},{5,1},{2,10},{10,14}... | collective-permute-start | bytes 196616 | tf_op jit(solution)/shard_map/ppermute | solution.py:141
  14.9 8.4 %collective-permute-start.6 = (bf16[256,128]{1,0:T(8,128)(2,1)S(1)}, bf16[256,128]{1,0:T(8,128)(2,1)S(1)}, u32[]{:S(2)}, u32[]{:S(2)}) collective-permute-start(bf16[256,128]{1,0:T(8,128)(2,1)S(1)} %get-tuple-element.63), channel_id=1, source_target_pairs={{0,4},{8,0},{12,8},{4,12},{1,5},{9,1},{13,9},{5,13},{2,6},{10,2},{... | collective-permute-start | bytes 196616 | tf_op jit(solution)/shard_map/ppermute | solution.py:141
  16.3 10.2 %collective-permute-start.8 = (bf16[2,256,256]{2,1,0:T(8,128)(2,1)S(1)}, bf16[2,256,256]{2,1,0:T(8,128)(2,1)S(1)}, u32[]{:S(2)}, u32[]{:S(2)}) collective-permute-start(bf16[2,256,256]{2,1,0:T(8,128)(2,1)S(1)} %collective-permute-done.1.refs_2_), channel_id=1, source_target_pairs={{0,2},{1,3},{2,0},{3,1},{4,6},{5,7},{6,4},{7,5},{8,10},{9,11},{10,... | collective-permute-start | bytes 786440 | tf_op jit(solution)/shard_map/ppermute | solution.py:145
  23.3 8.2 %collective-permute-start.9 = (bf16[2,256,256]{2,1,0:T(8,128)(2,1)S(1)}, bf16[2,256,256]{2,1,0:T(8,128)(2,1)S(1)}, u32[]{:S(2)}, u32[]{:S(2)}) collective-permute-start(bf16[2,256,256]{2,1,0:T(8,128)(2,1)S(1)} %collective-permute-done.4.refs_0_), channel_id=1, source_target_pairs={{0,8},{8,12},{12,4},{4,0},{1,9},{9,13},{13,5},{5,1},{2,10},{10,14}... | collective-permute-start | bytes 786440 | tf_op jit(solution)/shard_map/ppermute | solution.py:141
  24.5 2.0 %collective-permute-start.10 = (bf16[256,128]{1,0:T(8,128)(2,1)S(1)}, bf16[256,128]{1,0:T(8,128)(2,1)S(1)}, u32[]{:S(2)}, u32[]{:S(2)}) collective-permute-start(bf16[256,128]{1,0:T(8,128)(2,1)S(1)} %collective-permute-done.5.refs_5_), channel_id=1, source_target_pairs={{0,1},{1,0},{2,3},{3,2},{4,5},{5,4},{6,7},{7,6},{8,9},{9,8},{10,11... | collective-permute-start | bytes 196616 | tf_op jit(solution)/shard_map/ppermute | solution.py:145
  24.5 2.0 %collective-permute-start.11 = (bf16[256,128]{1,0:T(8,128)(2,1)S(1)}, bf16[256,128]{1,0:T(8,128)(2,1)S(1)}, u32[]{:S(2)}, u32[]{:S(2)}) collective-permute-start(bf16[256,128]{1,0:T(8,128)(2,1)S(1)} %collective-permute-done.6.refs_7_), channel_id=1, source_target_pairs={{0,1},{1,0},{2,3},{3,2},{4,5},{5,4},{6,7},{7,6},{8,9},{9,8},{10,11... | collective-permute-start | bytes 196616 | tf_op jit(solution)/shard_map/ppermute | solution.py:145
  25.0 14.8 %collective-permute-start.7 = (bf16[2,256,256]{2,1,0:T(8,128)(2,1)S(1)}, bf16[2,256,256]{2,1,0:T(8,128)(2,1)S(1)}, u32[]{:S(2)}, u32[]{:S(2)}) collective-permute-start(bf16[2,256,256]{2,1,0:T(8,128)(2,1)S(1)} %collective-permute-done.4.refs_0_), channel_id=1, source_target_pairs={{0,2},{1,3},{2,0},{3,1},{4,6},{5,7},{6,4},{7,5},{8,10},{9,11},{10,... | collective-permute-start | bytes 786440 | tf_op jit(solution)/shard_map/ppermute | solution.py:145
  31.5 8.4 %collective-permute-start.13 = (bf16[2,256,256]{2,1,0:T(8,128)(2,1)S(1)}, bf16[2,256,256]{2,1,0:T(8,128)(2,1)S(1)}, u32[]{:S(2)}, u32[]{:S(2)}) collective-permute-start(bf16[2,256,256]{2,1,0:T(8,128)(2,1)S(1)} %collective-permute-done.9.refs_2_), channel_id=1, source_target_pairs={{0,2},{1,3},{2,0},{3,1},{4,6},{5,7},{6,4},{7,5},{8,10},{9,11},{10,... | collective-permute-start | bytes 786440 | tf_op jit(solution)/shard_map/ppermute | solution.py:145
  33.0 6.9 %collective-permute-start.12 = (bf16[256,256]{1,0:T(8,128)(2,1)S(1)}, bf16[256,256]{1,0:T(8,128)(2,1)S(1)}, u32[]{:S(2)}, u32[]{:S(2)}) collective-permute-start(bf16[256,256]{1,0:T(8,128)(2,1)S(1)} %get-tuple-element.84), channel_id=1, source_target_pairs={{0,12},{8,4},{12,0},{4,8},{1,13},{9,5},{13,1},{5,9},{2,14},{10,6},... | collective-permute-start | bytes 393224 | tf_op jit(solution)/shard_map/ppermute | solution.py:141
  42.5 4.4 %collective-permute-start.14 = (bf16[4,256,256]{2,1,0:T(8,128)(2,1)S(1)}, bf16[4,256,256]{2,1,0:T(8,128)(2,1)S(1)}, u32[]{:S(2)}, u32[]{:S(2)}) collective-permute-start(bf16[4,256,256]{2,1,0:T(8,128)(2,1)S(1)} %get-tuple-element.97.mine), channel_id=1, source_target_pairs={{0,1},{1,0},{2,3},{3,2},{4,5},{5,4},{6,7},{7,6},{8,9},{9,8},{10,11... | collective-permute-start | bytes 1572872 | tf_op jit(solution)/shard_map/ppermute | solution.py:145
  42.6 10.6 %all-to-all-start = ((f32[16,1,128]{2,1,0:T(1,128)}), f32[16,1,128]{2,1,0:T(1,128)S(1)}, u32[]{:S(2)}, u32[]{:S(2)}) async-start(f32[16,1,128]{2,1,0:T(1,128)} %get-tuple-element.93), calls=%async_computation | async-start | bytes 16384 | tf_op jit(solution)/shard_map/all_to_all | solution.py:659
  48.0 10.7 %collective-permute-start.15 = (bf16[2,4,64,256]{3,2,1,0:T(8,128)(2,1)}, bf16[2,4,64,256]{3,2,1,0:T(8,128)(2,1)S(1)}, u32[]{:S(2)}, u32[]{:S(2)}) collective-permute-start(bf16[2,4,64,256]{3,2,1,0:T(8,128)(2,1)} %get-tuple-element.102), channel_id=1, source_target_pairs={{0,2},{1,3},{2,0},{3,1},{4,6},{5,7},{6,4},{7,5},{8,10},{9,11},{10,... | collective-permute-start | bytes 786440 | tf_op jit(solution)/shard_map/ppermute | solution.py:145
  57.5 11.9 %collective-permute-start.17 = (bf16[2,4,64,256]{3,2,1,0:T(8,128)(2,1)S(1)}, bf16[2,4,64,256]{3,2,1,0:T(8,128)(2,1)S(1)}, u32[]{:S(2)}, u32[]{:S(2)}) collective-permute-start(bf16[2,4,64,256]{3,2,1,0:T(8,128)(2,1)S(1)} %get-tuple-element.105), channel_id=1, source_target_pairs={{0,2},{1,3},{2,0},{3,1},{4,6},{5,7},{6,4},{7,5},{8,10},{9,11},{10,... | collective-permute-start | bytes 786440 | tf_op jit(solution)/shard_map/ppermute | solution.py:145
  58.0 11.4 %collective-permute-start.18 = (bf16[1,4,64,256]{3,2,1,0:T(8,128)(2,1)S(1)}, bf16[1,4,64,256]{3,2,1,0:T(8,128)(2,1)S(1)}, u32[]{:S(2)}, u32[]{:S(2)}) collective-permute-start(bf16[1,4,64,256]{3,2,1,0:T(8,128)(2,1)S(1)} %get-tuple-element.106), channel_id=1, source_target_pairs={{0,3},{1,2},{2,1},{3,0},{4,7},{5,6},{6,5},{7,4},{8,11},{9,10},{10,... | collective-permute-start | bytes 393224 | tf_op jit(solution)/shard_map/ppermute | solution.py:145
  58.7 10.7 %collective-permute-start.16 = (bf16[1,4,64,256]{3,2,1,0:T(8,128)(2,1)S(1)}, bf16[1,4,64,256]{3,2,1,0:T(8,128)(2,1)S(1)}, u32[]{:S(2)}, u32[]{:S(2)}) collective-permute-start(bf16[1,4,64,256]{3,2,1,0:T(8,128)(2,1)S(1)} %get-tuple-element.104), channel_id=1, source_target_pairs={{0,1},{1,0},{2,3},{3,2},{4,5},{5,4},{6,7},{7,6},{8,9},{9,8},{10,11... | collective-permute-start | bytes 393224 | tf_op jit(solution)/shard_map/ppermute | solution.py:145

commit v31 on v30

--- a/solution.py
+++ b/solution.py
@@ -161,13 +161,13 @@
         kept = {key: block for key, (block, _) in new.items() if key[1] == 0}
         kept.update(across)
         across = {key: block for key, (block, _) in new.items() if key[1] != 0}
-        due = order[:2] if j == 1 else order[2:] if j == n_blk - 1 else []
-        moved["psi"] = {d: onward(columns[d], d, n_blk) for d in due}
         if j == 0:
             columns, packed = pack()
             right = [packed[0]]
             right += [swap(part, 2 * e, n_op) for e, part in enumerate(packed[1:], 1)]
             moved["columns"] = columns
+        due = order[j : j + 1] if j < 2 else order[2:] if j == n_blk - 1 else []
+        moved["psi"] = {d: onward(columns[d], d, n_blk) for d in due}
         if j == 0:
             moved["right"] = right
         if j == 1:
@@ -176,8 +176,8 @@
             n_early = min(2, n_blk - 1)
             psi[0] = [columns[0]]
             moved["early"] = early(left, psi, n_early, tables)
-        if j == 2:
-            moved["other"] = {d: swap(psi[d][0], 1, n_op) for d in order[:2]}
+        if 1 <= j <= 2:
+            moved["other"] = {d: swap(psi[d][0], 1, n_op) for d in order[j - 1 : j]}
         if not kept:
             break
         waiting = {key: done for key, (_, done) in new.items()}

time: 71.6 us -> 71.9 us (level)
  waiting for transfers between devices: 18.4 us -> 21.8 us
  starting transfers between devices: 27.7 us -> 24.5 us
    ppermute x6, waiting for transfers between devices: 11.1 us -> 16.8 us  [onward(): return lax.ppermute(block, 'blk', pairs)]
    ppermute x13, waiting for transfers between devices: 3.95 us -> 1.65 us  [swap(): return lax.ppermute(block, 'op', [(i, i ^ e) for i in range(n_op)])]
    ppermute x13, starting transfers between devices: 11.6 us -> 9.39 us  [swap(): return lax.ppermute(block, 'op', [(i, i ^ e) for i in range(n_op)])]
    ppermute x6, starting transfers between devices: 11.8 us -> 10.6 us  [onward(): return lax.ppermute(block, 'blk', pairs)]
where the time goes in v31:
time: 71.9 us; the launch traced here: 71.7 us
  starting transfers between devices  24.5 us (34%)
  waiting for transfers between devices  21.8 us (30%)
  Pallas kernels  14.8 us (21%)
  blocking collectives  9.73 us (14%)
  between operations  0.77 us (1%)
    ppermute x6, waiting for transfers between devices, onward(): return lax.ppermute(block, 'blk', pairs)  16.8 us
    pallas_call x7, Pallas kernels, kernel(): pl.pallas_call(body, out_shape=[HBM(shape, dtype) if space == HBM else ja...  14.8 us
    ppermute x6, starting transfers between devices, onward(): return lax.ppermute(block, 'blk', pairs)  10.6 us
    all_to_all x1, blocking collectives, totals(): return lax.all_to_all(parts, ('blk', 'op'), 0, 0, tiled=True)  9.73 us
    ppermute x13, starting transfers between devices, swap(): return lax.ppermute(block, 'op', [(i, i ^ e) for i in range(n_op)])  9.39 us
    all_to_all x1, starting transfers between devices, totals(): return lax.all_to_all(parts, ('blk', 'op'), 0, 0, tiled=True)  4.53 us
    all_to_all x1, waiting for transfers between devices, totals(): return lax.all_to_all(parts, ('blk', 'op'), 0, 0, tiled=True)  3.36 us
    ppermute x13, waiting for transfers between devices, swap(): return lax.ppermute(block, 'op', [(i, i ^ e) for i in range(n_op)])  1.65 us
  transfers between devices with their start and end apart: 20, of which 7 were waited for; matrix products, arithmetic and copies ran while one was open for 0% of the time, Pallas kernels for 14%

profile of v31, /device:TPU:0, one launch (start us, length us, event | category | flops | bytes accessed | tf_op | source)
XLA Modules:
  0.0 71.7 jit_solution(10748959528916596355)
XLA Ops:
  0.6 0.0 copy-start.3
  0.6 0.0 copy-start
  0.7 4.1 %collective-permute-start.1 = (bf16[2,256,256]{2,1,0:T(8,128)(2,1)}, bf16[2,256,256]{2,1,0:T(8,128)(2,1)S(1)}, u32[]{:S(2)}, u32[]{:S(2)}) collective-permute-start(bf16[2,256,256]{2,1,0:T(8,128)(2,1)} %bitcast.2), channel_id=1, source_target_pairs={{0,8},{8,12},{12,4},{4,0},{1,9},{9,13},{13,5},{5,1},{2,10},{10,14}... | collective-permute-start | bytes 786440 | tf_op jit(solution)/shard_map/ppermute | solution.py:141
  4.7 0.0 copy-done.3
  4.7 0.0 collective-permute-start.2
  4.7 1.1 %collective-permute-done.2._ = s32[2]{0:T(128)S(1)} collective-permute-done((s32[2]{0:T(128)S(1)}, s32[2]{0:T(128)S(1)}, u32[]{:S(2)}, u32[]{:S(2)}) %collective-permute-start.2) | collective-permute-done | bytes 40 | tf_op jit(solution)/shard_map/ppermute | solution.py:145
  5.9 1.9 %shard_map.103 = (bf16[256,256]{1,0:T(8,128)(2,1)S(1)}, bf16[256,128]{1,0:T(8,128)(2,1)S(1)}, bf16[256,256]{1,0:T(8,128)(2,1)S(1)}, bf16[256,128]{1,0:T(8,128)(2...) custom-call(s32[2]{0:T(128)S(1)} %copy-done.3, s32[2]{0:T(128)S(1)} %collective-permute-done.2._, ...), custom_call_target="tpu_custom_call" | custom-call | bytes 1048576 | tf_op jit(solution)/shard_map/pallas_call | solution.py:113
  7.8 1.6 %collective-permute-start.4 = (bf16[144,256]{1,0:T(8,128)(2,1)S(1)}, bf16[144,256]{1,0:T(8,128)(2,1)S(1)}, u32[]{:S(2)}, u32[]{:S(2)}) collective-permute-start(bf16[144,256]{1,0:T(8,128)(2,1)S(1)} %get-tuple-element.59), channel_id=1, source_target_pairs={{0,2},{1,3},{2,0},{3,1},{4,6},{5,7},{6,4},{7,5},{8,10},{9,11},{10,... | collective-permute-start | bytes 221192 | tf_op jit(solution)/shard_map/ppermute | solution.py:145
  9.3 1.6 %collective-permute-start.3 = (bf16[256,128]{1,0:T(8,128)(2,1)S(1)}, bf16[256,128]{1,0:T(8,128)(2,1)S(1)}, u32[]{:S(2)}, u32[]{:S(2)}) collective-permute-start(bf16[256,128]{1,0:T(8,128)(2,1)S(1)} %get-tuple-element.55), channel_id=1, source_target_pairs={{0,8},{8,12},{12,4},{4,0},{1,9},{9,13},{13,5},{5,1},{2,10},{10,14}... | collective-permute-start | bytes 196616 | tf_op jit(solution)/shard_map/ppermute | solution.py:141
  10.9 0.0 copy-done
  10.9 0.5 collective-permute-start
  11.4 2.2 %collective-permute-done.3.refs_5_ = bf16[256,128]{1,0:T(8,128)(2,1)S(1)} collective-permute-done((bf16[256,128]{1,0:T(8,128)(2,1)S(1)}, bf16[256,128]{1,0:T(8,128)(2,1)S(1)}, u32[]{:S(2)}, u32[]{:S(2)}) %collective-permute-start.3) | collective-permute-done | bytes 65568 | tf_op jit(solution)/shard_map/ppermute | solution.py:141
  13.6 0.0 collective-permute-done.4.refs_1_.refs_5_
  13.6 0.0 collective-permute-done.1.refs_2_
  13.6 0.0 copy-start.1
  13.6 0.0 copy-start.2
  13.6 0.0 copy-start.4
  13.6 0.0 copy-start.5
  13.6 2.5 %collective-permute-start.5 = (bf16[2,256,256]{2,1,0:T(8,128)(2,1)S(1)}, bf16[2,256,256]{2,1,0:T(8,128)(2,1)S(1)}, u32[]{:S(2)}, u32[]{:S(2)}) collective-permute-start(bf16[2,256,256]{2,1,0:T(8,128)(2,1)S(1)} %collective-permute-done.1.refs_2_), channel_id=1, source_target_pairs={{0,8},{8,12},{12,4},{4,0},{1,9},{9,13},{13,5},{5,1},{2,10},{10,14}... | collective-permute-start | bytes 786440 | tf_op jit(solution)/shard_map/ppermute | solution.py:141
  16.2 0.0 collective-permute-start.7
  16.2 0.0 collective-permute-start.6
  16.2 0.7 %collective-permute-start.9 = (bf16[2,256,256]{2,1,0:T(8,128)(2,1)S(1)}, bf16[2,256,256]{2,1,0:T(8,128)(2,1)S(1)}, u32[]{:S(2)}, u32[]{:S(2)}) collective-permute-start(bf16[2,256,256]{2,1,0:T(8,128)(2,1)S(1)} %collective-permute-done.1.refs_2_), channel_id=1, source_target_pairs={{0,2},{1,3},{2,0},{3,1},{4,6},{5,7},{6,4},{7,5},{8,10},{9,11},{10,... | collective-permute-start | bytes 786440 | tf_op jit(solution)/shard_map/ppermute | solution.py:145
  16.9 0.0 copy-done.1
  16.9 0.0 copy-done.2
  16.9 0.0 copy-done.4
  16.9 0.0 copy-done.5
  16.9 1.3 %shard_map.104 = (s32[16]{0:T(128)S(1)}, s32[4]{0:T(128)S(1)}, s32[4]{0:T(128)S(1)}, f32[4,256,128]{2,1,0:T(8,128)S(1)}, f32[1,512]{1,0:T(1,128)S(1)}) custom-call(s32[4]{0:T(128)S(1)} %copy-done.4, s32[4]{0:T(128)S(1)} %copy-done.5, f32[4,256]{1,0:T(4,128)S(1)} %copy-done.1, f32[1,512]{1,0:T(1,128)S(1)} %bitcast.5, ...), custom_call_target="tpu_custom_call" | custom-call | tf_op jit(solution)/shard_map/pallas_call | solution.py:113
  18.3 0.5 collective-permute-done.refs_1_
  18.8 5.2 %collective-permute-done.7.refs_7_ = bf16[256,128]{1,0:T(8,128)(2,1)S(1)} collective-permute-done((bf16[256,128]{1,0:T(8,128)(2,1)S(1)}, bf16[256,128]{1,0:T(8,128)(2,1)S(1)}, u32[]{:S(2)}, u32[]{:S(2)}) %collective-permute-start.7) | collective-permute-done | bytes 65568 | tf_op jit(solution)/shard_map/ppermute | solution.py:141
  24.0 0.0 collective-permute-done.6.refs_6_
  24.0 0.0 collective-permute-done.5.refs_0_
  24.0 0.8 %collective-permute-start.10 = (bf16[2,256,256]{2,1,0:T(8,128)(2,1)S(1)}, bf16[2,256,256]{2,1,0:T(8,128)(2,1)S(1)}, u32[]{:S(2)}, u32[]{:S(2)}) collective-permute-start(bf16[2,256,256]{2,1,0:T(8,128)(2,1)S(1)} %collective-permute-done.5.refs_0_), channel_id=1, source_target_pairs={{0,8},{8,12},{12,4},{4,0},{1,9},{9,13},{13,5},{5,1},{2,10},{10,14}... | collective-permute-start | bytes 786440 | tf_op jit(solution)/shard_map/ppermute | solution.py:141
  24.8 0.0 collective-permute-start.11
  24.8 1.5 %collective-permute-start.8 = (bf16[2,256,256]{2,1,0:T(8,128)(2,1)S(1)}, bf16[2,256,256]{2,1,0:T(8,128)(2,1)S(1)}, u32[]{:S(2)}, u32[]{:S(2)}) collective-permute-start(bf16[2,256,256]{2,1,0:T(8,128)(2,1)S(1)} %collective-permute-done.5.refs_0_), channel_id=1, source_target_pairs={{0,2},{1,3},{2,0},{3,1},{4,6},{5,7},{6,4},{7,5},{8,10},{9,11},{10,... | collective-permute-start | bytes 786440 | tf_op jit(solution)/shard_map/ppermute | solution.py:145
  26.3 0.0 collective-permute-done.9.refs_3_
  26.3 0.0 collective-permute-done.11.refs_8_
  26.4 5.8 %collective-permute-done.10.refs_2_ = bf16[2,256,256]{2,1,0:T(8,128)(2,1)S(1)} collective-permute-done((bf16[2,256,256]{2,1,0:T(8,128)(2,1)S(1)}, bf16[2,256,256]{2,1,0:T(8,128)(2,1)S(1)}, u32[]{:S(2)}, u32[]{:S(2)}) %collective-permute-start.10) | collective-permute-done | bytes 262176 | tf_op jit(solution)/shard_map/ppermute | solution.py:141
  32.2 0.8 %collective-permute-start.13 = (bf16[2,256,256]{2,1,0:T(8,128)(2,1)S(1)}, bf16[2,256,256]{2,1,0:T(8,128)(2,1)S(1)}, u32[]{:S(2)}, u32[]{:S(2)}) collective-permute-start(bf16[2,256,256]{2,1,0:T(8,128)(2,1)S(1)} %collective-permute-done.10.refs_2_), channel_id=1, source_target_pairs={{0,2},{1,3},{2,0},{3,1},{4,6},{5,7},{6,4},{7,5},{8,10},{9,11},{10,... | collective-permute-start | bytes 786440 | tf_op jit(solution)/shard_map/ppermute | solution.py:145
  33.0 1.6 %collective-permute-start.12 = (bf16[256,256]{1,0:T(8,128)(2,1)S(1)}, bf16[256,256]{1,0:T(8,128)(2,1)S(1)}, u32[]{:S(2)}, u32[]{:S(2)}) collective-permute-start(bf16[256,256]{1,0:T(8,128)(2,1)S(1)} %get-tuple-element.82), channel_id=1, source_target_pairs={{0,12},{8,4},{12,0},{4,8},{1,13},{9,5},{13,1},{5,9},{2,14},{10,6},... | collective-permute-start | bytes 393224 | tf_op jit(solution)/shard_map/ppermute | solution.py:141
  34.6 1.7 %shard_map.105 = (bf16[2,256,256]{2,1,0:T(8,128)(2,1)S(1)}, bf16[2,4,256,256]{3,2,1,0:T(8,128)(2,1)S(1)}, bf16[2,2,2,256,256]{4,3,2,1,0:T(8,128)(2,1)}) custom-call(s32[4]{0:T(128)S(1)} %get-tuple-element.72.widths, bf16[2,256,256]{2,1,0:T(8,128)(2,1)S(1)} %bitcast.4, bf16[2,256,256]{2,1,0:T(8,128)(2,1)S(1)} %collective-permute-done.refs_1_, ...), custom_call_target="tpu_custom_call" | custom-call | flops 268435456 | bytes 4194304 | tf_op jit(solution)/shard_map/pallas_call | solution.py:113
  36.3 3.6 %collective-permute-done.12.refs_6_ = bf16[256,256]{1,0:T(8,128)(2,1)S(1)} collective-permute-done((bf16[256,256]{1,0:T(8,128)(2,1)S(1)}, bf16[256,256]{1,0:T(8,128)(2,1)S(1)}, u32[]{:S(2)}, u32[]{:S(2)}) %collective-permute-start.12) | collective-permute-done | bytes 131104 | tf_op jit(solution)/shard_map/ppermute | solution.py:141
  39.9 0.0 collective-permute-done.8.refs_1_
  39.9 0.0 collective-permute-done.13.refs_3_
  39.9 2.6 %shard_map.106 = (bf16[4,256,256]{2,1,0:T(8,128)(2,1)S(1)}, bf16[4,256,256]{2,1,0:T(8,128)(2,1)S(1)}, bf16[2,2,2,256,256]{4,3,2,1,0:T(8,128)(2,1)}, f32[16,1,128]{2,1,0:T(1,128)}) custom-call(s32[16]{0:T(128)S(1)} %get-tuple-element.71.src, s32[4]{0:T(128)S(1)} %get-tuple-element.72.widths, bf16[2,256,256]{2,1,0:T(8,128)(2,1)S(1)} %collective-permute-done.5.refs_0_, ...), custom_call_target="tpu_custom_call" | custom-call | flops 1073741824 | bytes 6291456 | tf_op jit(solution)/shard_map/pallas_call | solution.py:113
  42.6 0.1 collective-permute-start.14
  42.6 4.5 %all-to-all-start = ((f32[16,1,128]{2,1,0:T(1,128)}), f32[16,1,128]{2,1,0:T(1,128)S(1)}, u32[]{:S(2)}, u32[]{:S(2)}) async-start(f32[16,1,128]{2,1,0:T(1,128)} %get-tuple-element.91), calls=%async_computation | async-start | bytes 16384 | tf_op jit(solution)/shard_map/all_to_all | solution.py:659
  47.2 0.0 collective-permute-done.14.other
  47.2 1.0 %shard_map.107 = (f32[4,256,256]{2,1,0:T(8,128)S(1)}, bf16[2,4,64,256]{3,2,1,0:T(8,128)(2,1)}) custom-call(bf16[4,256,256]{2,1,0:T(8,128)(2,1)S(1)} %get-tuple-element.95.mine, bf16[4,256,256]{2,1,0:T(8,128)(2,1)S(1)} %collective-permute-done.14.other, bf16[4,256,256]{2,1,0:T(8,128)(2,1)S(1)} %get-tuple-element.94.raw_in.refs_3_, ...), custom_call_target="tpu_custom_call" | custom-call | bytes 4194304 | tf_op jit(solution)/shard_map/pallas_call | solution.py:113
  48.2 1.9 %collective-permute-start.15 = (bf16[2,4,64,256]{3,2,1,0:T(8,128)(2,1)}, bf16[2,4,64,256]{3,2,1,0:T(8,128)(2,1)S(1)}, u32[]{:S(2)}, u32[]{:S(2)}) collective-permute-start(bf16[2,4,64,256]{3,2,1,0:T(8,128)(2,1)} %get-tuple-element.100), channel_id=1, source_target_pairs={{0,2},{1,3},{2,0},{3,1},{4,6},{5,7},{6,4},{7,5},{8,10},{9,11},{10,... | collective-permute-start | bytes 786440 | tf_op jit(solution)/shard_map/ppermute | solution.py:145
  50.1 3.4 %all-to-all-done.refs_2_.parts1 = f32[16,1,128]{2,1,0:T(1,128)S(1)} async-done(((f32[16,1,128]{2,1,0:T(1,128)}), f32[16,1,128]{2,1,0:T(1,128)S(1)}, u32[]{:S(2)}, u32[]{:S(2)}) %all-to-all-start) | async-done | bytes 8224 | tf_op jit(solution)/shard_map/all_to_all | solution.py:659
  53.5 4.2 %shard_map.108 = (f32[16,1,128]{2,1,0:T(1,128)S(1)}, bf16[4,4,64,256]{3,2,1,0:T(8,128)(2,1)S(1)}, bf16[1,4,64,256]{3,2,1,0:T(8,128)(2,1)S(1)}, bf16[2,4,64,256]{...) custom-call(s32[16]{0:T(128)S(1)} %get-tuple-element.71.src, s32[4]{0:T(128)S(1)} %get-tuple-element.72.widths, ...), custom_call_target="tpu_custom_call" | custom-call | flops 4294967296 | bytes 25165824 | tf_op jit(solution)/shard_map/pallas_call | solution.py:113
  57.7 0.6 collective-permute-start.17
  58.3 0.6 collective-permute-start.18
  58.9 0.0 collective-permute-done.15.refs_0_
  58.9 1.0 %collective-permute-start.16 = (bf16[1,4,64,256]{3,2,1,0:T(8,128)(2,1)S(1)}, bf16[1,4,64,256]{3,2,1,0:T(8,128)(2,1)S(1)}, u32[]{:S(2)}, u32[]{:S(2)}) collective-permute-start(bf16[1,4,64,256]{3,2,1,0:T(8,128)(2,1)S(1)} %get-tuple-element.102), channel_id=1, source_target_pairs={{0,1},{1,0},{2,3},{3,2},{4,5},{5,4},{6,7},{7,6},{8,9},{9,8},{10,11... | collective-permute-start | bytes 393224 | tf_op jit(solution)/shard_map/ppermute | solution.py:145
  59.9 9.7 %all_to_all.10.parts2 = f32[16,1,128]{2,1,0:T(1,128)S(1)} all-to-all(f32[16,1,128]{2,1,0:T(1,128)S(1)} %get-tuple-element.97), channel_id=1, replica_groups=mesh['grp'=2,'blk'=4,'op'=4] {'blk','op'}, dimensions={0} | all-to-all | bytes 16384 | tf_op jit(solution)/shard_map/all_to_all | solution.py:659
  69.7 0.0 collective-permute-done.18.refs_3_
  69.7 0.0 collective-permute-done.17.refs_2_
  69.7 0.0 collective-permute-done.16.refs_1_
  69.7 2.0 %shard_map.109 = (bf16[4,64,512]{2,1,0:T(8,128)(2,1)}, bf16[4,64,512]{2,1,0:T(8,128)(2,1)}, f32[1]{0:T(128)}) custom-call(s32[4]{0:T(128)S(1)} %get-tuple-element.70.slots, f32[16,1,128]{2,1,0:T(1,128)S(1)} %all-to-all-done.refs_2_.parts1, f32[16,1,128]{2,1,0:T(1,128)S(1)} %all_to_all.10.parts2, f32[4,256,128]{2,1,0:T(8,128)S(1)} %get-tuple-element.89.refs_11_.diag.refs_5_, ...), custom_call_target="tpu_custom_call" | custom-call | bytes 4194304 | tf_op jit(solution)/shard_map/pallas_call | solution.py:113
Async XLA Ops:
  0.6 4.1 %copy-start.3 = (s32[2]{0:T(128)S(1)}, s32[2]{0:T(128)}, u32[]{:S(2)}) copy-start(s32[2]{0:T(128)} %shift.1) | copy-start | bytes 28
  0.6 10.3 %copy-start = (bf16[2,1,256,256]{3,2,1,0:T(8,128)(2,1)S(1)}, bf16[2,1,256,256]{3,2,1,0:T(8,128)(2,1)}, u32[]{:S(2)}) copy-start(bf16[2,1,256,256]{3,2,1,0:T(8,128)(2,1)} %param.9) | copy-start | bytes 786436
  0.7 13.0 %collective-permute-start.1 = (bf16[2,256,256]{2,1,0:T(8,128)(2,1)}, bf16[2,256,256]{2,1,0:T(8,128)(2,1)S(1)}, u32[]{:S(2)}, u32[]{:S(2)}) collective-permute-start(bf16[2,256,256]{2,1,0:T(8,128)(2,1)} %bitcast.2), channel_id=1, source_target_pairs={{0,8},{8,12},{12,4},{4,0},{1,9},{9,13},{13,5},{5,1},{2,10},{10,14}... | collective-permute-start | bytes 786440 | tf_op jit(solution)/shard_map/ppermute | solution.py:141
  4.7 1.1 %collective-permute-start.2 = (s32[2]{0:T(128)S(1)}, s32[2]{0:T(128)S(1)}, u32[]{:S(2)}, u32[]{:S(2)}) collective-permute-start(s32[2]{0:T(128)S(1)} %copy-done.3), channel_id=1, source_target_pairs={{0,1},{1,0},{2,3},{3,2},{4,5},{5,4},{6,7},{7,6},{8,9},{9,8},{10,11... | collective-permute-start | bytes 32 | tf_op jit(solution)/shard_map/ppermute | solution.py:145
  7.8 5.8 %collective-permute-start.4 = (bf16[144,256]{1,0:T(8,128)(2,1)S(1)}, bf16[144,256]{1,0:T(8,128)(2,1)S(1)}, u32[]{:S(2)}, u32[]{:S(2)}) collective-permute-start(bf16[144,256]{1,0:T(8,128)(2,1)S(1)} %get-tuple-element.59), channel_id=1, source_target_pairs={{0,2},{1,3},{2,0},{3,1},{4,6},{5,7},{6,4},{7,5},{8,10},{9,11},{10,... | collective-permute-start | bytes 221192 | tf_op jit(solution)/shard_map/ppermute | solution.py:145
  9.3 4.3 %collective-permute-start.3 = (bf16[256,128]{1,0:T(8,128)(2,1)S(1)}, bf16[256,128]{1,0:T(8,128)(2,1)S(1)}, u32[]{:S(2)}, u32[]{:S(2)}) collective-permute-start(bf16[256,128]{1,0:T(8,128)(2,1)S(1)} %get-tuple-element.55), channel_id=1, source_target_pairs={{0,8},{8,12},{12,4},{4,0},{1,9},{9,13},{13,5},{5,1},{2,10},{10,14}... | collective-permute-start | bytes 196616 | tf_op jit(solution)/shard_map/ppermute | solution.py:141
  10.9 7.9 %collective-permute-start = (bf16[2,256,256]{2,1,0:T(8,128)(2,1)S(1)}, bf16[2,256,256]{2,1,0:T(8,128)(2,1)S(1)}, u32[]{:S(2)}, u32[]{:S(2)}) collective-permute-start(bf16[2,256,256]{2,1,0:T(8,128)(2,1)S(1)} %bitcast.3), channel_id=1, source_target_pairs={{0,2},{1,3},{2,0},{3,1},{4,6},{5,7},{6,4},{7,5},{8,10},{9,11},{10,... | collective-permute-start | bytes 786440 | tf_op jit(solution)/shard_map/ppermute | solution.py:145
  13.6 3.3 %copy-start.1 = (f32[4,256]{1,0:T(4,128)S(1)}, f32[4,256]{1,0:T(4,128)}, u32[]{:S(2)}) copy-start(f32[4,256]{1,0:T(4,128)} %left_diag.1) | copy-start | bytes 12292
  13.6 3.3 %copy-start.2 = (f32[512]{0:T(512)S(1)}, f32[512]{0:T(512)}, u32[]{:S(2)}) copy-start(f32[512]{0:T(512)} %param.15) | copy-start | bytes 6148
  13.6 3.3 %copy-start.4 = (s32[4]{0:T(128)S(1)}, s32[4]{0:T(128)}, u32[]{:S(2)}) copy-start(s32[4]{0:T(128)} %sector.1) | copy-start | bytes 52
  13.6 3.3 %copy-start.5 = (s32[4]{0:T(128)S(1)}, s32[4]{0:T(128)}, u32[]{:S(2)}) copy-start(s32[4]{0:T(128)} %width.1) | copy-start | bytes 52
  13.6 10.3 %collective-permute-start.5 = (bf16[2,256,256]{2,1,0:T(8,128)(2,1)S(1)}, bf16[2,256,256]{2,1,0:T(8,128)(2,1)S(1)}, u32[]{:S(2)}, u32[]{:S(2)}) collective-permute-start(bf16[2,256,256]{2,1,0:T(8,128)(2,1)S(1)} %collective-permute-done.1.refs_2_), channel_id=1, source_target_pairs={{0,8},{8,12},{12,4},{4,0},{1,9},{9,13},{13,5},{5,1},{2,10},{10,14}... | collective-permute-start | bytes 786440 | tf_op jit(solution)/shard_map/ppermute | solution.py:141
  16.2 7.8 %collective-permute-start.7 = (bf16[256,128]{1,0:T(8,128)(2,1)S(1)}, bf16[256,128]{1,0:T(8,128)(2,1)S(1)}, u32[]{:S(2)}, u32[]{:S(2)}) collective-permute-start(bf16[256,128]{1,0:T(8,128)(2,1)S(1)} %get-tuple-element.62), channel_id=1, source_target_pairs={{0,4},{8,0},{12,8},{4,12},{1,5},{9,1},{13,9},{5,13},{2,6},{10,2},{... | collective-permute-start | bytes 196616 | tf_op jit(solution)/shard_map/ppermute | solution.py:141
  16.2 7.8 %collective-permute-start.6 = (bf16[256,128]{1,0:T(8,128)(2,1)S(1)}, bf16[256,128]{1,0:T(8,128)(2,1)S(1)}, u32[]{:S(2)}, u32[]{:S(2)}) collective-permute-start(bf16[256,128]{1,0:T(8,128)(2,1)S(1)} %collective-permute-done.3.refs_5_), channel_id=1, source_target_pairs={{0,1},{1,0},{2,3},{3,2},{4,5},{5,4},{6,7},{7,6},{8,9},{9,8},{10,11... | collective-permute-start | bytes 196616 | tf_op jit(solution)/shard_map/ppermute | solution.py:145
  16.2 10.2 %collective-permute-start.9 = (bf16[2,256,256]{2,1,0:T(8,128)(2,1)S(1)}, bf16[2,256,256]{2,1,0:T(8,128)(2,1)S(1)}, u32[]{:S(2)}, u32[]{:S(2)}) collective-permute-start(bf16[2,256,256]{2,1,0:T(8,128)(2,1)S(1)} %collective-permute-done.1.refs_2_), channel_id=1, source_target_pairs={{0,2},{1,3},{2,0},{3,1},{4,6},{5,7},{6,4},{7,5},{8,10},{9,11},{10,... | collective-permute-start | bytes 786440 | tf_op jit(solution)/shard_map/ppermute | solution.py:145
  24.0 8.2 %collective-permute-start.10 = (bf16[2,256,256]{2,1,0:T(8,128)(2,1)S(1)}, bf16[2,256,256]{2,1,0:T(8,128)(2,1)S(1)}, u32[]{:S(2)}, u32[]{:S(2)}) collective-permute-start(bf16[2,256,256]{2,1,0:T(8,128)(2,1)S(1)} %collective-permute-done.5.refs_0_), channel_id=1, source_target_pairs={{0,8},{8,12},{12,4},{4,0},{1,9},{9,13},{13,5},{5,1},{2,10},{10,14}... | collective-permute-start | bytes 786440 | tf_op jit(solution)/shard_map/ppermute | solution.py:141
  24.8 1.5 %collective-permute-start.11 = (bf16[256,128]{1,0:T(8,128)(2,1)S(1)}, bf16[256,128]{1,0:T(8,128)(2,1)S(1)}, u32[]{:S(2)}, u32[]{:S(2)}) collective-permute-start(bf16[256,128]{1,0:T(8,128)(2,1)S(1)} %collective-permute-done.7.refs_7_), channel_id=1, source_target_pairs={{0,1},{1,0},{2,3},{3,2},{4,5},{5,4},{6,7},{7,6},{8,9},{9,8},{10,11... | collective-permute-start | bytes 196616 | tf_op jit(solution)/shard_map/ppermute | solution.py:145
  24.8 15.1 %collective-permute-start.8 = (bf16[2,256,256]{2,1,0:T(8,128)(2,1)S(1)}, bf16[2,256,256]{2,1,0:T(8,128)(2,1)S(1)}, u32[]{:S(2)}, u32[]{:S(2)}) collective-permute-start(bf16[2,256,256]{2,1,0:T(8,128)(2,1)S(1)} %collective-permute-done.5.refs_0_), channel_id=1, source_target_pairs={{0,2},{1,3},{2,0},{3,1},{4,6},{5,7},{6,4},{7,5},{8,10},{9,11},{10,... | collective-permute-start | bytes 786440 | tf_op jit(solution)/shard_map/ppermute | solution.py:145
  32.2 7.7 %collective-permute-start.13 = (bf16[2,256,256]{2,1,0:T(8,128)(2,1)S(1)}, bf16[2,256,256]{2,1,0:T(8,128)(2,1)S(1)}, u32[]{:S(2)}, u32[]{:S(2)}) collective-permute-start(bf16[2,256,256]{2,1,0:T(8,128)(2,1)S(1)} %collective-permute-done.10.refs_2_), channel_id=1, source_target_pairs={{0,2},{1,3},{2,0},{3,1},{4,6},{5,7},{6,4},{7,5},{8,10},{9,11},{10,... | collective-permute-start | bytes 786440 | tf_op jit(solution)/shard_map/ppermute | solution.py:145
  33.0 6.9 %collective-permute-start.12 = (bf16[256,256]{1,0:T(8,128)(2,1)S(1)}, bf16[256,256]{1,0:T(8,128)(2,1)S(1)}, u32[]{:S(2)}, u32[]{:S(2)}) collective-permute-start(bf16[256,256]{1,0:T(8,128)(2,1)S(1)} %get-tuple-element.82), channel_id=1, source_target_pairs={{0,12},{8,4},{12,0},{4,8},{1,13},{9,5},{13,1},{5,9},{2,14},{10,6},... | collective-permute-start | bytes 393224 | tf_op jit(solution)/shard_map/ppermute | solution.py:141
  42.6 4.6 %collective-permute-start.14 = (bf16[4,256,256]{2,1,0:T(8,128)(2,1)S(1)}, bf16[4,256,256]{2,1,0:T(8,128)(2,1)S(1)}, u32[]{:S(2)}, u32[]{:S(2)}) collective-permute-start(bf16[4,256,256]{2,1,0:T(8,128)(2,1)S(1)} %get-tuple-element.95.mine), channel_id=1, source_target_pairs={{0,1},{1,0},{2,3},{3,2},{4,5},{5,4},{6,7},{7,6},{8,9},{9,8},{10,11... | collective-permute-start | bytes 1572872 | tf_op jit(solution)/shard_map/ppermute | solution.py:145
  42.6 10.9 %all-to-all-start = ((f32[16,1,128]{2,1,0:T(1,128)}), f32[16,1,128]{2,1,0:T(1,128)S(1)}, u32[]{:S(2)}, u32[]{:S(2)}) async-start(f32[16,1,128]{2,1,0:T(1,128)} %get-tuple-element.91), calls=%async_computation | async-start | bytes 16384 | tf_op jit(solution)/shard_map/all_to_all | solution.py:659
  48.2 10.7 %collective-permute-start.15 = (bf16[2,4,64,256]{3,2,1,0:T(8,128)(2,1)}, bf16[2,4,64,256]{3,2,1,0:T(8,128)(2,1)S(1)}, u32[]{:S(2)}, u32[]{:S(2)}) collective-permute-start(bf16[2,4,64,256]{3,2,1,0:T(8,128)(2,1)} %get-tuple-element.100), channel_id=1, source_target_pairs={{0,2},{1,3},{2,0},{3,1},{4,6},{5,7},{6,4},{7,5},{8,10},{9,11},{10,... | collective-permute-start | bytes 786440 | tf_op jit(solution)/shard_map/ppermute | solution.py:145
  57.7 11.9 %collective-permute-start.17 = (bf16[2,4,64,256]{3,2,1,0:T(8,128)(2,1)S(1)}, bf16[2,4,64,256]{3,2,1,0:T(8,128)(2,1)S(1)}, u32[]{:S(2)}, u32[]{:S(2)}) collective-permute-start(bf16[2,4,64,256]{3,2,1,0:T(8,128)(2,1)S(1)} %get-tuple-element.103), channel_id=1, source_target_pairs={{0,2},{1,3},{2,0},{3,1},{4,6},{5,7},{6,4},{7,5},{8,10},{9,11},{10,... | collective-permute-start | bytes 786440 | tf_op jit(solution)/shard_map/ppermute | solution.py:145
  58.3 11.4 %collective-permute-start.18 = (bf16[1,4,64,256]{3,2,1,0:T(8,128)(2,1)S(1)}, bf16[1,4,64,256]{3,2,1,0:T(8,128)(2,1)S(1)}, u32[]{:S(2)}, u32[]{:S(2)}) collective-permute-start(bf16[1,4,64,256]{3,2,1,0:T(8,128)(2,1)S(1)} %get-tuple-element.104), channel_id=1, source_target_pairs={{0,3},{1,2},{2,1},{3,0},{4,7},{5,6},{6,5},{7,4},{8,11},{9,10},{10,... | collective-permute-start | bytes 393224 | tf_op jit(solution)/shard_map/ppermute | solution.py:145
  58.9 10.7 %collective-permute-start.16 = (bf16[1,4,64,256]{3,2,1,0:T(8,128)(2,1)S(1)}, bf16[1,4,64,256]{3,2,1,0:T(8,128)(2,1)S(1)}, u32[]{:S(2)}, u32[]{:S(2)}) collective-permute-start(bf16[1,4,64,256]{3,2,1,0:T(8,128)(2,1)S(1)} %get-tuple-element.102), channel_id=1, source_target_pairs={{0,1},{1,0},{2,3},{3,2},{4,5},{5,4},{6,7},{7,6},{8,9},{9,8},{10,11... | collective-permute-start | bytes 393224 | tf_op jit(solution)/shard_map/ppermute | solution.py:145

commit v32 on v27

--- a/solution.py
+++ b/solution.py
@@ -481,13 +481,13 @@
         halves.append((whole(vv), whole(vc), vs))
     along = (halves[0][1] + halves[1][1]) / jnp.maximum(halves[0][0] + halves[1][0], 1e-30)
     terms = held.shape[2]
-    for copy in copies:
-        copy.wait()
     for d in range(n_blk):
         for h in range(2):
             part = slice(h * cols, (h + 1) * cols)
             vec = raw_in[d, :, part].astype(jnp.float32) * scale
             fld[d, :, part] = (corr[d, :, part] - along * vec).astype(jnp.bfloat16)
+    for d in range(n_blk):
+        copies[d].wait()
         left_products(fld[d], lambda at: held[d, at // terms], inter.at[d])
     zero = jnp.zeros((8, cols), jnp.float32)
     sums = [zero for _ in range(5)]

time: 70.9 us -> 71.2 us (level)
  no operation moved by 1% of the time
where the time goes in v32:
time: 71.2 us; the launch traced here: 70.9 us
  starting transfers between devices  27.6 us (39%)
  waiting for transfers between devices  17.8 us (25%)
  Pallas kernels  14.5 us (20%)
  blocking collectives  10.2 us (14%)
  between operations  0.76 us (1%)
    pallas_call x7, Pallas kernels, kernel(): pl.pallas_call(body, out_shape=[HBM(shape, dtype) if space == HBM else ja...  14.5 us
    ppermute x6, starting transfers between devices, onward(): return lax.ppermute(block, 'blk', pairs)  11.8 us
    ppermute x13, starting transfers between devices, swap(): return lax.ppermute(block, 'op', [(i, i ^ e) for i in range(n_op)])  11.1 us
    ppermute x6, waiting for transfers between devices, onward(): return lax.ppermute(block, 'blk', pairs)  10.5 us
    all_to_all x1, blocking collectives, totals(): return lax.all_to_all(parts, ('blk', 'op'), 0, 0, tiled=True)  10.2 us
    all_to_all x1, starting transfers between devices, totals(): return lax.all_to_all(parts, ('blk', 'op'), 0, 0, tiled=True)  4.63 us
    ppermute x13, waiting for transfers between devices, swap(): return lax.ppermute(block, 'op', [(i, i ^ e) for i in range(n_op)])  3.95 us
    all_to_all x1, waiting for transfers between devices, totals(): return lax.all_to_all(parts, ('blk', 'op'), 0, 0, tiled=True)  3.36 us
  transfers between devices with their start and end apart: 20, of which 6 were waited for; matrix products, arithmetic and copies ran while one was open for 0% of the time, Pallas kernels for 14%

profile of v32, /device:TPU:0, one launch (start us, length us, event | category | flops | bytes accessed | tf_op | source)
XLA Modules:
  0.0 70.9 jit_solution(14711723418460253341)
XLA Ops:
  0.6 0.0 copy-start.3
  0.6 0.0 copy-start
  0.7 4.1 %collective-permute-start.1 = (bf16[2,256,256]{2,1,0:T(8,128)(2,1)}, bf16[2,256,256]{2,1,0:T(8,128)(2,1)S(1)}, u32[]{:S(2)}, u32[]{:S(2)}) collective-permute-start(bf16[2,256,256]{2,1,0:T(8,128)(2,1)} %bitcast.2), channel_id=1, source_target_pairs={{0,8},{8,12},{12,4},{4,0},{1,9},{9,13},{13,5},{5,1},{2,10},{10,14}... | collective-permute-start | bytes 786440 | tf_op jit(solution)/shard_map/ppermute | solution.py:141
  4.7 0.0 copy-done.3
  4.7 0.0 collective-permute-start.2
  4.7 1.1 %collective-permute-done.2._ = s32[2]{0:T(128)S(1)} collective-permute-done((s32[2]{0:T(128)S(1)}, s32[2]{0:T(128)S(1)}, u32[]{:S(2)}, u32[]{:S(2)}) %collective-permute-start.2) | collective-permute-done | bytes 40 | tf_op jit(solution)/shard_map/ppermute | solution.py:145
  5.9 1.9 %shard_map.103 = (bf16[256,256]{1,0:T(8,128)(2,1)S(1)}, bf16[256,128]{1,0:T(8,128)(2,1)S(1)}, bf16[256,256]{1,0:T(8,128)(2,1)S(1)}, bf16[256,128]{1,0:T(8,128)(2...) custom-call(s32[2]{0:T(128)S(1)} %copy-done.3, s32[2]{0:T(128)S(1)} %collective-permute-done.2._, ...), custom_call_target="tpu_custom_call" | custom-call | bytes 1048576 | tf_op jit(solution)/shard_map/pallas_call | solution.py:113
  7.8 1.6 %collective-permute-start.3 = (bf16[144,256]{1,0:T(8,128)(2,1)S(1)}, bf16[144,256]{1,0:T(8,128)(2,1)S(1)}, u32[]{:S(2)}, u32[]{:S(2)}) collective-permute-start(bf16[144,256]{1,0:T(8,128)(2,1)S(1)} %get-tuple-element.59), channel_id=1, source_target_pairs={{0,2},{1,3},{2,0},{3,1},{4,6},{5,7},{6,4},{7,5},{8,10},{9,11},{10,... | collective-permute-start | bytes 221192 | tf_op jit(solution)/shard_map/ppermute | solution.py:145
  9.3 0.0 copy-done
  9.3 0.5 collective-permute-start
  9.9 2.8 %collective-permute-done.3.refs_1_.refs_5_ = bf16[144,256]{1,0:T(8,128)(2,1)S(1)} collective-permute-done((bf16[144,256]{1,0:T(8,128)(2,1)S(1)}, bf16[144,256]{1,0:T(8,128)(2,1)S(1)}, u32[]{:S(2)}, u32[]{:S(2)}) %collective-permute-start.3) | collective-permute-done | bytes 73760 | tf_op jit(solution)/shard_map/ppermute | solution.py:145
  12.7 0.0 collective-permute-done.1.refs_2_
  12.7 0.0 copy-start.1
  12.7 0.0 copy-start.2
  12.7 0.0 copy-start.4
  12.7 0.0 copy-start.5
  12.7 1.6 %collective-permute-start.4 = (bf16[2,256,256]{2,1,0:T(8,128)(2,1)S(1)}, bf16[2,256,256]{2,1,0:T(8,128)(2,1)S(1)}, u32[]{:S(2)}, u32[]{:S(2)}) collective-permute-start(bf16[2,256,256]{2,1,0:T(8,128)(2,1)S(1)} %collective-permute-done.1.refs_2_), channel_id=1, source_target_pairs={{0,8},{8,12},{12,4},{4,0},{1,9},{9,13},{13,5},{5,1},{2,10},{10,14}... | collective-permute-start | bytes 786440 | tf_op jit(solution)/shard_map/ppermute | solution.py:141
  14.3 0.6 collective-permute-start.5
  14.9 1.8 %collective-permute-start.7 = (bf16[2,256,256]{2,1,0:T(8,128)(2,1)S(1)}, bf16[2,256,256]{2,1,0:T(8,128)(2,1)S(1)}, u32[]{:S(2)}, u32[]{:S(2)}) collective-permute-start(bf16[2,256,256]{2,1,0:T(8,128)(2,1)S(1)} %collective-permute-done.1.refs_2_), channel_id=1, source_target_pairs={{0,2},{1,3},{2,0},{3,1},{4,6},{5,7},{6,4},{7,5},{8,10},{9,11},{10,... | collective-permute-start | bytes 786440 | tf_op jit(solution)/shard_map/ppermute | solution.py:145
  16.7 0.0 copy-done.1
  16.7 0.0 copy-done.2
  16.7 0.0 copy-done.4
  16.7 0.0 copy-done.5
  16.7 1.3 %shard_map.104 = (s32[16]{0:T(128)S(1)}, s32[4]{0:T(128)S(1)}, s32[4]{0:T(128)S(1)}, f32[4,256,128]{2,1,0:T(8,128)S(1)}, f32[1,512]{1,0:T(1,128)S(1)}) custom-call(s32[4]{0:T(128)S(1)} %copy-done.4, s32[4]{0:T(128)S(1)} %copy-done.5, f32[4,256]{1,0:T(4,128)S(1)} %copy-done.1, f32[1,512]{1,0:T(1,128)S(1)} %bitcast.5, ...), custom_call_target="tpu_custom_call" | custom-call | tf_op jit(solution)/shard_map/pallas_call | solution.py:113
  18.1 3.3 %collective-permute-done.5.refs_5_ = bf16[256,128]{1,0:T(8,128)(2,1)S(1)} collective-permute-done((bf16[256,128]{1,0:T(8,128)(2,1)S(1)}, bf16[256,128]{1,0:T(8,128)(2,1)S(1)}, u32[]{:S(2)}, u32[]{:S(2)}) %collective-permute-start.5) | collective-permute-done | bytes 65568 | tf_op jit(solution)/shard_map/ppermute | solution.py:141
  21.3 0.0 collective-permute-done.refs_1_
  21.3 0.0 collective-permute-done.4.refs_0_
  21.3 2.5 %collective-permute-start.8 = (bf16[2,256,256]{2,1,0:T(8,128)(2,1)S(1)}, bf16[2,256,256]{2,1,0:T(8,128)(2,1)S(1)}, u32[]{:S(2)}, u32[]{:S(2)}) collective-permute-start(bf16[2,256,256]{2,1,0:T(8,128)(2,1)S(1)} %collective-permute-done.4.refs_0_), channel_id=1, source_target_pairs={{0,8},{8,12},{12,4},{4,0},{1,9},{9,13},{13,5},{5,1},{2,10},{10,14}... | collective-permute-start | bytes 786440 | tf_op jit(solution)/shard_map/ppermute | solution.py:141
  23.8 0.0 collective-permute-start.10
  23.8 0.0 collective-permute-start.9
  23.8 1.5 %collective-permute-start.6 = (bf16[2,256,256]{2,1,0:T(8,128)(2,1)S(1)}, bf16[2,256,256]{2,1,0:T(8,128)(2,1)S(1)}, u32[]{:S(2)}, u32[]{:S(2)}) collective-permute-start(bf16[2,256,256]{2,1,0:T(8,128)(2,1)S(1)} %collective-permute-done.4.refs_0_), channel_id=1, source_target_pairs={{0,2},{1,3},{2,0},{3,1},{4,6},{5,7},{6,4},{7,5},{8,10},{9,11},{10,... | collective-permute-start | bytes 786440 | tf_op jit(solution)/shard_map/ppermute | solution.py:145
  25.3 5.1 %collective-permute-done.10.refs_7_ = bf16[256,128]{1,0:T(8,128)(2,1)S(1)} collective-permute-done((bf16[256,128]{1,0:T(8,128)(2,1)S(1)}, bf16[256,128]{1,0:T(8,128)(2,1)S(1)}, u32[]{:S(2)}, u32[]{:S(2)}) %collective-permute-start.10) | collective-permute-done | bytes 65568 | tf_op jit(solution)/shard_map/ppermute | solution.py:141
  30.4 0.0 collective-permute-done.7.refs_3_
  30.4 0.0 collective-permute-done.9.refs_6_
  30.4 0.0 collective-permute-done.8.refs_2_
  30.4 1.6 %collective-permute-start.13 = (bf16[2,256,256]{2,1,0:T(8,128)(2,1)S(1)}, bf16[2,256,256]{2,1,0:T(8,128)(2,1)S(1)}, u32[]{:S(2)}, u32[]{:S(2)}) collective-permute-start(bf16[2,256,256]{2,1,0:T(8,128)(2,1)S(1)} %collective-permute-done.8.refs_2_), channel_id=1, source_target_pairs={{0,2},{1,3},{2,0},{3,1},{4,6},{5,7},{6,4},{7,5},{8,10},{9,11},{10,... | collective-permute-start | bytes 786440 | tf_op jit(solution)/shard_map/ppermute | solution.py:145
  32.0 3.1 %collective-permute-start.12 = (bf16[256,256]{1,0:T(8,128)(2,1)S(1)}, bf16[256,256]{1,0:T(8,128)(2,1)S(1)}, u32[]{:S(2)}, u32[]{:S(2)}) collective-permute-start(bf16[256,256]{1,0:T(8,128)(2,1)S(1)} %get-tuple-element.82), channel_id=1, source_target_pairs={{0,12},{8,4},{12,0},{4,8},{1,13},{9,5},{13,1},{5,9},{2,14},{10,6},... | collective-permute-start | bytes 393224 | tf_op jit(solution)/shard_map/ppermute | solution.py:141
  35.1 0.0 collective-permute-start.11
  35.1 1.7 %shard_map.105 = (bf16[2,256,256]{2,1,0:T(8,128)(2,1)S(1)}, bf16[2,4,256,256]{3,2,1,0:T(8,128)(2,1)S(1)}, bf16[2,2,2,256,256]{4,3,2,1,0:T(8,128)(2,1)}) custom-call(s32[4]{0:T(128)S(1)} %get-tuple-element.70.widths, bf16[2,256,256]{2,1,0:T(8,128)(2,1)S(1)} %bitcast.4, bf16[2,256,256]{2,1,0:T(8,128)(2,1)S(1)} %collective-permute-done.refs_1_, ...), custom_call_target="tpu_custom_call" | custom-call | flops 268435456 | bytes 4194304 | tf_op jit(solution)/shard_map/pallas_call | solution.py:113
  36.8 2.0 %collective-permute-done.12.refs_6_ = bf16[256,256]{1,0:T(8,128)(2,1)S(1)} collective-permute-done((bf16[256,256]{1,0:T(8,128)(2,1)S(1)}, bf16[256,256]{1,0:T(8,128)(2,1)S(1)}, u32[]{:S(2)}, u32[]{:S(2)}) %collective-permute-start.12) | collective-permute-done | bytes 131104 | tf_op jit(solution)/shard_map/ppermute | solution.py:141
  38.8 0.0 collective-permute-done.6.refs_1_
  38.8 0.0 collective-permute-done.11.refs_8_
  38.8 0.0 collective-permute-done.13.refs_3_
  38.8 2.7 %shard_map.106 = (bf16[4,256,256]{2,1,0:T(8,128)(2,1)S(1)}, bf16[4,256,256]{2,1,0:T(8,128)(2,1)S(1)}, bf16[2,2,2,256,256]{4,3,2,1,0:T(8,128)(2,1)}, f32[16,1,128]{2,1,0:T(1,128)}) custom-call(s32[16]{0:T(128)S(1)} %get-tuple-element.69.src, s32[4]{0:T(128)S(1)} %get-tuple-element.70.widths, bf16[2,256,256]{2,1,0:T(8,128)(2,1)S(1)} %collective-permute-done.4.refs_0_, ...), custom_call_target="tpu_custom_call" | custom-call | flops 1073741824 | bytes 6291456 | tf_op jit(solution)/shard_map/pallas_call | solution.py:113
  41.5 0.1 collective-permute-start.14
  41.6 4.6 %all-to-all-start = ((f32[16,1,128]{2,1,0:T(1,128)}), f32[16,1,128]{2,1,0:T(1,128)S(1)}, u32[]{:S(2)}, u32[]{:S(2)}) async-start(f32[16,1,128]{2,1,0:T(1,128)} %get-tuple-element.91), calls=%async_computation | async-start | bytes 16384 | tf_op jit(solution)/shard_map/all_to_all | solution.py:661
  46.2 0.0 collective-permute-done.14.other
  46.2 1.0 %shard_map.107 = (f32[4,256,256]{2,1,0:T(8,128)S(1)}, bf16[2,4,64,256]{3,2,1,0:T(8,128)(2,1)}) custom-call(bf16[4,256,256]{2,1,0:T(8,128)(2,1)S(1)} %get-tuple-element.95.mine, bf16[4,256,256]{2,1,0:T(8,128)(2,1)S(1)} %collective-permute-done.14.other, bf16[4,256,256]{2,1,0:T(8,128)(2,1)S(1)} %get-tuple-element.94.raw_in.refs_3_, ...), custom_call_target="tpu_custom_call" | custom-call | bytes 4194304 | tf_op jit(solution)/shard_map/pallas_call | solution.py:113
  47.2 1.9 %collective-permute-start.15 = (bf16[2,4,64,256]{3,2,1,0:T(8,128)(2,1)}, bf16[2,4,64,256]{3,2,1,0:T(8,128)(2,1)S(1)}, u32[]{:S(2)}, u32[]{:S(2)}) collective-permute-start(bf16[2,4,64,256]{3,2,1,0:T(8,128)(2,1)} %get-tuple-element.100), channel_id=1, source_target_pairs={{0,2},{1,3},{2,0},{3,1},{4,6},{5,7},{6,4},{7,5},{8,10},{9,11},{10,... | collective-permute-start | bytes 786440 | tf_op jit(solution)/shard_map/ppermute | solution.py:145
  49.2 3.4 %all-to-all-done.refs_2_.parts1 = f32[16,1,128]{2,1,0:T(1,128)S(1)} async-done(((f32[16,1,128]{2,1,0:T(1,128)}), f32[16,1,128]{2,1,0:T(1,128)S(1)}, u32[]{:S(2)}, u32[]{:S(2)}) %all-to-all-start) | async-done | bytes 8224 | tf_op jit(solution)/shard_map/all_to_all | solution.py:661
  52.5 3.9 %shard_map.108 = (f32[16,1,128]{2,1,0:T(1,128)S(1)}, bf16[4,4,64,256]{3,2,1,0:T(8,128)(2,1)S(1)}, bf16[1,4,64,256]{3,2,1,0:T(8,128)(2,1)S(1)}, bf16[2,4,64,256]{...) custom-call(s32[16]{0:T(128)S(1)} %get-tuple-element.69.src, s32[4]{0:T(128)S(1)} %get-tuple-element.70.widths, ...), custom_call_target="tpu_custom_call" | custom-call | flops 4294967296 | bytes 25165824 | tf_op jit(solution)/shard_map/pallas_call | solution.py:113
  56.5 0.6 collective-permute-start.17
  57.1 0.6 collective-permute-start.18
  57.7 0.0 collective-permute-done.15.refs_0_
  57.7 1.0 %collective-permute-start.16 = (bf16[1,4,64,256]{3,2,1,0:T(8,128)(2,1)S(1)}, bf16[1,4,64,256]{3,2,1,0:T(8,128)(2,1)S(1)}, u32[]{:S(2)}, u32[]{:S(2)}) collective-permute-start(bf16[1,4,64,256]{3,2,1,0:T(8,128)(2,1)S(1)} %get-tuple-element.102), channel_id=1, source_target_pairs={{0,1},{1,0},{2,3},{3,2},{4,5},{5,4},{6,7},{7,6},{8,9},{9,8},{10,11... | collective-permute-start | bytes 393224 | tf_op jit(solution)/shard_map/ppermute | solution.py:145
  58.7 10.2 %all_to_all.10.parts2 = f32[16,1,128]{2,1,0:T(1,128)S(1)} all-to-all(f32[16,1,128]{2,1,0:T(1,128)S(1)} %get-tuple-element.97), channel_id=1, replica_groups=mesh['grp'=2,'blk'=4,'op'=4] {'blk','op'}, dimensions={0} | all-to-all | bytes 16384 | tf_op jit(solution)/shard_map/all_to_all | solution.py:661
  68.9 0.0 collective-permute-done.18.refs_3_
  68.9 0.0 collective-permute-done.17.refs_2_
  68.9 0.0 collective-permute-done.16.refs_1_
  68.9 2.0 %shard_map.109 = (bf16[4,64,512]{2,1,0:T(8,128)(2,1)}, bf16[4,64,512]{2,1,0:T(8,128)(2,1)}, f32[1]{0:T(128)}) custom-call(s32[4]{0:T(128)S(1)} %get-tuple-element.68.slots, f32[16,1,128]{2,1,0:T(1,128)S(1)} %all-to-all-done.refs_2_.parts1, f32[16,1,128]{2,1,0:T(1,128)S(1)} %all_to_all.10.parts2, f32[4,256,128]{2,1,0:T(8,128)S(1)} %get-tuple-element.89.refs_11_.diag.refs_5_, ...), custom_call_target="tpu_custom_call" | custom-call | bytes 4194304 | tf_op jit(solution)/shard_map/pallas_call | solution.py:113
Async XLA Ops:
  0.6 4.1 %copy-start.3 = (s32[2]{0:T(128)S(1)}, s32[2]{0:T(128)}, u32[]{:S(2)}) copy-start(s32[2]{0:T(128)} %shift.1) | copy-start | bytes 28
  0.6 8.7 %copy-start = (bf16[2,1,256,256]{3,2,1,0:T(8,128)(2,1)S(1)}, bf16[2,1,256,256]{3,2,1,0:T(8,128)(2,1)}, u32[]{:S(2)}) copy-start(bf16[2,1,256,256]{3,2,1,0:T(8,128)(2,1)} %param.9) | copy-start | bytes 786436
  0.7 12.0 %collective-permute-start.1 = (bf16[2,256,256]{2,1,0:T(8,128)(2,1)}, bf16[2,256,256]{2,1,0:T(8,128)(2,1)S(1)}, u32[]{:S(2)}, u32[]{:S(2)}) collective-permute-start(bf16[2,256,256]{2,1,0:T(8,128)(2,1)} %bitcast.2), channel_id=1, source_target_pairs={{0,8},{8,12},{12,4},{4,0},{1,9},{9,13},{13,5},{5,1},{2,10},{10,14}... | collective-permute-start | bytes 786440 | tf_op jit(solution)/shard_map/ppermute | solution.py:141
  4.7 1.1 %collective-permute-start.2 = (s32[2]{0:T(128)S(1)}, s32[2]{0:T(128)S(1)}, u32[]{:S(2)}, u32[]{:S(2)}) collective-permute-start(s32[2]{0:T(128)S(1)} %copy-done.3), channel_id=1, source_target_pairs={{0,1},{1,0},{2,3},{3,2},{4,5},{5,4},{6,7},{7,6},{8,9},{9,8},{10,11... | collective-permute-start | bytes 32 | tf_op jit(solution)/shard_map/ppermute | solution.py:145
  7.8 4.9 %collective-permute-start.3 = (bf16[144,256]{1,0:T(8,128)(2,1)S(1)}, bf16[144,256]{1,0:T(8,128)(2,1)S(1)}, u32[]{:S(2)}, u32[]{:S(2)}) collective-permute-start(bf16[144,256]{1,0:T(8,128)(2,1)S(1)} %get-tuple-element.59), channel_id=1, source_target_pairs={{0,2},{1,3},{2,0},{3,1},{4,6},{5,7},{6,4},{7,5},{8,10},{9,11},{10,... | collective-permute-start | bytes 221192 | tf_op jit(solution)/shard_map/ppermute | solution.py:145
  9.3 12.0 %collective-permute-start = (bf16[2,256,256]{2,1,0:T(8,128)(2,1)S(1)}, bf16[2,256,256]{2,1,0:T(8,128)(2,1)S(1)}, u32[]{:S(2)}, u32[]{:S(2)}) collective-permute-start(bf16[2,256,256]{2,1,0:T(8,128)(2,1)S(1)} %bitcast.3), channel_id=1, source_target_pairs={{0,2},{1,3},{2,0},{3,1},{4,6},{5,7},{6,4},{7,5},{8,10},{9,11},{10,... | collective-permute-start | bytes 786440 | tf_op jit(solution)/shard_map/ppermute | solution.py:145
  12.7 4.0 %copy-start.1 = (f32[4,256]{1,0:T(4,128)S(1)}, f32[4,256]{1,0:T(4,128)}, u32[]{:S(2)}) copy-start(f32[4,256]{1,0:T(4,128)} %left_diag.1) | copy-start | bytes 12292
  12.7 4.0 %copy-start.2 = (f32[512]{0:T(512)S(1)}, f32[512]{0:T(512)}, u32[]{:S(2)}) copy-start(f32[512]{0:T(512)} %param.15) | copy-start | bytes 6148
  12.7 4.0 %copy-start.4 = (s32[4]{0:T(128)S(1)}, s32[4]{0:T(128)}, u32[]{:S(2)}) copy-start(s32[4]{0:T(128)} %sector.1) | copy-start | bytes 52
  12.7 4.0 %copy-start.5 = (s32[4]{0:T(128)S(1)}, s32[4]{0:T(128)}, u32[]{:S(2)}) copy-start(s32[4]{0:T(128)} %width.1) | copy-start | bytes 52
  12.7 8.6 %collective-permute-start.4 = (bf16[2,256,256]{2,1,0:T(8,128)(2,1)S(1)}, bf16[2,256,256]{2,1,0:T(8,128)(2,1)S(1)}, u32[]{:S(2)}, u32[]{:S(2)}) collective-permute-start(bf16[2,256,256]{2,1,0:T(8,128)(2,1)S(1)} %collective-permute-done.1.refs_2_), channel_id=1, source_target_pairs={{0,8},{8,12},{12,4},{4,0},{1,9},{9,13},{13,5},{5,1},{2,10},{10,14}... | collective-permute-start | bytes 786440 | tf_op jit(solution)/shard_map/ppermute | solution.py:141
  14.3 7.0 %collective-permute-start.5 = (bf16[256,128]{1,0:T(8,128)(2,1)S(1)}, bf16[256,128]{1,0:T(8,128)(2,1)S(1)}, u32[]{:S(2)}, u32[]{:S(2)}) collective-permute-start(bf16[256,128]{1,0:T(8,128)(2,1)S(1)} %get-tuple-element.55), channel_id=1, source_target_pairs={{0,8},{8,12},{12,4},{4,0},{1,9},{9,13},{13,5},{5,1},{2,10},{10,14}... | collective-permute-start | bytes 196616 | tf_op jit(solution)/shard_map/ppermute | solution.py:141
  14.9 15.5 %collective-permute-start.7 = (bf16[2,256,256]{2,1,0:T(8,128)(2,1)S(1)}, bf16[2,256,256]{2,1,0:T(8,128)(2,1)S(1)}, u32[]{:S(2)}, u32[]{:S(2)}) collective-permute-start(bf16[2,256,256]{2,1,0:T(8,128)(2,1)S(1)} %collective-permute-done.1.refs_2_), channel_id=1, source_target_pairs={{0,2},{1,3},{2,0},{3,1},{4,6},{5,7},{6,4},{7,5},{8,10},{9,11},{10,... | collective-permute-start | bytes 786440 | tf_op jit(solution)/shard_map/ppermute | solution.py:145
  21.3 9.1 %collective-permute-start.8 = (bf16[2,256,256]{2,1,0:T(8,128)(2,1)S(1)}, bf16[2,256,256]{2,1,0:T(8,128)(2,1)S(1)}, u32[]{:S(2)}, u32[]{:S(2)}) collective-permute-start(bf16[2,256,256]{2,1,0:T(8,128)(2,1)S(1)} %collective-permute-done.4.refs_0_), channel_id=1, source_target_pairs={{0,8},{8,12},{12,4},{4,0},{1,9},{9,13},{13,5},{5,1},{2,10},{10,14}... | collective-permute-start | bytes 786440 | tf_op jit(solution)/shard_map/ppermute | solution.py:141
  23.8 6.6 %collective-permute-start.10 = (bf16[256,128]{1,0:T(8,128)(2,1)S(1)}, bf16[256,128]{1,0:T(8,128)(2,1)S(1)}, u32[]{:S(2)}, u32[]{:S(2)}) collective-permute-start(bf16[256,128]{1,0:T(8,128)(2,1)S(1)} %get-tuple-element.74), channel_id=1, source_target_pairs={{0,4},{8,0},{12,8},{4,12},{1,5},{9,1},{13,9},{5,13},{2,6},{10,2},{... | collective-permute-start | bytes 196616 | tf_op jit(solution)/shard_map/ppermute | solution.py:141
  23.8 6.6 %collective-permute-start.9 = (bf16[256,128]{1,0:T(8,128)(2,1)S(1)}, bf16[256,128]{1,0:T(8,128)(2,1)S(1)}, u32[]{:S(2)}, u32[]{:S(2)}) collective-permute-start(bf16[256,128]{1,0:T(8,128)(2,1)S(1)} %collective-permute-done.5.refs_5_), channel_id=1, source_target_pairs={{0,1},{1,0},{2,3},{3,2},{4,5},{5,4},{6,7},{7,6},{8,9},{9,8},{10,11... | collective-permute-start | bytes 196616 | tf_op jit(solution)/shard_map/ppermute | solution.py:145
  23.8 15.0 %collective-permute-start.6 = (bf16[2,256,256]{2,1,0:T(8,128)(2,1)S(1)}, bf16[2,256,256]{2,1,0:T(8,128)(2,1)S(1)}, u32[]{:S(2)}, u32[]{:S(2)}) collective-permute-start(bf16[2,256,256]{2,1,0:T(8,128)(2,1)S(1)} %collective-permute-done.4.refs_0_), channel_id=1, source_target_pairs={{0,2},{1,3},{2,0},{3,1},{4,6},{5,7},{6,4},{7,5},{8,10},{9,11},{10,... | collective-permute-start | bytes 786440 | tf_op jit(solution)/shard_map/ppermute | solution.py:145
  30.4 8.4 %collective-permute-start.13 = (bf16[2,256,256]{2,1,0:T(8,128)(2,1)S(1)}, bf16[2,256,256]{2,1,0:T(8,128)(2,1)S(1)}, u32[]{:S(2)}, u32[]{:S(2)}) collective-permute-start(bf16[2,256,256]{2,1,0:T(8,128)(2,1)S(1)} %collective-permute-done.8.refs_2_), channel_id=1, source_target_pairs={{0,2},{1,3},{2,0},{3,1},{4,6},{5,7},{6,4},{7,5},{8,10},{9,11},{10,... | collective-permute-start | bytes 786440 | tf_op jit(solution)/shard_map/ppermute | solution.py:145
  32.0 6.8 %collective-permute-start.12 = (bf16[256,256]{1,0:T(8,128)(2,1)S(1)}, bf16[256,256]{1,0:T(8,128)(2,1)S(1)}, u32[]{:S(2)}, u32[]{:S(2)}) collective-permute-start(bf16[256,256]{1,0:T(8,128)(2,1)S(1)} %get-tuple-element.82), channel_id=1, source_target_pairs={{0,12},{8,4},{12,0},{4,8},{1,13},{9,5},{13,1},{5,9},{2,14},{10,6},... | collective-permute-start | bytes 393224 | tf_op jit(solution)/shard_map/ppermute | solution.py:141
  35.1 3.7 %collective-permute-start.11 = (bf16[256,128]{1,0:T(8,128)(2,1)S(1)}, bf16[256,128]{1,0:T(8,128)(2,1)S(1)}, u32[]{:S(2)}, u32[]{:S(2)}) collective-permute-start(bf16[256,128]{1,0:T(8,128)(2,1)S(1)} %collective-permute-done.10.refs_7_), channel_id=1, source_target_pairs={{0,1},{1,0},{2,3},{3,2},{4,5},{5,4},{6,7},{7,6},{8,9},{9,8},{10,11... | collective-permute-start | bytes 196616 | tf_op jit(solution)/shard_map/ppermute | solution.py:145
  41.5 4.7 %collective-permute-start.14 = (bf16[4,256,256]{2,1,0:T(8,128)(2,1)S(1)}, bf16[4,256,256]{2,1,0:T(8,128)(2,1)S(1)}, u32[]{:S(2)}, u32[]{:S(2)}) collective-permute-start(bf16[4,256,256]{2,1,0:T(8,128)(2,1)S(1)} %get-tuple-element.95.mine), channel_id=1, source_target_pairs={{0,1},{1,0},{2,3},{3,2},{4,5},{5,4},{6,7},{7,6},{8,9},{9,8},{10,11... | collective-permute-start | bytes 1572872 | tf_op jit(solution)/shard_map/ppermute | solution.py:145
  41.6 11.0 %all-to-all-start = ((f32[16,1,128]{2,1,0:T(1,128)}), f32[16,1,128]{2,1,0:T(1,128)S(1)}, u32[]{:S(2)}, u32[]{:S(2)}) async-start(f32[16,1,128]{2,1,0:T(1,128)} %get-tuple-element.91), calls=%async_computation | async-start | bytes 16384 | tf_op jit(solution)/shard_map/all_to_all | solution.py:661
  47.2 10.4 %collective-permute-start.15 = (bf16[2,4,64,256]{3,2,1,0:T(8,128)(2,1)}, bf16[2,4,64,256]{3,2,1,0:T(8,128)(2,1)S(1)}, u32[]{:S(2)}, u32[]{:S(2)}) collective-permute-start(bf16[2,4,64,256]{3,2,1,0:T(8,128)(2,1)} %get-tuple-element.100), channel_id=1, source_target_pairs={{0,2},{1,3},{2,0},{3,1},{4,6},{5,7},{6,4},{7,5},{8,10},{9,11},{10,... | collective-permute-start | bytes 786440 | tf_op jit(solution)/shard_map/ppermute | solution.py:145
  56.5 12.5 %collective-permute-start.17 = (bf16[2,4,64,256]{3,2,1,0:T(8,128)(2,1)S(1)}, bf16[2,4,64,256]{3,2,1,0:T(8,128)(2,1)S(1)}, u32[]{:S(2)}, u32[]{:S(2)}) collective-permute-start(bf16[2,4,64,256]{3,2,1,0:T(8,128)(2,1)S(1)} %get-tuple-element.103), channel_id=1, source_target_pairs={{0,2},{1,3},{2,0},{3,1},{4,6},{5,7},{6,4},{7,5},{8,10},{9,11},{10,... | collective-permute-start | bytes 786440 | tf_op jit(solution)/shard_map/ppermute | solution.py:145
  57.1 11.9 %collective-permute-start.18 = (bf16[1,4,64,256]{3,2,1,0:T(8,128)(2,1)S(1)}, bf16[1,4,64,256]{3,2,1,0:T(8,128)(2,1)S(1)}, u32[]{:S(2)}, u32[]{:S(2)}) collective-permute-start(bf16[1,4,64,256]{3,2,1,0:T(8,128)(2,1)S(1)} %get-tuple-element.104), channel_id=1, source_target_pairs={{0,3},{1,2},{2,1},{3,0},{4,7},{5,6},{6,5},{7,4},{8,11},{9,10},{10,... | collective-permute-start | bytes 393224 | tf_op jit(solution)/shard_map/ppermute | solution.py:145
  57.7 11.3 %collective-permute-start.16 = (bf16[1,4,64,256]{3,2,1,0:T(8,128)(2,1)S(1)}, bf16[1,4,64,256]{3,2,1,0:T(8,128)(2,1)S(1)}, u32[]{:S(2)}, u32[]{:S(2)}) collective-permute-start(bf16[1,4,64,256]{3,2,1,0:T(8,128)(2,1)S(1)} %get-tuple-element.102), channel_id=1, source_target_pairs={{0,1},{1,0},{2,3},{3,2},{4,5},{5,4},{6,7},{7,6},{8,9},{9,8},{10,11... | collective-permute-start | bytes 393224 | tf_op jit(solution)/shard_map/ppermute | solution.py:145
